TPU v7x, 32 devices: a whole 2x2x4 slice. The times are simulated.
32 devices in a mesh: groups: 2 (over y), serve: 4 (over z), tensor: 4 (over x, core).
Axes of the slice: x: 2, y: 2, z: 4, core: 2. Of those that a mesh axis runs over, the one named last changes fastest.
Arguments:
- tokens: bfloat16 [12288, 4096], P(('groups', 'serve'), 'tensor'), parts along dimension 0, as said below
- norm_gain: bfloat16 [4096], P('tensor'), may hold values from 0.099609375 to 1.8984375
- kv_weight: bfloat16 [4096, 2048], P('tensor'), may hold values from -0.09375 to 0.09375
- live_blocks: int32 [8], P('groups'), parts along dimension 0, may hold values from 1 to 24, 48 in all
- span_offset: int32 [8], P('groups'), parts along dimension 0, may hold values from 0 to 2
Outputs:
- kv_cache: bfloat16 [12288, 2048], P(('groups', 'serve'), 'tensor'), parts along dimension 0
There are 2 independent parts, one for each index of `groups`. A program takes and returns all parts, laid end to end along the dimension named above; an argument that names none is the same for every part. Nothing has to cross between parts.
Inputs may be any that keep to these rules, and one draw needn't show every extreme that they name: `live_blocks`: the 4 lengths sum to exactly 48 row blocks; the longest is exactly 24. `span_offset`: every position stays below 2048. `tokens`: finite hidden states.
All inputs are finite; a program needn't handle non-finite values.
Results may differ from a plain program's by a relative error of at most 0.012.
Values may be sent and summed in bfloat16 or wider, within the bound.
No kernel may reach another device: no remote copies, remote signals or barrier semaphores. Data moves between devices by JAX's collectives and lax.ppermute only.
A program may use at most 64 MiB of HBM per device.

v0:
```python
import jax
import jax.numpy as jnp
from jax import lax
from jax.sharding import PartitionSpec as P

D = 4096
HD = 128
PAGE = 256
BLOCK = 64
HELP = 12


rope_base = 500000.0
norm_eps = 1e-05


def rotate_pairs(values, positions):
    half_dim = values.shape[-1] // 2
    inv_freq = rope_base ** (-(jnp.arange(half_dim, dtype=jnp.float32) * 2.0) / values.shape[-1])
    angles = positions.astype(jnp.float32)[:, None] * inv_freq[None, :]
    cosine = jnp.cos(angles)[:, None, :]
    sine_part = jnp.sin(angles)[:, None, :]
    key_part = values[:, :, 0, :]
    first_half = key_part[..., :half_dim]
    second = key_part[..., half_dim:]
    rotated = jnp.concatenate(
        [first_half * cosine - second * sine_part, second * cosine + first_half * sine_part],
        axis=-1,
    )
    return jnp.stack([rotated, values[:, :, 1, :]], axis=2)


def row_scales(row_block):
    wide_rows = row_block.astype(jnp.float32)
    squares = jnp.sum(wide_rows * wide_rows, axis=1)
    totals = lax.psum(squares, "tensor")
    return 1.0 / jnp.sqrt(totals / D + norm_eps)


def rebuild_rows(row_block, scales, positions, norm_gain, kv_weight):
    scaled = (row_block.astype(jnp.float32) * norm_gain.astype(jnp.float32)[None, :]).astype(
        jnp.bfloat16
    )
    partial_sums = jnp.dot(scaled, kv_weight, preferred_element_type=jnp.float32)
    summed = lax.psum_scatter(
        partial_sums.astype(jnp.bfloat16), "tensor", scatter_dimension=1, tiled=True
    ).astype(jnp.float32)
    head_count = summed.shape[1] // (2 * HD)
    values = (summed * scales[:, None]).reshape(summed.shape[0], head_count, 2, HD)
    return (
        rotate_pairs(values, positions)
        .reshape(summed.shape[0], summed.shape[1])
        .astype(jnp.bfloat16)
    )


def shards(tokens, norm_gain, kv_weight, live_blocks, span_offset):
    serve_count = lax.axis_size("serve")
    own_index = lax.axis_index("serve")
    slot_rows = tokens.shape[0]
    unit_count = slot_rows // BLOCK
    feature_count = tokens.shape[1]
    starts = jnp.cumsum(live_blocks) - live_blocks
    own_start = starts[own_index]
    own_length = live_blocks[own_index]
    keep_rows = jnp.arange(slot_rows, dtype=jnp.int32) < own_length * BLOCK
    capacity = -(-unit_count // serve_count)
    blocked = tokens.reshape(unit_count, BLOCK, feature_count)
    peer_ids = jnp.arange(serve_count, dtype=jnp.int32)
    slot_ids = jnp.arange(capacity, dtype=jnp.int32)
    send_block = (peer_ids[:, None] - own_start) % serve_count + slot_ids[None, :] * serve_count
    send_index = jnp.minimum(send_block, unit_count - 1).reshape(-1)
    outgoing = jnp.take(blocked, send_index, axis=0).reshape(
        serve_count, capacity, BLOCK, feature_count
    )
    incoming = lax.all_to_all(outgoing, "serve", split_axis=0, concat_axis=0, tiled=True)
    global_ids = own_index + jnp.arange(HELP, dtype=jnp.int32) * serve_count
    block_ends = starts + live_blocks
    owner_ids = jnp.sum((block_ends[None, :] <= global_ids[:, None]).astype(jnp.int32), axis=1)
    block_ids = global_ids - starts[owner_ids]
    flat_ids = owner_ids * capacity + block_ids // serve_count
    row_here = jnp.take(
        incoming.reshape(serve_count * capacity, BLOCK, feature_count), flat_ids, axis=0
    ).reshape(HELP * BLOCK, feature_count)
    positions = (
        (span_offset[owner_ids] * PAGE + block_ids * BLOCK)[:, None]
        + jnp.arange(BLOCK, dtype=jnp.int32)[None, :]
    ).reshape(-1)
    scales = row_scales(row_here)
    rebuilt = rebuild_rows(row_here, scales, positions, norm_gain, kv_weight)
    column_part = rebuilt.shape[1]
    result_blocks = rebuilt.reshape(HELP, BLOCK, column_part)
    back_first = (own_index - starts) % serve_count
    back_global = starts[:, None] + back_first[:, None] + slot_ids[None, :] * serve_count
    back_slot = jnp.minimum(back_global // serve_count, HELP - 1).reshape(-1)
    outgoing_kv = jnp.take(result_blocks, back_slot, axis=0).reshape(
        serve_count, capacity, BLOCK, column_part
    )
    returned = lax.all_to_all(outgoing_kv, "serve", split_axis=0, concat_axis=0, tiled=True)
    own_blocks = jnp.arange(unit_count, dtype=jnp.int32)
    from_helper = (own_start + own_blocks) % serve_count
    from_slot = own_blocks // serve_count
    assembled = jnp.take(
        returned.reshape(serve_count * capacity, BLOCK, column_part),
        from_helper * capacity + from_slot,
        axis=0,
    ).reshape(slot_rows, column_part)
    return jnp.where(keep_rows[:, None], assembled, jnp.zeros_like(assembled))


def solution(mesh):
    in_specs = (
        P(("groups", "serve"), "tensor"),
        P("tensor"),
        P("tensor", None),
        P("groups"),
        P("groups"),
    )
    out_specs = P(("groups", "serve"), "tensor")
    return jax.shard_map(shards, mesh=mesh, in_specs=in_specs, out_specs=out_specs, check_vma=False)
```

profile of v0, /device:TPU:0, one launch (start us, length us, event | category | flops | bytes accessed | tf_op | source)
XLA Modules:
  0.0 218.4 jit_solution(15490317664831493541)
XLA Ops:
  6.5 1.0 reduce-window.8
  7.5 0.7 fusion.6
  8.2 0.6 dynamic_slice.7
  8.8 0.6 and_select_fusion.4
  9.4 0.1 broadcast_add_fusion
  9.5 0.6 compare_and_fusion.2
  10.1 0.1 min.35
  10.2 2.5 %gather_fusion.1 = bf16[24,64,1024]{2,1,0:T(8,128)(2,1)} fusion(bf16[24,64,1024]{2,1,0:T(8,128)(2,1)S(1)} %bitcast.44, s32[1024]{0:T(1024)S(1)} %pad_clamp_fusion.3), kind=kCustom, calls=%fused_computation.1 | custom fusion | bytes 6291552 | tf_op jit(solution)/shard_map/jit(_take)/gather | solution.py:73
  12.7 3.9 %broadcast_select_fusion = bf16[4,6,64,1024]{3,2,1,0:T(8,128)(2,1)} fusion(bf16[4,6,64,1024]{3,2,1,0:T(8,128)(2,1)} %bitcast.45, pred[4,6]{1,0:T(4,128)(4,1)S(1)} %get-tuple-element.12), kind=kLoop, calls=%fused_computation.9 | loop fusion | flops 1572864 | bytes 6291480 | tf_op jit(solution)/shard_map/jit(_take)/select_n | solution.py:73
  16.6 6.4 %all-to-all-start = ((bf16[4,6,64,1024]{3,2,1,0:T(8,128)(2,1)}), bf16[4,6,64,1024]{3,2,1,0:T(8,128)(2,1)}, u32[]{:S(2)}, u32[]{:S(2)}) async-start(bf16[4,6,64,1024]{3,2,1,0:T(8,128)(2,1)} %broadcast_select_fusion), calls=%async_computation | async-start | bytes 6291456 | tf_op jit(solution)/shard_map/all_to_all | solution.py:76
  23.1 0.1 convert_reduce_fusion
  23.2 0.7 gather_fusion
  23.9 0.1 broadcast_in_dim.86
  23.9 0.1 broadcast_in_dim.87
  24.1 69.8 %all-to-all-done = bf16[4,6,64,1024]{3,2,1,0:T(8,128)(2,1)} async-done(((bf16[4,6,64,1024]{3,2,1,0:T(8,128)(2,1)}), bf16[4,6,64,1024]{3,2,1,0:T(8,128)(2,1)}, u32[]{:S(2)}, u32[]{:S(2)}) %all-to-all-start) | async-done | bytes 3145760 | tf_op jit(solution)/shard_map/all_to_all | solution.py:76
  93.8 3.7 %gather_fusion.2 = bf16[12,64,1024]{2,1,0:T(8,128)(2,1)} fusion(bf16[24,64,1024]{2,1,0:T(8,128)(2,1)} %bitcast.9, s32[1024]{0:T(1024)S(1)} %pad_clamp_fusion.2), kind=kCustom, calls=%fused_computation.2 | custom fusion | bytes 3145776 | tf_op jit(solution)/shard_map/jit(_take)/gather | solution.py:82
  97.6 1.6 bitcast_select_fusion.1
  99.2 7.0 %convolution_convert_fusion = bf16[768,2048]{1,0:T(8,128)(2,1)} fusion(bf16[1024,2048]{1,0:T(8,128)(2,1)} %param.7, bf16[768,1024]{1,0:T(8,128)(2,1)S(1)} %bitcast_select_fusion.1, f32[1024]{0:T(1024)S(1)} %convert_element_type.39), kind=kOutput, calls=%fused_computation.6 | convolution fusion | flops 3225157632 | bytes 8916992 | tf_op jit(solution)/shard_map/dot_general | solution.py:44
  106.2 0.6 copy-done.1
  106.8 0.7 gather_fusion.3
  107.5 0.1 add_convert_fusion.1
  107.6 0.1 convert_element_type.45
  107.6 0.1 add.344
  107.8 2.4 %multiply_cosine_fusion = (f32[768,64]{1,0:T(8,128)S(1)}, f32[768,64]{1,0:T(8,128)}) fusion(f32[64]{0:T(128)S(1)} %multiply_power_fusion, f32[768]{0:T(1024)S(1)} %convert_element_type.45), kind=kLoop, calls=%fused_computation.22 | loop fusion | flops 49152 | bytes 396544 | tf_op jit(solution)/shard_map/cos | solution.py:21
  110.2 2.2 multiply_reduce_fusion
  112.5 5.6 %psum.7 = f32[768]{0:T(1024)S(1)} all-reduce(f32[768]{0:T(1024)S(1)} %reduce_sum.25), channel_id=1, replica_groups=mesh['groups'=2,'serve'=4,'tensor'=4] {'tensor'}, use_global_device_ids=true, to_apply=%region_4.5 | all-reduce | flops 768 | bytes 6144 | tf_op jit(solution)/shard_map/psum | solution.py:36
  118.1 25.3 %reduce-scatter.2.cloned.1.call-done = bf16[768,512]{1,0:T(8,128)(2,1)} async-done(((bf16[768,2048]{1,0:T(8,128)(2,1)}), bf16[768,512]{1,0:T(8,128)(2,1)}) %reduce-scatter.2.cloned.1.call-update) | async-done | bytes 786448 | tf_op jit(solution)/shard_map/reduce_scatter | solution.py:45
  143.4 2.4 %convert_multiply_fusion = f32[768,512]{1,0:T(8,128)} fusion(bf16[768,512]{1,0:T(8,128)(2,1)} %reduce-scatter.2.cloned.1.call-done, f32[768]{0:T(1024)S(1)} %add_rsqrt_fusion), kind=kLoop, calls=%fused_computation.13 | loop fusion | flops 786432 | bytes 2362368 | tf_op jit(solution)/shard_map/mul | solution.py:49
  145.9 3.0 %reshape.501 = f32[768,2,2,128]{3,2,1,0:T(2,128)} reshape(f32[768,512]{1,0:T(8,128)} %convert_multiply_fusion) | data formatting | bytes 3145728 | tf_op jit(solution)/shard_map/reshape | solution.py:49
  148.9 1.4 copy-done.2
  150.3 0.8 slice.32
  151.3 0.8 copy-done.3
  152.1 0.4 subtract_convert_fusion
  152.5 0.2 maximum_bitcast_fusion
  152.8 0.1 pad_maximum_fusion
  152.8 1.7 copy.14
  154.5 3.1 %convert_element_type.46 = bf16[12,64,512]{2,1,0:T(8,128)(2,1)} reshape(bf16[768,2,2,128]{3,2,1,0:T(2,128)(2,1)} %copy.14) | data formatting | bytes 1572864 | tf_op jit(solution)/shard_map/convert_element_type | solution.py:53
  157.7 3.0 %gather_fusion.4 = bf16[24,64,512]{2,1,0:T(8,128)(2,1)} fusion(bf16[12,64,512]{2,1,0:T(8,128)(2,1)} %convert_element_type.46, s32[1024]{0:T(1024)S(1)} %pad_clamp_fusion.1), kind=kCustom, calls=%fused_computation.4 | custom fusion | bytes 3145824 | tf_op jit(solution)/shard_map/jit(_take)/gather | solution.py:96
  160.6 2.8 %broadcast_select_fusion.1 = bf16[4,6,64,512]{3,2,1,0:T(8,128)(2,1)} fusion(bf16[4,6,64,512]{3,2,1,0:T(8,128)(2,1)} %bitcast.47, pred[4,6]{1,0:T(4,128)(4,1)S(1)} %copy-done.5), kind=kLoop, calls=%fused_computation.15 | loop fusion | flops 786432 | bytes 3145752 | tf_op jit(solution)/shard_map/jit(_take)/select_n | solution.py:96
  163.4 4.7 %all-to-all-start.1 = ((bf16[4,6,64,512]{3,2,1,0:T(8,128)(2,1)}), bf16[4,6,64,512]{3,2,1,0:T(8,128)(2,1)}, u32[]{:S(2)}, u32[]{:S(2)}) async-start(bf16[4,6,64,512]{3,2,1,0:T(8,128)(2,1)} %broadcast_select_fusion.1), calls=%async_computation.2 | async-start | bytes 3145728 | tf_op jit(solution)/shard_map/all_to_all | solution.py:99
  168.1 0.6 dynamic_slice.6
  168.8 0.6 compare_and_fusion.3
  169.4 0.1 broadcast_in_dim.82
  169.5 0.1 broadcast_in_dim.83
  170.2 0.6 fusion.19
  170.9 34.3 %all-to-all-done.1 = bf16[4,6,64,512]{3,2,1,0:T(8,128)(2,1)} async-done(((bf16[4,6,64,512]{3,2,1,0:T(8,128)(2,1)}), bf16[4,6,64,512]{3,2,1,0:T(8,128)(2,1)}, u32[]{:S(2)}, u32[]{:S(2)}) %all-to-all-start.1) | async-done | bytes 1572896 | tf_op jit(solution)/shard_map/all_to_all | solution.py:99
  205.2 3.3 %gather_fusion.5 = bf16[24,64,512]{2,1,0:T(8,128)(2,1)} fusion(bf16[24,64,512]{2,1,0:T(8,128)(2,1)} %bitcast.17, s32[1024]{0:T(1024)S(1)} %pad_clamp_fusion), kind=kCustom, calls=%fused_computation.5 | custom fusion | bytes 3145824 | tf_op jit(solution)/shard_map/jit(_take)/gather | solution.py:103
  208.5 3.1 %fusion = bf16[1536,512]{1,0:T(8,128)(2,1)} fusion(bf16[24,64,512]{2,1,0:T(8,128)(2,1)} %gather_fusion.5, pred[1536]{0:T(1024)(128)(4,1)S(1)} %broadcast_in_dim.83, pred[1536]{0:T(1024)(128)(4,1)S(1)} %iota_compare_fusion), kind=kLoop, calls=%fused_computation.11 | loop fusion | flops 1572864 | bytes 3148800 | tf_op jit(solution)/shard_map/jit(_where)/select_n | solution.py:108
  (35 shorter events, 0.4 us)
Async XLA Ops:
  6.5 3.6 %copy-start = (bf16[1536,1024]{1,0:T(8,128)(2,1)S(1)}, bf16[1536,1024]{1,0:T(8,128)(2,1)}, u32[]{:S(2)}) copy-start(bf16[1536,1024]{1,0:T(8,128)(2,1)} %param.5) | copy-start | bytes 9437188
  16.6 7.4 %copy-start.4 = (bf16[1024]{0:T(1024)(128)(2,1)S(1)}, bf16[1024]{0:T(1024)(128)(2,1)}, u32[]{:S(2)}) copy-start(bf16[1024]{0:T(1024)(128)(2,1)} %param.6) | copy-start | bytes 6148
  16.6 77.2 %all-to-all-start = ((bf16[4,6,64,1024]{3,2,1,0:T(8,128)(2,1)}), bf16[4,6,64,1024]{3,2,1,0:T(8,128)(2,1)}, u32[]{:S(2)}, u32[]{:S(2)}) async-start(bf16[4,6,64,1024]{3,2,1,0:T(8,128)(2,1)} %broadcast_select_fusion), calls=%async_computation | async-start | bytes 6291456 | tf_op jit(solution)/shard_map/all_to_all | solution.py:76
  23.1 120.3 %reduce-scatter.2.cloned.1.call-start = ((), (), s32[]{:S(2)}) async-start(), calls=%async_computation.3 | async-start | bytes 3932160 | tf_op jit(solution)/shard_map/reduce_scatter | solution.py:45
  106.2 0.7 copy-start.1
  148.9 1.4 copy-start.2
  148.9 2.2 %slice-start = ((f32[768,2,2,128]{3,2,1,0:T(2,128)}), f32[768,2,1,128]{3,2,1,0:T(1,128)S(1)}, s32[]{:S(2)}) async-start(f32[768,2,2,128]{3,2,1,0:T(2,128)} %reshape.501), calls=%async_computation.4 | async-start | bytes 1572864 | tf_op jit(solution)/shard_map/slice | solution.py:23
  151.1 1.0 copy-start.3
  157.7 3.0 %copy-start.5 = (pred[4,6]{1,0:T(4,128)(4,1)S(1)}, pred[4,6]{1,0:T(4,128)(4,1)}, u32[]{:S(2)}) copy-start(pred[4,6]{1,0:T(4,128)(4,1)} %get-tuple-element.11) | copy-start | bytes 76
  163.4 4.7 %copy-start.6 = (s32[4]{0:T(128)S(1)}, s32[4]{0:T(128)}, u32[]{:S(2)}) copy-start(s32[4]{0:T(128)} %param.8) | copy-start | bytes 52
  163.4 41.8 %all-to-all-start.1 = ((bf16[4,6,64,512]{3,2,1,0:T(8,128)(2,1)}), bf16[4,6,64,512]{3,2,1,0:T(8,128)(2,1)}, u32[]{:S(2)}, u32[]{:S(2)}) async-start(bf16[4,6,64,512]{3,2,1,0:T(8,128)(2,1)} %broadcast_select_fusion.1), calls=%async_computation.2 | async-start | bytes 3145728 | tf_op jit(solution)/shard_map/all_to_all | solution.py:99
Sparse Core Ops, SparseCore 0:
  106.3 37.0 reduce-scatter.1
where the time goes:
time: 219 us; the launch traced here: 218 us
  waiting for transfers between devices  129 us (59%)
  local copies, waits for them, and re-layouts  27.4 us (13%)
  other arithmetic  23.7 us (11%)
  between operations  14.2 us (6%)
  starting transfers between devices  11.2 us (5%)
  matrix products  6.97 us (3%)
  blocking collectives  5.63 us (3%)
    all_to_all x1, waiting for transfers between devices, shards(): lax.all_to_all(outgoing, 'serve', split_axis=0, concat_axis=0, tiled=True)  69.8 us
    all_to_all x1, waiting for transfers between devices, shards(): lax.all_to_all(outgoing_kv, 'serve', split_axis=0, concat_axis=0, tiled=T...  34.3 us
    reduce_scatter x1, waiting for transfers between devices, rebuild_rows(): lax.psum_scatter(partial_sums.astype(jnp.bfloat16), 'tensor', scatter_dim...  25.3 us
    dot_general x1, matrix products, rebuild_rows(): jnp.dot(scaled, kv_weight, preferred_element_type=jnp.float32)  6.97 us
    all_to_all x1, starting transfers between devices, shards(): lax.all_to_all(outgoing, 'serve', split_axis=0, concat_axis=0, tiled=True)  6.45 us
    psum x1, blocking collectives, row_scales(): totals = lax.psum(squares, 'tensor')  5.63 us
    all_to_all x1, starting transfers between devices, shards(): lax.all_to_all(outgoing_kv, 'serve', split_axis=0, concat_axis=0, tiled=T...  4.73 us
  transfers between devices with their start and end apart: 3, of which 3 were waited for; matrix products, arithmetic and copies ran while one was open for 4% of the time, Pallas kernels for 0%

commit v1 on v0

v1 whole, which is shorter than its diff:
```python
import functools

import jax
import jax.numpy as jnp
from jax import lax
from jax.experimental import pallas as pl
from jax.experimental.pallas import tpu as pltpu
from jax.sharding import PartitionSpec as P

HD = 128
PAGE = 256
BLOCK = 64
LANES = 128

rope_base = 500000.0
norm_eps = 1e-05

TILE = 128
CHUNKS = (1, 2, 3, 3, 2, 1)
PIECES = (3, 9)


def scaled_rows(rows_ref, gain_ref):
    wide = rows_ref[...].astype(jnp.float32) * gain_ref[...].astype(jnp.float32)
    return wide.astype(jnp.bfloat16)


def pair_product(near_ref, far_ref, near_gain, far_gain, near_weight, far_weight):
    total = jnp.dot(
        scaled_rows(near_ref, near_gain), near_weight[...], preferred_element_type=jnp.float32
    )
    return total + jnp.dot(
        scaled_rows(far_ref, far_gain), far_weight[...], preferred_element_type=jnp.float32
    )


def partial_kernel(place, near, far, near_gain, far_gain, near_weight, far_weight, out):
    out[...] = pair_product(near, far, near_gain, far_gain, near_weight, far_weight).astype(out.dtype)


def squares_kernel(rows_ref, out):
    total = jnp.zeros((LANES, LANES), jnp.float32)
    for part in range(rows_ref.shape[1] // LANES):
        wide = rows_ref[:, part * LANES : (part + 1) * LANES].astype(jnp.float32)
        total += wide * wide
    out[0] = jnp.sum(jnp.transpose(total), axis=0, keepdims=True)


def finish_kernel(first_tile, model_dim, place, live, *refs):
    (near, far, near_gain, far_gain, near_weight, far_weight, squares, cosine, sine) = refs[:9]
    arrived, out = refs[9:-2], refs[-1]
    values = pair_product(near, far, near_gain, far_gain, near_weight, far_weight)
    for part in arrived:
        values += part[...].astype(jnp.float32)
    square_row = jnp.sum(squares[...], axis=0)
    on_diagonal = lax.broadcasted_iota(jnp.int32, (TILE, TILE), 0) == lax.broadcasted_iota(
        jnp.int32, (TILE, TILE), 1
    )
    totals = jnp.sum(jnp.where(on_diagonal, square_row, 0.0), axis=1, keepdims=True)
    scales = 1.0 / jnp.sqrt(totals / model_dim + norm_eps)
    row = (first_tile + pl.program_id(0)) * TILE + lax.broadcasted_iota(jnp.int32, (TILE, 1), 0)
    alive = row < live[place[2]] * BLOCK
    for start in range(0, out.shape[1], 2 * HD):
        key = values[:, start : start + HD] * scales
        turned = key * cosine[...] + pltpu.roll(key, HD // 2, 1) * sine[...]
        out[:, start : start + HD] = jnp.where(alive, turned, 0.0).astype(out.dtype)
        value = values[:, start + HD : start + 2 * HD] * scales
        out[:, start + HD : start + 2 * HD] = jnp.where(alive, value, 0.0).astype(out.dtype)


def shards(tokens, norm_gain, kv_weight, live_blocks, span_offset):
    tensor_count = lax.axis_size("tensor")
    chip_count = tensor_count // 2
    me = lax.axis_index("tensor")
    own_index = lax.axis_index("serve")
    slot_rows, depth = tokens.shape
    columns = kv_weight.shape[1] // tensor_count
    tiles = slot_rows // TILE
    model_dim = depth * tensor_count

    swap = [(i, i ^ 1) for i in range(tensor_count)]

    def shift(step):
        return [(i, (i + 2 * step) % tensor_count) for i in range(tensor_count)]

    def block_of(step):
        return (me + 2 * step) % tensor_count

    far_gain = lax.ppermute(norm_gain, "tensor", swap)
    far_weight = [None] * chip_count
    far_tokens = []
    for step in list(range(1, chip_count)) + [0]:
        sent = lax.dynamic_slice_in_dim(kv_weight, (block_of(step) ^ 1) * columns, columns, axis=1)
        far_weight[step] = lax.ppermute(sent, "tensor", swap)
    tile_at = 0
    for piece in PIECES:
        sent = tokens[tile_at * TILE : (tile_at + piece) * TILE]
        far_tokens.append((tile_at, lax.ppermute(sent, "tensor", swap)))
        tile_at += piece

    near_gain = norm_gain.reshape(1, depth)
    far_gain = far_gain.reshape(1, depth)

    own_squares = pl.pallas_call(
        squares_kernel,
        grid=(tiles,),
        in_specs=[pl.BlockSpec((TILE, depth), lambda i: (i, 0))],
        out_specs=pl.BlockSpec((1, 1, TILE), lambda i: (i, 0, 0)),
        out_shape=jax.ShapeDtypeStruct((tiles, 1, TILE), jnp.float32),
    )(tokens)
    flat = own_squares.reshape(tiles, TILE)
    pair_squares = flat + lax.ppermute(flat, "tensor", swap)
    squares = jnp.stack(
        [pair_squares] + [lax.ppermute(pair_squares, "tensor", shift(s)) for s in range(1, chip_count)]
    ).reshape(chip_count, tiles, 1, TILE)

    half = HD // 2
    inv_freq = rope_base ** (-(jnp.arange(half, dtype=jnp.float32) * 2.0) / HD)
    positions = span_offset[own_index] * PAGE + jnp.arange(slot_rows, dtype=jnp.int32)
    angles = positions.astype(jnp.float32)[:, None] * inv_freq[None, :]
    cosine, sine = jnp.cos(angles), jnp.sin(angles)
    cosine = jnp.concatenate([cosine, cosine], axis=1)
    sine = jnp.concatenate([-sine, sine], axis=1)

    def piece_at(tile):
        found = [p for p in far_tokens if p[0] <= tile]
        return found[-1]

    def operand_specs(first, piece_first):
        return [
            pl.BlockSpec((TILE, depth), lambda i, *_: (first + i, 0)),
            pl.BlockSpec((TILE, depth), lambda i, *_: (first - piece_first + i, 0)),
            pl.BlockSpec((1, depth), lambda i, *_: (0, 0)),
            pl.BlockSpec((1, depth), lambda i, *_: (0, 0)),
        ]

    def weight_specs(slot):
        return [
            pl.BlockSpec((depth, columns), lambda i, place, *_: (0, place[slot])),
            pl.BlockSpec((depth, columns), lambda i, *_: (0, 0)),
        ]

    params = pltpu.CompilerParams(vmem_limit_bytes=32 * 1024 * 1024)

    def product_cost(rows):
        return pl.CostEstimate(
            flops=4 * rows * depth * columns,
            bytes_accessed=4 * rows * depth + 4 * depth * columns + 2 * rows * columns,
            transcendentals=0,
        )

    def make_partial(first, count, step):
        piece_first, piece_rows = piece_at(first)
        place = jnp.stack([block_of(step), block_of(0), own_index]).astype(jnp.int32)
        return pl.pallas_call(
            partial_kernel,
            grid_spec=pltpu.PrefetchScalarGridSpec(
                num_scalar_prefetch=1,
                grid=(count,),
                in_specs=operand_specs(first, piece_first) + weight_specs(0),
                out_specs=pl.BlockSpec((TILE, columns), lambda i, *_: (i, 0)),
            ),
            out_shape=jax.ShapeDtypeStruct((count * TILE, columns), jnp.bfloat16),
            compiler_params=params,
            cost_estimate=product_cost(count * TILE),
        )(place, tokens, piece_rows, near_gain, far_gain, kv_weight, far_weight[step])

    def finish(first, count, arrived, result):
        piece_first, piece_rows = piece_at(first)
        place = jnp.stack([block_of(1), block_of(0), own_index]).astype(jnp.int32)
        operands = [tokens, piece_rows, near_gain, far_gain, kv_weight, far_weight[0], squares, cosine, sine]
        specs = (
            operand_specs(first, piece_first)
            + weight_specs(1)
            + [pl.BlockSpec((chip_count, None, 1, TILE), lambda i, *_: (0, first + i, 0, 0))]
            + [pl.BlockSpec((TILE, HD), lambda i, *_: (first + i, 0))] * 2
            + [pl.BlockSpec((TILE, columns), lambda i, *_: (i, 0))] * len(arrived)
        )
        operands += arrived
        if result is None:
            result = jnp.zeros((8, LANES), jnp.bfloat16)
            aliases = {}
        else:
            aliases = {2 + len(operands): 0}
        return pl.pallas_call(
            functools.partial(finish_kernel, first, model_dim),
            grid_spec=pltpu.PrefetchScalarGridSpec(
                num_scalar_prefetch=2,
                grid=(count,),
                in_specs=specs + [pl.BlockSpec(memory_space=pl.ANY)],
                out_specs=pl.BlockSpec((TILE, columns), lambda i, *_: (first + i, 0)),
            ),
            out_shape=jax.ShapeDtypeStruct((slot_rows, columns), jnp.bfloat16),
            input_output_aliases=aliases,
            compiler_params=params,
            cost_estimate=product_cost(count * TILE),
        )(place, live_blocks, *operands, result)

    arrivals = []
    first = 0
    for count in CHUNKS:
        arrived = []
        for step in range(1, chip_count):
            sent = make_partial(first, count, step)
            arrived.append(lax.ppermute(sent, "tensor", shift(step)))
        arrivals.append((first, count, arrived))
        first += count

    result = None
    for first, count, arrived in arrivals:
        result = finish(first, count, arrived, result)
    return result


def solution(mesh):
    in_specs = (
        P(("groups", "serve"), "tensor"),
        P("tensor"),
        P("tensor", None),
        P("groups"),
        P("groups"),
    )
    out_specs = P(("groups", "serve"), "tensor")
    return jax.shard_map(shards, mesh=mesh, in_specs=in_specs, out_specs=out_specs, check_vma=False)
```

time: 219 us -> 88.9 us (0.41)
  waiting for transfers between devices: 129 us -> 11.3 us
  Pallas kernels: 0 us -> 48.5 us
  other arithmetic: 23.7 us -> 4.52 us
  local copies, waits for them, and re-layouts: 27.4 us -> 12 us
  between operations: 14.2 us -> 0.78 us
  matrix products: 6.97 us -> 0 us
  blocking collectives: 5.63 us -> 0 us
    all_to_all x2 -> x0, waiting for transfers between devices: 104 us -> none  [the longest x1 69.8 us: shards(): lax.all_to_all(outgoing, 'serve', split_axis=0, concat_axis=0, tiled=True)]
    pallas_call x0 -> x13, Pallas kernels: none -> 48.5 us  [the longest x6 22.8 us: finish(): pl.pallas_call(functools.partial(finish_kernel, first, model_dim), grid_s...]
    reduce_scatter x1 -> x0, waiting for transfers between devices: 25.3 us -> none  [rebuild_rows(): lax.psum_scatter(partial_sums.astype(jnp.bfloat16), 'tensor', scatter_dim...]
    gather x6 -> x0, local copies, waits for them, and re-layouts: 13.8 us -> none  [the longest x1 3.73 us: shards(): jnp.take(incoming.reshape(serve_count * capacity, BLOCK, feature_count),...]
    select_n x10 -> x0, other arithmetic: 12.7 us -> none  [the longest x2 3.91 us: shards(): jnp.take(blocked, send_index, axis=0)]
    ppermute x0 -> x13, waiting for transfers between devices: none -> 11.3 us  [the longest x1 11.3 us: shards(): lax.ppermute(pair_squares, 'tensor', shift(s))]
    all_to_all x2 -> x0, starting transfers between devices: 11.2 us -> none  [the longest x1 6.45 us: shards(): lax.all_to_all(outgoing, 'serve', split_axis=0, concat_axis=0, tiled=True)]
    ppermute x0 -> x13, starting transfers between devices: none -> 10.9 us  [the longest x6 9.29 us: shards(): arrived.append(lax.ppermute(sent, 'tensor', shift(step)))]
  transfers between devices with their start and end apart: 3 -> 13, of which waited for: 3 -> 1; matrix products, arithmetic and copies ran while one was open for 4% -> 12% of each run, Pallas kernels for 0% -> 52%
where the time goes in v1:
time: 88.9 us; the launch traced here: 88.1 us
  Pallas kernels  48.5 us (55%)
  local copies, waits for them, and re-layouts  12 us (13%)
  waiting for transfers between devices  11.3 us (13%)
  starting transfers between devices  10.9 us (12%)
  other arithmetic  4.52 us (5%)
    pallas_call x6, Pallas kernels, finish(): pl.pallas_call(functools.partial(finish_kernel, first, model_dim), grid_s...  22.8 us
    pallas_call x6, Pallas kernels, make_partial(): pl.pallas_call(partial_kernel, grid_spec=pltpu.PrefetchScalarGridSpec(num...  17.8 us
    ppermute x1, waiting for transfers between devices, shards(): lax.ppermute(pair_squares, 'tensor', shift(s))  11.3 us
    ppermute x6, starting transfers between devices, shards(): arrived.append(lax.ppermute(sent, 'tensor', shift(step)))  9.29 us
    pallas_call x1, Pallas kernels, shards(): pl.pallas_call(squares_kernel, grid=(tiles,), in_specs=[pl.BlockSpec((TIL...  7.92 us
    slice x2, local copies, waits for them, and re-layouts, shards(): sent = tokens[tile_at * TILE:(tile_at + piece) * TILE]  5.42 us
    dynamic_slice x1, local copies, waits for them, and re-layouts, shards(): lax.dynamic_slice_in_dim(kv_weight, (block_of(step) ^ 1) * columns, colum...  3.01 us
    unnamed x17, local copies, waits for them, and re-layouts  2.91 us
  transfers between devices with their start and end apart: 13, of which 1 were waited for; matrix products, arithmetic and copies ran while one was open for 12% of the time, Pallas kernels for 52%

profile of v1, /device:TPU:0, one launch (start us, length us, event | category | flops | bytes accessed | tf_op | source)
XLA Modules:
  0.0 88.1 jit_solution(3597900368356304671)
XLA Ops:
  0.0 3.3 %slice.6 = bf16[1152,1024]{1,0:T(8,128)(2,1)} slice(bf16[1536,1024]{1,0:T(8,128)(2,1)} %refs_0_.11), slice={[384:1536], [0:1024]} | slice | bytes 4718592 | tf_op jit(solution)/shard_map/slice | solution.py:97
  3.3 0.5 collective-permute-start
  3.8 0.1 collective-permute-start.1
  3.8 2.1 %slice.7 = bf16[384,1024]{1,0:T(8,128)(2,1)} slice(bf16[1536,1024]{1,0:T(8,128)(2,1)} %refs_0_.11), slice={[0:384], [0:1024]} | slice | bytes 1572864 | tf_op jit(solution)/shard_map/slice | solution.py:97
  5.9 0.5 collective-permute-start.10
  6.4 3.0 %constant_dynamic-slice_fusion = (bf16[1024,512]{1,0:T(8,128)(2,1)}, bf16[1024,512]{1,0:T(8,128)(2,1)}) fusion(bf16[1024,2048]{1,0:T(8,128)(2,1)} %refs_4_.11, s32[]{:T(128)S(6)} %select_n.72, s32[]{:T(128)S(6)} %select_n.70), kind=kLoop, calls=%fused_computation.11 | loop fusion | bytes 4194312 | tf_op jit(solution)/shard_map/dynamic_slice | solution.py:93
  9.4 0.1 collective-permute-start.5
  9.5 0.5 collective-permute-start.2
  9.9 0.6 dynamic_slice.10
  11.1 2.8 %fusion = (f32[1536,64]{1,0:T(8,128)S(1)}, f32[1536,64]{1,0:T(8,128)S(1)}, f32[1536,64]{1,0:T(8,128)S(1)}) fusion(f32[64]{0:T(128)S(1)} %multiply_power_fusion, f32[1536]{0:T(1024)S(1)} %add_convert_fusion), kind=kLoop, calls=%fused_computation.4 | loop fusion | flops 196608 | bytes 1186048 | tf_op jit(solution)/shard_map/neg | solution.py:123
  13.9 1.6 %pad_maximum_fusion = (f32[1536,128]{1,0:T(8,128)}, f32[1536,128]{1,0:T(8,128)}) fusion(f32[1536,64]{1,0:T(8,128)S(1)} %get-tuple-element.9, f32[1536,64]{1,0:T(8,128)S(1)} %get-tuple-element.8, f32[1536,64]{1,0:T(8,128)S(1)} %get-tuple-element.7), kind=kLoop, calls=%fused_computation.2 | loop fusion | flops 393216 | bytes 2752512 | tf_op jit(solution)/shard_map/concatenate | solution.py:122
  15.5 0.1 pad_add_fusion.place
  15.6 7.9 %shard_map.55 = f32[12,1,128]{2,1,0:T(1,128)} custom-call(bf16[1536,1024]{1,0:T(8,128)(2,1)} %refs_0_.11), custom_call_target="tpu_custom_call" | custom-call | tf_op jit(solution)/shard_map/pallas_call | solution.py:104
  23.5 0.7 copy.24
  24.2 0.0 collective-permute-done.1
  24.2 0.1 collective-permute-start.3
  24.3 0.0 collective-permute-done.10.far.refs_1_
  24.3 0.0 collective-permute-done.5.far_weight
  24.3 0.0 copy-start
  24.3 2.2 %copy-done = bf16[1024,2048]{1,0:T(8,128)(2,1)S(1)} copy-done((bf16[1024,2048]{1,0:T(8,128)(2,1)S(1)}, bf16[1024,2048]{1,0:T(8,128)(2,1)}, u32[]{:S(2)}) %copy-start) | copy-done | bytes 4194328
  26.5 2.8 %shard_map.60 = bf16[256,512]{1,0:T(8,128)(2,1)S(1)} custom-call(s32[3]{0:T(128)S(1)} %pad_add_fusion.place, bf16[1536,1024]{1,0:T(8,128)(2,1)S(1)} %copy-done.1, bf16[384,1024]{1,0:T(8,128)(2,1)} %collective-permute-done.10.far.refs_1_, bf16[1,1024]{1,0:T(2,128)(2,1)S(1)} %reshape.26.near_gain.refs_2_, bf16[1,1024]{1,0:T(2,128)(2,1)S(1)} %reshape.27.far_gain.refs_3_, ...), custom_call_target="tpu_custom_call" | custom-call | flops 536870912 | bytes 3407872 | tf_op jit(solution)/shard_map/pallas_call | solution.py:155
  29.4 3.0 %collective-permute-start.11 = (bf16[256,512]{1,0:T(8,128)(2,1)S(1)}, bf16[256,512]{1,0:T(8,128)(2,1)S(1)}, u32[]{:S(2)}, u32[]{:S(2)}) collective-permute-start(bf16[256,512]{1,0:T(8,128)(2,1)S(1)} %shard_map.60), channel_id=1, source_target_pairs={{0,2},{1,3},{2,0},{3,1},{4,6},{5,7},{6,4},{7,5},{8,10},{9,11},{10,... | collective-permute-start | bytes 786440 | tf_op jit(solution)/shard_map/ppermute | solution.py:205
  32.4 0.0 collective-permute-done.far.refs_1_
  32.4 3.8 %shard_map.58 = bf16[384,512]{1,0:T(8,128)(2,1)S(1)} custom-call(s32[3]{0:T(128)S(1)} %pad_add_fusion.place, bf16[1536,1024]{1,0:T(8,128)(2,1)S(1)} %copy-done.1, bf16[1152,1024]{1,0:T(8,128)(2,1)} %collective-permute-done.far.refs_1_, bf16[1,1024]{1,0:T(2,128)(2,1)S(1)} %reshape.26.near_gain.refs_2_, bf16[1,1024]{1,0:T(2,128)(2,1)S(1)} %reshape.27.far_gain.refs_3_, ...), custom_call_target="tpu_custom_call" | custom-call | flops 805306368 | bytes 4063232 | tf_op jit(solution)/shard_map/pallas_call | solution.py:155
  36.2 0.1 collective-permute-start.8
  36.3 3.8 %shard_map.59 = bf16[384,512]{1,0:T(8,128)(2,1)S(1)} custom-call(s32[3]{0:T(128)S(1)} %pad_add_fusion.place, bf16[1536,1024]{1,0:T(8,128)(2,1)S(1)} %copy-done.1, bf16[1152,1024]{1,0:T(8,128)(2,1)} %collective-permute-done.far.refs_1_, bf16[1,1024]{1,0:T(2,128)(2,1)S(1)} %reshape.26.near_gain.refs_2_, bf16[1,1024]{1,0:T(2,128)(2,1)S(1)} %reshape.27.far_gain.refs_3_, ...), custom_call_target="tpu_custom_call" | custom-call | flops 805306368 | bytes 4063232 | tf_op jit(solution)/shard_map/pallas_call | solution.py:155
  40.1 2.1 %collective-permute-start.9 = (bf16[384,512]{1,0:T(8,128)(2,1)S(1)}, bf16[384,512]{1,0:T(8,128)(2,1)S(1)}, u32[]{:S(2)}, u32[]{:S(2)}) collective-permute-start(bf16[384,512]{1,0:T(8,128)(2,1)S(1)} %shard_map.59), channel_id=1, source_target_pairs={{0,2},{1,3},{2,0},{3,1},{4,6},{5,7},{6,4},{7,5},{8,10},{9,11},{10,... | collective-permute-start | bytes 1179656 | tf_op jit(solution)/shard_map/ppermute | solution.py:205
  42.1 0.0 collective-permute-done.3
  42.1 0.1 collective-permute-start.4
  42.2 2.3 %shard_map.61 = bf16[128,512]{1,0:T(8,128)(2,1)S(1)} custom-call(s32[3]{0:T(128)S(1)} %pad_add_fusion.place, bf16[1536,1024]{1,0:T(8,128)(2,1)S(1)} %copy-done.1, bf16[384,1024]{1,0:T(8,128)(2,1)} %collective-permute-done.10.far.refs_1_, bf16[1,1024]{1,0:T(2,128)(2,1)S(1)} %reshape.26.near_gain.refs_2_, bf16[1,1024]{1,0:T(2,128)(2,1)S(1)} %reshape.27.far_gain.refs_3_, ...), custom_call_target="tpu_custom_call" | custom-call | flops 268435456 | bytes 2752512 | tf_op jit(solution)/shard_map/pallas_call | solution.py:155
  44.6 0.0 copy-start.4
  44.6 11.3 %collective-permute-done.4 = f32[12,128]{1,0:T(8,128)S(1)} collective-permute-done((f32[12,128]{1,0:T(8,128)S(1)}, f32[12,128]{1,0:T(8,128)S(1)}, u32[]{:S(2)}, u32[]{:S(2)}) %collective-permute-start.4) | collective-permute-done | bytes 6176 | tf_op jit(solution)/shard_map/ppermute | solution.py:114
  55.9 1.7 %collective-permute-start.12 = (bf16[128,512]{1,0:T(8,128)(2,1)S(1)}, bf16[128,512]{1,0:T(8,128)(2,1)S(1)}, u32[]{:S(2)}, u32[]{:S(2)}) collective-permute-start(bf16[128,512]{1,0:T(8,128)(2,1)S(1)} %shard_map.61), channel_id=1, source_target_pairs={{0,2},{1,3},{2,0},{3,1},{4,6},{5,7},{6,4},{7,5},{8,10},{9,11},{10,... | collective-permute-start | bytes 393224 | tf_op jit(solution)/shard_map/ppermute | solution.py:205
  57.6 2.8 %shard_map.57 = bf16[256,512]{1,0:T(8,128)(2,1)S(1)} custom-call(s32[3]{0:T(128)S(1)} %pad_add_fusion.place, bf16[1536,1024]{1,0:T(8,128)(2,1)S(1)} %copy-done.1, bf16[1152,1024]{1,0:T(8,128)(2,1)} %collective-permute-done.far.refs_1_, bf16[1,1024]{1,0:T(2,128)(2,1)S(1)} %reshape.26.near_gain.refs_2_, bf16[1,1024]{1,0:T(2,128)(2,1)S(1)} %reshape.27.far_gain.refs_3_, ...), custom_call_target="tpu_custom_call" | custom-call | flops 536870912 | bytes 3407872 | tf_op jit(solution)/shard_map/pallas_call | solution.py:155
  60.5 0.0 collective-permute-done.2.refs_5_
  60.5 0.3 collective-permute-start.7
  60.9 0.0 collective-permute-done.12.refs_9_
  60.9 3.1 %shard_map.62.refs_10_ = bf16[1536,512]{1,0:T(8,128)(2,1)} custom-call(s32[3]{0:T(128)S(1)} %pad_add_fusion.place, s32[4]{0:T(128)S(1)} %copy-done.4, bf16[1536,1024]{1,0:T(8,128)(2,1)S(1)} %copy-done.1, bf16[384,1024]{1,0:T(8,128)(2,1)} %collective-permute-done.10.far.refs_1_, bf16[1,1024]{1,0:T(2,128)(2,1)S(1)} %reshape.26.near_gain.refs_2_, ...), custom_call_target="tpu_custom_call" | custom-call | flops 268435456 | bytes 2752512 | tf_op jit(solution)/shard_map/pallas_call | solution.py:185
  64.0 3.7 %shard_map.63.refs_10_ = bf16[1536,512]{1,0:T(8,128)(2,1)} custom-call(s32[3]{0:T(128)S(1)} %pad_add_fusion.place, s32[4]{0:T(128)S(1)} %copy-done.4, bf16[1536,1024]{1,0:T(8,128)(2,1)S(1)} %copy-done.1, bf16[384,1024]{1,0:T(8,128)(2,1)} %collective-permute-done.10.far.refs_1_, ...), custom_call_target="tpu_custom_call", output_to_operand_aliasing={{}: (12, {})} | custom-call | flops 536870912 | bytes 3407872 | tf_op jit(solution)/shard_map/pallas_call | solution.py:185
  67.7 2.3 %shard_map.56 = bf16[128,512]{1,0:T(8,128)(2,1)S(1)} custom-call(s32[3]{0:T(128)S(1)} %pad_add_fusion.place, bf16[1536,1024]{1,0:T(8,128)(2,1)S(1)} %copy-done.1, bf16[1152,1024]{1,0:T(8,128)(2,1)} %collective-permute-done.far.refs_1_, bf16[1,1024]{1,0:T(2,128)(2,1)S(1)} %reshape.26.near_gain.refs_2_, bf16[1,1024]{1,0:T(2,128)(2,1)S(1)} %reshape.27.far_gain.refs_3_, ...), custom_call_target="tpu_custom_call" | custom-call | flops 268435456 | bytes 2752512 | tf_op jit(solution)/shard_map/pallas_call | solution.py:155
  70.0 2.0 %collective-permute-start.6 = (bf16[128,512]{1,0:T(8,128)(2,1)S(1)}, bf16[128,512]{1,0:T(8,128)(2,1)S(1)}, u32[]{:S(2)}, u32[]{:S(2)}) collective-permute-start(bf16[128,512]{1,0:T(8,128)(2,1)S(1)} %shard_map.56), channel_id=1, source_target_pairs={{0,2},{1,3},{2,0},{3,1},{4,6},{5,7},{6,4},{7,5},{8,10},{9,11},{10,... | collective-permute-start | bytes 393224 | tf_op jit(solution)/shard_map/ppermute | solution.py:205
  72.0 0.0 collective-permute-done.9.refs_9_
  72.0 4.7 %shard_map.64.refs_10_ = bf16[1536,512]{1,0:T(8,128)(2,1)} custom-call(s32[3]{0:T(128)S(1)} %pad_add_fusion.place, s32[4]{0:T(128)S(1)} %copy-done.4, bf16[1536,1024]{1,0:T(8,128)(2,1)S(1)} %copy-done.1, bf16[1152,1024]{1,0:T(8,128)(2,1)} %collective-permute-done.far.refs_1_, ...), custom_call_target="tpu_custom_call", output_to_operand_aliasing={{}: (12, {})} | custom-call | flops 805306368 | bytes 4063232 | tf_op jit(solution)/shard_map/pallas_call | solution.py:185
  76.7 0.0 collective-permute-done.8.refs_9_
  76.7 4.7 %shard_map.65.refs_10_ = bf16[1536,512]{1,0:T(8,128)(2,1)} custom-call(s32[3]{0:T(128)S(1)} %pad_add_fusion.place, s32[4]{0:T(128)S(1)} %copy-done.4, bf16[1536,1024]{1,0:T(8,128)(2,1)S(1)} %copy-done.1, bf16[1152,1024]{1,0:T(8,128)(2,1)} %collective-permute-done.far.refs_1_, ...), custom_call_target="tpu_custom_call", output_to_operand_aliasing={{}: (12, {})} | custom-call | flops 805306368 | bytes 4063232 | tf_op jit(solution)/shard_map/pallas_call | solution.py:185
  81.3 3.7 %shard_map.66.refs_10_ = bf16[1536,512]{1,0:T(8,128)(2,1)} custom-call(s32[3]{0:T(128)S(1)} %pad_add_fusion.place, s32[4]{0:T(128)S(1)} %copy-done.4, bf16[1536,1024]{1,0:T(8,128)(2,1)S(1)} %copy-done.1, bf16[1152,1024]{1,0:T(8,128)(2,1)} %collective-permute-done.far.refs_1_, ...), custom_call_target="tpu_custom_call", output_to_operand_aliasing={{}: (12, {})} | custom-call | flops 536870912 | bytes 3407872 | tf_op jit(solution)/shard_map/pallas_call | solution.py:185
  85.0 0.0 collective-permute-done.6.refs_9_
  85.0 3.1 %shard_map.67 = bf16[1536,512]{1,0:T(8,128)(2,1)} custom-call(s32[3]{0:T(128)S(1)} %pad_add_fusion.place, s32[4]{0:T(128)S(1)} %copy-done.4, bf16[1536,1024]{1,0:T(8,128)(2,1)S(1)} %copy-done.1, bf16[1152,1024]{1,0:T(8,128)(2,1)} %collective-permute-done.far.refs_1_, bf16[1,1024]{1,0:T(2,128)(2,1)S(1)} %reshape.26.near_gain.refs_2_, ...), custom_call_target="tpu_custom_call", output_to_operand_aliasing={{}: (12, {})} | custom-call | flops 268435456 | bytes 2752512 | tf_op jit(solution)/shard_map/pallas_call | solution.py:185
  (23 shorter events, 0.1 us)
Async XLA Ops:
  0.0 3.8 %copy-start.6 = (bf16[1024]{0:T(1024)(128)(2,1)S(1)}, bf16[1024]{0:T(1024)(128)(2,1)}, u32[]{:S(2)}) copy-start(bf16[1024]{0:T(1024)(128)(2,1)} %param.6) | copy-start | bytes 6148
  3.3 29.1 %collective-permute-start = (bf16[1152,1024]{1,0:T(8,128)(2,1)}, bf16[1152,1024]{1,0:T(8,128)(2,1)}, u32[]{:S(2)}, u32[]{:S(2)}) collective-permute-start(bf16[1152,1024]{1,0:T(8,128)(2,1)} %slice.6), channel_id=1, source_target_pairs={{0,1},{1,0},{2,3},{3,2},{4,5},{5,4},{6,7},{7,6},{8,9},{9,8},{10,11... | collective-permute-start | bytes 7077896 | tf_op jit(solution)/shard_map/ppermute | solution.py:98
  3.8 20.5 %collective-permute-start.1 = (bf16[1024]{0:T(1024)(128)(2,1)S(1)}, bf16[1024]{0:T(1024)(128)(2,1)S(1)}, u32[]{:S(2)}, u32[]{:S(2)}) collective-permute-start(bf16[1024]{0:T(1024)(128)(2,1)S(1)} %copy-done.6), channel_id=1, source_target_pairs={{0,1},{1,0},{2,3},{3,2},{4,5},{5,4},{6,7},{7,6},{8,9},{9,8},{10,11... | collective-permute-start | bytes 6152 | tf_op jit(solution)/shard_map/ppermute | solution.py:89
  5.9 18.4 %collective-permute-start.10 = (bf16[384,1024]{1,0:T(8,128)(2,1)}, bf16[384,1024]{1,0:T(8,128)(2,1)}, u32[]{:S(2)}, u32[]{:S(2)}) collective-permute-start(bf16[384,1024]{1,0:T(8,128)(2,1)} %slice.7), channel_id=1, source_target_pairs={{0,1},{1,0},{2,3},{3,2},{4,5},{5,4},{6,7},{7,6},{8,9},{9,8},{10,11... | collective-permute-start | bytes 2359304 | tf_op jit(solution)/shard_map/ppermute | solution.py:98
  6.4 3.5 %copy-start.7 = (s32[4]{0:T(128)S(1)}, s32[4]{0:T(128)}, u32[]{:S(2)}) copy-start(s32[4]{0:T(128)} %param.9) | copy-start | bytes 52
  9.4 14.9 %collective-permute-start.5 = (bf16[1024,512]{1,0:T(8,128)(2,1)}, bf16[1024,512]{1,0:T(8,128)(2,1)}, u32[]{:S(2)}, u32[]{:S(2)}) collective-permute-start(bf16[1024,512]{1,0:T(8,128)(2,1)} %get-tuple-element.5), channel_id=1, source_target_pairs={{0,1},{1,0},{2,3},{3,2},{4,5},{5,4},{6,7},{7,6},{8,9},{9,8},{10,11... | collective-permute-start | bytes 3145736 | tf_op jit(solution)/shard_map/ppermute | solution.py:94
  9.5 51.0 %collective-permute-start.2 = (bf16[1024,512]{1,0:T(8,128)(2,1)}, bf16[1024,512]{1,0:T(8,128)(2,1)}, u32[]{:S(2)}, u32[]{:S(2)}) collective-permute-start(bf16[1024,512]{1,0:T(8,128)(2,1)} %get-tuple-element.6), channel_id=1, source_target_pairs={{0,1},{1,0},{2,3},{3,2},{4,5},{5,4},{6,7},{7,6},{8,9},{9,8},{10,11... | collective-permute-start | bytes 3145736 | tf_op jit(solution)/shard_map/ppermute | solution.py:94
  15.6 8.7 %copy-start.1 = (bf16[1536,1024]{1,0:T(8,128)(2,1)S(1)}, bf16[1536,1024]{1,0:T(8,128)(2,1)}, u32[]{:S(2)}) copy-start(bf16[1536,1024]{1,0:T(8,128)(2,1)} %refs_0_.11) | copy-start | bytes 9437188
  24.2 17.9 %collective-permute-start.3 = (f32[12,128]{1,0:T(8,128)S(1)}, f32[12,128]{1,0:T(8,128)S(1)}, u32[]{:S(2)}, u32[]{:S(2)}) collective-permute-start(f32[12,128]{1,0:T(8,128)S(1)} %bitcast.14), channel_id=1, source_target_pairs={{0,1},{1,0},{2,3},{3,2},{4,5},{5,4},{6,7},{7,6},{8,9},{9,8},{10,11... | collective-permute-start | bytes 18440 | tf_op jit(solution)/shard_map/ppermute | solution.py:112
  24.3 2.2 %copy-start = (bf16[1024,2048]{1,0:T(8,128)(2,1)S(1)}, bf16[1024,2048]{1,0:T(8,128)(2,1)}, u32[]{:S(2)}) copy-start(bf16[1024,2048]{1,0:T(8,128)(2,1)} %refs_4_.11) | copy-start | bytes 12582916
  29.4 34.6 %collective-permute-start.11 = (bf16[256,512]{1,0:T(8,128)(2,1)S(1)}, bf16[256,512]{1,0:T(8,128)(2,1)S(1)}, u32[]{:S(2)}, u32[]{:S(2)}) collective-permute-start(bf16[256,512]{1,0:T(8,128)(2,1)S(1)} %shard_map.60), channel_id=1, source_target_pairs={{0,2},{1,3},{2,0},{3,1},{4,6},{5,7},{6,4},{7,5},{8,10},{9,11},{10,... | collective-permute-start | bytes 786440 | tf_op jit(solution)/shard_map/ppermute | solution.py:205
  36.2 6.0 %copy-start.5 = (f32[12,1,128]{2,1,0:T(1,128)S(1)}, f32[12,1,128]{2,1,0:T(1,128)}, u32[]{:S(2)}) copy-start(f32[12,1,128]{2,1,0:T(1,128)} %shard_map.55) | copy-start | bytes 18436
  36.2 40.5 %collective-permute-start.8 = (bf16[384,512]{1,0:T(8,128)(2,1)S(1)}, bf16[384,512]{1,0:T(8,128)(2,1)S(1)}, u32[]{:S(2)}, u32[]{:S(2)}) collective-permute-start(bf16[384,512]{1,0:T(8,128)(2,1)S(1)} %shard_map.58), channel_id=1, source_target_pairs={{0,2},{1,3},{2,0},{3,1},{4,6},{5,7},{6,4},{7,5},{8,10},{9,11},{10,... | collective-permute-start | bytes 1179656 | tf_op jit(solution)/shard_map/ppermute | solution.py:205
  40.1 31.9 %collective-permute-start.9 = (bf16[384,512]{1,0:T(8,128)(2,1)S(1)}, bf16[384,512]{1,0:T(8,128)(2,1)S(1)}, u32[]{:S(2)}, u32[]{:S(2)}) collective-permute-start(bf16[384,512]{1,0:T(8,128)(2,1)S(1)} %shard_map.59), channel_id=1, source_target_pairs={{0,2},{1,3},{2,0},{3,1},{4,6},{5,7},{6,4},{7,5},{8,10},{9,11},{10,... | collective-permute-start | bytes 1179656 | tf_op jit(solution)/shard_map/ppermute | solution.py:205
  42.1 13.8 %collective-permute-start.4 = (f32[12,128]{1,0:T(8,128)S(1)}, f32[12,128]{1,0:T(8,128)S(1)}, u32[]{:S(2)}, u32[]{:S(2)}) collective-permute-start(f32[12,128]{1,0:T(8,128)S(1)} %fusion.1), channel_id=1, source_target_pairs={{0,2},{1,3},{2,0},{3,1},{4,6},{5,7},{6,4},{7,5},{8,10},{9,11},{10,... | collective-permute-start | bytes 18440 | tf_op jit(solution)/shard_map/ppermute | solution.py:114
  44.5 16.3 %copy-start.2 = (f32[1536,128]{1,0:T(8,128)S(1)}, f32[1536,128]{1,0:T(8,128)}, u32[]{:S(2)}) copy-start(f32[1536,128]{1,0:T(8,128)} %get-tuple-element.10.refs_7_) | copy-start | bytes 2359300
  44.6 16.3 %copy-start.3 = (f32[1536,128]{1,0:T(8,128)S(1)}, f32[1536,128]{1,0:T(8,128)}, u32[]{:S(2)}) copy-start(f32[1536,128]{1,0:T(8,128)} %get-tuple-element.11.refs_8_) | copy-start | bytes 2359300
  44.6 16.3 %copy-start.4 = (s32[4]{0:T(128)S(1)}, s32[4]{0:T(128)}, u32[]{:S(2)}) copy-start(s32[4]{0:T(128)} %live.11) | copy-start | bytes 52
  55.9 5.0 %collective-permute-start.12 = (bf16[128,512]{1,0:T(8,128)(2,1)S(1)}, bf16[128,512]{1,0:T(8,128)(2,1)S(1)}, u32[]{:S(2)}, u32[]{:S(2)}) collective-permute-start(bf16[128,512]{1,0:T(8,128)(2,1)S(1)} %shard_map.61), channel_id=1, source_target_pairs={{0,2},{1,3},{2,0},{3,1},{4,6},{5,7},{6,4},{7,5},{8,10},{9,11},{10,... | collective-permute-start | bytes 393224 | tf_op jit(solution)/shard_map/ppermute | solution.py:205
  60.5 20.8 %collective-permute-start.7 = (bf16[256,512]{1,0:T(8,128)(2,1)S(1)}, bf16[256,512]{1,0:T(8,128)(2,1)S(1)}, u32[]{:S(2)}, u32[]{:S(2)}) collective-permute-start(bf16[256,512]{1,0:T(8,128)(2,1)S(1)} %shard_map.57), channel_id=1, source_target_pairs={{0,2},{1,3},{2,0},{3,1},{4,6},{5,7},{6,4},{7,5},{8,10},{9,11},{10,... | collective-permute-start | bytes 786440 | tf_op jit(solution)/shard_map/ppermute | solution.py:205
  70.0 15.1 %collective-permute-start.6 = (bf16[128,512]{1,0:T(8,128)(2,1)S(1)}, bf16[128,512]{1,0:T(8,128)(2,1)S(1)}, u32[]{:S(2)}, u32[]{:S(2)}) collective-permute-start(bf16[128,512]{1,0:T(8,128)(2,1)S(1)} %shard_map.56), channel_id=1, source_target_pairs={{0,2},{1,3},{2,0},{3,1},{4,6},{5,7},{6,4},{7,5},{8,10},{9,11},{10,... | collective-permute-start | bytes 393224 | tf_op jit(solution)/shard_map/ppermute | solution.py:205

commit v2 on v1

v2 whole, which is shorter than its diff:
```python
import functools

import jax
import jax.numpy as jnp
from jax import lax
from jax.experimental import pallas as pl
from jax.experimental.pallas import tpu as pltpu
from jax.sharding import PartitionSpec as P

HD = 128
PAGE = 256
BLOCK = 64
LANES = 128

rope_base = 500000.0
norm_eps = 1e-05

TILE = 256
CHUNKS = (1, 2, 2, 1)

PARAMS = pltpu.CompilerParams(vmem_limit_bytes=24 * 1024 * 1024)


def square_sums(rows):
    total = jnp.zeros((rows.shape[0], LANES), jnp.float32)
    for part in range(rows.shape[1] // LANES):
        wide = rows[:, part * LANES : (part + 1) * LANES].astype(jnp.float32)
        total += wide * wide
    return total


def product_kernel(with_squares, place, rows_ref, gain_ref, keep_weight, send_weight, keep, send, *squares):
    scaled = rows_ref[...] * gain_ref[...]
    send[...] = jnp.dot(scaled, send_weight[...], preferred_element_type=jnp.float32).astype(send.dtype)
    keep[...] = jnp.dot(scaled, keep_weight[...], preferred_element_type=jnp.float32).astype(keep.dtype)
    if with_squares:
        total = square_sums(rows_ref[...])
        for part in range(TILE // LANES):
            turned = jnp.transpose(total[part * LANES : (part + 1) * LANES])
            squares[0][part] = jnp.sum(turned, axis=0, keepdims=True)


def finish_kernel(first_tile, model_dim, place, live, *refs):
    keep, received, squares, far_cos, far_sin, near_cos, near_sin = refs[:7]
    arrived, out = refs[7:-2], refs[-1]
    values = keep[...].astype(jnp.float32) + received[...].astype(jnp.float32)
    for part in arrived:
        values += part[...].astype(jnp.float32)
    on_diagonal = lax.broadcasted_iota(jnp.int32, (LANES, LANES), 0) == lax.broadcasted_iota(
        jnp.int32, (LANES, LANES), 1
    )
    square_rows = jnp.sum(squares[...], axis=0)
    totals = jnp.concatenate(
        [
            jnp.sum(jnp.where(on_diagonal, square_rows[part], 0.0), axis=1, keepdims=True)
            for part in range(TILE // LANES)
        ],
        axis=0,
    )
    scales = 1.0 / jnp.sqrt(totals / model_dim + norm_eps)
    tile = first_tile + pl.program_id(0)
    row = tile * TILE + lax.broadcasted_iota(jnp.int32, (TILE, 1), 0)
    alive = row < live[place[2]] * BLOCK
    sign = jnp.where(lax.broadcasted_iota(jnp.int32, (1, HD), 1) < HD // 2, -1.0, 1.0)
    cosines, sines = [], []
    for part in range(TILE // BLOCK):
        block_cos = far_cos[part]
        block_sin = far_sin[part]
        cosines.append(block_cos * near_cos[...] - block_sin * near_sin[...])
        sines.append((sign * block_sin) * near_cos[...] + (sign * block_cos) * near_sin[...])
    cosine = jnp.concatenate(cosines, axis=0)
    sine = jnp.concatenate(sines, axis=0)
    for start in range(0, out.shape[1], 2 * HD):
        key = values[:, start : start + HD] * scales
        turned = key * cosine + pltpu.roll(key, HD // 2, 1) * sine
        out[:, start : start + HD] = jnp.where(alive, turned, 0.0).astype(out.dtype)
        value = values[:, start + HD : start + 2 * HD] * scales
        out[:, start + HD : start + 2 * HD] = jnp.where(alive, value, 0.0).astype(out.dtype)


def shards(tokens, norm_gain, kv_weight, live_blocks, span_offset):
    tensor_count = lax.axis_size("tensor")
    chip_count = tensor_count // 2
    me = lax.axis_index("tensor")
    own_index = lax.axis_index("serve")
    slot_rows, depth = tokens.shape
    columns = kv_weight.shape[1] // tensor_count
    tiles = slot_rows // TILE
    model_dim = depth * tensor_count
    gain = norm_gain.reshape(1, depth)

    swap = [(i, i ^ 1) for i in range(tensor_count)]

    def shift(step):
        return [(i, (i + 2 * step) % tensor_count) for i in range(tensor_count)]

    def place_of(step):
        keep = (me + 2 * step) % tensor_count
        return jnp.stack([keep, keep ^ 1, own_index]).astype(jnp.int32)

    def product(place, first, count, with_squares):
        rows = count * TILE
        groups = TILE // LANES
        out_shape = [jax.ShapeDtypeStruct((rows, columns), jnp.bfloat16)] * 2
        out_specs = [pl.BlockSpec((TILE, columns), lambda i, *_: (i, 0))] * 2
        if with_squares:
            out_shape.append(jax.ShapeDtypeStruct((rows // LANES, 1, LANES), jnp.float32))
            out_specs.append(pl.BlockSpec((groups, 1, LANES), lambda i, *_: (i, 0, 0)))
        return pl.pallas_call(
            functools.partial(product_kernel, with_squares),
            grid_spec=pltpu.PrefetchScalarGridSpec(
                num_scalar_prefetch=1,
                grid=(count,),
                in_specs=[
                    pl.BlockSpec((TILE, depth), lambda i, *_: (first + i, 0)),
                    pl.BlockSpec((1, depth), lambda i, *_: (0, 0)),
                    pl.BlockSpec((depth, columns), lambda i, where: (0, where[0])),
                    pl.BlockSpec((depth, columns), lambda i, where: (0, where[1])),
                ],
                out_specs=out_specs,
            ),
            out_shape=out_shape,
            compiler_params=PARAMS,
            cost_estimate=pl.CostEstimate(
                flops=4 * rows * depth * columns,
                bytes_accessed=2 * rows * depth + 4 * depth * columns + 4 * rows * columns,
                transcendentals=0,
            ),
        )(place, tokens, gain, kv_weight, kv_weight)

    def tables(offset):
        half = HD // 2
        inv_freq = rope_base ** (-(jnp.arange(half, dtype=jnp.float32) * 2.0) / HD)
        inv_freq = jnp.concatenate([inv_freq, inv_freq])
        starts = offset * PAGE + BLOCK * jnp.arange(slot_rows // BLOCK, dtype=jnp.int32)
        far = starts.astype(jnp.float32)[:, None, None] * inv_freq
        near = jnp.arange(BLOCK, dtype=jnp.float32)[:, None] * inv_freq
        return [jnp.cos(far), jnp.sin(far), jnp.cos(near), jnp.sin(near)]

    def finish(first, count, keep, received, squares, table, arrived, result):
        blocks = TILE // BLOCK
        operands = [keep, received, squares] + table + arrived
        specs = (
            [pl.BlockSpec((TILE, columns), lambda i, *_: (first + i, 0))] * 2
            + [pl.BlockSpec((chip_count, TILE // LANES, 1, LANES), lambda i, *_: (0, first + i, 0, 0))]
            + [pl.BlockSpec((blocks, 1, HD), lambda i, *_: (first + i, 0, 0))] * 2
            + [pl.BlockSpec((BLOCK, HD), lambda i, *_: (0, 0))] * 2
            + [pl.BlockSpec((TILE, columns), lambda i, *_: (i, 0))] * len(arrived)
        )
        if result is None:
            result = keep
            aliases = {}
        else:
            aliases = {2 + len(operands): 0}
        return pl.pallas_call(
            functools.partial(finish_kernel, first, model_dim),
            grid_spec=pltpu.PrefetchScalarGridSpec(
                num_scalar_prefetch=2,
                grid=(count,),
                in_specs=specs + [pl.BlockSpec(memory_space=pl.ANY)],
                out_specs=pl.BlockSpec((TILE, columns), lambda i, *_: (first + i, 0)),
            ),
            out_shape=jax.ShapeDtypeStruct((slot_rows, columns), jnp.bfloat16),
            input_output_aliases=aliases,
            compiler_params=PARAMS,
            cost_estimate=pl.CostEstimate(
                flops=20 * count * TILE * columns, bytes_accessed=8 * count * TILE * columns, transcendentals=0
            ),
        )(place_of(0), live_blocks, *operands, result)

    others = range(1, chip_count)
    firsts = [sum(CHUNKS[:index]) for index in range(len(CHUNKS))]
    places = {step: place_of(step) for step in range(chip_count)}
    offset = span_offset[own_index]

    def start_chunk(index):
        made, sums = [], None
        for step in others:
            result = product(places[step], firsts[index], CHUNKS[index], step == 1)
            if step == 1:
                sums = result[2]
            made.append((result[0], lax.ppermute(result[1], "tensor", swap)))
        return made, sums

    def cross(made):
        sums = [
            (keep.astype(jnp.float32) + got.astype(jnp.float32)).astype(jnp.bfloat16) for keep, got in made
        ]
        sums, held = lax.optimization_barrier((sums, (places, offset)))
        return [lax.ppermute(part, "tensor", shift(step)) for step, part in zip(others, sums)], held

    chunk_count = len(CHUNKS)
    arrivals, square_parts = [], []
    pending = []
    for index in range(chunk_count):
        made, sums = start_chunk(index)
        square_parts.append(sums)
        pending.append(made)
        if len(pending) > 1:
            arrived, (places, offset) = cross(pending.pop(0))
            arrivals.append(arrived)
    keep, send = product(places[0], 0, tiles, False)
    received = lax.ppermute(send, "tensor", swap)
    arrived, (places, offset) = cross(pending.pop(0))
    arrivals.append(arrived)

    flat = jnp.concatenate(square_parts, axis=0).reshape(slot_rows // LANES, LANES)
    pair_squares = flat + lax.ppermute(flat, "tensor", swap)
    squares = jnp.stack(
        [pair_squares] + [lax.ppermute(pair_squares, "tensor", shift(step)) for step in others]
    ).reshape(chip_count, slot_rows // LANES, 1, LANES)
    table = tables(offset)

    result = None
    for first, count, arrived in zip(firsts, CHUNKS, arrivals):
        result = finish(first, count, keep, received, squares, table, arrived, result)
    return result


def solution(mesh):
    in_specs = (
        P(("groups", "serve"), "tensor"),
        P("tensor"),
        P("tensor", None),
        P("groups"),
        P("groups"),
    )
    out_specs = P(("groups", "serve"), "tensor")
    return jax.shard_map(shards, mesh=mesh, in_specs=in_specs, out_specs=out_specs, check_vma=False)
```

time: 88.9 us -> 72.3 us (0.81)
  Pallas kernels: 48.5 us -> 24.5 us
  waiting for transfers between devices: 11.3 us -> 22.6 us
  starting transfers between devices: 10.9 us -> 8.53 us
  local copies, waits for them, and re-layouts: 12 us -> 9.88 us
  other arithmetic: 4.52 us -> 5.51 us
    pallas_call x7 -> x5, Pallas kernels: 25.8 us -> 13.4 us  [product(): pl.pallas_call(functools.partial(product_kernel, with_squares), grid_spec...]
    pallas_call x6 -> x4, Pallas kernels: 22.8 us -> 11.1 us  [finish(): pl.pallas_call(functools.partial(finish_kernel, first, model_dim), grid_s...]
    ppermute x12 -> x10, waiting for transfers between devices: 11.3 us -> 21.2 us  [the longest x4 21.2 us: cross(): lax.ppermute(part, 'tensor', shift(step))]
    unnamed x17 -> x23, local copies, waits for them, and re-layouts: 2.91 us -> 8.51 us
    slice x2 -> x0, local copies, waits for them, and re-layouts: 5.42 us -> none  [shards(): sent = tokens[tile_at * TILE:(tile_at + piece) * TILE]]
    convert_element_type x1 -> x5, other arithmetic: 0.01 us -> 4.7 us  [the longest x4 4.7 us: cross(): (keep.astype(jnp.float32) + got.astype(jnp.float32)).astype(jnp.bfloat16)]
    dynamic_slice x2 -> x1, local copies, waits for them, and re-layouts: 3.6 us -> 0.66 us  [shards(): offset = span_offset[own_index]]
    ppermute x12 -> x10, starting transfers between devices: 10.9 us -> 8.02 us  [the longest x4 4.24 us: cross(): lax.ppermute(part, 'tensor', shift(step))]
  transfers between devices with their start and end apart: 13 -> 11, of which waited for: 1 -> 5; matrix products, arithmetic and copies ran while one was open for 12% -> 7% of each run, Pallas kernels for 52% -> 20%
where the time goes in v2:
time: 72.3 us; the launch traced here: 71.9 us
  Pallas kernels  24.5 us (34%)
  waiting for transfers between devices  22.6 us (31%)
  local copies, waits for them, and re-layouts  9.88 us (14%)
  starting transfers between devices  8.53 us (12%)
  other arithmetic  5.51 us (8%)
  between operations  0.8 us (1%)
    ppermute x4, waiting for transfers between devices, cross(): lax.ppermute(part, 'tensor', shift(step))  21.2 us
    pallas_call x5, Pallas kernels, product(): pl.pallas_call(functools.partial(product_kernel, with_squares), grid_spec...  13.4 us
    pallas_call x4, Pallas kernels, finish(): pl.pallas_call(functools.partial(finish_kernel, first, model_dim), grid_s...  11.1 us
    unnamed x23, local copies, waits for them, and re-layouts  8.51 us
    convert_element_type x4, other arithmetic, cross(): (keep.astype(jnp.float32) + got.astype(jnp.float32)).astype(jnp.bfloat16)  4.7 us
    ppermute x4, starting transfers between devices, cross(): lax.ppermute(part, 'tensor', shift(step))  4.24 us
    ppermute x1, starting transfers between devices, shards(): lax.ppermute(pair_squares, 'tensor', shift(step))  2.63 us
  transfers between devices with their start and end apart: 11, of which 5 were waited for; matrix products, arithmetic and copies ran while one was open for 7% of the time, Pallas kernels for 20%

profile of v2, /device:TPU:0, one launch (start us, length us, event | category | flops | bytes accessed | tf_op | source)
XLA Modules:
  0.0 71.9 jit_solution(11935400694160423694)
XLA Ops:
  0.0 0.7 reshape.104.gain_ref
  0.7 0.1 add_add_fusion.1.place
  0.8 2.2 %copy-done = bf16[1024,2048]{1,0:T(8,128)(2,1)S(1)} copy-done((bf16[1024,2048]{1,0:T(8,128)(2,1)S(1)}, bf16[1024,2048]{1,0:T(8,128)(2,1)}, u32[]{:S(2)}) %copy-start) | copy-done | bytes 4194328
  3.0 1.9 %copy-done.3 = bf16[1536,1024]{1,0:T(8,128)(2,1)S(1)} copy-done((bf16[1536,1024]{1,0:T(8,128)(2,1)S(1)}, bf16[1536,1024]{1,0:T(8,128)(2,1)}, u32[]{:S(2)}) %copy-start.3) | copy-done | bytes 3145752
  4.8 1.9 %shard_map.55 = (bf16[256,512]{1,0:T(8,128)(2,1)S(1)}, bf16[256,512]{1,0:T(8,128)(2,1)}, f32[2,1,128]{2,1,0:T(1,128)S(1)}) custom-call(s32[3]{0:T(128)S(1)} %add_add_fusion.1.place, bf16[1536,1024]{1,0:T(8,128)(2,1)S(1)} %copy-done.3, bf16[1,1024]{1,0:T(2,128)(2,1)S(1)} %reshape.104.gain_ref, bf16[1024,2048]{1,0:T(8,128)(2,1)S(1)} %copy-done, ...), custom_call_target="tpu_custom_call" | custom-call | flops 536870912 | bytes 3145728 | tf_op jit(solution)/shard_map/pallas_call | solution.py:109
  6.7 0.5 collective-permute-start
  7.2 2.6 %shard_map.57 = (bf16[512,512]{1,0:T(8,128)(2,1)S(1)}, bf16[512,512]{1,0:T(8,128)(2,1)}, f32[4,1,128]{2,1,0:T(1,128)S(1)}) custom-call(s32[3]{0:T(128)S(1)} %add_add_fusion.1.place, bf16[1536,1024]{1,0:T(8,128)(2,1)S(1)} %copy-done.3, bf16[1,1024]{1,0:T(2,128)(2,1)S(1)} %reshape.104.gain_ref, bf16[1024,2048]{1,0:T(8,128)(2,1)S(1)} %copy-done, ...), custom_call_target="tpu_custom_call" | custom-call | flops 1073741824 | bytes 4194304 | tf_op jit(solution)/shard_map/pallas_call | solution.py:109
  9.8 0.8 %copy-done.7 = bf16[512,512]{1,0:T(8,128)(2,1)} copy-done((bf16[512,512]{1,0:T(8,128)(2,1)}, bf16[512,512]{1,0:T(8,128)(2,1)S(1)}, u32[]{:S(2)}) %copy-start.7) | copy-done | bytes 524312
  10.6 0.1 collective-permute-start.2
  10.6 0.7 dynamic_slice.3
  11.3 0.1 add_add_fusion.place
  11.4 0.0 collective-permute-done
  11.4 1.7 %add_convert_fusion.3 = bf16[256,512]{1,0:T(8,128)(2,1)} fusion(bf16[256,512]{1,0:T(8,128)(2,1)} %collective-permute-done, bf16[256,512]{1,0:T(8,128)(2,1)S(1)} %get-tuple-element.32), kind=kLoop, calls=%fused_computation.3 | loop fusion | flops 524288 | bytes 786432 | tf_op jit(solution)/shard_map/convert_element_type | solution.py:187
  13.1 0.0 copy-done.4
  13.1 2.2 %copy-done.1 = bf16[1024,2048]{1,0:T(8,128)(2,1)S(1)} copy-done((bf16[1024,2048]{1,0:T(8,128)(2,1)S(1)}, bf16[1024,2048]{1,0:T(8,128)(2,1)}, u32[]{:S(2)}) %copy-start.1) | copy-done | bytes 4194328
  15.3 2.2 %shard_map.56 = (bf16[512,512]{1,0:T(8,128)(2,1)S(1)}, bf16[512,512]{1,0:T(8,128)(2,1)S(1)}, f32[4,1,128]{2,1,0:T(1,128)S(1)}) custom-call(s32[3]{0:T(128)S(1)} %add_add_fusion.1.place, bf16[1536,1024]{1,0:T(8,128)(2,1)S(1)} %copy-done.4, bf16[1,1024]{1,0:T(2,128)(2,1)S(1)} %reshape.104.gain_ref, bf16[1024,2048]{1,0:T(8,128)(2,1)S(1)} %copy-done.1, ...), custom_call_target="tpu_custom_call" | custom-call | flops 1073741824 | bytes 4194304 | tf_op jit(solution)/shard_map/pallas_call | solution.py:109
  17.5 0.5 collective-permute-start.1
  18.0 0.0 collective-permute-done.2
  18.0 2.0 %add_convert_fusion = bf16[512,512]{1,0:T(8,128)(2,1)} fusion(bf16[512,512]{1,0:T(8,128)(2,1)} %collective-permute-done.2, bf16[512,512]{1,0:T(8,128)(2,1)S(1)} %copy-done.8), kind=kLoop, calls=%fused_computation | loop fusion | flops 1048576 | bytes 1572864 | tf_op jit(solution)/shard_map/convert_element_type | solution.py:187
  20.0 0.0 collective-permute-done.1
  20.0 0.9 %add_convert_fusion.1 = bf16[512,512]{1,0:T(8,128)(2,1)} fusion(bf16[512,512]{1,0:T(8,128)(2,1)S(1)} %collective-permute-done.1, bf16[512,512]{1,0:T(8,128)(2,1)S(1)} %get-tuple-element.35), kind=kLoop, calls=%fused_computation.1 | loop fusion | flops 1048576 | bytes 1572864 | tf_op jit(solution)/shard_map/convert_element_type | solution.py:187
  20.9 5.5 %shard_map.58 = (bf16[1536,512]{1,0:T(8,128)(2,1)S(1)}, bf16[1536,512]{1,0:T(8,128)(2,1)}) custom-call(s32[3]{0:T(128)S(1)} %add_add_fusion.place, bf16[1536,1024]{1,0:T(8,128)(2,1)S(1)} %copy-done.4, bf16[1,1024]{1,0:T(2,128)(2,1)S(1)} %reshape.104.gain_ref, bf16[1024,2048]{1,0:T(8,128)(2,1)S(1)} %copy-done.2, bf16[1024,2048]{1,0:T(8,128)(2,1)S(1)} %copy-done.2), custom_call_target="tpu_custom_call" | custom-call | flops 3221225472 | bytes 8388608 | tf_op jit(solution)/shard_map/pallas_call | solution.py:109
  26.4 0.1 collective-permute-start.3
  26.5 1.3 %shard_map.59 = (bf16[256,512]{1,0:T(8,128)(2,1)S(1)}, bf16[256,512]{1,0:T(8,128)(2,1)S(1)}, f32[2,1,128]{2,1,0:T(1,128)S(1)}) custom-call(s32[3]{0:T(128)S(1)} %add_add_fusion.1.place, bf16[1536,1024]{1,0:T(8,128)(2,1)S(1)} %copy-done.4, bf16[1,1024]{1,0:T(2,128)(2,1)S(1)} %reshape.104.gain_ref, bf16[1024,2048]{1,0:T(8,128)(2,1)S(1)} %copy-done.2, ...), custom_call_target="tpu_custom_call" | custom-call | flops 536870912 | bytes 3145728 | tf_op jit(solution)/shard_map/pallas_call | solution.py:109
  27.8 0.5 collective-permute-start.4
  28.3 0.1 pad_maximum_fusion.1
  28.4 0.1 collective-permute-start.6
  28.5 1.4 %collective-permute-done.4 = f32[12,128]{1,0:T(8,128)S(1)} collective-permute-done((f32[12,128]{1,0:T(8,128)S(1)}, f32[12,128]{1,0:T(8,128)S(1)}, u32[]{:S(2)}, u32[]{:S(2)}) %collective-permute-start.4) | collective-permute-done | bytes 6176 | tf_op jit(solution)/shard_map/ppermute | solution.py:208
  29.9 2.6 %collective-permute-start.5 = (f32[12,128]{1,0:T(8,128)S(1)}, f32[12,128]{1,0:T(8,128)S(1)}, u32[]{:S(2)}, u32[]{:S(2)}) collective-permute-start(f32[12,128]{1,0:T(8,128)S(1)} %fusion.2), channel_id=1, source_target_pairs={{0,2},{1,3},{2,0},{3,1},{4,6},{5,7},{6,4},{7,5},{8,10},{9,11},{10,... | collective-permute-start | bytes 18440 | tf_op jit(solution)/shard_map/ppermute | solution.py:210
  32.5 0.1 fusion
  32.6 0.1 collective-permute-start.10
  32.7 2.0 %collective-permute-start.9 = (bf16[512,512]{1,0:T(8,128)(2,1)}, bf16[512,512]{1,0:T(8,128)(2,1)S(1)}, u32[]{:S(2)}, u32[]{:S(2)}) collective-permute-start(bf16[512,512]{1,0:T(8,128)(2,1)} %add_convert_fusion), channel_id=1, source_target_pairs={{0,2},{1,3},{2,0},{3,1},{4,6},{5,7},{6,4},{7,5},{8,10},{9,11},{10,... | collective-permute-start | bytes 1572872 | tf_op jit(solution)/shard_map/ppermute | solution.py:190
  34.7 0.0 collective-permute-done.5
  34.8 1.6 %collective-permute-start.8 = (bf16[512,512]{1,0:T(8,128)(2,1)}, bf16[512,512]{1,0:T(8,128)(2,1)S(1)}, u32[]{:S(2)}, u32[]{:S(2)}) collective-permute-start(bf16[512,512]{1,0:T(8,128)(2,1)} %add_convert_fusion.1), channel_id=1, source_target_pairs={{0,2},{1,3},{2,0},{3,1},{4,6},{5,7},{6,4},{7,5},{8,10},{9,11},{10,... | collective-permute-start | bytes 1572872 | tf_op jit(solution)/shard_map/ppermute | solution.py:190
  36.3 0.0 collective-permute-done.6
  36.3 0.1 add_convert_fusion.2
  36.4 0.6 collective-permute-start.7
  37.7 0.4 multiply_sine_fusion
  38.1 3.9 %collective-permute-done.10.refs_7_ = bf16[256,512]{1,0:T(8,128)(2,1)S(1)} collective-permute-done((bf16[256,512]{1,0:T(8,128)(2,1)}, bf16[256,512]{1,0:T(8,128)(2,1)S(1)}, u32[]{:S(2)}, u32[]{:S(2)}) %collective-permute-start.10) | collective-permute-done | bytes 262176 | tf_op jit(solution)/shard_map/ppermute | solution.py:190
  42.1 0.0 collective-permute-done.3.refs_1_
  42.1 1.4 %copy-done.6 = bf16[1536,512]{1,0:T(8,128)(2,1)S(1)} copy-done((bf16[1536,512]{1,0:T(8,128)(2,1)S(1)}, bf16[1536,512]{1,0:T(8,128)(2,1)}, u32[]{:S(2)}) %copy-start.6) | copy-done | bytes 1572888
  43.5 2.6 %shard_map.60.refs_8_ = bf16[1536,512]{1,0:T(8,128)(2,1)} custom-call(s32[3]{0:T(128)S(1)} %add_add_fusion.place, s32[4]{0:T(128)S(1)} %copy-done.9, bf16[1536,512]{1,0:T(8,128)(2,1)S(1)} %copy-done.6, bf16[1536,512]{1,0:T(8,128)(2,1)} %collective-permute-done.3.refs_1_, f32[2,12,1,128]{3,2,1,0:T(1,128)S(1)} %copy.17.refs_2_, ...), custom_call_target="tpu_custom_call" | custom-call | flops 2621440 | bytes 1048576 | tf_op jit(solution)/shard_map/pallas_call | solution.py:155
  46.1 7.2 %collective-permute-done.9.refs_7_ = bf16[512,512]{1,0:T(8,128)(2,1)S(1)} collective-permute-done((bf16[512,512]{1,0:T(8,128)(2,1)}, bf16[512,512]{1,0:T(8,128)(2,1)S(1)}, u32[]{:S(2)}, u32[]{:S(2)}) %collective-permute-start.9) | collective-permute-done | bytes 524320 | tf_op jit(solution)/shard_map/ppermute | solution.py:190
  53.3 3.0 %shard_map.61.refs_8_ = bf16[1536,512]{1,0:T(8,128)(2,1)} custom-call(s32[3]{0:T(128)S(1)} %add_add_fusion.place, s32[4]{0:T(128)S(1)} %copy-done.9, bf16[1536,512]{1,0:T(8,128)(2,1)S(1)} %copy-done.6, bf16[1536,512]{1,0:T(8,128)(2,1)} %collective-permute-done.3.refs_1_, f32[2,12,1,128]{3,2,1,0:T(1,128)S(1)} %copy.17.refs_2_, ...), custom_call_target="tpu_custom_call", output_to_operand_aliasing={{}: (10, {})} | custom-call | flops 5242880 | bytes 2097152 | tf_op jit(solution)/shard_map/pallas_call | solution.py:155
  56.3 8.3 %collective-permute-done.8.refs_7_ = bf16[512,512]{1,0:T(8,128)(2,1)S(1)} collective-permute-done((bf16[512,512]{1,0:T(8,128)(2,1)}, bf16[512,512]{1,0:T(8,128)(2,1)S(1)}, u32[]{:S(2)}, u32[]{:S(2)}) %collective-permute-start.8) | collective-permute-done | bytes 524320 | tf_op jit(solution)/shard_map/ppermute | solution.py:190
  64.5 3.0 %shard_map.62.refs_8_ = bf16[1536,512]{1,0:T(8,128)(2,1)} custom-call(s32[3]{0:T(128)S(1)} %add_add_fusion.place, s32[4]{0:T(128)S(1)} %copy-done.9, bf16[1536,512]{1,0:T(8,128)(2,1)S(1)} %copy-done.6, bf16[1536,512]{1,0:T(8,128)(2,1)} %collective-permute-done.3.refs_1_, f32[2,12,1,128]{3,2,1,0:T(1,128)S(1)} %copy.17.refs_2_, ...), custom_call_target="tpu_custom_call", output_to_operand_aliasing={{}: (10, {})} | custom-call | flops 5242880 | bytes 2097152 | tf_op jit(solution)/shard_map/pallas_call | solution.py:155
  67.5 1.8 %collective-permute-done.7.refs_7_ = bf16[256,512]{1,0:T(8,128)(2,1)S(1)} collective-permute-done((bf16[256,512]{1,0:T(8,128)(2,1)S(1)}, bf16[256,512]{1,0:T(8,128)(2,1)S(1)}, u32[]{:S(2)}, u32[]{:S(2)}) %collective-permute-start.7) | collective-permute-done | bytes 262176 | tf_op jit(solution)/shard_map/ppermute | solution.py:190
  69.3 2.6 %shard_map.63 = bf16[1536,512]{1,0:T(8,128)(2,1)} custom-call(s32[3]{0:T(128)S(1)} %add_add_fusion.place, s32[4]{0:T(128)S(1)} %copy-done.9, bf16[1536,512]{1,0:T(8,128)(2,1)S(1)} %copy-done.6, bf16[1536,512]{1,0:T(8,128)(2,1)} %collective-permute-done.3.refs_1_, f32[2,12,1,128]{3,2,1,0:T(1,128)S(1)} %copy.17.refs_2_, ...), custom_call_target="tpu_custom_call", output_to_operand_aliasing={{}: (10, {})} | custom-call | flops 2621440 | bytes 1048576 | tf_op jit(solution)/shard_map/pallas_call | solution.py:155
  (23 shorter events, 0.1 us)
Async XLA Ops:
  0.8 2.2 %copy-start = (bf16[1024,2048]{1,0:T(8,128)(2,1)S(1)}, bf16[1024,2048]{1,0:T(8,128)(2,1)}, u32[]{:S(2)}) copy-start(bf16[1024,2048]{1,0:T(8,128)(2,1)} %send_weight.9) | copy-start | bytes 12582916
  3.0 1.9 %copy-start.3 = (bf16[1536,1024]{1,0:T(8,128)(2,1)S(1)}, bf16[1536,1024]{1,0:T(8,128)(2,1)}, u32[]{:S(2)}) copy-start(bf16[1536,1024]{1,0:T(8,128)(2,1)} %rows_ref.9) | copy-start | bytes 9437188
  6.7 3.9 %copy-start.10 = (s32[4]{0:T(128)S(1)}, s32[4]{0:T(128)}, u32[]{:S(2)}) copy-start(s32[4]{0:T(128)} %param.9) | copy-start | bytes 52
  6.7 4.7 %collective-permute-start = (bf16[256,512]{1,0:T(8,128)(2,1)}, bf16[256,512]{1,0:T(8,128)(2,1)}, u32[]{:S(2)}, u32[]{:S(2)}) collective-permute-start(bf16[256,512]{1,0:T(8,128)(2,1)} %get-tuple-element.33), channel_id=1, source_target_pairs={{0,1},{1,0},{2,3},{3,2},{4,5},{5,4},{6,7},{7,6},{8,9},{9,8},{10,11... | collective-permute-start | bytes 786440 | tf_op jit(solution)/shard_map/ppermute | solution.py:182
  7.2 6.0 %copy-start.4 = (bf16[1536,1024]{1,0:T(8,128)(2,1)S(1)}, bf16[1536,1024]{1,0:T(8,128)(2,1)}, u32[]{:S(2)}) copy-start(bf16[1536,1024]{1,0:T(8,128)(2,1)} %rows_ref.9) | copy-start | bytes 9437188
  9.8 0.8 %copy-start.7 = (bf16[512,512]{1,0:T(8,128)(2,1)}, bf16[512,512]{1,0:T(8,128)(2,1)S(1)}, u32[]{:S(2)}) copy-start(bf16[512,512]{1,0:T(8,128)(2,1)S(1)} %get-tuple-element.37) | copy-start | bytes 1572868
  10.6 7.4 %collective-permute-start.2 = (bf16[512,512]{1,0:T(8,128)(2,1)}, bf16[512,512]{1,0:T(8,128)(2,1)}, u32[]{:S(2)}, u32[]{:S(2)}) collective-permute-start(bf16[512,512]{1,0:T(8,128)(2,1)} %get-tuple-element.38), channel_id=1, source_target_pairs={{0,1},{1,0},{2,3},{3,2},{4,5},{5,4},{6,7},{7,6},{8,9},{9,8},{10,11... | collective-permute-start | bytes 1572872 | tf_op jit(solution)/shard_map/ppermute | solution.py:182
  13.1 2.2 %copy-start.1 = (bf16[1024,2048]{1,0:T(8,128)(2,1)S(1)}, bf16[1024,2048]{1,0:T(8,128)(2,1)}, u32[]{:S(2)}) copy-start(bf16[1024,2048]{1,0:T(8,128)(2,1)} %send_weight.9) | copy-start | bytes 12582916
  15.3 2.7 %copy-start.8 = (bf16[512,512]{1,0:T(8,128)(2,1)S(1)}, bf16[512,512]{1,0:T(8,128)(2,1)}, u32[]{:S(2)}) copy-start(bf16[512,512]{1,0:T(8,128)(2,1)} %copy-done.7) | copy-start | bytes 1572868
  15.3 5.6 %copy-start.2 = (bf16[1024,2048]{1,0:T(8,128)(2,1)S(1)}, bf16[1024,2048]{1,0:T(8,128)(2,1)}, u32[]{:S(2)}) copy-start(bf16[1024,2048]{1,0:T(8,128)(2,1)} %send_weight.9) | copy-start | bytes 12582916
  17.5 2.5 %collective-permute-start.1 = (bf16[512,512]{1,0:T(8,128)(2,1)S(1)}, bf16[512,512]{1,0:T(8,128)(2,1)S(1)}, u32[]{:S(2)}, u32[]{:S(2)}) collective-permute-start(bf16[512,512]{1,0:T(8,128)(2,1)S(1)} %get-tuple-element.36), channel_id=1, source_target_pairs={{0,1},{1,0},{2,3},{3,2},{4,5},{5,4},{6,7},{7,6},{8,9},{9,8},{10,11... | collective-permute-start | bytes 1572872 | tf_op jit(solution)/shard_map/ppermute | solution.py:182
  26.4 1.3 %copy-start.5 = (bf16[1536,512]{1,0:T(8,128)(2,1)}, bf16[1536,512]{1,0:T(8,128)(2,1)S(1)}, u32[]{:S(2)}) copy-start(bf16[1536,512]{1,0:T(8,128)(2,1)S(1)} %get-tuple-element.45.refs_0_.refs_8_) | copy-start | bytes 4718596
  26.4 15.6 %collective-permute-start.3 = (bf16[1536,512]{1,0:T(8,128)(2,1)}, bf16[1536,512]{1,0:T(8,128)(2,1)}, u32[]{:S(2)}, u32[]{:S(2)}) collective-permute-start(bf16[1536,512]{1,0:T(8,128)(2,1)} %get-tuple-element.46), channel_id=1, source_target_pairs={{0,1},{1,0},{2,3},{3,2},{4,5},{5,4},{6,7},{7,6},{8,9},{9,8},{10,11... | collective-permute-start | bytes 4718600 | tf_op jit(solution)/shard_map/ppermute | solution.py:203
  26.5 15.6 %copy-start.9 = (s32[4]{0:T(128)S(1)}, s32[4]{0:T(128)}, u32[]{:S(2)}) copy-start(s32[4]{0:T(128)} %live.7) | copy-start | bytes 52
  27.8 2.0 %collective-permute-start.4 = (f32[12,128]{1,0:T(8,128)S(1)}, f32[12,128]{1,0:T(8,128)S(1)}, u32[]{:S(2)}, u32[]{:S(2)}) collective-permute-start(f32[12,128]{1,0:T(8,128)S(1)} %bitcast.16), channel_id=1, source_target_pairs={{0,1},{1,0},{2,3},{3,2},{4,5},{5,4},{6,7},{7,6},{8,9},{9,8},{10,11... | collective-permute-start | bytes 18440 | tf_op jit(solution)/shard_map/ppermute | solution.py:208
  28.4 7.9 %collective-permute-start.6 = (bf16[256,512]{1,0:T(8,128)(2,1)S(1)}, bf16[256,512]{1,0:T(8,128)(2,1)S(1)}, u32[]{:S(2)}, u32[]{:S(2)}) collective-permute-start(bf16[256,512]{1,0:T(8,128)(2,1)S(1)} %get-tuple-element.52), channel_id=1, source_target_pairs={{0,1},{1,0},{2,3},{3,2},{4,5},{5,4},{6,7},{7,6},{8,9},{9,8},{10,11... | collective-permute-start | bytes 786440 | tf_op jit(solution)/shard_map/ppermute | solution.py:182
  29.9 4.9 %collective-permute-start.5 = (f32[12,128]{1,0:T(8,128)S(1)}, f32[12,128]{1,0:T(8,128)S(1)}, u32[]{:S(2)}, u32[]{:S(2)}) collective-permute-start(f32[12,128]{1,0:T(8,128)S(1)} %fusion.2), channel_id=1, source_target_pairs={{0,2},{1,3},{2,0},{3,1},{4,6},{5,7},{6,4},{7,5},{8,10},{9,11},{10,... | collective-permute-start | bytes 18440 | tf_op jit(solution)/shard_map/ppermute | solution.py:210
  32.6 9.4 %collective-permute-start.10 = (bf16[256,512]{1,0:T(8,128)(2,1)}, bf16[256,512]{1,0:T(8,128)(2,1)S(1)}, u32[]{:S(2)}, u32[]{:S(2)}) collective-permute-start(bf16[256,512]{1,0:T(8,128)(2,1)} %add_convert_fusion.3), channel_id=1, source_target_pairs={{0,2},{1,3},{2,0},{3,1},{4,6},{5,7},{6,4},{7,5},{8,10},{9,11},{10,... | collective-permute-start | bytes 786440 | tf_op jit(solution)/shard_map/ppermute | solution.py:190
  32.7 20.6 %collective-permute-start.9 = (bf16[512,512]{1,0:T(8,128)(2,1)}, bf16[512,512]{1,0:T(8,128)(2,1)S(1)}, u32[]{:S(2)}, u32[]{:S(2)}) collective-permute-start(bf16[512,512]{1,0:T(8,128)(2,1)} %add_convert_fusion), channel_id=1, source_target_pairs={{0,2},{1,3},{2,0},{3,1},{4,6},{5,7},{6,4},{7,5},{8,10},{9,11},{10,... | collective-permute-start | bytes 1572872 | tf_op jit(solution)/shard_map/ppermute | solution.py:190
  34.8 29.8 %collective-permute-start.8 = (bf16[512,512]{1,0:T(8,128)(2,1)}, bf16[512,512]{1,0:T(8,128)(2,1)S(1)}, u32[]{:S(2)}, u32[]{:S(2)}) collective-permute-start(bf16[512,512]{1,0:T(8,128)(2,1)} %add_convert_fusion.1), channel_id=1, source_target_pairs={{0,2},{1,3},{2,0},{3,1},{4,6},{5,7},{6,4},{7,5},{8,10},{9,11},{10,... | collective-permute-start | bytes 1572872 | tf_op jit(solution)/shard_map/ppermute | solution.py:190
  36.4 32.9 %collective-permute-start.7 = (bf16[256,512]{1,0:T(8,128)(2,1)S(1)}, bf16[256,512]{1,0:T(8,128)(2,1)S(1)}, u32[]{:S(2)}, u32[]{:S(2)}) collective-permute-start(bf16[256,512]{1,0:T(8,128)(2,1)S(1)} %add_convert_fusion.2), channel_id=1, source_target_pairs={{0,2},{1,3},{2,0},{3,1},{4,6},{5,7},{6,4},{7,5},{8,10},{9,11},{10,... | collective-permute-start | bytes 786440 | tf_op jit(solution)/shard_map/ppermute | solution.py:190
  42.1 1.4 %copy-start.6 = (bf16[1536,512]{1,0:T(8,128)(2,1)S(1)}, bf16[1536,512]{1,0:T(8,128)(2,1)}, u32[]{:S(2)}) copy-start(bf16[1536,512]{1,0:T(8,128)(2,1)} %copy-done.5) | copy-start | bytes 4718596

commit v3 on v2

v3 whole, which is shorter than its diff:
```python
import functools

import jax
import jax.numpy as jnp
from jax import lax
from jax.experimental import pallas as pl
from jax.experimental.pallas import tpu as pltpu
from jax.sharding import PartitionSpec as P

HD = 128
PAGE = 256
BLOCK = 64
LANES = 128

rope_base = 500000.0
norm_eps = 1e-05

TILE = 256
CHUNKS = (1, 2, 2, 1)

WIDE = pltpu.CompilerParams(vmem_limit_bytes=60 * 1024 * 1024)
PARAMS = pltpu.CompilerParams(vmem_limit_bytes=16 * 1024 * 1024)
COST = pl.CostEstimate(flops=1, bytes_accessed=1, transcendentals=0)


def square_sums(rows):
    total = jnp.zeros((rows.shape[0], LANES), jnp.float32)
    for part in range(rows.shape[1] // LANES):
        wide = rows[:, part * LANES : (part + 1) * LANES].astype(jnp.float32)
        total += wide * wide
    return total


def product_kernel(with_squares, place, rows_ref, gain_ref, keep_weight, send_weight, keep, send, *squares):
    scaled = rows_ref[...] * gain_ref[...].reshape(1, gain_ref.shape[0])
    send[...] = jnp.dot(scaled, send_weight[...], preferred_element_type=jnp.float32).astype(send.dtype)
    keep[...] = jnp.dot(scaled, keep_weight[...], preferred_element_type=jnp.float32).astype(keep.dtype)
    if with_squares:
        total = square_sums(rows_ref[...])
        for part in range(TILE // LANES):
            turned = jnp.transpose(total[part * LANES : (part + 1) * LANES])
            row = pl.program_id(0) * (TILE // LANES) + part
            squares[0][pl.ds(row, 1), :] = jnp.sum(turned, axis=0, keepdims=True)


def add_kernel(keep, received, out):
    out[...] = (keep[...].astype(jnp.float32) + received[...].astype(jnp.float32)).astype(out.dtype)


def finish_kernel(first_tile, chip_count, model_dim, place, live, *refs):
    keep, received, far_cos, far_sin, near_cos, near_sin = refs[:6]
    squares, arrived, out = refs[6 : 6 + chip_count], refs[6 + chip_count : -2], refs[-1]
    values = keep[...].astype(jnp.float32) + received[...].astype(jnp.float32)
    for part in arrived:
        values += part[...].astype(jnp.float32)
    on_diagonal = lax.broadcasted_iota(jnp.int32, (LANES, LANES), 0) == lax.broadcasted_iota(
        jnp.int32, (LANES, LANES), 1
    )
    tile = first_tile + pl.program_id(0)
    columns = []
    for part in range(TILE // LANES):
        row = pl.ds(tile * (TILE // LANES) + part, 1)
        totals = functools.reduce(jnp.add, [ref[row, :] for ref in squares])
        columns.append(jnp.sum(jnp.where(on_diagonal, totals, 0.0), axis=1, keepdims=True))
    scales = 1.0 / jnp.sqrt(jnp.concatenate(columns, axis=0) / model_dim + norm_eps)
    row = tile * TILE + lax.broadcasted_iota(jnp.int32, (TILE, 1), 0)
    alive = row < live[place[2]] * BLOCK
    sign = jnp.where(lax.broadcasted_iota(jnp.int32, (1, HD), 1) < HD // 2, -1.0, 1.0)
    cosines, sines = [], []
    for part in range(TILE // BLOCK):
        block_cos = far_cos[part]
        block_sin = far_sin[part]
        cosines.append(block_cos * near_cos[...] - block_sin * near_sin[...])
        sines.append((sign * block_sin) * near_cos[...] + (sign * block_cos) * near_sin[...])
    cosine = jnp.concatenate(cosines, axis=0)
    sine = jnp.concatenate(sines, axis=0)
    for start in range(0, out.shape[1], 2 * HD):
        key = values[:, start : start + HD] * scales
        turned = key * cosine + pltpu.roll(key, HD // 2, 1) * sine
        out[:, start : start + HD] = jnp.where(alive, turned, 0.0).astype(out.dtype)
        value = values[:, start + HD : start + 2 * HD] * scales
        out[:, start + HD : start + 2 * HD] = jnp.where(alive, value, 0.0).astype(out.dtype)


def shards(tokens, norm_gain, kv_weight, live_blocks, span_offset):
    tensor_count = lax.axis_size("tensor")
    chip_count = tensor_count // 2
    me = lax.axis_index("tensor")
    own_index = lax.axis_index("serve")
    slot_rows, depth = tokens.shape
    columns = kv_weight.shape[1] // tensor_count
    tiles = slot_rows // TILE
    model_dim = depth * tensor_count

    swap = [(i, i ^ 1) for i in range(tensor_count)]

    def shift(step):
        return [(i, (i + 2 * step) % tensor_count) for i in range(tensor_count)]

    def place_of(step):
        keep = (me + 2 * step) % tensor_count
        return jnp.stack([keep, keep ^ 1, own_index]).astype(jnp.int32)

    def product(place, first, count, with_squares):
        rows = count * TILE
        out_shape = [jax.ShapeDtypeStruct((rows, columns), jnp.bfloat16)] * 2
        out_specs = [pl.BlockSpec((TILE, columns), lambda i, *_: (i, 0))] * 2
        if with_squares:
            out_shape.append(jax.ShapeDtypeStruct((rows // LANES, LANES), jnp.float32))
            out_specs.append(pl.BlockSpec((rows // LANES, LANES), lambda i, *_: (0, 0)))
        return pl.pallas_call(
            functools.partial(product_kernel, with_squares),
            grid_spec=pltpu.PrefetchScalarGridSpec(
                num_scalar_prefetch=1,
                grid=(count,),
                in_specs=[
                    pl.BlockSpec((TILE, depth), lambda i, *_: (first + i, 0)),
                    pl.BlockSpec((depth,), lambda i, *_: (0,)),
                    pl.BlockSpec((depth, columns), lambda i, where: (0, where[0])),
                    pl.BlockSpec((depth, columns), lambda i, where: (0, where[1])),
                ],
                out_specs=out_specs,
            ),
            out_shape=out_shape,
            compiler_params=WIDE,
            cost_estimate=COST,
        )(place, tokens, norm_gain, kv_weight, kv_weight)

    def tables(offset):
        half = HD // 2
        inv_freq = rope_base ** (-(jnp.arange(half, dtype=jnp.float32) * 2.0) / HD)
        inv_freq = jnp.concatenate([inv_freq, inv_freq])
        starts = offset * PAGE + BLOCK * jnp.arange(slot_rows // BLOCK, dtype=jnp.int32)
        far = starts.astype(jnp.float32)[:, None, None] * inv_freq
        near = jnp.arange(BLOCK, dtype=jnp.float32)[:, None] * inv_freq
        return [jnp.cos(far), jnp.sin(far), jnp.cos(near), jnp.sin(near)]

    def finish(first, count, keep, received, table, squares, arrived, result):
        blocks = TILE // BLOCK
        operands = [keep, received] + table + squares + arrived
        specs = (
            [pl.BlockSpec((TILE, columns), lambda i, *_: (first + i, 0))] * 2
            + [pl.BlockSpec((blocks, 1, HD), lambda i, *_: (first + i, 0, 0))] * 2
            + [pl.BlockSpec((BLOCK, HD), lambda i, *_: (0, 0))] * 2
            + [pl.BlockSpec((slot_rows // LANES, LANES), lambda i, *_: (0, 0))] * chip_count
            + [pl.BlockSpec((TILE, columns), lambda i, *_: (i, 0))] * len(arrived)
        )
        if result is None:
            result = keep
            aliases = {}
        else:
            aliases = {2 + len(operands): 0}
        return pl.pallas_call(
            functools.partial(finish_kernel, first, chip_count, model_dim),
            grid_spec=pltpu.PrefetchScalarGridSpec(
                num_scalar_prefetch=2,
                grid=(count,),
                in_specs=specs + [pl.BlockSpec(memory_space=pl.ANY)],
                out_specs=pl.BlockSpec((TILE, columns), lambda i, *_: (first + i, 0)),
            ),
            out_shape=jax.ShapeDtypeStruct((slot_rows, columns), jnp.bfloat16),
            input_output_aliases=aliases,
            compiler_params=PARAMS,
            cost_estimate=COST,
        )(place_of(0), live_blocks, *operands, result)

    others = range(1, chip_count)
    firsts = [sum(CHUNKS[:index]) for index in range(len(CHUNKS))]
    chunk_count = len(CHUNKS)
    places = {step: place_of(step) for step in range(chip_count)}

    def start_chunk(index):
        return [product(places[step], firsts[index], CHUNKS[index], False) for step in others]

    def add_halves(made):
        return [
            pl.pallas_call(
                add_kernel,
                out_shape=jax.ShapeDtypeStruct(keep.shape, keep.dtype),
                compiler_params=PARAMS,
                cost_estimate=COST,
            )(keep, lax.ppermute(send, "tensor", swap))
            for keep, send in made
        ]

    def cross(sums):
        return [lax.ppermute(part, "tensor", shift(step)) for step, part in zip(others, sums)]

    def own_inputs(own, table):
        keep, send, own_squares = own
        received = lax.ppermute(send, "tensor", swap)
        pair_squares = own_squares + lax.ppermute(own_squares, "tensor", swap)
        squares = [pair_squares] + [lax.ppermute(pair_squares, "tensor", shift(step)) for step in others]
        return [keep, received, table, squares]

    hold = lax.optimization_barrier
    arrivals = []
    own, inputs, result, finished = None, None, None, 0
    made = start_chunk(0)
    made, places = hold((made, places))
    sums = add_halves(made)
    made = start_chunk(1)
    sums, made, places, span_offset = hold((sums, made, places, span_offset))
    for stage in range(1, chunk_count + 1):
        arrived = cross(sums)
        if stage < chunk_count:
            sums = add_halves(made)
        if stage + 1 < chunk_count:
            made = start_chunk(stage + 1)
        if stage == 2:
            own = product(places[0], 0, tiles, True), tables(span_offset[own_index])
        if stage == 3:
            inputs = own_inputs(*own)
        if stage >= 3:
            for index in range(finished, stage - 1):
                result = finish(firsts[index], CHUNKS[index], *inputs, arrivals[index], result)
            finished = stage - 1
        arrived, sums, made, places, span_offset, own, inputs, result = hold(
            (arrived, sums, made, places, span_offset, own, inputs, result)
        )
        arrivals.append(arrived)
    for index in range(finished, chunk_count):
        result = finish(firsts[index], CHUNKS[index], *inputs, arrivals[index], result)
    return result


def solution(mesh):
    in_specs = (
        P(("groups", "serve"), "tensor"),
        P("tensor"),
        P("tensor", None),
        P("groups"),
        P("groups"),
    )
    out_specs = P(("groups", "serve"), "tensor")
    return jax.shard_map(shards, mesh=mesh, in_specs=in_specs, out_specs=out_specs, check_vma=False)
```

time: 72.3 us -> 63.5 us (0.88)
  Pallas kernels: 24.5 us -> 33.1 us
  local copies, waits for them, and re-layouts: 9.88 us -> 1.66 us
  other arithmetic: 5.51 us -> 1.32 us
  waiting for transfers between devices: 22.6 us -> 19 us
  starting transfers between devices: 8.53 us -> 7.14 us
    ppermute x4, waiting for transfers between devices: 21.2 us -> 7.05 us  [cross(): lax.ppermute(part, 'tensor', shift(step))]
    pallas_call x5, Pallas kernels: 13.4 us -> 25.4 us  [product(): pl.pallas_call(functools.partial(product_kernel, with_squares), grid_spec...]
    ppermute x7, waiting for transfers between devices: 1.41 us -> 12 us  [the longest x1 9.49 us: own_inputs(): lax.ppermute(pair_squares, 'tensor', shift(step))]
    unnamed x23 -> x20, local copies, waits for them, and re-layouts: 8.51 us -> 0.99 us
    convert_element_type x4 -> x0, other arithmetic: 4.7 us -> none  [cross(): (keep.astype(jnp.float32) + got.astype(jnp.float32)).astype(jnp.bfloat16)]
    pallas_call x4 -> x8, Pallas kernels: 11.1 us -> 7.67 us  [the longest x4 7.3 us: finish(): pl.pallas_call(functools.partial(finish_kernel, first, chip_count, model_...]
    ppermute x7, starting transfers between devices: 4.29 us -> 2.03 us  [the longest x4 0.71 us: add_halves(): lax.ppermute(send, 'tensor', swap)]
    ppermute x4, starting transfers between devices: 4.24 us -> 5.12 us  [cross(): lax.ppermute(part, 'tensor', shift(step))]
  transfers between devices with their start and end apart: 11 -> 11, of which waited for: 5 -> 5; matrix products, arithmetic and copies ran while one was open for 7% -> 2% of each run, Pallas kernels for 20% -> 44%
where the time goes in v3:
time: 63.5 us; the launch traced here: 63.1 us
  Pallas kernels  33.1 us (52%)
  waiting for transfers between devices  19 us (30%)
  starting transfers between devices  7.14 us (11%)
  local copies, waits for them, and re-layouts  1.66 us (3%)
  other arithmetic  1.32 us (2%)
  between operations  0.84 us (1%)
    pallas_call x5, Pallas kernels, product(): pl.pallas_call(functools.partial(product_kernel, with_squares), grid_spec...  25.4 us
    ppermute x1, waiting for transfers between devices, own_inputs(): lax.ppermute(pair_squares, 'tensor', shift(step))  9.49 us
    pallas_call x4, Pallas kernels, finish(): pl.pallas_call(functools.partial(finish_kernel, first, chip_count, model_...  7.3 us
    ppermute x4, waiting for transfers between devices, cross(): lax.ppermute(part, 'tensor', shift(step))  7.05 us
    ppermute x4, starting transfers between devices, cross(): lax.ppermute(part, 'tensor', shift(step))  5.12 us
    ppermute x1, waiting for transfers between devices, own_inputs(): pair_squares = own_squares + lax.ppermute(own_squares, 'tensor', swap)  2.41 us
  transfers between devices with their start and end apart: 11, of which 5 were waited for; matrix products, arithmetic and copies ran while one was open for 2% of the time, Pallas kernels for 44%

profile of v3, /device:TPU:0, one launch (start us, length us, event | category | flops | bytes accessed | tf_op | source)
XLA Modules:
  0.0 63.1 jit_solution(17639513176285558667)
XLA Ops:
  0.0 0.7 %add_add_fusion = (s32[3]{0:T(128)}, s32[3]{0:T(128)}) fusion(s32[1]{0:T(128)} %bitcast.1, s32[1]{0:T(128)} %bitcast, s32[1]{0:T(128)} %bitcast.2, s32[1]{0:T(128)} %bitcast.4, s32[1]{0:T(128)} %bitcast.3), kind=kLoop, calls=%fused_computation.5 | loop fusion | flops 12 | bytes 44 | tf_op jit(solution)/shard_map/stack | solution.py:102
  0.7 3.8 %shard_map.55 = (bf16[256,512]{1,0:T(8,128)(2,1)}, bf16[256,512]{1,0:T(8,128)(2,1)}) custom-call(s32[3]{0:T(128)} %get-tuple-element.84.place, bf16[1536,1024]{1,0:T(8,128)(2,1)} %rows_ref.9, bf16[1024]{0:T(1024)(128)(2,1)} %gain_ref.9, bf16[1024,2048]{1,0:T(8,128)(2,1)} %send_weight.9, bf16[1024,2048]{1,0:T(8,128)(2,1)} %send_weight.9), custom_call_target="tpu_custom_call" | custom-call | flops 1 | bytes 1 | tf_op jit(solution)/shard_map/pallas_call | solution.py:111
  4.5 0.5 collective-permute-start
  4.9 4.6 %shard_map.57 = (bf16[512,512]{1,0:T(8,128)(2,1)}, bf16[512,512]{1,0:T(8,128)(2,1)}) custom-call(s32[3]{0:T(128)} %get-tuple-element.84.place, bf16[1536,1024]{1,0:T(8,128)(2,1)} %rows_ref.9, bf16[1024]{0:T(1024)(128)(2,1)} %gain_ref.9, bf16[1024,2048]{1,0:T(8,128)(2,1)} %send_weight.9, bf16[1024,2048]{1,0:T(8,128)(2,1)} %send_weight.9), custom_call_target="tpu_custom_call" | custom-call | flops 1 | bytes 1 | tf_op jit(solution)/shard_map/pallas_call | solution.py:111
  9.5 0.0 collective-permute-done.received
  9.5 0.0 copy-done.4
  9.5 0.1 shard_map.56
  9.6 0.3 collective-permute-start.2
  9.8 2.8 %collective-permute-start.1 = (bf16[256,512]{1,0:T(8,128)(2,1)S(1)}, bf16[256,512]{1,0:T(8,128)(2,1)S(1)}, u32[]{:S(2)}, u32[]{:S(2)}) collective-permute-start(bf16[256,512]{1,0:T(8,128)(2,1)S(1)} %shard_map.56), channel_id=1, source_target_pairs={{0,2},{1,3},{2,0},{3,1},{4,6},{5,7},{6,4},{7,5},{8,10},{9,11},{10,... | collective-permute-start | bytes 786440 | tf_op jit(solution)/shard_map/ppermute | solution.py:187
  12.7 0.1 pad_maximum_fusion
  12.7 4.7 %shard_map.59 = (bf16[512,512]{1,0:T(8,128)(2,1)}, bf16[512,512]{1,0:T(8,128)(2,1)}) custom-call(s32[3]{0:T(128)} %get-tuple-element.84.place, bf16[1536,1024]{1,0:T(8,128)(2,1)} %rows_ref.9, bf16[1024]{0:T(1024)(128)(2,1)} %gain_ref.9, bf16[1024,2048]{1,0:T(8,128)(2,1)} %send_weight.9, bf16[1024,2048]{1,0:T(8,128)(2,1)} %send_weight.9), custom_call_target="tpu_custom_call" | custom-call | flops 1 | bytes 1 | tf_op jit(solution)/shard_map/pallas_call | solution.py:111
  17.4 0.0 collective-permute-done.2.received
  17.4 0.0 copy-done.2
  17.5 0.1 shard_map.58
  17.6 1.7 %collective-permute-done.1.refs_8_ = bf16[256,512]{1,0:T(8,128)(2,1)S(1)} collective-permute-done((bf16[256,512]{1,0:T(8,128)(2,1)S(1)}, bf16[256,512]{1,0:T(8,128)(2,1)S(1)}, u32[]{:S(2)}, u32[]{:S(2)}) %collective-permute-start.1) | collective-permute-done | bytes 262176 | tf_op jit(solution)/shard_map/ppermute | solution.py:187
  19.3 0.0 collective-permute-start.4
  19.3 1.7 %collective-permute-start.3 = (bf16[512,512]{1,0:T(8,128)(2,1)S(1)}, bf16[512,512]{1,0:T(8,128)(2,1)S(1)}, u32[]{:S(2)}, u32[]{:S(2)}) collective-permute-start(bf16[512,512]{1,0:T(8,128)(2,1)S(1)} %shard_map.58), channel_id=1, source_target_pairs={{0,2},{1,3},{2,0},{3,1},{4,6},{5,7},{6,4},{7,5},{8,10},{9,11},{10,... | collective-permute-start | bytes 1572872 | tf_op jit(solution)/shard_map/ppermute | solution.py:187
  21.0 0.1 fusion
  21.2 8.4 %shard_map.62 = (bf16[1536,512]{1,0:T(8,128)(2,1)}, bf16[1536,512]{1,0:T(8,128)(2,1)}, f32[12,128]{1,0:T(8,128)}) custom-call(s32[3]{0:T(128)} %get-tuple-element.87.place, bf16[1536,1024]{1,0:T(8,128)(2,1)} %rows_ref.9, bf16[1024]{0:T(1024)(128)(2,1)} %gain_ref.9, bf16[1024,2048]{1,0:T(8,128)(2,1)} %send_weight.9, bf16[1024,2048]{1,0:T(8,128)(2,1)} %send_weight.9), custom_call_target="tpu_custom_call" | custom-call | flops 1 | bytes 1 | tf_op jit(solution)/shard_map/pallas_call | solution.py:111
  29.5 0.0 copy-start.8
  29.6 4.0 %shard_map.61 = (bf16[256,512]{1,0:T(8,128)(2,1)}, bf16[256,512]{1,0:T(8,128)(2,1)}) custom-call(s32[3]{0:T(128)} %get-tuple-element.84.place, bf16[1536,1024]{1,0:T(8,128)(2,1)} %rows_ref.9, bf16[1024]{0:T(1024)(128)(2,1)} %gain_ref.9, bf16[1024,2048]{1,0:T(8,128)(2,1)} %send_weight.9, bf16[1024,2048]{1,0:T(8,128)(2,1)} %send_weight.9), custom_call_target="tpu_custom_call" | custom-call | flops 1 | bytes 1 | tf_op jit(solution)/shard_map/pallas_call | solution.py:111
  33.5 0.0 copy-start.6
  33.6 0.7 %dynamic_slice.3 = s32[1]{0:T(128)} dynamic-slice(s32[4]{0:T(128)S(1)} %copy-done.9, s32[]{:T(128)S(6)} %select_n.24), dynamic_slice_sizes={1} | dynamic-slice | bytes 12 | tf_op jit(solution)/shard_map/dynamic_slice | solution.py:211
  34.9 0.4 multiply_sine_fusion
  35.4 0.0 collective-permute-done.4.received
  35.4 0.1 shard_map.60
  35.5 0.0 collective-permute-done.3.refs_8_
  35.5 0.0 copy-done.8
  35.5 0.3 collective-permute-start.7
  35.8 0.3 collective-permute-start.5
  36.1 0.0 collective-permute-start.6
  36.1 0.0 copy-done.7
  36.1 0.5 collective-permute-start.8
  36.6 2.4 %collective-permute-done.8 = f32[12,128]{1,0:T(8,128)S(1)} collective-permute-done((f32[12,128]{1,0:T(8,128)S(1)}, f32[12,128]{1,0:T(8,128)S(1)}, u32[]{:S(2)}, u32[]{:S(2)}) %collective-permute-start.8) | collective-permute-done | bytes 6176 | tf_op jit(solution)/shard_map/ppermute | solution.py:192
  39.0 0.5 collective-permute-start.9
  39.5 0.1 collective-permute-done.6.received
  39.6 0.9 %copy-done.3 = bf16[256,512]{1,0:T(8,128)(2,1)S(1)} copy-done((bf16[256,512]{1,0:T(8,128)(2,1)S(1)}, bf16[256,512]{1,0:T(8,128)(2,1)}, u32[]{:S(2)}) %copy-start.3) | copy-done | bytes 262168
  40.6 0.1 shard_map.63
  40.6 9.5 %collective-permute-done.9.refs_7_ = f32[12,128]{1,0:T(8,128)S(1)} collective-permute-done((f32[12,128]{1,0:T(8,128)S(1)}, f32[12,128]{1,0:T(8,128)S(1)}, u32[]{:S(2)}, u32[]{:S(2)}) %collective-permute-start.9) | collective-permute-done | bytes 6176 | tf_op jit(solution)/shard_map/ppermute | solution.py:193
  50.1 0.0 collective-permute-done.7.refs_1_
  50.1 0.0 copy-done.6
  50.1 1.6 %shard_map.64.refs_9_ = bf16[1536,512]{1,0:T(8,128)(2,1)} custom-call(s32[3]{0:T(128)S(1)} %copy-done.5, s32[4]{0:T(128)S(1)} %copy-done.6, bf16[1536,512]{1,0:T(8,128)(2,1)S(1)} %copy-done, bf16[1536,512]{1,0:T(8,128)(2,1)S(1)} %collective-permute-done.7.refs_1_, f32[24,1,128]{2,1,0:T(1,128)S(1)} %get-tuple-element.117.refs_2_, ...), custom_call_target="tpu_custom_call" | custom-call | flops 1 | bytes 1 | tf_op jit(solution)/shard_map/pallas_call | solution.py:153
  51.8 2.0 %shard_map.65.refs_9_ = bf16[1536,512]{1,0:T(8,128)(2,1)} custom-call(s32[3]{0:T(128)S(1)} %copy-done.5, s32[4]{0:T(128)S(1)} %copy-done.6, bf16[1536,512]{1,0:T(8,128)(2,1)S(1)} %copy-done, bf16[1536,512]{1,0:T(8,128)(2,1)S(1)} %collective-permute-done.7.refs_1_, f32[24,1,128]{2,1,0:T(1,128)S(1)} %get-tuple-element.117.refs_2_, ...), custom_call_target="tpu_custom_call", output_to_operand_aliasing={{}: (11, {})} | custom-call | flops 1 | bytes 1 | tf_op jit(solution)/shard_map/pallas_call | solution.py:153
  53.8 0.0 collective-permute-done.5.refs_8_
  53.8 0.3 collective-permute-start.10
  54.1 2.0 %shard_map.66.refs_9_ = bf16[1536,512]{1,0:T(8,128)(2,1)} custom-call(s32[3]{0:T(128)S(1)} %copy-done.5, s32[4]{0:T(128)S(1)} %copy-done.6, bf16[1536,512]{1,0:T(8,128)(2,1)S(1)} %copy-done, bf16[1536,512]{1,0:T(8,128)(2,1)S(1)} %collective-permute-done.7.refs_1_, f32[24,1,128]{2,1,0:T(1,128)S(1)} %get-tuple-element.117.refs_2_, ...), custom_call_target="tpu_custom_call", output_to_operand_aliasing={{}: (11, {})} | custom-call | flops 1 | bytes 1 | tf_op jit(solution)/shard_map/pallas_call | solution.py:153
  56.1 5.4 %collective-permute-done.10.refs_8_ = bf16[256,512]{1,0:T(8,128)(2,1)S(1)} collective-permute-done((bf16[256,512]{1,0:T(8,128)(2,1)S(1)}, bf16[256,512]{1,0:T(8,128)(2,1)S(1)}, u32[]{:S(2)}, u32[]{:S(2)}) %collective-permute-start.10) | collective-permute-done | bytes 262176 | tf_op jit(solution)/shard_map/ppermute | solution.py:187
  61.5 1.6 %shard_map.67 = bf16[1536,512]{1,0:T(8,128)(2,1)} custom-call(s32[3]{0:T(128)S(1)} %copy-done.5, s32[4]{0:T(128)S(1)} %copy-done.6, bf16[1536,512]{1,0:T(8,128)(2,1)S(1)} %copy-done, bf16[1536,512]{1,0:T(8,128)(2,1)S(1)} %collective-permute-done.7.refs_1_, f32[24,1,128]{2,1,0:T(1,128)S(1)} %get-tuple-element.117.refs_2_, ...), custom_call_target="tpu_custom_call", output_to_operand_aliasing={{}: (11, {})} | custom-call | flops 1 | bytes 1 | tf_op jit(solution)/shard_map/pallas_call | solution.py:153
  (15 shorter events, 0.0 us)
Async XLA Ops:
  4.5 5.0 %copy-start.4 = (bf16[256,512]{1,0:T(8,128)(2,1)S(1)}, bf16[256,512]{1,0:T(8,128)(2,1)}, u32[]{:S(2)}) copy-start(bf16[256,512]{1,0:T(8,128)(2,1)} %get-tuple-element.67.keep) | copy-start | bytes 786436
  4.5 5.0 %collective-permute-start = (bf16[256,512]{1,0:T(8,128)(2,1)}, bf16[256,512]{1,0:T(8,128)(2,1)S(1)}, u32[]{:S(2)}, u32[]{:S(2)}) collective-permute-start(bf16[256,512]{1,0:T(8,128)(2,1)} %get-tuple-element.68), channel_id=1, source_target_pairs={{0,1},{1,0},{2,3},{3,2},{4,5},{5,4},{6,7},{7,6},{8,9},{9,8},{10,11... | collective-permute-start | bytes 786440 | tf_op jit(solution)/shard_map/ppermute | solution.py:182
  9.6 7.9 %collective-permute-start.2 = (bf16[512,512]{1,0:T(8,128)(2,1)}, bf16[512,512]{1,0:T(8,128)(2,1)S(1)}, u32[]{:S(2)}, u32[]{:S(2)}) collective-permute-start(bf16[512,512]{1,0:T(8,128)(2,1)} %get-tuple-element.75), channel_id=1, source_target_pairs={{0,1},{1,0},{2,3},{3,2},{4,5},{5,4},{6,7},{7,6},{8,9},{9,8},{10,11... | collective-permute-start | bytes 1572872 | tf_op jit(solution)/shard_map/ppermute | solution.py:182
  9.8 9.4 %collective-permute-start.1 = (bf16[256,512]{1,0:T(8,128)(2,1)S(1)}, bf16[256,512]{1,0:T(8,128)(2,1)S(1)}, u32[]{:S(2)}, u32[]{:S(2)}) collective-permute-start(bf16[256,512]{1,0:T(8,128)(2,1)S(1)} %shard_map.56), channel_id=1, source_target_pairs={{0,2},{1,3},{2,0},{3,1},{4,6},{5,7},{6,4},{7,5},{8,10},{9,11},{10,... | collective-permute-start | bytes 786440 | tf_op jit(solution)/shard_map/ppermute | solution.py:187
  12.7 4.7 %copy-start.2 = (bf16[512,512]{1,0:T(8,128)(2,1)S(1)}, bf16[512,512]{1,0:T(8,128)(2,1)}, u32[]{:S(2)}) copy-start(bf16[512,512]{1,0:T(8,128)(2,1)} %get-tuple-element.74.keep) | copy-start | bytes 1572868
  19.3 16.1 %collective-permute-start.4 = (bf16[512,512]{1,0:T(8,128)(2,1)}, bf16[512,512]{1,0:T(8,128)(2,1)S(1)}, u32[]{:S(2)}, u32[]{:S(2)}) collective-permute-start(bf16[512,512]{1,0:T(8,128)(2,1)} %get-tuple-element.83), channel_id=1, source_target_pairs={{0,1},{1,0},{2,3},{3,2},{4,5},{5,4},{6,7},{7,6},{8,9},{9,8},{10,11... | collective-permute-start | bytes 1572872 | tf_op jit(solution)/shard_map/ppermute | solution.py:182
  19.3 16.2 %collective-permute-start.3 = (bf16[512,512]{1,0:T(8,128)(2,1)S(1)}, bf16[512,512]{1,0:T(8,128)(2,1)S(1)}, u32[]{:S(2)}, u32[]{:S(2)}) collective-permute-start(bf16[512,512]{1,0:T(8,128)(2,1)S(1)} %shard_map.58), channel_id=1, source_target_pairs={{0,2},{1,3},{2,0},{3,1},{4,6},{5,7},{6,4},{7,5},{8,10},{9,11},{10,... | collective-permute-start | bytes 1572872 | tf_op jit(solution)/shard_map/ppermute | solution.py:187
  29.5 4.0 %copy-start.9 = (s32[4]{0:T(128)S(1)}, s32[4]{0:T(128)}, u32[]{:S(2)}) copy-start(s32[4]{0:T(128)} %param.9) | copy-start | bytes 52
  29.5 5.8 %copy-start.1 = (bf16[512,512]{1,0:T(8,128)(2,1)S(1)}, bf16[512,512]{1,0:T(8,128)(2,1)}, u32[]{:S(2)}) copy-start(bf16[512,512]{1,0:T(8,128)(2,1)} %get-tuple-element.82.keep) | copy-start | bytes 1572868
  29.5 6.0 %copy-start.8 = (bf16[1536,512]{1,0:T(8,128)(2,1)S(1)}, bf16[1536,512]{1,0:T(8,128)(2,1)}, u32[]{:S(2)}) copy-start(bf16[1536,512]{1,0:T(8,128)(2,1)} %get-tuple-element.96) | copy-start | bytes 4718596
  33.5 2.6 %copy-start.7 = (f32[12,128]{1,0:T(8,128)S(1)}, f32[12,128]{1,0:T(8,128)}, u32[]{:S(2)}) copy-start(f32[12,128]{1,0:T(8,128)} %get-tuple-element.97) | copy-start | bytes 18436
  33.5 16.6 %copy-start = (bf16[1536,512]{1,0:T(8,128)(2,1)S(1)}, bf16[1536,512]{1,0:T(8,128)(2,1)}, u32[]{:S(2)}) copy-start(bf16[1536,512]{1,0:T(8,128)(2,1)} %get-tuple-element.115.refs_0_.refs_9_) | copy-start | bytes 4718596
  33.5 16.6 %copy-start.5 = (s32[3]{0:T(128)S(1)}, s32[3]{0:T(128)}, u32[]{:S(2)}) copy-start(s32[3]{0:T(128)} %get-tuple-element.87.place) | copy-start | bytes 40
  33.5 16.6 %copy-start.6 = (s32[4]{0:T(128)S(1)}, s32[4]{0:T(128)}, u32[]{:S(2)}) copy-start(s32[4]{0:T(128)} %live.7) | copy-start | bytes 52
  35.5 14.6 %collective-permute-start.7 = (bf16[1536,512]{1,0:T(8,128)(2,1)S(1)}, bf16[1536,512]{1,0:T(8,128)(2,1)S(1)}, u32[]{:S(2)}, u32[]{:S(2)}) collective-permute-start(bf16[1536,512]{1,0:T(8,128)(2,1)S(1)} %copy-done.8), channel_id=1, source_target_pairs={{0,1},{1,0},{2,3},{3,2},{4,5},{5,4},{6,7},{7,6},{8,9},{9,8},{10,11... | collective-permute-start | bytes 4718600 | tf_op jit(solution)/shard_map/ppermute | solution.py:191
  35.8 18.0 %collective-permute-start.5 = (bf16[512,512]{1,0:T(8,128)(2,1)S(1)}, bf16[512,512]{1,0:T(8,128)(2,1)S(1)}, u32[]{:S(2)}, u32[]{:S(2)}) collective-permute-start(bf16[512,512]{1,0:T(8,128)(2,1)S(1)} %shard_map.60), channel_id=1, source_target_pairs={{0,2},{1,3},{2,0},{3,1},{4,6},{5,7},{6,4},{7,5},{8,10},{9,11},{10,... | collective-permute-start | bytes 1572872 | tf_op jit(solution)/shard_map/ppermute | solution.py:187
  36.1 3.5 %collective-permute-start.6 = (bf16[256,512]{1,0:T(8,128)(2,1)}, bf16[256,512]{1,0:T(8,128)(2,1)S(1)}, u32[]{:S(2)}, u32[]{:S(2)}) collective-permute-start(bf16[256,512]{1,0:T(8,128)(2,1)} %get-tuple-element.94), channel_id=1, source_target_pairs={{0,1},{1,0},{2,3},{3,2},{4,5},{5,4},{6,7},{7,6},{8,9},{9,8},{10,11... | collective-permute-start | bytes 786440 | tf_op jit(solution)/shard_map/ppermute | solution.py:182
  36.1 2.9 %collective-permute-start.8 = (f32[12,128]{1,0:T(8,128)S(1)}, f32[12,128]{1,0:T(8,128)S(1)}, u32[]{:S(2)}, u32[]{:S(2)}) collective-permute-start(f32[12,128]{1,0:T(8,128)S(1)} %copy-done.7), channel_id=1, source_target_pairs={{0,1},{1,0},{2,3},{3,2},{4,5},{5,4},{6,7},{7,6},{8,9},{9,8},{10,11... | collective-permute-start | bytes 18440 | tf_op jit(solution)/shard_map/ppermute | solution.py:192
  39.0 11.1 %collective-permute-start.9 = (f32[12,128]{1,0:T(8,128)S(1)}, f32[12,128]{1,0:T(8,128)S(1)}, u32[]{:S(2)}, u32[]{:S(2)}) collective-permute-start(f32[12,128]{1,0:T(8,128)S(1)} %add.36.refs_6_), channel_id=1, source_target_pairs={{0,2},{1,3},{2,0},{3,1},{4,6},{5,7},{6,4},{7,5},{8,10},{9,11},{10,... | collective-permute-start | bytes 18440 | tf_op jit(solution)/shard_map/ppermute | solution.py:193
  39.6 1.0 %copy-start.3 = (bf16[256,512]{1,0:T(8,128)(2,1)S(1)}, bf16[256,512]{1,0:T(8,128)(2,1)}, u32[]{:S(2)}) copy-start(bf16[256,512]{1,0:T(8,128)(2,1)} %get-tuple-element.93.keep) | copy-start | bytes 786436
  53.8 7.7 %collective-permute-start.10 = (bf16[256,512]{1,0:T(8,128)(2,1)S(1)}, bf16[256,512]{1,0:T(8,128)(2,1)S(1)}, u32[]{:S(2)}, u32[]{:S(2)}) collective-permute-start(bf16[256,512]{1,0:T(8,128)(2,1)S(1)} %shard_map.63), channel_id=1, source_target_pairs={{0,2},{1,3},{2,0},{3,1},{4,6},{5,7},{6,4},{7,5},{8,10},{9,11},{10,... | collective-permute-start | bytes 786440 | tf_op jit(solution)/shard_map/ppermute | solution.py:187

commit v4 on v3

--- a/solution.py
+++ b/solution.py
@@ -31,23 +31,76 @@
     return total
 
 
-def product_kernel(with_squares, place, rows_ref, gain_ref, keep_weight, send_weight, keep, send, *squares):
-    scaled = rows_ref[...] * gain_ref[...].reshape(1, gain_ref.shape[0])
-    send[...] = jnp.dot(scaled, send_weight[...], preferred_element_type=jnp.float32).astype(send.dtype)
-    keep[...] = jnp.dot(scaled, keep_weight[...], preferred_element_type=jnp.float32).astype(keep.dtype)
-    if with_squares:
-        total = square_sums(rows_ref[...])
-        for part in range(TILE // LANES):
-            turned = jnp.transpose(total[part * LANES : (part + 1) * LANES])
-            row = pl.program_id(0) * (TILE // LANES) + part
-            squares[0][pl.ds(row, 1), :] = jnp.sum(turned, axis=0, keepdims=True)
+def product_kernel(step, chip_count, chunks, with_squares, tokens, gain, weight, *refs):
+    outs = refs[: 2 * len(chunks)]
+    squares = refs[2 * len(chunks)] if with_squares else None
+    rows_buf, weight_buf, gain_buf, weight_sems, row_sems, gain_sem = refs[-6:]
+    depth, width = weight_buf.shape
+    me = lax.axis_index("tensor")
+    chip = lax.rem(lax.div(me, 2) + step, chip_count)
+    core = lax.rem(me, 2)
+    place = pl.ds(pl.multiple_of(chip * width, width), width)
+    cuts = weight_sems.shape[0]
+    cut = depth // cuts
+
+    copies = [pltpu.make_async_copy(gain, gain_buf, gain_sem)]
+    weight_copies = [
+        pltpu.make_async_copy(
+            weight.at[pl.ds(index * cut, cut), place],
+            weight_buf.at[pl.ds(index * cut, cut), :],
+            weight_sems.at[index],
+        )
+        for index in range(cuts)
+    ]
+    row_copies, at = [], 0
+    for index, (first, count) in enumerate(chunks):
+        row_copies.append(
+            pltpu.make_async_copy(
+                tokens.at[pl.ds(first * TILE, count * TILE), :],
+                rows_buf.at[pl.ds(at, count * TILE), :],
+                row_sems.at[index],
+            )
+        )
+        at += count * TILE
+    for copy in copies + row_copies[:1] + weight_copies + row_copies[1:]:
+        copy.start()
+
+    copies[0].wait()
+    gains = gain_buf[...].reshape(1, depth)
+    at = 0
+    for index, (first, count) in enumerate(chunks):
+        row_copies[index].wait()
+        for tile in range(count):
+            rows = rows_buf[pl.ds(at, TILE), :]
+            scaled = rows * gains
+            if index == 0 and tile == 0:
+                product = jnp.zeros((TILE, width), jnp.float32)
+                for part in range(cuts):
+                    weight_copies[part].wait()
+                    span = slice(part * cut, (part + 1) * cut)
+                    product += jnp.dot(
+                        scaled[:, span], weight_buf[span, :], preferred_element_type=jnp.float32
+                    )
+            else:
+                product = jnp.dot(scaled, weight_buf[...], preferred_element_type=jnp.float32)
+            left = product[:, : width // 2].astype(jnp.bfloat16)
+            right = product[:, width // 2 :].astype(jnp.bfloat16)
+            inside = pl.ds(tile * TILE, TILE)
+            outs[2 * index][inside, :] = jnp.where(core == 0, left, right)
+            outs[2 * index + 1][inside, :] = jnp.where(core == 0, right, left)
+            if with_squares:
+                total = square_sums(rows)
+                for part in range(TILE // LANES):
+                    turned = jnp.transpose(total[part * LANES : (part + 1) * LANES])
+                    squares[pl.ds(at // LANES + part, 1), :] = jnp.sum(turned, axis=0, keepdims=True)
+            at += TILE
 
 
 def add_kernel(keep, received, out):
     out[...] = (keep[...].astype(jnp.float32) + received[...].astype(jnp.float32)).astype(out.dtype)
 
 
-def finish_kernel(first_tile, chip_count, model_dim, place, live, *refs):
+def finish_kernel(first_tile, chip_count, model_dim, live, *refs):
     keep, received, far_cos, far_sin, near_cos, near_sin = refs[:6]
     squares, arrived, out = refs[6 : 6 + chip_count], refs[6 + chip_count : -2], refs[-1]
     values = keep[...].astype(jnp.float32) + received[...].astype(jnp.float32)
@@ -64,7 +117,7 @@
         columns.append(jnp.sum(jnp.where(on_diagonal, totals, 0.0), axis=1, keepdims=True))
     scales = 1.0 / jnp.sqrt(jnp.concatenate(columns, axis=0) / model_dim + norm_eps)
     row = tile * TILE + lax.broadcasted_iota(jnp.int32, (TILE, 1), 0)
-    alive = row < live[place[2]] * BLOCK
+    alive = row < live[lax.axis_index("serve")] * BLOCK
     sign = jnp.where(lax.broadcasted_iota(jnp.int32, (1, HD), 1) < HD // 2, -1.0, 1.0)
     cosines, sines = [], []
     for part in range(TILE // BLOCK):
@@ -97,34 +150,30 @@
     def shift(step):
         return [(i, (i + 2 * step) % tensor_count) for i in range(tensor_count)]
 
-    def place_of(step):
-        keep = (me + 2 * step) % tensor_count
-        return jnp.stack([keep, keep ^ 1, own_index]).astype(jnp.int32)
-
-    def product(place, first, count, with_squares):
-        rows = count * TILE
-        out_shape = [jax.ShapeDtypeStruct((rows, columns), jnp.bfloat16)] * 2
-        out_specs = [pl.BlockSpec((TILE, columns), lambda i, *_: (i, 0))] * 2
+    def product(gain, step, chunks, with_squares):
+        rows = [count * TILE for _, count in chunks]
+        out_shape = [
+            jax.ShapeDtypeStruct((size, columns), jnp.bfloat16) for size in rows for _ in range(2)
+        ]
         if with_squares:
-            out_shape.append(jax.ShapeDtypeStruct((rows // LANES, LANES), jnp.float32))
-            out_specs.append(pl.BlockSpec((rows // LANES, LANES), lambda i, *_: (0, 0)))
-        return pl.pallas_call(
-            functools.partial(product_kernel, with_squares),
-            grid_spec=pltpu.PrefetchScalarGridSpec(
-                num_scalar_prefetch=1,
-                grid=(count,),
-                in_specs=[
-                    pl.BlockSpec((TILE, depth), lambda i, *_: (first + i, 0)),
-                    pl.BlockSpec((depth,), lambda i, *_: (0,)),
-                    pl.BlockSpec((depth, columns), lambda i, where: (0, where[0])),
-                    pl.BlockSpec((depth, columns), lambda i, where: (0, where[1])),
-                ],
-                out_specs=out_specs,
-            ),
+            out_shape.append(jax.ShapeDtypeStruct((sum(rows) // LANES, LANES), jnp.float32))
+        made = pl.pallas_call(
+            functools.partial(product_kernel, step, chip_count, chunks, with_squares),
+            in_specs=[pl.BlockSpec(memory_space=pl.ANY)] * 3,
             out_shape=out_shape,
+            scratch_shapes=[
+                pltpu.VMEM((sum(rows), depth), jnp.bfloat16),
+                pltpu.VMEM((depth, 2 * columns), jnp.bfloat16),
+                pltpu.VMEM((depth,), jnp.bfloat16),
+                pltpu.SemaphoreType.DMA((4,)),
+                pltpu.SemaphoreType.DMA((len(chunks),)),
+                pltpu.SemaphoreType.DMA,
+            ],
             compiler_params=WIDE,
             cost_estimate=COST,
-        )(place, tokens, norm_gain, kv_weight, kv_weight)
+        )(tokens, gain, kv_weight)
+        pairs = [(made[2 * index], made[2 * index + 1]) for index in range(len(chunks))]
+        return (pairs, made[-1]) if with_squares else pairs
 
     def tables(offset):
         half = HD // 2
@@ -149,11 +198,11 @@
             result = keep
             aliases = {}
         else:
-            aliases = {2 + len(operands): 0}
+            aliases = {1 + len(operands): 0}
         return pl.pallas_call(
             functools.partial(finish_kernel, first, chip_count, model_dim),
             grid_spec=pltpu.PrefetchScalarGridSpec(
-                num_scalar_prefetch=2,
+                num_scalar_prefetch=1,
                 grid=(count,),
                 in_specs=specs + [pl.BlockSpec(memory_space=pl.ANY)],
                 out_specs=pl.BlockSpec((TILE, columns), lambda i, *_: (first + i, 0)),
@@ -162,15 +211,16 @@
             input_output_aliases=aliases,
             compiler_params=PARAMS,
             cost_estimate=COST,
-        )(place_of(0), live_blocks, *operands, result)
+        )(live_blocks, *operands, result)
 
     others = range(1, chip_count)
     firsts = [sum(CHUNKS[:index]) for index in range(len(CHUNKS))]
     chunk_count = len(CHUNKS)
-    places = {step: place_of(step) for step in range(chip_count)}
-
-    def start_chunk(index):
-        return [product(places[step], firsts[index], CHUNKS[index], False) for step in others]
+
+    def start_chunks(gain, wanted):
+        chunks = [(firsts[index], CHUNKS[index]) for index in wanted]
+        made = [product(gain, step, chunks, False) for step in others]
+        return [[per_step[index] for per_step in made] for index in range(len(wanted))]
 
     def add_halves(made):
         return [
@@ -186,37 +236,35 @@
     def cross(sums):
         return [lax.ppermute(part, "tensor", shift(step)) for step, part in zip(others, sums)]
 
-    def own_inputs(own, table):
-        keep, send, own_squares = own
-        received = lax.ppermute(send, "tensor", swap)
-        pair_squares = own_squares + lax.ppermute(own_squares, "tensor", swap)
-        squares = [pair_squares] + [lax.ppermute(pair_squares, "tensor", shift(step)) for step in others]
-        return [keep, received, table, squares]
-
     hold = lax.optimization_barrier
-    arrivals = []
+    gain, arrivals = norm_gain, []
     own, inputs, result, finished = None, None, None, 0
-    made = start_chunk(0)
-    made, places = hold((made, places))
+    (made,) = start_chunks(gain, [0])
+    made, gain = hold((made, gain))
     sums = add_halves(made)
-    made = start_chunk(1)
-    sums, made, places, span_offset = hold((sums, made, places, span_offset))
+    waiting = start_chunks(gain, [1])
+    sums, waiting, gain, span_offset = hold((sums, waiting, gain, span_offset))
     for stage in range(1, chunk_count + 1):
         arrived = cross(sums)
         if stage < chunk_count:
-            sums = add_halves(made)
-        if stage + 1 < chunk_count:
-            made = start_chunk(stage + 1)
+            sums = add_halves(waiting.pop(0))
+        if stage == 1:
+            waiting += start_chunks(gain, list(range(2, chunk_count)))
         if stage == 2:
-            own = product(places[0], 0, tiles, True), tables(span_offset[own_index])
+            ((keep, send),), squares = product(gain, 0, [(0, tiles)], True)
+            squares += lax.ppermute(squares, "tensor", swap)
+            own = keep, send, squares, tables(span_offset[own_index])
         if stage == 3:
-            inputs = own_inputs(*own)
-        if stage >= 3:
+            keep, send, squares, table = own
+            received = lax.ppermute(send, "tensor", swap)
+            squares = [squares] + [lax.ppermute(squares, "tensor", shift(step)) for step in others]
+            inputs = keep, received, table, squares
+        if stage >= 4:
             for index in range(finished, stage - 1):
                 result = finish(firsts[index], CHUNKS[index], *inputs, arrivals[index], result)
             finished = stage - 1
-        arrived, sums, made, places, span_offset, own, inputs, result = hold(
-            (arrived, sums, made, places, span_offset, own, inputs, result)
+        arrived, sums, waiting, gain, span_offset, own, inputs, result = hold(
+            (arrived, sums, waiting, gain, span_offset, own, inputs, result)
         )
         arrivals.append(arrived)
     for index in range(finished, chunk_count):

time: 63.5 us -> 55.9 us (0.88)
  Pallas kernels: 33.1 us -> 27 us
  waiting for transfers between devices: 19 us -> 16.1 us
  starting transfers between devices: 7.14 us -> 9.61 us
  local copies, waits for them, and re-layouts: 1.66 us -> 0.71 us
    pallas_call x5 -> x4, Pallas kernels: 25.4 us -> 19.3 us  [product(): pl.pallas_call(functools.partial(product_kernel, step, chip_count, chunks...]
    ppermute x4, waiting for transfers between devices: 7.05 us -> 3.9 us  [cross(): lax.ppermute(part, 'tensor', shift(step))]
    ppermute x4, starting transfers between devices: 5.12 us -> 8.16 us  [cross(): lax.ppermute(part, 'tensor', shift(step))]
    ppermute x4, waiting for transfers between devices: 0.06 us -> 1.53 us  [add_halves(): lax.ppermute(send, 'tensor', swap)]
    ppermute x3, waiting for transfers between devices: 11.9 us -> 10.7 us  [the longest x1 10.7 us: shards(): lax.ppermute(squares, 'tensor', shift(step))]
    unnamed x20 -> x18, local copies, waits for them, and re-layouts: 0.99 us -> 0.05 us
    ppermute x3, starting transfers between devices: 1.31 us -> 0.58 us  [the longest x1 0.29 us: shards(): squares += lax.ppermute(squares, 'tensor', swap)]
    add x1, other arithmetic: 0.01 us -> 0.7 us  [shards(): squares += lax.ppermute(squares, 'tensor', swap)]
  transfers between devices with their start and end apart: 11 -> 11, of which waited for: 5 -> 5; matrix products, arithmetic and copies ran while one was open for 2% -> 4% of each run, Pallas kernels for 44% -> 40%
where the time goes in v4:
time: 55.9 us; the launch traced here: 55.7 us
  Pallas kernels  27 us (48%)
  waiting for transfers between devices  16.1 us (29%)
  starting transfers between devices  9.61 us (17%)
  other arithmetic  1.35 us (2%)
  between operations  0.88 us (2%)
  local copies, waits for them, and re-layouts  0.71 us (1%)
    pallas_call x4, Pallas kernels, product(): pl.pallas_call(functools.partial(product_kernel, step, chip_count, chunks...  19.3 us
    ppermute x1, waiting for transfers between devices, shards(): lax.ppermute(squares, 'tensor', shift(step))  10.7 us
    ppermute x4, starting transfers between devices, cross(): lax.ppermute(part, 'tensor', shift(step))  8.16 us
    pallas_call x4, Pallas kernels, finish(): pl.pallas_call(functools.partial(finish_kernel, first, chip_count, model_...  7.35 us
    ppermute x4, waiting for transfers between devices, cross(): lax.ppermute(part, 'tensor', shift(step))  3.9 us
    ppermute x4, waiting for transfers between devices, add_halves(): lax.ppermute(send, 'tensor', swap)  1.53 us
  transfers between devices with their start and end apart: 11, of which 5 were waited for; matrix products, arithmetic and copies ran while one was open for 4% of the time, Pallas kernels for 40%

profile of v4, /device:TPU:0, one launch (start us, length us, event | category | flops | bytes accessed | tf_op | source)
XLA Modules:
  0.0 55.7 jit_solution(17394972938212620207)
XLA Ops:
  0.0 3.0 %shard_map.55 = (bf16[256,512]{1,0:T(8,128)(2,1)}, bf16[256,512]{1,0:T(8,128)(2,1)}) custom-call(bf16[1536,1024]{1,0:T(8,128)(2,1)} %tokens.7, bf16[1024]{0:T(1024)(128)(2,1)} %gain.4, bf16[1024,2048]{1,0:T(8,128)(2,1)} %weight.7), custom_call_target="tpu_custom_call" | custom-call | flops 1 | bytes 1 | tf_op jit(solution)/shard_map/pallas_call | solution.py:160
  3.0 0.0 copy-start.4
  3.0 0.5 collective-permute-start
  3.6 4.0 %shard_map.57 = (bf16[512,512]{1,0:T(8,128)(2,1)}, bf16[512,512]{1,0:T(8,128)(2,1)}) custom-call(bf16[1536,1024]{1,0:T(8,128)(2,1)} %tokens.7, bf16[1024]{0:T(1024)(128)(2,1)} %gain.4, bf16[1024,2048]{1,0:T(8,128)(2,1)} %weight.7), custom_call_target="tpu_custom_call" | custom-call | flops 1 | bytes 1 | tf_op jit(solution)/shard_map/pallas_call | solution.py:160
  7.5 0.0 collective-permute-done.received
  7.5 0.0 copy-done.4
  7.5 0.1 shard_map.56
  7.6 0.1 collective-permute-start.2
  7.7 2.9 %collective-permute-start.1 = (bf16[256,512]{1,0:T(8,128)(2,1)S(1)}, bf16[256,512]{1,0:T(8,128)(2,1)S(1)}, u32[]{:S(2)}, u32[]{:S(2)}) collective-permute-start(bf16[256,512]{1,0:T(8,128)(2,1)S(1)} %shard_map.56), channel_id=1, source_target_pairs={{0,2},{1,3},{2,0},{3,1},{4,6},{5,7},{6,4},{7,5},{8,10},{9,11},{10,... | collective-permute-start | bytes 786440 | tf_op jit(solution)/shard_map/ppermute | solution.py:237
  10.7 0.1 pad_maximum_fusion
  10.8 4.5 %shard_map.59 = (bf16[512,512]{1,0:T(8,128)(2,1)}, bf16[512,512]{1,0:T(8,128)(2,1)}, bf16[256,512]{1,0:T(8,128)(2,1)}, bf16[256,512]{1,0:T(8,128)(2,1)}) custom-call(bf16[1536,1024]{1,0:T(8,128)(2,1)} %tokens.7, bf16[1024]{0:T(1024)(128)(2,1)} %gain.4, bf16[1024,2048]{1,0:T(8,128)(2,1)} %weight.7), custom_call_target="tpu_custom_call" | custom-call | flops 1 | bytes 1 | tf_op jit(solution)/shard_map/pallas_call | solution.py:160
  15.3 0.0 copy-start.6
  15.3 0.0 collective-permute-done.2.received
  15.3 0.0 copy-done.2
  15.3 0.1 shard_map.58
  15.5 1.8 %collective-permute-done.1.refs_8_ = bf16[256,512]{1,0:T(8,128)(2,1)S(1)} collective-permute-done((bf16[256,512]{1,0:T(8,128)(2,1)S(1)}, bf16[256,512]{1,0:T(8,128)(2,1)S(1)}, u32[]{:S(2)}, u32[]{:S(2)}) %collective-permute-start.1) | collective-permute-done | bytes 262176 | tf_op jit(solution)/shard_map/ppermute | solution.py:237
  17.2 0.0 copy-done.6
  17.2 0.0 collective-permute-start.4
  17.2 1.7 %collective-permute-start.3 = (bf16[512,512]{1,0:T(8,128)(2,1)S(1)}, bf16[512,512]{1,0:T(8,128)(2,1)S(1)}, u32[]{:S(2)}, u32[]{:S(2)}) collective-permute-start(bf16[512,512]{1,0:T(8,128)(2,1)S(1)} %shard_map.58), channel_id=1, source_target_pairs={{0,2},{1,3},{2,0},{3,1},{4,6},{5,7},{6,4},{7,5},{8,10},{9,11},{10,... | collective-permute-start | bytes 1572872 | tf_op jit(solution)/shard_map/ppermute | solution.py:237
  19.0 0.1 fusion
  19.1 0.0 copy-start.8
  19.1 0.0 copy-start.1
  19.2 7.8 %shard_map.61 = (bf16[1536,512]{1,0:T(8,128)(2,1)}, bf16[1536,512]{1,0:T(8,128)(2,1)}, f32[12,128]{1,0:T(8,128)}) custom-call(bf16[1536,1024]{1,0:T(8,128)(2,1)} %tokens.7, bf16[1024]{0:T(1024)(128)(2,1)} %gain.4, bf16[1024,2048]{1,0:T(8,128)(2,1)} %weight.7), custom_call_target="tpu_custom_call" | custom-call | flops 1 | bytes 1 | tf_op jit(solution)/shard_map/pallas_call | solution.py:160
  27.0 0.0 copy-start
  27.0 0.0 copy-start.5
  27.0 0.3 collective-permute-start.5
  27.3 0.7 %dynamic_slice.3 = s32[1]{0:T(128)} dynamic-slice(s32[4]{0:T(128)S(1)} %copy-done.8, s32[]{:T(128)S(6)} %select_n.3), dynamic_slice_sizes={1} | dynamic-slice | bytes 12 | tf_op jit(solution)/shard_map/dynamic_slice | solution.py:256
  28.6 0.4 multiply_sine_fusion
  29.1 0.0 collective-permute-done.5
  29.1 0.7 %add.16.refs_6_ = f32[12,128]{1,0:T(8,128)S(1)} add(f32[12,128]{1,0:T(8,128)} %get-tuple-element.88, f32[12,128]{1,0:T(8,128)S(1)} %collective-permute-done.5) | non-fusion elementwise | flops 1536 | bytes 18432 | tf_op jit(solution)/shard_map/add | solution.py:255
  29.8 0.0 collective-permute-done.4.received
  29.8 0.1 shard_map.60
  29.9 1.7 %collective-permute-done.3.refs_8_ = bf16[512,512]{1,0:T(8,128)(2,1)S(1)} collective-permute-done((bf16[512,512]{1,0:T(8,128)(2,1)S(1)}, bf16[512,512]{1,0:T(8,128)(2,1)S(1)}, u32[]{:S(2)}, u32[]{:S(2)}) %collective-permute-start.3) | collective-permute-done | bytes 524320 | tf_op jit(solution)/shard_map/ppermute | solution.py:237
  31.6 0.0 collective-permute-start.8
  31.6 1.7 %collective-permute-start.6 = (bf16[512,512]{1,0:T(8,128)(2,1)S(1)}, bf16[512,512]{1,0:T(8,128)(2,1)S(1)}, u32[]{:S(2)}, u32[]{:S(2)}) collective-permute-start(bf16[512,512]{1,0:T(8,128)(2,1)S(1)} %shard_map.60), channel_id=1, source_target_pairs={{0,2},{1,3},{2,0},{3,1},{4,6},{5,7},{6,4},{7,5},{8,10},{9,11},{10,... | collective-permute-start | bytes 1572872 | tf_op jit(solution)/shard_map/ppermute | solution.py:237
  33.3 0.2 collective-permute-start.7
  33.5 0.3 collective-permute-start.9
  33.8 1.5 %collective-permute-done.7.received = bf16[256,512]{1,0:T(8,128)(2,1)S(1)} collective-permute-done((bf16[256,512]{1,0:T(8,128)(2,1)S(1)}, bf16[256,512]{1,0:T(8,128)(2,1)S(1)}, u32[]{:S(2)}, u32[]{:S(2)}) %collective-permute-start.7) | collective-permute-done | bytes 262176 | tf_op jit(solution)/shard_map/ppermute | solution.py:232
  35.4 0.1 shard_map.62
  35.4 10.7 %collective-permute-done.9.refs_7_ = f32[12,128]{1,0:T(8,128)S(1)} collective-permute-done((f32[12,128]{1,0:T(8,128)S(1)}, f32[12,128]{1,0:T(8,128)S(1)}, u32[]{:S(2)}, u32[]{:S(2)}) %collective-permute-start.9) | collective-permute-done | bytes 6176 | tf_op jit(solution)/shard_map/ppermute | solution.py:260
  46.1 0.0 collective-permute-done.6.refs_8_
  46.1 0.0 collective-permute-done.8.refs_1_
  46.1 1.7 %collective-permute-start.10 = (bf16[256,512]{1,0:T(8,128)(2,1)S(1)}, bf16[256,512]{1,0:T(8,128)(2,1)S(1)}, u32[]{:S(2)}, u32[]{:S(2)}) collective-permute-start(bf16[256,512]{1,0:T(8,128)(2,1)S(1)} %shard_map.62), channel_id=1, source_target_pairs={{0,2},{1,3},{2,0},{3,1},{4,6},{5,7},{6,4},{7,5},{8,10},{9,11},{10,... | collective-permute-start | bytes 786440 | tf_op jit(solution)/shard_map/ppermute | solution.py:237
  47.8 1.6 %shard_map.63.refs_9_ = bf16[1536,512]{1,0:T(8,128)(2,1)} custom-call(s32[4]{0:T(128)S(1)} %copy-done.5, bf16[1536,512]{1,0:T(8,128)(2,1)S(1)} %copy-done, bf16[1536,512]{1,0:T(8,128)(2,1)S(1)} %collective-permute-done.8.refs_1_, f32[24,1,128]{2,1,0:T(1,128)S(1)} %get-tuple-element.113.refs_2_, f32[24,1,128]{2,1,0:T(1,128)S(1)} %get-tuple-element.114.refs_3_, ...), custom_call_target="tpu_custom_call" | custom-call | flops 1 | bytes 1 | tf_op jit(solution)/shard_map/pallas_call | solution.py:202
  49.5 2.0 %shard_map.64.refs_9_ = bf16[1536,512]{1,0:T(8,128)(2,1)} custom-call(s32[4]{0:T(128)S(1)} %copy-done.5, bf16[1536,512]{1,0:T(8,128)(2,1)S(1)} %copy-done, bf16[1536,512]{1,0:T(8,128)(2,1)S(1)} %collective-permute-done.8.refs_1_, f32[24,1,128]{2,1,0:T(1,128)S(1)} %get-tuple-element.113.refs_2_, ...), custom_call_target="tpu_custom_call", output_to_operand_aliasing={{}: (10, {})} | custom-call | flops 1 | bytes 1 | tf_op jit(solution)/shard_map/pallas_call | solution.py:202
  51.5 2.0 %shard_map.65.refs_9_ = bf16[1536,512]{1,0:T(8,128)(2,1)} custom-call(s32[4]{0:T(128)S(1)} %copy-done.5, bf16[1536,512]{1,0:T(8,128)(2,1)S(1)} %copy-done, bf16[1536,512]{1,0:T(8,128)(2,1)S(1)} %collective-permute-done.8.refs_1_, f32[24,1,128]{2,1,0:T(1,128)S(1)} %get-tuple-element.113.refs_2_, ...), custom_call_target="tpu_custom_call", output_to_operand_aliasing={{}: (10, {})} | custom-call | flops 1 | bytes 1 | tf_op jit(solution)/shard_map/pallas_call | solution.py:202
  53.5 0.5 collective-permute-done.10.refs_8_
  54.0 1.6 %shard_map.66 = bf16[1536,512]{1,0:T(8,128)(2,1)} custom-call(s32[4]{0:T(128)S(1)} %copy-done.5, bf16[1536,512]{1,0:T(8,128)(2,1)S(1)} %copy-done, bf16[1536,512]{1,0:T(8,128)(2,1)S(1)} %collective-permute-done.8.refs_1_, f32[24,1,128]{2,1,0:T(1,128)S(1)} %get-tuple-element.113.refs_2_, ...), custom_call_target="tpu_custom_call", output_to_operand_aliasing={{}: (10, {})} | custom-call | flops 1 | bytes 1 | tf_op jit(solution)/shard_map/pallas_call | solution.py:202
  (11 shorter events, 0.0 us)
Async XLA Ops:
  3.0 4.5 %copy-start.4 = (bf16[256,512]{1,0:T(8,128)(2,1)S(1)}, bf16[256,512]{1,0:T(8,128)(2,1)}, u32[]{:S(2)}) copy-start(bf16[256,512]{1,0:T(8,128)(2,1)} %get-tuple-element.65.keep) | copy-start | bytes 786436
  3.0 4.5 %collective-permute-start = (bf16[256,512]{1,0:T(8,128)(2,1)}, bf16[256,512]{1,0:T(8,128)(2,1)S(1)}, u32[]{:S(2)}, u32[]{:S(2)}) collective-permute-start(bf16[256,512]{1,0:T(8,128)(2,1)} %get-tuple-element.66), channel_id=1, source_target_pairs={{0,1},{1,0},{2,3},{3,2},{4,5},{5,4},{6,7},{7,6},{8,9},{9,8},{10,11... | collective-permute-start | bytes 786440 | tf_op jit(solution)/shard_map/ppermute | solution.py:232
  7.6 7.7 %collective-permute-start.2 = (bf16[512,512]{1,0:T(8,128)(2,1)}, bf16[512,512]{1,0:T(8,128)(2,1)S(1)}, u32[]{:S(2)}, u32[]{:S(2)}) collective-permute-start(bf16[512,512]{1,0:T(8,128)(2,1)} %get-tuple-element.72), channel_id=1, source_target_pairs={{0,1},{1,0},{2,3},{3,2},{4,5},{5,4},{6,7},{7,6},{8,9},{9,8},{10,11... | collective-permute-start | bytes 1572872 | tf_op jit(solution)/shard_map/ppermute | solution.py:232
  7.7 9.5 %collective-permute-start.1 = (bf16[256,512]{1,0:T(8,128)(2,1)S(1)}, bf16[256,512]{1,0:T(8,128)(2,1)S(1)}, u32[]{:S(2)}, u32[]{:S(2)}) collective-permute-start(bf16[256,512]{1,0:T(8,128)(2,1)S(1)} %shard_map.56), channel_id=1, source_target_pairs={{0,2},{1,3},{2,0},{3,1},{4,6},{5,7},{6,4},{7,5},{8,10},{9,11},{10,... | collective-permute-start | bytes 786440 | tf_op jit(solution)/shard_map/ppermute | solution.py:237
  10.8 4.6 %copy-start.2 = (bf16[512,512]{1,0:T(8,128)(2,1)S(1)}, bf16[512,512]{1,0:T(8,128)(2,1)}, u32[]{:S(2)}) copy-start(bf16[512,512]{1,0:T(8,128)(2,1)} %get-tuple-element.71.keep) | copy-start | bytes 1572868
  15.3 1.9 %copy-start.6 = (bf16[512,512]{1,0:T(8,128)(2,1)S(1)}, bf16[512,512]{1,0:T(8,128)(2,1)}, u32[]{:S(2)}) copy-start(bf16[512,512]{1,0:T(8,128)(2,1)} %get-tuple-element.81) | copy-start | bytes 1572868
  17.2 12.6 %collective-permute-start.4 = (bf16[512,512]{1,0:T(8,128)(2,1)S(1)}, bf16[512,512]{1,0:T(8,128)(2,1)S(1)}, u32[]{:S(2)}, u32[]{:S(2)}) collective-permute-start(bf16[512,512]{1,0:T(8,128)(2,1)S(1)} %copy-done.6), channel_id=1, source_target_pairs={{0,1},{1,0},{2,3},{3,2},{4,5},{5,4},{6,7},{7,6},{8,9},{9,8},{10,11... | collective-permute-start | bytes 1572872 | tf_op jit(solution)/shard_map/ppermute | solution.py:232
  17.2 14.3 %collective-permute-start.3 = (bf16[512,512]{1,0:T(8,128)(2,1)S(1)}, bf16[512,512]{1,0:T(8,128)(2,1)S(1)}, u32[]{:S(2)}, u32[]{:S(2)}) collective-permute-start(bf16[512,512]{1,0:T(8,128)(2,1)S(1)} %shard_map.58), channel_id=1, source_target_pairs={{0,2},{1,3},{2,0},{3,1},{4,6},{5,7},{6,4},{7,5},{8,10},{9,11},{10,... | collective-permute-start | bytes 1572872 | tf_op jit(solution)/shard_map/ppermute | solution.py:237
  19.1 8.2 %copy-start.8 = (s32[4]{0:T(128)S(1)}, s32[4]{0:T(128)}, u32[]{:S(2)}) copy-start(s32[4]{0:T(128)} %param.9) | copy-start | bytes 52
  19.1 10.7 %copy-start.1 = (bf16[512,512]{1,0:T(8,128)(2,1)S(1)}, bf16[512,512]{1,0:T(8,128)(2,1)}, u32[]{:S(2)}) copy-start(bf16[512,512]{1,0:T(8,128)(2,1)} %get-tuple-element.80.keep) | copy-start | bytes 1572868
  19.1 14.2 %copy-start.7 = (bf16[256,512]{1,0:T(8,128)(2,1)S(1)}, bf16[256,512]{1,0:T(8,128)(2,1)}, u32[]{:S(2)}) copy-start(bf16[256,512]{1,0:T(8,128)(2,1)} %get-tuple-element.91) | copy-start | bytes 786436
  19.1 16.2 %copy-start.3 = (bf16[256,512]{1,0:T(8,128)(2,1)S(1)}, bf16[256,512]{1,0:T(8,128)(2,1)}, u32[]{:S(2)}) copy-start(bf16[256,512]{1,0:T(8,128)(2,1)} %get-tuple-element.90.keep) | copy-start | bytes 786436
  27.0 20.9 %copy-start = (bf16[1536,512]{1,0:T(8,128)(2,1)S(1)}, bf16[1536,512]{1,0:T(8,128)(2,1)}, u32[]{:S(2)}) copy-start(bf16[1536,512]{1,0:T(8,128)(2,1)} %get-tuple-element.111.refs_0_.refs_9_) | copy-start | bytes 4718596
  27.0 20.9 %copy-start.5 = (s32[4]{0:T(128)S(1)}, s32[4]{0:T(128)}, u32[]{:S(2)}) copy-start(s32[4]{0:T(128)} %live.7) | copy-start | bytes 52
  27.0 2.1 %collective-permute-start.5 = (f32[12,128]{1,0:T(8,128)}, f32[12,128]{1,0:T(8,128)S(1)}, u32[]{:S(2)}, u32[]{:S(2)}) collective-permute-start(f32[12,128]{1,0:T(8,128)} %get-tuple-element.88), channel_id=1, source_target_pairs={{0,1},{1,0},{2,3},{3,2},{4,5},{5,4},{6,7},{7,6},{8,9},{9,8},{10,11... | collective-permute-start | bytes 18440 | tf_op jit(solution)/shard_map/ppermute | solution.py:255
  31.6 14.5 %collective-permute-start.8 = (bf16[1536,512]{1,0:T(8,128)(2,1)}, bf16[1536,512]{1,0:T(8,128)(2,1)S(1)}, u32[]{:S(2)}, u32[]{:S(2)}) collective-permute-start(bf16[1536,512]{1,0:T(8,128)(2,1)} %get-tuple-element.92), channel_id=1, source_target_pairs={{0,1},{1,0},{2,3},{3,2},{4,5},{5,4},{6,7},{7,6},{8,9},{9,8},{10,11... | collective-permute-start | bytes 4718600 | tf_op jit(solution)/shard_map/ppermute | solution.py:259
  31.6 14.5 %collective-permute-start.6 = (bf16[512,512]{1,0:T(8,128)(2,1)S(1)}, bf16[512,512]{1,0:T(8,128)(2,1)S(1)}, u32[]{:S(2)}, u32[]{:S(2)}) collective-permute-start(bf16[512,512]{1,0:T(8,128)(2,1)S(1)} %shard_map.60), channel_id=1, source_target_pairs={{0,2},{1,3},{2,0},{3,1},{4,6},{5,7},{6,4},{7,5},{8,10},{9,11},{10,... | collective-permute-start | bytes 1572872 | tf_op jit(solution)/shard_map/ppermute | solution.py:237
  33.3 2.0 %collective-permute-start.7 = (bf16[256,512]{1,0:T(8,128)(2,1)S(1)}, bf16[256,512]{1,0:T(8,128)(2,1)S(1)}, u32[]{:S(2)}, u32[]{:S(2)}) collective-permute-start(bf16[256,512]{1,0:T(8,128)(2,1)S(1)} %copy-done.7), channel_id=1, source_target_pairs={{0,1},{1,0},{2,3},{3,2},{4,5},{5,4},{6,7},{7,6},{8,9},{9,8},{10,11... | collective-permute-start | bytes 786440 | tf_op jit(solution)/shard_map/ppermute | solution.py:232
  33.5 12.5 %collective-permute-start.9 = (f32[12,128]{1,0:T(8,128)S(1)}, f32[12,128]{1,0:T(8,128)S(1)}, u32[]{:S(2)}, u32[]{:S(2)}) collective-permute-start(f32[12,128]{1,0:T(8,128)S(1)} %add.16.refs_6_), channel_id=1, source_target_pairs={{0,2},{1,3},{2,0},{3,1},{4,6},{5,7},{6,4},{7,5},{8,10},{9,11},{10,... | collective-permute-start | bytes 18440 | tf_op jit(solution)/shard_map/ppermute | solution.py:260
  46.1 7.9 %collective-permute-start.10 = (bf16[256,512]{1,0:T(8,128)(2,1)S(1)}, bf16[256,512]{1,0:T(8,128)(2,1)S(1)}, u32[]{:S(2)}, u32[]{:S(2)}) collective-permute-start(bf16[256,512]{1,0:T(8,128)(2,1)S(1)} %shard_map.62), channel_id=1, source_target_pairs={{0,2},{1,3},{2,0},{3,1},{4,6},{5,7},{6,4},{7,5},{8,10},{9,11},{10,... | collective-permute-start | bytes 786440 | tf_op jit(solution)/shard_map/ppermute | solution.py:237

commit v5 on v4

--- a/solution.py
+++ b/solution.py
@@ -18,8 +18,8 @@
 TILE = 256
 CHUNKS = (1, 2, 2, 1)
 
-WIDE = pltpu.CompilerParams(vmem_limit_bytes=60 * 1024 * 1024)
 PARAMS = pltpu.CompilerParams(vmem_limit_bytes=16 * 1024 * 1024)
+FIRST = pltpu.CompilerParams(vmem_limit_bytes=48 * 1024 * 1024)
 COST = pl.CostEstimate(flops=1, bytes_accessed=1, transcendentals=0)
 
 
@@ -31,56 +31,67 @@
     return total
 
 
-def product_kernel(step, chip_count, chunks, with_squares, tokens, gain, weight, *refs):
-    outs = refs[: 2 * len(chunks)]
-    squares = refs[2 * len(chunks)] if with_squares else None
-    rows_buf, weight_buf, gain_buf, weight_sems, row_sems, gain_sem = refs[-6:]
+def product_kernel(step, chip_count, chunks, with_squares, load_weight, load_rows, tokens, gain, weight, *refs):
+    outs = list(refs[: 2 * len(chunks)])
+    refs = list(refs[2 * len(chunks) :])
+    squares = refs.pop(0) if with_squares else None
+    weight_buf = refs.pop(0) if load_weight else weight
+    rows_buf = refs.pop(0) if load_rows else tokens
+    gain_buf, weight_sems, row_sems, gain_sem = refs
     depth, width = weight_buf.shape
     me = lax.axis_index("tensor")
-    chip = lax.rem(lax.div(me, 2) + step, chip_count)
     core = lax.rem(me, 2)
-    place = pl.ds(pl.multiple_of(chip * width, width), width)
-    cuts = weight_sems.shape[0]
+    cuts = weight_sems.shape[0] if load_weight else 1
     cut = depth // cuts
 
-    copies = [pltpu.make_async_copy(gain, gain_buf, gain_sem)]
-    weight_copies = [
-        pltpu.make_async_copy(
-            weight.at[pl.ds(index * cut, cut), place],
-            weight_buf.at[pl.ds(index * cut, cut), :],
-            weight_sems.at[index],
-        )
-        for index in range(cuts)
-    ]
-    row_copies, at = [], 0
+    gain_copy = pltpu.make_async_copy(gain, gain_buf, gain_sem)
+    weight_copies = []
+    if load_weight:
+        chip = lax.rem(lax.div(me, 2) + step, chip_count)
+        place = pl.ds(pl.multiple_of(chip * width, width), width)
+        weight_copies = [
+            pltpu.make_async_copy(
+                weight.at[pl.ds(index * cut, cut), place],
+                weight_buf.at[pl.ds(index * cut, cut), :],
+                weight_sems.at[index],
+            )
+            for index in range(cuts)
+        ]
+    row_copies = []
+    if load_rows:
+        first, count = chunks[0]
+        edges = [0, first * TILE, (first + count) * TILE, tokens.shape[0]]
+        row_copies = [
+            pltpu.make_async_copy(
+                tokens.at[pl.ds(low, high - low), :], rows_buf.at[pl.ds(low, high - low), :], row_sems.at[index]
+            )
+            for index, (low, high) in enumerate(zip(edges, edges[1:]))
+            if low < high
+        ]
+        if first:
+            row_copies[:2] = row_copies[1::-1]
+    for copy in [gain_copy] + row_copies[:1] + weight_copies + row_copies[1:]:
+        copy.start()
+
+    gain_copy.wait()
+    gains = gain_buf[...].reshape(1, depth)
     for index, (first, count) in enumerate(chunks):
-        row_copies.append(
-            pltpu.make_async_copy(
-                tokens.at[pl.ds(first * TILE, count * TILE), :],
-                rows_buf.at[pl.ds(at, count * TILE), :],
-                row_sems.at[index],
-            )
-        )
-        at += count * TILE
-    for copy in copies + row_copies[:1] + weight_copies + row_copies[1:]:
-        copy.start()
-
-    copies[0].wait()
-    gains = gain_buf[...].reshape(1, depth)
-    at = 0
-    for index, (first, count) in enumerate(chunks):
-        row_copies[index].wait()
+        for copy in row_copies if index == 1 else row_copies[:1] if index == 0 else []:
+            copy.wait()
+        row_copies = row_copies[1:] if index == 0 else []
         for tile in range(count):
+            at = (first + tile) * TILE
             rows = rows_buf[pl.ds(at, TILE), :]
             scaled = rows * gains
-            if index == 0 and tile == 0:
+            if weight_copies:
                 product = jnp.zeros((TILE, width), jnp.float32)
-                for part in range(cuts):
-                    weight_copies[part].wait()
+                for part, copy in enumerate(weight_copies):
+                    copy.wait()
                     span = slice(part * cut, (part + 1) * cut)
                     product += jnp.dot(
                         scaled[:, span], weight_buf[span, :], preferred_element_type=jnp.float32
                     )
+                weight_copies = []
             else:
                 product = jnp.dot(scaled, weight_buf[...], preferred_element_type=jnp.float32)
             left = product[:, : width // 2].astype(jnp.bfloat16)
@@ -92,8 +103,9 @@
                 total = square_sums(rows)
                 for part in range(TILE // LANES):
                     turned = jnp.transpose(total[part * LANES : (part + 1) * LANES])
-                    squares[pl.ds(at // LANES + part, 1), :] = jnp.sum(turned, axis=0, keepdims=True)
-            at += TILE
+                    squares[at // LANES + part : at // LANES + part + 1, :] = jnp.sum(turned, axis=0, keepdims=True)
+    for copy in row_copies:
+        copy.wait()
 
 
 def add_kernel(keep, received, out):
@@ -150,30 +162,34 @@
     def shift(step):
         return [(i, (i + 2 * step) % tensor_count) for i in range(tensor_count)]
 
-    def product(gain, step, chunks, with_squares):
-        rows = [count * TILE for _, count in chunks]
+    def product(gain, step, chunks, with_squares=False, weight=None, rows=None):
+        vmem = pl.BlockSpec(memory_space=pltpu.VMEM)
+        hbm = pl.BlockSpec(memory_space=pltpu.HBM)
         out_shape = [
-            jax.ShapeDtypeStruct((size, columns), jnp.bfloat16) for size in rows for _ in range(2)
+            jax.ShapeDtypeStruct((count * TILE, columns), jnp.bfloat16) for _, count in chunks for _ in range(2)
         ]
         if with_squares:
-            out_shape.append(jax.ShapeDtypeStruct((sum(rows) // LANES, LANES), jnp.float32))
+            out_shape.append(jax.ShapeDtypeStruct((slot_rows // LANES, LANES), jnp.float32))
+        if weight is None:
+            out_shape.append(jax.ShapeDtypeStruct((depth, 2 * columns), jnp.bfloat16))
+        if rows is None:
+            out_shape.append(jax.ShapeDtypeStruct(tokens.shape, tokens.dtype))
         made = pl.pallas_call(
-            functools.partial(product_kernel, step, chip_count, chunks, with_squares),
-            in_specs=[pl.BlockSpec(memory_space=pl.ANY)] * 3,
+            functools.partial(product_kernel, step, chip_count, chunks, with_squares, weight is None, rows is None),
+            in_specs=[hbm if rows is None else vmem, hbm, hbm if weight is None else vmem],
             out_shape=out_shape,
+            out_specs=[vmem] * len(out_shape),
             scratch_shapes=[
-                pltpu.VMEM((sum(rows), depth), jnp.bfloat16),
-                pltpu.VMEM((depth, 2 * columns), jnp.bfloat16),
                 pltpu.VMEM((depth,), jnp.bfloat16),
                 pltpu.SemaphoreType.DMA((4,)),
-                pltpu.SemaphoreType.DMA((len(chunks),)),
+                pltpu.SemaphoreType.DMA((3,)),
                 pltpu.SemaphoreType.DMA,
             ],
-            compiler_params=WIDE,
+            compiler_params=FIRST if rows is None else PARAMS,
             cost_estimate=COST,
-        )(tokens, gain, kv_weight)
+        )(tokens if rows is None else rows, gain, kv_weight if weight is None else weight)
         pairs = [(made[2 * index], made[2 * index + 1]) for index in range(len(chunks))]
-        return (pairs, made[-1]) if with_squares else pairs
+        return [pairs] + list(made[2 * len(chunks) :])
 
     def tables(offset):
         half = HD // 2
@@ -217,10 +233,17 @@
     firsts = [sum(CHUNKS[:index]) for index in range(len(CHUNKS))]
     chunk_count = len(CHUNKS)
 
-    def start_chunks(gain, wanted):
+    def start_chunks(gain, wanted, kept):
         chunks = [(firsts[index], CHUNKS[index]) for index in wanted]
-        made = [product(gain, step, chunks, False) for step in others]
-        return [[per_step[index] for per_step in made] for index in range(len(wanted))]
+        made = []
+        for step in others:
+            results = product(gain, step, chunks, weight=kept.get(step), rows=kept.get("rows"))
+            made.append(results[0])
+            if step not in kept:
+                kept[step] = results[1]
+            if "rows" not in kept:
+                kept["rows"] = results[2]
+        return [[pairs[index] for pairs in made] for index in range(len(wanted))]
 
     def add_halves(made):
         return [
@@ -237,21 +260,23 @@
         return [lax.ppermute(part, "tensor", shift(step)) for step, part in zip(others, sums)]
 
     hold = lax.optimization_barrier
-    gain, arrivals = norm_gain, []
-    own, inputs, result, finished = None, None, None, 0
-    (made,) = start_chunks(gain, [0])
+    gain, kept, arrivals = norm_gain, {}, []
+    own, inputs, result, finished, arrived = None, None, None, 0, None
+    (made,) = start_chunks(gain, [0], kept)
     made, gain = hold((made, gain))
     sums = add_halves(made)
-    waiting = start_chunks(gain, [1])
+    waiting = start_chunks(gain, [1], kept)
     sums, waiting, gain, span_offset = hold((sums, waiting, gain, span_offset))
-    for stage in range(1, chunk_count + 1):
-        arrived = cross(sums)
+    for stage in range(1, chunk_count + 2):
+        before, arrived = arrived, None
+        if stage <= chunk_count:
+            arrived = cross(sums)
         if stage < chunk_count:
             sums = add_halves(waiting.pop(0))
         if stage == 1:
-            waiting += start_chunks(gain, list(range(2, chunk_count)))
+            waiting += start_chunks(gain, list(range(2, chunk_count)), kept)
         if stage == 2:
-            ((keep, send),), squares = product(gain, 0, [(0, tiles)], True)
+            ((keep, send),), squares, _ = product(gain, 0, [(0, tiles)], True, rows=kept["rows"])
             squares += lax.ppermute(squares, "tensor", swap)
             own = keep, send, squares, tables(span_offset[own_index])
         if stage == 3:
@@ -260,13 +285,14 @@
             squares = [squares] + [lax.ppermute(squares, "tensor", shift(step)) for step in others]
             inputs = keep, received, table, squares
         if stage >= 4:
-            for index in range(finished, stage - 1):
+            for index in range(finished, stage - 2):
                 result = finish(firsts[index], CHUNKS[index], *inputs, arrivals[index], result)
-            finished = stage - 1
-        arrived, sums, waiting, gain, span_offset, own, inputs, result = hold(
-            (arrived, sums, waiting, gain, span_offset, own, inputs, result)
+            finished = stage - 2
+        before, sums, waiting, gain, span_offset, own, inputs, result = hold(
+            (before, sums, waiting, gain, span_offset, own, inputs, result)
         )
-        arrivals.append(arrived)
+        if before is not None:
+            arrivals.append(before)
     for index in range(finished, chunk_count):
         result = finish(firsts[index], CHUNKS[index], *inputs, arrivals[index], result)
     return result

time: 55.9 us -> 57.6 us (1.030)
  Pallas kernels: 27 us -> 19.7 us
  waiting for transfers between devices: 16.1 us -> 22.8 us
  local copies, waits for them, and re-layouts: 0.71 us -> 3.67 us
  other arithmetic: 1.35 us -> 0.66 us
    pallas_call x4, Pallas kernels: 19.3 us -> 11 us  [product(): pl.pallas_call(functools.partial(product_kernel, step, chip_count, chunks...]
    ppermute x4, waiting for transfers between devices: 3.9 us -> 11.7 us  [cross(): lax.ppermute(part, 'tensor', shift(step))]
    unnamed x18, local copies, waits for them, and re-layouts: 0.05 us -> 3.09 us
    ppermute x4, starting transfers between devices: 8.16 us -> 6.35 us  [cross(): lax.ppermute(part, 'tensor', shift(step))]
    ppermute x4, waiting for transfers between devices: 1.53 us -> 0.01 us  [add_halves(): lax.ppermute(send, 'tensor', swap)]
    ppermute x1, starting transfers between devices: 0.29 us -> 1.74 us  [shards(): lax.ppermute(squares, 'tensor', shift(step))]
    pallas_call x4, Pallas kernels: 0.37 us -> 1.41 us  [add_halves(): pl.pallas_call(add_kernel, out_shape=jax.ShapeDtypeStruct(keep.shape, kee...]
    add x1, other arithmetic: 0.7 us -> 0.01 us  [shards(): squares += lax.ppermute(squares, 'tensor', swap)]
  transfers between devices with their start and end apart: 11 -> 11, of which waited for: 5 -> 4; matrix products, arithmetic and copies ran while one was open for 4% -> 2% of each run, Pallas kernels for 40% -> 25%
where the time goes in v5:
time: 57.6 us; the launch traced here: 57.4 us
  waiting for transfers between devices  22.8 us (40%)
  Pallas kernels  19.7 us (34%)
  starting transfers between devices  9.74 us (17%)
  local copies, waits for them, and re-layouts  3.67 us (6%)
  between operations  0.81 us (1%)
  other arithmetic  0.66 us (1%)
    ppermute x4, waiting for transfers between devices, cross(): lax.ppermute(part, 'tensor', shift(step))  11.7 us
    ppermute x1, waiting for transfers between devices, shards(): lax.ppermute(squares, 'tensor', shift(step))  11 us
    pallas_call x4, Pallas kernels, product(): pl.pallas_call(functools.partial(product_kernel, step, chip_count, chunks...  11 us
    pallas_call x4, Pallas kernels, finish(): pl.pallas_call(functools.partial(finish_kernel, first, chip_count, model_...  7.35 us
    ppermute x4, starting transfers between devices, cross(): lax.ppermute(part, 'tensor', shift(step))  6.35 us
    unnamed x18, local copies, waits for them, and re-layouts  3.09 us
    ppermute x1, starting transfers between devices, shards(): lax.ppermute(squares, 'tensor', shift(step))  1.74 us
    pallas_call x4, Pallas kernels, add_halves(): pl.pallas_call(add_kernel, out_shape=jax.ShapeDtypeStruct(keep.shape, kee...  1.41 us
  transfers between devices with their start and end apart: 11, of which 4 were waited for; matrix products, arithmetic and copies ran while one was open for 2% of the time, Pallas kernels for 25%

profile of v5, /device:TPU:0, one launch (start us, length us, event | category | flops | bytes accessed | tf_op | source)
XLA Modules:
  0.0 57.4 jit_solution(512492520853904815)
XLA Ops:
  0.0 0.7 %copy-done.5 = bf16[1024]{0:T(1024)(128)(2,1)S(1)} copy-done((bf16[1024]{0:T(1024)(128)(2,1)S(1)}, bf16[1024]{0:T(1024)(128)(2,1)}, u32[]{:S(2)}) %copy-start.5) | copy-done | bytes 2072
  0.7 2.6 %shard_map.55 = (bf16[256,512]{1,0:T(8,128)(2,1)S(1)}, bf16[256,512]{1,0:T(8,128)(2,1)S(1)}, bf16[1024,1024]{1,0:T(8,128)(2,1)S(1)}, bf16[1536,1024]{1,0:T(8,128)(2,1)S(1)}) custom-call(bf16[1536,1024]{1,0:T(8,128)(2,1)} %tokens.1, bf16[1024]{0:T(1024)(128)(2,1)S(1)} %copy-done.5, bf16[1024,2048]{1,0:T(8,128)(2,1)} %weight.3), custom_call_target="tpu_custom_call" | custom-call | flops 1 | bytes 1 | tf_op jit(solution)/shard_map/pallas_call | solution.py:177
  3.3 0.0 copy-start.1
  3.3 0.5 collective-permute-start
  3.8 2.2 %shard_map.57 = (bf16[512,512]{1,0:T(8,128)(2,1)S(1)}, bf16[512,512]{1,0:T(8,128)(2,1)}) custom-call(bf16[1536,1024]{1,0:T(8,128)(2,1)S(1)} %get-tuple-element.78.tokens, bf16[1024]{0:T(1024)(128)(2,1)S(1)} %copy-done.5, bf16[1024,1024]{1,0:T(8,128)(2,1)S(1)} %get-tuple-element.80.weight), custom_call_target="tpu_custom_call" | custom-call | flops 1 | bytes 1 | tf_op jit(solution)/shard_map/pallas_call | solution.py:177
  6.0 0.0 copy-done.1
  6.0 0.0 copy-start.3
  6.0 0.8 %copy-done.3 = bf16[512,512]{1,0:T(8,128)(2,1)} copy-done((bf16[512,512]{1,0:T(8,128)(2,1)}, bf16[512,512]{1,0:T(8,128)(2,1)S(1)}, u32[]{:S(2)}) %copy-start.3) | copy-done | bytes 524312
  6.8 0.0 collective-permute-done.received
  6.8 0.1 shard_map.56
  6.9 0.1 collective-permute-start.1
  7.0 0.1 pad_maximum_fusion
  7.1 0.0 copy-done.6
  7.1 1.6 %copy-done.2 = bf16[1024,1024]{1,0:T(8,128)(2,1)S(1)} copy-done((bf16[1024,1024]{1,0:T(8,128)(2,1)S(1)}, bf16[1024,1024]{1,0:T(8,128)(2,1)}, u32[]{:S(2)}) %copy-start.2) | copy-done | bytes 2097176
  8.7 1.9 %shard_map.59 = (bf16[512,512]{1,0:T(8,128)(2,1)S(1)}, bf16[512,512]{1,0:T(8,128)(2,1)S(1)}, bf16[256,512]{1,0:T(8,128)(2,1)S(1)}, bf16[256,512]{1,0:T(8,128)(2,1)S(1)}) custom-call(bf16[1536,1024]{1,0:T(8,128)(2,1)S(1)} %get-tuple-element.78.tokens, bf16[1024]{0:T(1024)(128)(2,1)S(1)} %copy-done.6, bf16[1024,1024]{1,0:T(8,128)(2,1)S(1)} %copy-done.2), custom_call_target="tpu_custom_call" | custom-call | flops 1 | bytes 1 | tf_op jit(solution)/shard_map/pallas_call | solution.py:177
  10.6 0.0 collective-permute-done.1.received
  10.7 0.0 copy-done.4
  10.7 1.2 %shard_map.58 = bf16[512,512]{1,0:T(8,128)(2,1)S(1)} custom-call(bf16[512,512]{1,0:T(8,128)(2,1)S(1)} %copy-done.4, bf16[512,512]{1,0:T(8,128)(2,1)} %collective-permute-done.1.received), custom_call_target="tpu_custom_call" | custom-call | flops 1 | bytes 1 | tf_op jit(solution)/shard_map/pallas_call | solution.py:250
  11.8 0.5 collective-permute-start.4
  12.3 0.1 fusion
  12.5 0.0 copy-start.8
  12.5 2.6 %collective-permute-start.3 = (bf16[256,512]{1,0:T(8,128)(2,1)S(1)}, bf16[256,512]{1,0:T(8,128)(2,1)S(1)}, u32[]{:S(2)}, u32[]{:S(2)}) collective-permute-start(bf16[256,512]{1,0:T(8,128)(2,1)S(1)} %shard_map.56), channel_id=1, source_target_pairs={{0,2},{1,3},{2,0},{3,1},{4,6},{5,7},{6,4},{7,5},{8,10},{9,11},{10,... | collective-permute-start | bytes 786440 | tf_op jit(solution)/shard_map/ppermute | solution.py:260
  15.1 4.2 %shard_map.61 = (bf16[1536,512]{1,0:T(8,128)(2,1)S(1)}, bf16[1536,512]{1,0:T(8,128)(2,1)S(1)}, f32[12,128]{1,0:T(8,128)S(1)}, bf16[1024,1024]{1,0:T(8,128)(2,1)}) custom-call(bf16[1536,1024]{1,0:T(8,128)(2,1)S(1)} %get-tuple-element.78.tokens, bf16[1024]{0:T(1024)(128)(2,1)S(1)} %copy-done.6, bf16[1024,2048]{1,0:T(8,128)(2,1)S(1)} %copy-done), custom_call_target="tpu_custom_call" | custom-call | flops 1 | bytes 1 | tf_op jit(solution)/shard_map/pallas_call | solution.py:177
  19.3 0.0 copy-start.7
  19.3 0.3 collective-permute-start.5
  19.6 0.6 %dynamic_slice.3 = s32[1]{0:T(128)} dynamic-slice(s32[4]{0:T(128)S(1)} %copy-done.8, s32[]{:T(128)S(6)} %select_n.3), dynamic_slice_sizes={1} | dynamic-slice | bytes 12 | tf_op jit(solution)/shard_map/dynamic_slice | solution.py:281
  20.9 0.4 multiply_sine_fusion
  21.3 0.0 collective-permute-done.5
  21.3 0.0 collective-permute-done.4.received
  21.3 0.1 shard_map.60
  21.4 0.6 %collective-permute-done.3.refs_8_ = bf16[256,512]{1,0:T(8,128)(2,1)S(1)} collective-permute-done((bf16[256,512]{1,0:T(8,128)(2,1)S(1)}, bf16[256,512]{1,0:T(8,128)(2,1)S(1)}, u32[]{:S(2)}, u32[]{:S(2)}) %collective-permute-start.3) | collective-permute-done | bytes 262176 | tf_op jit(solution)/shard_map/ppermute | solution.py:260
  22.0 0.0 collective-permute-start.7
  22.0 1.7 %collective-permute-start.2 = (bf16[512,512]{1,0:T(8,128)(2,1)S(1)}, bf16[512,512]{1,0:T(8,128)(2,1)S(1)}, u32[]{:S(2)}, u32[]{:S(2)}) collective-permute-start(bf16[512,512]{1,0:T(8,128)(2,1)S(1)} %shard_map.58), channel_id=1, source_target_pairs={{0,2},{1,3},{2,0},{3,1},{4,6},{5,7},{6,4},{7,5},{8,10},{9,11},{10,... | collective-permute-start | bytes 1572872 | tf_op jit(solution)/shard_map/ppermute | solution.py:260
  23.8 0.2 collective-permute-start.6
  24.0 0.3 collective-permute-start.10
  24.3 1.7 %collective-permute-start.8 = (f32[12,128]{1,0:T(8,128)S(1)}, f32[12,128]{1,0:T(8,128)S(1)}, u32[]{:S(2)}, u32[]{:S(2)}) collective-permute-start(f32[12,128]{1,0:T(8,128)S(1)} %add.16.refs_6_), channel_id=1, source_target_pairs={{0,2},{1,3},{2,0},{3,1},{4,6},{5,7},{6,4},{7,5},{8,10},{9,11},{10,... | collective-permute-start | bytes 18440 | tf_op jit(solution)/shard_map/ppermute | solution.py:285
  26.0 0.0 collective-permute-done.6.received
  26.0 0.1 shard_map.62
  26.1 10.7 %collective-permute-done.2.refs_8_ = bf16[512,512]{1,0:T(8,128)(2,1)S(1)} collective-permute-done((bf16[512,512]{1,0:T(8,128)(2,1)S(1)}, bf16[512,512]{1,0:T(8,128)(2,1)S(1)}, u32[]{:S(2)}, u32[]{:S(2)}) %collective-permute-start.2) | collective-permute-done | bytes 524320 | tf_op jit(solution)/shard_map/ppermute | solution.py:260
  36.8 11.0 %collective-permute-done.8.refs_7_ = f32[12,128]{1,0:T(8,128)S(1)} collective-permute-done((f32[12,128]{1,0:T(8,128)S(1)}, f32[12,128]{1,0:T(8,128)S(1)}, u32[]{:S(2)}, u32[]{:S(2)}) %collective-permute-start.8) | collective-permute-done | bytes 6176 | tf_op jit(solution)/shard_map/ppermute | solution.py:285
  47.8 0.0 collective-permute-done.7.refs_1_
  47.8 1.7 %collective-permute-start.9 = (bf16[256,512]{1,0:T(8,128)(2,1)S(1)}, bf16[256,512]{1,0:T(8,128)(2,1)S(1)}, u32[]{:S(2)}, u32[]{:S(2)}) collective-permute-start(bf16[256,512]{1,0:T(8,128)(2,1)S(1)} %shard_map.62), channel_id=1, source_target_pairs={{0,2},{1,3},{2,0},{3,1},{4,6},{5,7},{6,4},{7,5},{8,10},{9,11},{10,... | collective-permute-start | bytes 786440 | tf_op jit(solution)/shard_map/ppermute | solution.py:260
  49.5 1.6 %shard_map.63.refs_9_ = bf16[1536,512]{1,0:T(8,128)(2,1)} custom-call(s32[4]{0:T(128)S(1)} %copy-done.7, bf16[1536,512]{1,0:T(8,128)(2,1)S(1)} %get-tuple-element.133.refs_0_.refs_9_, bf16[1536,512]{1,0:T(8,128)(2,1)S(1)} %collective-permute-done.7.refs_1_, f32[24,1,128]{2,1,0:T(1,128)S(1)} %get-tuple-element.135.refs_2_, ...), custom_call_target="tpu_custom_call" | custom-call | flops 1 | bytes 1 | tf_op jit(solution)/shard_map/pallas_call | solution.py:218
  51.2 2.0 %shard_map.64.refs_9_ = bf16[1536,512]{1,0:T(8,128)(2,1)} custom-call(s32[4]{0:T(128)S(1)} %copy-done.7, bf16[1536,512]{1,0:T(8,128)(2,1)S(1)} %get-tuple-element.133.refs_0_.refs_9_, bf16[1536,512]{1,0:T(8,128)(2,1)S(1)} %collective-permute-done.7.refs_1_, f32[24,1,128]{2,1,0:T(1,128)S(1)} %get-tuple-element.135.refs_2_, ...), custom_call_target="tpu_custom_call", output_to_operand_aliasing={{}: (10, {})} | custom-call | flops 1 | bytes 1 | tf_op jit(solution)/shard_map/pallas_call | solution.py:218
  53.2 0.0 collective-permute-done.10.refs_8_
  53.2 2.0 %shard_map.65.refs_9_ = bf16[1536,512]{1,0:T(8,128)(2,1)} custom-call(s32[4]{0:T(128)S(1)} %copy-done.7, bf16[1536,512]{1,0:T(8,128)(2,1)S(1)} %get-tuple-element.133.refs_0_.refs_9_, bf16[1536,512]{1,0:T(8,128)(2,1)S(1)} %collective-permute-done.7.refs_1_, f32[24,1,128]{2,1,0:T(1,128)S(1)} %get-tuple-element.135.refs_2_, ...), custom_call_target="tpu_custom_call", output_to_operand_aliasing={{}: (10, {})} | custom-call | flops 1 | bytes 1 | tf_op jit(solution)/shard_map/pallas_call | solution.py:218
  55.2 0.5 collective-permute-done.9.refs_8_
  55.7 1.6 %shard_map.66 = bf16[1536,512]{1,0:T(8,128)(2,1)} custom-call(s32[4]{0:T(128)S(1)} %copy-done.7, bf16[1536,512]{1,0:T(8,128)(2,1)S(1)} %get-tuple-element.133.refs_0_.refs_9_, bf16[1536,512]{1,0:T(8,128)(2,1)S(1)} %collective-permute-done.7.refs_1_, f32[24,1,128]{2,1,0:T(1,128)S(1)} %get-tuple-element.135.refs_2_, ...), custom_call_target="tpu_custom_call", output_to_operand_aliasing={{}: (10, {})} | custom-call | flops 1 | bytes 1 | tf_op jit(solution)/shard_map/pallas_call | solution.py:218
  (11 shorter events, 0.0 us)
Async XLA Ops:
  0.0 0.7 %copy-start.5 = (bf16[1024]{0:T(1024)(128)(2,1)S(1)}, bf16[1024]{0:T(1024)(128)(2,1)}, u32[]{:S(2)}) copy-start(bf16[1024]{0:T(1024)(128)(2,1)} %gain.4) | copy-start | bytes 6148
  3.3 2.7 %copy-start.1 = (bf16[1024,1024]{1,0:T(8,128)(2,1)}, bf16[1024,1024]{1,0:T(8,128)(2,1)S(1)}, u32[]{:S(2)}) copy-start(bf16[1024,1024]{1,0:T(8,128)(2,1)S(1)} %get-tuple-element.80.weight) | copy-start | bytes 6291460
  3.3 3.5 %collective-permute-start = (bf16[256,512]{1,0:T(8,128)(2,1)S(1)}, bf16[256,512]{1,0:T(8,128)(2,1)S(1)}, u32[]{:S(2)}, u32[]{:S(2)}) collective-permute-start(bf16[256,512]{1,0:T(8,128)(2,1)S(1)} %get-tuple-element.77), channel_id=1, source_target_pairs={{0,1},{1,0},{2,3},{3,2},{4,5},{5,4},{6,7},{7,6},{8,9},{9,8},{10,11... | collective-permute-start | bytes 786440 | tf_op jit(solution)/shard_map/ppermute | solution.py:255
  3.8 3.3 %copy-start.6 = (bf16[1024]{0:T(1024)(128)(2,1)S(1)}, bf16[1024]{0:T(1024)(128)(2,1)}, u32[]{:S(2)}) copy-start(bf16[1024]{0:T(1024)(128)(2,1)} %gain.4) | copy-start | bytes 6148
  6.0 0.8 %copy-start.3 = (bf16[512,512]{1,0:T(8,128)(2,1)}, bf16[512,512]{1,0:T(8,128)(2,1)S(1)}, u32[]{:S(2)}) copy-start(bf16[512,512]{1,0:T(8,128)(2,1)S(1)} %get-tuple-element.83.keep) | copy-start | bytes 1572868
  6.9 3.8 %collective-permute-start.1 = (bf16[512,512]{1,0:T(8,128)(2,1)}, bf16[512,512]{1,0:T(8,128)(2,1)}, u32[]{:S(2)}, u32[]{:S(2)}) collective-permute-start(bf16[512,512]{1,0:T(8,128)(2,1)} %get-tuple-element.84), channel_id=1, source_target_pairs={{0,1},{1,0},{2,3},{3,2},{4,5},{5,4},{6,7},{7,6},{8,9},{9,8},{10,11... | collective-permute-start | bytes 1572872 | tf_op jit(solution)/shard_map/ppermute | solution.py:255
  7.1 1.6 %copy-start.2 = (bf16[1024,1024]{1,0:T(8,128)(2,1)S(1)}, bf16[1024,1024]{1,0:T(8,128)(2,1)}, u32[]{:S(2)}) copy-start(bf16[1024,1024]{1,0:T(8,128)(2,1)} %copy-done.1) | copy-start | bytes 6291460
  8.7 2.0 %copy-start.4 = (bf16[512,512]{1,0:T(8,128)(2,1)S(1)}, bf16[512,512]{1,0:T(8,128)(2,1)}, u32[]{:S(2)}) copy-start(bf16[512,512]{1,0:T(8,128)(2,1)} %copy-done.3) | copy-start | bytes 1572868
  8.7 6.4 %copy-start = (bf16[1024,2048]{1,0:T(8,128)(2,1)S(1)}, bf16[1024,2048]{1,0:T(8,128)(2,1)}, u32[]{:S(2)}) copy-start(bf16[1024,2048]{1,0:T(8,128)(2,1)} %weight.3) | copy-start | bytes 12582916
  11.8 9.5 %collective-permute-start.4 = (bf16[512,512]{1,0:T(8,128)(2,1)S(1)}, bf16[512,512]{1,0:T(8,128)(2,1)S(1)}, u32[]{:S(2)}, u32[]{:S(2)}) collective-permute-start(bf16[512,512]{1,0:T(8,128)(2,1)S(1)} %get-tuple-element.94), channel_id=1, source_target_pairs={{0,1},{1,0},{2,3},{3,2},{4,5},{5,4},{6,7},{7,6},{8,9},{9,8},{10,11... | collective-permute-start | bytes 1572872 | tf_op jit(solution)/shard_map/ppermute | solution.py:255
  12.5 7.1 %copy-start.8 = (s32[4]{0:T(128)S(1)}, s32[4]{0:T(128)}, u32[]{:S(2)}) copy-start(s32[4]{0:T(128)} %param.9) | copy-start | bytes 52
  12.5 9.5 %collective-permute-start.3 = (bf16[256,512]{1,0:T(8,128)(2,1)S(1)}, bf16[256,512]{1,0:T(8,128)(2,1)S(1)}, u32[]{:S(2)}, u32[]{:S(2)}) collective-permute-start(bf16[256,512]{1,0:T(8,128)(2,1)S(1)} %shard_map.56), channel_id=1, source_target_pairs={{0,2},{1,3},{2,0},{3,1},{4,6},{5,7},{6,4},{7,5},{8,10},{9,11},{10,... | collective-permute-start | bytes 786440 | tf_op jit(solution)/shard_map/ppermute | solution.py:260
  19.3 30.2 %copy-start.7 = (s32[4]{0:T(128)S(1)}, s32[4]{0:T(128)}, u32[]{:S(2)}) copy-start(s32[4]{0:T(128)} %live.7) | copy-start | bytes 52
  19.3 1.9 %collective-permute-start.5 = (f32[12,128]{1,0:T(8,128)S(1)}, f32[12,128]{1,0:T(8,128)S(1)}, u32[]{:S(2)}, u32[]{:S(2)}) collective-permute-start(f32[12,128]{1,0:T(8,128)S(1)} %get-tuple-element.101), channel_id=1, source_target_pairs={{0,1},{1,0},{2,3},{3,2},{4,5},{5,4},{6,7},{7,6},{8,9},{9,8},{10,11... | collective-permute-start | bytes 18440 | tf_op jit(solution)/shard_map/ppermute | solution.py:280
  22.0 25.8 %collective-permute-start.7 = (bf16[1536,512]{1,0:T(8,128)(2,1)S(1)}, bf16[1536,512]{1,0:T(8,128)(2,1)S(1)}, u32[]{:S(2)}, u32[]{:S(2)}) collective-permute-start(bf16[1536,512]{1,0:T(8,128)(2,1)S(1)} %get-tuple-element.104), channel_id=1, source_target_pairs={{0,1},{1,0},{2,3},{3,2},{4,5},{5,4},{6,7},{7,6},{8,9},{9,8},{10,11... | collective-permute-start | bytes 4718600 | tf_op jit(solution)/shard_map/ppermute | solution.py:284
  22.0 14.7 %collective-permute-start.2 = (bf16[512,512]{1,0:T(8,128)(2,1)S(1)}, bf16[512,512]{1,0:T(8,128)(2,1)S(1)}, u32[]{:S(2)}, u32[]{:S(2)}) collective-permute-start(bf16[512,512]{1,0:T(8,128)(2,1)S(1)} %shard_map.58), channel_id=1, source_target_pairs={{0,2},{1,3},{2,0},{3,1},{4,6},{5,7},{6,4},{7,5},{8,10},{9,11},{10,... | collective-permute-start | bytes 1572872 | tf_op jit(solution)/shard_map/ppermute | solution.py:260
  23.8 2.3 %collective-permute-start.6 = (bf16[256,512]{1,0:T(8,128)(2,1)S(1)}, bf16[256,512]{1,0:T(8,128)(2,1)S(1)}, u32[]{:S(2)}, u32[]{:S(2)}) collective-permute-start(bf16[256,512]{1,0:T(8,128)(2,1)S(1)} %get-tuple-element.103), channel_id=1, source_target_pairs={{0,1},{1,0},{2,3},{3,2},{4,5},{5,4},{6,7},{7,6},{8,9},{9,8},{10,11... | collective-permute-start | bytes 786440 | tf_op jit(solution)/shard_map/ppermute | solution.py:255
  24.0 29.2 %collective-permute-start.10 = (bf16[512,512]{1,0:T(8,128)(2,1)S(1)}, bf16[512,512]{1,0:T(8,128)(2,1)S(1)}, u32[]{:S(2)}, u32[]{:S(2)}) collective-permute-start(bf16[512,512]{1,0:T(8,128)(2,1)S(1)} %shard_map.60), channel_id=1, source_target_pairs={{0,2},{1,3},{2,0},{3,1},{4,6},{5,7},{6,4},{7,5},{8,10},{9,11},{10,... | collective-permute-start | bytes 1572872 | tf_op jit(solution)/shard_map/ppermute | solution.py:260
  24.3 23.5 %collective-permute-start.8 = (f32[12,128]{1,0:T(8,128)S(1)}, f32[12,128]{1,0:T(8,128)S(1)}, u32[]{:S(2)}, u32[]{:S(2)}) collective-permute-start(f32[12,128]{1,0:T(8,128)S(1)} %add.16.refs_6_), channel_id=1, source_target_pairs={{0,2},{1,3},{2,0},{3,1},{4,6},{5,7},{6,4},{7,5},{8,10},{9,11},{10,... | collective-permute-start | bytes 18440 | tf_op jit(solution)/shard_map/ppermute | solution.py:285
  47.8 7.9 %collective-permute-start.9 = (bf16[256,512]{1,0:T(8,128)(2,1)S(1)}, bf16[256,512]{1,0:T(8,128)(2,1)S(1)}, u32[]{:S(2)}, u32[]{:S(2)}) collective-permute-start(bf16[256,512]{1,0:T(8,128)(2,1)S(1)} %shard_map.62), channel_id=1, source_target_pairs={{0,2},{1,3},{2,0},{3,1},{4,6},{5,7},{6,4},{7,5},{8,10},{9,11},{10,... | collective-permute-start | bytes 786440 | tf_op jit(solution)/shard_map/ppermute | solution.py:260

commit v6 on v5

--- a/solution.py
+++ b/solution.py
@@ -16,7 +16,7 @@
 norm_eps = 1e-05
 
 TILE = 256
-CHUNKS = (1, 2, 2, 1)
+CHUNKS = (2, 2, 2)
 
 PARAMS = pltpu.CompilerParams(vmem_limit_bytes=16 * 1024 * 1024)
 FIRST = pltpu.CompilerParams(vmem_limit_bytes=48 * 1024 * 1024)
@@ -31,12 +31,14 @@
     return total
 
 
-def product_kernel(step, chip_count, chunks, with_squares, load_weight, load_rows, tokens, gain, weight, *refs):
-    outs = list(refs[: 2 * len(chunks)])
-    refs = list(refs[2 * len(chunks) :])
+def product_kernel(step, chip_count, chunks, loaded, load, with_squares, load_weight, tokens, gain, weight, *refs):
+    refs = list(refs)
+    sources = [(first, count, refs.pop(0)) for first, count in loaded]
+    outs = [refs.pop(0) for _ in range(2 * len(chunks))]
     squares = refs.pop(0) if with_squares else None
     weight_buf = refs.pop(0) if load_weight else weight
-    rows_buf = refs.pop(0) if load_rows else tokens
+    if load:
+        sources.append((*load, refs.pop(0)))
     gain_buf, weight_sems, row_sems, gain_sem = refs
     depth, width = weight_buf.shape
     me = lax.axis_index("tensor")
@@ -57,31 +59,27 @@
             )
             for index in range(cuts)
         ]
-    row_copies = []
-    if load_rows:
-        first, count = chunks[0]
-        edges = [0, first * TILE, (first + count) * TILE, tokens.shape[0]]
-        row_copies = [
-            pltpu.make_async_copy(
-                tokens.at[pl.ds(low, high - low), :], rows_buf.at[pl.ds(low, high - low), :], row_sems.at[index]
+    row_copies = {}
+    if load:
+        first, count = load
+        for index in range(count):
+            row_copies[first + index] = pltpu.make_async_copy(
+                tokens.at[pl.ds((first + index) * TILE, TILE), :],
+                sources[-1][2].at[pl.ds(index * TILE, TILE), :],
+                row_sems.at[index],
             )
-            for index, (low, high) in enumerate(zip(edges, edges[1:]))
-            if low < high
-        ]
-        if first:
-            row_copies[:2] = row_copies[1::-1]
-    for copy in [gain_copy] + row_copies[:1] + weight_copies + row_copies[1:]:
+    in_order = list(row_copies.values())
+    for copy in [gain_copy] + in_order[:1] + weight_copies + in_order[1:]:
         copy.start()
 
     gain_copy.wait()
     gains = gain_buf[...].reshape(1, depth)
     for index, (first, count) in enumerate(chunks):
-        for copy in row_copies if index == 1 else row_copies[:1] if index == 0 else []:
-            copy.wait()
-        row_copies = row_copies[1:] if index == 0 else []
-        for tile in range(count):
-            at = (first + tile) * TILE
-            rows = rows_buf[pl.ds(at, TILE), :]
+        for tile in range(first, first + count):
+            if tile in row_copies:
+                row_copies.pop(tile).wait()
+            low, _, source = [entry for entry in sources if entry[0] <= tile < entry[0] + entry[1]][0]
+            rows = source[pl.ds((tile - low) * TILE, TILE), :]
             scaled = rows * gains
             if weight_copies:
                 product = jnp.zeros((TILE, width), jnp.float32)
@@ -96,15 +94,16 @@
                 product = jnp.dot(scaled, weight_buf[...], preferred_element_type=jnp.float32)
             left = product[:, : width // 2].astype(jnp.bfloat16)
             right = product[:, width // 2 :].astype(jnp.bfloat16)
-            inside = pl.ds(tile * TILE, TILE)
+            inside = pl.ds((tile - first) * TILE, TILE)
             outs[2 * index][inside, :] = jnp.where(core == 0, left, right)
             outs[2 * index + 1][inside, :] = jnp.where(core == 0, right, left)
             if with_squares:
                 total = square_sums(rows)
                 for part in range(TILE // LANES):
                     turned = jnp.transpose(total[part * LANES : (part + 1) * LANES])
-                    squares[at // LANES + part : at // LANES + part + 1, :] = jnp.sum(turned, axis=0, keepdims=True)
-    for copy in row_copies:
+                    row = tile * (TILE // LANES) + part
+                    squares[row : row + 1, :] = jnp.sum(turned, axis=0, keepdims=True)
+    for copy in row_copies.values():
         copy.wait()
 
 
@@ -112,9 +111,9 @@
     out[...] = (keep[...].astype(jnp.float32) + received[...].astype(jnp.float32)).astype(out.dtype)
 
 
-def finish_kernel(first_tile, chip_count, model_dim, live, *refs):
+def finish_kernel(first_tile, tensor_count, model_dim, live, *refs):
     keep, received, far_cos, far_sin, near_cos, near_sin = refs[:6]
-    squares, arrived, out = refs[6 : 6 + chip_count], refs[6 + chip_count : -2], refs[-1]
+    squares, arrived, out = refs[6 : 6 + tensor_count], refs[6 + tensor_count : -2], refs[-1]
     values = keep[...].astype(jnp.float32) + received[...].astype(jnp.float32)
     for part in arrived:
         values += part[...].astype(jnp.float32)
@@ -162,9 +161,11 @@
     def shift(step):
         return [(i, (i + 2 * step) % tensor_count) for i in range(tensor_count)]
 
-    def product(gain, step, chunks, with_squares=False, weight=None, rows=None):
+    def product(gain, step, chunks, kept, load=None, with_squares=False):
         vmem = pl.BlockSpec(memory_space=pltpu.VMEM)
         hbm = pl.BlockSpec(memory_space=pltpu.HBM)
+        weight = kept.get(step)
+        loaded = kept["rows"]
         out_shape = [
             jax.ShapeDtypeStruct((count * TILE, columns), jnp.bfloat16) for _, count in chunks for _ in range(2)
         ]
@@ -172,24 +173,38 @@
             out_shape.append(jax.ShapeDtypeStruct((slot_rows // LANES, LANES), jnp.float32))
         if weight is None:
             out_shape.append(jax.ShapeDtypeStruct((depth, 2 * columns), jnp.bfloat16))
-        if rows is None:
-            out_shape.append(jax.ShapeDtypeStruct(tokens.shape, tokens.dtype))
+        if load:
+            out_shape.append(jax.ShapeDtypeStruct((load[1] * TILE, depth), jnp.bfloat16))
         made = pl.pallas_call(
-            functools.partial(product_kernel, step, chip_count, chunks, with_squares, weight is None, rows is None),
-            in_specs=[hbm if rows is None else vmem, hbm, hbm if weight is None else vmem],
+            functools.partial(
+                product_kernel,
+                step,
+                chip_count,
+                chunks,
+                [entry[:2] for entry in loaded],
+                load,
+                with_squares,
+                weight is None,
+            ),
+            in_specs=[hbm, hbm, hbm if weight is None else vmem] + [vmem] * len(loaded),
             out_shape=out_shape,
             out_specs=[vmem] * len(out_shape),
             scratch_shapes=[
                 pltpu.VMEM((depth,), jnp.bfloat16),
                 pltpu.SemaphoreType.DMA((4,)),
-                pltpu.SemaphoreType.DMA((3,)),
+                pltpu.SemaphoreType.DMA((tiles,)),
                 pltpu.SemaphoreType.DMA,
             ],
-            compiler_params=FIRST if rows is None else PARAMS,
+            compiler_params=PARAMS if loaded else FIRST,
             cost_estimate=COST,
-        )(tokens if rows is None else rows, gain, kv_weight if weight is None else weight)
-        pairs = [(made[2 * index], made[2 * index + 1]) for index in range(len(chunks))]
-        return [pairs] + list(made[2 * len(chunks) :])
+        )(tokens, gain, kv_weight if weight is None else weight, *[entry[2] for entry in loaded])
+        made = list(made)
+        if load:
+            kept["rows"] = loaded + [(*load, made.pop())]
+        if weight is None:
+            kept[step] = made.pop()
+        squares = made.pop() if with_squares else None
+        return list(zip(made[::2], made[1::2])), squares
 
     def tables(offset):
         half = HD // 2
@@ -207,7 +222,7 @@
             [pl.BlockSpec((TILE, columns), lambda i, *_: (first + i, 0))] * 2
             + [pl.BlockSpec((blocks, 1, HD), lambda i, *_: (first + i, 0, 0))] * 2
             + [pl.BlockSpec((BLOCK, HD), lambda i, *_: (0, 0))] * 2
-            + [pl.BlockSpec((slot_rows // LANES, LANES), lambda i, *_: (0, 0))] * chip_count
+            + [pl.BlockSpec((slot_rows // LANES, LANES), lambda i, *_: (0, 0))] * tensor_count
             + [pl.BlockSpec((TILE, columns), lambda i, *_: (i, 0))] * len(arrived)
         )
         if result is None:
@@ -216,7 +231,7 @@
         else:
             aliases = {1 + len(operands): 0}
         return pl.pallas_call(
-            functools.partial(finish_kernel, first, chip_count, model_dim),
+            functools.partial(finish_kernel, first, tensor_count, model_dim),
             grid_spec=pltpu.PrefetchScalarGridSpec(
                 num_scalar_prefetch=1,
                 grid=(count,),
@@ -233,17 +248,11 @@
     firsts = [sum(CHUNKS[:index]) for index in range(len(CHUNKS))]
     chunk_count = len(CHUNKS)
 
-    def start_chunks(gain, wanted, kept):
-        chunks = [(firsts[index], CHUNKS[index]) for index in wanted]
+    def start_chunk(gain, index, kept, load=None):
         made = []
         for step in others:
-            results = product(gain, step, chunks, weight=kept.get(step), rows=kept.get("rows"))
-            made.append(results[0])
-            if step not in kept:
-                kept[step] = results[1]
-            if "rows" not in kept:
-                kept["rows"] = results[2]
-        return [[pairs[index] for pairs in made] for index in range(len(wanted))]
+            made += product(gain, step, [(firsts[index], CHUNKS[index])], kept, load if step == 1 else None)[0]
+        return made
 
     def add_halves(made):
         return [
@@ -260,41 +269,33 @@
         return [lax.ppermute(part, "tensor", shift(step)) for step, part in zip(others, sums)]
 
     hold = lax.optimization_barrier
-    gain, kept, arrivals = norm_gain, {}, []
-    own, inputs, result, finished, arrived = None, None, None, 0, None
-    (made,) = start_chunks(gain, [0], kept)
+    gain, kept = norm_gain, {"rows": []}
+    made = start_chunk(gain, 0, kept, (0, CHUNKS[0]))
     made, gain = hold((made, gain))
     sums = add_halves(made)
-    waiting = start_chunks(gain, [1], kept)
-    sums, waiting, gain, span_offset = hold((sums, waiting, gain, span_offset))
-    for stage in range(1, chunk_count + 2):
-        before, arrived = arrived, None
-        if stage <= chunk_count:
-            arrived = cross(sums)
-        if stage < chunk_count:
-            sums = add_halves(waiting.pop(0))
-        if stage == 1:
-            waiting += start_chunks(gain, list(range(2, chunk_count)), kept)
-        if stage == 2:
-            ((keep, send),), squares, _ = product(gain, 0, [(0, tiles)], True, rows=kept["rows"])
-            squares += lax.ppermute(squares, "tensor", swap)
-            own = keep, send, squares, tables(span_offset[own_index])
-        if stage == 3:
-            keep, send, squares, table = own
-            received = lax.ppermute(send, "tensor", swap)
-            squares = [squares] + [lax.ppermute(squares, "tensor", shift(step)) for step in others]
-            inputs = keep, received, table, squares
-        if stage >= 4:
-            for index in range(finished, stage - 2):
-                result = finish(firsts[index], CHUNKS[index], *inputs, arrivals[index], result)
-            finished = stage - 2
-        before, sums, waiting, gain, span_offset, own, inputs, result = hold(
-            (before, sums, waiting, gain, span_offset, own, inputs, result)
+    made = start_chunk(gain, 1, kept, (CHUNKS[0], tiles - CHUNKS[0]))
+    sums, made, gain, span_offset = hold((sums, made, gain, span_offset))
+
+    arrived = cross(sums)
+    sums = add_halves(made)
+    waiting = [start_chunk(gain, index, kept) for index in range(2, chunk_count)]
+    ((keep, send),), squares = product(gain, 0, [(0, tiles)], kept, with_squares=True)
+    squares = [squares] + [
+        lax.ppermute(squares, "tensor", [(i, (i + step) % tensor_count) for i in range(tensor_count)])
+        for step in range(1, tensor_count)
+    ]
+    table = tables(span_offset[own_index])
+    arrived, sums, waiting, keep, send, squares, table = hold(
+        (arrived, sums, waiting, keep, send, squares, table)
+    )
+
+    arrivals = [arrived, cross(sums)] + [cross(add_halves(made)) for made in waiting]
+    received = lax.ppermute(send, "tensor", swap)
+    result = None
+    for index in range(chunk_count):
+        result = finish(
+            firsts[index], CHUNKS[index], keep, received, table, squares, arrivals[index], result
         )
-        if before is not None:
-            arrivals.append(before)
-    for index in range(finished, chunk_count):
-        result = finish(firsts[index], CHUNKS[index], *inputs, arrivals[index], result)
     return result
 
 

time: 57.6 us -> 56.8 us (0.986)
  local copies, waits for them, and re-layouts: 3.67 us -> 9.14 us
  waiting for transfers between devices: 22.8 us -> 17.5 us
  starting transfers between devices: 9.74 us -> 9.15 us
    ppermute x2 -> x3, waiting for transfers between devices: 11 us -> 0.01 us  [shards(): lax.ppermute(squares, 'tensor', [(i, (i + step) % tensor_count) for i in...]
    unnamed x18 -> x38, local copies, waits for them, and re-layouts: 3.09 us -> 8.56 us
    ppermute x4 -> x3, waiting for transfers between devices: 11.7 us -> 15.5 us  [cross(): lax.ppermute(part, 'tensor', shift(step))]
    ppermute x4 -> x3, waiting for transfers between devices: 0.01 us -> 2 us  [add_halves(): lax.ppermute(send, 'tensor', swap)]
    pallas_call x4 -> x3, Pallas kernels: 7.35 us -> 6.2 us  [finish(): pl.pallas_call(functools.partial(finish_kernel, first, tensor_count, mode...]
    ppermute x4 -> x3, starting transfers between devices: 6.35 us -> 5.97 us  [cross(): lax.ppermute(part, 'tensor', shift(step))]
    ppermute x4 -> x3, starting transfers between devices: 1.38 us -> 1.19 us  [add_halves(): lax.ppermute(send, 'tensor', swap)]
    ppermute x2 -> x3, starting transfers between devices: 2 us -> 1.88 us  [shards(): lax.ppermute(squares, 'tensor', [(i, (i + step) % tensor_count) for i in...]
  transfers between devices with their start and end apart: 11 -> 10, of which waited for: 4 -> 3; matrix products, arithmetic and copies ran while one was open for 2% -> 2% of each run, Pallas kernels for 25% -> 21%
where the time goes in v6:
time: 56.8 us; the launch traced here: 56.5 us
  Pallas kernels  19.2 us (34%)
  waiting for transfers between devices  17.5 us (31%)
  starting transfers between devices  9.15 us (16%)
  local copies, waits for them, and re-layouts  9.14 us (16%)
  between operations  0.89 us (2%)
  other arithmetic  0.65 us (1%)
    ppermute x3, waiting for transfers between devices, cross(): lax.ppermute(part, 'tensor', shift(step))  15.5 us
    pallas_call x4, Pallas kernels, product(): pl.pallas_call(functools.partial(product_kernel, step, chip_count, chunks...  11.5 us
    unnamed x38, local copies, waits for them, and re-layouts  8.56 us
    pallas_call x3, Pallas kernels, finish(): pl.pallas_call(functools.partial(finish_kernel, first, tensor_count, mode...  6.2 us
    ppermute x3, starting transfers between devices, cross(): lax.ppermute(part, 'tensor', shift(step))  5.97 us
    ppermute x3, waiting for transfers between devices, add_halves(): lax.ppermute(send, 'tensor', swap)  2 us
    ppermute x3, starting transfers between devices, shards(): lax.ppermute(squares, 'tensor', [(i, (i + step) % tensor_count) for i in...  1.88 us
    pallas_call x3, Pallas kernels, add_halves(): pl.pallas_call(add_kernel, out_shape=jax.ShapeDtypeStruct(keep.shape, kee...  1.47 us
  transfers between devices with their start and end apart: 10, of which 3 were waited for; matrix products, arithmetic and copies ran while one was open for 2% of the time, Pallas kernels for 21%

profile of v6, /device:TPU:0, one launch (start us, length us, event | category | flops | bytes accessed | tf_op | source)
XLA Modules:
  0.0 56.5 jit_solution(7560258043502983959)
XLA Ops:
  0.0 0.7 %copy-done.13 = bf16[1024]{0:T(1024)(128)(2,1)S(1)} copy-done((bf16[1024]{0:T(1024)(128)(2,1)S(1)}, bf16[1024]{0:T(1024)(128)(2,1)}, u32[]{:S(2)}) %copy-start.13) | copy-done | bytes 2072
  0.7 4.1 %shard_map.55 = (bf16[512,512]{1,0:T(8,128)(2,1)S(1)}, bf16[512,512]{1,0:T(8,128)(2,1)}, bf16[1024,1024]{1,0:T(8,128)(2,1)S(1)}, bf16[512,1024]{1,0:T(8,128)(2,1)S(1)}) custom-call(bf16[1536,1024]{1,0:T(8,128)(2,1)} %tokens.7, bf16[1024]{0:T(1024)(128)(2,1)S(1)} %copy-done.13, bf16[1024,2048]{1,0:T(8,128)(2,1)} %weight.3), custom_call_target="tpu_custom_call" | custom-call | flops 1 | bytes 1 | tf_op jit(solution)/shard_map/pallas_call | solution.py:178
  4.8 0.0 copy-start.2
  4.8 0.0 copy-start.4
  4.8 0.0 copy-start.11
  4.8 0.5 collective-permute-start
  5.3 0.0 copy-done
  5.3 1.7 %shard_map.57 = (bf16[512,512]{1,0:T(8,128)(2,1)S(1)}, bf16[512,512]{1,0:T(8,128)(2,1)S(1)}, bf16[1024,1024]{1,0:T(8,128)(2,1)S(1)}) custom-call(bf16[1536,1024]{1,0:T(8,128)(2,1)S(1)} %copy-done, bf16[1024]{0:T(1024)(128)(2,1)S(1)} %copy-done.13, bf16[1024,1024]{1,0:T(8,128)(2,1)S(1)} %get-tuple-element.44.weight, ...), custom_call_target="tpu_custom_call" | custom-call | flops 1 | bytes 1 | tf_op jit(solution)/shard_map/pallas_call | solution.py:178
  7.1 1.3 %copy-done.6 = bf16[1024,1024]{1,0:T(8,128)(2,1)} copy-done((bf16[1024,1024]{1,0:T(8,128)(2,1)}, bf16[1024,1024]{1,0:T(8,128)(2,1)S(1)}, u32[]{:S(2)}) %copy-start.6) | copy-done | bytes 2097176
  8.4 0.8 %copy-done.9 = bf16[512,512]{1,0:T(8,128)(2,1)} copy-done((bf16[512,512]{1,0:T(8,128)(2,1)}, bf16[512,512]{1,0:T(8,128)(2,1)S(1)}, u32[]{:S(2)}) %copy-start.9) | copy-done | bytes 524312
  9.2 0.8 %copy-done.16 = bf16[512,512]{1,0:T(8,128)(2,1)} copy-done((bf16[512,512]{1,0:T(8,128)(2,1)}, bf16[512,512]{1,0:T(8,128)(2,1)S(1)}, u32[]{:S(2)}) %copy-start.16) | copy-done | bytes 524312
  10.0 0.1 pad_maximum_fusion
  10.1 0.0 collective-permute-done.received
  10.1 1.1 %copy-done.12 = bf16[512,512]{1,0:T(8,128)(2,1)S(1)} copy-done((bf16[512,512]{1,0:T(8,128)(2,1)S(1)}, bf16[512,512]{1,0:T(8,128)(2,1)}, u32[]{:S(2)}) %copy-start.12) | copy-done | bytes 524312
  11.2 1.2 %shard_map.56 = bf16[512,512]{1,0:T(8,128)(2,1)S(1)} custom-call(bf16[512,512]{1,0:T(8,128)(2,1)S(1)} %copy-done.12, bf16[512,512]{1,0:T(8,128)(2,1)} %collective-permute-done.received), custom_call_target="tpu_custom_call" | custom-call | flops 1 | bytes 1 | tf_op jit(solution)/shard_map/pallas_call | solution.py:259
  12.5 2.6 %collective-permute-start.1 = (bf16[512,512]{1,0:T(8,128)(2,1)S(1)}, bf16[512,512]{1,0:T(8,128)(2,1)S(1)}, u32[]{:S(2)}, u32[]{:S(2)}) collective-permute-start(bf16[512,512]{1,0:T(8,128)(2,1)S(1)} %shard_map.56), channel_id=1, source_target_pairs={{0,2},{1,3},{2,0},{3,1},{4,6},{5,7},{6,4},{7,5},{8,10},{9,11},{10,... | collective-permute-start | bytes 1572872 | tf_op jit(solution)/shard_map/ppermute | solution.py:269
  15.1 0.2 collective-permute-start.2
  15.3 0.1 fusion
  15.4 0.0 copy-start.1
  15.4 2.2 %copy-done.1 = bf16[1024,2048]{1,0:T(8,128)(2,1)S(1)} copy-done((bf16[1024,2048]{1,0:T(8,128)(2,1)S(1)}, bf16[1024,2048]{1,0:T(8,128)(2,1)}, u32[]{:S(2)}) %copy-start.1) | copy-done | bytes 4194328
  17.6 1.6 %copy-done.7 = bf16[1024,1024]{1,0:T(8,128)(2,1)S(1)} copy-done((bf16[1024,1024]{1,0:T(8,128)(2,1)S(1)}, bf16[1024,1024]{1,0:T(8,128)(2,1)}, u32[]{:S(2)}) %copy-start.7) | copy-done | bytes 2097176
  19.2 4.3 %shard_map.60 = (bf16[1536,512]{1,0:T(8,128)(2,1)S(1)}, bf16[1536,512]{1,0:T(8,128)(2,1)S(1)}, f32[12,128]{1,0:T(8,128)S(1)}, bf16[1024,1024]{1,0:T(8,128)(2,1)}) custom-call(bf16[1536,1024]{1,0:T(8,128)(2,1)S(1)} %copy-done, bf16[1024]{0:T(1024)(128)(2,1)S(1)} %copy-done.14, bf16[1024,2048]{1,0:T(8,128)(2,1)S(1)} %copy-done.1, ...), custom_call_target="tpu_custom_call" | custom-call | flops 1 | bytes 1 | tf_op jit(solution)/shard_map/pallas_call | solution.py:178
  23.5 0.4 collective-permute-start.3
  23.9 0.1 collective-permute-start.4
  24.0 1.4 %collective-permute-start.5 = (f32[12,128]{1,0:T(8,128)S(1)}, f32[12,128]{1,0:T(8,128)S(1)}, u32[]{:S(2)}, u32[]{:S(2)}) collective-permute-start(f32[12,128]{1,0:T(8,128)S(1)} %get-tuple-element.65.refs_6_), channel_id=1, source_target_pairs={{0,3},{1,0},{2,1},{3,2},{4,7},{5,4},{6,5},{7,6},{8,11},{9,8},{10,9... | collective-permute-start | bytes 18440 | tf_op jit(solution)/shard_map/ppermute | solution.py:284
  25.4 0.6 %dynamic_slice.3 = s32[1]{0:T(128)} dynamic-slice(s32[4]{0:T(128)S(1)} %copy-done.18, s32[]{:T(128)S(6)} %select_n.3), dynamic_slice_sizes={1} | dynamic-slice | bytes 12 | tf_op jit(solution)/shard_map/dynamic_slice | solution.py:287
  26.7 0.4 multiply_sine_fusion
  27.1 1.4 %shard_map.59 = (bf16[512,512]{1,0:T(8,128)(2,1)S(1)}, bf16[512,512]{1,0:T(8,128)(2,1)S(1)}) custom-call(bf16[1536,1024]{1,0:T(8,128)(2,1)S(1)} %copy-done, bf16[1024]{0:T(1024)(128)(2,1)S(1)} %copy-done.14, bf16[1024,1024]{1,0:T(8,128)(2,1)S(1)} %copy-done.5, bf16[512,1024]{1,0:T(8,128)(2,1)S(1)} %copy-done.3, bf16[1024,1024]{1,0:T(8,128)(2,1)S(1)} %copy-done.8), custom_call_target="tpu_custom_call" | custom-call | flops 1 | bytes 1 | tf_op jit(solution)/shard_map/pallas_call | solution.py:178
  28.5 0.0 copy-start.15
  28.5 0.0 collective-permute-done.2.received
  28.6 0.1 shard_map.58
  28.7 0.0 collective-permute-done.3.refs_7_
  28.7 0.0 collective-permute-done.4.refs_8_
  28.7 0.0 collective-permute-done.5.refs_9_
  28.7 0.0 collective-permute-done.1.refs_10_
  28.7 0.1 collective-permute-start.6
  28.8 0.5 collective-permute-start.7
  29.3 1.7 %collective-permute-start.9 = (bf16[512,512]{1,0:T(8,128)(2,1)S(1)}, bf16[512,512]{1,0:T(8,128)(2,1)S(1)}, u32[]{:S(2)}, u32[]{:S(2)}) collective-permute-start(bf16[512,512]{1,0:T(8,128)(2,1)S(1)} %shard_map.58), channel_id=1, source_target_pairs={{0,2},{1,3},{2,0},{3,1},{4,6},{5,7},{6,4},{7,5},{8,10},{9,11},{10,... | collective-permute-start | bytes 1572872 | tf_op jit(solution)/shard_map/ppermute | solution.py:269
  31.0 2.0 %collective-permute-done.7.received = bf16[512,512]{1,0:T(8,128)(2,1)S(1)} collective-permute-done((bf16[512,512]{1,0:T(8,128)(2,1)S(1)}, bf16[512,512]{1,0:T(8,128)(2,1)S(1)}, u32[]{:S(2)}, u32[]{:S(2)}) %collective-permute-start.7) | collective-permute-done | bytes 524320 | tf_op jit(solution)/shard_map/ppermute | solution.py:264
  33.0 0.1 shard_map.61
  33.1 1.7 %collective-permute-start.8 = (bf16[512,512]{1,0:T(8,128)(2,1)S(1)}, bf16[512,512]{1,0:T(8,128)(2,1)S(1)}, u32[]{:S(2)}, u32[]{:S(2)}) collective-permute-start(bf16[512,512]{1,0:T(8,128)(2,1)S(1)} %shard_map.61), channel_id=1, source_target_pairs={{0,2},{1,3},{2,0},{3,1},{4,6},{5,7},{6,4},{7,5},{8,10},{9,11},{10,... | collective-permute-start | bytes 1572872 | tf_op jit(solution)/shard_map/ppermute | solution.py:269
  34.8 0.0 collective-permute-done.6.refs_1_
  34.8 0.0 copy-done.15
  34.8 2.1 %shard_map.62.refs_11_ = bf16[1536,512]{1,0:T(8,128)(2,1)} custom-call(s32[4]{0:T(128)S(1)} %copy-done.15, bf16[1536,512]{1,0:T(8,128)(2,1)S(1)} %get-tuple-element.59.refs_0_.refs_11_, bf16[1536,512]{1,0:T(8,128)(2,1)S(1)} %collective-permute-done.6.refs_1_, f32[24,1,128]{2,1,0:T(1,128)S(1)} %get-tuple-element.61.refs_2_, ...), custom_call_target="tpu_custom_call" | custom-call | flops 1 | bytes 1 | tf_op jit(solution)/shard_map/pallas_call | solution.py:233
  36.9 7.2 %collective-permute-done.9.refs_10_ = bf16[512,512]{1,0:T(8,128)(2,1)S(1)} collective-permute-done((bf16[512,512]{1,0:T(8,128)(2,1)S(1)}, bf16[512,512]{1,0:T(8,128)(2,1)S(1)}, u32[]{:S(2)}, u32[]{:S(2)}) %collective-permute-start.9) | collective-permute-done | bytes 524320 | tf_op jit(solution)/shard_map/ppermute | solution.py:269
  44.1 2.1 %shard_map.63.refs_11_ = bf16[1536,512]{1,0:T(8,128)(2,1)} custom-call(s32[4]{0:T(128)S(1)} %copy-done.15, bf16[1536,512]{1,0:T(8,128)(2,1)S(1)} %get-tuple-element.59.refs_0_.refs_11_, bf16[1536,512]{1,0:T(8,128)(2,1)S(1)} %collective-permute-done.6.refs_1_, f32[24,1,128]{2,1,0:T(1,128)S(1)} %get-tuple-element.61.refs_2_, ...), custom_call_target="tpu_custom_call", output_to_operand_aliasing={{}: (12, {})} | custom-call | flops 1 | bytes 1 | tf_op jit(solution)/shard_map/pallas_call | solution.py:233
  46.2 8.3 %collective-permute-done.8.refs_10_ = bf16[512,512]{1,0:T(8,128)(2,1)S(1)} collective-permute-done((bf16[512,512]{1,0:T(8,128)(2,1)S(1)}, bf16[512,512]{1,0:T(8,128)(2,1)S(1)}, u32[]{:S(2)}, u32[]{:S(2)}) %collective-permute-start.8) | collective-permute-done | bytes 524320 | tf_op jit(solution)/shard_map/ppermute | solution.py:269
  54.5 2.1 %shard_map.64 = bf16[1536,512]{1,0:T(8,128)(2,1)} custom-call(s32[4]{0:T(128)S(1)} %copy-done.15, bf16[1536,512]{1,0:T(8,128)(2,1)S(1)} %get-tuple-element.59.refs_0_.refs_11_, bf16[1536,512]{1,0:T(8,128)(2,1)S(1)} %collective-permute-done.6.refs_1_, f32[24,1,128]{2,1,0:T(1,128)S(1)} %get-tuple-element.61.refs_2_, ...), custom_call_target="tpu_custom_call", output_to_operand_aliasing={{}: (12, {})} | custom-call | flops 1 | bytes 1 | tf_op jit(solution)/shard_map/pallas_call | solution.py:233
  (26 shorter events, 0.1 us)
Async XLA Ops:
  0.0 0.7 %copy-start.13 = (bf16[1024]{0:T(1024)(128)(2,1)S(1)}, bf16[1024]{0:T(1024)(128)(2,1)}, u32[]{:S(2)}) copy-start(bf16[1024]{0:T(1024)(128)(2,1)} %gain.4) | copy-start | bytes 6148
  0.7 4.6 %copy-start = (bf16[1536,1024]{1,0:T(8,128)(2,1)S(1)}, bf16[1536,1024]{1,0:T(8,128)(2,1)}, u32[]{:S(2)}) copy-start(bf16[1536,1024]{1,0:T(8,128)(2,1)} %tokens.7) | copy-start | bytes 9437188
  4.8 2.3 %copy-start.2 = (bf16[512,1024]{1,0:T(8,128)(2,1)}, bf16[512,1024]{1,0:T(8,128)(2,1)S(1)}, u32[]{:S(2)}) copy-start(bf16[512,1024]{1,0:T(8,128)(2,1)S(1)} %get-tuple-element.45.refs_0_) | copy-start | bytes 3145732
  4.8 2.3 %copy-start.4 = (bf16[1024,1024]{1,0:T(8,128)(2,1)}, bf16[1024,1024]{1,0:T(8,128)(2,1)S(1)}, u32[]{:S(2)}) copy-start(bf16[1024,1024]{1,0:T(8,128)(2,1)S(1)} %get-tuple-element.44.weight) | copy-start | bytes 6291460
  4.8 2.3 %copy-start.11 = (bf16[512,512]{1,0:T(8,128)(2,1)}, bf16[512,512]{1,0:T(8,128)(2,1)S(1)}, u32[]{:S(2)}) copy-start(bf16[512,512]{1,0:T(8,128)(2,1)S(1)} %get-tuple-element.41.keep) | copy-start | bytes 1572868
  4.8 5.3 %collective-permute-start = (bf16[512,512]{1,0:T(8,128)(2,1)}, bf16[512,512]{1,0:T(8,128)(2,1)}, u32[]{:S(2)}, u32[]{:S(2)}) collective-permute-start(bf16[512,512]{1,0:T(8,128)(2,1)} %get-tuple-element.42), channel_id=1, source_target_pairs={{0,1},{1,0},{2,3},{3,2},{4,5},{5,4},{6,7},{7,6},{8,9},{9,8},{10,11... | collective-permute-start | bytes 1572872 | tf_op jit(solution)/shard_map/ppermute | solution.py:264
  7.1 1.3 %copy-start.6 = (bf16[1024,1024]{1,0:T(8,128)(2,1)}, bf16[1024,1024]{1,0:T(8,128)(2,1)S(1)}, u32[]{:S(2)}) copy-start(bf16[1024,1024]{1,0:T(8,128)(2,1)S(1)} %get-tuple-element.52.refs_1_) | copy-start | bytes 6291460
  8.4 0.8 %copy-start.9 = (bf16[512,512]{1,0:T(8,128)(2,1)}, bf16[512,512]{1,0:T(8,128)(2,1)S(1)}, u32[]{:S(2)}) copy-start(bf16[512,512]{1,0:T(8,128)(2,1)S(1)} %get-tuple-element.49.keep) | copy-start | bytes 1572868
  9.2 0.8 %copy-start.16 = (bf16[512,512]{1,0:T(8,128)(2,1)}, bf16[512,512]{1,0:T(8,128)(2,1)S(1)}, u32[]{:S(2)}) copy-start(bf16[512,512]{1,0:T(8,128)(2,1)S(1)} %get-tuple-element.50) | copy-start | bytes 1572868
  10.0 5.4 %copy-start.14 = (bf16[1024]{0:T(1024)(128)(2,1)S(1)}, bf16[1024]{0:T(1024)(128)(2,1)}, u32[]{:S(2)}) copy-start(bf16[1024]{0:T(1024)(128)(2,1)} %gain.4) | copy-start | bytes 6148
  10.0 5.4 %copy-start.3 = (bf16[512,1024]{1,0:T(8,128)(2,1)S(1)}, bf16[512,1024]{1,0:T(8,128)(2,1)}, u32[]{:S(2)}) copy-start(bf16[512,1024]{1,0:T(8,128)(2,1)} %copy-done.2) | copy-start | bytes 3145732
  10.1 1.1 %copy-start.12 = (bf16[512,512]{1,0:T(8,128)(2,1)S(1)}, bf16[512,512]{1,0:T(8,128)(2,1)}, u32[]{:S(2)}) copy-start(bf16[512,512]{1,0:T(8,128)(2,1)} %copy-done.11) | copy-start | bytes 1572868
  11.2 3.8 %copy-start.17 = (bf16[512,512]{1,0:T(8,128)(2,1)S(1)}, bf16[512,512]{1,0:T(8,128)(2,1)}, u32[]{:S(2)}) copy-start(bf16[512,512]{1,0:T(8,128)(2,1)} %copy-done.16) | copy-start | bytes 1572868
  12.5 16.3 %collective-permute-start.1 = (bf16[512,512]{1,0:T(8,128)(2,1)S(1)}, bf16[512,512]{1,0:T(8,128)(2,1)S(1)}, u32[]{:S(2)}, u32[]{:S(2)}) collective-permute-start(bf16[512,512]{1,0:T(8,128)(2,1)S(1)} %shard_map.56), channel_id=1, source_target_pairs={{0,2},{1,3},{2,0},{3,1},{4,6},{5,7},{6,4},{7,5},{8,10},{9,11},{10,... | collective-permute-start | bytes 1572872 | tf_op jit(solution)/shard_map/ppermute | solution.py:269
  15.1 13.5 %collective-permute-start.2 = (bf16[512,512]{1,0:T(8,128)(2,1)S(1)}, bf16[512,512]{1,0:T(8,128)(2,1)S(1)}, u32[]{:S(2)}, u32[]{:S(2)}) collective-permute-start(bf16[512,512]{1,0:T(8,128)(2,1)S(1)} %copy-done.17), channel_id=1, source_target_pairs={{0,1},{1,0},{2,3},{3,2},{4,5},{5,4},{6,7},{7,6},{8,9},{9,8},{10,11... | collective-permute-start | bytes 1572872 | tf_op jit(solution)/shard_map/ppermute | solution.py:264
  15.4 2.2 %copy-start.1 = (bf16[1024,2048]{1,0:T(8,128)(2,1)S(1)}, bf16[1024,2048]{1,0:T(8,128)(2,1)}, u32[]{:S(2)}) copy-start(bf16[1024,2048]{1,0:T(8,128)(2,1)} %weight.3) | copy-start | bytes 12582916
  17.6 1.6 %copy-start.7 = (bf16[1024,1024]{1,0:T(8,128)(2,1)S(1)}, bf16[1024,1024]{1,0:T(8,128)(2,1)}, u32[]{:S(2)}) copy-start(bf16[1024,1024]{1,0:T(8,128)(2,1)} %copy-done.6) | copy-start | bytes 6291460
  19.2 6.2 %copy-start.18 = (s32[4]{0:T(128)S(1)}, s32[4]{0:T(128)}, u32[]{:S(2)}) copy-start(s32[4]{0:T(128)} %param.9) | copy-start | bytes 52
  19.2 7.9 %copy-start.5 = (bf16[1024,1024]{1,0:T(8,128)(2,1)S(1)}, bf16[1024,1024]{1,0:T(8,128)(2,1)}, u32[]{:S(2)}) copy-start(bf16[1024,1024]{1,0:T(8,128)(2,1)} %copy-done.4) | copy-start | bytes 6291460
  19.2 7.9 %copy-start.8 = (bf16[1024,1024]{1,0:T(8,128)(2,1)S(1)}, bf16[1024,1024]{1,0:T(8,128)(2,1)}, u32[]{:S(2)}) copy-start(bf16[1024,1024]{1,0:T(8,128)(2,1)} %copy-done.6) | copy-start | bytes 6291460
  23.5 5.1 %collective-permute-start.3 = (f32[12,128]{1,0:T(8,128)S(1)}, f32[12,128]{1,0:T(8,128)S(1)}, u32[]{:S(2)}, u32[]{:S(2)}) collective-permute-start(f32[12,128]{1,0:T(8,128)S(1)} %get-tuple-element.65.refs_6_), channel_id=1, source_target_pairs={{0,1},{1,2},{2,3},{3,0},{4,5},{5,6},{6,7},{7,4},{8,9},{9,10},{10,1... | collective-permute-start | bytes 18440 | tf_op jit(solution)/shard_map/ppermute | solution.py:284
  23.9 4.8 %collective-permute-start.4 = (f32[12,128]{1,0:T(8,128)S(1)}, f32[12,128]{1,0:T(8,128)S(1)}, u32[]{:S(2)}, u32[]{:S(2)}) collective-permute-start(f32[12,128]{1,0:T(8,128)S(1)} %get-tuple-element.65.refs_6_), channel_id=1, source_target_pairs={{0,2},{1,3},{2,0},{3,1},{4,6},{5,7},{6,4},{7,5},{8,10},{9,11},{10,... | collective-permute-start | bytes 18440 | tf_op jit(solution)/shard_map/ppermute | solution.py:284
  24.0 4.7 %collective-permute-start.5 = (f32[12,128]{1,0:T(8,128)S(1)}, f32[12,128]{1,0:T(8,128)S(1)}, u32[]{:S(2)}, u32[]{:S(2)}) collective-permute-start(f32[12,128]{1,0:T(8,128)S(1)} %get-tuple-element.65.refs_6_), channel_id=1, source_target_pairs={{0,3},{1,0},{2,1},{3,2},{4,7},{5,4},{6,5},{7,6},{8,11},{9,8},{10,9... | collective-permute-start | bytes 18440 | tf_op jit(solution)/shard_map/ppermute | solution.py:284
  27.1 1.4 %copy-start.10 = (bf16[512,512]{1,0:T(8,128)(2,1)S(1)}, bf16[512,512]{1,0:T(8,128)(2,1)}, u32[]{:S(2)}) copy-start(bf16[512,512]{1,0:T(8,128)(2,1)} %copy-done.9) | copy-start | bytes 1572868
  28.5 6.3 %copy-start.15 = (s32[4]{0:T(128)S(1)}, s32[4]{0:T(128)}, u32[]{:S(2)}) copy-start(s32[4]{0:T(128)} %live.5) | copy-start | bytes 52
  28.7 6.1 %collective-permute-start.6 = (bf16[1536,512]{1,0:T(8,128)(2,1)S(1)}, bf16[1536,512]{1,0:T(8,128)(2,1)S(1)}, u32[]{:S(2)}, u32[]{:S(2)}) collective-permute-start(bf16[1536,512]{1,0:T(8,128)(2,1)S(1)} %get-tuple-element.60), channel_id=1, source_target_pairs={{0,1},{1,0},{2,3},{3,2},{4,5},{5,4},{6,7},{7,6},{8,9},{9,8},{10,11... | collective-permute-start | bytes 4718600 | tf_op jit(solution)/shard_map/ppermute | solution.py:293
  28.8 4.1 %collective-permute-start.7 = (bf16[512,512]{1,0:T(8,128)(2,1)S(1)}, bf16[512,512]{1,0:T(8,128)(2,1)S(1)}, u32[]{:S(2)}, u32[]{:S(2)}) collective-permute-start(bf16[512,512]{1,0:T(8,128)(2,1)S(1)} %get-tuple-element.70), channel_id=1, source_target_pairs={{0,1},{1,0},{2,3},{3,2},{4,5},{5,4},{6,7},{7,6},{8,9},{9,8},{10,11... | collective-permute-start | bytes 1572872 | tf_op jit(solution)/shard_map/ppermute | solution.py:264
  29.3 14.8 %collective-permute-start.9 = (bf16[512,512]{1,0:T(8,128)(2,1)S(1)}, bf16[512,512]{1,0:T(8,128)(2,1)S(1)}, u32[]{:S(2)}, u32[]{:S(2)}) collective-permute-start(bf16[512,512]{1,0:T(8,128)(2,1)S(1)} %shard_map.58), channel_id=1, source_target_pairs={{0,2},{1,3},{2,0},{3,1},{4,6},{5,7},{6,4},{7,5},{8,10},{9,11},{10,... | collective-permute-start | bytes 1572872 | tf_op jit(solution)/shard_map/ppermute | solution.py:269
  33.1 21.4 %collective-permute-start.8 = (bf16[512,512]{1,0:T(8,128)(2,1)S(1)}, bf16[512,512]{1,0:T(8,128)(2,1)S(1)}, u32[]{:S(2)}, u32[]{:S(2)}) collective-permute-start(bf16[512,512]{1,0:T(8,128)(2,1)S(1)} %shard_map.61), channel_id=1, source_target_pairs={{0,2},{1,3},{2,0},{3,1},{4,6},{5,7},{6,4},{7,5},{8,10},{9,11},{10,... | collective-permute-start | bytes 1572872 | tf_op jit(solution)/shard_map/ppermute | solution.py:269

commit v7 on v6

v7 whole, which is shorter than its diff:
```python
import functools

import jax
import jax.numpy as jnp
import numpy as np
from jax import lax
from jax.experimental import pallas as pl
from jax.experimental.pallas import tpu as pltpu
from jax.sharding import PartitionSpec as P

HD = 128
PAGE = 256
BLOCK = 64
LANES = 128

rope_base = 500000.0
norm_eps = 1e-05

TILE = 256
CHUNKS = (2, 2, 2)

PARAMS = pltpu.CompilerParams(vmem_limit_bytes=16 * 1024 * 1024)
FIRST = pltpu.CompilerParams(vmem_limit_bytes=56 * 1024 * 1024)
COST = pl.CostEstimate(flops=1, bytes_accessed=1, transcendentals=0)


def square_sums(rows):
    total = jnp.zeros((rows.shape[0], LANES), jnp.float32)
    for part in range(rows.shape[1] // LANES):
        wide = rows[:, part * LANES : (part + 1) * LANES].astype(jnp.float32)
        total += wide * wide
    return total


def product_kernel(step, chip_count, chunks, staged, with_squares, tokens, gain, weight, *refs):
    refs = list(refs)
    outs = [refs.pop(0) for _ in range(2 * len(chunks))]
    squares = refs.pop(0) if with_squares else None
    depth, width = tokens.shape[1], 2 * outs[0].shape[1]
    me = lax.axis_index("tensor")
    core = lax.rem(me, 2)
    chip = lax.rem(lax.div(me, 2) + step, chip_count)
    place = pl.ds(pl.multiple_of(chip * width, width), width)

    weight_copies, row_copies = [], {}
    if staged:
        rows_buf, weight_buf, gain_buf, weight_sems, row_sems, gain_sem = refs
        cuts = weight_sems.shape[0]
        cut = depth // cuts
        gain_copy = pltpu.make_async_copy(gain, gain_buf, gain_sem)
        weight_copies = [
            pltpu.make_async_copy(
                weight.at[pl.ds(index * cut, cut), place],
                weight_buf.at[pl.ds(index * cut, cut), :],
                weight_sems.at[index],
            )
            for index in range(cuts)
        ]
        at = 0
        for first, count in chunks:
            for tile in range(first, first + count):
                buf = rows_buf.at[pl.ds(at * TILE, TILE), :]
                row_copies[tile] = (
                    pltpu.make_async_copy(tokens.at[pl.ds(tile * TILE, TILE), :], buf, row_sems.at[at]),
                    buf,
                )
                at += 1
        in_order = [copy for copy, _ in row_copies.values()]
        for copy in [gain_copy] + in_order[:1] + weight_copies + in_order[1:]:
            copy.start()
        gain_copy.wait()
        gains = gain_buf[...].reshape(1, depth)
    else:
        gains = gain[...].reshape(1, depth)

    for index, (first, count) in enumerate(chunks):
        for tile in range(first, first + count):
            if staged:
                row_copies[tile][0].wait()
                rows = row_copies[tile][1][...]
            else:
                rows = tokens[pl.ds(tile * TILE, TILE), :]
            scaled = rows * gains
            if weight_copies:
                product = jnp.zeros((TILE, width), jnp.float32)
                for part, copy in enumerate(weight_copies):
                    copy.wait()
                    span = slice(part * cut, (part + 1) * cut)
                    product += jnp.dot(
                        scaled[:, span], weight_buf[span, :], preferred_element_type=jnp.float32
                    )
                weight_copies = []
            else:
                columns = weight_buf[...] if staged else weight[:, place]
                product = jnp.dot(scaled, columns, preferred_element_type=jnp.float32)
            left = product[:, : width // 2].astype(jnp.bfloat16)
            right = product[:, width // 2 :].astype(jnp.bfloat16)
            inside = pl.ds((tile - first) * TILE, TILE)
            outs[2 * index][inside, :] = jnp.where(core == 0, left, right)
            outs[2 * index + 1][inside, :] = jnp.where(core == 0, right, left)
            if with_squares:
                total = square_sums(rows)
                for part in range(TILE // LANES):
                    turned = jnp.transpose(total[part * LANES : (part + 1) * LANES])
                    row = tile * (TILE // LANES) + part
                    squares[row : row + 1, :] = jnp.sum(turned, axis=0, keepdims=True)


def add_kernel(keep, received, out):
    out[...] = (keep[...].astype(jnp.float32) + received[...].astype(jnp.float32)).astype(out.dtype)


def table_kernel(span, frequencies, far_cos, far_sin, near_cos, near_sin):
    blocks = far_cos.shape[0]
    start = span[lax.axis_index("serve")] * PAGE
    first = start + BLOCK * lax.broadcasted_iota(jnp.int32, (blocks, HD), 0)
    far = first.astype(jnp.float32) * frequencies[...]
    near = lax.broadcasted_iota(jnp.int32, (BLOCK, HD), 0).astype(jnp.float32) * frequencies[...]
    far_cos[...] = jnp.cos(far)
    far_sin[...] = jnp.sin(far)
    near_cos[...] = jnp.cos(near)
    near_sin[...] = jnp.sin(near)


def finish_kernel(first_tile, tensor_count, model_dim, live, *refs):
    keep, received, far_cos, far_sin, near_cos, near_sin = refs[:6]
    squares, arrived, out = refs[6 : 6 + tensor_count], refs[6 + tensor_count : -2], refs[-1]
    values = keep[...].astype(jnp.float32) + received[...].astype(jnp.float32)
    for part in arrived:
        values += part[...].astype(jnp.float32)
    on_diagonal = lax.broadcasted_iota(jnp.int32, (LANES, LANES), 0) == lax.broadcasted_iota(
        jnp.int32, (LANES, LANES), 1
    )
    tile = first_tile + pl.program_id(0)
    columns = []
    for part in range(TILE // LANES):
        row = pl.ds(tile * (TILE // LANES) + part, 1)
        totals = functools.reduce(jnp.add, [ref[row, :] for ref in squares])
        columns.append(jnp.sum(jnp.where(on_diagonal, totals, 0.0), axis=1, keepdims=True))
    scales = 1.0 / jnp.sqrt(jnp.concatenate(columns, axis=0) / model_dim + norm_eps)
    row = tile * TILE + lax.broadcasted_iota(jnp.int32, (TILE, 1), 0)
    alive = row < live[lax.axis_index("serve")] * BLOCK
    sign = jnp.where(lax.broadcasted_iota(jnp.int32, (1, HD), 1) < HD // 2, -1.0, 1.0)
    cosines, sines = [], []
    for part in range(TILE // BLOCK):
        block = pl.ds(tile * (TILE // BLOCK) + part, 1)
        block_cos = far_cos[block, :]
        block_sin = far_sin[block, :]
        cosines.append(block_cos * near_cos[...] - block_sin * near_sin[...])
        sines.append((sign * block_sin) * near_cos[...] + (sign * block_cos) * near_sin[...])
    cosine = jnp.concatenate(cosines, axis=0)
    sine = jnp.concatenate(sines, axis=0)
    for start in range(0, out.shape[1], 2 * HD):
        key = values[:, start : start + HD] * scales
        turned = key * cosine + pltpu.roll(key, HD // 2, 1) * sine
        out[:, start : start + HD] = jnp.where(alive, turned, 0.0).astype(out.dtype)
        value = values[:, start + HD : start + 2 * HD] * scales
        out[:, start + HD : start + 2 * HD] = jnp.where(alive, value, 0.0).astype(out.dtype)


def shards(tokens, norm_gain, kv_weight, live_blocks, span_offset):
    tensor_count = lax.axis_size("tensor")
    chip_count = tensor_count // 2
    me = lax.axis_index("tensor")
    slot_rows, depth = tokens.shape
    columns = kv_weight.shape[1] // tensor_count
    tiles = slot_rows // TILE
    model_dim = depth * tensor_count

    swap = [(i, i ^ 1) for i in range(tensor_count)]

    def shift(step):
        return [(i, (i + 2 * step) % tensor_count) for i in range(tensor_count)]

    def product(gain, step, chunks, staged=False, with_squares=False):
        vmem = pl.BlockSpec(memory_space=pltpu.VMEM)
        out_shape = [
            jax.ShapeDtypeStruct((count * TILE, columns), jnp.bfloat16) for _, count in chunks for _ in range(2)
        ]
        if with_squares:
            out_shape.append(jax.ShapeDtypeStruct((slot_rows // LANES, LANES), jnp.float32))
        count = sum(count for _, count in chunks)
        scratch = [
            pltpu.VMEM((count * TILE, depth), jnp.bfloat16),
            pltpu.VMEM((depth, 2 * columns), jnp.bfloat16),
            pltpu.VMEM((depth,), jnp.bfloat16),
            pltpu.SemaphoreType.DMA((4,)),
            pltpu.SemaphoreType.DMA((count,)),
            pltpu.SemaphoreType.DMA,
        ]
        made = pl.pallas_call(
            functools.partial(product_kernel, step, chip_count, chunks, staged, with_squares),
            in_specs=[pl.BlockSpec(memory_space=pltpu.HBM) if staged else vmem] * 3,
            out_shape=out_shape,
            out_specs=[vmem] * len(out_shape),
            scratch_shapes=scratch if staged else [],
            compiler_params=FIRST if staged else PARAMS,
            cost_estimate=COST,
        )(tokens, gain, kv_weight)
        made = list(made)
        squares = made.pop() if with_squares else None
        return list(zip(made[::2], made[1::2])), squares

    def tables(span_offset):
        frequencies = rope_base ** (-(np.arange(HD // 2, dtype=np.float32) * 2.0) / HD)
        frequencies = np.concatenate([frequencies, frequencies])[None, :].astype(np.float32)
        shapes = [(slot_rows // BLOCK, HD)] * 2 + [(BLOCK, HD)] * 2
        made = pl.pallas_call(
            table_kernel,
            in_specs=[pl.BlockSpec(memory_space=pltpu.SMEM), pl.BlockSpec(memory_space=pltpu.VMEM)],
            out_shape=[jax.ShapeDtypeStruct(shape, jnp.float32) for shape in shapes],
            out_specs=[pl.BlockSpec(memory_space=pltpu.VMEM)] * 4,
            compiler_params=PARAMS,
            cost_estimate=COST,
        )(span_offset, jnp.asarray(frequencies))
        return list(made)

    def finish(first, count, keep, received, table, squares, arrived, result):
        operands = [keep, received] + table + squares + arrived
        specs = (
            [pl.BlockSpec((TILE, columns), lambda i, *_: (first + i, 0))] * 2
            + [pl.BlockSpec((slot_rows // BLOCK, HD), lambda i, *_: (0, 0))] * 2
            + [pl.BlockSpec((BLOCK, HD), lambda i, *_: (0, 0))] * 2
            + [pl.BlockSpec((slot_rows // LANES, LANES), lambda i, *_: (0, 0))] * tensor_count
            + [pl.BlockSpec((TILE, columns), lambda i, *_: (i, 0))] * len(arrived)
        )
        if result is None:
            result = keep
            aliases = {}
        else:
            aliases = {1 + len(operands): 0}
        return pl.pallas_call(
            functools.partial(finish_kernel, first, tensor_count, model_dim),
            grid_spec=pltpu.PrefetchScalarGridSpec(
                num_scalar_prefetch=1,
                grid=(count,),
                in_specs=specs + [pl.BlockSpec(memory_space=pl.ANY)],
                out_specs=pl.BlockSpec((TILE, columns), lambda i, *_: (first + i, 0)),
            ),
            out_shape=jax.ShapeDtypeStruct((slot_rows, columns), jnp.bfloat16),
            input_output_aliases=aliases,
            compiler_params=PARAMS,
            cost_estimate=COST,
        )(live_blocks, *operands, result)

    others = range(1, chip_count)
    firsts = [sum(CHUNKS[:index]) for index in range(len(CHUNKS))]
    chunk_count = len(CHUNKS)

    def start_chunk(gain, index, staged=False):
        made = []
        for step in others:
            made += product(gain, step, [(firsts[index], CHUNKS[index])], staged)[0]
        return made

    def add_halves(made):
        return [
            pl.pallas_call(
                add_kernel,
                out_shape=jax.ShapeDtypeStruct(keep.shape, keep.dtype),
                compiler_params=PARAMS,
                cost_estimate=COST,
            )(keep, lax.ppermute(send, "tensor", swap))
            for keep, send in made
        ]

    def cross(sums):
        return [lax.ppermute(part, "tensor", shift(step)) for step, part in zip(others, sums)]

    hold = lax.optimization_barrier
    made = start_chunk(norm_gain, 0, staged=True)
    made, gain = hold((made, norm_gain))
    sums = add_halves(made)
    made = start_chunk(gain, 1)
    sums, made, gain, span_offset = hold((sums, made, gain, span_offset))

    arrived = cross(sums)
    sums = add_halves(made)
    waiting = [start_chunk(gain, index) for index in range(2, chunk_count)]
    ((keep, send),), squares = product(gain, 0, [(0, tiles)], with_squares=True)
    squares = [squares] + [
        lax.ppermute(squares, "tensor", [(i, (i + step) % tensor_count) for i in range(tensor_count)])
        for step in range(1, tensor_count)
    ]
    table = tables(span_offset)
    arrived, sums, waiting, keep, send, squares, table = hold(
        (arrived, sums, waiting, keep, send, squares, table)
    )

    arrivals = [arrived, cross(sums)] + [cross(add_halves(made)) for made in waiting]
    received = lax.ppermute(send, "tensor", swap)
    result = None
    for index in range(chunk_count):
        result = finish(
            firsts[index], CHUNKS[index], keep, received, table, squares, arrivals[index], result
        )
    return result


def solution(mesh):
    in_specs = (
        P(("groups", "serve"), "tensor"),
        P("tensor"),
        P("tensor", None),
        P("groups"),
        P("groups"),
    )
    out_specs = P(("groups", "serve"), "tensor")
    return jax.shard_map(shards, mesh=mesh, in_specs=in_specs, out_specs=out_specs, check_vma=False)
```

time: 56.8 us -> 50.3 us (0.89)
  local copies, waits for them, and re-layouts: 9.14 us -> 0.04 us
  waiting for transfers between devices: 17.5 us -> 22.9 us
  Pallas kernels: 19.2 us -> 17.7 us
  between operations: 0.89 us -> 0.13 us
  other arithmetic: 0.65 us -> 0 us
    unnamed x38 -> x14, local copies, waits for them, and re-layouts: 8.56 us -> 0.04 us
    ppermute x3, waiting for transfers between devices: 0.01 us -> 5.1 us  [shards(): lax.ppermute(squares, 'tensor', [(i, (i + step) % tensor_count) for i in...]
    pallas_call x4, Pallas kernels: 11.5 us -> 10.4 us  [product(): pl.pallas_call(functools.partial(product_kernel, step, chip_count, chunks...]
    pallas_call x3, Pallas kernels: 1.47 us -> 0.37 us  [add_halves(): pl.pallas_call(add_kernel, out_shape=jax.ShapeDtypeStruct(keep.shape, kee...]
    pallas_call x0 -> x1, Pallas kernels: none -> 0.72 us  [tables(): pl.pallas_call(table_kernel, in_specs=[pl.BlockSpec(memory_space=pltpu.SM...]
    dynamic_slice x1 -> x0, local copies, waits for them, and re-layouts: 0.58 us -> none  [shards(): table = tables(span_offset[own_index])]
  transfers between devices with their start and end apart: 10 -> 10, of which waited for: 3 -> 6; matrix products, arithmetic and copies ran while one was open for 2% -> 0% of each run, Pallas kernels for 21% -> 23%
where the time goes in v7:
time: 50.3 us; the launch traced here: 50.1 us
  waiting for transfers between devices  22.9 us (46%)
  Pallas kernels  17.7 us (35%)
  starting transfers between devices  9.42 us (19%)
    ppermute x3, waiting for transfers between devices, cross(): lax.ppermute(part, 'tensor', shift(step))  15.4 us
    pallas_call x4, Pallas kernels, product(): pl.pallas_call(functools.partial(product_kernel, step, chip_count, chunks...  10.4 us
    pallas_call x3, Pallas kernels, finish(): pl.pallas_call(functools.partial(finish_kernel, first, tensor_count, mode...  6.22 us
    ppermute x3, starting transfers between devices, cross(): lax.ppermute(part, 'tensor', shift(step))  6.19 us
    ppermute x3, waiting for transfers between devices, shards(): lax.ppermute(squares, 'tensor', [(i, (i + step) % tensor_count) for i in...  5.1 us
    ppermute x3, waiting for transfers between devices, add_halves(): lax.ppermute(send, 'tensor', swap)  2.37 us
    ppermute x3, starting transfers between devices, shards(): lax.ppermute(squares, 'tensor', [(i, (i + step) % tensor_count) for i in...  1.76 us
    ppermute x3, starting transfers between devices, add_halves(): lax.ppermute(send, 'tensor', swap)  1.46 us
  transfers between devices with their start and end apart: 10, of which 6 were waited for; matrix products, arithmetic and copies ran while one was open for 0% of the time, Pallas kernels for 23%

profile of v7, /device:TPU:0, one launch (start us, length us, event | category | flops | bytes accessed | tf_op | source)
XLA Modules:
  0.0 50.1 jit_solution(17847653019135979586)
XLA Ops:
  0.0 0.0 copy-start.3
  0.0 0.0 copy-start
  0.0 0.0 copy-start.1
  0.0 4.1 %shard_map.64 = (bf16[512,512]{1,0:T(8,128)(2,1)}, bf16[512,512]{1,0:T(8,128)(2,1)}) custom-call(bf16[1536,1024]{1,0:T(8,128)(2,1)} %tokens.7, bf16[1024]{0:T(1024)(128)(2,1)} %gain.4, bf16[1024,2048]{1,0:T(8,128)(2,1)} %weight.7), custom_call_target="tpu_custom_call" | custom-call | flops 1 | bytes 1 | tf_op jit(solution)/shard_map/pallas_call | solution.py:191
  4.1 0.0 copy-start.2
  4.1 0.5 %collective-permute-start = (bf16[512,512]{1,0:T(8,128)(2,1)}, bf16[512,512]{1,0:T(8,128)(2,1)S(1)}, u32[]{:S(2)}, u32[]{:S(2)}) collective-permute-start(bf16[512,512]{1,0:T(8,128)(2,1)} %get-tuple-element.43), channel_id=1, source_target_pairs={{0,1},{1,0},{2,3},{3,2},{4,5},{5,4},{6,7},{7,6},{8,9},{9,8},{10,11... | collective-permute-start | bytes 1572872 | tf_op jit(solution)/shard_map/ppermute | solution.py:263
  4.6 0.0 copy-done.3
  4.6 0.0 copy-done
  4.7 0.0 copy-done.1
  4.7 1.3 %shard_map.66 = (bf16[512,512]{1,0:T(8,128)(2,1)S(1)}, bf16[512,512]{1,0:T(8,128)(2,1)S(1)}) custom-call(bf16[1536,1024]{1,0:T(8,128)(2,1)S(1)} %copy-done.1, bf16[1024]{0:T(1024)(128)(2,1)S(1)} %copy-done.3, bf16[1024,2048]{1,0:T(8,128)(2,1)S(1)} %copy-done), custom_call_target="tpu_custom_call" | custom-call | flops 1 | bytes 1 | tf_op jit(solution)/shard_map/pallas_call | solution.py:191
  5.9 0.5 collective-permute-done.received
  6.4 0.0 copy-done.2
  6.4 0.1 shard_map.65
  6.5 0.4 collective-permute-start.2
  7.0 2.6 %collective-permute-start.1 = (bf16[512,512]{1,0:T(8,128)(2,1)S(1)}, bf16[512,512]{1,0:T(8,128)(2,1)S(1)}, u32[]{:S(2)}, u32[]{:S(2)}) collective-permute-start(bf16[512,512]{1,0:T(8,128)(2,1)S(1)} %shard_map.65), channel_id=1, source_target_pairs={{0,2},{1,3},{2,0},{3,1},{4,6},{5,7},{6,4},{7,5},{8,10},{9,11},{10,... | collective-permute-start | bytes 1572872 | tf_op jit(solution)/shard_map/ppermute | solution.py:268
  9.6 3.7 %shard_map.69 = (bf16[1536,512]{1,0:T(8,128)(2,1)S(1)}, bf16[1536,512]{1,0:T(8,128)(2,1)S(1)}, f32[12,128]{1,0:T(8,128)S(1)}) custom-call(bf16[1536,1024]{1,0:T(8,128)(2,1)S(1)} %copy-done.1, bf16[1024]{0:T(1024)(128)(2,1)S(1)} %copy-done.3, bf16[1024,2048]{1,0:T(8,128)(2,1)S(1)} %copy-done), custom_call_target="tpu_custom_call" | custom-call | flops 1 | bytes 1 | tf_op jit(solution)/shard_map/pallas_call | solution.py:191
  13.3 0.0 copy-start.5
  13.3 0.0 copy-start.6
  13.4 0.1 collective-permute-start.5
  13.4 1.7 %collective-permute-start.4 = (f32[12,128]{1,0:T(8,128)S(1)}, f32[12,128]{1,0:T(8,128)S(1)}, u32[]{:S(2)}, u32[]{:S(2)}) collective-permute-start(f32[12,128]{1,0:T(8,128)S(1)} %get-tuple-element.67.refs_6_), channel_id=1, source_target_pairs={{0,2},{1,3},{2,0},{3,1},{4,6},{5,7},{6,4},{7,5},{8,10},{9,11},{10,... | collective-permute-start | bytes 18440 | tf_op jit(solution)/shard_map/ppermute | solution.py:282
  15.1 0.0 collective-permute-start.3
  15.1 1.3 %shard_map.68 = (bf16[512,512]{1,0:T(8,128)(2,1)S(1)}, bf16[512,512]{1,0:T(8,128)(2,1)S(1)}) custom-call(bf16[1536,1024]{1,0:T(8,128)(2,1)S(1)} %copy-done.1, bf16[1024]{0:T(1024)(128)(2,1)S(1)} %copy-done.3, bf16[1024,2048]{1,0:T(8,128)(2,1)S(1)} %copy-done), custom_call_target="tpu_custom_call" | custom-call | flops 1 | bytes 1 | tf_op jit(solution)/shard_map/pallas_call | solution.py:191
  16.4 0.0 copy-done.5
  16.4 0.0 copy-done.6
  16.4 0.7 %shard_map.70 = (f32[24,128]{1,0:T(8,128)S(1)}, f32[24,128]{1,0:T(8,128)S(1)}, f32[64,128]{1,0:T(8,128)S(1)}, f32[64,128]{1,0:T(8,128)S(1)}) custom-call(s32[4]{0:T(128)S(1)} %copy-done.5, f32[1,128]{1,0:T(1,128)S(1)} %copy-done.6), custom_call_target="tpu_custom_call" | custom-call | flops 1 | bytes 1 | tf_op jit(solution)/shard_map/pallas_call | solution.py:208
  17.1 0.0 copy-start.4
  17.2 0.0 collective-permute-done.2.received
  17.2 0.1 shard_map.67
  17.3 4.3 %collective-permute-done.5.refs_9_ = f32[12,128]{1,0:T(8,128)S(1)} collective-permute-done((f32[12,128]{1,0:T(8,128)S(1)}, f32[12,128]{1,0:T(8,128)S(1)}, u32[]{:S(2)}, u32[]{:S(2)}) %collective-permute-start.5) | collective-permute-done | bytes 6176 | tf_op jit(solution)/shard_map/ppermute | solution.py:282
  21.6 0.8 %collective-permute-done.4.refs_8_ = f32[12,128]{1,0:T(8,128)S(1)} collective-permute-done((f32[12,128]{1,0:T(8,128)S(1)}, f32[12,128]{1,0:T(8,128)S(1)}, u32[]{:S(2)}, u32[]{:S(2)}) %collective-permute-start.4) | collective-permute-done | bytes 6176 | tf_op jit(solution)/shard_map/ppermute | solution.py:282
  22.4 0.0 collective-permute-done.3.refs_7_
  22.4 0.0 collective-permute-done.1.refs_10_
  22.4 0.0 collective-permute-start.6
  22.4 0.5 collective-permute-start.7
  22.9 1.7 %collective-permute-start.9 = (bf16[512,512]{1,0:T(8,128)(2,1)S(1)}, bf16[512,512]{1,0:T(8,128)(2,1)S(1)}, u32[]{:S(2)}, u32[]{:S(2)}) collective-permute-start(bf16[512,512]{1,0:T(8,128)(2,1)S(1)} %shard_map.67), channel_id=1, source_target_pairs={{0,2},{1,3},{2,0},{3,1},{4,6},{5,7},{6,4},{7,5},{8,10},{9,11},{10,... | collective-permute-start | bytes 1572872 | tf_op jit(solution)/shard_map/ppermute | solution.py:268
  24.7 1.9 %collective-permute-done.7.received = bf16[512,512]{1,0:T(8,128)(2,1)S(1)} collective-permute-done((bf16[512,512]{1,0:T(8,128)(2,1)S(1)}, bf16[512,512]{1,0:T(8,128)(2,1)S(1)}, u32[]{:S(2)}, u32[]{:S(2)}) %collective-permute-start.7) | collective-permute-done | bytes 524320 | tf_op jit(solution)/shard_map/ppermute | solution.py:263
  26.6 0.1 shard_map.71
  26.7 1.8 %collective-permute-start.8 = (bf16[512,512]{1,0:T(8,128)(2,1)S(1)}, bf16[512,512]{1,0:T(8,128)(2,1)S(1)}, u32[]{:S(2)}, u32[]{:S(2)}) collective-permute-start(bf16[512,512]{1,0:T(8,128)(2,1)S(1)} %shard_map.71), channel_id=1, source_target_pairs={{0,2},{1,3},{2,0},{3,1},{4,6},{5,7},{6,4},{7,5},{8,10},{9,11},{10,... | collective-permute-start | bytes 1572872 | tf_op jit(solution)/shard_map/ppermute | solution.py:268
  28.5 0.0 collective-permute-done.6.refs_1_
  28.5 0.0 copy-done.4
  28.5 2.1 %shard_map.72.refs_11_ = bf16[1536,512]{1,0:T(8,128)(2,1)} custom-call(s32[4]{0:T(128)S(1)} %copy-done.4, bf16[1536,512]{1,0:T(8,128)(2,1)S(1)} %get-tuple-element.61.refs_0_.refs_11_, bf16[1536,512]{1,0:T(8,128)(2,1)S(1)} %collective-permute-done.6.refs_1_, f32[24,128]{1,0:T(8,128)S(1)} %get-tuple-element.63.refs_2_, ...), custom_call_target="tpu_custom_call" | custom-call | flops 1 | bytes 1 | tf_op jit(solution)/shard_map/pallas_call | solution.py:232
  30.6 7.1 %collective-permute-done.9.refs_10_ = bf16[512,512]{1,0:T(8,128)(2,1)S(1)} collective-permute-done((bf16[512,512]{1,0:T(8,128)(2,1)S(1)}, bf16[512,512]{1,0:T(8,128)(2,1)S(1)}, u32[]{:S(2)}, u32[]{:S(2)}) %collective-permute-start.9) | collective-permute-done | bytes 524320 | tf_op jit(solution)/shard_map/ppermute | solution.py:268
  37.7 2.1 %shard_map.73.refs_11_ = bf16[1536,512]{1,0:T(8,128)(2,1)} custom-call(s32[4]{0:T(128)S(1)} %copy-done.4, bf16[1536,512]{1,0:T(8,128)(2,1)S(1)} %get-tuple-element.61.refs_0_.refs_11_, bf16[1536,512]{1,0:T(8,128)(2,1)S(1)} %collective-permute-done.6.refs_1_, f32[24,128]{1,0:T(8,128)S(1)} %get-tuple-element.63.refs_2_, ...), custom_call_target="tpu_custom_call", output_to_operand_aliasing={{}: (12, {})} | custom-call | flops 1 | bytes 1 | tf_op jit(solution)/shard_map/pallas_call | solution.py:232
  39.8 8.3 %collective-permute-done.8.refs_10_ = bf16[512,512]{1,0:T(8,128)(2,1)S(1)} collective-permute-done((bf16[512,512]{1,0:T(8,128)(2,1)S(1)}, bf16[512,512]{1,0:T(8,128)(2,1)S(1)}, u32[]{:S(2)}, u32[]{:S(2)}) %collective-permute-start.8) | collective-permute-done | bytes 524320 | tf_op jit(solution)/shard_map/ppermute | solution.py:268
  48.0 2.1 %shard_map.74 = bf16[1536,512]{1,0:T(8,128)(2,1)} custom-call(s32[4]{0:T(128)S(1)} %copy-done.4, bf16[1536,512]{1,0:T(8,128)(2,1)S(1)} %get-tuple-element.61.refs_0_.refs_11_, bf16[1536,512]{1,0:T(8,128)(2,1)S(1)} %collective-permute-done.6.refs_1_, f32[24,128]{1,0:T(8,128)S(1)} %get-tuple-element.63.refs_2_, ...), custom_call_target="tpu_custom_call", output_to_operand_aliasing={{}: (12, {})} | custom-call | flops 1 | bytes 1 | tf_op jit(solution)/shard_map/pallas_call | solution.py:232
Async XLA Ops:
  0.0 4.6 %copy-start.3 = (bf16[1024]{0:T(1024)(128)(2,1)S(1)}, bf16[1024]{0:T(1024)(128)(2,1)}, u32[]{:S(2)}) copy-start(bf16[1024]{0:T(1024)(128)(2,1)} %gain.4) | copy-start | bytes 6148
  0.0 4.6 %copy-start = (bf16[1024,2048]{1,0:T(8,128)(2,1)S(1)}, bf16[1024,2048]{1,0:T(8,128)(2,1)}, u32[]{:S(2)}) copy-start(bf16[1024,2048]{1,0:T(8,128)(2,1)} %weight.7) | copy-start | bytes 12582916
  0.0 4.6 %copy-start.1 = (bf16[1536,1024]{1,0:T(8,128)(2,1)S(1)}, bf16[1536,1024]{1,0:T(8,128)(2,1)}, u32[]{:S(2)}) copy-start(bf16[1536,1024]{1,0:T(8,128)(2,1)} %tokens.7) | copy-start | bytes 9437188
  4.1 2.3 %copy-start.2 = (bf16[512,512]{1,0:T(8,128)(2,1)S(1)}, bf16[512,512]{1,0:T(8,128)(2,1)}, u32[]{:S(2)}) copy-start(bf16[512,512]{1,0:T(8,128)(2,1)} %get-tuple-element.42.keep) | copy-start | bytes 1572868
  4.1 2.3 %collective-permute-start = (bf16[512,512]{1,0:T(8,128)(2,1)}, bf16[512,512]{1,0:T(8,128)(2,1)S(1)}, u32[]{:S(2)}, u32[]{:S(2)}) collective-permute-start(bf16[512,512]{1,0:T(8,128)(2,1)} %get-tuple-element.43), channel_id=1, source_target_pairs={{0,1},{1,0},{2,3},{3,2},{4,5},{5,4},{6,7},{7,6},{8,9},{9,8},{10,11... | collective-permute-start | bytes 1572872 | tf_op jit(solution)/shard_map/ppermute | solution.py:263
  6.5 10.6 %collective-permute-start.2 = (bf16[512,512]{1,0:T(8,128)(2,1)S(1)}, bf16[512,512]{1,0:T(8,128)(2,1)S(1)}, u32[]{:S(2)}, u32[]{:S(2)}) collective-permute-start(bf16[512,512]{1,0:T(8,128)(2,1)S(1)} %get-tuple-element.49), channel_id=1, source_target_pairs={{0,1},{1,0},{2,3},{3,2},{4,5},{5,4},{6,7},{7,6},{8,9},{9,8},{10,11... | collective-permute-start | bytes 1572872 | tf_op jit(solution)/shard_map/ppermute | solution.py:263
  7.0 15.4 %collective-permute-start.1 = (bf16[512,512]{1,0:T(8,128)(2,1)S(1)}, bf16[512,512]{1,0:T(8,128)(2,1)S(1)}, u32[]{:S(2)}, u32[]{:S(2)}) collective-permute-start(bf16[512,512]{1,0:T(8,128)(2,1)S(1)} %shard_map.65), channel_id=1, source_target_pairs={{0,2},{1,3},{2,0},{3,1},{4,6},{5,7},{6,4},{7,5},{8,10},{9,11},{10,... | collective-permute-start | bytes 1572872 | tf_op jit(solution)/shard_map/ppermute | solution.py:268
  13.3 3.1 %copy-start.5 = (s32[4]{0:T(128)S(1)}, s32[4]{0:T(128)}, u32[]{:S(2)}) copy-start(s32[4]{0:T(128)} %span) | copy-start | bytes 52
  13.3 3.1 %copy-start.6 = (f32[1,128]{1,0:T(1,128)S(1)}, f32[1,128]{1,0:T(1,128)}, u32[]{:S(2)}) copy-start(f32[1,128]{1,0:T(1,128)} %constant.2.clone.frequencies) | copy-start | bytes 1540
  13.4 8.2 %collective-permute-start.5 = (f32[12,128]{1,0:T(8,128)S(1)}, f32[12,128]{1,0:T(8,128)S(1)}, u32[]{:S(2)}, u32[]{:S(2)}) collective-permute-start(f32[12,128]{1,0:T(8,128)S(1)} %get-tuple-element.67.refs_6_), channel_id=1, source_target_pairs={{0,3},{1,0},{2,1},{3,2},{4,7},{5,4},{6,5},{7,6},{8,11},{9,8},{10,9... | collective-permute-start | bytes 18440 | tf_op jit(solution)/shard_map/ppermute | solution.py:282
  13.4 9.0 %collective-permute-start.4 = (f32[12,128]{1,0:T(8,128)S(1)}, f32[12,128]{1,0:T(8,128)S(1)}, u32[]{:S(2)}, u32[]{:S(2)}) collective-permute-start(f32[12,128]{1,0:T(8,128)S(1)} %get-tuple-element.67.refs_6_), channel_id=1, source_target_pairs={{0,2},{1,3},{2,0},{3,1},{4,6},{5,7},{6,4},{7,5},{8,10},{9,11},{10,... | collective-permute-start | bytes 18440 | tf_op jit(solution)/shard_map/ppermute | solution.py:282
  15.1 7.3 %collective-permute-start.3 = (f32[12,128]{1,0:T(8,128)S(1)}, f32[12,128]{1,0:T(8,128)S(1)}, u32[]{:S(2)}, u32[]{:S(2)}) collective-permute-start(f32[12,128]{1,0:T(8,128)S(1)} %get-tuple-element.67.refs_6_), channel_id=1, source_target_pairs={{0,1},{1,2},{2,3},{3,0},{4,5},{5,6},{6,7},{7,4},{8,9},{9,10},{10,1... | collective-permute-start | bytes 18440 | tf_op jit(solution)/shard_map/ppermute | solution.py:282
  17.1 11.4 %copy-start.4 = (s32[4]{0:T(128)S(1)}, s32[4]{0:T(128)}, u32[]{:S(2)}) copy-start(s32[4]{0:T(128)} %live.5) | copy-start | bytes 52
  22.4 6.1 %collective-permute-start.6 = (bf16[1536,512]{1,0:T(8,128)(2,1)S(1)}, bf16[1536,512]{1,0:T(8,128)(2,1)S(1)}, u32[]{:S(2)}, u32[]{:S(2)}) collective-permute-start(bf16[1536,512]{1,0:T(8,128)(2,1)S(1)} %get-tuple-element.62), channel_id=1, source_target_pairs={{0,1},{1,0},{2,3},{3,2},{4,5},{5,4},{6,7},{7,6},{8,9},{9,8},{10,11... | collective-permute-start | bytes 4718600 | tf_op jit(solution)/shard_map/ppermute | solution.py:291
  22.4 4.2 %collective-permute-start.7 = (bf16[512,512]{1,0:T(8,128)(2,1)S(1)}, bf16[512,512]{1,0:T(8,128)(2,1)S(1)}, u32[]{:S(2)}, u32[]{:S(2)}) collective-permute-start(bf16[512,512]{1,0:T(8,128)(2,1)S(1)} %get-tuple-element.72), channel_id=1, source_target_pairs={{0,1},{1,0},{2,3},{3,2},{4,5},{5,4},{6,7},{7,6},{8,9},{9,8},{10,11... | collective-permute-start | bytes 1572872 | tf_op jit(solution)/shard_map/ppermute | solution.py:263
  22.9 14.8 %collective-permute-start.9 = (bf16[512,512]{1,0:T(8,128)(2,1)S(1)}, bf16[512,512]{1,0:T(8,128)(2,1)S(1)}, u32[]{:S(2)}, u32[]{:S(2)}) collective-permute-start(bf16[512,512]{1,0:T(8,128)(2,1)S(1)} %shard_map.67), channel_id=1, source_target_pairs={{0,2},{1,3},{2,0},{3,1},{4,6},{5,7},{6,4},{7,5},{8,10},{9,11},{10,... | collective-permute-start | bytes 1572872 | tf_op jit(solution)/shard_map/ppermute | solution.py:268
  26.7 21.4 %collective-permute-start.8 = (bf16[512,512]{1,0:T(8,128)(2,1)S(1)}, bf16[512,512]{1,0:T(8,128)(2,1)S(1)}, u32[]{:S(2)}, u32[]{:S(2)}) collective-permute-start(bf16[512,512]{1,0:T(8,128)(2,1)S(1)} %shard_map.71), channel_id=1, source_target_pairs={{0,2},{1,3},{2,0},{3,1},{4,6},{5,7},{6,4},{7,5},{8,10},{9,11},{10,... | collective-permute-start | bytes 1572872 | tf_op jit(solution)/shard_map/ppermute | solution.py:268

commit v8 on v7

--- a/solution.py
+++ b/solution.py
@@ -17,7 +17,7 @@
 norm_eps = 1e-05
 
 TILE = 256
-CHUNKS = (2, 2, 2)
+CHUNKS = (2, 3, 1)
 
 PARAMS = pltpu.CompilerParams(vmem_limit_bytes=16 * 1024 * 1024)
 FIRST = pltpu.CompilerParams(vmem_limit_bytes=56 * 1024 * 1024)
@@ -122,40 +122,46 @@
     near_sin[...] = jnp.sin(near)
 
 
-def finish_kernel(first_tile, tensor_count, model_dim, live, *refs):
-    keep, received, far_cos, far_sin, near_cos, near_sin = refs[:6]
-    squares, arrived, out = refs[6 : 6 + tensor_count], refs[6 + tensor_count : -2], refs[-1]
-    values = keep[...].astype(jnp.float32) + received[...].astype(jnp.float32)
-    for part in arrived:
-        values += part[...].astype(jnp.float32)
+def finish_kernel(first, count, tensor_count, model_dim, *refs):
+    live, keep, received, far_cos, far_sin, near_cos, near_sin = refs[:7]
+    squares, arrived = refs[7 : 7 + tensor_count], refs[7 + tensor_count : -4]
+    out, staged, sems = refs[-3:]
     on_diagonal = lax.broadcasted_iota(jnp.int32, (LANES, LANES), 0) == lax.broadcasted_iota(
         jnp.int32, (LANES, LANES), 1
     )
-    tile = first_tile + pl.program_id(0)
-    columns = []
-    for part in range(TILE // LANES):
-        row = pl.ds(tile * (TILE // LANES) + part, 1)
-        totals = functools.reduce(jnp.add, [ref[row, :] for ref in squares])
-        columns.append(jnp.sum(jnp.where(on_diagonal, totals, 0.0), axis=1, keepdims=True))
-    scales = 1.0 / jnp.sqrt(jnp.concatenate(columns, axis=0) / model_dim + norm_eps)
-    row = tile * TILE + lax.broadcasted_iota(jnp.int32, (TILE, 1), 0)
-    alive = row < live[lax.axis_index("serve")] * BLOCK
     sign = jnp.where(lax.broadcasted_iota(jnp.int32, (1, HD), 1) < HD // 2, -1.0, 1.0)
-    cosines, sines = [], []
-    for part in range(TILE // BLOCK):
-        block = pl.ds(tile * (TILE // BLOCK) + part, 1)
-        block_cos = far_cos[block, :]
-        block_sin = far_sin[block, :]
-        cosines.append(block_cos * near_cos[...] - block_sin * near_sin[...])
-        sines.append((sign * block_sin) * near_cos[...] + (sign * block_cos) * near_sin[...])
-    cosine = jnp.concatenate(cosines, axis=0)
-    sine = jnp.concatenate(sines, axis=0)
-    for start in range(0, out.shape[1], 2 * HD):
-        key = values[:, start : start + HD] * scales
-        turned = key * cosine + pltpu.roll(key, HD // 2, 1) * sine
-        out[:, start : start + HD] = jnp.where(alive, turned, 0.0).astype(out.dtype)
-        value = values[:, start + HD : start + 2 * HD] * scales
-        out[:, start + HD : start + 2 * HD] = jnp.where(alive, value, 0.0).astype(out.dtype)
+    live_rows = live[lax.axis_index("serve")] * BLOCK
+    copies = []
+    for index in range(count):
+        start = (first + index) * TILE
+        rows, inside = pl.ds(start, TILE), pl.ds(index * TILE, TILE)
+        values = keep[rows, :].astype(jnp.float32) + received[rows, :].astype(jnp.float32)
+        for part in arrived:
+            values += part[inside, :].astype(jnp.float32)
+        columns = []
+        for row in range(start // LANES, (start + TILE) // LANES):
+            totals = functools.reduce(jnp.add, [ref[row : row + 1, :] for ref in squares])
+            columns.append(jnp.sum(jnp.where(on_diagonal, totals, 0.0), axis=1, keepdims=True))
+        scales = 1.0 / jnp.sqrt(jnp.concatenate(columns, axis=0) / model_dim + norm_eps)
+        alive = start + lax.broadcasted_iota(jnp.int32, (TILE, 1), 0) < live_rows
+        cosines, sines = [], []
+        for block in range(start // BLOCK, (start + TILE) // BLOCK):
+            block_cos = far_cos[block : block + 1, :]
+            block_sin = far_sin[block : block + 1, :]
+            cosines.append(block_cos * near_cos[...] - block_sin * near_sin[...])
+            sines.append((sign * block_sin) * near_cos[...] + (sign * block_cos) * near_sin[...])
+        cosine = jnp.concatenate(cosines, axis=0)
+        sine = jnp.concatenate(sines, axis=0)
+        for low in range(0, out.shape[1], 2 * HD):
+            key = values[:, low : low + HD] * scales
+            turned = key * cosine + pltpu.roll(key, HD // 2, 1) * sine
+            staged[inside, low : low + HD] = jnp.where(alive, turned, 0.0).astype(out.dtype)
+            value = values[:, low + HD : low + 2 * HD] * scales
+            staged[inside, low + HD : low + 2 * HD] = jnp.where(alive, value, 0.0).astype(out.dtype)
+        copies.append(pltpu.make_async_copy(staged.at[inside, :], out.at[rows, :], sems.at[index]))
+        copies[-1].start()
+    for copy in copies:
+        copy.wait()
 
 
 def shards(tokens, norm_gain, kv_weight, live_blocks, span_offset):
@@ -216,32 +222,23 @@
         return list(made)
 
     def finish(first, count, keep, received, table, squares, arrived, result):
-        operands = [keep, received] + table + squares + arrived
-        specs = (
-            [pl.BlockSpec((TILE, columns), lambda i, *_: (first + i, 0))] * 2
-            + [pl.BlockSpec((slot_rows // BLOCK, HD), lambda i, *_: (0, 0))] * 2
-            + [pl.BlockSpec((BLOCK, HD), lambda i, *_: (0, 0))] * 2
-            + [pl.BlockSpec((slot_rows // LANES, LANES), lambda i, *_: (0, 0))] * tensor_count
-            + [pl.BlockSpec((TILE, columns), lambda i, *_: (i, 0))] * len(arrived)
-        )
+        vmem = pl.BlockSpec(memory_space=pltpu.VMEM)
+        operands = [live_blocks, keep, received] + table + squares + arrived
+        aliases = {len(operands): 0}
         if result is None:
-            result = keep
-            aliases = {}
-        else:
-            aliases = {1 + len(operands): 0}
+            result, aliases = jnp.zeros((1,), jnp.bfloat16), {}
         return pl.pallas_call(
-            functools.partial(finish_kernel, first, tensor_count, model_dim),
-            grid_spec=pltpu.PrefetchScalarGridSpec(
-                num_scalar_prefetch=1,
-                grid=(count,),
-                in_specs=specs + [pl.BlockSpec(memory_space=pl.ANY)],
-                out_specs=pl.BlockSpec((TILE, columns), lambda i, *_: (first + i, 0)),
-            ),
+            functools.partial(finish_kernel, first, count, tensor_count, model_dim),
+            in_specs=[pl.BlockSpec(memory_space=pltpu.SMEM)]
+            + [vmem] * (len(operands) - 1)
+            + [pl.BlockSpec(memory_space=pl.ANY)],
             out_shape=jax.ShapeDtypeStruct((slot_rows, columns), jnp.bfloat16),
+            out_specs=pl.BlockSpec(memory_space=pltpu.HBM),
+            scratch_shapes=[pltpu.VMEM((count * TILE, columns), jnp.bfloat16), pltpu.SemaphoreType.DMA((count,))],
             input_output_aliases=aliases,
             compiler_params=PARAMS,
             cost_estimate=COST,
-        )(live_blocks, *operands, result)
+        )(*operands, result)
 
     others = range(1, chip_count)
     firsts = [sum(CHUNKS[:index]) for index in range(len(CHUNKS))]

time: 50.3 us -> 49.8 us (0.990)
    ppermute x3, waiting for transfers between devices: 2.37 us -> 1.82 us  [add_halves(): lax.ppermute(send, 'tensor', swap)]
  transfers between devices with their start and end apart: 10 -> 10, of which waited for: 6 -> 5; matrix products, arithmetic and copies ran while one was open for 0% -> 0% of each run, Pallas kernels for 23% -> 23%
where the time goes in v8:
time: 49.8 us; the launch traced here: 49.6 us
  waiting for transfers between devices  23.1 us (46%)
  Pallas kernels  17.3 us (35%)
  starting transfers between devices  9.03 us (18%)
    ppermute x3, waiting for transfers between devices, cross(): lax.ppermute(part, 'tensor', shift(step))  15.7 us
    pallas_call x4, Pallas kernels, product(): pl.pallas_call(functools.partial(product_kernel, step, chip_count, chunks...  10.4 us
    ppermute x3, starting transfers between devices, cross(): lax.ppermute(part, 'tensor', shift(step))  6.35 us
    pallas_call x3, Pallas kernels, finish(): pl.pallas_call(functools.partial(finish_kernel, first, count, tensor_coun...  5.87 us
    ppermute x3, waiting for transfers between devices, shards(): lax.ppermute(squares, 'tensor', [(i, (i + step) % tensor_count) for i in...  5.59 us
    ppermute x3, waiting for transfers between devices, add_halves(): lax.ppermute(send, 'tensor', swap)  1.82 us
    ppermute x3, starting transfers between devices, shards(): lax.ppermute(squares, 'tensor', [(i, (i + step) % tensor_count) for i in...  1.66 us
    ppermute x3, starting transfers between devices, add_halves(): lax.ppermute(send, 'tensor', swap)  1.01 us
  transfers between devices with their start and end apart: 10, of which 5 were waited for; matrix products, arithmetic and copies ran while one was open for 0% of the time, Pallas kernels for 23%

profile of v8, /device:TPU:0, one launch (start us, length us, event | category | flops | bytes accessed | tf_op | source)
XLA Modules:
  0.0 49.6 jit_solution(15861189821345473215)
XLA Ops:
  0.0 0.0 copy-start.3
  0.0 0.0 copy-start
  0.0 0.0 copy-start.1
  0.0 4.1 %shard_map.64 = (bf16[512,512]{1,0:T(8,128)(2,1)}, bf16[512,512]{1,0:T(8,128)(2,1)}) custom-call(bf16[1536,1024]{1,0:T(8,128)(2,1)} %tokens.7, bf16[1024]{0:T(1024)(128)(2,1)} %gain.4, bf16[1024,2048]{1,0:T(8,128)(2,1)} %weight.7), custom_call_target="tpu_custom_call" | custom-call | flops 1 | bytes 1 | tf_op jit(solution)/shard_map/pallas_call | solution.py:197
  4.1 0.0 copy-start.2
  4.1 0.5 %collective-permute-start = (bf16[512,512]{1,0:T(8,128)(2,1)}, bf16[512,512]{1,0:T(8,128)(2,1)S(1)}, u32[]{:S(2)}, u32[]{:S(2)}) collective-permute-start(bf16[512,512]{1,0:T(8,128)(2,1)} %get-tuple-element.43), channel_id=1, source_target_pairs={{0,1},{1,0},{2,3},{3,2},{4,5},{5,4},{6,7},{7,6},{8,9},{9,8},{10,11... | collective-permute-start | bytes 1572872 | tf_op jit(solution)/shard_map/ppermute | solution.py:260
  4.6 0.0 copy-done.3
  4.6 0.0 copy-done
  4.7 0.0 copy-done.1
  4.7 1.8 %shard_map.66 = (bf16[768,512]{1,0:T(8,128)(2,1)S(1)}, bf16[768,512]{1,0:T(8,128)(2,1)S(1)}) custom-call(bf16[1536,1024]{1,0:T(8,128)(2,1)S(1)} %copy-done.1, bf16[1024]{0:T(1024)(128)(2,1)S(1)} %copy-done.3, bf16[1024,2048]{1,0:T(8,128)(2,1)S(1)} %copy-done), custom_call_target="tpu_custom_call" | custom-call | flops 1 | bytes 1 | tf_op jit(solution)/shard_map/pallas_call | solution.py:197
  6.5 0.0 collective-permute-done.received
  6.5 0.0 copy-done.2
  6.5 0.1 shard_map.65
  6.6 0.3 collective-permute-start.2
  7.0 2.7 %collective-permute-start.1 = (bf16[512,512]{1,0:T(8,128)(2,1)S(1)}, bf16[512,512]{1,0:T(8,128)(2,1)S(1)}, u32[]{:S(2)}, u32[]{:S(2)}) collective-permute-start(bf16[512,512]{1,0:T(8,128)(2,1)S(1)} %shard_map.65), channel_id=1, source_target_pairs={{0,2},{1,3},{2,0},{3,1},{4,6},{5,7},{6,4},{7,5},{8,10},{9,11},{10,... | collective-permute-start | bytes 1572872 | tf_op jit(solution)/shard_map/ppermute | solution.py:265
  9.7 3.7 %shard_map.69 = (bf16[1536,512]{1,0:T(8,128)(2,1)S(1)}, bf16[1536,512]{1,0:T(8,128)(2,1)S(1)}, f32[12,128]{1,0:T(8,128)S(1)}) custom-call(bf16[1536,1024]{1,0:T(8,128)(2,1)S(1)} %copy-done.1, bf16[1024]{0:T(1024)(128)(2,1)S(1)} %copy-done.3, bf16[1024,2048]{1,0:T(8,128)(2,1)S(1)} %copy-done), custom_call_target="tpu_custom_call" | custom-call | flops 1 | bytes 1 | tf_op jit(solution)/shard_map/pallas_call | solution.py:197
  13.4 0.0 copy-start.5
  13.4 0.0 copy-start.6
  13.4 0.1 collective-permute-start.5
  13.5 1.6 %collective-permute-start.4 = (f32[12,128]{1,0:T(8,128)S(1)}, f32[12,128]{1,0:T(8,128)S(1)}, u32[]{:S(2)}, u32[]{:S(2)}) collective-permute-start(f32[12,128]{1,0:T(8,128)S(1)} %get-tuple-element.67.refs_7_), channel_id=1, source_target_pairs={{0,2},{1,3},{2,0},{3,1},{4,6},{5,7},{6,4},{7,5},{8,10},{9,11},{10,... | collective-permute-start | bytes 18440 | tf_op jit(solution)/shard_map/ppermute | solution.py:279
  15.1 0.0 collective-permute-start.3
  15.1 0.7 %shard_map.68 = (bf16[256,512]{1,0:T(8,128)(2,1)S(1)}, bf16[256,512]{1,0:T(8,128)(2,1)S(1)}) custom-call(bf16[1536,1024]{1,0:T(8,128)(2,1)S(1)} %copy-done.1, bf16[1024]{0:T(1024)(128)(2,1)S(1)} %copy-done.3, bf16[1024,2048]{1,0:T(8,128)(2,1)S(1)} %copy-done), custom_call_target="tpu_custom_call" | custom-call | flops 1 | bytes 1 | tf_op jit(solution)/shard_map/pallas_call | solution.py:197
  15.8 0.0 copy-done.5
  15.9 0.0 copy-done.6
  15.9 0.7 %shard_map.70 = (f32[24,128]{1,0:T(8,128)S(1)}, f32[24,128]{1,0:T(8,128)S(1)}, f32[64,128]{1,0:T(8,128)S(1)}, f32[64,128]{1,0:T(8,128)S(1)}) custom-call(s32[4]{0:T(128)S(1)} %copy-done.5, f32[1,128]{1,0:T(1,128)S(1)} %copy-done.6), custom_call_target="tpu_custom_call" | custom-call | flops 1 | bytes 1 | tf_op jit(solution)/shard_map/pallas_call | solution.py:214
  16.6 0.0 copy-start.4
  16.6 0.0 collective-permute-done.2.received
  16.6 0.2 shard_map.67
  16.8 4.8 %collective-permute-done.5.refs_10_ = f32[12,128]{1,0:T(8,128)S(1)} collective-permute-done((f32[12,128]{1,0:T(8,128)S(1)}, f32[12,128]{1,0:T(8,128)S(1)}, u32[]{:S(2)}, u32[]{:S(2)}) %collective-permute-start.5) | collective-permute-done | bytes 6176 | tf_op jit(solution)/shard_map/ppermute | solution.py:279
  21.6 0.8 %collective-permute-done.4.refs_9_ = f32[12,128]{1,0:T(8,128)S(1)} collective-permute-done((f32[12,128]{1,0:T(8,128)S(1)}, f32[12,128]{1,0:T(8,128)S(1)}, u32[]{:S(2)}, u32[]{:S(2)}) %collective-permute-start.4) | collective-permute-done | bytes 6176 | tf_op jit(solution)/shard_map/ppermute | solution.py:279
  22.4 0.0 collective-permute-done.3.refs_8_
  22.4 0.0 collective-permute-done.1.refs_11_
  22.4 0.0 collective-permute-start.6
  22.4 1.8 %collective-permute-start.9 = (bf16[768,512]{1,0:T(8,128)(2,1)S(1)}, bf16[768,512]{1,0:T(8,128)(2,1)S(1)}, u32[]{:S(2)}, u32[]{:S(2)}) collective-permute-start(bf16[768,512]{1,0:T(8,128)(2,1)S(1)} %shard_map.67), channel_id=1, source_target_pairs={{0,2},{1,3},{2,0},{3,1},{4,6},{5,7},{6,4},{7,5},{8,10},{9,11},{10,... | collective-permute-start | bytes 2359304 | tf_op jit(solution)/shard_map/ppermute | solution.py:265
  24.2 0.2 collective-permute-start.7
  24.4 1.8 %collective-permute-done.7.received = bf16[256,512]{1,0:T(8,128)(2,1)S(1)} collective-permute-done((bf16[256,512]{1,0:T(8,128)(2,1)S(1)}, bf16[256,512]{1,0:T(8,128)(2,1)S(1)}, u32[]{:S(2)}, u32[]{:S(2)}) %collective-permute-start.7) | collective-permute-done | bytes 262176 | tf_op jit(solution)/shard_map/ppermute | solution.py:260
  26.2 0.1 shard_map.71
  26.3 1.8 %collective-permute-start.8 = (bf16[256,512]{1,0:T(8,128)(2,1)S(1)}, bf16[256,512]{1,0:T(8,128)(2,1)S(1)}, u32[]{:S(2)}, u32[]{:S(2)}) collective-permute-start(bf16[256,512]{1,0:T(8,128)(2,1)S(1)} %shard_map.71), channel_id=1, source_target_pairs={{0,2},{1,3},{2,0},{3,1},{4,6},{5,7},{6,4},{7,5},{8,10},{9,11},{10,... | collective-permute-start | bytes 786440 | tf_op jit(solution)/shard_map/ppermute | solution.py:265
  28.1 0.0 collective-permute-done.6.refs_2_
  28.1 0.0 copy-done.4
  28.1 2.0 %shard_map.72.refs_12_ = bf16[1536,512]{1,0:T(8,128)(2,1)} custom-call(s32[4]{0:T(128)S(1)} %copy-done.4, bf16[1536,512]{1,0:T(8,128)(2,1)S(1)} %get-tuple-element.61.refs_1_, bf16[1536,512]{1,0:T(8,128)(2,1)S(1)} %collective-permute-done.6.refs_2_, f32[24,128]{1,0:T(8,128)S(1)} %get-tuple-element.63.refs_3_, f32[24,128]{1,0:T(8,128)S(1)} %get-tuple-element.64.refs_4_, ...), custom_call_target="tpu_custom_call" | custom-call | flops 1 | bytes 1 | tf_op jit(solution)/shard_map/pallas_call | solution.py:230
  30.0 12.8 %collective-permute-done.9.refs_11_ = bf16[768,512]{1,0:T(8,128)(2,1)S(1)} collective-permute-done((bf16[768,512]{1,0:T(8,128)(2,1)S(1)}, bf16[768,512]{1,0:T(8,128)(2,1)S(1)}, u32[]{:S(2)}, u32[]{:S(2)}) %collective-permute-start.9) | collective-permute-done | bytes 786464 | tf_op jit(solution)/shard_map/ppermute | solution.py:265
  42.8 2.3 %shard_map.73.refs_12_ = bf16[1536,512]{1,0:T(8,128)(2,1)} custom-call(s32[4]{0:T(128)S(1)} %copy-done.4, bf16[1536,512]{1,0:T(8,128)(2,1)S(1)} %get-tuple-element.61.refs_1_, bf16[1536,512]{1,0:T(8,128)(2,1)S(1)} %collective-permute-done.6.refs_2_, f32[24,128]{1,0:T(8,128)S(1)} %get-tuple-element.63.refs_3_, ...), custom_call_target="tpu_custom_call", output_to_operand_aliasing={{}: (12, {})} | custom-call | flops 1 | bytes 1 | tf_op jit(solution)/shard_map/pallas_call | solution.py:230
  45.1 2.9 %collective-permute-done.8.refs_11_ = bf16[256,512]{1,0:T(8,128)(2,1)S(1)} collective-permute-done((bf16[256,512]{1,0:T(8,128)(2,1)S(1)}, bf16[256,512]{1,0:T(8,128)(2,1)S(1)}, u32[]{:S(2)}, u32[]{:S(2)}) %collective-permute-start.8) | collective-permute-done | bytes 262176 | tf_op jit(solution)/shard_map/ppermute | solution.py:265
  48.0 1.6 %shard_map.74 = bf16[1536,512]{1,0:T(8,128)(2,1)} custom-call(s32[4]{0:T(128)S(1)} %copy-done.4, bf16[1536,512]{1,0:T(8,128)(2,1)S(1)} %get-tuple-element.61.refs_1_, bf16[1536,512]{1,0:T(8,128)(2,1)S(1)} %collective-permute-done.6.refs_2_, f32[24,128]{1,0:T(8,128)S(1)} %get-tuple-element.63.refs_3_, ...), custom_call_target="tpu_custom_call", output_to_operand_aliasing={{}: (12, {})} | custom-call | flops 1 | bytes 1 | tf_op jit(solution)/shard_map/pallas_call | solution.py:230
Async XLA Ops:
  0.0 4.6 %copy-start.3 = (bf16[1024]{0:T(1024)(128)(2,1)S(1)}, bf16[1024]{0:T(1024)(128)(2,1)}, u32[]{:S(2)}) copy-start(bf16[1024]{0:T(1024)(128)(2,1)} %gain.4) | copy-start | bytes 6148
  0.0 4.6 %copy-start = (bf16[1024,2048]{1,0:T(8,128)(2,1)S(1)}, bf16[1024,2048]{1,0:T(8,128)(2,1)}, u32[]{:S(2)}) copy-start(bf16[1024,2048]{1,0:T(8,128)(2,1)} %weight.7) | copy-start | bytes 12582916
  0.0 4.6 %copy-start.1 = (bf16[1536,1024]{1,0:T(8,128)(2,1)S(1)}, bf16[1536,1024]{1,0:T(8,128)(2,1)}, u32[]{:S(2)}) copy-start(bf16[1536,1024]{1,0:T(8,128)(2,1)} %tokens.7) | copy-start | bytes 9437188
  4.1 2.4 %copy-start.2 = (bf16[512,512]{1,0:T(8,128)(2,1)S(1)}, bf16[512,512]{1,0:T(8,128)(2,1)}, u32[]{:S(2)}) copy-start(bf16[512,512]{1,0:T(8,128)(2,1)} %get-tuple-element.42.keep) | copy-start | bytes 1572868
  4.1 2.4 %collective-permute-start = (bf16[512,512]{1,0:T(8,128)(2,1)}, bf16[512,512]{1,0:T(8,128)(2,1)S(1)}, u32[]{:S(2)}, u32[]{:S(2)}) collective-permute-start(bf16[512,512]{1,0:T(8,128)(2,1)} %get-tuple-element.43), channel_id=1, source_target_pairs={{0,1},{1,0},{2,3},{3,2},{4,5},{5,4},{6,7},{7,6},{8,9},{9,8},{10,11... | collective-permute-start | bytes 1572872 | tf_op jit(solution)/shard_map/ppermute | solution.py:260
  6.6 10.0 %collective-permute-start.2 = (bf16[768,512]{1,0:T(8,128)(2,1)S(1)}, bf16[768,512]{1,0:T(8,128)(2,1)S(1)}, u32[]{:S(2)}, u32[]{:S(2)}) collective-permute-start(bf16[768,512]{1,0:T(8,128)(2,1)S(1)} %get-tuple-element.49), channel_id=1, source_target_pairs={{0,1},{1,0},{2,3},{3,2},{4,5},{5,4},{6,7},{7,6},{8,9},{9,8},{10,11... | collective-permute-start | bytes 2359304 | tf_op jit(solution)/shard_map/ppermute | solution.py:260
  7.0 15.4 %collective-permute-start.1 = (bf16[512,512]{1,0:T(8,128)(2,1)S(1)}, bf16[512,512]{1,0:T(8,128)(2,1)S(1)}, u32[]{:S(2)}, u32[]{:S(2)}) collective-permute-start(bf16[512,512]{1,0:T(8,128)(2,1)S(1)} %shard_map.65), channel_id=1, source_target_pairs={{0,2},{1,3},{2,0},{3,1},{4,6},{5,7},{6,4},{7,5},{8,10},{9,11},{10,... | collective-permute-start | bytes 1572872 | tf_op jit(solution)/shard_map/ppermute | solution.py:265
  13.4 2.4 %copy-start.5 = (s32[4]{0:T(128)S(1)}, s32[4]{0:T(128)}, u32[]{:S(2)}) copy-start(s32[4]{0:T(128)} %span) | copy-start | bytes 52
  13.4 2.4 %copy-start.6 = (f32[1,128]{1,0:T(1,128)S(1)}, f32[1,128]{1,0:T(1,128)}, u32[]{:S(2)}) copy-start(f32[1,128]{1,0:T(1,128)} %constant.4.clone.frequencies) | copy-start | bytes 1540
  13.4 8.1 %collective-permute-start.5 = (f32[12,128]{1,0:T(8,128)S(1)}, f32[12,128]{1,0:T(8,128)S(1)}, u32[]{:S(2)}, u32[]{:S(2)}) collective-permute-start(f32[12,128]{1,0:T(8,128)S(1)} %get-tuple-element.67.refs_7_), channel_id=1, source_target_pairs={{0,3},{1,0},{2,1},{3,2},{4,7},{5,4},{6,5},{7,6},{8,11},{9,8},{10,9... | collective-permute-start | bytes 18440 | tf_op jit(solution)/shard_map/ppermute | solution.py:279
  13.5 8.9 %collective-permute-start.4 = (f32[12,128]{1,0:T(8,128)S(1)}, f32[12,128]{1,0:T(8,128)S(1)}, u32[]{:S(2)}, u32[]{:S(2)}) collective-permute-start(f32[12,128]{1,0:T(8,128)S(1)} %get-tuple-element.67.refs_7_), channel_id=1, source_target_pairs={{0,2},{1,3},{2,0},{3,1},{4,6},{5,7},{6,4},{7,5},{8,10},{9,11},{10,... | collective-permute-start | bytes 18440 | tf_op jit(solution)/shard_map/ppermute | solution.py:279
  15.1 7.3 %collective-permute-start.3 = (f32[12,128]{1,0:T(8,128)S(1)}, f32[12,128]{1,0:T(8,128)S(1)}, u32[]{:S(2)}, u32[]{:S(2)}) collective-permute-start(f32[12,128]{1,0:T(8,128)S(1)} %get-tuple-element.67.refs_7_), channel_id=1, source_target_pairs={{0,1},{1,2},{2,3},{3,0},{4,5},{5,6},{6,7},{7,4},{8,9},{9,10},{10,1... | collective-permute-start | bytes 18440 | tf_op jit(solution)/shard_map/ppermute | solution.py:279
  16.6 11.5 %copy-start.4 = (s32[4]{0:T(128)S(1)}, s32[4]{0:T(128)}, u32[]{:S(2)}) copy-start(s32[4]{0:T(128)} %refs_0_.5) | copy-start | bytes 52
  22.4 5.7 %collective-permute-start.6 = (bf16[1536,512]{1,0:T(8,128)(2,1)S(1)}, bf16[1536,512]{1,0:T(8,128)(2,1)S(1)}, u32[]{:S(2)}, u32[]{:S(2)}) collective-permute-start(bf16[1536,512]{1,0:T(8,128)(2,1)S(1)} %get-tuple-element.62), channel_id=1, source_target_pairs={{0,1},{1,0},{2,3},{3,2},{4,5},{5,4},{6,7},{7,6},{8,9},{9,8},{10,11... | collective-permute-start | bytes 4718600 | tf_op jit(solution)/shard_map/ppermute | solution.py:288
  22.4 20.4 %collective-permute-start.9 = (bf16[768,512]{1,0:T(8,128)(2,1)S(1)}, bf16[768,512]{1,0:T(8,128)(2,1)S(1)}, u32[]{:S(2)}, u32[]{:S(2)}) collective-permute-start(bf16[768,512]{1,0:T(8,128)(2,1)S(1)} %shard_map.67), channel_id=1, source_target_pairs={{0,2},{1,3},{2,0},{3,1},{4,6},{5,7},{6,4},{7,5},{8,10},{9,11},{10,... | collective-permute-start | bytes 2359304 | tf_op jit(solution)/shard_map/ppermute | solution.py:265
  24.2 2.0 %collective-permute-start.7 = (bf16[256,512]{1,0:T(8,128)(2,1)S(1)}, bf16[256,512]{1,0:T(8,128)(2,1)S(1)}, u32[]{:S(2)}, u32[]{:S(2)}) collective-permute-start(bf16[256,512]{1,0:T(8,128)(2,1)S(1)} %get-tuple-element.72), channel_id=1, source_target_pairs={{0,1},{1,0},{2,3},{3,2},{4,5},{5,4},{6,7},{7,6},{8,9},{9,8},{10,11... | collective-permute-start | bytes 786440 | tf_op jit(solution)/shard_map/ppermute | solution.py:260
  26.3 21.7 %collective-permute-start.8 = (bf16[256,512]{1,0:T(8,128)(2,1)S(1)}, bf16[256,512]{1,0:T(8,128)(2,1)S(1)}, u32[]{:S(2)}, u32[]{:S(2)}) collective-permute-start(bf16[256,512]{1,0:T(8,128)(2,1)S(1)} %shard_map.71), channel_id=1, source_target_pairs={{0,2},{1,3},{2,0},{3,1},{4,6},{5,7},{6,4},{7,5},{8,10},{9,11},{10,... | collective-permute-start | bytes 786440 | tf_op jit(solution)/shard_map/ppermute | solution.py:265

commit v9 on v8

v9 whole, which is shorter than its diff:
```python
import functools

import jax
import jax.numpy as jnp
import numpy as np
from jax import lax
from jax.experimental import pallas as pl
from jax.experimental.pallas import tpu as pltpu
from jax.sharding import PartitionSpec as P

HD = 128
PAGE = 256
BLOCK = 64
LANES = 128

rope_base = 500000.0
norm_eps = 1e-05

TILE = 256
CHUNKS = (2, 3, 1)

PARAMS = pltpu.CompilerParams(vmem_limit_bytes=16 * 1024 * 1024)
FIRST = pltpu.CompilerParams(vmem_limit_bytes=56 * 1024 * 1024)
COST = pl.CostEstimate(flops=1, bytes_accessed=1, transcendentals=0)


def square_sums(rows):
    total = jnp.zeros((rows.shape[0], LANES), jnp.float32)
    for part in range(rows.shape[1] // LANES):
        wide = rows[:, part * LANES : (part + 1) * LANES].astype(jnp.float32)
        total += wide * wide
    return total


def product_kernel(step, chip_count, first, count, staged, with_squares, tokens, gain, weight, *refs):
    keep, send = refs[:2]
    squares = refs[2] if with_squares else None
    depth, width = tokens.shape[1], 2 * keep.shape[1]
    me = lax.axis_index("tensor")
    core = lax.rem(me, 2)
    chip = lax.rem(lax.div(me, 2) + step, chip_count)
    place = pl.ds(pl.multiple_of(chip * width, width), width)

    def split(product, inside):
        left = product[:, : width // 2].astype(jnp.bfloat16)
        right = product[:, width // 2 :].astype(jnp.bfloat16)
        keep[inside, :] = jnp.where(core == 0, left, right)
        send[inside, :] = jnp.where(core == 0, right, left)

    if staged:
        rows_buf, weight_buf, gain_buf, total, weight_sems, row_sem, gain_sem = refs[2:]
        cuts = weight_sems.shape[0]
        cut = depth // cuts
        gain_copy = pltpu.make_async_copy(gain, gain_buf, gain_sem)
        row_copy = pltpu.make_async_copy(tokens.at[pl.ds(first * TILE, count * TILE), :], rows_buf, row_sem)
        weight_copies = [
            pltpu.make_async_copy(
                weight.at[pl.ds(index * cut, cut), place],
                weight_buf.at[pl.ds(index * cut, cut), :],
                weight_sems.at[index],
            )
            for index in range(cuts)
        ]
        for copy in [gain_copy, row_copy] + weight_copies:
            copy.start()
        gain_copy.wait()
        row_copy.wait()
        gains = gain_buf[...].reshape(1, depth)

        @pl.loop(0, count * TILE // BLOCK)
        def _(block):
            inside = pl.ds(pl.multiple_of(block * BLOCK, BLOCK), BLOCK)
            rows_buf[inside, :] = rows_buf[inside, :] * gains

        for index, copy in enumerate(weight_copies):
            copy.wait()
            span = slice(index * cut, (index + 1) * cut)

            @pl.loop(0, count)
            def _(tile):
                inside = pl.ds(pl.multiple_of(tile * TILE, TILE), TILE)
                part = jnp.dot(rows_buf[inside, span], weight_buf[span, :], preferred_element_type=jnp.float32)
                if index:
                    part += total[inside, :]
                if index + 1 < cuts:
                    total[inside, :] = part
                else:
                    split(part, inside)

        return

    gains = gain[...].reshape(1, depth)

    @pl.loop(0, count)
    def _(tile):
        source = pl.multiple_of((first + tile) * TILE, TILE)
        rows = tokens[pl.ds(source, TILE), :]
        split(
            jnp.dot(rows * gains, weight[:, place], preferred_element_type=jnp.float32),
            pl.ds(pl.multiple_of(tile * TILE, TILE), TILE),
        )
        if with_squares:
            for part in range(TILE // LANES):
                sums = square_sums(rows[part * LANES : (part + 1) * LANES])
                row = (first + tile) * (TILE // LANES) + part
                squares[pl.ds(row, 1), :] = jnp.sum(jnp.transpose(sums), axis=0, keepdims=True)


def add_kernel(keep, received, out):
    out[...] = (keep[...].astype(jnp.float32) + received[...].astype(jnp.float32)).astype(out.dtype)


def table_kernel(live, span, frequencies, limit, far_cos, far_sin, near_cos, near_sin):
    limit[...] = jnp.full(limit.shape, live[lax.axis_index("serve")] * BLOCK, jnp.int32)
    blocks = far_cos.shape[0]
    start = span[lax.axis_index("serve")] * PAGE
    first = start + BLOCK * lax.broadcasted_iota(jnp.int32, (blocks, HD), 0)
    far = first.astype(jnp.float32) * frequencies[...]
    near = lax.broadcasted_iota(jnp.int32, (BLOCK, HD), 0).astype(jnp.float32) * frequencies[...]
    far_cos[...] = jnp.cos(far)
    far_sin[...] = jnp.sin(far)
    near_cos[...] = jnp.cos(near)
    near_sin[...] = jnp.sin(near)


def finish_kernel(first, count, tensor_count, model_dim, *refs):
    keep, received, limit, far_cos, far_sin, near_cos, near_sin = refs[:7]
    squares, arrived = refs[7 : 7 + tensor_count], refs[7 + tensor_count : -4]
    out, staged, sems = refs[-3:]
    blocks = count * TILE // BLOCK
    first_block = first * TILE // BLOCK
    shape = (BLOCK, LANES)
    sign = jnp.where(lax.broadcasted_iota(jnp.int32, (1, HD), 1) < HD // 2, -1.0, 1.0)

    def copy_of(index):
        inside = pl.ds(pl.multiple_of(index * BLOCK, BLOCK), BLOCK)
        rows = pl.ds(pl.multiple_of((first_block + index) * BLOCK, BLOCK), BLOCK)
        return pltpu.make_async_copy(staged.at[inside, :], out.at[rows, :], sems.at[index])

    @pl.loop(0, blocks)
    def _(index):
        block = first_block + index
        start = pl.multiple_of(block * BLOCK, BLOCK)
        rows, inside = pl.ds(start, BLOCK), pl.ds(pl.multiple_of(index * BLOCK, BLOCK), BLOCK)
        values = keep[rows, :].astype(jnp.float32) + received[rows, :].astype(jnp.float32)
        for part in arrived:
            values += part[inside, :].astype(jnp.float32)
        line = lax.rem(start, LANES) + lax.broadcasted_iota(jnp.int32, shape, 0)
        totals = functools.reduce(jnp.add, [ref[pl.ds(lax.div(start, LANES), 1), :] for ref in squares])
        picked = jnp.where(line == lax.broadcasted_iota(jnp.int32, shape, 1), totals, 0.0)
        scales = 1.0 / jnp.sqrt(jnp.sum(picked, axis=1, keepdims=True) / model_dim + norm_eps)
        alive = start + lax.broadcasted_iota(jnp.int32, shape, 0) < limit[0:1, :]
        block_cos = far_cos[pl.ds(block, 1), :]
        block_sin = far_sin[pl.ds(block, 1), :]
        cosine = block_cos * near_cos[...] - block_sin * near_sin[...]
        sine = (sign * block_sin) * near_cos[...] + (sign * block_cos) * near_sin[...]
        for low in range(0, out.shape[1], 2 * HD):
            key = values[:, low : low + HD] * scales
            turned = key * cosine + pltpu.roll(key, HD // 2, 1) * sine
            staged[inside, low : low + HD] = jnp.where(alive, turned, 0.0).astype(out.dtype)
            value = values[:, low + HD : low + 2 * HD] * scales
            staged[inside, low + HD : low + 2 * HD] = jnp.where(alive, value, 0.0).astype(out.dtype)
        copy_of(index).start()

    @pl.loop(0, blocks)
    def _(index):
        copy_of(index).wait()


def shards(tokens, norm_gain, kv_weight, live_blocks, span_offset):
    tensor_count = lax.axis_size("tensor")
    chip_count = tensor_count // 2
    me = lax.axis_index("tensor")
    slot_rows, depth = tokens.shape
    columns = kv_weight.shape[1] // tensor_count
    tiles = slot_rows // TILE
    model_dim = depth * tensor_count

    swap = [(i, i ^ 1) for i in range(tensor_count)]

    def shift(step):
        return [(i, (i + 2 * step) % tensor_count) for i in range(tensor_count)]

    def product(gain, step, first, count, staged=False, with_squares=False):
        vmem = pl.BlockSpec(memory_space=pltpu.VMEM)
        out_shape = [jax.ShapeDtypeStruct((count * TILE, columns), jnp.bfloat16)] * 2
        if with_squares:
            out_shape.append(jax.ShapeDtypeStruct((slot_rows // LANES, LANES), jnp.float32))
        scratch = [
            pltpu.VMEM((count * TILE, depth), jnp.bfloat16),
            pltpu.VMEM((depth, 2 * columns), jnp.bfloat16),
            pltpu.VMEM((depth,), jnp.bfloat16),
            pltpu.VMEM((count * TILE, 2 * columns), jnp.float32),
            pltpu.SemaphoreType.DMA((4,)),
            pltpu.SemaphoreType.DMA,
            pltpu.SemaphoreType.DMA,
        ]
        return pl.pallas_call(
            functools.partial(product_kernel, step, chip_count, first, count, staged, with_squares),
            in_specs=[pl.BlockSpec(memory_space=pltpu.HBM) if staged else vmem] * 3,
            out_shape=out_shape,
            out_specs=[vmem] * len(out_shape),
            scratch_shapes=scratch if staged else [],
            compiler_params=FIRST if staged else PARAMS,
            cost_estimate=COST,
        )(tokens, gain, kv_weight)

    def tables(span_offset):
        frequencies = rope_base ** (-(np.arange(HD // 2, dtype=np.float32) * 2.0) / HD)
        frequencies = np.concatenate([frequencies, frequencies])[None, :].astype(np.float32)
        shapes = [(slot_rows // BLOCK, HD)] * 2 + [(BLOCK, HD)] * 2
        made = pl.pallas_call(
            table_kernel,
            in_specs=[pl.BlockSpec(memory_space=pltpu.SMEM)] * 2 + [pl.BlockSpec(memory_space=pltpu.VMEM)],
            out_shape=[jax.ShapeDtypeStruct((8, LANES), jnp.int32)]
            + [jax.ShapeDtypeStruct(shape, jnp.float32) for shape in shapes],
            out_specs=[pl.BlockSpec(memory_space=pltpu.VMEM)] * 5,
            compiler_params=PARAMS,
            cost_estimate=COST,
        )(live_blocks, span_offset, jnp.asarray(frequencies))
        return list(made)

    def finish(first, count, keep, received, table, squares, arrived, result):
        vmem = pl.BlockSpec(memory_space=pltpu.VMEM)
        operands = [keep, received] + table + squares + arrived
        aliases = {len(operands): 0}
        if result is None:
            result, aliases = jnp.zeros((1,), jnp.bfloat16), {}
        return pl.pallas_call(
            functools.partial(finish_kernel, first, count, tensor_count, model_dim),
            in_specs=[vmem] * len(operands) + [pl.BlockSpec(memory_space=pl.ANY)],
            out_shape=jax.ShapeDtypeStruct((slot_rows, columns), jnp.bfloat16),
            out_specs=pl.BlockSpec(memory_space=pltpu.HBM),
            scratch_shapes=[pltpu.VMEM((count * TILE, columns), jnp.bfloat16), pltpu.SemaphoreType.DMA((count * TILE // BLOCK,))],
            input_output_aliases=aliases,
            compiler_params=PARAMS,
            cost_estimate=COST,
        )(*operands, result)

    others = range(1, chip_count)
    firsts = [sum(CHUNKS[:index]) for index in range(len(CHUNKS))]
    chunk_count = len(CHUNKS)

    def start_chunk(gain, index, staged=False):
        made = []
        for step in others:
            made.append(product(gain, step, firsts[index], CHUNKS[index], staged))
        return made

    def add_halves(made):
        return [
            pl.pallas_call(
                add_kernel,
                out_shape=jax.ShapeDtypeStruct(keep.shape, keep.dtype),
                compiler_params=PARAMS,
                cost_estimate=COST,
            )(keep, lax.ppermute(send, "tensor", swap))
            for keep, send in made
        ]

    def cross(sums):
        return [lax.ppermute(part, "tensor", shift(step)) for step, part in zip(others, sums)]

    hold = lax.optimization_barrier
    made = start_chunk(norm_gain, 0, staged=True)
    made, gain = hold((made, norm_gain))
    sums = add_halves(made)
    made = start_chunk(gain, 1)
    sums, made, gain, span_offset = hold((sums, made, gain, span_offset))

    arrived = cross(sums)
    sums = add_halves(made)
    waiting = [start_chunk(gain, index) for index in range(2, chunk_count)]
    keep, send, squares = product(gain, 0, 0, tiles, with_squares=True)
    squares = [squares] + [
        lax.ppermute(squares, "tensor", [(i, (i + step) % tensor_count) for i in range(tensor_count)])
        for step in range(1, tensor_count)
    ]
    table = tables(span_offset)
    arrived, sums, waiting, keep, send, squares, table = hold(
        (arrived, sums, waiting, keep, send, squares, table)
    )

    arrivals = [arrived, cross(sums)] + [cross(add_halves(made)) for made in waiting]
    received = lax.ppermute(send, "tensor", swap)
    result = None
    for index in range(chunk_count):
        result = finish(
            firsts[index], CHUNKS[index], keep, received, table, squares, arrivals[index], result
        )
    return result


def solution(mesh):
    in_specs = (
        P(("groups", "serve"), "tensor"),
        P("tensor"),
        P("tensor", None),
        P("groups"),
        P("groups"),
    )
    out_specs = P(("groups", "serve"), "tensor")
    return jax.shard_map(shards, mesh=mesh, in_specs=in_specs, out_specs=out_specs, check_vma=False)
```

time: 49.8 us -> 50.6 us (1.016)
  Pallas kernels: 17.3 us -> 20 us
  waiting for transfers between devices: 23.1 us -> 21.4 us
    pallas_call x4, Pallas kernels: 10.4 us -> 12.1 us  [product(): pl.pallas_call(functools.partial(product_kernel, step, chip_count, first,...]
    ppermute x3, waiting for transfers between devices: 15.7 us -> 14.6 us  [cross(): lax.ppermute(part, 'tensor', shift(step))]
    pallas_call x3, Pallas kernels: 5.87 us -> 6.79 us  [finish(): pl.pallas_call(functools.partial(finish_kernel, first, count, tensor_coun...]
    ppermute x3, waiting for transfers between devices: 5.59 us -> 5.01 us  [shards(): lax.ppermute(squares, 'tensor', [(i, (i + step) % tensor_count) for i in...]
  transfers between devices with their start and end apart: 10 -> 10, of which waited for: 5 -> 5; matrix products, arithmetic and copies ran while one was open for 0% -> 0% of each run, Pallas kernels for 23% -> 27%
where the time goes in v9:
time: 50.6 us; the launch traced here: 50.5 us
  waiting for transfers between devices  21.4 us (42%)
  Pallas kernels  20 us (40%)
  starting transfers between devices  8.84 us (17%)
    ppermute x3, waiting for transfers between devices, cross(): lax.ppermute(part, 'tensor', shift(step))  14.6 us
    pallas_call x4, Pallas kernels, product(): pl.pallas_call(functools.partial(product_kernel, step, chip_count, first,...  12.1 us
    pallas_call x3, Pallas kernels, finish(): pl.pallas_call(functools.partial(finish_kernel, first, count, tensor_coun...  6.79 us
    ppermute x3, starting transfers between devices, cross(): lax.ppermute(part, 'tensor', shift(step))  6.55 us
    ppermute x3, waiting for transfers between devices, shards(): lax.ppermute(squares, 'tensor', [(i, (i + step) % tensor_count) for i in...  5.01 us
    ppermute x3, waiting for transfers between devices, add_halves(): lax.ppermute(send, 'tensor', swap)  1.82 us
    ppermute x3, starting transfers between devices, shards(): lax.ppermute(squares, 'tensor', [(i, (i + step) % tensor_count) for i in...  1.47 us
  transfers between devices with their start and end apart: 10, of which 5 were waited for; matrix products, arithmetic and copies ran while one was open for 0% of the time, Pallas kernels for 27%

profile of v9, /device:TPU:0, one launch (start us, length us, event | category | flops | bytes accessed | tf_op | source)
XLA Modules:
  0.0 50.5 jit_solution(13610596433443318824)
XLA Ops:
  0.0 0.0 copy-start.3
  0.0 0.0 copy-start
  0.0 0.0 copy-start.1
  0.0 5.0 %shard_map.64 = (bf16[512,512]{1,0:T(8,128)(2,1)}, bf16[512,512]{1,0:T(8,128)(2,1)}) custom-call(bf16[1536,1024]{1,0:T(8,128)(2,1)} %tokens.7, bf16[1024]{0:T(1024)(128)(2,1)} %gain.4, bf16[1024,2048]{1,0:T(8,128)(2,1)} %weight.7), custom_call_target="tpu_custom_call" | custom-call | flops 1 | bytes 1 | tf_op jit(solution)/shard_map/pallas_call | solution.py:198
  5.0 0.0 copy-start.2
  5.0 0.5 %collective-permute-start = (bf16[512,512]{1,0:T(8,128)(2,1)}, bf16[512,512]{1,0:T(8,128)(2,1)S(1)}, u32[]{:S(2)}, u32[]{:S(2)}) collective-permute-start(bf16[512,512]{1,0:T(8,128)(2,1)} %get-tuple-element.45), channel_id=1, source_target_pairs={{0,1},{1,0},{2,3},{3,2},{4,5},{5,4},{6,7},{7,6},{8,9},{9,8},{10,11... | collective-permute-start | bytes 1572872 | tf_op jit(solution)/shard_map/ppermute | solution.py:257
  5.5 0.0 copy-done.3
  5.5 0.0 copy-done
  5.5 0.0 copy-done.1
  5.5 2.2 %shard_map.66 = (bf16[768,512]{1,0:T(8,128)(2,1)S(1)}, bf16[768,512]{1,0:T(8,128)(2,1)S(1)}) custom-call(bf16[1536,1024]{1,0:T(8,128)(2,1)S(1)} %copy-done.1, bf16[1024]{0:T(1024)(128)(2,1)S(1)} %copy-done.3, bf16[1024,2048]{1,0:T(8,128)(2,1)S(1)} %copy-done), custom_call_target="tpu_custom_call" | custom-call | flops 1 | bytes 1 | tf_op jit(solution)/shard_map/pallas_call | solution.py:198
  7.7 0.0 collective-permute-done.received
  7.7 0.0 copy-done.2
  7.7 0.1 shard_map.65
  7.9 0.1 collective-permute-start.2
  8.0 2.9 %collective-permute-start.1 = (bf16[512,512]{1,0:T(8,128)(2,1)S(1)}, bf16[512,512]{1,0:T(8,128)(2,1)S(1)}, u32[]{:S(2)}, u32[]{:S(2)}) collective-permute-start(bf16[512,512]{1,0:T(8,128)(2,1)S(1)} %shard_map.65), channel_id=1, source_target_pairs={{0,2},{1,3},{2,0},{3,1},{4,6},{5,7},{6,4},{7,5},{8,10},{9,11},{10,... | collective-permute-start | bytes 1572872 | tf_op jit(solution)/shard_map/ppermute | solution.py:262
  10.9 4.3 %shard_map.69 = (bf16[1536,512]{1,0:T(8,128)(2,1)S(1)}, bf16[1536,512]{1,0:T(8,128)(2,1)S(1)}, f32[12,128]{1,0:T(8,128)S(1)}) custom-call(bf16[1536,1024]{1,0:T(8,128)(2,1)S(1)} %copy-done.1, bf16[1024]{0:T(1024)(128)(2,1)S(1)} %copy-done.3, bf16[1024,2048]{1,0:T(8,128)(2,1)S(1)} %copy-done), custom_call_target="tpu_custom_call" | custom-call | flops 1 | bytes 1 | tf_op jit(solution)/shard_map/pallas_call | solution.py:198
  15.2 0.0 copy-start.4
  15.2 0.0 copy-start.5
  15.2 0.0 copy-start.6
  15.3 0.1 collective-permute-start.5
  15.3 1.4 %collective-permute-start.4 = (f32[12,128]{1,0:T(8,128)S(1)}, f32[12,128]{1,0:T(8,128)S(1)}, u32[]{:S(2)}, u32[]{:S(2)}) collective-permute-start(f32[12,128]{1,0:T(8,128)S(1)} %get-tuple-element.71.refs_7_), channel_id=1, source_target_pairs={{0,2},{1,3},{2,0},{3,1},{4,6},{5,7},{6,4},{7,5},{8,10},{9,11},{10,... | collective-permute-start | bytes 18440 | tf_op jit(solution)/shard_map/ppermute | solution.py:276
  16.7 0.0 collective-permute-start.3
  16.7 0.7 %shard_map.68 = (bf16[256,512]{1,0:T(8,128)(2,1)S(1)}, bf16[256,512]{1,0:T(8,128)(2,1)S(1)}) custom-call(bf16[1536,1024]{1,0:T(8,128)(2,1)S(1)} %copy-done.1, bf16[1024]{0:T(1024)(128)(2,1)S(1)} %copy-done.3, bf16[1024,2048]{1,0:T(8,128)(2,1)S(1)} %copy-done), custom_call_target="tpu_custom_call" | custom-call | flops 1 | bytes 1 | tf_op jit(solution)/shard_map/pallas_call | solution.py:198
  17.5 0.0 copy-done.4
  17.5 0.0 copy-done.5
  17.5 0.0 copy-done.6
  17.5 0.7 %shard_map.70 = (s32[8,128]{1,0:T(8,128)S(1)}, f32[24,128]{1,0:T(8,128)S(1)}, f32[24,128]{1,0:T(8,128)S(1)}, f32[64,128]{1,0:T(8,128)S(1)}, f32[64,128]{1,0:T(8,128)S(1)}) custom-call(s32[4]{0:T(128)S(1)} %copy-done.4, s32[4]{0:T(128)S(1)} %copy-done.5, f32[1,128]{1,0:T(1,128)S(1)} %copy-done.6), custom_call_target="tpu_custom_call" | custom-call | flops 1 | bytes 1 | tf_op jit(solution)/shard_map/pallas_call | solution.py:212
  18.2 0.0 collective-permute-done.2.received
  18.2 0.2 shard_map.67
  18.4 4.2 %collective-permute-done.5.refs_10_ = f32[12,128]{1,0:T(8,128)S(1)} collective-permute-done((f32[12,128]{1,0:T(8,128)S(1)}, f32[12,128]{1,0:T(8,128)S(1)}, u32[]{:S(2)}, u32[]{:S(2)}) %collective-permute-start.5) | collective-permute-done | bytes 6176 | tf_op jit(solution)/shard_map/ppermute | solution.py:276
  22.6 0.8 %collective-permute-done.4.refs_9_ = f32[12,128]{1,0:T(8,128)S(1)} collective-permute-done((f32[12,128]{1,0:T(8,128)S(1)}, f32[12,128]{1,0:T(8,128)S(1)}, u32[]{:S(2)}, u32[]{:S(2)}) %collective-permute-start.4) | collective-permute-done | bytes 6176 | tf_op jit(solution)/shard_map/ppermute | solution.py:276
  23.4 0.0 collective-permute-done.3.refs_8_
  23.4 0.0 collective-permute-done.1.refs_11_
  23.4 0.0 collective-permute-start.6
  23.5 1.8 %collective-permute-start.9 = (bf16[768,512]{1,0:T(8,128)(2,1)S(1)}, bf16[768,512]{1,0:T(8,128)(2,1)S(1)}, u32[]{:S(2)}, u32[]{:S(2)}) collective-permute-start(bf16[768,512]{1,0:T(8,128)(2,1)S(1)} %shard_map.67), channel_id=1, source_target_pairs={{0,2},{1,3},{2,0},{3,1},{4,6},{5,7},{6,4},{7,5},{8,10},{9,11},{10,... | collective-permute-start | bytes 2359304 | tf_op jit(solution)/shard_map/ppermute | solution.py:262
  25.3 0.2 collective-permute-start.7
  25.4 1.8 %collective-permute-done.7.received = bf16[256,512]{1,0:T(8,128)(2,1)S(1)} collective-permute-done((bf16[256,512]{1,0:T(8,128)(2,1)S(1)}, bf16[256,512]{1,0:T(8,128)(2,1)S(1)}, u32[]{:S(2)}, u32[]{:S(2)}) %collective-permute-start.7) | collective-permute-done | bytes 262176 | tf_op jit(solution)/shard_map/ppermute | solution.py:257
  27.2 0.1 shard_map.71
  27.3 1.8 %collective-permute-start.8 = (bf16[256,512]{1,0:T(8,128)(2,1)S(1)}, bf16[256,512]{1,0:T(8,128)(2,1)S(1)}, u32[]{:S(2)}, u32[]{:S(2)}) collective-permute-start(bf16[256,512]{1,0:T(8,128)(2,1)S(1)} %shard_map.71), channel_id=1, source_target_pairs={{0,2},{1,3},{2,0},{3,1},{4,6},{5,7},{6,4},{7,5},{8,10},{9,11},{10,... | collective-permute-start | bytes 786440 | tf_op jit(solution)/shard_map/ppermute | solution.py:262
  29.1 0.0 collective-permute-done.6.refs_1_
  29.1 2.3 %shard_map.72.refs_12_ = bf16[1536,512]{1,0:T(8,128)(2,1)} custom-call(bf16[1536,512]{1,0:T(8,128)(2,1)S(1)} %get-tuple-element.64.refs_0_, bf16[1536,512]{1,0:T(8,128)(2,1)S(1)} %collective-permute-done.6.refs_1_, s32[8,128]{1,0:T(8,128)S(1)} %get-tuple-element.66.refs_2_, f32[24,128]{1,0:T(8,128)S(1)} %get-tuple-element.67.refs_3_, ...), custom_call_target="tpu_custom_call" | custom-call | flops 1 | bytes 1 | tf_op jit(solution)/shard_map/pallas_call | solution.py:229
  31.4 12.5 %collective-permute-done.9.refs_11_ = bf16[768,512]{1,0:T(8,128)(2,1)S(1)} collective-permute-done((bf16[768,512]{1,0:T(8,128)(2,1)S(1)}, bf16[768,512]{1,0:T(8,128)(2,1)S(1)}, u32[]{:S(2)}, u32[]{:S(2)}) %collective-permute-start.9) | collective-permute-done | bytes 786464 | tf_op jit(solution)/shard_map/ppermute | solution.py:262
  43.9 3.1 %shard_map.73.refs_12_ = bf16[1536,512]{1,0:T(8,128)(2,1)} custom-call(bf16[1536,512]{1,0:T(8,128)(2,1)S(1)} %get-tuple-element.64.refs_0_, bf16[1536,512]{1,0:T(8,128)(2,1)S(1)} %collective-permute-done.6.refs_1_, s32[8,128]{1,0:T(8,128)S(1)} %get-tuple-element.66.refs_2_, ...), custom_call_target="tpu_custom_call", output_to_operand_aliasing={{}: (12, {})} | custom-call | flops 1 | bytes 1 | tf_op jit(solution)/shard_map/pallas_call | solution.py:229
  46.9 2.1 %collective-permute-done.8.refs_11_ = bf16[256,512]{1,0:T(8,128)(2,1)S(1)} collective-permute-done((bf16[256,512]{1,0:T(8,128)(2,1)S(1)}, bf16[256,512]{1,0:T(8,128)(2,1)S(1)}, u32[]{:S(2)}, u32[]{:S(2)}) %collective-permute-start.8) | collective-permute-done | bytes 262176 | tf_op jit(solution)/shard_map/ppermute | solution.py:262
  49.0 1.5 %shard_map.74 = bf16[1536,512]{1,0:T(8,128)(2,1)} custom-call(bf16[1536,512]{1,0:T(8,128)(2,1)S(1)} %get-tuple-element.64.refs_0_, bf16[1536,512]{1,0:T(8,128)(2,1)S(1)} %collective-permute-done.6.refs_1_, s32[8,128]{1,0:T(8,128)S(1)} %get-tuple-element.66.refs_2_, f32[24,128]{1,0:T(8,128)S(1)} %get-tuple-element.67.refs_3_, ...), custom_call_target="tpu_custom_call", output_to_operand_aliasing={{}: (12, {})} | custom-call | flops 1 | bytes 1 | tf_op jit(solution)/shard_map/pallas_call | solution.py:229
Async XLA Ops:
  0.0 5.5 %copy-start.3 = (bf16[1024]{0:T(1024)(128)(2,1)S(1)}, bf16[1024]{0:T(1024)(128)(2,1)}, u32[]{:S(2)}) copy-start(bf16[1024]{0:T(1024)(128)(2,1)} %gain.4) | copy-start | bytes 6148
  0.0 5.5 %copy-start = (bf16[1024,2048]{1,0:T(8,128)(2,1)S(1)}, bf16[1024,2048]{1,0:T(8,128)(2,1)}, u32[]{:S(2)}) copy-start(bf16[1024,2048]{1,0:T(8,128)(2,1)} %weight.7) | copy-start | bytes 12582916
  0.0 5.5 %copy-start.1 = (bf16[1536,1024]{1,0:T(8,128)(2,1)S(1)}, bf16[1536,1024]{1,0:T(8,128)(2,1)}, u32[]{:S(2)}) copy-start(bf16[1536,1024]{1,0:T(8,128)(2,1)} %tokens.7) | copy-start | bytes 9437188
  5.0 2.7 %copy-start.2 = (bf16[512,512]{1,0:T(8,128)(2,1)S(1)}, bf16[512,512]{1,0:T(8,128)(2,1)}, u32[]{:S(2)}) copy-start(bf16[512,512]{1,0:T(8,128)(2,1)} %get-tuple-element.44.keep) | copy-start | bytes 1572868
  5.0 2.7 %collective-permute-start = (bf16[512,512]{1,0:T(8,128)(2,1)}, bf16[512,512]{1,0:T(8,128)(2,1)S(1)}, u32[]{:S(2)}, u32[]{:S(2)}) collective-permute-start(bf16[512,512]{1,0:T(8,128)(2,1)} %get-tuple-element.45), channel_id=1, source_target_pairs={{0,1},{1,0},{2,3},{3,2},{4,5},{5,4},{6,7},{7,6},{8,9},{9,8},{10,11... | collective-permute-start | bytes 1572872 | tf_op jit(solution)/shard_map/ppermute | solution.py:257
  7.9 10.4 %collective-permute-start.2 = (bf16[768,512]{1,0:T(8,128)(2,1)S(1)}, bf16[768,512]{1,0:T(8,128)(2,1)S(1)}, u32[]{:S(2)}, u32[]{:S(2)}) collective-permute-start(bf16[768,512]{1,0:T(8,128)(2,1)S(1)} %get-tuple-element.51), channel_id=1, source_target_pairs={{0,1},{1,0},{2,3},{3,2},{4,5},{5,4},{6,7},{7,6},{8,9},{9,8},{10,11... | collective-permute-start | bytes 2359304 | tf_op jit(solution)/shard_map/ppermute | solution.py:257
  8.0 15.5 %collective-permute-start.1 = (bf16[512,512]{1,0:T(8,128)(2,1)S(1)}, bf16[512,512]{1,0:T(8,128)(2,1)S(1)}, u32[]{:S(2)}, u32[]{:S(2)}) collective-permute-start(bf16[512,512]{1,0:T(8,128)(2,1)S(1)} %shard_map.65), channel_id=1, source_target_pairs={{0,2},{1,3},{2,0},{3,1},{4,6},{5,7},{6,4},{7,5},{8,10},{9,11},{10,... | collective-permute-start | bytes 1572872 | tf_op jit(solution)/shard_map/ppermute | solution.py:262
  15.2 2.2 %copy-start.4 = (s32[4]{0:T(128)S(1)}, s32[4]{0:T(128)}, u32[]{:S(2)}) copy-start(s32[4]{0:T(128)} %live.1) | copy-start | bytes 52
  15.2 2.2 %copy-start.5 = (s32[4]{0:T(128)S(1)}, s32[4]{0:T(128)}, u32[]{:S(2)}) copy-start(s32[4]{0:T(128)} %span) | copy-start | bytes 52
  15.2 2.2 %copy-start.6 = (f32[1,128]{1,0:T(1,128)S(1)}, f32[1,128]{1,0:T(1,128)}, u32[]{:S(2)}) copy-start(f32[1,128]{1,0:T(1,128)} %constant.4.clone.frequencies) | copy-start | bytes 1540
  15.3 7.3 %collective-permute-start.5 = (f32[12,128]{1,0:T(8,128)S(1)}, f32[12,128]{1,0:T(8,128)S(1)}, u32[]{:S(2)}, u32[]{:S(2)}) collective-permute-start(f32[12,128]{1,0:T(8,128)S(1)} %get-tuple-element.71.refs_7_), channel_id=1, source_target_pairs={{0,3},{1,0},{2,1},{3,2},{4,7},{5,4},{6,5},{7,6},{8,11},{9,8},{10,9... | collective-permute-start | bytes 18440 | tf_op jit(solution)/shard_map/ppermute | solution.py:276
  15.3 8.1 %collective-permute-start.4 = (f32[12,128]{1,0:T(8,128)S(1)}, f32[12,128]{1,0:T(8,128)S(1)}, u32[]{:S(2)}, u32[]{:S(2)}) collective-permute-start(f32[12,128]{1,0:T(8,128)S(1)} %get-tuple-element.71.refs_7_), channel_id=1, source_target_pairs={{0,2},{1,3},{2,0},{3,1},{4,6},{5,7},{6,4},{7,5},{8,10},{9,11},{10,... | collective-permute-start | bytes 18440 | tf_op jit(solution)/shard_map/ppermute | solution.py:276
  16.7 6.7 %collective-permute-start.3 = (f32[12,128]{1,0:T(8,128)S(1)}, f32[12,128]{1,0:T(8,128)S(1)}, u32[]{:S(2)}, u32[]{:S(2)}) collective-permute-start(f32[12,128]{1,0:T(8,128)S(1)} %get-tuple-element.71.refs_7_), channel_id=1, source_target_pairs={{0,1},{1,2},{2,3},{3,0},{4,5},{5,6},{6,7},{7,4},{8,9},{9,10},{10,1... | collective-permute-start | bytes 18440 | tf_op jit(solution)/shard_map/ppermute | solution.py:276
  23.4 5.7 %collective-permute-start.6 = (bf16[1536,512]{1,0:T(8,128)(2,1)S(1)}, bf16[1536,512]{1,0:T(8,128)(2,1)S(1)}, u32[]{:S(2)}, u32[]{:S(2)}) collective-permute-start(bf16[1536,512]{1,0:T(8,128)(2,1)S(1)} %get-tuple-element.65), channel_id=1, source_target_pairs={{0,1},{1,0},{2,3},{3,2},{4,5},{5,4},{6,7},{7,6},{8,9},{9,8},{10,11... | collective-permute-start | bytes 4718600 | tf_op jit(solution)/shard_map/ppermute | solution.py:285
  23.5 20.4 %collective-permute-start.9 = (bf16[768,512]{1,0:T(8,128)(2,1)S(1)}, bf16[768,512]{1,0:T(8,128)(2,1)S(1)}, u32[]{:S(2)}, u32[]{:S(2)}) collective-permute-start(bf16[768,512]{1,0:T(8,128)(2,1)S(1)} %shard_map.67), channel_id=1, source_target_pairs={{0,2},{1,3},{2,0},{3,1},{4,6},{5,7},{6,4},{7,5},{8,10},{9,11},{10,... | collective-permute-start | bytes 2359304 | tf_op jit(solution)/shard_map/ppermute | solution.py:262
  25.3 2.0 %collective-permute-start.7 = (bf16[256,512]{1,0:T(8,128)(2,1)S(1)}, bf16[256,512]{1,0:T(8,128)(2,1)S(1)}, u32[]{:S(2)}, u32[]{:S(2)}) collective-permute-start(bf16[256,512]{1,0:T(8,128)(2,1)S(1)} %get-tuple-element.76), channel_id=1, source_target_pairs={{0,1},{1,0},{2,3},{3,2},{4,5},{5,4},{6,7},{7,6},{8,9},{9,8},{10,11... | collective-permute-start | bytes 786440 | tf_op jit(solution)/shard_map/ppermute | solution.py:257
  27.3 21.7 %collective-permute-start.8 = (bf16[256,512]{1,0:T(8,128)(2,1)S(1)}, bf16[256,512]{1,0:T(8,128)(2,1)S(1)}, u32[]{:S(2)}, u32[]{:S(2)}) collective-permute-start(bf16[256,512]{1,0:T(8,128)(2,1)S(1)} %shard_map.71), channel_id=1, source_target_pairs={{0,2},{1,3},{2,0},{3,1},{4,6},{5,7},{6,4},{7,5},{8,10},{9,11},{10,... | collective-permute-start | bytes 786440 | tf_op jit(solution)/shard_map/ppermute | solution.py:262

commit v10 on v8

--- a/solution.py
+++ b/solution.py
@@ -17,7 +17,7 @@
 norm_eps = 1e-05
 
 TILE = 256
-CHUNKS = (2, 3, 1)
+CHUNKS = (2, 2, 2)
 
 PARAMS = pltpu.CompilerParams(vmem_limit_bytes=16 * 1024 * 1024)
 FIRST = pltpu.CompilerParams(vmem_limit_bytes=56 * 1024 * 1024)
@@ -110,7 +110,8 @@
     out[...] = (keep[...].astype(jnp.float32) + received[...].astype(jnp.float32)).astype(out.dtype)
 
 
-def table_kernel(span, frequencies, far_cos, far_sin, near_cos, near_sin):
+def table_kernel(live, span, frequencies, limit, far_cos, far_sin, near_cos, near_sin):
+    limit[...] = jnp.full(limit.shape, live[lax.axis_index("serve")] * BLOCK, jnp.int32)
     blocks = far_cos.shape[0]
     start = span[lax.axis_index("serve")] * PAGE
     first = start + BLOCK * lax.broadcasted_iota(jnp.int32, (blocks, HD), 0)
@@ -123,19 +124,18 @@
 
 
 def finish_kernel(first, count, tensor_count, model_dim, *refs):
-    live, keep, received, far_cos, far_sin, near_cos, near_sin = refs[:7]
+    keep, received, limit, far_cos, far_sin, near_cos, near_sin = refs[:7]
     squares, arrived = refs[7 : 7 + tensor_count], refs[7 + tensor_count : -4]
     out, staged, sems = refs[-3:]
     on_diagonal = lax.broadcasted_iota(jnp.int32, (LANES, LANES), 0) == lax.broadcasted_iota(
         jnp.int32, (LANES, LANES), 1
     )
     sign = jnp.where(lax.broadcasted_iota(jnp.int32, (1, HD), 1) < HD // 2, -1.0, 1.0)
-    live_rows = live[lax.axis_index("serve")] * BLOCK
     copies = []
     for index in range(count):
         start = (first + index) * TILE
         rows, inside = pl.ds(start, TILE), pl.ds(index * TILE, TILE)
-        values = keep[rows, :].astype(jnp.float32) + received[rows, :].astype(jnp.float32)
+        values = keep[inside, :].astype(jnp.float32) + received[inside, :].astype(jnp.float32)
         for part in arrived:
             values += part[inside, :].astype(jnp.float32)
         columns = []
@@ -143,7 +143,7 @@
             totals = functools.reduce(jnp.add, [ref[row : row + 1, :] for ref in squares])
             columns.append(jnp.sum(jnp.where(on_diagonal, totals, 0.0), axis=1, keepdims=True))
         scales = 1.0 / jnp.sqrt(jnp.concatenate(columns, axis=0) / model_dim + norm_eps)
-        alive = start + lax.broadcasted_iota(jnp.int32, (TILE, 1), 0) < live_rows
+        alive = start + lax.broadcasted_iota(jnp.int32, (TILE, LANES), 0) < limit[0:1, :]
         cosines, sines = [], []
         for block in range(start // BLOCK, (start + TILE) // BLOCK):
             block_cos = far_cos[block : block + 1, :]
@@ -213,25 +213,24 @@
         shapes = [(slot_rows // BLOCK, HD)] * 2 + [(BLOCK, HD)] * 2
         made = pl.pallas_call(
             table_kernel,
-            in_specs=[pl.BlockSpec(memory_space=pltpu.SMEM), pl.BlockSpec(memory_space=pltpu.VMEM)],
-            out_shape=[jax.ShapeDtypeStruct(shape, jnp.float32) for shape in shapes],
-            out_specs=[pl.BlockSpec(memory_space=pltpu.VMEM)] * 4,
+            in_specs=[pl.BlockSpec(memory_space=pltpu.SMEM)] * 2 + [pl.BlockSpec(memory_space=pltpu.VMEM)],
+            out_shape=[jax.ShapeDtypeStruct((8, LANES), jnp.int32)]
+            + [jax.ShapeDtypeStruct(shape, jnp.float32) for shape in shapes],
+            out_specs=[pl.BlockSpec(memory_space=pltpu.VMEM)] * 5,
             compiler_params=PARAMS,
             cost_estimate=COST,
-        )(span_offset, jnp.asarray(frequencies))
+        )(live_blocks, span_offset, jnp.asarray(frequencies))
         return list(made)
 
     def finish(first, count, keep, received, table, squares, arrived, result):
         vmem = pl.BlockSpec(memory_space=pltpu.VMEM)
-        operands = [live_blocks, keep, received] + table + squares + arrived
+        operands = [keep, received] + table + squares + arrived
         aliases = {len(operands): 0}
         if result is None:
             result, aliases = jnp.zeros((1,), jnp.bfloat16), {}
         return pl.pallas_call(
             functools.partial(finish_kernel, first, count, tensor_count, model_dim),
-            in_specs=[pl.BlockSpec(memory_space=pltpu.SMEM)]
-            + [vmem] * (len(operands) - 1)
-            + [pl.BlockSpec(memory_space=pl.ANY)],
+            in_specs=[vmem] * len(operands) + [pl.BlockSpec(memory_space=pl.ANY)],
             out_shape=jax.ShapeDtypeStruct((slot_rows, columns), jnp.bfloat16),
             out_specs=pl.BlockSpec(memory_space=pltpu.HBM),
             scratch_shapes=[pltpu.VMEM((count * TILE, columns), jnp.bfloat16), pltpu.SemaphoreType.DMA((count,))],
@@ -244,11 +243,11 @@
     firsts = [sum(CHUNKS[:index]) for index in range(len(CHUNKS))]
     chunk_count = len(CHUNKS)
 
-    def start_chunk(gain, index, staged=False):
-        made = []
-        for step in others:
-            made += product(gain, step, [(firsts[index], CHUNKS[index])], staged)[0]
-        return made
+    chunks = list(zip(firsts, CHUNKS))
+
+    def start_chunks(gain, wanted, staged=False):
+        made = [product(gain, step, wanted, staged)[0] for step in others]
+        return [list(parts) for parts in zip(*made)]
 
     def add_halves(made):
         return [
@@ -265,32 +264,24 @@
         return [lax.ppermute(part, "tensor", shift(step)) for step, part in zip(others, sums)]
 
     hold = lax.optimization_barrier
-    made = start_chunk(norm_gain, 0, staged=True)
+    (made,) = start_chunks(norm_gain, chunks[:1], staged=True)
     made, gain = hold((made, norm_gain))
     sums = add_halves(made)
-    made = start_chunk(gain, 1)
-    sums, made, gain, span_offset = hold((sums, made, gain, span_offset))
-
-    arrived = cross(sums)
-    sums = add_halves(made)
-    waiting = [start_chunk(gain, index) for index in range(2, chunk_count)]
-    ((keep, send),), squares = product(gain, 0, [(0, tiles)], with_squares=True)
+    waiting = start_chunks(gain, chunks[1:])
+    sums, waiting, gain, span_offset, live_blocks = hold((sums, waiting, gain, span_offset, live_blocks))
+
+    arrivals = [cross(sums)] + [cross(add_halves(made)) for made in waiting]
+    own, squares = product(gain, 0, chunks, with_squares=True)
     squares = [squares] + [
         lax.ppermute(squares, "tensor", [(i, (i + step) % tensor_count) for i in range(tensor_count)])
         for step in range(1, tensor_count)
     ]
     table = tables(span_offset)
-    arrived, sums, waiting, keep, send, squares, table = hold(
-        (arrived, sums, waiting, keep, send, squares, table)
-    )
-
-    arrivals = [arrived, cross(sums)] + [cross(add_halves(made)) for made in waiting]
-    received = lax.ppermute(send, "tensor", swap)
+
     result = None
-    for index in range(chunk_count):
-        result = finish(
-            firsts[index], CHUNKS[index], keep, received, table, squares, arrivals[index], result
-        )
+    for (first, count), (keep, send), arrived in zip(chunks, own, arrivals):
+        received = lax.ppermute(send, "tensor", swap)
+        result = finish(first, count, keep, received, table, squares, arrived, result)
     return result
 
 

time: 49.8 us -> 49.8 us (level)
  waiting for transfers between devices: 23.1 us -> 25.1 us
  Pallas kernels: 17.3 us -> 15.5 us
    ppermute x3, waiting for transfers between devices: 15.7 us -> 19.4 us  [cross(): lax.ppermute(part, 'tensor', shift(step))]
    ppermute x3, waiting for transfers between devices: 1.82 us -> 0.01 us  [add_halves(): lax.ppermute(send, 'tensor', swap)]
    ppermute x3, starting transfers between devices: 6.35 us -> 4.66 us  [cross(): lax.ppermute(part, 'tensor', shift(step))]
    pallas_call x3, Pallas kernels: 5.87 us -> 4.18 us  [finish(): pl.pallas_call(functools.partial(finish_kernel, first, count, tensor_coun...]
    ppermute x1 -> x3, starting transfers between devices: 0.01 us -> 1.21 us  [shards(): received = lax.ppermute(send, 'tensor', swap)]
    pallas_call x4 -> x3, Pallas kernels: 10.4 us -> 10.2 us  [product(): pl.pallas_call(functools.partial(product_kernel, step, chip_count, chunks...]
  transfers between devices with their start and end apart: 10 -> 12, of which waited for: 5 -> 4; matrix products, arithmetic and copies ran while one was open for 0% -> 0% of each run, Pallas kernels for 23% -> 20%
where the time goes in v10:
time: 49.8 us; the launch traced here: 49.6 us
  waiting for transfers between devices  25.1 us (50%)
  Pallas kernels  15.5 us (31%)
  starting transfers between devices  8.82 us (18%)
    ppermute x3, waiting for transfers between devices, cross(): lax.ppermute(part, 'tensor', shift(step))  19.4 us
    pallas_call x3, Pallas kernels, product(): pl.pallas_call(functools.partial(product_kernel, step, chip_count, chunks...  10.2 us
    ppermute x3, waiting for transfers between devices, shards(): lax.ppermute(squares, 'tensor', [(i, (i + step) % tensor_count) for i in...  5.78 us
    ppermute x3, starting transfers between devices, cross(): lax.ppermute(part, 'tensor', shift(step))  4.66 us
    pallas_call x3, Pallas kernels, finish(): pl.pallas_call(functools.partial(finish_kernel, first, count, tensor_coun...  4.18 us
    ppermute x3, starting transfers between devices, shards(): lax.ppermute(squares, 'tensor', [(i, (i + step) % tensor_count) for i in...  1.85 us
    ppermute x3, starting transfers between devices, shards(): received = lax.ppermute(send, 'tensor', swap)  1.21 us
    ppermute x3, starting transfers between devices, add_halves(): lax.ppermute(send, 'tensor', swap)  1.1 us
  transfers between devices with their start and end apart: 12, of which 4 were waited for; matrix products, arithmetic and copies ran while one was open for 0% of the time, Pallas kernels for 20%

profile of v10, /device:TPU:0, one launch (start us, length us, event | category | flops | bytes accessed | tf_op | source)
XLA Modules:
  0.0 49.6 jit_solution(9786044896704483842)
XLA Ops:
  0.0 0.0 copy-start.3
  0.0 0.0 copy-start
  0.0 0.0 copy-start.1
  0.0 4.1 %shard_map.64 = (bf16[512,512]{1,0:T(8,128)(2,1)}, bf16[512,512]{1,0:T(8,128)(2,1)}) custom-call(bf16[1536,1024]{1,0:T(8,128)(2,1)} %tokens.5, bf16[1024]{0:T(1024)(128)(2,1)} %gain.3, bf16[1024,2048]{1,0:T(8,128)(2,1)} %weight.5), custom_call_target="tpu_custom_call" | custom-call | flops 1 | bytes 1 | tf_op jit(solution)/shard_map/pallas_call | solution.py:197
  4.1 0.0 copy-start.2
  4.1 0.5 %collective-permute-start = (bf16[512,512]{1,0:T(8,128)(2,1)}, bf16[512,512]{1,0:T(8,128)(2,1)S(1)}, u32[]{:S(2)}, u32[]{:S(2)}) collective-permute-start(bf16[512,512]{1,0:T(8,128)(2,1)} %get-tuple-element.37), channel_id=1, source_target_pairs={{0,1},{1,0},{2,3},{3,2},{4,5},{5,4},{6,7},{7,6},{8,9},{9,8},{10,11... | collective-permute-start | bytes 1572872 | tf_op jit(solution)/shard_map/ppermute | solution.py:259
  4.6 0.0 copy-done.3
  4.7 0.0 copy-done
  4.7 0.0 copy-done.1
  4.7 2.4 %shard_map.66 = (bf16[512,512]{1,0:T(8,128)(2,1)S(1)}, bf16[512,512]{1,0:T(8,128)(2,1)S(1)}, bf16[512,512]{1,0:T(8,128)(2,1)S(1)}, bf16[512,512]{1,0:T(8,128)(2,1)S(1)}) custom-call(bf16[1536,1024]{1,0:T(8,128)(2,1)S(1)} %copy-done.1, bf16[1024]{0:T(1024)(128)(2,1)S(1)} %copy-done.3, bf16[1024,2048]{1,0:T(8,128)(2,1)S(1)} %copy-done), custom_call_target="tpu_custom_call" | custom-call | flops 1 | bytes 1 | tf_op jit(solution)/shard_map/pallas_call | solution.py:197
  7.0 0.0 collective-permute-done.received
  7.0 0.0 copy-done.2
  7.0 0.1 shard_map.65
  7.2 0.1 collective-permute-start.5
  7.3 0.5 collective-permute-start.8
  7.8 2.6 %collective-permute-start.11 = (bf16[512,512]{1,0:T(8,128)(2,1)S(1)}, bf16[512,512]{1,0:T(8,128)(2,1)S(1)}, u32[]{:S(2)}, u32[]{:S(2)}) collective-permute-start(bf16[512,512]{1,0:T(8,128)(2,1)S(1)} %shard_map.65), channel_id=1, source_target_pairs={{0,2},{1,3},{2,0},{3,1},{4,6},{5,7},{6,4},{7,5},{8,10},{9,11},{10,... | collective-permute-start | bytes 1572872 | tf_op jit(solution)/shard_map/ppermute | solution.py:264
  10.3 3.7 %shard_map.67 = (bf16[512,512]{1,0:T(8,128)(2,1)S(1)}, bf16[512,512]{1,0:T(8,128)(2,1)S(1)}, bf16[512,512]{1,0:T(8,128)(2,1)S(1)}, bf16[512,512]{1,0:T(8,128)(2,...) custom-call(bf16[1536,1024]{1,0:T(8,128)(2,1)S(1)} %copy-done.1, ...), custom_call_target="tpu_custom_call" | custom-call | flops 1 | bytes 1 | tf_op jit(solution)/shard_map/pallas_call | solution.py:197
  14.1 0.1 collective-permute-start.4
  14.1 1.8 %collective-permute-start.3 = (f32[12,128]{1,0:T(8,128)S(1)}, f32[12,128]{1,0:T(8,128)S(1)}, u32[]{:S(2)}, u32[]{:S(2)}) collective-permute-start(f32[12,128]{1,0:T(8,128)S(1)} %get-tuple-element.53.refs_7_), channel_id=1, source_target_pairs={{0,2},{1,3},{2,0},{3,1},{4,6},{5,7},{6,4},{7,5},{8,10},{9,11},{10,... | collective-permute-start | bytes 18440 | tf_op jit(solution)/shard_map/ppermute | solution.py:276
  15.9 0.0 collective-permute-done.5.received
  15.9 0.0 collective-permute-start.2
  15.9 0.0 collective-permute-done.8.received
  15.9 0.0 copy-start.4
  15.9 0.0 copy-start.5
  15.9 0.0 copy-start.6
  15.9 0.5 collective-permute-start.10
  16.4 0.1 shard_map.69
  16.5 0.1 shard_map.70
  16.7 5.7 %collective-permute-done.4.refs_10_ = f32[12,128]{1,0:T(8,128)S(1)} collective-permute-done((f32[12,128]{1,0:T(8,128)S(1)}, f32[12,128]{1,0:T(8,128)S(1)}, u32[]{:S(2)}, u32[]{:S(2)}) %collective-permute-start.4) | collective-permute-done | bytes 6176 | tf_op jit(solution)/shard_map/ppermute | solution.py:276
  22.4 0.8 %collective-permute-start.7 = (bf16[512,512]{1,0:T(8,128)(2,1)S(1)}, bf16[512,512]{1,0:T(8,128)(2,1)S(1)}, u32[]{:S(2)}, u32[]{:S(2)}) collective-permute-start(bf16[512,512]{1,0:T(8,128)(2,1)S(1)} %get-tuple-element.57), channel_id=1, source_target_pairs={{0,1},{1,0},{2,3},{3,2},{4,5},{5,4},{6,7},{7,6},{8,9},{9,8},{10,11... | collective-permute-start | bytes 1572872 | tf_op jit(solution)/shard_map/ppermute | solution.py:283
  23.1 0.1 collective-permute-done.3.refs_9_
  23.2 1.8 %collective-permute-start.9 = (bf16[512,512]{1,0:T(8,128)(2,1)S(1)}, bf16[512,512]{1,0:T(8,128)(2,1)S(1)}, u32[]{:S(2)}, u32[]{:S(2)}) collective-permute-start(bf16[512,512]{1,0:T(8,128)(2,1)S(1)} %shard_map.70), channel_id=1, source_target_pairs={{0,2},{1,3},{2,0},{3,1},{4,6},{5,7},{6,4},{7,5},{8,10},{9,11},{10,... | collective-permute-start | bytes 1572872 | tf_op jit(solution)/shard_map/ppermute | solution.py:264
  24.9 0.0 collective-permute-done.2.refs_8_
  24.9 0.0 collective-permute-start.1
  25.0 0.0 collective-permute-done.11.refs_11_
  25.0 0.3 collective-permute-start.6
  25.3 0.0 copy-done.4
  25.3 0.0 copy-done.5
  25.3 0.0 copy-done.6
  25.3 0.7 %shard_map.68 = (s32[8,128]{1,0:T(8,128)S(1)}, f32[24,128]{1,0:T(8,128)S(1)}, f32[24,128]{1,0:T(8,128)S(1)}, f32[64,128]{1,0:T(8,128)S(1)}, f32[64,128]{1,0:T(8,128)S(1)}) custom-call(s32[4]{0:T(128)S(1)} %copy-done.4, s32[4]{0:T(128)S(1)} %copy-done.5, f32[1,128]{1,0:T(1,128)S(1)} %copy-done.6), custom_call_target="tpu_custom_call" | custom-call | flops 1 | bytes 1 | tf_op jit(solution)/shard_map/pallas_call | solution.py:214
  26.0 0.0 collective-permute-done.10.refs_1_
  26.0 1.4 %shard_map.71.refs_12_ = bf16[1536,512]{1,0:T(8,128)(2,1)} custom-call(bf16[512,512]{1,0:T(8,128)(2,1)S(1)} %get-tuple-element.60.refs_0_, bf16[512,512]{1,0:T(8,128)(2,1)S(1)} %collective-permute-done.10.refs_1_, s32[8,128]{1,0:T(8,128)S(1)} %get-tuple-element.48.refs_2_, f32[24,128]{1,0:T(8,128)S(1)} %get-tuple-element.49.refs_3_, ...), custom_call_target="tpu_custom_call" | custom-call | flops 1 | bytes 1 | tf_op jit(solution)/shard_map/pallas_call | solution.py:231
  27.4 0.0 collective-permute-done.7.refs_1_
  27.4 10.5 %collective-permute-done.9.refs_11_ = bf16[512,512]{1,0:T(8,128)(2,1)S(1)} collective-permute-done((bf16[512,512]{1,0:T(8,128)(2,1)S(1)}, bf16[512,512]{1,0:T(8,128)(2,1)S(1)}, u32[]{:S(2)}, u32[]{:S(2)}) %collective-permute-start.9) | collective-permute-done | bytes 524320 | tf_op jit(solution)/shard_map/ppermute | solution.py:264
  38.0 1.4 %shard_map.72.refs_12_ = bf16[1536,512]{1,0:T(8,128)(2,1)} custom-call(bf16[512,512]{1,0:T(8,128)(2,1)S(1)} %get-tuple-element.56.refs_0_, bf16[512,512]{1,0:T(8,128)(2,1)S(1)} %collective-permute-done.7.refs_1_, s32[8,128]{1,0:T(8,128)S(1)} %get-tuple-element.48.refs_2_, f32[24,128]{1,0:T(8,128)S(1)} %get-tuple-element.49.refs_3_, ...), custom_call_target="tpu_custom_call", output_to_operand_aliasing={{}: (12, {})} | custom-call | flops 1 | bytes 1 | tf_op jit(solution)/shard_map/pallas_call | solution.py:231
  39.4 0.0 collective-permute-done.1.refs_1_
  39.4 8.8 %collective-permute-done.6.refs_11_ = bf16[512,512]{1,0:T(8,128)(2,1)S(1)} collective-permute-done((bf16[512,512]{1,0:T(8,128)(2,1)S(1)}, bf16[512,512]{1,0:T(8,128)(2,1)S(1)}, u32[]{:S(2)}, u32[]{:S(2)}) %collective-permute-start.6) | collective-permute-done | bytes 524320 | tf_op jit(solution)/shard_map/ppermute | solution.py:264
  48.2 1.4 %shard_map.73 = bf16[1536,512]{1,0:T(8,128)(2,1)} custom-call(bf16[512,512]{1,0:T(8,128)(2,1)S(1)} %get-tuple-element.44.refs_0_, bf16[512,512]{1,0:T(8,128)(2,1)S(1)} %collective-permute-done.1.refs_1_, s32[8,128]{1,0:T(8,128)S(1)} %get-tuple-element.48.refs_2_, f32[24,128]{1,0:T(8,128)S(1)} %get-tuple-element.49.refs_3_, ...), custom_call_target="tpu_custom_call", output_to_operand_aliasing={{}: (12, {})} | custom-call | flops 1 | bytes 1 | tf_op jit(solution)/shard_map/pallas_call | solution.py:231
Async XLA Ops:
  0.0 4.6 %copy-start.3 = (bf16[1024]{0:T(1024)(128)(2,1)S(1)}, bf16[1024]{0:T(1024)(128)(2,1)}, u32[]{:S(2)}) copy-start(bf16[1024]{0:T(1024)(128)(2,1)} %gain.3) | copy-start | bytes 6148
  0.0 4.6 %copy-start = (bf16[1024,2048]{1,0:T(8,128)(2,1)S(1)}, bf16[1024,2048]{1,0:T(8,128)(2,1)}, u32[]{:S(2)}) copy-start(bf16[1024,2048]{1,0:T(8,128)(2,1)} %weight.5) | copy-start | bytes 12582916
  0.0 4.7 %copy-start.1 = (bf16[1536,1024]{1,0:T(8,128)(2,1)S(1)}, bf16[1536,1024]{1,0:T(8,128)(2,1)}, u32[]{:S(2)}) copy-start(bf16[1536,1024]{1,0:T(8,128)(2,1)} %tokens.5) | copy-start | bytes 9437188
  4.1 2.9 %copy-start.2 = (bf16[512,512]{1,0:T(8,128)(2,1)S(1)}, bf16[512,512]{1,0:T(8,128)(2,1)}, u32[]{:S(2)}) copy-start(bf16[512,512]{1,0:T(8,128)(2,1)} %get-tuple-element.36.keep) | copy-start | bytes 1572868
  4.1 2.9 %collective-permute-start = (bf16[512,512]{1,0:T(8,128)(2,1)}, bf16[512,512]{1,0:T(8,128)(2,1)S(1)}, u32[]{:S(2)}, u32[]{:S(2)}) collective-permute-start(bf16[512,512]{1,0:T(8,128)(2,1)} %get-tuple-element.37), channel_id=1, source_target_pairs={{0,1},{1,0},{2,3},{3,2},{4,5},{5,4},{6,7},{7,6},{8,9},{9,8},{10,11... | collective-permute-start | bytes 1572872 | tf_op jit(solution)/shard_map/ppermute | solution.py:259
  7.2 8.7 %collective-permute-start.5 = (bf16[512,512]{1,0:T(8,128)(2,1)S(1)}, bf16[512,512]{1,0:T(8,128)(2,1)S(1)}, u32[]{:S(2)}, u32[]{:S(2)}) collective-permute-start(bf16[512,512]{1,0:T(8,128)(2,1)S(1)} %get-tuple-element.55), channel_id=1, source_target_pairs={{0,1},{1,0},{2,3},{3,2},{4,5},{5,4},{6,7},{7,6},{8,9},{9,8},{10,11... | collective-permute-start | bytes 1572872 | tf_op jit(solution)/shard_map/ppermute | solution.py:259
  7.3 8.6 %collective-permute-start.8 = (bf16[512,512]{1,0:T(8,128)(2,1)S(1)}, bf16[512,512]{1,0:T(8,128)(2,1)S(1)}, u32[]{:S(2)}, u32[]{:S(2)}) collective-permute-start(bf16[512,512]{1,0:T(8,128)(2,1)S(1)} %get-tuple-element.59), channel_id=1, source_target_pairs={{0,1},{1,0},{2,3},{3,2},{4,5},{5,4},{6,7},{7,6},{8,9},{9,8},{10,11... | collective-permute-start | bytes 1572872 | tf_op jit(solution)/shard_map/ppermute | solution.py:259
  7.8 17.2 %collective-permute-start.11 = (bf16[512,512]{1,0:T(8,128)(2,1)S(1)}, bf16[512,512]{1,0:T(8,128)(2,1)S(1)}, u32[]{:S(2)}, u32[]{:S(2)}) collective-permute-start(bf16[512,512]{1,0:T(8,128)(2,1)S(1)} %shard_map.65), channel_id=1, source_target_pairs={{0,2},{1,3},{2,0},{3,1},{4,6},{5,7},{6,4},{7,5},{8,10},{9,11},{10,... | collective-permute-start | bytes 1572872 | tf_op jit(solution)/shard_map/ppermute | solution.py:264
  14.1 8.3 %collective-permute-start.4 = (f32[12,128]{1,0:T(8,128)S(1)}, f32[12,128]{1,0:T(8,128)S(1)}, u32[]{:S(2)}, u32[]{:S(2)}) collective-permute-start(f32[12,128]{1,0:T(8,128)S(1)} %get-tuple-element.53.refs_7_), channel_id=1, source_target_pairs={{0,3},{1,0},{2,1},{3,2},{4,7},{5,4},{6,5},{7,6},{8,11},{9,8},{10,9... | collective-permute-start | bytes 18440 | tf_op jit(solution)/shard_map/ppermute | solution.py:276
  14.1 9.0 %collective-permute-start.3 = (f32[12,128]{1,0:T(8,128)S(1)}, f32[12,128]{1,0:T(8,128)S(1)}, u32[]{:S(2)}, u32[]{:S(2)}) collective-permute-start(f32[12,128]{1,0:T(8,128)S(1)} %get-tuple-element.53.refs_7_), channel_id=1, source_target_pairs={{0,2},{1,3},{2,0},{3,1},{4,6},{5,7},{6,4},{7,5},{8,10},{9,11},{10,... | collective-permute-start | bytes 18440 | tf_op jit(solution)/shard_map/ppermute | solution.py:276
  15.9 9.0 %collective-permute-start.2 = (f32[12,128]{1,0:T(8,128)S(1)}, f32[12,128]{1,0:T(8,128)S(1)}, u32[]{:S(2)}, u32[]{:S(2)}) collective-permute-start(f32[12,128]{1,0:T(8,128)S(1)} %get-tuple-element.53.refs_7_), channel_id=1, source_target_pairs={{0,1},{1,2},{2,3},{3,0},{4,5},{5,6},{6,7},{7,4},{8,9},{9,10},{10,1... | collective-permute-start | bytes 18440 | tf_op jit(solution)/shard_map/ppermute | solution.py:276
  15.9 9.4 %copy-start.4 = (s32[4]{0:T(128)S(1)}, s32[4]{0:T(128)}, u32[]{:S(2)}) copy-start(s32[4]{0:T(128)} %live) | copy-start | bytes 52
  15.9 9.4 %copy-start.5 = (s32[4]{0:T(128)S(1)}, s32[4]{0:T(128)}, u32[]{:S(2)}) copy-start(s32[4]{0:T(128)} %span) | copy-start | bytes 52
  15.9 9.4 %copy-start.6 = (f32[1,128]{1,0:T(1,128)S(1)}, f32[1,128]{1,0:T(1,128)}, u32[]{:S(2)}) copy-start(f32[1,128]{1,0:T(1,128)} %constant.4.clone.frequencies) | copy-start | bytes 1540
  15.9 10.1 %collective-permute-start.10 = (bf16[512,512]{1,0:T(8,128)(2,1)S(1)}, bf16[512,512]{1,0:T(8,128)(2,1)S(1)}, u32[]{:S(2)}, u32[]{:S(2)}) collective-permute-start(bf16[512,512]{1,0:T(8,128)(2,1)S(1)} %get-tuple-element.61), channel_id=1, source_target_pairs={{0,1},{1,0},{2,3},{3,2},{4,5},{5,4},{6,7},{7,6},{8,9},{9,8},{10,11... | collective-permute-start | bytes 1572872 | tf_op jit(solution)/shard_map/ppermute | solution.py:283
  22.4 5.1 %collective-permute-start.7 = (bf16[512,512]{1,0:T(8,128)(2,1)S(1)}, bf16[512,512]{1,0:T(8,128)(2,1)S(1)}, u32[]{:S(2)}, u32[]{:S(2)}) collective-permute-start(bf16[512,512]{1,0:T(8,128)(2,1)S(1)} %get-tuple-element.57), channel_id=1, source_target_pairs={{0,1},{1,0},{2,3},{3,2},{4,5},{5,4},{6,7},{7,6},{8,9},{9,8},{10,11... | collective-permute-start | bytes 1572872 | tf_op jit(solution)/shard_map/ppermute | solution.py:283
  23.2 14.8 %collective-permute-start.9 = (bf16[512,512]{1,0:T(8,128)(2,1)S(1)}, bf16[512,512]{1,0:T(8,128)(2,1)S(1)}, u32[]{:S(2)}, u32[]{:S(2)}) collective-permute-start(bf16[512,512]{1,0:T(8,128)(2,1)S(1)} %shard_map.70), channel_id=1, source_target_pairs={{0,2},{1,3},{2,0},{3,1},{4,6},{5,7},{6,4},{7,5},{8,10},{9,11},{10,... | collective-permute-start | bytes 1572872 | tf_op jit(solution)/shard_map/ppermute | solution.py:264
  24.9 14.4 %collective-permute-start.1 = (bf16[512,512]{1,0:T(8,128)(2,1)S(1)}, bf16[512,512]{1,0:T(8,128)(2,1)S(1)}, u32[]{:S(2)}, u32[]{:S(2)}) collective-permute-start(bf16[512,512]{1,0:T(8,128)(2,1)S(1)} %get-tuple-element.45), channel_id=1, source_target_pairs={{0,1},{1,0},{2,3},{3,2},{4,5},{5,4},{6,7},{7,6},{8,9},{9,8},{10,11... | collective-permute-start | bytes 1572872 | tf_op jit(solution)/shard_map/ppermute | solution.py:283
  25.0 23.3 %collective-permute-start.6 = (bf16[512,512]{1,0:T(8,128)(2,1)S(1)}, bf16[512,512]{1,0:T(8,128)(2,1)S(1)}, u32[]{:S(2)}, u32[]{:S(2)}) collective-permute-start(bf16[512,512]{1,0:T(8,128)(2,1)S(1)} %shard_map.69), channel_id=1, source_target_pairs={{0,2},{1,3},{2,0},{3,1},{4,6},{5,7},{6,4},{7,5},{8,10},{9,11},{10,... | collective-permute-start | bytes 1572872 | tf_op jit(solution)/shard_map/ppermute | solution.py:264

commit v11 on v10

--- a/solution.py
+++ b/solution.py
@@ -12,6 +12,7 @@
 PAGE = 256
 BLOCK = 64
 LANES = 128
+SUBLANES = 8
 
 rope_base = 500000.0
 norm_eps = 1e-05
@@ -32,8 +33,30 @@
     return total
 
 
-def product_kernel(step, chip_count, chunks, staged, with_squares, tokens, gain, weight, *refs):
+def packed(squares, width):
+    per_row = width // LANES
+    row = lax.broadcasted_iota(jnp.int32, (2 * SUBLANES, LANES), 0)
+    parts = []
+    for place in range(per_row):
+        part = jnp.zeros((2 * SUBLANES, LANES), jnp.float32)
+        for index, line in enumerate(squares[place::per_row]):
+            high = line.astype(jnp.bfloat16).astype(jnp.float32)
+            part = jnp.where(row == index, high, part)
+            part = jnp.where(row == SUBLANES + index, line - high, part)
+        parts.append(part)
+    return jnp.concatenate(parts, axis=1).astype(jnp.bfloat16)
+
+
+def unpacked(ref, line):
+    index, place = divmod(line, ref.shape[1] // LANES)
+    part = ref[pl.ds(ref.shape[0] - 2 * SUBLANES, 2 * SUBLANES), place * LANES : (place + 1) * LANES]
+    part = part.astype(jnp.float32)
+    return part[index : index + 1] + part[SUBLANES + index : SUBLANES + index + 1]
+
+
+def product_kernel(step, chip_count, chunks, carrier, staged, with_squares, tokens, gain, weight, *refs):
     refs = list(refs)
+    known = refs.pop(0) if carrier is not None else None
     outs = [refs.pop(0) for _ in range(2 * len(chunks))]
     squares = refs.pop(0) if with_squares else None
     depth, width = tokens.shape[1], 2 * outs[0].shape[1]
@@ -73,6 +96,8 @@
     else:
         gains = gain[...].reshape(1, depth)
 
+    if carrier is not None:
+        squares[...] = known[...]
     for index, (first, count) in enumerate(chunks):
         for tile in range(first, first + count):
             if staged:
@@ -104,10 +129,25 @@
                     turned = jnp.transpose(total[part * LANES : (part + 1) * LANES])
                     row = tile * (TILE // LANES) + part
                     squares[row : row + 1, :] = jnp.sum(turned, axis=0, keepdims=True)
+    if carrier is not None:
+        lines = [squares[line : line + 1, :] for line in range(squares.shape[0])]
+        out = outs[2 * carrier + 1]
+        out[pl.ds(out.shape[0] - 2 * SUBLANES, 2 * SUBLANES), :] = packed(lines, out.shape[1])
 
 
 def add_kernel(keep, received, out):
     out[...] = (keep[...].astype(jnp.float32) + received[...].astype(jnp.float32)).astype(out.dtype)
+
+
+def add_carrier_kernel(keep, received, squares, out, pair_squares):
+    rows = pl.ds(0, keep.shape[0])
+    total = keep[...].astype(jnp.float32) + received[rows, :].astype(jnp.float32)
+    out[rows, :] = total.astype(out.dtype)
+    lines = []
+    for line in range(squares.shape[0]):
+        lines.append(squares[line : line + 1, :] + unpacked(received, line))
+        pair_squares[line : line + 1, :] = lines[-1]
+    out[pl.ds(keep.shape[0], 2 * SUBLANES), :] = packed(lines, out.shape[1])
 
 
 def table_kernel(live, span, frequencies, limit, far_cos, far_sin, near_cos, near_sin):
@@ -123,9 +163,9 @@
     near_sin[...] = jnp.sin(near)
 
 
-def finish_kernel(first, count, tensor_count, model_dim, *refs):
+def finish_kernel(first, count, chip_count, model_dim, *refs):
     keep, received, limit, far_cos, far_sin, near_cos, near_sin = refs[:7]
-    squares, arrived = refs[7 : 7 + tensor_count], refs[7 + tensor_count : -4]
+    pair_squares, carriers, arrived = refs[7], refs[8 : 7 + chip_count], refs[7 + chip_count : -4]
     out, staged, sems = refs[-3:]
     on_diagonal = lax.broadcasted_iota(jnp.int32, (LANES, LANES), 0) == lax.broadcasted_iota(
         jnp.int32, (LANES, LANES), 1
@@ -140,7 +180,9 @@
             values += part[inside, :].astype(jnp.float32)
         columns = []
         for row in range(start // LANES, (start + TILE) // LANES):
-            totals = functools.reduce(jnp.add, [ref[row : row + 1, :] for ref in squares])
+            totals = pair_squares[row : row + 1, :]
+            for ref in carriers:
+                totals += unpacked(ref, row)
             columns.append(jnp.sum(jnp.where(on_diagonal, totals, 0.0), axis=1, keepdims=True))
         scales = 1.0 / jnp.sqrt(jnp.concatenate(columns, axis=0) / model_dim + norm_eps)
         alive = start + lax.broadcasted_iota(jnp.int32, (TILE, LANES), 0) < limit[0:1, :]
@@ -178,11 +220,14 @@
     def shift(step):
         return [(i, (i + 2 * step) % tensor_count) for i in range(tensor_count)]
 
-    def product(gain, step, chunks, staged=False, with_squares=False):
+    def product(gain, step, chunks, staged=False, with_squares=False, carrier=None, known=None):
         vmem = pl.BlockSpec(memory_space=pltpu.VMEM)
         out_shape = [
             jax.ShapeDtypeStruct((count * TILE, columns), jnp.bfloat16) for _, count in chunks for _ in range(2)
         ]
+        if carrier is not None:
+            size = out_shape[2 * carrier].shape[0] + 2 * SUBLANES
+            out_shape[2 * carrier + 1] = jax.ShapeDtypeStruct((size, columns), jnp.bfloat16)
         if with_squares:
             out_shape.append(jax.ShapeDtypeStruct((slot_rows // LANES, LANES), jnp.float32))
         count = sum(count for _, count in chunks)
@@ -195,14 +240,14 @@
             pltpu.SemaphoreType.DMA,
         ]
         made = pl.pallas_call(
-            functools.partial(product_kernel, step, chip_count, chunks, staged, with_squares),
-            in_specs=[pl.BlockSpec(memory_space=pltpu.HBM) if staged else vmem] * 3,
+            functools.partial(product_kernel, step, chip_count, chunks, carrier, staged, with_squares),
+            in_specs=[pl.BlockSpec(memory_space=pltpu.HBM) if staged else vmem] * 3 + [vmem] * (known is not None),
             out_shape=out_shape,
             out_specs=[vmem] * len(out_shape),
             scratch_shapes=scratch if staged else [],
             compiler_params=FIRST if staged else PARAMS,
             cost_estimate=COST,
-        )(tokens, gain, kv_weight)
+        )(tokens, gain, kv_weight, *([] if known is None else [known]))
         made = list(made)
         squares = made.pop() if with_squares else None
         return list(zip(made[::2], made[1::2])), squares
@@ -229,7 +274,7 @@
         if result is None:
             result, aliases = jnp.zeros((1,), jnp.bfloat16), {}
         return pl.pallas_call(
-            functools.partial(finish_kernel, first, count, tensor_count, model_dim),
+            functools.partial(finish_kernel, first, count, chip_count, model_dim),
             in_specs=[vmem] * len(operands) + [pl.BlockSpec(memory_space=pl.ANY)],
             out_shape=jax.ShapeDtypeStruct((slot_rows, columns), jnp.bfloat16),
             out_specs=pl.BlockSpec(memory_space=pltpu.HBM),
@@ -244,10 +289,6 @@
     chunk_count = len(CHUNKS)
 
     chunks = list(zip(firsts, CHUNKS))
-
-    def start_chunks(gain, wanted, staged=False):
-        made = [product(gain, step, wanted, staged)[0] for step in others]
-        return [list(parts) for parts in zip(*made)]
 
     def add_halves(made):
         return [
@@ -260,23 +301,46 @@
             for keep, send in made
         ]
 
+    def add_carriers(made, squares):
+        added = [
+            pl.pallas_call(
+                add_carrier_kernel,
+                out_shape=[
+                    jax.ShapeDtypeStruct(send.shape, send.dtype),
+                    jax.ShapeDtypeStruct(squares.shape, squares.dtype),
+                ],
+                compiler_params=PARAMS,
+                cost_estimate=COST,
+            )(keep, lax.ppermute(send, "tensor", swap), squares)
+            for keep, send in made
+        ]
+        return [sums for sums, _ in added], added[0][1]
+
     def cross(sums):
         return [lax.ppermute(part, "tensor", shift(step)) for step, part in zip(others, sums)]
 
     hold = lax.optimization_barrier
-    (made,) = start_chunks(norm_gain, chunks[:1], staged=True)
-    made, gain = hold((made, norm_gain))
+    made, known = [], []
+    for step in others:
+        halves, squares = product(norm_gain, step, chunks[:1], staged=True, with_squares=True)
+        made += halves
+        known.append(squares)
+    made, gain, known = hold((made, norm_gain, known))
     sums = add_halves(made)
-    waiting = start_chunks(gain, chunks[1:])
-    sums, waiting, gain, span_offset, live_blocks = hold((sums, waiting, gain, span_offset, live_blocks))
-
-    arrivals = [cross(sums)] + [cross(add_halves(made)) for made in waiting]
-    own, squares = product(gain, 0, chunks, with_squares=True)
-    squares = [squares] + [
-        lax.ppermute(squares, "tensor", [(i, (i + step) % tensor_count) for i in range(tensor_count)])
-        for step in range(1, tensor_count)
-    ]
+    waiting = []
+    for step, squares in zip(others, known):
+        halves, squares = product(gain, step, chunks[1:], with_squares=True, carrier=0, known=squares)
+        waiting.append(halves)
+    waiting = [list(parts) for parts in zip(*waiting)]
+    sums, waiting, squares, gain, span_offset, live_blocks = hold(
+        (sums, waiting, squares, gain, span_offset, live_blocks)
+    )
+
+    carrying, pair_squares = add_carriers(waiting[0], squares)
+    arrivals = [cross(sums), cross(carrying)] + [cross(add_halves(made)) for made in waiting[1:]]
+    own, _ = product(gain, 0, chunks)
     table = tables(span_offset)
+    squares = [pair_squares] + arrivals[1]
 
     result = None
     for (first, count), (keep, send), arrived in zip(chunks, own, arrivals):

time: 49.8 us -> 48.1 us (0.966)
  waiting for transfers between devices: 25.1 us -> 23.8 us
  starting transfers between devices: 8.82 us -> 7.82 us
  local copies, waits for them, and re-layouts: 0.04 us -> 0.73 us
    ppermute x3 -> x1, waiting for transfers between devices: 5.78 us -> 0.01 us  [add_carriers(): lax.ppermute(send, 'tensor', swap)]
    ppermute x3, waiting for transfers between devices: 19.4 us -> 23.8 us  [cross(): lax.ppermute(part, 'tensor', shift(step))]
    ppermute x3 -> x1, starting transfers between devices: 1.85 us -> 0.15 us  [add_carriers(): lax.ppermute(send, 'tensor', swap)]
    ppermute x3, starting transfers between devices: 4.66 us -> 6.07 us  [cross(): lax.ppermute(part, 'tensor', shift(step))]
    unnamed x14 -> x16, local copies, waits for them, and re-layouts: 0.04 us -> 0.73 us
    ppermute x3, starting transfers between devices: 1.21 us -> 0.65 us  [shards(): received = lax.ppermute(send, 'tensor', swap)]
    ppermute x3 -> x2, starting transfers between devices: 1.1 us -> 0.94 us  [add_halves(): lax.ppermute(send, 'tensor', swap)]
    pallas_call x3 -> x4, Pallas kernels: 4.18 us -> 4.34 us  [the longest x3 4.2 us: finish(): pl.pallas_call(functools.partial(finish_kernel, first, count, chip_count,...]
  transfers between devices with their start and end apart: 12 -> 9, of which waited for: 4 -> 3; matrix products, arithmetic and copies ran while one was open for 0% -> 0% of each run, Pallas kernels for 20% -> 20%
where the time goes in v11:
time: 48.1 us; the launch traced here: 47.9 us
  waiting for transfers between devices  23.8 us (49%)
  Pallas kernels  15.4 us (32%)
  starting transfers between devices  7.82 us (16%)
  local copies, waits for them, and re-layouts  0.73 us (2%)
    ppermute x3, waiting for transfers between devices, cross(): lax.ppermute(part, 'tensor', shift(step))  23.8 us
    pallas_call x3, Pallas kernels, product(): pl.pallas_call(functools.partial(product_kernel, step, chip_count, chunks...  10.1 us
    ppermute x3, starting transfers between devices, cross(): lax.ppermute(part, 'tensor', shift(step))  6.07 us
    pallas_call x3, Pallas kernels, finish(): pl.pallas_call(functools.partial(finish_kernel, first, count, chip_count,...  4.2 us
  transfers between devices with their start and end apart: 9, of which 3 were waited for; matrix products, arithmetic and copies ran while one was open for 0% of the time, Pallas kernels for 20%

profile of v11, /device:TPU:0, one launch (start us, length us, event | category | flops | bytes accessed | tf_op | source)
XLA Modules:
  0.0 47.9 jit_solution(6516381032307469728)
XLA Ops:
  0.0 0.0 copy-start.3
  0.0 0.0 copy-start
  0.0 0.0 copy-start.1
  0.0 4.1 %shard_map.64 = (bf16[512,512]{1,0:T(8,128)(2,1)}, bf16[512,512]{1,0:T(8,128)(2,1)}, f32[12,128]{1,0:T(8,128)}) custom-call(bf16[1536,1024]{1,0:T(8,128)(2,1)} %tokens.5, bf16[1024]{0:T(1024)(128)(2,1)} %gain.3, bf16[1024,2048]{1,0:T(8,128)(2,1)} %weight.5), custom_call_target="tpu_custom_call" | custom-call | flops 1 | bytes 1 | tf_op jit(solution)/shard_map/pallas_call | solution.py:242
  4.1 0.0 copy-start.2
  4.1 0.5 %collective-permute-start = (bf16[512,512]{1,0:T(8,128)(2,1)}, bf16[512,512]{1,0:T(8,128)(2,1)S(1)}, u32[]{:S(2)}, u32[]{:S(2)}) collective-permute-start(bf16[512,512]{1,0:T(8,128)(2,1)} %get-tuple-element.43), channel_id=1, source_target_pairs={{0,1},{1,0},{2,3},{3,2},{4,5},{5,4},{6,7},{7,6},{8,9},{9,8},{10,11... | collective-permute-start | bytes 1572872 | tf_op jit(solution)/shard_map/ppermute | solution.py:300
  4.7 0.0 copy-done.3
  4.7 0.0 copy-done
  4.7 0.0 copy-done.1
  4.7 0.0 copy-start.4
  4.7 0.7 %copy-done.4 = f32[12,128]{1,0:T(8,128)S(1)} copy-done((f32[12,128]{1,0:T(8,128)S(1)}, f32[12,128]{1,0:T(8,128)}, u32[]{:S(2)}) %copy-start.4) | copy-done | bytes 6168
  5.4 2.5 %shard_map.66 = (bf16[512,512]{1,0:T(8,128)(2,1)S(1)}, bf16[528,512]{1,0:T(8,128)(2,1)S(1)}, bf16[512,512]{1,0:T(8,128)(2,1)S(1)}, bf16[512,512]{1,0:T(8,128)(2,1)S(1)}, f32[12,128]{1,0:T(8,128)S(1)}) custom-call(bf16[1536,1024]{1,0:T(8,128)(2,1)S(1)} %copy-done.1, bf16[1024]{0:T(1024)(128)(2,1)S(1)} %copy-done.3, bf16[1024,2048]{1,0:T(8,128)(2,1)S(1)} %copy-done, ...), custom_call_target="tpu_custom_call" | custom-call | flops 1 | bytes 1 | tf_op jit(solution)/shard_map/pallas_call | solution.py:242
  7.9 0.0 collective-permute-done.received
  7.9 0.0 copy-done.2
  7.9 0.1 shard_map.65
  8.1 0.2 collective-permute-start.2
  8.2 0.4 collective-permute-start.4
  8.6 2.6 %collective-permute-start.8 = (bf16[512,512]{1,0:T(8,128)(2,1)S(1)}, bf16[512,512]{1,0:T(8,128)(2,1)S(1)}, u32[]{:S(2)}, u32[]{:S(2)}) collective-permute-start(bf16[512,512]{1,0:T(8,128)(2,1)S(1)} %shard_map.65), channel_id=1, source_target_pairs={{0,2},{1,3},{2,0},{3,1},{4,6},{5,7},{6,4},{7,5},{8,10},{9,11},{10,... | collective-permute-start | bytes 1572872 | tf_op jit(solution)/shard_map/ppermute | solution.py:320
  11.2 0.0 collective-permute-done.2.received
  11.2 0.1 shard_map.69
  11.3 1.6 %collective-permute-start.3 = (bf16[528,512]{1,0:T(8,128)(2,1)S(1)}, bf16[528,512]{1,0:T(8,128)(2,1)S(1)}, u32[]{:S(2)}, u32[]{:S(2)}) collective-permute-start(bf16[528,512]{1,0:T(8,128)(2,1)S(1)} %get-tuple-element.65), channel_id=1, source_target_pairs={{0,2},{1,3},{2,0},{3,1},{4,6},{5,7},{6,4},{7,5},{8,10},{9,11},{10,... | collective-permute-start | bytes 1622024 | tf_op jit(solution)/shard_map/ppermute | solution.py:320
  12.9 3.5 %shard_map.67 = (bf16[512,512]{1,0:T(8,128)(2,1)S(1)}, bf16[512,512]{1,0:T(8,128)(2,1)S(1)}, bf16[512,512]{1,0:T(8,128)(2,1)S(1)}, bf16[512,512]{1,0:T(8,128)(2,...) custom-call(bf16[1536,1024]{1,0:T(8,128)(2,1)S(1)} %copy-done.1, bf16[1024]{0:T(1024)(128)(2,1)S(1)} %copy-done.3, ...), custom_call_target="tpu_custom_call" | custom-call | flops 1 | bytes 1 | tf_op jit(solution)/shard_map/pallas_call | solution.py:242
  16.4 0.0 copy-start.5
  16.4 0.0 copy-start.6
  16.4 0.0 copy-start.7
  16.4 0.1 collective-permute-start.7
  16.5 0.4 collective-permute-start.1
  17.0 0.0 collective-permute-done.4.received
  17.0 0.1 collective-permute-start.6
  17.1 0.1 shard_map.70
  17.2 6.8 %collective-permute-done.8.refs_9_ = bf16[512,512]{1,0:T(8,128)(2,1)S(1)} collective-permute-done((bf16[512,512]{1,0:T(8,128)(2,1)S(1)}, bf16[512,512]{1,0:T(8,128)(2,1)S(1)}, u32[]{:S(2)}, u32[]{:S(2)}) %collective-permute-start.8) | collective-permute-done | bytes 524320 | tf_op jit(solution)/shard_map/ppermute | solution.py:320
  24.0 1.9 %collective-permute-start.5 = (bf16[512,512]{1,0:T(8,128)(2,1)S(1)}, bf16[512,512]{1,0:T(8,128)(2,1)S(1)}, u32[]{:S(2)}, u32[]{:S(2)}) collective-permute-start(bf16[512,512]{1,0:T(8,128)(2,1)S(1)} %shard_map.70), channel_id=1, source_target_pairs={{0,2},{1,3},{2,0},{3,1},{4,6},{5,7},{6,4},{7,5},{8,10},{9,11},{10,... | collective-permute-start | bytes 1572872 | tf_op jit(solution)/shard_map/ppermute | solution.py:320
  25.9 0.0 copy-done.5
  25.9 0.0 copy-done.6
  25.9 0.0 copy-done.7
  25.9 0.7 %shard_map.68 = (s32[8,128]{1,0:T(8,128)S(1)}, f32[24,128]{1,0:T(8,128)S(1)}, f32[24,128]{1,0:T(8,128)S(1)}, f32[64,128]{1,0:T(8,128)S(1)}, f32[64,128]{1,0:T(8,128)S(1)}) custom-call(s32[4]{0:T(128)S(1)} %copy-done.5, s32[4]{0:T(128)S(1)} %copy-done.6, f32[1,128]{1,0:T(1,128)S(1)} %copy-done.7), custom_call_target="tpu_custom_call" | custom-call | flops 1 | bytes 1 | tf_op jit(solution)/shard_map/pallas_call | solution.py:259
  26.7 0.0 collective-permute-done.7.refs_1_
  26.7 8.9 %collective-permute-done.3.refs_8_.refs_9_ = bf16[528,512]{1,0:T(8,128)(2,1)S(1)} collective-permute-done((bf16[528,512]{1,0:T(8,128)(2,1)S(1)}, bf16[528,512]{1,0:T(8,128)(2,1)S(1)}, u32[]{:S(2)}, u32[]{:S(2)}) %collective-permute-start.3) | collective-permute-done | bytes 540704 | tf_op jit(solution)/shard_map/ppermute | solution.py:320
  35.6 1.4 %shard_map.71.refs_10_ = bf16[1536,512]{1,0:T(8,128)(2,1)} custom-call(bf16[512,512]{1,0:T(8,128)(2,1)S(1)} %get-tuple-element.70.refs_0_, bf16[512,512]{1,0:T(8,128)(2,1)S(1)} %collective-permute-done.7.refs_1_, s32[8,128]{1,0:T(8,128)S(1)} %get-tuple-element.56.refs_2_, f32[24,128]{1,0:T(8,128)S(1)} %get-tuple-element.57.refs_3_, ...), custom_call_target="tpu_custom_call" | custom-call | flops 1 | bytes 1 | tf_op jit(solution)/shard_map/pallas_call | solution.py:276
  37.0 0.0 collective-permute-done.6.refs_1_
  37.0 1.4 %shard_map.72.refs_10_ = bf16[1536,512]{1,0:T(8,128)(2,1)} custom-call(bf16[512,512]{1,0:T(8,128)(2,1)S(1)} %get-tuple-element.68.refs_0_, bf16[512,512]{1,0:T(8,128)(2,1)S(1)} %collective-permute-done.6.refs_1_, s32[8,128]{1,0:T(8,128)S(1)} %get-tuple-element.56.refs_2_, f32[24,128]{1,0:T(8,128)S(1)} %get-tuple-element.57.refs_3_, ...), custom_call_target="tpu_custom_call", output_to_operand_aliasing={{}: (10, {})} | custom-call | flops 1 | bytes 1 | tf_op jit(solution)/shard_map/pallas_call | solution.py:276
  38.4 0.0 collective-permute-done.1.refs_1_
  38.4 8.1 %collective-permute-done.5.refs_9_ = bf16[512,512]{1,0:T(8,128)(2,1)S(1)} collective-permute-done((bf16[512,512]{1,0:T(8,128)(2,1)S(1)}, bf16[512,512]{1,0:T(8,128)(2,1)S(1)}, u32[]{:S(2)}, u32[]{:S(2)}) %collective-permute-start.5) | collective-permute-done | bytes 524320 | tf_op jit(solution)/shard_map/ppermute | solution.py:320
  46.5 1.4 %shard_map.73 = bf16[1536,512]{1,0:T(8,128)(2,1)} custom-call(bf16[512,512]{1,0:T(8,128)(2,1)S(1)} %get-tuple-element.52.refs_0_, bf16[512,512]{1,0:T(8,128)(2,1)S(1)} %collective-permute-done.1.refs_1_, s32[8,128]{1,0:T(8,128)S(1)} %get-tuple-element.56.refs_2_, f32[24,128]{1,0:T(8,128)S(1)} %get-tuple-element.57.refs_3_, ...), custom_call_target="tpu_custom_call", output_to_operand_aliasing={{}: (10, {})} | custom-call | flops 1 | bytes 1 | tf_op jit(solution)/shard_map/pallas_call | solution.py:276
Async XLA Ops:
  0.0 4.7 %copy-start.3 = (bf16[1024]{0:T(1024)(128)(2,1)S(1)}, bf16[1024]{0:T(1024)(128)(2,1)}, u32[]{:S(2)}) copy-start(bf16[1024]{0:T(1024)(128)(2,1)} %gain.3) | copy-start | bytes 6148
  0.0 4.7 %copy-start = (bf16[1024,2048]{1,0:T(8,128)(2,1)S(1)}, bf16[1024,2048]{1,0:T(8,128)(2,1)}, u32[]{:S(2)}) copy-start(bf16[1024,2048]{1,0:T(8,128)(2,1)} %weight.5) | copy-start | bytes 12582916
  0.0 4.7 %copy-start.1 = (bf16[1536,1024]{1,0:T(8,128)(2,1)S(1)}, bf16[1536,1024]{1,0:T(8,128)(2,1)}, u32[]{:S(2)}) copy-start(bf16[1536,1024]{1,0:T(8,128)(2,1)} %tokens.5) | copy-start | bytes 9437188
  4.1 3.8 %copy-start.2 = (bf16[512,512]{1,0:T(8,128)(2,1)S(1)}, bf16[512,512]{1,0:T(8,128)(2,1)}, u32[]{:S(2)}) copy-start(bf16[512,512]{1,0:T(8,128)(2,1)} %get-tuple-element.42.keep) | copy-start | bytes 1572868
  4.1 3.8 %collective-permute-start = (bf16[512,512]{1,0:T(8,128)(2,1)}, bf16[512,512]{1,0:T(8,128)(2,1)S(1)}, u32[]{:S(2)}, u32[]{:S(2)}) collective-permute-start(bf16[512,512]{1,0:T(8,128)(2,1)} %get-tuple-element.43), channel_id=1, source_target_pairs={{0,1},{1,0},{2,3},{3,2},{4,5},{5,4},{6,7},{7,6},{8,9},{9,8},{10,11... | collective-permute-start | bytes 1572872 | tf_op jit(solution)/shard_map/ppermute | solution.py:300
  4.7 0.7 %copy-start.4 = (f32[12,128]{1,0:T(8,128)S(1)}, f32[12,128]{1,0:T(8,128)}, u32[]{:S(2)}) copy-start(f32[12,128]{1,0:T(8,128)} %get-tuple-element.45.refs_0_) | copy-start | bytes 18436
  8.1 3.1 %collective-permute-start.2 = (bf16[528,512]{1,0:T(8,128)(2,1)S(1)}, bf16[528,512]{1,0:T(8,128)(2,1)S(1)}, u32[]{:S(2)}, u32[]{:S(2)}) collective-permute-start(bf16[528,512]{1,0:T(8,128)(2,1)S(1)} %get-tuple-element.62), channel_id=1, source_target_pairs={{0,1},{1,0},{2,3},{3,2},{4,5},{5,4},{6,7},{7,6},{8,9},{9,8},{10,11... | collective-permute-start | bytes 1622024 | tf_op jit(solution)/shard_map/ppermute | solution.py:314
  8.2 8.8 %collective-permute-start.4 = (bf16[512,512]{1,0:T(8,128)(2,1)S(1)}, bf16[512,512]{1,0:T(8,128)(2,1)S(1)}, u32[]{:S(2)}, u32[]{:S(2)}) collective-permute-start(bf16[512,512]{1,0:T(8,128)(2,1)S(1)} %get-tuple-element.67), channel_id=1, source_target_pairs={{0,1},{1,0},{2,3},{3,2},{4,5},{5,4},{6,7},{7,6},{8,9},{9,8},{10,11... | collective-permute-start | bytes 1572872 | tf_op jit(solution)/shard_map/ppermute | solution.py:300
  8.6 15.3 %collective-permute-start.8 = (bf16[512,512]{1,0:T(8,128)(2,1)S(1)}, bf16[512,512]{1,0:T(8,128)(2,1)S(1)}, u32[]{:S(2)}, u32[]{:S(2)}) collective-permute-start(bf16[512,512]{1,0:T(8,128)(2,1)S(1)} %shard_map.65), channel_id=1, source_target_pairs={{0,2},{1,3},{2,0},{3,1},{4,6},{5,7},{6,4},{7,5},{8,10},{9,11},{10,... | collective-permute-start | bytes 1572872 | tf_op jit(solution)/shard_map/ppermute | solution.py:320
  11.3 24.2 %collective-permute-start.3 = (bf16[528,512]{1,0:T(8,128)(2,1)S(1)}, bf16[528,512]{1,0:T(8,128)(2,1)S(1)}, u32[]{:S(2)}, u32[]{:S(2)}) collective-permute-start(bf16[528,512]{1,0:T(8,128)(2,1)S(1)} %get-tuple-element.65), channel_id=1, source_target_pairs={{0,2},{1,3},{2,0},{3,1},{4,6},{5,7},{6,4},{7,5},{8,10},{9,11},{10,... | collective-permute-start | bytes 1622024 | tf_op jit(solution)/shard_map/ppermute | solution.py:320
  16.4 9.6 %copy-start.5 = (s32[4]{0:T(128)S(1)}, s32[4]{0:T(128)}, u32[]{:S(2)}) copy-start(s32[4]{0:T(128)} %live) | copy-start | bytes 52
  16.4 9.6 %copy-start.6 = (s32[4]{0:T(128)S(1)}, s32[4]{0:T(128)}, u32[]{:S(2)}) copy-start(s32[4]{0:T(128)} %span) | copy-start | bytes 52
  16.4 9.5 %copy-start.7 = (f32[1,128]{1,0:T(1,128)S(1)}, f32[1,128]{1,0:T(1,128)}, u32[]{:S(2)}) copy-start(f32[1,128]{1,0:T(1,128)} %constant.4.clone.frequencies) | copy-start | bytes 1540
  16.4 10.3 %collective-permute-start.7 = (bf16[512,512]{1,0:T(8,128)(2,1)S(1)}, bf16[512,512]{1,0:T(8,128)(2,1)S(1)}, u32[]{:S(2)}, u32[]{:S(2)}) collective-permute-start(bf16[512,512]{1,0:T(8,128)(2,1)S(1)} %get-tuple-element.71), channel_id=1, source_target_pairs={{0,1},{1,0},{2,3},{3,2},{4,5},{5,4},{6,7},{7,6},{8,9},{9,8},{10,11... | collective-permute-start | bytes 1572872 | tf_op jit(solution)/shard_map/ppermute | solution.py:347
  16.5 21.9 %collective-permute-start.1 = (bf16[512,512]{1,0:T(8,128)(2,1)S(1)}, bf16[512,512]{1,0:T(8,128)(2,1)S(1)}, u32[]{:S(2)}, u32[]{:S(2)}) collective-permute-start(bf16[512,512]{1,0:T(8,128)(2,1)S(1)} %get-tuple-element.53), channel_id=1, source_target_pairs={{0,1},{1,0},{2,3},{3,2},{4,5},{5,4},{6,7},{7,6},{8,9},{9,8},{10,11... | collective-permute-start | bytes 1572872 | tf_op jit(solution)/shard_map/ppermute | solution.py:347
  17.0 20.0 %collective-permute-start.6 = (bf16[512,512]{1,0:T(8,128)(2,1)S(1)}, bf16[512,512]{1,0:T(8,128)(2,1)S(1)}, u32[]{:S(2)}, u32[]{:S(2)}) collective-permute-start(bf16[512,512]{1,0:T(8,128)(2,1)S(1)} %get-tuple-element.69), channel_id=1, source_target_pairs={{0,1},{1,0},{2,3},{3,2},{4,5},{5,4},{6,7},{7,6},{8,9},{9,8},{10,11... | collective-permute-start | bytes 1572872 | tf_op jit(solution)/shard_map/ppermute | solution.py:347
  24.0 22.6 %collective-permute-start.5 = (bf16[512,512]{1,0:T(8,128)(2,1)S(1)}, bf16[512,512]{1,0:T(8,128)(2,1)S(1)}, u32[]{:S(2)}, u32[]{:S(2)}) collective-permute-start(bf16[512,512]{1,0:T(8,128)(2,1)S(1)} %shard_map.70), channel_id=1, source_target_pairs={{0,2},{1,3},{2,0},{3,1},{4,6},{5,7},{6,4},{7,5},{8,10},{9,11},{10,... | collective-permute-start | bytes 1572872 | tf_op jit(solution)/shard_map/ppermute | solution.py:320

commit v12 on v11

--- a/solution.py
+++ b/solution.py
@@ -18,6 +18,8 @@
 norm_eps = 1e-05
 
 TILE = 256
+CUTS = 4
+SPLIT = 4
 CHUNKS = (2, 2, 2)
 
 PARAMS = pltpu.CompilerParams(vmem_limit_bytes=16 * 1024 * 1024)
@@ -54,11 +56,10 @@
     return part[index : index + 1] + part[SUBLANES + index : SUBLANES + index + 1]
 
 
-def product_kernel(step, chip_count, chunks, carrier, staged, with_squares, tokens, gain, weight, *refs):
+def product_kernel(step, chip_count, chunks, carrier, staged, tokens, gain, weight, *refs):
     refs = list(refs)
-    known = refs.pop(0) if carrier is not None else None
     outs = [refs.pop(0) for _ in range(2 * len(chunks))]
-    squares = refs.pop(0) if with_squares else None
+    squares = refs.pop(0) if carrier is not None else None
     depth, width = tokens.shape[1], 2 * outs[0].shape[1]
     me = lax.axis_index("tensor")
     core = lax.rem(me, 2)
@@ -68,48 +69,45 @@
     weight_copies, row_copies = [], {}
     if staged:
         rows_buf, weight_buf, gain_buf, weight_sems, row_sems, gain_sem = refs
-        cuts = weight_sems.shape[0]
-        cut = depth // cuts
+        cut, piece = depth // CUTS, depth // CUTS // SPLIT
         gain_copy = pltpu.make_async_copy(gain, gain_buf, gain_sem)
-        weight_copies = [
-            pltpu.make_async_copy(
-                weight.at[pl.ds(index * cut, cut), place],
-                weight_buf.at[pl.ds(index * cut, cut), :],
-                weight_sems.at[index],
+        for index in range(CUTS * SPLIT):
+            some = pl.ds(index * piece, piece)
+            weight_copies.append(
+                pltpu.make_async_copy(weight.at[some, place], weight_buf.at[some, :], weight_sems.at[index])
             )
-            for index in range(cuts)
-        ]
-        at = 0
+        at, size = 0, TILE // SPLIT
         for first, count in chunks:
             for tile in range(first, first + count):
-                buf = rows_buf.at[pl.ds(at * TILE, TILE), :]
-                row_copies[tile] = (
-                    pltpu.make_async_copy(tokens.at[pl.ds(tile * TILE, TILE), :], buf, row_sems.at[at]),
-                    buf,
-                )
+                copies = []
+                for part in range(SPLIT):
+                    some = pl.ds(at * TILE + part * size, size)
+                    rows = tokens.at[pl.ds(tile * TILE + part * size, size), :]
+                    copies.append(pltpu.make_async_copy(rows, rows_buf.at[some, :], row_sems.at[at * SPLIT + part]))
+                row_copies[tile] = copies, rows_buf.at[pl.ds(at * TILE, TILE), :]
                 at += 1
-        in_order = [copy for copy, _ in row_copies.values()]
-        for copy in [gain_copy] + in_order[:1] + weight_copies + in_order[1:]:
+        in_order = [copies for copies, _ in row_copies.values()]
+        for copy in [gain_copy] + in_order[0] + weight_copies + sum(in_order[1:], []):
             copy.start()
         gain_copy.wait()
         gains = gain_buf[...].reshape(1, depth)
     else:
         gains = gain[...].reshape(1, depth)
 
-    if carrier is not None:
-        squares[...] = known[...]
     for index, (first, count) in enumerate(chunks):
         for tile in range(first, first + count):
             if staged:
-                row_copies[tile][0].wait()
+                for copy in row_copies[tile][0]:
+                    copy.wait()
                 rows = row_copies[tile][1][...]
             else:
                 rows = tokens[pl.ds(tile * TILE, TILE), :]
             scaled = rows * gains
             if weight_copies:
                 product = jnp.zeros((TILE, width), jnp.float32)
-                for part, copy in enumerate(weight_copies):
-                    copy.wait()
+                for part in range(CUTS):
+                    for copy in weight_copies[part * SPLIT : (part + 1) * SPLIT]:
+                        copy.wait()
                     span = slice(part * cut, (part + 1) * cut)
                     product += jnp.dot(
                         scaled[:, span], weight_buf[span, :], preferred_element_type=jnp.float32
@@ -123,13 +121,10 @@
             inside = pl.ds((tile - first) * TILE, TILE)
             outs[2 * index][inside, :] = jnp.where(core == 0, left, right)
             outs[2 * index + 1][inside, :] = jnp.where(core == 0, right, left)
-            if with_squares:
-                total = square_sums(rows)
-                for part in range(TILE // LANES):
-                    turned = jnp.transpose(total[part * LANES : (part + 1) * LANES])
-                    row = tile * (TILE // LANES) + part
-                    squares[row : row + 1, :] = jnp.sum(turned, axis=0, keepdims=True)
     if carrier is not None:
+        for line in range(squares.shape[0]):
+            total = square_sums(tokens[pl.ds(line * LANES, LANES), :])
+            squares[line : line + 1, :] = jnp.sum(jnp.transpose(total), axis=0, keepdims=True)
         lines = [squares[line : line + 1, :] for line in range(squares.shape[0])]
         out = outs[2 * carrier + 1]
         out[pl.ds(out.shape[0] - 2 * SUBLANES, 2 * SUBLANES), :] = packed(lines, out.shape[1])
@@ -220,7 +215,7 @@
     def shift(step):
         return [(i, (i + 2 * step) % tensor_count) for i in range(tensor_count)]
 
-    def product(gain, step, chunks, staged=False, with_squares=False, carrier=None, known=None):
+    def product(gain, step, chunks, staged=False, carrier=None):
         vmem = pl.BlockSpec(memory_space=pltpu.VMEM)
         out_shape = [
             jax.ShapeDtypeStruct((count * TILE, columns), jnp.bfloat16) for _, count in chunks for _ in range(2)
@@ -228,28 +223,27 @@
         if carrier is not None:
             size = out_shape[2 * carrier].shape[0] + 2 * SUBLANES
             out_shape[2 * carrier + 1] = jax.ShapeDtypeStruct((size, columns), jnp.bfloat16)
-        if with_squares:
             out_shape.append(jax.ShapeDtypeStruct((slot_rows // LANES, LANES), jnp.float32))
         count = sum(count for _, count in chunks)
         scratch = [
             pltpu.VMEM((count * TILE, depth), jnp.bfloat16),
             pltpu.VMEM((depth, 2 * columns), jnp.bfloat16),
             pltpu.VMEM((depth,), jnp.bfloat16),
-            pltpu.SemaphoreType.DMA((4,)),
-            pltpu.SemaphoreType.DMA((count,)),
+            pltpu.SemaphoreType.DMA((CUTS * SPLIT,)),
+            pltpu.SemaphoreType.DMA((count * SPLIT,)),
             pltpu.SemaphoreType.DMA,
         ]
         made = pl.pallas_call(
-            functools.partial(product_kernel, step, chip_count, chunks, carrier, staged, with_squares),
-            in_specs=[pl.BlockSpec(memory_space=pltpu.HBM) if staged else vmem] * 3 + [vmem] * (known is not None),
+            functools.partial(product_kernel, step, chip_count, chunks, carrier, staged),
+            in_specs=[pl.BlockSpec(memory_space=pltpu.HBM) if staged else vmem] * 3,
             out_shape=out_shape,
             out_specs=[vmem] * len(out_shape),
             scratch_shapes=scratch if staged else [],
             compiler_params=FIRST if staged else PARAMS,
             cost_estimate=COST,
-        )(tokens, gain, kv_weight, *([] if known is None else [known]))
+        )(tokens, gain, kv_weight)
         made = list(made)
-        squares = made.pop() if with_squares else None
+        squares = made.pop() if carrier is not None else None
         return list(zip(made[::2], made[1::2])), squares
 
     def tables(span_offset):
@@ -320,16 +314,12 @@
         return [lax.ppermute(part, "tensor", shift(step)) for step, part in zip(others, sums)]
 
     hold = lax.optimization_barrier
-    made, known = [], []
-    for step in others:
-        halves, squares = product(norm_gain, step, chunks[:1], staged=True, with_squares=True)
-        made += halves
-        known.append(squares)
-    made, gain, known = hold((made, norm_gain, known))
+    made = [product(norm_gain, step, chunks[:1], staged=True)[0][0] for step in others]
+    made, gain = hold((made, norm_gain))
     sums = add_halves(made)
     waiting = []
-    for step, squares in zip(others, known):
-        halves, squares = product(gain, step, chunks[1:], with_squares=True, carrier=0, known=squares)
+    for step in others:
+        halves, squares = product(gain, step, chunks[1:], carrier=0)
         waiting.append(halves)
     waiting = [list(parts) for parts in zip(*waiting)]
     sums, waiting, squares, gain, span_offset, live_blocks = hold(

time: 48.1 us -> 48.2 us (level)
  Pallas kernels: 15.4 us -> 16.2 us
  local copies, waits for them, and re-layouts: 0.73 us -> 0.04 us
    pallas_call x3, Pallas kernels: 10.1 us -> 10.9 us  [product(): pl.pallas_call(functools.partial(product_kernel, step, chip_count, chunks...]
    unnamed x16 -> x14, local copies, waits for them, and re-layouts: 0.73 us -> 0.04 us
  transfers between devices with their start and end apart: 9 -> 9, of which waited for: 3 -> 3; matrix products, arithmetic and copies ran while one was open for 0% -> 0% of each run, Pallas kernels for 20% -> 21%
where the time goes in v12:
time: 48.2 us; the launch traced here: 48 us
  waiting for transfers between devices  23.8 us (49%)
  Pallas kernels  16.2 us (34%)
  starting transfers between devices  7.84 us (16%)
    ppermute x3, waiting for transfers between devices, cross(): lax.ppermute(part, 'tensor', shift(step))  23.8 us
    pallas_call x3, Pallas kernels, product(): pl.pallas_call(functools.partial(product_kernel, step, chip_count, chunks...  10.9 us
    ppermute x3, starting transfers between devices, cross(): lax.ppermute(part, 'tensor', shift(step))  6.07 us
    pallas_call x3, Pallas kernels, finish(): pl.pallas_call(functools.partial(finish_kernel, first, count, chip_count,...  4.2 us
    ppermute x2, starting transfers between devices, add_halves(): lax.ppermute(send, 'tensor', swap)  1.01 us
  transfers between devices with their start and end apart: 9, of which 3 were waited for; matrix products, arithmetic and copies ran while one was open for 0% of the time, Pallas kernels for 21%

profile of v12, /device:TPU:0, one launch (start us, length us, event | category | flops | bytes accessed | tf_op | source)
XLA Modules:
  0.0 48.0 jit_solution(9947832983373929118)
XLA Ops:
  0.0 0.0 copy-start.3
  0.0 0.0 copy-start
  0.0 0.0 copy-start.1
  0.0 4.6 %shard_map.64 = (bf16[512,512]{1,0:T(8,128)(2,1)}, bf16[512,512]{1,0:T(8,128)(2,1)}) custom-call(bf16[1536,1024]{1,0:T(8,128)(2,1)} %tokens.5, bf16[1024]{0:T(1024)(128)(2,1)} %gain.3, bf16[1024,2048]{1,0:T(8,128)(2,1)} %weight.5), custom_call_target="tpu_custom_call" | custom-call | flops 1 | bytes 1 | tf_op jit(solution)/shard_map/pallas_call | solution.py:236
  4.6 0.0 copy-start.2
  4.6 0.5 %collective-permute-start = (bf16[512,512]{1,0:T(8,128)(2,1)}, bf16[512,512]{1,0:T(8,128)(2,1)S(1)}, u32[]{:S(2)}, u32[]{:S(2)}) collective-permute-start(bf16[512,512]{1,0:T(8,128)(2,1)} %get-tuple-element.40), channel_id=1, source_target_pairs={{0,1},{1,0},{2,3},{3,2},{4,5},{5,4},{6,7},{7,6},{8,9},{9,8},{10,11... | collective-permute-start | bytes 1572872 | tf_op jit(solution)/shard_map/ppermute | solution.py:294
  5.2 0.0 copy-done.3
  5.2 0.0 copy-done
  5.2 0.0 copy-done.1
  5.2 2.8 %shard_map.66 = (bf16[512,512]{1,0:T(8,128)(2,1)S(1)}, bf16[528,512]{1,0:T(8,128)(2,1)S(1)}, bf16[512,512]{1,0:T(8,128)(2,1)S(1)}, bf16[512,512]{1,0:T(8,128)(2,1)S(1)}, f32[12,128]{1,0:T(8,128)S(1)}) custom-call(bf16[1536,1024]{1,0:T(8,128)(2,1)S(1)} %copy-done.1, bf16[1024]{0:T(1024)(128)(2,1)S(1)} %copy-done.3, bf16[1024,2048]{1,0:T(8,128)(2,1)S(1)} %copy-done), custom_call_target="tpu_custom_call" | custom-call | flops 1 | bytes 1 | tf_op jit(solution)/shard_map/pallas_call | solution.py:236
  8.0 0.0 collective-permute-done.received
  8.0 0.0 copy-done.2
  8.0 0.1 shard_map.65
  8.1 0.1 collective-permute-start.2
  8.2 0.5 collective-permute-start.4
  8.7 2.6 %collective-permute-start.8 = (bf16[512,512]{1,0:T(8,128)(2,1)S(1)}, bf16[512,512]{1,0:T(8,128)(2,1)S(1)}, u32[]{:S(2)}, u32[]{:S(2)}) collective-permute-start(bf16[512,512]{1,0:T(8,128)(2,1)S(1)} %shard_map.65), channel_id=1, source_target_pairs={{0,2},{1,3},{2,0},{3,1},{4,6},{5,7},{6,4},{7,5},{8,10},{9,11},{10,... | collective-permute-start | bytes 1572872 | tf_op jit(solution)/shard_map/ppermute | solution.py:314
  11.3 0.0 collective-permute-done.2.received
  11.3 0.1 shard_map.69
  11.4 1.6 %collective-permute-start.3 = (bf16[528,512]{1,0:T(8,128)(2,1)S(1)}, bf16[528,512]{1,0:T(8,128)(2,1)S(1)}, u32[]{:S(2)}, u32[]{:S(2)}) collective-permute-start(bf16[528,512]{1,0:T(8,128)(2,1)S(1)} %get-tuple-element.61), channel_id=1, source_target_pairs={{0,2},{1,3},{2,0},{3,1},{4,6},{5,7},{6,4},{7,5},{8,10},{9,11},{10,... | collective-permute-start | bytes 1622024 | tf_op jit(solution)/shard_map/ppermute | solution.py:314
  13.0 3.5 %shard_map.67 = (bf16[512,512]{1,0:T(8,128)(2,1)S(1)}, bf16[512,512]{1,0:T(8,128)(2,1)S(1)}, bf16[512,512]{1,0:T(8,128)(2,1)S(1)}, bf16[512,512]{1,0:T(8,128)(2,...) custom-call(bf16[1536,1024]{1,0:T(8,128)(2,1)S(1)} %copy-done.1, bf16[1024]{0:T(1024)(128)(2,1)S(1)} %copy-done.3, ...), custom_call_target="tpu_custom_call" | custom-call | flops 1 | bytes 1 | tf_op jit(solution)/shard_map/pallas_call | solution.py:236
  16.4 0.0 copy-start.4
  16.5 0.0 copy-start.5
  16.5 0.0 copy-start.6
  16.5 0.1 collective-permute-start.7
  16.6 0.4 collective-permute-start.1
  17.1 0.0 collective-permute-done.4.received
  17.1 0.1 collective-permute-start.6
  17.1 0.1 shard_map.70
  17.3 6.8 %collective-permute-done.8.refs_9_ = bf16[512,512]{1,0:T(8,128)(2,1)S(1)} collective-permute-done((bf16[512,512]{1,0:T(8,128)(2,1)S(1)}, bf16[512,512]{1,0:T(8,128)(2,1)S(1)}, u32[]{:S(2)}, u32[]{:S(2)}) %collective-permute-start.8) | collective-permute-done | bytes 524320 | tf_op jit(solution)/shard_map/ppermute | solution.py:314
  24.1 1.9 %collective-permute-start.5 = (bf16[512,512]{1,0:T(8,128)(2,1)S(1)}, bf16[512,512]{1,0:T(8,128)(2,1)S(1)}, u32[]{:S(2)}, u32[]{:S(2)}) collective-permute-start(bf16[512,512]{1,0:T(8,128)(2,1)S(1)} %shard_map.70), channel_id=1, source_target_pairs={{0,2},{1,3},{2,0},{3,1},{4,6},{5,7},{6,4},{7,5},{8,10},{9,11},{10,... | collective-permute-start | bytes 1572872 | tf_op jit(solution)/shard_map/ppermute | solution.py:314
  26.0 0.0 copy-done.4
  26.0 0.0 copy-done.5
  26.0 0.0 copy-done.6
  26.0 0.7 %shard_map.68 = (s32[8,128]{1,0:T(8,128)S(1)}, f32[24,128]{1,0:T(8,128)S(1)}, f32[24,128]{1,0:T(8,128)S(1)}, f32[64,128]{1,0:T(8,128)S(1)}, f32[64,128]{1,0:T(8,128)S(1)}) custom-call(s32[4]{0:T(128)S(1)} %copy-done.4, s32[4]{0:T(128)S(1)} %copy-done.5, f32[1,128]{1,0:T(1,128)S(1)} %copy-done.6), custom_call_target="tpu_custom_call" | custom-call | flops 1 | bytes 1 | tf_op jit(solution)/shard_map/pallas_call | solution.py:253
  26.7 0.0 collective-permute-done.7.refs_1_
  26.8 8.9 %collective-permute-done.3.refs_8_.refs_9_ = bf16[528,512]{1,0:T(8,128)(2,1)S(1)} collective-permute-done((bf16[528,512]{1,0:T(8,128)(2,1)S(1)}, bf16[528,512]{1,0:T(8,128)(2,1)S(1)}, u32[]{:S(2)}, u32[]{:S(2)}) %collective-permute-start.3) | collective-permute-done | bytes 540704 | tf_op jit(solution)/shard_map/ppermute | solution.py:314
  35.6 1.4 %shard_map.71.refs_10_ = bf16[1536,512]{1,0:T(8,128)(2,1)} custom-call(bf16[512,512]{1,0:T(8,128)(2,1)S(1)} %get-tuple-element.66.refs_0_, bf16[512,512]{1,0:T(8,128)(2,1)S(1)} %collective-permute-done.7.refs_1_, s32[8,128]{1,0:T(8,128)S(1)} %get-tuple-element.52.refs_2_, f32[24,128]{1,0:T(8,128)S(1)} %get-tuple-element.53.refs_3_, ...), custom_call_target="tpu_custom_call" | custom-call | flops 1 | bytes 1 | tf_op jit(solution)/shard_map/pallas_call | solution.py:270
  37.0 0.0 collective-permute-done.6.refs_1_
  37.1 1.4 %shard_map.72.refs_10_ = bf16[1536,512]{1,0:T(8,128)(2,1)} custom-call(bf16[512,512]{1,0:T(8,128)(2,1)S(1)} %get-tuple-element.64.refs_0_, bf16[512,512]{1,0:T(8,128)(2,1)S(1)} %collective-permute-done.6.refs_1_, s32[8,128]{1,0:T(8,128)S(1)} %get-tuple-element.52.refs_2_, f32[24,128]{1,0:T(8,128)S(1)} %get-tuple-element.53.refs_3_, ...), custom_call_target="tpu_custom_call", output_to_operand_aliasing={{}: (10, {})} | custom-call | flops 1 | bytes 1 | tf_op jit(solution)/shard_map/pallas_call | solution.py:270
  38.5 0.0 collective-permute-done.1.refs_1_
  38.5 8.1 %collective-permute-done.5.refs_9_ = bf16[512,512]{1,0:T(8,128)(2,1)S(1)} collective-permute-done((bf16[512,512]{1,0:T(8,128)(2,1)S(1)}, bf16[512,512]{1,0:T(8,128)(2,1)S(1)}, u32[]{:S(2)}, u32[]{:S(2)}) %collective-permute-start.5) | collective-permute-done | bytes 524320 | tf_op jit(solution)/shard_map/ppermute | solution.py:314
  46.6 1.4 %shard_map.73 = bf16[1536,512]{1,0:T(8,128)(2,1)} custom-call(bf16[512,512]{1,0:T(8,128)(2,1)S(1)} %get-tuple-element.48.refs_0_, bf16[512,512]{1,0:T(8,128)(2,1)S(1)} %collective-permute-done.1.refs_1_, s32[8,128]{1,0:T(8,128)S(1)} %get-tuple-element.52.refs_2_, f32[24,128]{1,0:T(8,128)S(1)} %get-tuple-element.53.refs_3_, ...), custom_call_target="tpu_custom_call", output_to_operand_aliasing={{}: (10, {})} | custom-call | flops 1 | bytes 1 | tf_op jit(solution)/shard_map/pallas_call | solution.py:270
Async XLA Ops:
  0.0 5.2 %copy-start.3 = (bf16[1024]{0:T(1024)(128)(2,1)S(1)}, bf16[1024]{0:T(1024)(128)(2,1)}, u32[]{:S(2)}) copy-start(bf16[1024]{0:T(1024)(128)(2,1)} %gain.3) | copy-start | bytes 6148
  0.0 5.2 %copy-start = (bf16[1024,2048]{1,0:T(8,128)(2,1)S(1)}, bf16[1024,2048]{1,0:T(8,128)(2,1)}, u32[]{:S(2)}) copy-start(bf16[1024,2048]{1,0:T(8,128)(2,1)} %weight.5) | copy-start | bytes 12582916
  0.0 5.2 %copy-start.1 = (bf16[1536,1024]{1,0:T(8,128)(2,1)S(1)}, bf16[1536,1024]{1,0:T(8,128)(2,1)}, u32[]{:S(2)}) copy-start(bf16[1536,1024]{1,0:T(8,128)(2,1)} %tokens.5) | copy-start | bytes 9437188
  4.6 3.4 %copy-start.2 = (bf16[512,512]{1,0:T(8,128)(2,1)S(1)}, bf16[512,512]{1,0:T(8,128)(2,1)}, u32[]{:S(2)}) copy-start(bf16[512,512]{1,0:T(8,128)(2,1)} %get-tuple-element.39.keep) | copy-start | bytes 1572868
  4.6 3.4 %collective-permute-start = (bf16[512,512]{1,0:T(8,128)(2,1)}, bf16[512,512]{1,0:T(8,128)(2,1)S(1)}, u32[]{:S(2)}, u32[]{:S(2)}) collective-permute-start(bf16[512,512]{1,0:T(8,128)(2,1)} %get-tuple-element.40), channel_id=1, source_target_pairs={{0,1},{1,0},{2,3},{3,2},{4,5},{5,4},{6,7},{7,6},{8,9},{9,8},{10,11... | collective-permute-start | bytes 1572872 | tf_op jit(solution)/shard_map/ppermute | solution.py:294
  8.1 3.1 %collective-permute-start.2 = (bf16[528,512]{1,0:T(8,128)(2,1)S(1)}, bf16[528,512]{1,0:T(8,128)(2,1)S(1)}, u32[]{:S(2)}, u32[]{:S(2)}) collective-permute-start(bf16[528,512]{1,0:T(8,128)(2,1)S(1)} %get-tuple-element.58), channel_id=1, source_target_pairs={{0,1},{1,0},{2,3},{3,2},{4,5},{5,4},{6,7},{7,6},{8,9},{9,8},{10,11... | collective-permute-start | bytes 1622024 | tf_op jit(solution)/shard_map/ppermute | solution.py:308
  8.2 8.8 %collective-permute-start.4 = (bf16[512,512]{1,0:T(8,128)(2,1)S(1)}, bf16[512,512]{1,0:T(8,128)(2,1)S(1)}, u32[]{:S(2)}, u32[]{:S(2)}) collective-permute-start(bf16[512,512]{1,0:T(8,128)(2,1)S(1)} %get-tuple-element.63), channel_id=1, source_target_pairs={{0,1},{1,0},{2,3},{3,2},{4,5},{5,4},{6,7},{7,6},{8,9},{9,8},{10,11... | collective-permute-start | bytes 1572872 | tf_op jit(solution)/shard_map/ppermute | solution.py:294
  8.7 15.3 %collective-permute-start.8 = (bf16[512,512]{1,0:T(8,128)(2,1)S(1)}, bf16[512,512]{1,0:T(8,128)(2,1)S(1)}, u32[]{:S(2)}, u32[]{:S(2)}) collective-permute-start(bf16[512,512]{1,0:T(8,128)(2,1)S(1)} %shard_map.65), channel_id=1, source_target_pairs={{0,2},{1,3},{2,0},{3,1},{4,6},{5,7},{6,4},{7,5},{8,10},{9,11},{10,... | collective-permute-start | bytes 1572872 | tf_op jit(solution)/shard_map/ppermute | solution.py:314
  11.4 24.2 %collective-permute-start.3 = (bf16[528,512]{1,0:T(8,128)(2,1)S(1)}, bf16[528,512]{1,0:T(8,128)(2,1)S(1)}, u32[]{:S(2)}, u32[]{:S(2)}) collective-permute-start(bf16[528,512]{1,0:T(8,128)(2,1)S(1)} %get-tuple-element.61), channel_id=1, source_target_pairs={{0,2},{1,3},{2,0},{3,1},{4,6},{5,7},{6,4},{7,5},{8,10},{9,11},{10,... | collective-permute-start | bytes 1622024 | tf_op jit(solution)/shard_map/ppermute | solution.py:314
  16.4 9.6 %copy-start.4 = (s32[4]{0:T(128)S(1)}, s32[4]{0:T(128)}, u32[]{:S(2)}) copy-start(s32[4]{0:T(128)} %live) | copy-start | bytes 52
  16.5 9.6 %copy-start.5 = (s32[4]{0:T(128)S(1)}, s32[4]{0:T(128)}, u32[]{:S(2)}) copy-start(s32[4]{0:T(128)} %span) | copy-start | bytes 52
  16.5 9.5 %copy-start.6 = (f32[1,128]{1,0:T(1,128)S(1)}, f32[1,128]{1,0:T(1,128)}, u32[]{:S(2)}) copy-start(f32[1,128]{1,0:T(1,128)} %constant.4.clone.frequencies) | copy-start | bytes 1540
  16.5 10.3 %collective-permute-start.7 = (bf16[512,512]{1,0:T(8,128)(2,1)S(1)}, bf16[512,512]{1,0:T(8,128)(2,1)S(1)}, u32[]{:S(2)}, u32[]{:S(2)}) collective-permute-start(bf16[512,512]{1,0:T(8,128)(2,1)S(1)} %get-tuple-element.67), channel_id=1, source_target_pairs={{0,1},{1,0},{2,3},{3,2},{4,5},{5,4},{6,7},{7,6},{8,9},{9,8},{10,11... | collective-permute-start | bytes 1572872 | tf_op jit(solution)/shard_map/ppermute | solution.py:337
  16.6 21.9 %collective-permute-start.1 = (bf16[512,512]{1,0:T(8,128)(2,1)S(1)}, bf16[512,512]{1,0:T(8,128)(2,1)S(1)}, u32[]{:S(2)}, u32[]{:S(2)}) collective-permute-start(bf16[512,512]{1,0:T(8,128)(2,1)S(1)} %get-tuple-element.49), channel_id=1, source_target_pairs={{0,1},{1,0},{2,3},{3,2},{4,5},{5,4},{6,7},{7,6},{8,9},{9,8},{10,11... | collective-permute-start | bytes 1572872 | tf_op jit(solution)/shard_map/ppermute | solution.py:337
  17.1 20.0 %collective-permute-start.6 = (bf16[512,512]{1,0:T(8,128)(2,1)S(1)}, bf16[512,512]{1,0:T(8,128)(2,1)S(1)}, u32[]{:S(2)}, u32[]{:S(2)}) collective-permute-start(bf16[512,512]{1,0:T(8,128)(2,1)S(1)} %get-tuple-element.65), channel_id=1, source_target_pairs={{0,1},{1,0},{2,3},{3,2},{4,5},{5,4},{6,7},{7,6},{8,9},{9,8},{10,11... | collective-permute-start | bytes 1572872 | tf_op jit(solution)/shard_map/ppermute | solution.py:337
  24.1 22.6 %collective-permute-start.5 = (bf16[512,512]{1,0:T(8,128)(2,1)S(1)}, bf16[512,512]{1,0:T(8,128)(2,1)S(1)}, u32[]{:S(2)}, u32[]{:S(2)}) collective-permute-start(bf16[512,512]{1,0:T(8,128)(2,1)S(1)} %shard_map.70), channel_id=1, source_target_pairs={{0,2},{1,3},{2,0},{3,1},{4,6},{5,7},{6,4},{7,5},{8,10},{9,11},{10,... | collective-permute-start | bytes 1572872 | tf_op jit(solution)/shard_map/ppermute | solution.py:314

commit v13 on v12

v13 whole, which is shorter than its diff:
```python
import functools

import jax
import jax.numpy as jnp
import numpy as np
from jax import lax
from jax.experimental import pallas as pl
from jax.experimental.pallas import tpu as pltpu
from jax.sharding import PartitionSpec as P

HD = 128
PAGE = 256
BLOCK = 64
LANES = 128
SUBLANES = 8

rope_base = 500000.0
norm_eps = 1e-05

TILE = 256
CUTS = 4
CHUNKS = (2, 1, 3)

PARAMS = pltpu.CompilerParams(vmem_limit_bytes=16 * 1024 * 1024)
FIRST = pltpu.CompilerParams(vmem_limit_bytes=56 * 1024 * 1024)
LATER = pl.CostEstimate(flops=20000000000, bytes_accessed=1, transcendentals=0)
COST = pl.CostEstimate(flops=1, bytes_accessed=1, transcendentals=0)


def square_sums(rows):
    total = jnp.zeros((rows.shape[0], LANES), jnp.float32)
    for part in range(rows.shape[1] // LANES):
        wide = rows[:, part * LANES : (part + 1) * LANES].astype(jnp.float32)
        total += wide * wide
    return total


def packed(squares, width):
    per_row = width // LANES
    row = lax.broadcasted_iota(jnp.int32, (2 * SUBLANES, LANES), 0)
    parts = []
    for place in range(per_row):
        part = jnp.zeros((2 * SUBLANES, LANES), jnp.float32)
        for index, line in enumerate(squares[place::per_row]):
            high = line.astype(jnp.bfloat16).astype(jnp.float32)
            part = jnp.where(row == index, high, part)
            part = jnp.where(row == SUBLANES + index, line - high, part)
        parts.append(part)
    return jnp.concatenate(parts, axis=1).astype(jnp.bfloat16)


def unpacked(ref, line):
    index, place = divmod(line, ref.shape[1] // LANES)
    part = ref[pl.ds(ref.shape[0] - 2 * SUBLANES, 2 * SUBLANES), place * LANES : (place + 1) * LANES]
    part = part.astype(jnp.float32)
    return part[index : index + 1] + part[SUBLANES + index : SUBLANES + index + 1]


def product_kernel(step, chip_count, first, staged, carrier, tokens, gain, weight, *refs):
    refs = list(refs)
    keep, send = refs.pop(0), refs.pop(0)
    squares = refs.pop(0) if carrier else None
    count = keep.shape[0] // TILE
    depth, width = tokens.shape[1], 2 * keep.shape[1]
    me = lax.axis_index("tensor")
    core = lax.rem(me, 2)
    chip = lax.rem(lax.div(me, 2) + step, chip_count)
    place = pl.ds(pl.multiple_of(chip * width, width), width)

    weight_copies, row_copies = [], []
    if staged:
        rows_buf, weight_buf, gain_buf, weight_sems, row_sems, gain_sem = refs
        cut = depth // CUTS
        gain_copy = pltpu.make_async_copy(gain, gain_buf, gain_sem)
        for index in range(CUTS):
            some = pl.ds(index * cut, cut)
            weight_copies.append(
                pltpu.make_async_copy(weight.at[some, place], weight_buf.at[some, :], weight_sems.at[index])
            )
        for tile in range(count):
            rows = tokens.at[pl.ds((first + tile) * TILE, TILE), :]
            row_copies.append(
                pltpu.make_async_copy(rows, rows_buf.at[pl.ds(tile * TILE, TILE), :], row_sems.at[tile])
            )
        for copy in [gain_copy] + row_copies[:1] + weight_copies + row_copies[1:]:
            copy.start()
        gain_copy.wait()
        gains = gain_buf[...].reshape(1, depth)
    else:
        gains = gain[...].reshape(1, depth)

    lines = []
    for tile in range(count):
        inside = pl.ds(tile * TILE, TILE)
        if staged:
            row_copies[tile].wait()
            rows = rows_buf[inside, :]
        else:
            rows = tokens[pl.ds((first + tile) * TILE, TILE), :]
        scaled = rows * gains
        if weight_copies:
            product = jnp.zeros((TILE, width), jnp.float32)
            for index, copy in enumerate(weight_copies):
                copy.wait()
                span = slice(index * cut, (index + 1) * cut)
                product += jnp.dot(scaled[:, span], weight_buf[span, :], preferred_element_type=jnp.float32)
            weight_copies = []
        else:
            columns = weight_buf[...] if staged else weight[:, place]
            product = jnp.dot(scaled, columns, preferred_element_type=jnp.float32)
        left = product[:, : width // 2].astype(jnp.bfloat16)
        right = product[:, width // 2 :].astype(jnp.bfloat16)
        keep[inside, :] = jnp.where(core == 0, left, right)
        send[inside, :] = jnp.where(core == 0, right, left)
        if carrier:
            total = square_sums(rows)
            for part in range(TILE // LANES):
                turned = jnp.transpose(total[part * LANES : (part + 1) * LANES])
                lines.append(jnp.sum(turned, axis=0, keepdims=True))
                squares[len(lines) - 1 : len(lines), :] = lines[-1]
    if carrier:
        send[pl.ds(keep.shape[0], 2 * SUBLANES), :] = packed(lines, send.shape[1])


def add_carrier_kernel(keep, received, squares, out, pair_squares):
    rows = pl.ds(0, keep.shape[0])
    total = keep[...].astype(jnp.float32) + received[rows, :].astype(jnp.float32)
    out[rows, :] = total.astype(out.dtype)
    lines = []
    for line in range(squares.shape[0]):
        lines.append(squares[line : line + 1, :] + unpacked(received, line))
        pair_squares[line : line + 1, :] = lines[-1]
    out[pl.ds(keep.shape[0], 2 * SUBLANES), :] = packed(lines, out.shape[1])


def table_kernel(live, span, frequencies, limit, far_cos, far_sin, near_cos, near_sin):
    limit[...] = jnp.full(limit.shape, live[lax.axis_index("serve")] * BLOCK, jnp.int32)
    blocks = far_cos.shape[0]
    start = span[lax.axis_index("serve")] * PAGE
    first = start + BLOCK * lax.broadcasted_iota(jnp.int32, (blocks, HD), 0)
    far = first.astype(jnp.float32) * frequencies[...]
    near = lax.broadcasted_iota(jnp.int32, (BLOCK, HD), 0).astype(jnp.float32) * frequencies[...]
    far_cos[...] = jnp.cos(far)
    far_sin[...] = jnp.sin(far)
    near_cos[...] = jnp.cos(near)
    near_sin[...] = jnp.sin(near)


def finish_kernel(first, count, model_dim, *refs):
    keep, received, limit, far_cos, far_sin, near_cos, near_sin = refs[:7]
    pair_squares, arrived = refs[7], refs[8:-4]
    out, staged, sems = refs[-3:]
    on_diagonal = lax.broadcasted_iota(jnp.int32, (LANES, LANES), 0) == lax.broadcasted_iota(
        jnp.int32, (LANES, LANES), 1
    )
    sign = jnp.where(lax.broadcasted_iota(jnp.int32, (1, HD), 1) < HD // 2, -1.0, 1.0)
    copies = []
    for index in range(count):
        start = (first + index) * TILE
        rows, inside = pl.ds(start, TILE), pl.ds(index * TILE, TILE)
        values = keep[inside, :].astype(jnp.float32) + received[inside, :].astype(jnp.float32)
        for part in arrived:
            values += part[inside, :].astype(jnp.float32)
        columns = []
        for line in range(index * TILE // LANES, (index + 1) * TILE // LANES):
            totals = pair_squares[line : line + 1, :]
            for ref in arrived:
                totals += unpacked(ref, line)
            columns.append(jnp.sum(jnp.where(on_diagonal, totals, 0.0), axis=1, keepdims=True))
        scales = 1.0 / jnp.sqrt(jnp.concatenate(columns, axis=0) / model_dim + norm_eps)
        alive = start + lax.broadcasted_iota(jnp.int32, (TILE, LANES), 0) < limit[0:1, :]
        cosines, sines = [], []
        for block in range(start // BLOCK, (start + TILE) // BLOCK):
            block_cos = far_cos[block : block + 1, :]
            block_sin = far_sin[block : block + 1, :]
            cosines.append(block_cos * near_cos[...] - block_sin * near_sin[...])
            sines.append((sign * block_sin) * near_cos[...] + (sign * block_cos) * near_sin[...])
        cosine = jnp.concatenate(cosines, axis=0)
        sine = jnp.concatenate(sines, axis=0)
        for low in range(0, out.shape[1], 2 * HD):
            key = values[:, low : low + HD] * scales
            turned = key * cosine + pltpu.roll(key, HD // 2, 1) * sine
            staged[inside, low : low + HD] = jnp.where(alive, turned, 0.0).astype(out.dtype)
            value = values[:, low + HD : low + 2 * HD] * scales
            staged[inside, low + HD : low + 2 * HD] = jnp.where(alive, value, 0.0).astype(out.dtype)
        copies.append(pltpu.make_async_copy(staged.at[inside, :], out.at[rows, :], sems.at[index]))
        copies[-1].start()
    for copy in copies:
        copy.wait()


def shards(tokens, norm_gain, kv_weight, live_blocks, span_offset):
    tensor_count = lax.axis_size("tensor")
    chip_count = tensor_count // 2
    me = lax.axis_index("tensor")
    slot_rows, depth = tokens.shape
    columns = kv_weight.shape[1] // tensor_count
    tiles = slot_rows // TILE
    model_dim = depth * tensor_count

    swap = [(i, i ^ 1) for i in range(tensor_count)]

    def shift(step):
        return [(i, (i + 2 * step) % tensor_count) for i in range(tensor_count)]

    def product(gain, step, first, count, staged=False, carrier=True):
        vmem = pl.BlockSpec(memory_space=pltpu.VMEM)
        rows = count * TILE
        out_shape = [jax.ShapeDtypeStruct((rows, columns), jnp.bfloat16)] * 2
        if carrier:
            out_shape[1] = jax.ShapeDtypeStruct((rows + 2 * SUBLANES, columns), jnp.bfloat16)
            out_shape.append(jax.ShapeDtypeStruct((rows // LANES, LANES), jnp.float32))
        scratch = [
            pltpu.VMEM((rows, depth), jnp.bfloat16),
            pltpu.VMEM((depth, 2 * columns), jnp.bfloat16),
            pltpu.VMEM((depth,), jnp.bfloat16),
            pltpu.SemaphoreType.DMA((CUTS,)),
            pltpu.SemaphoreType.DMA((count,)),
            pltpu.SemaphoreType.DMA,
        ]
        return pl.pallas_call(
            functools.partial(product_kernel, step, chip_count, first, staged, carrier),
            in_specs=[pl.BlockSpec(memory_space=pltpu.HBM) if staged else vmem] * 3,
            out_shape=out_shape,
            out_specs=[vmem] * len(out_shape),
            scratch_shapes=scratch if staged else [],
            compiler_params=FIRST if staged else PARAMS,
            cost_estimate=COST,
        )(tokens, gain, kv_weight)

    def tables(span_offset):
        frequencies = rope_base ** (-(np.arange(HD // 2, dtype=np.float32) * 2.0) / HD)
        frequencies = np.concatenate([frequencies, frequencies])[None, :].astype(np.float32)
        shapes = [(slot_rows // BLOCK, HD)] * 2 + [(BLOCK, HD)] * 2
        made = pl.pallas_call(
            table_kernel,
            in_specs=[pl.BlockSpec(memory_space=pltpu.SMEM)] * 2 + [pl.BlockSpec(memory_space=pltpu.VMEM)],
            out_shape=[jax.ShapeDtypeStruct((8, LANES), jnp.int32)]
            + [jax.ShapeDtypeStruct(shape, jnp.float32) for shape in shapes],
            out_specs=[pl.BlockSpec(memory_space=pltpu.VMEM)] * 5,
            compiler_params=PARAMS,
            cost_estimate=COST,
        )(live_blocks, span_offset, jnp.asarray(frequencies))
        return list(made)

    def finish(first, count, keep, received, table, squares, arrived, result):
        vmem = pl.BlockSpec(memory_space=pltpu.VMEM)
        operands = [keep, received] + table + [squares] + arrived
        aliases = {len(operands): 0}
        if result is None:
            result, aliases = jnp.zeros((1,), jnp.bfloat16), {}
        return pl.pallas_call(
            functools.partial(finish_kernel, first, count, model_dim),
            in_specs=[vmem] * len(operands) + [pl.BlockSpec(memory_space=pl.ANY)],
            out_shape=jax.ShapeDtypeStruct((slot_rows, columns), jnp.bfloat16),
            out_specs=pl.BlockSpec(memory_space=pltpu.HBM),
            scratch_shapes=[pltpu.VMEM((count * TILE, columns), jnp.bfloat16), pltpu.SemaphoreType.DMA((count,))],
            input_output_aliases=aliases,
            compiler_params=PARAMS,
            cost_estimate=LATER,
        )(*operands, result)

    others = range(1, chip_count)
    firsts = [sum(CHUNKS[:index]) for index in range(len(CHUNKS))]
    chunk_count = len(CHUNKS)

    chunks = list(zip(firsts, CHUNKS))

    def add_halves(made):
        added = [
            pl.pallas_call(
                add_carrier_kernel,
                out_shape=[
                    jax.ShapeDtypeStruct(send.shape, send.dtype),
                    jax.ShapeDtypeStruct(squares.shape, squares.dtype),
                ],
                compiler_params=PARAMS,
                cost_estimate=COST,
            )(keep, lax.ppermute(send, "tensor", swap), squares)
            for keep, send, squares in made
        ]
        return [sums for sums, _ in added], added[0][1]

    def cross(sums):
        return [lax.ppermute(part, "tensor", shift(step)) for step, part in zip(others, sums)]

    hold = lax.optimization_barrier
    made = [product(norm_gain, step, *chunks[0], staged=True) for step in others]
    made, gain = hold((made, norm_gain))
    sums = add_halves(made)
    made = [product(gain, step, *chunks[1]) for step in others]
    sums, made, gain, span_offset, live_blocks = hold((sums, made, gain, span_offset, live_blocks))

    arrivals = [(cross(sums[0]), sums[1])]
    for index in range(1, chunk_count):
        if index > 1:
            made = [product(gain, step, *chunks[index]) for step in others]
        sums = add_halves(made)
        arrivals.append((cross(sums[0]), sums[1]))
    own = [product(gain, 0, first, count, carrier=False) for first, count in chunks]
    table = tables(span_offset)

    result = None
    for (first, count), (keep, send), (arrived, squares) in zip(chunks, own, arrivals):
        received = lax.ppermute(send, "tensor", swap)
        result = finish(first, count, keep, received, table, squares, arrived, result)
    return result


def solution(mesh):
    in_specs = (
        P(("groups", "serve"), "tensor"),
        P("tensor"),
        P("tensor", None),
        P("groups"),
        P("groups"),
    )
    out_specs = P(("groups", "serve"), "tensor")
    return jax.shard_map(shards, mesh=mesh, in_specs=in_specs, out_specs=out_specs, check_vma=False)
```

time: 48.2 us -> 47.1 us (0.977)
  starting transfers between devices: 7.84 us -> 7.03 us
    ppermute x2 -> x3, waiting for transfers between devices: 0.01 us -> 1.04 us  [add_halves(): lax.ppermute(send, 'tensor', swap)]
    ppermute x3, waiting for transfers between devices: 23.8 us -> 22.8 us  [cross(): lax.ppermute(part, 'tensor', shift(step))]
    ppermute x3, starting transfers between devices: 6.07 us -> 5.21 us  [cross(): lax.ppermute(part, 'tensor', shift(step))]
    ppermute x2 -> x3, starting transfers between devices: 1.01 us -> 1.47 us  [add_halves(): lax.ppermute(send, 'tensor', swap)]
    pallas_call x9 -> x12, Pallas kernels: 15.5 us -> 15.2 us  [the longest x6 10.6 us: product(): pl.pallas_call(functools.partial(product_kernel, step, chip_count, first,...]
  transfers between devices with their start and end apart: 9 -> 9, of which waited for: 3 -> 4; matrix products, arithmetic and copies ran while one was open for 0% -> 0% of each run, Pallas kernels for 21% -> 21%
where the time goes in v13:
time: 47.1 us; the launch traced here: 47 us
  waiting for transfers between devices  23.8 us (51%)
  Pallas kernels  15.9 us (34%)
  starting transfers between devices  7.03 us (15%)
    ppermute x3, waiting for transfers between devices, cross(): lax.ppermute(part, 'tensor', shift(step))  22.8 us
    pallas_call x6, Pallas kernels, product(): pl.pallas_call(functools.partial(product_kernel, step, chip_count, first,...  10.6 us
    ppermute x3, starting transfers between devices, cross(): lax.ppermute(part, 'tensor', shift(step))  5.21 us
    pallas_call x3, Pallas kernels, finish(): pl.pallas_call(functools.partial(finish_kernel, first, count, model_dim),...  4.21 us
    ppermute x3, starting transfers between devices, add_halves(): lax.ppermute(send, 'tensor', swap)  1.47 us
    ppermute x3, waiting for transfers between devices, add_halves(): lax.ppermute(send, 'tensor', swap)  1.04 us
  transfers between devices with their start and end apart: 9, of which 4 were waited for; matrix products, arithmetic and copies ran while one was open for 0% of the time, Pallas kernels for 21%

profile of v13, /device:TPU:0, one launch (start us, length us, event | category | flops | bytes accessed | tf_op | source)
XLA Modules:
  0.0 47.0 jit_solution(4029803421894184362)
XLA Ops:
  0.0 0.0 copy-start.3
  0.0 0.0 copy-start
  0.0 0.0 copy-start.1
  0.0 4.1 %shard_map.64 = (bf16[512,512]{1,0:T(8,128)(2,1)}, bf16[528,512]{1,0:T(8,128)(2,1)}, f32[4,128]{1,0:T(4,128)}) custom-call(bf16[1536,1024]{1,0:T(8,128)(2,1)} %tokens.11, bf16[1024]{0:T(1024)(128)(2,1)} %gain.6, bf16[1024,2048]{1,0:T(8,128)(2,1)} %weight.11), custom_call_target="tpu_custom_call" | custom-call | flops 1 | bytes 1 | tf_op jit(solution)/shard_map/pallas_call | solution.py:221
  4.1 0.0 copy-start.2
  4.1 0.0 copy-start.4
  4.1 0.5 %collective-permute-start = (bf16[528,512]{1,0:T(8,128)(2,1)}, bf16[528,512]{1,0:T(8,128)(2,1)S(1)}, u32[]{:S(2)}, u32[]{:S(2)}) collective-permute-start(bf16[528,512]{1,0:T(8,128)(2,1)} %get-tuple-element.47), channel_id=1, source_target_pairs={{0,1},{1,0},{2,3},{3,2},{4,5},{5,4},{6,7},{7,6},{8,9},{9,8},{10,11... | collective-permute-start | bytes 1622024 | tf_op jit(solution)/shard_map/ppermute | solution.py:279
  4.7 0.0 copy-done.3
  4.7 0.0 copy-done
  4.7 0.0 copy-done.1
  4.7 0.7 %shard_map.66 = (bf16[256,512]{1,0:T(8,128)(2,1)S(1)}, bf16[272,512]{1,0:T(8,128)(2,1)S(1)}, f32[2,128]{1,0:T(2,128)S(1)}) custom-call(bf16[1536,1024]{1,0:T(8,128)(2,1)S(1)} %copy-done.1, bf16[1024]{0:T(1024)(128)(2,1)S(1)} %copy-done.3, bf16[1024,2048]{1,0:T(8,128)(2,1)S(1)} %copy-done), custom_call_target="tpu_custom_call" | custom-call | flops 1 | bytes 1 | tf_op jit(solution)/shard_map/pallas_call | solution.py:221
  5.4 1.0 %collective-permute-done.received = bf16[528,512]{1,0:T(8,128)(2,1)S(1)} collective-permute-done((bf16[528,512]{1,0:T(8,128)(2,1)}, bf16[528,512]{1,0:T(8,128)(2,1)S(1)}, u32[]{:S(2)}, u32[]{:S(2)}) %collective-permute-start) | collective-permute-done | bytes 540704 | tf_op jit(solution)/shard_map/ppermute | solution.py:279
  6.4 0.0 copy-done.2
  6.4 0.0 copy-done.4
  6.4 0.1 shard_map.65
  6.6 2.9 %collective-permute-start.8 = (bf16[528,512]{1,0:T(8,128)(2,1)S(1)}, bf16[528,512]{1,0:T(8,128)(2,1)S(1)}, u32[]{:S(2)}, u32[]{:S(2)}) collective-permute-start(bf16[528,512]{1,0:T(8,128)(2,1)S(1)} %get-tuple-element.80), channel_id=1, source_target_pairs={{0,2},{1,3},{2,0},{3,1},{4,6},{5,7},{6,4},{7,5},{8,10},{9,11},{10,... | collective-permute-start | bytes 1622024 | tf_op jit(solution)/shard_map/ppermute | solution.py:285
  9.5 1.3 %shard_map.73 = (bf16[512,512]{1,0:T(8,128)(2,1)S(1)}, bf16[512,512]{1,0:T(8,128)(2,1)S(1)}) custom-call(bf16[1536,1024]{1,0:T(8,128)(2,1)S(1)} %copy-done.1, bf16[1024]{0:T(1024)(128)(2,1)S(1)} %copy-done.3, bf16[1024,2048]{1,0:T(8,128)(2,1)S(1)} %copy-done), custom_call_target="tpu_custom_call" | custom-call | flops 1 | bytes 1 | tf_op jit(solution)/shard_map/pallas_call | solution.py:221
  10.8 0.1 collective-permute-start.7
  10.9 0.5 %collective-permute-start.5 = (bf16[272,512]{1,0:T(8,128)(2,1)S(1)}, bf16[272,512]{1,0:T(8,128)(2,1)S(1)}, u32[]{:S(2)}, u32[]{:S(2)}) collective-permute-start(bf16[272,512]{1,0:T(8,128)(2,1)S(1)} %get-tuple-element.73), channel_id=1, source_target_pairs={{0,1},{1,0},{2,3},{3,2},{4,5},{5,4},{6,7},{7,6},{8,9},{9,8},{10,11... | collective-permute-start | bytes 835592 | tf_op jit(solution)/shard_map/ppermute | solution.py:279
  11.4 0.7 %shard_map.71 = (bf16[256,512]{1,0:T(8,128)(2,1)S(1)}, bf16[256,512]{1,0:T(8,128)(2,1)S(1)}) custom-call(bf16[1536,1024]{1,0:T(8,128)(2,1)S(1)} %copy-done.1, bf16[1024]{0:T(1024)(128)(2,1)S(1)} %copy-done.3, bf16[1024,2048]{1,0:T(8,128)(2,1)S(1)} %copy-done), custom_call_target="tpu_custom_call" | custom-call | flops 1 | bytes 1 | tf_op jit(solution)/shard_map/pallas_call | solution.py:221
  12.1 1.9 %shard_map.69 = (bf16[768,512]{1,0:T(8,128)(2,1)S(1)}, bf16[784,512]{1,0:T(8,128)(2,1)S(1)}, f32[6,128]{1,0:T(8,128)S(1)}) custom-call(bf16[1536,1024]{1,0:T(8,128)(2,1)S(1)} %copy-done.1, bf16[1024]{0:T(1024)(128)(2,1)S(1)} %copy-done.3, bf16[1024,2048]{1,0:T(8,128)(2,1)S(1)} %copy-done), custom_call_target="tpu_custom_call" | custom-call | flops 1 | bytes 1 | tf_op jit(solution)/shard_map/pallas_call | solution.py:221
  14.0 0.0 copy-start.5
  14.0 0.0 copy-start.6
  14.0 0.0 copy-start.7
  14.1 1.8 %shard_map.67 = (bf16[768,512]{1,0:T(8,128)(2,1)S(1)}, bf16[768,512]{1,0:T(8,128)(2,1)S(1)}) custom-call(bf16[1536,1024]{1,0:T(8,128)(2,1)S(1)} %copy-done.1, bf16[1024]{0:T(1024)(128)(2,1)S(1)} %copy-done.3, bf16[1024,2048]{1,0:T(8,128)(2,1)S(1)} %copy-done), custom_call_target="tpu_custom_call" | custom-call | flops 1 | bytes 1 | tf_op jit(solution)/shard_map/pallas_call | solution.py:221
  15.9 0.1 collective-permute-start.4
  16.0 0.4 collective-permute-start.2
  16.5 0.0 copy-done.5
  16.5 0.0 copy-done.6
  16.5 0.0 copy-done.7
  16.5 0.7 %shard_map.68 = (s32[8,128]{1,0:T(8,128)S(1)}, f32[24,128]{1,0:T(8,128)S(1)}, f32[24,128]{1,0:T(8,128)S(1)}, f32[64,128]{1,0:T(8,128)S(1)}, f32[64,128]{1,0:T(8,128)S(1)}) custom-call(s32[4]{0:T(128)S(1)} %copy-done.5, s32[4]{0:T(128)S(1)} %copy-done.6, f32[1,128]{1,0:T(1,128)S(1)} %copy-done.7), custom_call_target="tpu_custom_call" | custom-call | flops 1 | bytes 1 | tf_op jit(solution)/shard_map/pallas_call | solution.py:235
  17.2 0.0 collective-permute-done.5.received
  17.2 0.1 collective-permute-start.1
  17.4 0.1 shard_map.72
  17.4 0.0 collective-permute-done.7.refs_1_
  17.4 0.2 collective-permute-start.6
  17.6 5.0 %collective-permute-done.8.refs_8_ = bf16[528,512]{1,0:T(8,128)(2,1)S(1)} collective-permute-done((bf16[528,512]{1,0:T(8,128)(2,1)S(1)}, bf16[528,512]{1,0:T(8,128)(2,1)S(1)}, u32[]{:S(2)}, u32[]{:S(2)}) %collective-permute-start.8) | collective-permute-done | bytes 540704 | tf_op jit(solution)/shard_map/ppermute | solution.py:285
  22.6 1.4 %shard_map.74.refs_9_ = bf16[1536,512]{1,0:T(8,128)(2,1)} custom-call(bf16[512,512]{1,0:T(8,128)(2,1)S(1)} %get-tuple-element.77.refs_0_, bf16[512,512]{1,0:T(8,128)(2,1)S(1)} %collective-permute-done.7.refs_1_, s32[8,128]{1,0:T(8,128)S(1)} %get-tuple-element.60.refs_2_, f32[24,128]{1,0:T(8,128)S(1)} %get-tuple-element.61.refs_3_, ...), custom_call_target="tpu_custom_call" | custom-call | flops 20000000000 | bytes 1 | tf_op jit(solution)/shard_map/pallas_call | solution.py:252
  24.0 0.0 collective-permute-done.2.received
  24.0 0.2 shard_map.70
  24.2 2.1 %collective-permute-start.3 = (bf16[784,512]{1,0:T(8,128)(2,1)S(1)}, bf16[784,512]{1,0:T(8,128)(2,1)S(1)}, u32[]{:S(2)}, u32[]{:S(2)}) collective-permute-start(bf16[784,512]{1,0:T(8,128)(2,1)S(1)} %get-tuple-element.69), channel_id=1, source_target_pairs={{0,2},{1,3},{2,0},{3,1},{4,6},{5,7},{6,4},{7,5},{8,10},{9,11},{10,... | collective-permute-start | bytes 2408456 | tf_op jit(solution)/shard_map/ppermute | solution.py:285
  26.3 0.0 collective-permute-done.4.refs_1_
  26.3 2.2 %collective-permute-done.6.refs_8_ = bf16[272,512]{1,0:T(8,128)(2,1)S(1)} collective-permute-done((bf16[272,512]{1,0:T(8,128)(2,1)S(1)}, bf16[272,512]{1,0:T(8,128)(2,1)S(1)}, u32[]{:S(2)}, u32[]{:S(2)}) %collective-permute-start.6) | collective-permute-done | bytes 278560 | tf_op jit(solution)/shard_map/ppermute | solution.py:285
  28.5 1.1 %shard_map.75.refs_9_ = bf16[1536,512]{1,0:T(8,128)(2,1)} custom-call(bf16[256,512]{1,0:T(8,128)(2,1)S(1)} %get-tuple-element.70.refs_0_, bf16[256,512]{1,0:T(8,128)(2,1)S(1)} %collective-permute-done.4.refs_1_, s32[8,128]{1,0:T(8,128)S(1)} %get-tuple-element.60.refs_2_, f32[24,128]{1,0:T(8,128)S(1)} %get-tuple-element.61.refs_3_, ...), custom_call_target="tpu_custom_call", output_to_operand_aliasing={{}: (9, {})} | custom-call | flops 20000000000 | bytes 1 | tf_op jit(solution)/shard_map/pallas_call | solution.py:252
  29.7 0.0 collective-permute-done.1.refs_1_
  29.7 15.6 %collective-permute-done.3.refs_8_ = bf16[784,512]{1,0:T(8,128)(2,1)S(1)} collective-permute-done((bf16[784,512]{1,0:T(8,128)(2,1)S(1)}, bf16[784,512]{1,0:T(8,128)(2,1)S(1)}, u32[]{:S(2)}, u32[]{:S(2)}) %collective-permute-start.3) | collective-permute-done | bytes 802848 | tf_op jit(solution)/shard_map/ppermute | solution.py:285
  45.3 1.7 %shard_map.76 = bf16[1536,512]{1,0:T(8,128)(2,1)} custom-call(bf16[768,512]{1,0:T(8,128)(2,1)S(1)} %get-tuple-element.56.refs_0_, bf16[768,512]{1,0:T(8,128)(2,1)S(1)} %collective-permute-done.1.refs_1_, s32[8,128]{1,0:T(8,128)S(1)} %get-tuple-element.60.refs_2_, f32[24,128]{1,0:T(8,128)S(1)} %get-tuple-element.61.refs_3_, ...), custom_call_target="tpu_custom_call", output_to_operand_aliasing={{}: (9, {})} | custom-call | flops 20000000000 | bytes 1 | tf_op jit(solution)/shard_map/pallas_call | solution.py:252
Async XLA Ops:
  0.0 4.7 %copy-start.3 = (bf16[1024]{0:T(1024)(128)(2,1)S(1)}, bf16[1024]{0:T(1024)(128)(2,1)}, u32[]{:S(2)}) copy-start(bf16[1024]{0:T(1024)(128)(2,1)} %gain.6) | copy-start | bytes 6148
  0.0 4.7 %copy-start = (bf16[1024,2048]{1,0:T(8,128)(2,1)S(1)}, bf16[1024,2048]{1,0:T(8,128)(2,1)}, u32[]{:S(2)}) copy-start(bf16[1024,2048]{1,0:T(8,128)(2,1)} %weight.11) | copy-start | bytes 12582916
  0.0 4.7 %copy-start.1 = (bf16[1536,1024]{1,0:T(8,128)(2,1)S(1)}, bf16[1536,1024]{1,0:T(8,128)(2,1)}, u32[]{:S(2)}) copy-start(bf16[1536,1024]{1,0:T(8,128)(2,1)} %tokens.11) | copy-start | bytes 9437188
  4.1 2.3 %copy-start.2 = (bf16[512,512]{1,0:T(8,128)(2,1)S(1)}, bf16[512,512]{1,0:T(8,128)(2,1)}, u32[]{:S(2)}) copy-start(bf16[512,512]{1,0:T(8,128)(2,1)} %get-tuple-element.46.keep) | copy-start | bytes 1572868
  4.1 2.3 %copy-start.4 = (f32[4,128]{1,0:T(4,128)S(1)}, f32[4,128]{1,0:T(4,128)}, u32[]{:S(2)}) copy-start(f32[4,128]{1,0:T(4,128)} %get-tuple-element.48.squares) | copy-start | bytes 6148
  4.1 2.3 %collective-permute-start = (bf16[528,512]{1,0:T(8,128)(2,1)}, bf16[528,512]{1,0:T(8,128)(2,1)S(1)}, u32[]{:S(2)}, u32[]{:S(2)}) collective-permute-start(bf16[528,512]{1,0:T(8,128)(2,1)} %get-tuple-element.47), channel_id=1, source_target_pairs={{0,1},{1,0},{2,3},{3,2},{4,5},{5,4},{6,7},{7,6},{8,9},{9,8},{10,11... | collective-permute-start | bytes 1622024 | tf_op jit(solution)/shard_map/ppermute | solution.py:279
  6.6 16.0 %collective-permute-start.8 = (bf16[528,512]{1,0:T(8,128)(2,1)S(1)}, bf16[528,512]{1,0:T(8,128)(2,1)S(1)}, u32[]{:S(2)}, u32[]{:S(2)}) collective-permute-start(bf16[528,512]{1,0:T(8,128)(2,1)S(1)} %get-tuple-element.80), channel_id=1, source_target_pairs={{0,2},{1,3},{2,0},{3,1},{4,6},{5,7},{6,4},{7,5},{8,10},{9,11},{10,... | collective-permute-start | bytes 1622024 | tf_op jit(solution)/shard_map/ppermute | solution.py:285
  10.8 6.7 %collective-permute-start.7 = (bf16[512,512]{1,0:T(8,128)(2,1)S(1)}, bf16[512,512]{1,0:T(8,128)(2,1)S(1)}, u32[]{:S(2)}, u32[]{:S(2)}) collective-permute-start(bf16[512,512]{1,0:T(8,128)(2,1)S(1)} %get-tuple-element.78), channel_id=1, source_target_pairs={{0,1},{1,0},{2,3},{3,2},{4,5},{5,4},{6,7},{7,6},{8,9},{9,8},{10,11... | collective-permute-start | bytes 1572872 | tf_op jit(solution)/shard_map/ppermute | solution.py:305
  10.9 6.3 %collective-permute-start.5 = (bf16[272,512]{1,0:T(8,128)(2,1)S(1)}, bf16[272,512]{1,0:T(8,128)(2,1)S(1)}, u32[]{:S(2)}, u32[]{:S(2)}) collective-permute-start(bf16[272,512]{1,0:T(8,128)(2,1)S(1)} %get-tuple-element.73), channel_id=1, source_target_pairs={{0,1},{1,0},{2,3},{3,2},{4,5},{5,4},{6,7},{7,6},{8,9},{9,8},{10,11... | collective-permute-start | bytes 835592 | tf_op jit(solution)/shard_map/ppermute | solution.py:279
  14.0 2.5 %copy-start.5 = (s32[4]{0:T(128)S(1)}, s32[4]{0:T(128)}, u32[]{:S(2)}) copy-start(s32[4]{0:T(128)} %live) | copy-start | bytes 52
  14.0 2.4 %copy-start.6 = (s32[4]{0:T(128)S(1)}, s32[4]{0:T(128)}, u32[]{:S(2)}) copy-start(s32[4]{0:T(128)} %span) | copy-start | bytes 52
  14.0 2.4 %copy-start.7 = (f32[1,128]{1,0:T(1,128)S(1)}, f32[1,128]{1,0:T(1,128)}, u32[]{:S(2)}) copy-start(f32[1,128]{1,0:T(1,128)} %constant.4.clone.frequencies) | copy-start | bytes 1540
  15.9 10.4 %collective-permute-start.4 = (bf16[256,512]{1,0:T(8,128)(2,1)S(1)}, bf16[256,512]{1,0:T(8,128)(2,1)S(1)}, u32[]{:S(2)}, u32[]{:S(2)}) collective-permute-start(bf16[256,512]{1,0:T(8,128)(2,1)S(1)} %get-tuple-element.71), channel_id=1, source_target_pairs={{0,1},{1,0},{2,3},{3,2},{4,5},{5,4},{6,7},{7,6},{8,9},{9,8},{10,11... | collective-permute-start | bytes 786440 | tf_op jit(solution)/shard_map/ppermute | solution.py:305
  16.0 8.0 %collective-permute-start.2 = (bf16[784,512]{1,0:T(8,128)(2,1)S(1)}, bf16[784,512]{1,0:T(8,128)(2,1)S(1)}, u32[]{:S(2)}, u32[]{:S(2)}) collective-permute-start(bf16[784,512]{1,0:T(8,128)(2,1)S(1)} %get-tuple-element.66), channel_id=1, source_target_pairs={{0,1},{1,0},{2,3},{3,2},{4,5},{5,4},{6,7},{7,6},{8,9},{9,8},{10,11... | collective-permute-start | bytes 2408456 | tf_op jit(solution)/shard_map/ppermute | solution.py:279
  17.2 12.4 %collective-permute-start.1 = (bf16[768,512]{1,0:T(8,128)(2,1)S(1)}, bf16[768,512]{1,0:T(8,128)(2,1)S(1)}, u32[]{:S(2)}, u32[]{:S(2)}) collective-permute-start(bf16[768,512]{1,0:T(8,128)(2,1)S(1)} %get-tuple-element.57), channel_id=1, source_target_pairs={{0,1},{1,0},{2,3},{3,2},{4,5},{5,4},{6,7},{7,6},{8,9},{9,8},{10,11... | collective-permute-start | bytes 2359304 | tf_op jit(solution)/shard_map/ppermute | solution.py:305
  17.4 11.1 %collective-permute-start.6 = (bf16[272,512]{1,0:T(8,128)(2,1)S(1)}, bf16[272,512]{1,0:T(8,128)(2,1)S(1)}, u32[]{:S(2)}, u32[]{:S(2)}) collective-permute-start(bf16[272,512]{1,0:T(8,128)(2,1)S(1)} %get-tuple-element.76), channel_id=1, source_target_pairs={{0,2},{1,3},{2,0},{3,1},{4,6},{5,7},{6,4},{7,5},{8,10},{9,11},{10,... | collective-permute-start | bytes 835592 | tf_op jit(solution)/shard_map/ppermute | solution.py:285
  24.2 21.1 %collective-permute-start.3 = (bf16[784,512]{1,0:T(8,128)(2,1)S(1)}, bf16[784,512]{1,0:T(8,128)(2,1)S(1)}, u32[]{:S(2)}, u32[]{:S(2)}) collective-permute-start(bf16[784,512]{1,0:T(8,128)(2,1)S(1)} %get-tuple-element.69), channel_id=1, source_target_pairs={{0,2},{1,3},{2,0},{3,1},{4,6},{5,7},{6,4},{7,5},{8,10},{9,11},{10,... | collective-permute-start | bytes 2408456 | tf_op jit(solution)/shard_map/ppermute | solution.py:285

commit v14 on v13

--- a/solution.py
+++ b/solution.py
@@ -22,8 +22,9 @@
 CHUNKS = (2, 1, 3)
 
 PARAMS = pltpu.CompilerParams(vmem_limit_bytes=16 * 1024 * 1024)
-FIRST = pltpu.CompilerParams(vmem_limit_bytes=56 * 1024 * 1024)
+FIRST = pltpu.CompilerParams(vmem_limit_bytes=53248 * 1024)
 LATER = pl.CostEstimate(flops=20000000000, bytes_accessed=1, transcendentals=0)
+HEAVY = pl.CostEstimate(flops=1000000000000, bytes_accessed=1, transcendentals=0)
 COST = pl.CostEstimate(flops=1, bytes_accessed=1, transcendentals=0)
 
 
@@ -122,15 +123,19 @@
         send[pl.ds(keep.shape[0], 2 * SUBLANES), :] = packed(lines, send.shape[1])
 
 
-def add_carrier_kernel(keep, received, squares, out, pair_squares):
-    rows = pl.ds(0, keep.shape[0])
-    total = keep[...].astype(jnp.float32) + received[rows, :].astype(jnp.float32)
-    out[rows, :] = total.astype(out.dtype)
+def add_carrier_kernel(keep, received, squares, pair_squares, out, *rest):
+    low = 0
+    for part in (out, *rest):
+        size = part.shape[0] - (2 * SUBLANES if part is out else 0)
+        rows = pl.ds(low, size)
+        total = keep[rows, :].astype(jnp.float32) + received[rows, :].astype(jnp.float32)
+        part[pl.ds(0, size), :] = total.astype(part.dtype)
+        low += size
     lines = []
     for line in range(squares.shape[0]):
         lines.append(squares[line : line + 1, :] + unpacked(received, line))
         pair_squares[line : line + 1, :] = lines[-1]
-    out[pl.ds(keep.shape[0], 2 * SUBLANES), :] = packed(lines, out.shape[1])
+    out[pl.ds(out.shape[0] - 2 * SUBLANES, 2 * SUBLANES), :] = packed(lines, out.shape[1])
 
 
 def table_kernel(live, span, frequencies, limit, far_cos, far_sin, near_cos, near_sin):
@@ -146,9 +151,10 @@
     near_sin[...] = jnp.sin(near)
 
 
-def finish_kernel(first, count, model_dim, *refs):
+def finish_kernel(first, at, count, chip_count, model_dim, *refs):
     keep, received, limit, far_cos, far_sin, near_cos, near_sin = refs[:7]
-    pair_squares, arrived = refs[7], refs[8:-4]
+    pair_squares, carriers = refs[7], refs[8 : 7 + chip_count]
+    arrived = refs[7 + chip_count : -4] if at else carriers
     out, staged, sems = refs[-3:]
     on_diagonal = lax.broadcasted_iota(jnp.int32, (LANES, LANES), 0) == lax.broadcasted_iota(
         jnp.int32, (LANES, LANES), 1
@@ -156,15 +162,16 @@
     sign = jnp.where(lax.broadcasted_iota(jnp.int32, (1, HD), 1) < HD // 2, -1.0, 1.0)
     copies = []
     for index in range(count):
-        start = (first + index) * TILE
+        start = (first + at + index) * TILE
         rows, inside = pl.ds(start, TILE), pl.ds(index * TILE, TILE)
-        values = keep[inside, :].astype(jnp.float32) + received[inside, :].astype(jnp.float32)
+        of_chunk = pl.ds((at + index) * TILE, TILE)
+        values = keep[of_chunk, :].astype(jnp.float32) + received[of_chunk, :].astype(jnp.float32)
         for part in arrived:
             values += part[inside, :].astype(jnp.float32)
         columns = []
-        for line in range(index * TILE // LANES, (index + 1) * TILE // LANES):
+        for line in range((at + index) * TILE // LANES, (at + index + 1) * TILE // LANES):
             totals = pair_squares[line : line + 1, :]
-            for ref in arrived:
+            for ref in carriers:
                 totals += unpacked(ref, line)
             columns.append(jnp.sum(jnp.where(on_diagonal, totals, 0.0), axis=1, keepdims=True))
         scales = 1.0 / jnp.sqrt(jnp.concatenate(columns, axis=0) / model_dim + norm_eps)
@@ -225,7 +232,7 @@
             out_specs=[vmem] * len(out_shape),
             scratch_shapes=scratch if staged else [],
             compiler_params=FIRST if staged else PARAMS,
-            cost_estimate=COST,
+            cost_estimate=HEAVY if staged else COST,
         )(tokens, gain, kv_weight)
 
     def tables(span_offset):
@@ -243,14 +250,14 @@
         )(live_blocks, span_offset, jnp.asarray(frequencies))
         return list(made)
 
-    def finish(first, count, keep, received, table, squares, arrived, result):
+    def finish(first, at, count, keep, received, table, squares, carriers, arrived, result):
         vmem = pl.BlockSpec(memory_space=pltpu.VMEM)
-        operands = [keep, received] + table + [squares] + arrived
+        operands = [keep, received] + table + [squares] + carriers + (arrived if at else [])
         aliases = {len(operands): 0}
         if result is None:
             result, aliases = jnp.zeros((1,), jnp.bfloat16), {}
         return pl.pallas_call(
-            functools.partial(finish_kernel, first, count, model_dim),
+            functools.partial(finish_kernel, first, at, count, chip_count, model_dim),
             in_specs=[vmem] * len(operands) + [pl.BlockSpec(memory_space=pl.ANY)],
             out_shape=jax.ShapeDtypeStruct((slot_rows, columns), jnp.bfloat16),
             out_specs=pl.BlockSpec(memory_space=pltpu.HBM),
@@ -266,20 +273,20 @@
 
     chunks = list(zip(firsts, CHUNKS))
 
-    def add_halves(made):
+    def add_halves(made, counts):
+        sizes = [count * TILE for count in counts]
+        sizes[0] += 2 * SUBLANES
         added = [
             pl.pallas_call(
                 add_carrier_kernel,
-                out_shape=[
-                    jax.ShapeDtypeStruct(send.shape, send.dtype),
-                    jax.ShapeDtypeStruct(squares.shape, squares.dtype),
-                ],
+                out_shape=[jax.ShapeDtypeStruct(squares.shape, squares.dtype)]
+                + [jax.ShapeDtypeStruct((size, columns), keep.dtype) for size in sizes],
                 compiler_params=PARAMS,
                 cost_estimate=COST,
             )(keep, lax.ppermute(send, "tensor", swap), squares)
             for keep, send, squares in made
         ]
-        return [sums for sums, _ in added], added[0][1]
+        return [list(parts) for parts in zip(*[parts[1:] for parts in added])], added[0][0]
 
     def cross(sums):
         return [lax.ppermute(part, "tensor", shift(step)) for step, part in zip(others, sums)]
@@ -287,23 +294,26 @@
     hold = lax.optimization_barrier
     made = [product(norm_gain, step, *chunks[0], staged=True) for step in others]
     made, gain = hold((made, norm_gain))
-    sums = add_halves(made)
-    made = [product(gain, step, *chunks[1]) for step in others]
-    sums, made, gain, span_offset, live_blocks = hold((sums, made, gain, span_offset, live_blocks))
-
-    arrivals = [(cross(sums[0]), sums[1])]
+    sums = add_halves(made, chunks[0][1:])
+    sums, gain, span_offset, live_blocks = hold((sums, gain, span_offset, live_blocks))
+
+    arrivals = [([cross(part) for part in sums[0]], sums[1])]
     for index in range(1, chunk_count):
-        if index > 1:
-            made = [product(gain, step, *chunks[index]) for step in others]
-        sums = add_halves(made)
-        arrivals.append((cross(sums[0]), sums[1]))
+        made = [product(gain, step, *chunks[index]) for step in others]
+        count = chunks[index][1]
+        sums = add_halves(made, (count - 1, 1) if count > 2 else (count,))
+        arrivals.append(([cross(part) for part in sums[0]], sums[1]))
     own = [product(gain, 0, first, count, carrier=False) for first, count in chunks]
     table = tables(span_offset)
 
     result = None
     for (first, count), (keep, send), (arrived, squares) in zip(chunks, own, arrivals):
         received = lax.ppermute(send, "tensor", swap)
-        result = finish(first, count, keep, received, table, squares, arrived, result)
+        at = 0
+        for part in arrived:
+            size = part[0].shape[0] // TILE
+            result = finish(first, at, size, keep, received, table, squares, arrived[0], part, result)
+            at += size
     return result
 
 

time: 47.1 us -> 49.5 us (1.051)
  local copies, waits for them, and re-layouts: 0.04 us -> 4.78 us
  waiting for transfers between devices: 23.8 us -> 21.3 us
    unnamed x16 -> x12, local copies, waits for them, and re-layouts: 0.04 us -> 4.78 us
    ppermute x3 -> x4, waiting for transfers between devices: 22.8 us -> 19.7 us  [cross(): lax.ppermute(part, 'tensor', shift(step))]
    pallas_call x6 -> x7, Pallas kernels: 4.6 us -> 5.46 us  [the longest x4 5.05 us: finish(): pl.pallas_call(functools.partial(finish_kernel, first, at, count, chip_co...]
    pallas_call x6, Pallas kernels: 10.6 us -> 9.72 us  [product(): pl.pallas_call(functools.partial(product_kernel, step, chip_count, first,...]
    ppermute x3, waiting for transfers between devices: 1.04 us -> 1.57 us  [add_halves(): lax.ppermute(send, 'tensor', swap)]
    ppermute x3 -> x4, starting transfers between devices: 5.21 us -> 5.31 us  [cross(): lax.ppermute(part, 'tensor', shift(step))]
  transfers between devices with their start and end apart: 9 -> 10, of which waited for: 4 -> 4; matrix products, arithmetic and copies ran while one was open for 0% -> 0% of each run, Pallas kernels for 21% -> 23%
where the time goes in v14:
time: 49.5 us; the launch traced here: 49.3 us
  waiting for transfers between devices  21.3 us (43%)
  Pallas kernels  15.9 us (32%)
  starting transfers between devices  7.17 us (14%)
  local copies, waits for them, and re-layouts  4.78 us (10%)
    ppermute x4, waiting for transfers between devices, cross(): lax.ppermute(part, 'tensor', shift(step))  19.7 us
    pallas_call x6, Pallas kernels, product(): pl.pallas_call(functools.partial(product_kernel, step, chip_count, first,...  9.72 us
    ppermute x4, starting transfers between devices, cross(): lax.ppermute(part, 'tensor', shift(step))  5.31 us
    pallas_call x4, Pallas kernels, finish(): pl.pallas_call(functools.partial(finish_kernel, first, at, count, chip_co...  5.05 us
    unnamed x12, local copies, waits for them, and re-layouts  4.78 us
    ppermute x3, waiting for transfers between devices, add_halves(): lax.ppermute(send, 'tensor', swap)  1.57 us
    ppermute x3, starting transfers between devices, add_halves(): lax.ppermute(send, 'tensor', swap)  1.55 us
  transfers between devices with their start and end apart: 10, of which 4 were waited for; matrix products, arithmetic and copies ran while one was open for 0% of the time, Pallas kernels for 23%

profile of v14, /device:TPU:0, one launch (start us, length us, event | category | flops | bytes accessed | tf_op | source)
XLA Modules:
  0.0 49.3 jit_solution(2300500328560862064)
XLA Ops:
  0.0 0.0 copy-start.2
  0.0 0.7 %copy-done.2 = bf16[1024]{0:T(1024)(128)(2,1)S(1)} copy-done((bf16[1024]{0:T(1024)(128)(2,1)S(1)}, bf16[1024]{0:T(1024)(128)(2,1)}, u32[]{:S(2)}) %copy-start.2) | copy-done | bytes 2072
  0.7 3.1 %shard_map.64 = (bf16[512,512]{1,0:T(8,128)(2,1)S(1)}, bf16[528,512]{1,0:T(8,128)(2,1)S(1)}, f32[4,128]{1,0:T(4,128)S(1)}) custom-call(bf16[1536,1024]{1,0:T(8,128)(2,1)} %tokens.11, bf16[1024]{0:T(1024)(128)(2,1)S(1)} %copy-done.2, bf16[1024,2048]{1,0:T(8,128)(2,1)} %weight.11), custom_call_target="tpu_custom_call" | custom-call | flops 999999995904 | bytes 1 | tf_op jit(solution)/shard_map/pallas_call | solution.py:228
  3.8 0.5 %collective-permute-start = (bf16[528,512]{1,0:T(8,128)(2,1)S(1)}, bf16[528,512]{1,0:T(8,128)(2,1)S(1)}, u32[]{:S(2)}, u32[]{:S(2)}) collective-permute-start(bf16[528,512]{1,0:T(8,128)(2,1)S(1)} %get-tuple-element.45), channel_id=1, source_target_pairs={{0,1},{1,0},{2,3},{3,2},{4,5},{5,4},{6,7},{7,6},{8,9},{9,8},{10,11... | collective-permute-start | bytes 1622024 | tf_op jit(solution)/shard_map/ppermute | solution.py:286
  4.3 1.6 %collective-permute-done.received = bf16[528,512]{1,0:T(8,128)(2,1)S(1)} collective-permute-done((bf16[528,512]{1,0:T(8,128)(2,1)S(1)}, bf16[528,512]{1,0:T(8,128)(2,1)S(1)}, u32[]{:S(2)}, u32[]{:S(2)}) %collective-permute-start) | collective-permute-done | bytes 540704 | tf_op jit(solution)/shard_map/ppermute | solution.py:286
  5.8 0.1 shard_map.65
  6.0 2.9 %collective-permute-start.9 = (bf16[528,512]{1,0:T(8,128)(2,1)S(1)}, bf16[528,512]{1,0:T(8,128)(2,1)S(1)}, u32[]{:S(2)}, u32[]{:S(2)}) collective-permute-start(bf16[528,512]{1,0:T(8,128)(2,1)S(1)} %get-tuple-element.76), channel_id=1, source_target_pairs={{0,2},{1,3},{2,0},{3,1},{4,6},{5,7},{6,4},{7,5},{8,10},{9,11},{10,... | collective-permute-start | bytes 1622024 | tf_op jit(solution)/shard_map/ppermute | solution.py:292
  8.9 0.0 copy-start
  8.9 2.2 %copy-done = bf16[1024,2048]{1,0:T(8,128)(2,1)S(1)} copy-done((bf16[1024,2048]{1,0:T(8,128)(2,1)S(1)}, bf16[1024,2048]{1,0:T(8,128)(2,1)}, u32[]{:S(2)}) %copy-start) | copy-done | bytes 4194328
  11.1 0.0 copy-start.1
  11.1 1.9 %copy-done.1 = bf16[1536,1024]{1,0:T(8,128)(2,1)S(1)} copy-done((bf16[1536,1024]{1,0:T(8,128)(2,1)S(1)}, bf16[1536,1024]{1,0:T(8,128)(2,1)}, u32[]{:S(2)}) %copy-start.1) | copy-done | bytes 3145752
  13.0 1.3 %shard_map.73 = (bf16[512,512]{1,0:T(8,128)(2,1)S(1)}, bf16[512,512]{1,0:T(8,128)(2,1)S(1)}) custom-call(bf16[1536,1024]{1,0:T(8,128)(2,1)S(1)} %copy-done.1, bf16[1024]{0:T(1024)(128)(2,1)S(1)} %copy-done.2, bf16[1024,2048]{1,0:T(8,128)(2,1)S(1)} %copy-done), custom_call_target="tpu_custom_call" | custom-call | flops 1 | bytes 1 | tf_op jit(solution)/shard_map/pallas_call | solution.py:228
  14.3 0.1 collective-permute-start.8
  14.4 0.7 %shard_map.71 = (bf16[256,512]{1,0:T(8,128)(2,1)S(1)}, bf16[272,512]{1,0:T(8,128)(2,1)S(1)}, f32[2,128]{1,0:T(2,128)S(1)}) custom-call(bf16[1536,1024]{1,0:T(8,128)(2,1)S(1)} %copy-done.1, bf16[1024]{0:T(1024)(128)(2,1)S(1)} %copy-done.2, bf16[1024,2048]{1,0:T(8,128)(2,1)S(1)} %copy-done), custom_call_target="tpu_custom_call" | custom-call | flops 1 | bytes 1 | tf_op jit(solution)/shard_map/pallas_call | solution.py:228
  15.1 0.6 %collective-permute-start.6 = (bf16[272,512]{1,0:T(8,128)(2,1)S(1)}, bf16[272,512]{1,0:T(8,128)(2,1)S(1)}, u32[]{:S(2)}, u32[]{:S(2)}) collective-permute-start(bf16[272,512]{1,0:T(8,128)(2,1)S(1)} %get-tuple-element.69), channel_id=1, source_target_pairs={{0,1},{1,0},{2,3},{3,2},{4,5},{5,4},{6,7},{7,6},{8,9},{9,8},{10,11... | collective-permute-start | bytes 835592 | tf_op jit(solution)/shard_map/ppermute | solution.py:286
  15.7 0.7 %shard_map.70 = (bf16[256,512]{1,0:T(8,128)(2,1)S(1)}, bf16[256,512]{1,0:T(8,128)(2,1)S(1)}) custom-call(bf16[1536,1024]{1,0:T(8,128)(2,1)S(1)} %copy-done.1, bf16[1024]{0:T(1024)(128)(2,1)S(1)} %copy-done.2, bf16[1024,2048]{1,0:T(8,128)(2,1)S(1)} %copy-done), custom_call_target="tpu_custom_call" | custom-call | flops 1 | bytes 1 | tf_op jit(solution)/shard_map/pallas_call | solution.py:228
  16.4 2.0 %shard_map.68 = (bf16[768,512]{1,0:T(8,128)(2,1)S(1)}, bf16[784,512]{1,0:T(8,128)(2,1)S(1)}, f32[6,128]{1,0:T(8,128)S(1)}) custom-call(bf16[1536,1024]{1,0:T(8,128)(2,1)S(1)} %copy-done.1, bf16[1024]{0:T(1024)(128)(2,1)S(1)} %copy-done.2, bf16[1024,2048]{1,0:T(8,128)(2,1)S(1)} %copy-done), custom_call_target="tpu_custom_call" | custom-call | flops 1 | bytes 1 | tf_op jit(solution)/shard_map/pallas_call | solution.py:228
  18.4 0.0 copy-start.3
  18.4 0.0 copy-start.4
  18.5 0.0 copy-start.5
  18.5 1.9 %shard_map.66 = (bf16[768,512]{1,0:T(8,128)(2,1)S(1)}, bf16[768,512]{1,0:T(8,128)(2,1)S(1)}) custom-call(bf16[1536,1024]{1,0:T(8,128)(2,1)S(1)} %copy-done.1, bf16[1024]{0:T(1024)(128)(2,1)S(1)} %copy-done.2, bf16[1024,2048]{1,0:T(8,128)(2,1)S(1)} %copy-done), custom_call_target="tpu_custom_call" | custom-call | flops 1 | bytes 1 | tf_op jit(solution)/shard_map/pallas_call | solution.py:228
  20.4 0.1 collective-permute-start.5
  20.4 0.5 collective-permute-start.2
  20.9 0.0 copy-done.3
  20.9 0.0 copy-done.4
  20.9 0.0 copy-done.5
  20.9 0.7 %shard_map.67 = (s32[8,128]{1,0:T(8,128)S(1)}, f32[24,128]{1,0:T(8,128)S(1)}, f32[24,128]{1,0:T(8,128)S(1)}, f32[64,128]{1,0:T(8,128)S(1)}, f32[64,128]{1,0:T(8,128)S(1)}) custom-call(s32[4]{0:T(128)S(1)} %copy-done.3, s32[4]{0:T(128)S(1)} %copy-done.4, f32[1,128]{1,0:T(1,128)S(1)} %copy-done.5), custom_call_target="tpu_custom_call" | custom-call | flops 1 | bytes 1 | tf_op jit(solution)/shard_map/pallas_call | solution.py:242
  21.7 0.0 collective-permute-done.6.received
  21.7 0.1 collective-permute-start.1
  21.8 0.1 shard_map.72
  21.9 0.0 collective-permute-done.8.refs_1_
  21.9 0.2 collective-permute-start.7
  22.1 0.0 collective-permute-done.9.refs_8_
  22.1 1.4 %shard_map.74.refs_9_ = bf16[1536,512]{1,0:T(8,128)(2,1)} custom-call(bf16[512,512]{1,0:T(8,128)(2,1)S(1)} %get-tuple-element.73.refs_0_, bf16[512,512]{1,0:T(8,128)(2,1)S(1)} %collective-permute-done.8.refs_1_, s32[8,128]{1,0:T(8,128)S(1)} %get-tuple-element.55.refs_2_, f32[24,128]{1,0:T(8,128)S(1)} %get-tuple-element.56.refs_3_, ...), custom_call_target="tpu_custom_call" | custom-call | flops 20000000000 | bytes 1 | tf_op jit(solution)/shard_map/pallas_call | solution.py:259
  23.5 0.0 collective-permute-done.2.received
  23.5 0.2 shard_map.69
  23.7 2.0 %collective-permute-start.3 = (bf16[528,512]{1,0:T(8,128)(2,1)S(1)}, bf16[528,512]{1,0:T(8,128)(2,1)S(1)}, u32[]{:S(2)}, u32[]{:S(2)}) collective-permute-start(bf16[528,512]{1,0:T(8,128)(2,1)S(1)} %get-tuple-element.64), channel_id=1, source_target_pairs={{0,2},{1,3},{2,0},{3,1},{4,6},{5,7},{6,4},{7,5},{8,10},{9,11},{10,... | collective-permute-start | bytes 1622024 | tf_op jit(solution)/shard_map/ppermute | solution.py:292
  25.7 0.0 collective-permute-done.5.refs_1_
  25.7 5.7 %collective-permute-done.7.refs_8_ = bf16[272,512]{1,0:T(8,128)(2,1)S(1)} collective-permute-done((bf16[272,512]{1,0:T(8,128)(2,1)S(1)}, bf16[272,512]{1,0:T(8,128)(2,1)S(1)}, u32[]{:S(2)}, u32[]{:S(2)}) %collective-permute-start.7) | collective-permute-done | bytes 278560 | tf_op jit(solution)/shard_map/ppermute | solution.py:292
  31.4 1.1 %shard_map.75.refs_9_ = bf16[1536,512]{1,0:T(8,128)(2,1)} custom-call(bf16[256,512]{1,0:T(8,128)(2,1)S(1)} %get-tuple-element.66.refs_0_, bf16[256,512]{1,0:T(8,128)(2,1)S(1)} %collective-permute-done.5.refs_1_, s32[8,128]{1,0:T(8,128)S(1)} %get-tuple-element.55.refs_2_, f32[24,128]{1,0:T(8,128)S(1)} %get-tuple-element.56.refs_3_, ...), custom_call_target="tpu_custom_call", output_to_operand_aliasing={{}: (9, {})} | custom-call | flops 20000000000 | bytes 1 | tf_op jit(solution)/shard_map/pallas_call | solution.py:259
  32.5 0.2 collective-permute-start.4
  32.8 0.0 collective-permute-done.1.refs_1_
  32.8 10.2 %collective-permute-done.3.refs_8_ = bf16[528,512]{1,0:T(8,128)(2,1)S(1)} collective-permute-done((bf16[528,512]{1,0:T(8,128)(2,1)S(1)}, bf16[528,512]{1,0:T(8,128)(2,1)S(1)}, u32[]{:S(2)}, u32[]{:S(2)}) %collective-permute-start.3) | collective-permute-done | bytes 540704 | tf_op jit(solution)/shard_map/ppermute | solution.py:292
  43.0 1.4 %shard_map.76.refs_10_ = bf16[1536,512]{1,0:T(8,128)(2,1)} custom-call(bf16[768,512]{1,0:T(8,128)(2,1)S(1)} %get-tuple-element.51.refs_0_, bf16[768,512]{1,0:T(8,128)(2,1)S(1)} %collective-permute-done.1.refs_1_, s32[8,128]{1,0:T(8,128)S(1)} %get-tuple-element.55.refs_2_, f32[24,128]{1,0:T(8,128)S(1)} %get-tuple-element.56.refs_3_, ...), custom_call_target="tpu_custom_call", output_to_operand_aliasing={{}: (9, {})} | custom-call | flops 20000000000 | bytes 1 | tf_op jit(solution)/shard_map/pallas_call | solution.py:259
  44.4 3.7 %collective-permute-done.4.refs_9_ = bf16[256,512]{1,0:T(8,128)(2,1)S(1)} collective-permute-done((bf16[256,512]{1,0:T(8,128)(2,1)S(1)}, bf16[256,512]{1,0:T(8,128)(2,1)S(1)}, u32[]{:S(2)}, u32[]{:S(2)}) %collective-permute-start.4) | collective-permute-done | bytes 262176 | tf_op jit(solution)/shard_map/ppermute | solution.py:292
  48.2 1.1 %shard_map.77 = bf16[1536,512]{1,0:T(8,128)(2,1)} custom-call(bf16[768,512]{1,0:T(8,128)(2,1)S(1)} %get-tuple-element.51.refs_0_, bf16[768,512]{1,0:T(8,128)(2,1)S(1)} %collective-permute-done.1.refs_1_, s32[8,128]{1,0:T(8,128)S(1)} %get-tuple-element.55.refs_2_, f32[24,128]{1,0:T(8,128)S(1)} %get-tuple-element.56.refs_3_, ...), custom_call_target="tpu_custom_call", output_to_operand_aliasing={{}: (10, {})} | custom-call | flops 20000000000 | bytes 1 | tf_op jit(solution)/shard_map/pallas_call | solution.py:259
Async XLA Ops:
  0.0 0.7 %copy-start.2 = (bf16[1024]{0:T(1024)(128)(2,1)S(1)}, bf16[1024]{0:T(1024)(128)(2,1)}, u32[]{:S(2)}) copy-start(bf16[1024]{0:T(1024)(128)(2,1)} %gain.6) | copy-start | bytes 6148
  3.8 2.1 %collective-permute-start = (bf16[528,512]{1,0:T(8,128)(2,1)S(1)}, bf16[528,512]{1,0:T(8,128)(2,1)S(1)}, u32[]{:S(2)}, u32[]{:S(2)}) collective-permute-start(bf16[528,512]{1,0:T(8,128)(2,1)S(1)} %get-tuple-element.45), channel_id=1, source_target_pairs={{0,1},{1,0},{2,3},{3,2},{4,5},{5,4},{6,7},{7,6},{8,9},{9,8},{10,11... | collective-permute-start | bytes 1622024 | tf_op jit(solution)/shard_map/ppermute | solution.py:286
  6.0 16.1 %collective-permute-start.9 = (bf16[528,512]{1,0:T(8,128)(2,1)S(1)}, bf16[528,512]{1,0:T(8,128)(2,1)S(1)}, u32[]{:S(2)}, u32[]{:S(2)}) collective-permute-start(bf16[528,512]{1,0:T(8,128)(2,1)S(1)} %get-tuple-element.76), channel_id=1, source_target_pairs={{0,2},{1,3},{2,0},{3,1},{4,6},{5,7},{6,4},{7,5},{8,10},{9,11},{10,... | collective-permute-start | bytes 1622024 | tf_op jit(solution)/shard_map/ppermute | solution.py:292
  8.9 2.2 %copy-start = (bf16[1024,2048]{1,0:T(8,128)(2,1)S(1)}, bf16[1024,2048]{1,0:T(8,128)(2,1)}, u32[]{:S(2)}) copy-start(bf16[1024,2048]{1,0:T(8,128)(2,1)} %weight.11) | copy-start | bytes 12582916
  11.1 1.9 %copy-start.1 = (bf16[1536,1024]{1,0:T(8,128)(2,1)S(1)}, bf16[1536,1024]{1,0:T(8,128)(2,1)}, u32[]{:S(2)}) copy-start(bf16[1536,1024]{1,0:T(8,128)(2,1)} %tokens.11) | copy-start | bytes 9437188
  14.3 7.6 %collective-permute-start.8 = (bf16[512,512]{1,0:T(8,128)(2,1)S(1)}, bf16[512,512]{1,0:T(8,128)(2,1)S(1)}, u32[]{:S(2)}, u32[]{:S(2)}) collective-permute-start(bf16[512,512]{1,0:T(8,128)(2,1)S(1)} %get-tuple-element.74), channel_id=1, source_target_pairs={{0,1},{1,0},{2,3},{3,2},{4,5},{5,4},{6,7},{7,6},{8,9},{9,8},{10,11... | collective-permute-start | bytes 1572872 | tf_op jit(solution)/shard_map/ppermute | solution.py:311
  15.1 6.5 %collective-permute-start.6 = (bf16[272,512]{1,0:T(8,128)(2,1)S(1)}, bf16[272,512]{1,0:T(8,128)(2,1)S(1)}, u32[]{:S(2)}, u32[]{:S(2)}) collective-permute-start(bf16[272,512]{1,0:T(8,128)(2,1)S(1)} %get-tuple-element.69), channel_id=1, source_target_pairs={{0,1},{1,0},{2,3},{3,2},{4,5},{5,4},{6,7},{7,6},{8,9},{9,8},{10,11... | collective-permute-start | bytes 835592 | tf_op jit(solution)/shard_map/ppermute | solution.py:286
  18.4 2.5 %copy-start.3 = (s32[4]{0:T(128)S(1)}, s32[4]{0:T(128)}, u32[]{:S(2)}) copy-start(s32[4]{0:T(128)} %live) | copy-start | bytes 52
  18.4 2.5 %copy-start.4 = (s32[4]{0:T(128)S(1)}, s32[4]{0:T(128)}, u32[]{:S(2)}) copy-start(s32[4]{0:T(128)} %span) | copy-start | bytes 52
  18.5 2.5 %copy-start.5 = (f32[1,128]{1,0:T(1,128)S(1)}, f32[1,128]{1,0:T(1,128)}, u32[]{:S(2)}) copy-start(f32[1,128]{1,0:T(1,128)} %constant.4.clone.frequencies) | copy-start | bytes 1540
  20.4 5.3 %collective-permute-start.5 = (bf16[256,512]{1,0:T(8,128)(2,1)S(1)}, bf16[256,512]{1,0:T(8,128)(2,1)S(1)}, u32[]{:S(2)}, u32[]{:S(2)}) collective-permute-start(bf16[256,512]{1,0:T(8,128)(2,1)S(1)} %get-tuple-element.67), channel_id=1, source_target_pairs={{0,1},{1,0},{2,3},{3,2},{4,5},{5,4},{6,7},{7,6},{8,9},{9,8},{10,11... | collective-permute-start | bytes 786440 | tf_op jit(solution)/shard_map/ppermute | solution.py:311
  20.4 3.0 %collective-permute-start.2 = (bf16[784,512]{1,0:T(8,128)(2,1)S(1)}, bf16[784,512]{1,0:T(8,128)(2,1)S(1)}, u32[]{:S(2)}, u32[]{:S(2)}) collective-permute-start(bf16[784,512]{1,0:T(8,128)(2,1)S(1)} %get-tuple-element.61), channel_id=1, source_target_pairs={{0,1},{1,0},{2,3},{3,2},{4,5},{5,4},{6,7},{7,6},{8,9},{9,8},{10,11... | collective-permute-start | bytes 2408456 | tf_op jit(solution)/shard_map/ppermute | solution.py:286
  21.7 11.1 %collective-permute-start.1 = (bf16[768,512]{1,0:T(8,128)(2,1)S(1)}, bf16[768,512]{1,0:T(8,128)(2,1)S(1)}, u32[]{:S(2)}, u32[]{:S(2)}) collective-permute-start(bf16[768,512]{1,0:T(8,128)(2,1)S(1)} %get-tuple-element.52), channel_id=1, source_target_pairs={{0,1},{1,0},{2,3},{3,2},{4,5},{5,4},{6,7},{7,6},{8,9},{9,8},{10,11... | collective-permute-start | bytes 2359304 | tf_op jit(solution)/shard_map/ppermute | solution.py:311
  21.9 9.5 %collective-permute-start.7 = (bf16[272,512]{1,0:T(8,128)(2,1)S(1)}, bf16[272,512]{1,0:T(8,128)(2,1)S(1)}, u32[]{:S(2)}, u32[]{:S(2)}) collective-permute-start(bf16[272,512]{1,0:T(8,128)(2,1)S(1)} %get-tuple-element.72), channel_id=1, source_target_pairs={{0,2},{1,3},{2,0},{3,1},{4,6},{5,7},{6,4},{7,5},{8,10},{9,11},{10,... | collective-permute-start | bytes 835592 | tf_op jit(solution)/shard_map/ppermute | solution.py:292
  23.7 19.3 %collective-permute-start.3 = (bf16[528,512]{1,0:T(8,128)(2,1)S(1)}, bf16[528,512]{1,0:T(8,128)(2,1)S(1)}, u32[]{:S(2)}, u32[]{:S(2)}) collective-permute-start(bf16[528,512]{1,0:T(8,128)(2,1)S(1)} %get-tuple-element.64), channel_id=1, source_target_pairs={{0,2},{1,3},{2,0},{3,1},{4,6},{5,7},{6,4},{7,5},{8,10},{9,11},{10,... | collective-permute-start | bytes 1622024 | tf_op jit(solution)/shard_map/ppermute | solution.py:292
  32.5 15.6 %collective-permute-start.4 = (bf16[256,512]{1,0:T(8,128)(2,1)S(1)}, bf16[256,512]{1,0:T(8,128)(2,1)S(1)}, u32[]{:S(2)}, u32[]{:S(2)}) collective-permute-start(bf16[256,512]{1,0:T(8,128)(2,1)S(1)} %get-tuple-element.65), channel_id=1, source_target_pairs={{0,2},{1,3},{2,0},{3,1},{4,6},{5,7},{6,4},{7,5},{8,10},{9,11},{10,... | collective-permute-start | bytes 786440 | tf_op jit(solution)/shard_map/ppermute | solution.py:292

commit v15 on v14

--- a/solution.py
+++ b/solution.py
@@ -22,9 +22,8 @@
 CHUNKS = (2, 1, 3)
 
 PARAMS = pltpu.CompilerParams(vmem_limit_bytes=16 * 1024 * 1024)
-FIRST = pltpu.CompilerParams(vmem_limit_bytes=53248 * 1024)
+FIRST = pltpu.CompilerParams(vmem_limit_bytes=57344 * 1024)
 LATER = pl.CostEstimate(flops=20000000000, bytes_accessed=1, transcendentals=0)
-HEAVY = pl.CostEstimate(flops=1000000000000, bytes_accessed=1, transcendentals=0)
 COST = pl.CostEstimate(flops=1, bytes_accessed=1, transcendentals=0)
 
 
@@ -232,10 +231,10 @@
             out_specs=[vmem] * len(out_shape),
             scratch_shapes=scratch if staged else [],
             compiler_params=FIRST if staged else PARAMS,
-            cost_estimate=HEAVY if staged else COST,
+            cost_estimate=COST,
         )(tokens, gain, kv_weight)
 
-    def tables(span_offset):
+    def tables(live_blocks, span_offset):
         frequencies = rope_base ** (-(np.arange(HD // 2, dtype=np.float32) * 2.0) / HD)
         frequencies = np.concatenate([frequencies, frequencies])[None, :].astype(np.float32)
         shapes = [(slot_rows // BLOCK, HD)] * 2 + [(BLOCK, HD)] * 2
@@ -295,16 +294,20 @@
     made = [product(norm_gain, step, *chunks[0], staged=True) for step in others]
     made, gain = hold((made, norm_gain))
     sums = add_halves(made, chunks[0][1:])
-    sums, gain, span_offset, live_blocks = hold((sums, gain, span_offset, live_blocks))
+    made = [product(gain, step, *chunks[1]) for step in others]
+    sums, made, gain, span_offset, live_blocks = hold((sums, made, gain, span_offset, live_blocks))
 
     arrivals = [([cross(part) for part in sums[0]], sums[1])]
     for index in range(1, chunk_count):
-        made = [product(gain, step, *chunks[index]) for step in others]
+        if index > 1:
+            made = [product(gain, step, *chunks[index]) for step in others]
         count = chunks[index][1]
         sums = add_halves(made, (count - 1, 1) if count > 2 else (count,))
         arrivals.append(([cross(part) for part in sums[0]], sums[1]))
-    own = [product(gain, 0, first, count, carrier=False) for first, count in chunks]
-    table = tables(span_offset)
+    arrivals[0], late, span_offset, live_blocks = hold((arrivals[0], gain, span_offset, live_blocks))
+    own = [product(gain, 0, *chunk, carrier=False)[:2] for chunk in chunks[:-1]]
+    own.append(product(late, 0, *chunks[-1], carrier=False)[:2])
+    table = tables(live_blocks, span_offset)
 
     result = None
     for (first, count), (keep, send), (arrived, squares) in zip(chunks, own, arrivals):

time: 49.5 us -> 48.8 us (0.986)
  local copies, waits for them, and re-layouts: 4.78 us -> 0.04 us
  waiting for transfers between devices: 21.3 us -> 24 us
  Pallas kernels: 15.9 us -> 16.7 us
  starting transfers between devices: 7.17 us -> 7.75 us
    unnamed x12 -> x16, local copies, waits for them, and re-layouts: 4.78 us -> 0.04 us
    ppermute x4, waiting for transfers between devices: 19.7 us -> 22.9 us  [cross(): lax.ppermute(part, 'tensor', shift(step))]
    pallas_call x6, Pallas kernels: 9.72 us -> 10.5 us  [product(): pl.pallas_call(functools.partial(product_kernel, step, chip_count, first,...]
    ppermute x4, starting transfers between devices: 5.31 us -> 6.01 us  [cross(): lax.ppermute(part, 'tensor', shift(step))]
    ppermute x3, waiting for transfers between devices: 1.57 us -> 1.04 us  [add_halves(): lax.ppermute(send, 'tensor', swap)]
where the time goes in v15:
time: 48.8 us; the launch traced here: 48.6 us
  waiting for transfers between devices  24 us (49%)
  Pallas kernels  16.7 us (34%)
  starting transfers between devices  7.75 us (16%)
    ppermute x4, waiting for transfers between devices, cross(): lax.ppermute(part, 'tensor', shift(step))  22.9 us
    pallas_call x6, Pallas kernels, product(): pl.pallas_call(functools.partial(product_kernel, step, chip_count, first,...  10.5 us
    ppermute x4, starting transfers between devices, cross(): lax.ppermute(part, 'tensor', shift(step))  6.01 us
    pallas_call x4, Pallas kernels, finish(): pl.pallas_call(functools.partial(finish_kernel, first, at, count, chip_co...  5.03 us
    ppermute x3, starting transfers between devices, add_halves(): lax.ppermute(send, 'tensor', swap)  1.46 us
    ppermute x3, waiting for transfers between devices, add_halves(): lax.ppermute(send, 'tensor', swap)  1.04 us
  transfers between devices with their start and end apart: 10, of which 4 were waited for; matrix products, arithmetic and copies ran while one was open for 0% of the time, Pallas kernels for 23%

profile of v15, /device:TPU:0, one launch (start us, length us, event | category | flops | bytes accessed | tf_op | source)
XLA Modules:
  0.0 48.6 jit_solution(12433727535846228394)
XLA Ops:
  0.0 0.0 copy-start.3
  0.0 4.1 %shard_map.64 = (bf16[512,512]{1,0:T(8,128)(2,1)}, bf16[528,512]{1,0:T(8,128)(2,1)}, f32[4,128]{1,0:T(4,128)}) custom-call(bf16[1536,1024]{1,0:T(8,128)(2,1)} %tokens.11, bf16[1024]{0:T(1024)(128)(2,1)} %gain.6, bf16[1024,2048]{1,0:T(8,128)(2,1)} %weight.11), custom_call_target="tpu_custom_call" | custom-call | flops 1 | bytes 1 | tf_op jit(solution)/shard_map/pallas_call | solution.py:227
  4.1 0.0 copy-start.2
  4.1 0.0 copy-start.4
  4.1 0.5 %collective-permute-start = (bf16[528,512]{1,0:T(8,128)(2,1)}, bf16[528,512]{1,0:T(8,128)(2,1)S(1)}, u32[]{:S(2)}, u32[]{:S(2)}) collective-permute-start(bf16[528,512]{1,0:T(8,128)(2,1)} %get-tuple-element.53), channel_id=1, source_target_pairs={{0,1},{1,0},{2,3},{3,2},{4,5},{5,4},{6,7},{7,6},{8,9},{9,8},{10,11... | collective-permute-start | bytes 1622024 | tf_op jit(solution)/shard_map/ppermute | solution.py:285
  4.7 0.0 copy-done.3
  4.7 0.0 copy-done
  4.7 0.0 copy-done.1
  4.7 0.7 %shard_map.66 = (bf16[256,512]{1,0:T(8,128)(2,1)S(1)}, bf16[272,512]{1,0:T(8,128)(2,1)S(1)}, f32[2,128]{1,0:T(2,128)S(1)}) custom-call(bf16[1536,1024]{1,0:T(8,128)(2,1)S(1)} %copy-done.1, bf16[1024]{0:T(1024)(128)(2,1)S(1)} %copy-done.3, bf16[1024,2048]{1,0:T(8,128)(2,1)S(1)} %copy-done), custom_call_target="tpu_custom_call" | custom-call | flops 1 | bytes 1 | tf_op jit(solution)/shard_map/pallas_call | solution.py:227
  5.4 1.0 %collective-permute-done.received = bf16[528,512]{1,0:T(8,128)(2,1)S(1)} collective-permute-done((bf16[528,512]{1,0:T(8,128)(2,1)}, bf16[528,512]{1,0:T(8,128)(2,1)S(1)}, u32[]{:S(2)}, u32[]{:S(2)}) %collective-permute-start) | collective-permute-done | bytes 540704 | tf_op jit(solution)/shard_map/ppermute | solution.py:285
  6.4 0.0 copy-done.2
  6.4 0.0 copy-done.4
  6.4 0.1 shard_map.65
  6.6 2.9 %collective-permute-start.1 = (bf16[528,512]{1,0:T(8,128)(2,1)S(1)}, bf16[528,512]{1,0:T(8,128)(2,1)S(1)}, u32[]{:S(2)}, u32[]{:S(2)}) collective-permute-start(bf16[528,512]{1,0:T(8,128)(2,1)S(1)} %get-tuple-element.61), channel_id=1, source_target_pairs={{0,2},{1,3},{2,0},{3,1},{4,6},{5,7},{6,4},{7,5},{8,10},{9,11},{10,... | collective-permute-start | bytes 1622024 | tf_op jit(solution)/shard_map/ppermute | solution.py:291
  9.5 1.3 %shard_map.73 = (bf16[512,512]{1,0:T(8,128)(2,1)S(1)}, bf16[512,512]{1,0:T(8,128)(2,1)S(1)}) custom-call(bf16[1536,1024]{1,0:T(8,128)(2,1)S(1)} %copy-done.1, bf16[1024]{0:T(1024)(128)(2,1)S(1)} %copy-done.3, bf16[1024,2048]{1,0:T(8,128)(2,1)S(1)} %copy-done), custom_call_target="tpu_custom_call" | custom-call | flops 1 | bytes 1 | tf_op jit(solution)/shard_map/pallas_call | solution.py:227
  10.8 0.1 collective-permute-start.9
  10.9 0.5 %collective-permute-start.7 = (bf16[272,512]{1,0:T(8,128)(2,1)S(1)}, bf16[272,512]{1,0:T(8,128)(2,1)S(1)}, u32[]{:S(2)}, u32[]{:S(2)}) collective-permute-start(bf16[272,512]{1,0:T(8,128)(2,1)S(1)} %get-tuple-element.85), channel_id=1, source_target_pairs={{0,1},{1,0},{2,3},{3,2},{4,5},{5,4},{6,7},{7,6},{8,9},{9,8},{10,11... | collective-permute-start | bytes 835592 | tf_op jit(solution)/shard_map/ppermute | solution.py:285
  11.4 0.7 %shard_map.71 = (bf16[256,512]{1,0:T(8,128)(2,1)S(1)}, bf16[256,512]{1,0:T(8,128)(2,1)S(1)}) custom-call(bf16[1536,1024]{1,0:T(8,128)(2,1)S(1)} %copy-done.1, bf16[1024]{0:T(1024)(128)(2,1)S(1)} %copy-done.3, bf16[1024,2048]{1,0:T(8,128)(2,1)S(1)} %copy-done), custom_call_target="tpu_custom_call" | custom-call | flops 1 | bytes 1 | tf_op jit(solution)/shard_map/pallas_call | solution.py:227
  12.1 1.9 %shard_map.69 = (bf16[768,512]{1,0:T(8,128)(2,1)S(1)}, bf16[784,512]{1,0:T(8,128)(2,1)S(1)}, f32[6,128]{1,0:T(8,128)S(1)}) custom-call(bf16[1536,1024]{1,0:T(8,128)(2,1)S(1)} %copy-done.1, bf16[1024]{0:T(1024)(128)(2,1)S(1)} %copy-done.3, bf16[1024,2048]{1,0:T(8,128)(2,1)S(1)} %copy-done), custom_call_target="tpu_custom_call" | custom-call | flops 1 | bytes 1 | tf_op jit(solution)/shard_map/pallas_call | solution.py:227
  14.0 0.1 collective-permute-start.6
  14.2 0.4 collective-permute-start.3
  14.6 0.0 collective-permute-done.7.received
  14.6 0.1 shard_map.72
  14.7 0.0 copy-start.5
  14.7 0.0 copy-start.6
  14.7 0.0 copy-start.7
  14.7 0.1 collective-permute-start.8
  14.8 7.8 %collective-permute-done.1.refs_8_ = bf16[528,512]{1,0:T(8,128)(2,1)S(1)} collective-permute-done((bf16[528,512]{1,0:T(8,128)(2,1)S(1)}, bf16[528,512]{1,0:T(8,128)(2,1)S(1)}, u32[]{:S(2)}, u32[]{:S(2)}) %collective-permute-start.1) | collective-permute-done | bytes 540704 | tf_op jit(solution)/shard_map/ppermute | solution.py:291
  22.6 1.8 %shard_map.67 = (bf16[768,512]{1,0:T(8,128)(2,1)S(1)}, bf16[768,512]{1,0:T(8,128)(2,1)S(1)}) custom-call(bf16[1536,1024]{1,0:T(8,128)(2,1)S(1)} %copy-done.1, bf16[1024]{0:T(1024)(128)(2,1)S(1)} %copy-done.3, bf16[1024,2048]{1,0:T(8,128)(2,1)S(1)} %copy-done), custom_call_target="tpu_custom_call" | custom-call | flops 1 | bytes 1 | tf_op jit(solution)/shard_map/pallas_call | solution.py:227
  24.4 0.1 collective-permute-start.2
  24.5 0.0 copy-done.5
  24.5 0.0 copy-done.6
  24.5 0.0 copy-done.7
  24.5 0.7 %shard_map.68 = (s32[8,128]{1,0:T(8,128)S(1)}, f32[24,128]{1,0:T(8,128)S(1)}, f32[24,128]{1,0:T(8,128)S(1)}, f32[64,128]{1,0:T(8,128)S(1)}, f32[64,128]{1,0:T(8,128)S(1)}) custom-call(s32[4]{0:T(128)S(1)} %copy-done.5, s32[4]{0:T(128)S(1)} %copy-done.6, f32[1,128]{1,0:T(1,128)S(1)} %copy-done.7), custom_call_target="tpu_custom_call" | custom-call | flops 1 | bytes 1 | tf_op jit(solution)/shard_map/pallas_call | solution.py:241
  25.2 0.0 collective-permute-done.9.refs_1_
  25.2 1.4 %shard_map.74.refs_9_ = bf16[1536,512]{1,0:T(8,128)(2,1)} custom-call(bf16[512,512]{1,0:T(8,128)(2,1)S(1)} %get-tuple-element.89.refs_0_, bf16[512,512]{1,0:T(8,128)(2,1)S(1)} %collective-permute-done.9.refs_1_, s32[8,128]{1,0:T(8,128)S(1)} %get-tuple-element.71.refs_2_, f32[24,128]{1,0:T(8,128)S(1)} %get-tuple-element.72.refs_3_, ...), custom_call_target="tpu_custom_call" | custom-call | flops 20000000000 | bytes 1 | tf_op jit(solution)/shard_map/pallas_call | solution.py:258
  26.7 0.0 collective-permute-done.3.received
  26.7 0.2 shard_map.70
  26.9 2.1 %collective-permute-start.4 = (bf16[528,512]{1,0:T(8,128)(2,1)S(1)}, bf16[528,512]{1,0:T(8,128)(2,1)S(1)}, u32[]{:S(2)}, u32[]{:S(2)}) collective-permute-start(bf16[528,512]{1,0:T(8,128)(2,1)S(1)} %get-tuple-element.80), channel_id=1, source_target_pairs={{0,2},{1,3},{2,0},{3,1},{4,6},{5,7},{6,4},{7,5},{8,10},{9,11},{10,... | collective-permute-start | bytes 1622024 | tf_op jit(solution)/shard_map/ppermute | solution.py:291
  29.0 0.0 collective-permute-done.6.refs_1_
  29.0 0.0 collective-permute-done.8.refs_8_
  29.0 1.1 %shard_map.75.refs_9_ = bf16[1536,512]{1,0:T(8,128)(2,1)} custom-call(bf16[256,512]{1,0:T(8,128)(2,1)S(1)} %get-tuple-element.82.refs_0_, bf16[256,512]{1,0:T(8,128)(2,1)S(1)} %collective-permute-done.6.refs_1_, s32[8,128]{1,0:T(8,128)S(1)} %get-tuple-element.71.refs_2_, f32[24,128]{1,0:T(8,128)S(1)} %get-tuple-element.72.refs_3_, ...), custom_call_target="tpu_custom_call", output_to_operand_aliasing={{}: (9, {})} | custom-call | flops 20000000000 | bytes 1 | tf_op jit(solution)/shard_map/pallas_call | solution.py:258
  30.1 0.9 %collective-permute-start.5 = (bf16[256,512]{1,0:T(8,128)(2,1)S(1)}, bf16[256,512]{1,0:T(8,128)(2,1)S(1)}, u32[]{:S(2)}, u32[]{:S(2)}) collective-permute-start(bf16[256,512]{1,0:T(8,128)(2,1)S(1)} %get-tuple-element.81), channel_id=1, source_target_pairs={{0,2},{1,3},{2,0},{3,1},{4,6},{5,7},{6,4},{7,5},{8,10},{9,11},{10,... | collective-permute-start | bytes 786440 | tf_op jit(solution)/shard_map/ppermute | solution.py:291
  31.0 0.0 collective-permute-done.2.refs_1_
  31.0 11.2 %collective-permute-done.4.refs_8_ = bf16[528,512]{1,0:T(8,128)(2,1)S(1)} collective-permute-done((bf16[528,512]{1,0:T(8,128)(2,1)S(1)}, bf16[528,512]{1,0:T(8,128)(2,1)S(1)}, u32[]{:S(2)}, u32[]{:S(2)}) %collective-permute-start.4) | collective-permute-done | bytes 540704 | tf_op jit(solution)/shard_map/ppermute | solution.py:291
  42.1 1.4 %shard_map.76.refs_10_ = bf16[1536,512]{1,0:T(8,128)(2,1)} custom-call(bf16[768,512]{1,0:T(8,128)(2,1)S(1)} %get-tuple-element.67.refs_0_, bf16[768,512]{1,0:T(8,128)(2,1)S(1)} %collective-permute-done.2.refs_1_, s32[8,128]{1,0:T(8,128)S(1)} %get-tuple-element.71.refs_2_, f32[24,128]{1,0:T(8,128)S(1)} %get-tuple-element.72.refs_3_, ...), custom_call_target="tpu_custom_call", output_to_operand_aliasing={{}: (9, {})} | custom-call | flops 20000000000 | bytes 1 | tf_op jit(solution)/shard_map/pallas_call | solution.py:258
  43.5 4.0 %collective-permute-done.5.refs_9_ = bf16[256,512]{1,0:T(8,128)(2,1)S(1)} collective-permute-done((bf16[256,512]{1,0:T(8,128)(2,1)S(1)}, bf16[256,512]{1,0:T(8,128)(2,1)S(1)}, u32[]{:S(2)}, u32[]{:S(2)}) %collective-permute-start.5) | collective-permute-done | bytes 262176 | tf_op jit(solution)/shard_map/ppermute | solution.py:291
  47.5 1.1 %shard_map.77 = bf16[1536,512]{1,0:T(8,128)(2,1)} custom-call(bf16[768,512]{1,0:T(8,128)(2,1)S(1)} %get-tuple-element.67.refs_0_, bf16[768,512]{1,0:T(8,128)(2,1)S(1)} %collective-permute-done.2.refs_1_, s32[8,128]{1,0:T(8,128)S(1)} %get-tuple-element.71.refs_2_, f32[24,128]{1,0:T(8,128)S(1)} %get-tuple-element.72.refs_3_, ...), custom_call_target="tpu_custom_call", output_to_operand_aliasing={{}: (10, {})} | custom-call | flops 20000000000 | bytes 1 | tf_op jit(solution)/shard_map/pallas_call | solution.py:258
  (2 shorter events, 0.0 us)
Async XLA Ops:
  0.0 4.7 %copy-start.3 = (bf16[1024]{0:T(1024)(128)(2,1)S(1)}, bf16[1024]{0:T(1024)(128)(2,1)}, u32[]{:S(2)}) copy-start(bf16[1024]{0:T(1024)(128)(2,1)} %gain.6) | copy-start | bytes 6148
  0.0 4.7 %copy-start = (bf16[1024,2048]{1,0:T(8,128)(2,1)S(1)}, bf16[1024,2048]{1,0:T(8,128)(2,1)}, u32[]{:S(2)}) copy-start(bf16[1024,2048]{1,0:T(8,128)(2,1)} %weight.11) | copy-start | bytes 12582916
  0.0 4.7 %copy-start.1 = (bf16[1536,1024]{1,0:T(8,128)(2,1)S(1)}, bf16[1536,1024]{1,0:T(8,128)(2,1)}, u32[]{:S(2)}) copy-start(bf16[1536,1024]{1,0:T(8,128)(2,1)} %tokens.11) | copy-start | bytes 9437188
  4.1 2.3 %copy-start.2 = (bf16[512,512]{1,0:T(8,128)(2,1)S(1)}, bf16[512,512]{1,0:T(8,128)(2,1)}, u32[]{:S(2)}) copy-start(bf16[512,512]{1,0:T(8,128)(2,1)} %get-tuple-element.52.keep) | copy-start | bytes 1572868
  4.1 2.3 %copy-start.4 = (f32[4,128]{1,0:T(4,128)S(1)}, f32[4,128]{1,0:T(4,128)}, u32[]{:S(2)}) copy-start(f32[4,128]{1,0:T(4,128)} %get-tuple-element.54.squares) | copy-start | bytes 6148
  4.1 2.3 %collective-permute-start = (bf16[528,512]{1,0:T(8,128)(2,1)}, bf16[528,512]{1,0:T(8,128)(2,1)S(1)}, u32[]{:S(2)}, u32[]{:S(2)}) collective-permute-start(bf16[528,512]{1,0:T(8,128)(2,1)} %get-tuple-element.53), channel_id=1, source_target_pairs={{0,1},{1,0},{2,3},{3,2},{4,5},{5,4},{6,7},{7,6},{8,9},{9,8},{10,11... | collective-permute-start | bytes 1622024 | tf_op jit(solution)/shard_map/ppermute | solution.py:285
  6.6 16.0 %collective-permute-start.1 = (bf16[528,512]{1,0:T(8,128)(2,1)S(1)}, bf16[528,512]{1,0:T(8,128)(2,1)S(1)}, u32[]{:S(2)}, u32[]{:S(2)}) collective-permute-start(bf16[528,512]{1,0:T(8,128)(2,1)S(1)} %get-tuple-element.61), channel_id=1, source_target_pairs={{0,2},{1,3},{2,0},{3,1},{4,6},{5,7},{6,4},{7,5},{8,10},{9,11},{10,... | collective-permute-start | bytes 1622024 | tf_op jit(solution)/shard_map/ppermute | solution.py:291
  10.8 14.4 %collective-permute-start.9 = (bf16[512,512]{1,0:T(8,128)(2,1)S(1)}, bf16[512,512]{1,0:T(8,128)(2,1)S(1)}, u32[]{:S(2)}, u32[]{:S(2)}) collective-permute-start(bf16[512,512]{1,0:T(8,128)(2,1)S(1)} %get-tuple-element.90), channel_id=1, source_target_pairs={{0,1},{1,0},{2,3},{3,2},{4,5},{5,4},{6,7},{7,6},{8,9},{9,8},{10,11... | collective-permute-start | bytes 1572872 | tf_op jit(solution)/shard_map/ppermute | solution.py:314
  10.9 3.7 %collective-permute-start.7 = (bf16[272,512]{1,0:T(8,128)(2,1)S(1)}, bf16[272,512]{1,0:T(8,128)(2,1)S(1)}, u32[]{:S(2)}, u32[]{:S(2)}) collective-permute-start(bf16[272,512]{1,0:T(8,128)(2,1)S(1)} %get-tuple-element.85), channel_id=1, source_target_pairs={{0,1},{1,0},{2,3},{3,2},{4,5},{5,4},{6,7},{7,6},{8,9},{9,8},{10,11... | collective-permute-start | bytes 835592 | tf_op jit(solution)/shard_map/ppermute | solution.py:285
  14.0 15.0 %collective-permute-start.6 = (bf16[256,512]{1,0:T(8,128)(2,1)S(1)}, bf16[256,512]{1,0:T(8,128)(2,1)S(1)}, u32[]{:S(2)}, u32[]{:S(2)}) collective-permute-start(bf16[256,512]{1,0:T(8,128)(2,1)S(1)} %get-tuple-element.83), channel_id=1, source_target_pairs={{0,1},{1,0},{2,3},{3,2},{4,5},{5,4},{6,7},{7,6},{8,9},{9,8},{10,11... | collective-permute-start | bytes 786440 | tf_op jit(solution)/shard_map/ppermute | solution.py:314
  14.2 12.5 %collective-permute-start.3 = (bf16[784,512]{1,0:T(8,128)(2,1)S(1)}, bf16[784,512]{1,0:T(8,128)(2,1)S(1)}, u32[]{:S(2)}, u32[]{:S(2)}) collective-permute-start(bf16[784,512]{1,0:T(8,128)(2,1)S(1)} %get-tuple-element.77), channel_id=1, source_target_pairs={{0,1},{1,0},{2,3},{3,2},{4,5},{5,4},{6,7},{7,6},{8,9},{9,8},{10,11... | collective-permute-start | bytes 2408456 | tf_op jit(solution)/shard_map/ppermute | solution.py:285
  14.7 9.8 %copy-start.5 = (s32[4]{0:T(128)S(1)}, s32[4]{0:T(128)}, u32[]{:S(2)}) copy-start(s32[4]{0:T(128)} %live) | copy-start | bytes 52
  14.7 9.8 %copy-start.6 = (s32[4]{0:T(128)S(1)}, s32[4]{0:T(128)}, u32[]{:S(2)}) copy-start(s32[4]{0:T(128)} %span) | copy-start | bytes 52
  14.7 9.8 %copy-start.7 = (f32[1,128]{1,0:T(1,128)S(1)}, f32[1,128]{1,0:T(1,128)}, u32[]{:S(2)}) copy-start(f32[1,128]{1,0:T(1,128)} %constant.4.clone.frequencies) | copy-start | bytes 1540
  14.7 14.3 %collective-permute-start.8 = (bf16[272,512]{1,0:T(8,128)(2,1)S(1)}, bf16[272,512]{1,0:T(8,128)(2,1)S(1)}, u32[]{:S(2)}, u32[]{:S(2)}) collective-permute-start(bf16[272,512]{1,0:T(8,128)(2,1)S(1)} %get-tuple-element.88), channel_id=1, source_target_pairs={{0,2},{1,3},{2,0},{3,1},{4,6},{5,7},{6,4},{7,5},{8,10},{9,11},{10,... | collective-permute-start | bytes 835592 | tf_op jit(solution)/shard_map/ppermute | solution.py:291
  24.4 6.6 %collective-permute-start.2 = (bf16[768,512]{1,0:T(8,128)(2,1)S(1)}, bf16[768,512]{1,0:T(8,128)(2,1)S(1)}, u32[]{:S(2)}, u32[]{:S(2)}) collective-permute-start(bf16[768,512]{1,0:T(8,128)(2,1)S(1)} %get-tuple-element.68), channel_id=1, source_target_pairs={{0,1},{1,0},{2,3},{3,2},{4,5},{5,4},{6,7},{7,6},{8,9},{9,8},{10,11... | collective-permute-start | bytes 2359304 | tf_op jit(solution)/shard_map/ppermute | solution.py:314
  26.9 15.3 %collective-permute-start.4 = (bf16[528,512]{1,0:T(8,128)(2,1)S(1)}, bf16[528,512]{1,0:T(8,128)(2,1)S(1)}, u32[]{:S(2)}, u32[]{:S(2)}) collective-permute-start(bf16[528,512]{1,0:T(8,128)(2,1)S(1)} %get-tuple-element.80), channel_id=1, source_target_pairs={{0,2},{1,3},{2,0},{3,1},{4,6},{5,7},{6,4},{7,5},{8,10},{9,11},{10,... | collective-permute-start | bytes 1622024 | tf_op jit(solution)/shard_map/ppermute | solution.py:291
  30.1 17.4 %collective-permute-start.5 = (bf16[256,512]{1,0:T(8,128)(2,1)S(1)}, bf16[256,512]{1,0:T(8,128)(2,1)S(1)}, u32[]{:S(2)}, u32[]{:S(2)}) collective-permute-start(bf16[256,512]{1,0:T(8,128)(2,1)S(1)} %get-tuple-element.81), channel_id=1, source_target_pairs={{0,2},{1,3},{2,0},{3,1},{4,6},{5,7},{6,4},{7,5},{8,10},{9,11},{10,... | collective-permute-start | bytes 786440 | tf_op jit(solution)/shard_map/ppermute | solution.py:291

commit v16 on v15

--- a/solution.py
+++ b/solution.py
@@ -22,7 +22,7 @@
 CHUNKS = (2, 1, 3)
 
 PARAMS = pltpu.CompilerParams(vmem_limit_bytes=16 * 1024 * 1024)
-FIRST = pltpu.CompilerParams(vmem_limit_bytes=57344 * 1024)
+FIRST = pltpu.CompilerParams(vmem_limit_bytes=56 * 1024 * 1024)
 LATER = pl.CostEstimate(flops=20000000000, bytes_accessed=1, transcendentals=0)
 COST = pl.CostEstimate(flops=1, bytes_accessed=1, transcendentals=0)
 
@@ -234,7 +234,7 @@
             cost_estimate=COST,
         )(tokens, gain, kv_weight)
 
-    def tables(live_blocks, span_offset):
+    def tables(span_offset):
         frequencies = rope_base ** (-(np.arange(HD // 2, dtype=np.float32) * 2.0) / HD)
         frequencies = np.concatenate([frequencies, frequencies])[None, :].astype(np.float32)
         shapes = [(slot_rows // BLOCK, HD)] * 2 + [(BLOCK, HD)] * 2
@@ -304,10 +304,8 @@
         count = chunks[index][1]
         sums = add_halves(made, (count - 1, 1) if count > 2 else (count,))
         arrivals.append(([cross(part) for part in sums[0]], sums[1]))
-    arrivals[0], late, span_offset, live_blocks = hold((arrivals[0], gain, span_offset, live_blocks))
-    own = [product(gain, 0, *chunk, carrier=False)[:2] for chunk in chunks[:-1]]
-    own.append(product(late, 0, *chunks[-1], carrier=False)[:2])
-    table = tables(live_blocks, span_offset)
+    own = [product(gain, 0, first, count, carrier=False) for first, count in chunks]
+    table = tables(span_offset)
 
     result = None
     for (first, count), (keep, send), (arrived, squares) in zip(chunks, own, arrivals):

time: 48.8 us -> 46.5 us (0.953)
  waiting for transfers between devices: 24 us -> 20.3 us
  starting transfers between devices: 7.75 us -> 9.15 us
    ppermute x4, waiting for transfers between devices: 22.9 us -> 19.3 us  [cross(): lax.ppermute(part, 'tensor', shift(step))]
    ppermute x4, starting transfers between devices: 6.01 us -> 7.33 us  [cross(): lax.ppermute(part, 'tensor', shift(step))]
  transfers between devices with their start and end apart: 10 -> 10, of which waited for: 4 -> 5; matrix products, arithmetic and copies ran while one was open for 0% -> 0% of each run, Pallas kernels for 23% -> 24%
where the time goes in v16:
time: 46.5 us; the launch traced here: 46.4 us
  waiting for transfers between devices  20.3 us (44%)
  Pallas kernels  16.7 us (36%)
  starting transfers between devices  9.15 us (20%)
    ppermute x4, waiting for transfers between devices, cross(): lax.ppermute(part, 'tensor', shift(step))  19.3 us
    pallas_call x6, Pallas kernels, product(): pl.pallas_call(functools.partial(product_kernel, step, chip_count, first,...  10.6 us
    ppermute x4, starting transfers between devices, cross(): lax.ppermute(part, 'tensor', shift(step))  7.33 us
    pallas_call x4, Pallas kernels, finish(): pl.pallas_call(functools.partial(finish_kernel, first, at, count, chip_co...  5 us
    ppermute x3, starting transfers between devices, add_halves(): lax.ppermute(send, 'tensor', swap)  1.47 us
    ppermute x3, waiting for transfers between devices, add_halves(): lax.ppermute(send, 'tensor', swap)  1.04 us
  transfers between devices with their start and end apart: 10, of which 5 were waited for; matrix products, arithmetic and copies ran while one was open for 0% of the time, Pallas kernels for 24%

profile of v16, /device:TPU:0, one launch (start us, length us, event | category | flops | bytes accessed | tf_op | source)
XLA Modules:
  0.0 46.4 jit_solution(4601242878835170082)
XLA Ops:
  0.0 0.0 copy-start.3
  0.0 4.1 %shard_map.64 = (bf16[512,512]{1,0:T(8,128)(2,1)}, bf16[528,512]{1,0:T(8,128)(2,1)}, f32[4,128]{1,0:T(4,128)}) custom-call(bf16[1536,1024]{1,0:T(8,128)(2,1)} %tokens.11, bf16[1024]{0:T(1024)(128)(2,1)} %gain.6, bf16[1024,2048]{1,0:T(8,128)(2,1)} %weight.11), custom_call_target="tpu_custom_call" | custom-call | flops 1 | bytes 1 | tf_op jit(solution)/shard_map/pallas_call | solution.py:227
  4.1 0.0 copy-start.2
  4.1 0.0 copy-start.4
  4.1 0.5 %collective-permute-start = (bf16[528,512]{1,0:T(8,128)(2,1)}, bf16[528,512]{1,0:T(8,128)(2,1)S(1)}, u32[]{:S(2)}, u32[]{:S(2)}) collective-permute-start(bf16[528,512]{1,0:T(8,128)(2,1)} %get-tuple-element.48), channel_id=1, source_target_pairs={{0,1},{1,0},{2,3},{3,2},{4,5},{5,4},{6,7},{7,6},{8,9},{9,8},{10,11... | collective-permute-start | bytes 1622024 | tf_op jit(solution)/shard_map/ppermute | solution.py:285
  4.7 0.0 copy-done.3
  4.7 0.0 copy-done
  4.7 0.0 copy-done.1
  4.7 0.7 %shard_map.66 = (bf16[256,512]{1,0:T(8,128)(2,1)S(1)}, bf16[272,512]{1,0:T(8,128)(2,1)S(1)}, f32[2,128]{1,0:T(2,128)S(1)}) custom-call(bf16[1536,1024]{1,0:T(8,128)(2,1)S(1)} %copy-done.1, bf16[1024]{0:T(1024)(128)(2,1)S(1)} %copy-done.3, bf16[1024,2048]{1,0:T(8,128)(2,1)S(1)} %copy-done), custom_call_target="tpu_custom_call" | custom-call | flops 1 | bytes 1 | tf_op jit(solution)/shard_map/pallas_call | solution.py:227
  5.4 1.0 %collective-permute-done.received = bf16[528,512]{1,0:T(8,128)(2,1)S(1)} collective-permute-done((bf16[528,512]{1,0:T(8,128)(2,1)}, bf16[528,512]{1,0:T(8,128)(2,1)S(1)}, u32[]{:S(2)}, u32[]{:S(2)}) %collective-permute-start) | collective-permute-done | bytes 540704 | tf_op jit(solution)/shard_map/ppermute | solution.py:285
  6.4 0.0 copy-done.2
  6.4 0.0 copy-done.4
  6.4 0.1 shard_map.65
  6.6 2.9 %collective-permute-start.9 = (bf16[528,512]{1,0:T(8,128)(2,1)S(1)}, bf16[528,512]{1,0:T(8,128)(2,1)S(1)}, u32[]{:S(2)}, u32[]{:S(2)}) collective-permute-start(bf16[528,512]{1,0:T(8,128)(2,1)S(1)} %get-tuple-element.82), channel_id=1, source_target_pairs={{0,2},{1,3},{2,0},{3,1},{4,6},{5,7},{6,4},{7,5},{8,10},{9,11},{10,... | collective-permute-start | bytes 1622024 | tf_op jit(solution)/shard_map/ppermute | solution.py:291
  9.5 1.3 %shard_map.73 = (bf16[512,512]{1,0:T(8,128)(2,1)S(1)}, bf16[512,512]{1,0:T(8,128)(2,1)S(1)}) custom-call(bf16[1536,1024]{1,0:T(8,128)(2,1)S(1)} %copy-done.1, bf16[1024]{0:T(1024)(128)(2,1)S(1)} %copy-done.3, bf16[1024,2048]{1,0:T(8,128)(2,1)S(1)} %copy-done), custom_call_target="tpu_custom_call" | custom-call | flops 1 | bytes 1 | tf_op jit(solution)/shard_map/pallas_call | solution.py:227
  10.8 0.1 collective-permute-start.8
  10.9 0.5 %collective-permute-start.6 = (bf16[272,512]{1,0:T(8,128)(2,1)S(1)}, bf16[272,512]{1,0:T(8,128)(2,1)S(1)}, u32[]{:S(2)}, u32[]{:S(2)}) collective-permute-start(bf16[272,512]{1,0:T(8,128)(2,1)S(1)} %get-tuple-element.75), channel_id=1, source_target_pairs={{0,1},{1,0},{2,3},{3,2},{4,5},{5,4},{6,7},{7,6},{8,9},{9,8},{10,11... | collective-permute-start | bytes 835592 | tf_op jit(solution)/shard_map/ppermute | solution.py:285
  11.4 0.7 %shard_map.71 = (bf16[256,512]{1,0:T(8,128)(2,1)S(1)}, bf16[256,512]{1,0:T(8,128)(2,1)S(1)}) custom-call(bf16[1536,1024]{1,0:T(8,128)(2,1)S(1)} %copy-done.1, bf16[1024]{0:T(1024)(128)(2,1)S(1)} %copy-done.3, bf16[1024,2048]{1,0:T(8,128)(2,1)S(1)} %copy-done), custom_call_target="tpu_custom_call" | custom-call | flops 1 | bytes 1 | tf_op jit(solution)/shard_map/pallas_call | solution.py:227
  12.1 1.9 %shard_map.69 = (bf16[768,512]{1,0:T(8,128)(2,1)S(1)}, bf16[784,512]{1,0:T(8,128)(2,1)S(1)}, f32[6,128]{1,0:T(8,128)S(1)}) custom-call(bf16[1536,1024]{1,0:T(8,128)(2,1)S(1)} %copy-done.1, bf16[1024]{0:T(1024)(128)(2,1)S(1)} %copy-done.3, bf16[1024,2048]{1,0:T(8,128)(2,1)S(1)} %copy-done), custom_call_target="tpu_custom_call" | custom-call | flops 1 | bytes 1 | tf_op jit(solution)/shard_map/pallas_call | solution.py:227
  14.0 0.0 copy-start.5
  14.0 0.0 copy-start.6
  14.0 0.0 copy-start.7
  14.1 1.8 %shard_map.67 = (bf16[768,512]{1,0:T(8,128)(2,1)S(1)}, bf16[768,512]{1,0:T(8,128)(2,1)S(1)}) custom-call(bf16[1536,1024]{1,0:T(8,128)(2,1)S(1)} %copy-done.1, bf16[1024]{0:T(1024)(128)(2,1)S(1)} %copy-done.3, bf16[1024,2048]{1,0:T(8,128)(2,1)S(1)} %copy-done), custom_call_target="tpu_custom_call" | custom-call | flops 1 | bytes 1 | tf_op jit(solution)/shard_map/pallas_call | solution.py:227
  15.9 0.1 collective-permute-start.5
  16.0 0.4 collective-permute-start.2
  16.5 0.0 copy-done.5
  16.5 0.0 copy-done.6
  16.5 0.0 copy-done.7
  16.5 0.7 %shard_map.68 = (s32[8,128]{1,0:T(8,128)S(1)}, f32[24,128]{1,0:T(8,128)S(1)}, f32[24,128]{1,0:T(8,128)S(1)}, f32[64,128]{1,0:T(8,128)S(1)}, f32[64,128]{1,0:T(8,128)S(1)}) custom-call(s32[4]{0:T(128)S(1)} %copy-done.5, s32[4]{0:T(128)S(1)} %copy-done.6, f32[1,128]{1,0:T(1,128)S(1)} %copy-done.7), custom_call_target="tpu_custom_call" | custom-call | flops 1 | bytes 1 | tf_op jit(solution)/shard_map/pallas_call | solution.py:241
  17.2 0.0 collective-permute-done.6.received
  17.2 0.1 collective-permute-start.1
  17.4 0.1 shard_map.72
  17.4 0.0 collective-permute-done.8.refs_1_
  17.4 0.2 collective-permute-start.7
  17.6 5.0 %collective-permute-done.9.refs_8_ = bf16[528,512]{1,0:T(8,128)(2,1)S(1)} collective-permute-done((bf16[528,512]{1,0:T(8,128)(2,1)S(1)}, bf16[528,512]{1,0:T(8,128)(2,1)S(1)}, u32[]{:S(2)}, u32[]{:S(2)}) %collective-permute-start.9) | collective-permute-done | bytes 540704 | tf_op jit(solution)/shard_map/ppermute | solution.py:291
  22.6 1.4 %shard_map.74.refs_9_ = bf16[1536,512]{1,0:T(8,128)(2,1)} custom-call(bf16[512,512]{1,0:T(8,128)(2,1)S(1)} %get-tuple-element.79.refs_0_, bf16[512,512]{1,0:T(8,128)(2,1)S(1)} %collective-permute-done.8.refs_1_, s32[8,128]{1,0:T(8,128)S(1)} %get-tuple-element.61.refs_2_, f32[24,128]{1,0:T(8,128)S(1)} %get-tuple-element.62.refs_3_, ...), custom_call_target="tpu_custom_call" | custom-call | flops 20000000000 | bytes 1 | tf_op jit(solution)/shard_map/pallas_call | solution.py:258
  24.0 0.0 collective-permute-done.2.received
  24.0 0.2 shard_map.70
  24.2 2.1 %collective-permute-start.3 = (bf16[528,512]{1,0:T(8,128)(2,1)S(1)}, bf16[528,512]{1,0:T(8,128)(2,1)S(1)}, u32[]{:S(2)}, u32[]{:S(2)}) collective-permute-start(bf16[528,512]{1,0:T(8,128)(2,1)S(1)} %get-tuple-element.70), channel_id=1, source_target_pairs={{0,2},{1,3},{2,0},{3,1},{4,6},{5,7},{6,4},{7,5},{8,10},{9,11},{10,... | collective-permute-start | bytes 1622024 | tf_op jit(solution)/shard_map/ppermute | solution.py:291
  26.3 0.0 collective-permute-done.5.refs_1_
  26.3 2.2 %collective-permute-done.7.refs_8_ = bf16[272,512]{1,0:T(8,128)(2,1)S(1)} collective-permute-done((bf16[272,512]{1,0:T(8,128)(2,1)S(1)}, bf16[272,512]{1,0:T(8,128)(2,1)S(1)}, u32[]{:S(2)}, u32[]{:S(2)}) %collective-permute-start.7) | collective-permute-done | bytes 278560 | tf_op jit(solution)/shard_map/ppermute | solution.py:291
  28.5 1.1 %shard_map.75.refs_9_ = bf16[1536,512]{1,0:T(8,128)(2,1)} custom-call(bf16[256,512]{1,0:T(8,128)(2,1)S(1)} %get-tuple-element.72.refs_0_, bf16[256,512]{1,0:T(8,128)(2,1)S(1)} %collective-permute-done.5.refs_1_, s32[8,128]{1,0:T(8,128)S(1)} %get-tuple-element.61.refs_2_, f32[24,128]{1,0:T(8,128)S(1)} %get-tuple-element.62.refs_3_, ...), custom_call_target="tpu_custom_call", output_to_operand_aliasing={{}: (9, {})} | custom-call | flops 20000000000 | bytes 1 | tf_op jit(solution)/shard_map/pallas_call | solution.py:258
  29.7 2.1 %collective-permute-start.4 = (bf16[256,512]{1,0:T(8,128)(2,1)S(1)}, bf16[256,512]{1,0:T(8,128)(2,1)S(1)}, u32[]{:S(2)}, u32[]{:S(2)}) collective-permute-start(bf16[256,512]{1,0:T(8,128)(2,1)S(1)} %get-tuple-element.71), channel_id=1, source_target_pairs={{0,2},{1,3},{2,0},{3,1},{4,6},{5,7},{6,4},{7,5},{8,10},{9,11},{10,... | collective-permute-start | bytes 786440 | tf_op jit(solution)/shard_map/ppermute | solution.py:291
  31.8 0.0 collective-permute-done.1.refs_1_
  31.8 8.3 %collective-permute-done.3.refs_8_ = bf16[528,512]{1,0:T(8,128)(2,1)S(1)} collective-permute-done((bf16[528,512]{1,0:T(8,128)(2,1)S(1)}, bf16[528,512]{1,0:T(8,128)(2,1)S(1)}, u32[]{:S(2)}, u32[]{:S(2)}) %collective-permute-start.3) | collective-permute-done | bytes 540704 | tf_op jit(solution)/shard_map/ppermute | solution.py:291
  40.1 1.4 %shard_map.76.refs_10_ = bf16[1536,512]{1,0:T(8,128)(2,1)} custom-call(bf16[768,512]{1,0:T(8,128)(2,1)S(1)} %get-tuple-element.57.refs_0_, bf16[768,512]{1,0:T(8,128)(2,1)S(1)} %collective-permute-done.1.refs_1_, s32[8,128]{1,0:T(8,128)S(1)} %get-tuple-element.61.refs_2_, f32[24,128]{1,0:T(8,128)S(1)} %get-tuple-element.62.refs_3_, ...), custom_call_target="tpu_custom_call", output_to_operand_aliasing={{}: (9, {})} | custom-call | flops 20000000000 | bytes 1 | tf_op jit(solution)/shard_map/pallas_call | solution.py:258
  41.5 3.7 %collective-permute-done.4.refs_9_ = bf16[256,512]{1,0:T(8,128)(2,1)S(1)} collective-permute-done((bf16[256,512]{1,0:T(8,128)(2,1)S(1)}, bf16[256,512]{1,0:T(8,128)(2,1)S(1)}, u32[]{:S(2)}, u32[]{:S(2)}) %collective-permute-start.4) | collective-permute-done | bytes 262176 | tf_op jit(solution)/shard_map/ppermute | solution.py:291
  45.3 1.1 %shard_map.77 = bf16[1536,512]{1,0:T(8,128)(2,1)} custom-call(bf16[768,512]{1,0:T(8,128)(2,1)S(1)} %get-tuple-element.57.refs_0_, bf16[768,512]{1,0:T(8,128)(2,1)S(1)} %collective-permute-done.1.refs_1_, s32[8,128]{1,0:T(8,128)S(1)} %get-tuple-element.61.refs_2_, f32[24,128]{1,0:T(8,128)S(1)} %get-tuple-element.62.refs_3_, ...), custom_call_target="tpu_custom_call", output_to_operand_aliasing={{}: (10, {})} | custom-call | flops 20000000000 | bytes 1 | tf_op jit(solution)/shard_map/pallas_call | solution.py:258
  (2 shorter events, 0.0 us)
Async XLA Ops:
  0.0 4.7 %copy-start.3 = (bf16[1024]{0:T(1024)(128)(2,1)S(1)}, bf16[1024]{0:T(1024)(128)(2,1)}, u32[]{:S(2)}) copy-start(bf16[1024]{0:T(1024)(128)(2,1)} %gain.6) | copy-start | bytes 6148
  0.0 4.7 %copy-start = (bf16[1024,2048]{1,0:T(8,128)(2,1)S(1)}, bf16[1024,2048]{1,0:T(8,128)(2,1)}, u32[]{:S(2)}) copy-start(bf16[1024,2048]{1,0:T(8,128)(2,1)} %weight.11) | copy-start | bytes 12582916
  0.0 4.7 %copy-start.1 = (bf16[1536,1024]{1,0:T(8,128)(2,1)S(1)}, bf16[1536,1024]{1,0:T(8,128)(2,1)}, u32[]{:S(2)}) copy-start(bf16[1536,1024]{1,0:T(8,128)(2,1)} %tokens.11) | copy-start | bytes 9437188
  4.1 2.3 %copy-start.2 = (bf16[512,512]{1,0:T(8,128)(2,1)S(1)}, bf16[512,512]{1,0:T(8,128)(2,1)}, u32[]{:S(2)}) copy-start(bf16[512,512]{1,0:T(8,128)(2,1)} %get-tuple-element.47.keep) | copy-start | bytes 1572868
  4.1 2.3 %copy-start.4 = (f32[4,128]{1,0:T(4,128)S(1)}, f32[4,128]{1,0:T(4,128)}, u32[]{:S(2)}) copy-start(f32[4,128]{1,0:T(4,128)} %get-tuple-element.49.squares) | copy-start | bytes 6148
  4.1 2.3 %collective-permute-start = (bf16[528,512]{1,0:T(8,128)(2,1)}, bf16[528,512]{1,0:T(8,128)(2,1)S(1)}, u32[]{:S(2)}, u32[]{:S(2)}) collective-permute-start(bf16[528,512]{1,0:T(8,128)(2,1)} %get-tuple-element.48), channel_id=1, source_target_pairs={{0,1},{1,0},{2,3},{3,2},{4,5},{5,4},{6,7},{7,6},{8,9},{9,8},{10,11... | collective-permute-start | bytes 1622024 | tf_op jit(solution)/shard_map/ppermute | solution.py:285
  6.6 16.0 %collective-permute-start.9 = (bf16[528,512]{1,0:T(8,128)(2,1)S(1)}, bf16[528,512]{1,0:T(8,128)(2,1)S(1)}, u32[]{:S(2)}, u32[]{:S(2)}) collective-permute-start(bf16[528,512]{1,0:T(8,128)(2,1)S(1)} %get-tuple-element.82), channel_id=1, source_target_pairs={{0,2},{1,3},{2,0},{3,1},{4,6},{5,7},{6,4},{7,5},{8,10},{9,11},{10,... | collective-permute-start | bytes 1622024 | tf_op jit(solution)/shard_map/ppermute | solution.py:291
  10.8 6.7 %collective-permute-start.8 = (bf16[512,512]{1,0:T(8,128)(2,1)S(1)}, bf16[512,512]{1,0:T(8,128)(2,1)S(1)}, u32[]{:S(2)}, u32[]{:S(2)}) collective-permute-start(bf16[512,512]{1,0:T(8,128)(2,1)S(1)} %get-tuple-element.80), channel_id=1, source_target_pairs={{0,1},{1,0},{2,3},{3,2},{4,5},{5,4},{6,7},{7,6},{8,9},{9,8},{10,11... | collective-permute-start | bytes 1572872 | tf_op jit(solution)/shard_map/ppermute | solution.py:312
  10.9 6.3 %collective-permute-start.6 = (bf16[272,512]{1,0:T(8,128)(2,1)S(1)}, bf16[272,512]{1,0:T(8,128)(2,1)S(1)}, u32[]{:S(2)}, u32[]{:S(2)}) collective-permute-start(bf16[272,512]{1,0:T(8,128)(2,1)S(1)} %get-tuple-element.75), channel_id=1, source_target_pairs={{0,1},{1,0},{2,3},{3,2},{4,5},{5,4},{6,7},{7,6},{8,9},{9,8},{10,11... | collective-permute-start | bytes 835592 | tf_op jit(solution)/shard_map/ppermute | solution.py:285
  14.0 2.5 %copy-start.5 = (s32[4]{0:T(128)S(1)}, s32[4]{0:T(128)}, u32[]{:S(2)}) copy-start(s32[4]{0:T(128)} %live) | copy-start | bytes 52
  14.0 2.4 %copy-start.6 = (s32[4]{0:T(128)S(1)}, s32[4]{0:T(128)}, u32[]{:S(2)}) copy-start(s32[4]{0:T(128)} %span) | copy-start | bytes 52
  14.0 2.4 %copy-start.7 = (f32[1,128]{1,0:T(1,128)S(1)}, f32[1,128]{1,0:T(1,128)}, u32[]{:S(2)}) copy-start(f32[1,128]{1,0:T(1,128)} %constant.4.clone.frequencies) | copy-start | bytes 1540
  15.9 10.4 %collective-permute-start.5 = (bf16[256,512]{1,0:T(8,128)(2,1)S(1)}, bf16[256,512]{1,0:T(8,128)(2,1)S(1)}, u32[]{:S(2)}, u32[]{:S(2)}) collective-permute-start(bf16[256,512]{1,0:T(8,128)(2,1)S(1)} %get-tuple-element.73), channel_id=1, source_target_pairs={{0,1},{1,0},{2,3},{3,2},{4,5},{5,4},{6,7},{7,6},{8,9},{9,8},{10,11... | collective-permute-start | bytes 786440 | tf_op jit(solution)/shard_map/ppermute | solution.py:312
  16.0 8.0 %collective-permute-start.2 = (bf16[784,512]{1,0:T(8,128)(2,1)S(1)}, bf16[784,512]{1,0:T(8,128)(2,1)S(1)}, u32[]{:S(2)}, u32[]{:S(2)}) collective-permute-start(bf16[784,512]{1,0:T(8,128)(2,1)S(1)} %get-tuple-element.67), channel_id=1, source_target_pairs={{0,1},{1,0},{2,3},{3,2},{4,5},{5,4},{6,7},{7,6},{8,9},{9,8},{10,11... | collective-permute-start | bytes 2408456 | tf_op jit(solution)/shard_map/ppermute | solution.py:285
  17.2 14.6 %collective-permute-start.1 = (bf16[768,512]{1,0:T(8,128)(2,1)S(1)}, bf16[768,512]{1,0:T(8,128)(2,1)S(1)}, u32[]{:S(2)}, u32[]{:S(2)}) collective-permute-start(bf16[768,512]{1,0:T(8,128)(2,1)S(1)} %get-tuple-element.58), channel_id=1, source_target_pairs={{0,1},{1,0},{2,3},{3,2},{4,5},{5,4},{6,7},{7,6},{8,9},{9,8},{10,11... | collective-permute-start | bytes 2359304 | tf_op jit(solution)/shard_map/ppermute | solution.py:312
  17.4 11.1 %collective-permute-start.7 = (bf16[272,512]{1,0:T(8,128)(2,1)S(1)}, bf16[272,512]{1,0:T(8,128)(2,1)S(1)}, u32[]{:S(2)}, u32[]{:S(2)}) collective-permute-start(bf16[272,512]{1,0:T(8,128)(2,1)S(1)} %get-tuple-element.78), channel_id=1, source_target_pairs={{0,2},{1,3},{2,0},{3,1},{4,6},{5,7},{6,4},{7,5},{8,10},{9,11},{10,... | collective-permute-start | bytes 835592 | tf_op jit(solution)/shard_map/ppermute | solution.py:291
  24.2 15.9 %collective-permute-start.3 = (bf16[528,512]{1,0:T(8,128)(2,1)S(1)}, bf16[528,512]{1,0:T(8,128)(2,1)S(1)}, u32[]{:S(2)}, u32[]{:S(2)}) collective-permute-start(bf16[528,512]{1,0:T(8,128)(2,1)S(1)} %get-tuple-element.70), channel_id=1, source_target_pairs={{0,2},{1,3},{2,0},{3,1},{4,6},{5,7},{6,4},{7,5},{8,10},{9,11},{10,... | collective-permute-start | bytes 1622024 | tf_op jit(solution)/shard_map/ppermute | solution.py:291
  29.7 15.6 %collective-permute-start.4 = (bf16[256,512]{1,0:T(8,128)(2,1)S(1)}, bf16[256,512]{1,0:T(8,128)(2,1)S(1)}, u32[]{:S(2)}, u32[]{:S(2)}) collective-permute-start(bf16[256,512]{1,0:T(8,128)(2,1)S(1)} %get-tuple-element.71), channel_id=1, source_target_pairs={{0,2},{1,3},{2,0},{3,1},{4,6},{5,7},{6,4},{7,5},{8,10},{9,11},{10,... | collective-permute-start | bytes 786440 | tf_op jit(solution)/shard_map/ppermute | solution.py:291

commit v17 on v14

--- a/solution.py
+++ b/solution.py
@@ -302,8 +302,11 @@
         made = [product(gain, step, *chunks[index]) for step in others]
         count = chunks[index][1]
         sums = add_halves(made, (count - 1, 1) if count > 2 else (count,))
+        if index == 2:
+            sums, late = hold((sums, gain))
         arrivals.append(([cross(part) for part in sums[0]], sums[1]))
-    own = [product(gain, 0, first, count, carrier=False) for first, count in chunks]
+    own = [product(gain, 0, *chunk, carrier=False) for chunk in chunks[:-1]]
+    own.append(product(late, 0, *chunks[-1], carrier=False))
     table = tables(span_offset)
 
     result = None

time: 49.5 us -> 47.1 us (0.952)
  waiting for transfers between devices: 21.3 us -> 19.2 us
    ppermute x4, waiting for transfers between devices: 19.7 us -> 17.6 us  [cross(): lax.ppermute(part, 'tensor', shift(step))]
    unnamed x12 -> x14, local copies, waits for them, and re-layouts: 4.78 us -> 4.78 us
  transfers between devices with their start and end apart: 10 -> 10, of which waited for: 4 -> 5; matrix products, arithmetic and copies ran while one was open for 0% -> 0% of each run, Pallas kernels for 23% -> 24%
where the time goes in v17:
time: 47.1 us; the launch traced here: 46.9 us
  waiting for transfers between devices  19.2 us (41%)
  Pallas kernels  15.8 us (34%)
  starting transfers between devices  6.97 us (15%)
  local copies, waits for them, and re-layouts  4.78 us (10%)
    ppermute x4, waiting for transfers between devices, cross(): lax.ppermute(part, 'tensor', shift(step))  17.6 us
    pallas_call x6, Pallas kernels, product(): pl.pallas_call(functools.partial(product_kernel, step, chip_count, first,...  9.68 us
    ppermute x4, starting transfers between devices, cross(): lax.ppermute(part, 'tensor', shift(step))  5.18 us
    pallas_call x4, Pallas kernels, finish(): pl.pallas_call(functools.partial(finish_kernel, first, at, count, chip_co...  5 us
    unnamed x14, local copies, waits for them, and re-layouts  4.78 us
    ppermute x3, waiting for transfers between devices, add_halves(): lax.ppermute(send, 'tensor', swap)  1.57 us
    ppermute x3, starting transfers between devices, add_halves(): lax.ppermute(send, 'tensor', swap)  1.56 us
  transfers between devices with their start and end apart: 10, of which 5 were waited for; matrix products, arithmetic and copies ran while one was open for 0% of the time, Pallas kernels for 24%

profile of v17, /device:TPU:0, one launch (start us, length us, event | category | flops | bytes accessed | tf_op | source)
XLA Modules:
  0.0 46.9 jit_solution(11008092137872435020)
XLA Ops:
  0.0 0.0 copy-start.3
  0.0 0.7 %copy-done.3 = bf16[1024]{0:T(1024)(128)(2,1)S(1)} copy-done((bf16[1024]{0:T(1024)(128)(2,1)S(1)}, bf16[1024]{0:T(1024)(128)(2,1)}, u32[]{:S(2)}) %copy-start.3) | copy-done | bytes 2072
  0.7 3.1 %shard_map.64 = (bf16[512,512]{1,0:T(8,128)(2,1)S(1)}, bf16[528,512]{1,0:T(8,128)(2,1)S(1)}, f32[4,128]{1,0:T(4,128)S(1)}) custom-call(bf16[1536,1024]{1,0:T(8,128)(2,1)} %tokens.11, bf16[1024]{0:T(1024)(128)(2,1)S(1)} %copy-done.3, bf16[1024,2048]{1,0:T(8,128)(2,1)} %weight.11), custom_call_target="tpu_custom_call" | custom-call | flops 999999995904 | bytes 1 | tf_op jit(solution)/shard_map/pallas_call | solution.py:228
  3.8 0.5 %collective-permute-start = (bf16[528,512]{1,0:T(8,128)(2,1)S(1)}, bf16[528,512]{1,0:T(8,128)(2,1)S(1)}, u32[]{:S(2)}, u32[]{:S(2)}) collective-permute-start(bf16[528,512]{1,0:T(8,128)(2,1)S(1)} %get-tuple-element.49), channel_id=1, source_target_pairs={{0,1},{1,0},{2,3},{3,2},{4,5},{5,4},{6,7},{7,6},{8,9},{9,8},{10,11... | collective-permute-start | bytes 1622024 | tf_op jit(solution)/shard_map/ppermute | solution.py:286
  4.3 1.6 %collective-permute-done.received = bf16[528,512]{1,0:T(8,128)(2,1)S(1)} collective-permute-done((bf16[528,512]{1,0:T(8,128)(2,1)S(1)}, bf16[528,512]{1,0:T(8,128)(2,1)S(1)}, u32[]{:S(2)}, u32[]{:S(2)}) %collective-permute-start) | collective-permute-done | bytes 540704 | tf_op jit(solution)/shard_map/ppermute | solution.py:286
  5.8 0.1 shard_map.65
  6.0 2.9 %collective-permute-start.9 = (bf16[528,512]{1,0:T(8,128)(2,1)S(1)}, bf16[528,512]{1,0:T(8,128)(2,1)S(1)}, u32[]{:S(2)}, u32[]{:S(2)}) collective-permute-start(bf16[528,512]{1,0:T(8,128)(2,1)S(1)} %get-tuple-element.84), channel_id=1, source_target_pairs={{0,2},{1,3},{2,0},{3,1},{4,6},{5,7},{6,4},{7,5},{8,10},{9,11},{10,... | collective-permute-start | bytes 1622024 | tf_op jit(solution)/shard_map/ppermute | solution.py:292
  8.9 0.0 copy-start
  8.9 2.2 %copy-done = bf16[1024,2048]{1,0:T(8,128)(2,1)S(1)} copy-done((bf16[1024,2048]{1,0:T(8,128)(2,1)S(1)}, bf16[1024,2048]{1,0:T(8,128)(2,1)}, u32[]{:S(2)}) %copy-start) | copy-done | bytes 4194328
  11.1 0.0 copy-start.1
  11.1 1.9 %copy-done.1 = bf16[1536,1024]{1,0:T(8,128)(2,1)S(1)} copy-done((bf16[1536,1024]{1,0:T(8,128)(2,1)S(1)}, bf16[1536,1024]{1,0:T(8,128)(2,1)}, u32[]{:S(2)}) %copy-start.1) | copy-done | bytes 3145752
  13.0 1.3 %shard_map.73 = (bf16[512,512]{1,0:T(8,128)(2,1)S(1)}, bf16[512,512]{1,0:T(8,128)(2,1)S(1)}) custom-call(bf16[1536,1024]{1,0:T(8,128)(2,1)S(1)} %copy-done.1, bf16[1024]{0:T(1024)(128)(2,1)S(1)} %copy-done.3, bf16[1024,2048]{1,0:T(8,128)(2,1)S(1)} %copy-done), custom_call_target="tpu_custom_call" | custom-call | flops 1 | bytes 1 | tf_op jit(solution)/shard_map/pallas_call | solution.py:228
  14.3 0.1 collective-permute-start.8
  14.4 0.7 %shard_map.71 = (bf16[256,512]{1,0:T(8,128)(2,1)S(1)}, bf16[272,512]{1,0:T(8,128)(2,1)S(1)}, f32[2,128]{1,0:T(2,128)S(1)}) custom-call(bf16[1536,1024]{1,0:T(8,128)(2,1)S(1)} %copy-done.1, bf16[1024]{0:T(1024)(128)(2,1)S(1)} %copy-done.3, bf16[1024,2048]{1,0:T(8,128)(2,1)S(1)} %copy-done), custom_call_target="tpu_custom_call" | custom-call | flops 1 | bytes 1 | tf_op jit(solution)/shard_map/pallas_call | solution.py:228
  15.1 0.6 %collective-permute-start.6 = (bf16[272,512]{1,0:T(8,128)(2,1)S(1)}, bf16[272,512]{1,0:T(8,128)(2,1)S(1)}, u32[]{:S(2)}, u32[]{:S(2)}) collective-permute-start(bf16[272,512]{1,0:T(8,128)(2,1)S(1)} %get-tuple-element.77), channel_id=1, source_target_pairs={{0,1},{1,0},{2,3},{3,2},{4,5},{5,4},{6,7},{7,6},{8,9},{9,8},{10,11... | collective-permute-start | bytes 835592 | tf_op jit(solution)/shard_map/ppermute | solution.py:286
  15.7 0.7 %shard_map.70 = (bf16[256,512]{1,0:T(8,128)(2,1)S(1)}, bf16[256,512]{1,0:T(8,128)(2,1)S(1)}) custom-call(bf16[1536,1024]{1,0:T(8,128)(2,1)S(1)} %copy-done.1, bf16[1024]{0:T(1024)(128)(2,1)S(1)} %copy-done.3, bf16[1024,2048]{1,0:T(8,128)(2,1)S(1)} %copy-done), custom_call_target="tpu_custom_call" | custom-call | flops 1 | bytes 1 | tf_op jit(solution)/shard_map/pallas_call | solution.py:228
  16.4 0.0 copy-start.4
  16.4 0.0 copy-start.5
  16.5 0.0 copy-start.6
  16.5 2.0 %shard_map.66 = (bf16[768,512]{1,0:T(8,128)(2,1)S(1)}, bf16[784,512]{1,0:T(8,128)(2,1)S(1)}, f32[6,128]{1,0:T(8,128)S(1)}) custom-call(bf16[1536,1024]{1,0:T(8,128)(2,1)S(1)} %copy-done.1, bf16[1024]{0:T(1024)(128)(2,1)S(1)} %copy-done.3, bf16[1024,2048]{1,0:T(8,128)(2,1)S(1)} %copy-done), custom_call_target="tpu_custom_call" | custom-call | flops 1 | bytes 1 | tf_op jit(solution)/shard_map/pallas_call | solution.py:228
  18.5 0.1 collective-permute-start.5
  18.6 0.5 %collective-permute-start.1 = (bf16[784,512]{1,0:T(8,128)(2,1)S(1)}, bf16[784,512]{1,0:T(8,128)(2,1)S(1)}, u32[]{:S(2)}, u32[]{:S(2)}) collective-permute-start(bf16[784,512]{1,0:T(8,128)(2,1)S(1)} %get-tuple-element.56), channel_id=1, source_target_pairs={{0,1},{1,0},{2,3},{3,2},{4,5},{5,4},{6,7},{7,6},{8,9},{9,8},{10,11... | collective-permute-start | bytes 2408456 | tf_op jit(solution)/shard_map/ppermute | solution.py:286
  19.1 0.0 copy-done.4
  19.1 0.0 copy-done.5
  19.1 0.0 copy-done.6
  19.1 0.7 %shard_map.69 = (s32[8,128]{1,0:T(8,128)S(1)}, f32[24,128]{1,0:T(8,128)S(1)}, f32[24,128]{1,0:T(8,128)S(1)}, f32[64,128]{1,0:T(8,128)S(1)}, f32[64,128]{1,0:T(8,128)S(1)}) custom-call(s32[4]{0:T(128)S(1)} %copy-done.4, s32[4]{0:T(128)S(1)} %copy-done.5, f32[1,128]{1,0:T(1,128)S(1)} %copy-done.6), custom_call_target="tpu_custom_call" | custom-call | flops 1 | bytes 1 | tf_op jit(solution)/shard_map/pallas_call | solution.py:242
  19.8 0.0 collective-permute-done.6.received
  19.8 0.1 shard_map.72
  19.9 0.1 collective-permute-start.7
  20.0 0.0 collective-permute-done.8.refs_1_
  20.0 1.5 %collective-permute-done.9.refs_8_ = bf16[528,512]{1,0:T(8,128)(2,1)S(1)} collective-permute-done((bf16[528,512]{1,0:T(8,128)(2,1)S(1)}, bf16[528,512]{1,0:T(8,128)(2,1)S(1)}, u32[]{:S(2)}, u32[]{:S(2)}) %collective-permute-start.9) | collective-permute-done | bytes 540704 | tf_op jit(solution)/shard_map/ppermute | solution.py:292
  21.5 0.0 copy-start.2
  21.5 1.4 %shard_map.74.refs_9_ = bf16[1536,512]{1,0:T(8,128)(2,1)} custom-call(bf16[512,512]{1,0:T(8,128)(2,1)S(1)} %get-tuple-element.81.refs_0_, bf16[512,512]{1,0:T(8,128)(2,1)S(1)} %collective-permute-done.8.refs_1_, s32[8,128]{1,0:T(8,128)S(1)} %get-tuple-element.66.refs_2_, f32[24,128]{1,0:T(8,128)S(1)} %get-tuple-element.67.refs_3_, ...), custom_call_target="tpu_custom_call" | custom-call | flops 20000000000 | bytes 1 | tf_op jit(solution)/shard_map/pallas_call | solution.py:259
  22.9 0.0 collective-permute-done.1.received
  22.9 0.2 shard_map.67
  23.1 2.1 %collective-permute-start.3 = (bf16[528,512]{1,0:T(8,128)(2,1)S(1)}, bf16[528,512]{1,0:T(8,128)(2,1)S(1)}, u32[]{:S(2)}, u32[]{:S(2)}) collective-permute-start(bf16[528,512]{1,0:T(8,128)(2,1)S(1)} %get-tuple-element.72), channel_id=1, source_target_pairs={{0,2},{1,3},{2,0},{3,1},{4,6},{5,7},{6,4},{7,5},{8,10},{9,11},{10,... | collective-permute-start | bytes 1622024 | tf_op jit(solution)/shard_map/ppermute | solution.py:292
  25.2 0.0 copy-done.2
  25.2 1.8 %shard_map.68 = (bf16[768,512]{1,0:T(8,128)(2,1)S(1)}, bf16[768,512]{1,0:T(8,128)(2,1)S(1)}) custom-call(bf16[1536,1024]{1,0:T(8,128)(2,1)S(1)} %copy-done.2, bf16[1024]{0:T(1024)(128)(2,1)S(1)} %copy-done.3, bf16[1024,2048]{1,0:T(8,128)(2,1)S(1)} %copy-done), custom_call_target="tpu_custom_call" | custom-call | flops 1 | bytes 1 | tf_op jit(solution)/shard_map/pallas_call | solution.py:228
  27.0 0.1 collective-permute-start.2
  27.1 0.0 collective-permute-done.5.refs_1_
  27.1 2.3 %collective-permute-done.7.refs_8_ = bf16[272,512]{1,0:T(8,128)(2,1)S(1)} collective-permute-done((bf16[272,512]{1,0:T(8,128)(2,1)S(1)}, bf16[272,512]{1,0:T(8,128)(2,1)S(1)}, u32[]{:S(2)}, u32[]{:S(2)}) %collective-permute-start.7) | collective-permute-done | bytes 278560 | tf_op jit(solution)/shard_map/ppermute | solution.py:292
  29.5 1.1 %shard_map.75.refs_9_ = bf16[1536,512]{1,0:T(8,128)(2,1)} custom-call(bf16[256,512]{1,0:T(8,128)(2,1)S(1)} %get-tuple-element.74.refs_0_, bf16[256,512]{1,0:T(8,128)(2,1)S(1)} %collective-permute-done.5.refs_1_, s32[8,128]{1,0:T(8,128)S(1)} %get-tuple-element.66.refs_2_, f32[24,128]{1,0:T(8,128)S(1)} %get-tuple-element.67.refs_3_, ...), custom_call_target="tpu_custom_call", output_to_operand_aliasing={{}: (9, {})} | custom-call | flops 20000000000 | bytes 1 | tf_op jit(solution)/shard_map/pallas_call | solution.py:259
  30.6 0.1 collective-permute-start.4
  30.7 10.4 %collective-permute-done.3.refs_8_ = bf16[528,512]{1,0:T(8,128)(2,1)S(1)} collective-permute-done((bf16[528,512]{1,0:T(8,128)(2,1)S(1)}, bf16[528,512]{1,0:T(8,128)(2,1)S(1)}, u32[]{:S(2)}, u32[]{:S(2)}) %collective-permute-start.3) | collective-permute-done | bytes 540704 | tf_op jit(solution)/shard_map/ppermute | solution.py:292
  41.0 0.0 collective-permute-done.2.refs_1_
  41.0 1.4 %shard_map.76.refs_10_ = bf16[1536,512]{1,0:T(8,128)(2,1)} custom-call(bf16[768,512]{1,0:T(8,128)(2,1)S(1)} %get-tuple-element.62.refs_0_, bf16[768,512]{1,0:T(8,128)(2,1)S(1)} %collective-permute-done.2.refs_1_, s32[8,128]{1,0:T(8,128)S(1)} %get-tuple-element.66.refs_2_, f32[24,128]{1,0:T(8,128)S(1)} %get-tuple-element.67.refs_3_, ...), custom_call_target="tpu_custom_call", output_to_operand_aliasing={{}: (9, {})} | custom-call | flops 20000000000 | bytes 1 | tf_op jit(solution)/shard_map/pallas_call | solution.py:259
  42.5 3.3 %collective-permute-done.4.refs_9_ = bf16[256,512]{1,0:T(8,128)(2,1)S(1)} collective-permute-done((bf16[256,512]{1,0:T(8,128)(2,1)S(1)}, bf16[256,512]{1,0:T(8,128)(2,1)S(1)}, u32[]{:S(2)}, u32[]{:S(2)}) %collective-permute-start.4) | collective-permute-done | bytes 262176 | tf_op jit(solution)/shard_map/ppermute | solution.py:292
  45.8 1.1 %shard_map.77 = bf16[1536,512]{1,0:T(8,128)(2,1)} custom-call(bf16[768,512]{1,0:T(8,128)(2,1)S(1)} %get-tuple-element.62.refs_0_, bf16[768,512]{1,0:T(8,128)(2,1)S(1)} %collective-permute-done.2.refs_1_, s32[8,128]{1,0:T(8,128)S(1)} %get-tuple-element.66.refs_2_, f32[24,128]{1,0:T(8,128)S(1)} %get-tuple-element.67.refs_3_, ...), custom_call_target="tpu_custom_call", output_to_operand_aliasing={{}: (10, {})} | custom-call | flops 20000000000 | bytes 1 | tf_op jit(solution)/shard_map/pallas_call | solution.py:259
Async XLA Ops:
  0.0 0.7 %copy-start.3 = (bf16[1024]{0:T(1024)(128)(2,1)S(1)}, bf16[1024]{0:T(1024)(128)(2,1)}, u32[]{:S(2)}) copy-start(bf16[1024]{0:T(1024)(128)(2,1)} %gain.6) | copy-start | bytes 6148
  3.8 2.1 %collective-permute-start = (bf16[528,512]{1,0:T(8,128)(2,1)S(1)}, bf16[528,512]{1,0:T(8,128)(2,1)S(1)}, u32[]{:S(2)}, u32[]{:S(2)}) collective-permute-start(bf16[528,512]{1,0:T(8,128)(2,1)S(1)} %get-tuple-element.49), channel_id=1, source_target_pairs={{0,1},{1,0},{2,3},{3,2},{4,5},{5,4},{6,7},{7,6},{8,9},{9,8},{10,11... | collective-permute-start | bytes 1622024 | tf_op jit(solution)/shard_map/ppermute | solution.py:286
  6.0 15.5 %collective-permute-start.9 = (bf16[528,512]{1,0:T(8,128)(2,1)S(1)}, bf16[528,512]{1,0:T(8,128)(2,1)S(1)}, u32[]{:S(2)}, u32[]{:S(2)}) collective-permute-start(bf16[528,512]{1,0:T(8,128)(2,1)S(1)} %get-tuple-element.84), channel_id=1, source_target_pairs={{0,2},{1,3},{2,0},{3,1},{4,6},{5,7},{6,4},{7,5},{8,10},{9,11},{10,... | collective-permute-start | bytes 1622024 | tf_op jit(solution)/shard_map/ppermute | solution.py:292
  8.9 2.2 %copy-start = (bf16[1024,2048]{1,0:T(8,128)(2,1)S(1)}, bf16[1024,2048]{1,0:T(8,128)(2,1)}, u32[]{:S(2)}) copy-start(bf16[1024,2048]{1,0:T(8,128)(2,1)} %weight.11) | copy-start | bytes 12582916
  11.1 1.9 %copy-start.1 = (bf16[1536,1024]{1,0:T(8,128)(2,1)S(1)}, bf16[1536,1024]{1,0:T(8,128)(2,1)}, u32[]{:S(2)}) copy-start(bf16[1536,1024]{1,0:T(8,128)(2,1)} %tokens.11) | copy-start | bytes 9437188
  14.3 5.7 %collective-permute-start.8 = (bf16[512,512]{1,0:T(8,128)(2,1)S(1)}, bf16[512,512]{1,0:T(8,128)(2,1)S(1)}, u32[]{:S(2)}, u32[]{:S(2)}) collective-permute-start(bf16[512,512]{1,0:T(8,128)(2,1)S(1)} %get-tuple-element.82), channel_id=1, source_target_pairs={{0,1},{1,0},{2,3},{3,2},{4,5},{5,4},{6,7},{7,6},{8,9},{9,8},{10,11... | collective-permute-start | bytes 1572872 | tf_op jit(solution)/shard_map/ppermute | solution.py:314
  15.1 4.7 %collective-permute-start.6 = (bf16[272,512]{1,0:T(8,128)(2,1)S(1)}, bf16[272,512]{1,0:T(8,128)(2,1)S(1)}, u32[]{:S(2)}, u32[]{:S(2)}) collective-permute-start(bf16[272,512]{1,0:T(8,128)(2,1)S(1)} %get-tuple-element.77), channel_id=1, source_target_pairs={{0,1},{1,0},{2,3},{3,2},{4,5},{5,4},{6,7},{7,6},{8,9},{9,8},{10,11... | collective-permute-start | bytes 835592 | tf_op jit(solution)/shard_map/ppermute | solution.py:286
  16.4 2.6 %copy-start.4 = (s32[4]{0:T(128)S(1)}, s32[4]{0:T(128)}, u32[]{:S(2)}) copy-start(s32[4]{0:T(128)} %live) | copy-start | bytes 52
  16.4 2.6 %copy-start.5 = (s32[4]{0:T(128)S(1)}, s32[4]{0:T(128)}, u32[]{:S(2)}) copy-start(s32[4]{0:T(128)} %span) | copy-start | bytes 52
  16.5 2.6 %copy-start.6 = (f32[1,128]{1,0:T(1,128)S(1)}, f32[1,128]{1,0:T(1,128)}, u32[]{:S(2)}) copy-start(f32[1,128]{1,0:T(1,128)} %constant.4.clone.frequencies) | copy-start | bytes 1540
  18.5 8.6 %collective-permute-start.5 = (bf16[256,512]{1,0:T(8,128)(2,1)S(1)}, bf16[256,512]{1,0:T(8,128)(2,1)S(1)}, u32[]{:S(2)}, u32[]{:S(2)}) collective-permute-start(bf16[256,512]{1,0:T(8,128)(2,1)S(1)} %get-tuple-element.75), channel_id=1, source_target_pairs={{0,1},{1,0},{2,3},{3,2},{4,5},{5,4},{6,7},{7,6},{8,9},{9,8},{10,11... | collective-permute-start | bytes 786440 | tf_op jit(solution)/shard_map/ppermute | solution.py:314
  18.6 4.3 %collective-permute-start.1 = (bf16[784,512]{1,0:T(8,128)(2,1)S(1)}, bf16[784,512]{1,0:T(8,128)(2,1)S(1)}, u32[]{:S(2)}, u32[]{:S(2)}) collective-permute-start(bf16[784,512]{1,0:T(8,128)(2,1)S(1)} %get-tuple-element.56), channel_id=1, source_target_pairs={{0,1},{1,0},{2,3},{3,2},{4,5},{5,4},{6,7},{7,6},{8,9},{9,8},{10,11... | collective-permute-start | bytes 2408456 | tf_op jit(solution)/shard_map/ppermute | solution.py:286
  19.9 9.6 %collective-permute-start.7 = (bf16[272,512]{1,0:T(8,128)(2,1)S(1)}, bf16[272,512]{1,0:T(8,128)(2,1)S(1)}, u32[]{:S(2)}, u32[]{:S(2)}) collective-permute-start(bf16[272,512]{1,0:T(8,128)(2,1)S(1)} %get-tuple-element.80), channel_id=1, source_target_pairs={{0,2},{1,3},{2,0},{3,1},{4,6},{5,7},{6,4},{7,5},{8,10},{9,11},{10,... | collective-permute-start | bytes 835592 | tf_op jit(solution)/shard_map/ppermute | solution.py:292
  21.5 3.7 %copy-start.2 = (bf16[1536,1024]{1,0:T(8,128)(2,1)S(1)}, bf16[1536,1024]{1,0:T(8,128)(2,1)}, u32[]{:S(2)}) copy-start(bf16[1536,1024]{1,0:T(8,128)(2,1)} %tokens.11) | copy-start | bytes 9437188
  23.1 17.9 %collective-permute-start.3 = (bf16[528,512]{1,0:T(8,128)(2,1)S(1)}, bf16[528,512]{1,0:T(8,128)(2,1)S(1)}, u32[]{:S(2)}, u32[]{:S(2)}) collective-permute-start(bf16[528,512]{1,0:T(8,128)(2,1)S(1)} %get-tuple-element.72), channel_id=1, source_target_pairs={{0,2},{1,3},{2,0},{3,1},{4,6},{5,7},{6,4},{7,5},{8,10},{9,11},{10,... | collective-permute-start | bytes 1622024 | tf_op jit(solution)/shard_map/ppermute | solution.py:292
  27.0 14.0 %collective-permute-start.2 = (bf16[768,512]{1,0:T(8,128)(2,1)S(1)}, bf16[768,512]{1,0:T(8,128)(2,1)S(1)}, u32[]{:S(2)}, u32[]{:S(2)}) collective-permute-start(bf16[768,512]{1,0:T(8,128)(2,1)S(1)} %get-tuple-element.63), channel_id=1, source_target_pairs={{0,1},{1,0},{2,3},{3,2},{4,5},{5,4},{6,7},{7,6},{8,9},{9,8},{10,11... | collective-permute-start | bytes 2359304 | tf_op jit(solution)/shard_map/ppermute | solution.py:314
  30.6 15.2 %collective-permute-start.4 = (bf16[256,512]{1,0:T(8,128)(2,1)S(1)}, bf16[256,512]{1,0:T(8,128)(2,1)S(1)}, u32[]{:S(2)}, u32[]{:S(2)}) collective-permute-start(bf16[256,512]{1,0:T(8,128)(2,1)S(1)} %get-tuple-element.73), channel_id=1, source_target_pairs={{0,2},{1,3},{2,0},{3,1},{4,6},{5,7},{6,4},{7,5},{8,10},{9,11},{10,... | collective-permute-start | bytes 786440 | tf_op jit(solution)/shard_map/ppermute | solution.py:292

commit v18 on v17

--- a/solution.py
+++ b/solution.py
@@ -235,7 +235,7 @@
             cost_estimate=HEAVY if staged else COST,
         )(tokens, gain, kv_weight)
 
-    def tables(span_offset):
+    def tables(live_blocks, span_offset):
         frequencies = rope_base ** (-(np.arange(HD // 2, dtype=np.float32) * 2.0) / HD)
         frequencies = np.concatenate([frequencies, frequencies])[None, :].astype(np.float32)
         shapes = [(slot_rows // BLOCK, HD)] * 2 + [(BLOCK, HD)] * 2
@@ -293,9 +293,10 @@
 
     hold = lax.optimization_barrier
     made = [product(norm_gain, step, *chunks[0], staged=True) for step in others]
-    made, gain = hold((made, norm_gain))
+    made, gain, span_offset, live_blocks = hold((made, norm_gain, span_offset, live_blocks))
+    table = tables(live_blocks, span_offset)
     sums = add_halves(made, chunks[0][1:])
-    sums, gain, span_offset, live_blocks = hold((sums, gain, span_offset, live_blocks))
+    sums, gain, table = hold((sums, gain, table))
 
     arrivals = [([cross(part) for part in sums[0]], sums[1])]
     for index in range(1, chunk_count):
@@ -307,7 +308,6 @@
         arrivals.append(([cross(part) for part in sums[0]], sums[1]))
     own = [product(gain, 0, *chunk, carrier=False) for chunk in chunks[:-1]]
     own.append(product(late, 0, *chunks[-1], carrier=False))
-    table = tables(span_offset)
 
     result = None
     for (first, count), (keep, send), (arrived, squares) in zip(chunks, own, arrivals):

time: 47.1 us -> 46.4 us (0.985)
  waiting for transfers between devices: 19.2 us -> 16.7 us
  starting transfers between devices: 6.97 us -> 8.74 us
    ppermute x4, waiting for transfers between devices: 17.6 us -> 15.8 us  [cross(): lax.ppermute(part, 'tensor', shift(step))]
    ppermute x4, starting transfers between devices: 5.18 us -> 6.95 us  [cross(): lax.ppermute(part, 'tensor', shift(step))]
    ppermute x3, waiting for transfers between devices: 1.57 us -> 0.83 us  [add_halves(): lax.ppermute(send, 'tensor', swap)]
  transfers between devices with their start and end apart: 10 -> 10, of which waited for: 5 -> 5; matrix products, arithmetic and copies ran while one was open for 0% -> 0% of each run, Pallas kernels for 24% -> 25%
where the time goes in v18:
time: 46.4 us; the launch traced here: 46.1 us
  waiting for transfers between devices  16.7 us (36%)
  Pallas kernels  15.8 us (34%)
  starting transfers between devices  8.74 us (19%)
  local copies, waits for them, and re-layouts  4.77 us (10%)
    ppermute x4, waiting for transfers between devices, cross(): lax.ppermute(part, 'tensor', shift(step))  15.8 us
    pallas_call x6, Pallas kernels, product(): pl.pallas_call(functools.partial(product_kernel, step, chip_count, first,...  9.71 us
    ppermute x4, starting transfers between devices, cross(): lax.ppermute(part, 'tensor', shift(step))  6.95 us
    pallas_call x4, Pallas kernels, finish(): pl.pallas_call(functools.partial(finish_kernel, first, at, count, chip_co...  5 us
    unnamed x14, local copies, waits for them, and re-layouts  4.77 us
    ppermute x3, starting transfers between devices, add_halves(): lax.ppermute(send, 'tensor', swap)  1.56 us
  transfers between devices with their start and end apart: 10, of which 5 were waited for; matrix products, arithmetic and copies ran while one was open for 0% of the time, Pallas kernels for 25%

profile of v18, /device:TPU:0, one launch (start us, length us, event | category | flops | bytes accessed | tf_op | source)
XLA Modules:
  0.0 46.1 jit_solution(14466131457364282133)
XLA Ops:
  0.0 0.0 copy-start.3
  0.0 0.7 %copy-done.3 = bf16[1024]{0:T(1024)(128)(2,1)S(1)} copy-done((bf16[1024]{0:T(1024)(128)(2,1)S(1)}, bf16[1024]{0:T(1024)(128)(2,1)}, u32[]{:S(2)}) %copy-start.3) | copy-done | bytes 2072
  0.7 0.0 copy-start.4
  0.7 0.0 copy-start.5
  0.7 0.0 copy-start.6
  0.7 3.1 %shard_map.64 = (bf16[512,512]{1,0:T(8,128)(2,1)S(1)}, bf16[528,512]{1,0:T(8,128)(2,1)S(1)}, f32[4,128]{1,0:T(4,128)S(1)}) custom-call(bf16[1536,1024]{1,0:T(8,128)(2,1)} %tokens.11, bf16[1024]{0:T(1024)(128)(2,1)S(1)} %copy-done.3, bf16[1024,2048]{1,0:T(8,128)(2,1)} %weight.11), custom_call_target="tpu_custom_call" | custom-call | flops 999999995904 | bytes 1 | tf_op jit(solution)/shard_map/pallas_call | solution.py:228
  3.8 0.5 %collective-permute-start = (bf16[528,512]{1,0:T(8,128)(2,1)S(1)}, bf16[528,512]{1,0:T(8,128)(2,1)S(1)}, u32[]{:S(2)}, u32[]{:S(2)}) collective-permute-start(bf16[528,512]{1,0:T(8,128)(2,1)S(1)} %get-tuple-element.54), channel_id=1, source_target_pairs={{0,1},{1,0},{2,3},{3,2},{4,5},{5,4},{6,7},{7,6},{8,9},{9,8},{10,11... | collective-permute-start | bytes 1622024 | tf_op jit(solution)/shard_map/ppermute | solution.py:286
  4.3 0.0 copy-done.4
  4.3 0.0 copy-done.5
  4.3 0.0 copy-done.6
  4.3 0.7 %shard_map.66 = (s32[8,128]{1,0:T(8,128)S(1)}, f32[24,128]{1,0:T(8,128)S(1)}, f32[24,128]{1,0:T(8,128)S(1)}, f32[64,128]{1,0:T(8,128)S(1)}, f32[64,128]{1,0:T(8,128)S(1)}) custom-call(s32[4]{0:T(128)S(1)} %copy-done.4, s32[4]{0:T(128)S(1)} %copy-done.5, f32[1,128]{1,0:T(1,128)S(1)} %copy-done.6), custom_call_target="tpu_custom_call" | custom-call | flops 1 | bytes 1 | tf_op jit(solution)/shard_map/pallas_call | solution.py:242
  5.1 0.8 %collective-permute-done.received = bf16[528,512]{1,0:T(8,128)(2,1)S(1)} collective-permute-done((bf16[528,512]{1,0:T(8,128)(2,1)S(1)}, bf16[528,512]{1,0:T(8,128)(2,1)S(1)}, u32[]{:S(2)}, u32[]{:S(2)}) %collective-permute-start) | collective-permute-done | bytes 540704 | tf_op jit(solution)/shard_map/ppermute | solution.py:286
  5.9 0.1 shard_map.65
  6.0 2.9 %collective-permute-start.9 = (bf16[528,512]{1,0:T(8,128)(2,1)S(1)}, bf16[528,512]{1,0:T(8,128)(2,1)S(1)}, u32[]{:S(2)}, u32[]{:S(2)}) collective-permute-start(bf16[528,512]{1,0:T(8,128)(2,1)S(1)} %get-tuple-element.94), channel_id=1, source_target_pairs={{0,2},{1,3},{2,0},{3,1},{4,6},{5,7},{6,4},{7,5},{8,10},{9,11},{10,... | collective-permute-start | bytes 1622024 | tf_op jit(solution)/shard_map/ppermute | solution.py:292
  9.0 0.0 copy-start
  9.0 2.2 %copy-done = bf16[1024,2048]{1,0:T(8,128)(2,1)S(1)} copy-done((bf16[1024,2048]{1,0:T(8,128)(2,1)S(1)}, bf16[1024,2048]{1,0:T(8,128)(2,1)}, u32[]{:S(2)}) %copy-start) | copy-done | bytes 4194328
  11.1 0.0 copy-start.1
  11.1 1.9 %copy-done.1 = bf16[1536,1024]{1,0:T(8,128)(2,1)S(1)} copy-done((bf16[1536,1024]{1,0:T(8,128)(2,1)S(1)}, bf16[1536,1024]{1,0:T(8,128)(2,1)}, u32[]{:S(2)}) %copy-start.1) | copy-done | bytes 3145752
  13.0 1.3 %shard_map.73 = (bf16[512,512]{1,0:T(8,128)(2,1)S(1)}, bf16[512,512]{1,0:T(8,128)(2,1)S(1)}) custom-call(bf16[1536,1024]{1,0:T(8,128)(2,1)S(1)} %copy-done.1, bf16[1024]{0:T(1024)(128)(2,1)S(1)} %copy-done.3, bf16[1024,2048]{1,0:T(8,128)(2,1)S(1)} %copy-done), custom_call_target="tpu_custom_call" | custom-call | flops 1 | bytes 1 | tf_op jit(solution)/shard_map/pallas_call | solution.py:228
  14.3 0.1 collective-permute-start.8
  14.4 0.7 %shard_map.71 = (bf16[256,512]{1,0:T(8,128)(2,1)S(1)}, bf16[272,512]{1,0:T(8,128)(2,1)S(1)}, f32[2,128]{1,0:T(2,128)S(1)}) custom-call(bf16[1536,1024]{1,0:T(8,128)(2,1)S(1)} %copy-done.1, bf16[1024]{0:T(1024)(128)(2,1)S(1)} %copy-done.3, bf16[1024,2048]{1,0:T(8,128)(2,1)S(1)} %copy-done), custom_call_target="tpu_custom_call" | custom-call | flops 1 | bytes 1 | tf_op jit(solution)/shard_map/pallas_call | solution.py:228
  15.2 0.6 %collective-permute-start.6 = (bf16[272,512]{1,0:T(8,128)(2,1)S(1)}, bf16[272,512]{1,0:T(8,128)(2,1)S(1)}, u32[]{:S(2)}, u32[]{:S(2)}) collective-permute-start(bf16[272,512]{1,0:T(8,128)(2,1)S(1)} %get-tuple-element.87), channel_id=1, source_target_pairs={{0,1},{1,0},{2,3},{3,2},{4,5},{5,4},{6,7},{7,6},{8,9},{9,8},{10,11... | collective-permute-start | bytes 835592 | tf_op jit(solution)/shard_map/ppermute | solution.py:286
  15.7 0.7 %shard_map.70 = (bf16[256,512]{1,0:T(8,128)(2,1)S(1)}, bf16[256,512]{1,0:T(8,128)(2,1)S(1)}) custom-call(bf16[1536,1024]{1,0:T(8,128)(2,1)S(1)} %copy-done.1, bf16[1024]{0:T(1024)(128)(2,1)S(1)} %copy-done.3, bf16[1024,2048]{1,0:T(8,128)(2,1)S(1)} %copy-done), custom_call_target="tpu_custom_call" | custom-call | flops 1 | bytes 1 | tf_op jit(solution)/shard_map/pallas_call | solution.py:228
  16.5 2.0 %shard_map.67 = (bf16[768,512]{1,0:T(8,128)(2,1)S(1)}, bf16[784,512]{1,0:T(8,128)(2,1)S(1)}, f32[6,128]{1,0:T(8,128)S(1)}) custom-call(bf16[1536,1024]{1,0:T(8,128)(2,1)S(1)} %copy-done.1, bf16[1024]{0:T(1024)(128)(2,1)S(1)} %copy-done.3, bf16[1024,2048]{1,0:T(8,128)(2,1)S(1)} %copy-done), custom_call_target="tpu_custom_call" | custom-call | flops 1 | bytes 1 | tf_op jit(solution)/shard_map/pallas_call | solution.py:228
  18.5 0.1 collective-permute-start.5
  18.6 0.5 %collective-permute-start.1 = (bf16[784,512]{1,0:T(8,128)(2,1)S(1)}, bf16[784,512]{1,0:T(8,128)(2,1)S(1)}, u32[]{:S(2)}, u32[]{:S(2)}) collective-permute-start(bf16[784,512]{1,0:T(8,128)(2,1)S(1)} %get-tuple-element.68), channel_id=1, source_target_pairs={{0,1},{1,0},{2,3},{3,2},{4,5},{5,4},{6,7},{7,6},{8,9},{9,8},{10,11... | collective-permute-start | bytes 2408456 | tf_op jit(solution)/shard_map/ppermute | solution.py:286
  19.1 0.0 collective-permute-done.6.received
  19.1 0.1 shard_map.72
  19.1 0.1 collective-permute-start.7
  19.2 0.0 collective-permute-done.8.refs_1_
  19.2 2.4 %collective-permute-done.9.refs_8_ = bf16[528,512]{1,0:T(8,128)(2,1)S(1)} collective-permute-done((bf16[528,512]{1,0:T(8,128)(2,1)S(1)}, bf16[528,512]{1,0:T(8,128)(2,1)S(1)}, u32[]{:S(2)}, u32[]{:S(2)}) %collective-permute-start.9) | collective-permute-done | bytes 540704 | tf_op jit(solution)/shard_map/ppermute | solution.py:292
  21.6 0.0 copy-start.2
  21.6 1.4 %shard_map.74.refs_9_ = bf16[1536,512]{1,0:T(8,128)(2,1)} custom-call(bf16[512,512]{1,0:T(8,128)(2,1)S(1)} %get-tuple-element.91.refs_0_, bf16[512,512]{1,0:T(8,128)(2,1)S(1)} %collective-permute-done.8.refs_1_, s32[8,128]{1,0:T(8,128)S(1)} %get-tuple-element.76.refs_2_, f32[24,128]{1,0:T(8,128)S(1)} %get-tuple-element.77.refs_3_, ...), custom_call_target="tpu_custom_call" | custom-call | flops 20000000000 | bytes 1 | tf_op jit(solution)/shard_map/pallas_call | solution.py:259
  23.0 0.0 collective-permute-done.1.received
  23.0 0.2 shard_map.68
  23.2 2.5 %collective-permute-start.3 = (bf16[528,512]{1,0:T(8,128)(2,1)S(1)}, bf16[528,512]{1,0:T(8,128)(2,1)S(1)}, u32[]{:S(2)}, u32[]{:S(2)}) collective-permute-start(bf16[528,512]{1,0:T(8,128)(2,1)S(1)} %get-tuple-element.82), channel_id=1, source_target_pairs={{0,2},{1,3},{2,0},{3,1},{4,6},{5,7},{6,4},{7,5},{8,10},{9,11},{10,... | collective-permute-start | bytes 1622024 | tf_op jit(solution)/shard_map/ppermute | solution.py:292
  25.7 0.0 copy-done.2
  25.8 1.8 %shard_map.69 = (bf16[768,512]{1,0:T(8,128)(2,1)S(1)}, bf16[768,512]{1,0:T(8,128)(2,1)S(1)}) custom-call(bf16[1536,1024]{1,0:T(8,128)(2,1)S(1)} %copy-done.2, bf16[1024]{0:T(1024)(128)(2,1)S(1)} %copy-done.3, bf16[1024,2048]{1,0:T(8,128)(2,1)S(1)} %copy-done), custom_call_target="tpu_custom_call" | custom-call | flops 1 | bytes 1 | tf_op jit(solution)/shard_map/pallas_call | solution.py:228
  27.6 0.1 collective-permute-start.2
  27.7 0.0 collective-permute-done.5.refs_1_
  27.7 1.0 %collective-permute-done.7.refs_8_ = bf16[272,512]{1,0:T(8,128)(2,1)S(1)} collective-permute-done((bf16[272,512]{1,0:T(8,128)(2,1)S(1)}, bf16[272,512]{1,0:T(8,128)(2,1)S(1)}, u32[]{:S(2)}, u32[]{:S(2)}) %collective-permute-start.7) | collective-permute-done | bytes 278560 | tf_op jit(solution)/shard_map/ppermute | solution.py:292
  28.7 1.1 %shard_map.75.refs_9_ = bf16[1536,512]{1,0:T(8,128)(2,1)} custom-call(bf16[256,512]{1,0:T(8,128)(2,1)S(1)} %get-tuple-element.84.refs_0_, bf16[256,512]{1,0:T(8,128)(2,1)S(1)} %collective-permute-done.5.refs_1_, s32[8,128]{1,0:T(8,128)S(1)} %get-tuple-element.76.refs_2_, f32[24,128]{1,0:T(8,128)S(1)} %get-tuple-element.77.refs_3_, ...), custom_call_target="tpu_custom_call", output_to_operand_aliasing={{}: (9, {})} | custom-call | flops 20000000000 | bytes 1 | tf_op jit(solution)/shard_map/pallas_call | solution.py:259
  29.8 1.4 %collective-permute-start.4 = (bf16[256,512]{1,0:T(8,128)(2,1)S(1)}, bf16[256,512]{1,0:T(8,128)(2,1)S(1)}, u32[]{:S(2)}, u32[]{:S(2)}) collective-permute-start(bf16[256,512]{1,0:T(8,128)(2,1)S(1)} %get-tuple-element.83), channel_id=1, source_target_pairs={{0,2},{1,3},{2,0},{3,1},{4,6},{5,7},{6,4},{7,5},{8,10},{9,11},{10,... | collective-permute-start | bytes 786440 | tf_op jit(solution)/shard_map/ppermute | solution.py:292
  31.2 9.1 %collective-permute-done.3.refs_8_ = bf16[528,512]{1,0:T(8,128)(2,1)S(1)} collective-permute-done((bf16[528,512]{1,0:T(8,128)(2,1)S(1)}, bf16[528,512]{1,0:T(8,128)(2,1)S(1)}, u32[]{:S(2)}, u32[]{:S(2)}) %collective-permute-start.3) | collective-permute-done | bytes 540704 | tf_op jit(solution)/shard_map/ppermute | solution.py:292
  40.3 0.0 collective-permute-done.2.refs_1_
  40.3 1.4 %shard_map.76.refs_10_ = bf16[1536,512]{1,0:T(8,128)(2,1)} custom-call(bf16[768,512]{1,0:T(8,128)(2,1)S(1)} %get-tuple-element.74.refs_0_, bf16[768,512]{1,0:T(8,128)(2,1)S(1)} %collective-permute-done.2.refs_1_, s32[8,128]{1,0:T(8,128)S(1)} %get-tuple-element.76.refs_2_, f32[24,128]{1,0:T(8,128)S(1)} %get-tuple-element.77.refs_3_, ...), custom_call_target="tpu_custom_call", output_to_operand_aliasing={{}: (9, {})} | custom-call | flops 20000000000 | bytes 1 | tf_op jit(solution)/shard_map/pallas_call | solution.py:259
  41.7 3.3 %collective-permute-done.4.refs_9_ = bf16[256,512]{1,0:T(8,128)(2,1)S(1)} collective-permute-done((bf16[256,512]{1,0:T(8,128)(2,1)S(1)}, bf16[256,512]{1,0:T(8,128)(2,1)S(1)}, u32[]{:S(2)}, u32[]{:S(2)}) %collective-permute-start.4) | collective-permute-done | bytes 262176 | tf_op jit(solution)/shard_map/ppermute | solution.py:292
  45.0 1.1 %shard_map.77 = bf16[1536,512]{1,0:T(8,128)(2,1)} custom-call(bf16[768,512]{1,0:T(8,128)(2,1)S(1)} %get-tuple-element.74.refs_0_, bf16[768,512]{1,0:T(8,128)(2,1)S(1)} %collective-permute-done.2.refs_1_, s32[8,128]{1,0:T(8,128)S(1)} %get-tuple-element.76.refs_2_, f32[24,128]{1,0:T(8,128)S(1)} %get-tuple-element.77.refs_3_, ...), custom_call_target="tpu_custom_call", output_to_operand_aliasing={{}: (10, {})} | custom-call | flops 20000000000 | bytes 1 | tf_op jit(solution)/shard_map/pallas_call | solution.py:259
Async XLA Ops:
  0.0 0.7 %copy-start.3 = (bf16[1024]{0:T(1024)(128)(2,1)S(1)}, bf16[1024]{0:T(1024)(128)(2,1)}, u32[]{:S(2)}) copy-start(bf16[1024]{0:T(1024)(128)(2,1)} %gain.6) | copy-start | bytes 6148
  0.7 3.6 %copy-start.4 = (s32[4]{0:T(128)S(1)}, s32[4]{0:T(128)}, u32[]{:S(2)}) copy-start(s32[4]{0:T(128)} %live) | copy-start | bytes 52
  0.7 3.6 %copy-start.5 = (s32[4]{0:T(128)S(1)}, s32[4]{0:T(128)}, u32[]{:S(2)}) copy-start(s32[4]{0:T(128)} %span) | copy-start | bytes 52
  0.7 3.6 %copy-start.6 = (f32[1,128]{1,0:T(1,128)S(1)}, f32[1,128]{1,0:T(1,128)}, u32[]{:S(2)}) copy-start(f32[1,128]{1,0:T(1,128)} %constant.4.clone.frequencies) | copy-start | bytes 1540
  3.8 2.1 %collective-permute-start = (bf16[528,512]{1,0:T(8,128)(2,1)S(1)}, bf16[528,512]{1,0:T(8,128)(2,1)S(1)}, u32[]{:S(2)}, u32[]{:S(2)}) collective-permute-start(bf16[528,512]{1,0:T(8,128)(2,1)S(1)} %get-tuple-element.54), channel_id=1, source_target_pairs={{0,1},{1,0},{2,3},{3,2},{4,5},{5,4},{6,7},{7,6},{8,9},{9,8},{10,11... | collective-permute-start | bytes 1622024 | tf_op jit(solution)/shard_map/ppermute | solution.py:286
  6.0 15.6 %collective-permute-start.9 = (bf16[528,512]{1,0:T(8,128)(2,1)S(1)}, bf16[528,512]{1,0:T(8,128)(2,1)S(1)}, u32[]{:S(2)}, u32[]{:S(2)}) collective-permute-start(bf16[528,512]{1,0:T(8,128)(2,1)S(1)} %get-tuple-element.94), channel_id=1, source_target_pairs={{0,2},{1,3},{2,0},{3,1},{4,6},{5,7},{6,4},{7,5},{8,10},{9,11},{10,... | collective-permute-start | bytes 1622024 | tf_op jit(solution)/shard_map/ppermute | solution.py:292
  9.0 2.2 %copy-start = (bf16[1024,2048]{1,0:T(8,128)(2,1)S(1)}, bf16[1024,2048]{1,0:T(8,128)(2,1)}, u32[]{:S(2)}) copy-start(bf16[1024,2048]{1,0:T(8,128)(2,1)} %weight.11) | copy-start | bytes 12582916
  11.1 1.9 %copy-start.1 = (bf16[1536,1024]{1,0:T(8,128)(2,1)S(1)}, bf16[1536,1024]{1,0:T(8,128)(2,1)}, u32[]{:S(2)}) copy-start(bf16[1536,1024]{1,0:T(8,128)(2,1)} %tokens.11) | copy-start | bytes 9437188
  14.3 4.9 %collective-permute-start.8 = (bf16[512,512]{1,0:T(8,128)(2,1)S(1)}, bf16[512,512]{1,0:T(8,128)(2,1)S(1)}, u32[]{:S(2)}, u32[]{:S(2)}) collective-permute-start(bf16[512,512]{1,0:T(8,128)(2,1)S(1)} %get-tuple-element.92), channel_id=1, source_target_pairs={{0,1},{1,0},{2,3},{3,2},{4,5},{5,4},{6,7},{7,6},{8,9},{9,8},{10,11... | collective-permute-start | bytes 1572872 | tf_op jit(solution)/shard_map/ppermute | solution.py:314
  15.2 3.9 %collective-permute-start.6 = (bf16[272,512]{1,0:T(8,128)(2,1)S(1)}, bf16[272,512]{1,0:T(8,128)(2,1)S(1)}, u32[]{:S(2)}, u32[]{:S(2)}) collective-permute-start(bf16[272,512]{1,0:T(8,128)(2,1)S(1)} %get-tuple-element.87), channel_id=1, source_target_pairs={{0,1},{1,0},{2,3},{3,2},{4,5},{5,4},{6,7},{7,6},{8,9},{9,8},{10,11... | collective-permute-start | bytes 835592 | tf_op jit(solution)/shard_map/ppermute | solution.py:286
  18.5 9.2 %collective-permute-start.5 = (bf16[256,512]{1,0:T(8,128)(2,1)S(1)}, bf16[256,512]{1,0:T(8,128)(2,1)S(1)}, u32[]{:S(2)}, u32[]{:S(2)}) collective-permute-start(bf16[256,512]{1,0:T(8,128)(2,1)S(1)} %get-tuple-element.85), channel_id=1, source_target_pairs={{0,1},{1,0},{2,3},{3,2},{4,5},{5,4},{6,7},{7,6},{8,9},{9,8},{10,11... | collective-permute-start | bytes 786440 | tf_op jit(solution)/shard_map/ppermute | solution.py:314
  18.6 4.4 %collective-permute-start.1 = (bf16[784,512]{1,0:T(8,128)(2,1)S(1)}, bf16[784,512]{1,0:T(8,128)(2,1)S(1)}, u32[]{:S(2)}, u32[]{:S(2)}) collective-permute-start(bf16[784,512]{1,0:T(8,128)(2,1)S(1)} %get-tuple-element.68), channel_id=1, source_target_pairs={{0,1},{1,0},{2,3},{3,2},{4,5},{5,4},{6,7},{7,6},{8,9},{9,8},{10,11... | collective-permute-start | bytes 2408456 | tf_op jit(solution)/shard_map/ppermute | solution.py:286
  19.1 9.6 %collective-permute-start.7 = (bf16[272,512]{1,0:T(8,128)(2,1)S(1)}, bf16[272,512]{1,0:T(8,128)(2,1)S(1)}, u32[]{:S(2)}, u32[]{:S(2)}) collective-permute-start(bf16[272,512]{1,0:T(8,128)(2,1)S(1)} %get-tuple-element.90), channel_id=1, source_target_pairs={{0,2},{1,3},{2,0},{3,1},{4,6},{5,7},{6,4},{7,5},{8,10},{9,11},{10,... | collective-permute-start | bytes 835592 | tf_op jit(solution)/shard_map/ppermute | solution.py:292
  21.6 4.2 %copy-start.2 = (bf16[1536,1024]{1,0:T(8,128)(2,1)S(1)}, bf16[1536,1024]{1,0:T(8,128)(2,1)}, u32[]{:S(2)}) copy-start(bf16[1536,1024]{1,0:T(8,128)(2,1)} %tokens.11) | copy-start | bytes 9437188
  23.2 17.1 %collective-permute-start.3 = (bf16[528,512]{1,0:T(8,128)(2,1)S(1)}, bf16[528,512]{1,0:T(8,128)(2,1)S(1)}, u32[]{:S(2)}, u32[]{:S(2)}) collective-permute-start(bf16[528,512]{1,0:T(8,128)(2,1)S(1)} %get-tuple-element.82), channel_id=1, source_target_pairs={{0,2},{1,3},{2,0},{3,1},{4,6},{5,7},{6,4},{7,5},{8,10},{9,11},{10,... | collective-permute-start | bytes 1622024 | tf_op jit(solution)/shard_map/ppermute | solution.py:292
  27.6 12.7 %collective-permute-start.2 = (bf16[768,512]{1,0:T(8,128)(2,1)S(1)}, bf16[768,512]{1,0:T(8,128)(2,1)S(1)}, u32[]{:S(2)}, u32[]{:S(2)}) collective-permute-start(bf16[768,512]{1,0:T(8,128)(2,1)S(1)} %get-tuple-element.75), channel_id=1, source_target_pairs={{0,1},{1,0},{2,3},{3,2},{4,5},{5,4},{6,7},{7,6},{8,9},{9,8},{10,11... | collective-permute-start | bytes 2359304 | tf_op jit(solution)/shard_map/ppermute | solution.py:314
  29.8 15.2 %collective-permute-start.4 = (bf16[256,512]{1,0:T(8,128)(2,1)S(1)}, bf16[256,512]{1,0:T(8,128)(2,1)S(1)}, u32[]{:S(2)}, u32[]{:S(2)}) collective-permute-start(bf16[256,512]{1,0:T(8,128)(2,1)S(1)} %get-tuple-element.83), channel_id=1, source_target_pairs={{0,2},{1,3},{2,0},{3,1},{4,6},{5,7},{6,4},{7,5},{8,10},{9,11},{10,... | collective-permute-start | bytes 786440 | tf_op jit(solution)/shard_map/ppermute | solution.py:292

commit v19 on v18

--- a/solution.py
+++ b/solution.py
@@ -28,12 +28,15 @@
 COST = pl.CostEstimate(flops=1, bytes_accessed=1, transcendentals=0)
 
 
-def square_sums(rows):
-    total = jnp.zeros((rows.shape[0], LANES), jnp.float32)
-    for part in range(rows.shape[1] // LANES):
-        wide = rows[:, part * LANES : (part + 1) * LANES].astype(jnp.float32)
-        total += wide * wide
-    return total
+def square_lines(rows):
+    lines = []
+    for low in range(0, rows.shape[0], LANES):
+        total = jnp.zeros((LANES, LANES), jnp.float32)
+        for part in range(rows.shape[1] // LANES):
+            wide = rows[low : low + LANES, part * LANES : (part + 1) * LANES].astype(jnp.float32)
+            total += wide * wide
+        lines.append(jnp.sum(jnp.transpose(total), axis=0, keepdims=True))
+    return lines
 
 
 def packed(squares, width):
@@ -57,7 +60,7 @@
     return part[index : index + 1] + part[SUBLANES + index : SUBLANES + index + 1]
 
 
-def product_kernel(step, chip_count, first, staged, carrier, tokens, gain, weight, *refs):
+def product_kernel(step, chip_count, first, staged, carrier, more, tokens, gain, weight, *refs):
     refs = list(refs)
     keep, send = refs.pop(0), refs.pop(0)
     squares = refs.pop(0) if carrier else None
@@ -114,28 +117,31 @@
         keep[inside, :] = jnp.where(core == 0, left, right)
         send[inside, :] = jnp.where(core == 0, right, left)
         if carrier:
-            total = square_sums(rows)
-            for part in range(TILE // LANES):
-                turned = jnp.transpose(total[part * LANES : (part + 1) * LANES])
-                lines.append(jnp.sum(turned, axis=0, keepdims=True))
-                squares[len(lines) - 1 : len(lines), :] = lines[-1]
+            lines += square_lines(rows)
+    for tile in range(count, count + more):
+        lines += square_lines(tokens[pl.ds((first + tile) * TILE, TILE), :])
     if carrier:
+        for index, line in enumerate(lines):
+            squares[index : index + 1, :] = line
         send[pl.ds(keep.shape[0], 2 * SUBLANES), :] = packed(lines, send.shape[1])
 
 
-def add_carrier_kernel(keep, received, squares, pair_squares, out, *rest):
+def add_kernel(lines, keep, received, *refs):
+    refs = list(refs)
+    squares, pair_squares = (refs.pop(0), refs.pop(0)) if lines else (None, None)
     low = 0
-    for part in (out, *rest):
-        size = part.shape[0] - (2 * SUBLANES if part is out else 0)
+    for out in refs:
+        size = out.shape[0] - (2 * SUBLANES if lines and out is refs[0] else 0)
         rows = pl.ds(low, size)
         total = keep[rows, :].astype(jnp.float32) + received[rows, :].astype(jnp.float32)
-        part[pl.ds(0, size), :] = total.astype(part.dtype)
+        out[pl.ds(0, size), :] = total.astype(out.dtype)
         low += size
-    lines = []
-    for line in range(squares.shape[0]):
-        lines.append(squares[line : line + 1, :] + unpacked(received, line))
-        pair_squares[line : line + 1, :] = lines[-1]
-    out[pl.ds(out.shape[0] - 2 * SUBLANES, 2 * SUBLANES), :] = packed(lines, out.shape[1])
+    if lines:
+        totals = []
+        for line in range(lines):
+            totals.append(squares[line : line + 1, :] + unpacked(received, line))
+            pair_squares[line : line + 1, :] = totals[-1]
+        refs[0][pl.ds(refs[0].shape[0] - 2 * SUBLANES, 2 * SUBLANES), :] = packed(totals, refs[0].shape[1])
 
 
 def table_kernel(live, span, frequencies, limit, far_cos, far_sin, near_cos, near_sin):
@@ -151,10 +157,10 @@
     near_sin[...] = jnp.sin(near)
 
 
-def finish_kernel(first, at, count, chip_count, model_dim, *refs):
+def finish_kernel(first, at, line_at, count, chip_count, model_dim, *refs):
     keep, received, limit, far_cos, far_sin, near_cos, near_sin = refs[:7]
     pair_squares, carriers = refs[7], refs[8 : 7 + chip_count]
-    arrived = refs[7 + chip_count : -4] if at else carriers
+    arrived = refs[7 + chip_count : -4] or carriers
     out, staged, sems = refs[-3:]
     on_diagonal = lax.broadcasted_iota(jnp.int32, (LANES, LANES), 0) == lax.broadcasted_iota(
         jnp.int32, (LANES, LANES), 1
@@ -169,7 +175,7 @@
         for part in arrived:
             values += part[inside, :].astype(jnp.float32)
         columns = []
-        for line in range((at + index) * TILE // LANES, (at + index + 1) * TILE // LANES):
+        for line in range((line_at + index) * TILE // LANES, (line_at + index + 1) * TILE // LANES):
             totals = pair_squares[line : line + 1, :]
             for ref in carriers:
                 totals += unpacked(ref, line)
@@ -210,13 +216,13 @@
     def shift(step):
         return [(i, (i + 2 * step) % tensor_count) for i in range(tensor_count)]
 
-    def product(gain, step, first, count, staged=False, carrier=True):
+    def product(gain, step, first, count, staged=False, carrier=True, more=0):
         vmem = pl.BlockSpec(memory_space=pltpu.VMEM)
         rows = count * TILE
         out_shape = [jax.ShapeDtypeStruct((rows, columns), jnp.bfloat16)] * 2
         if carrier:
             out_shape[1] = jax.ShapeDtypeStruct((rows + 2 * SUBLANES, columns), jnp.bfloat16)
-            out_shape.append(jax.ShapeDtypeStruct((rows // LANES, LANES), jnp.float32))
+            out_shape.append(jax.ShapeDtypeStruct((rows // LANES + more * TILE // LANES, LANES), jnp.float32))
         scratch = [
             pltpu.VMEM((rows, depth), jnp.bfloat16),
             pltpu.VMEM((depth, 2 * columns), jnp.bfloat16),
@@ -226,7 +232,7 @@
             pltpu.SemaphoreType.DMA,
         ]
         return pl.pallas_call(
-            functools.partial(product_kernel, step, chip_count, first, staged, carrier),
+            functools.partial(product_kernel, step, chip_count, first, staged, carrier, more),
             in_specs=[pl.BlockSpec(memory_space=pltpu.HBM) if staged else vmem] * 3,
             out_shape=out_shape,
             out_specs=[vmem] * len(out_shape),
@@ -250,14 +256,14 @@
         )(live_blocks, span_offset, jnp.asarray(frequencies))
         return list(made)
 
-    def finish(first, at, count, keep, received, table, squares, carriers, arrived, result):
+    def finish(first, at, line_at, count, keep, received, table, squares, carriers, arrived, result):
         vmem = pl.BlockSpec(memory_space=pltpu.VMEM)
-        operands = [keep, received] + table + [squares] + carriers + (arrived if at else [])
+        operands = [keep, received] + table + [squares] + carriers + (arrived if arrived is not carriers else [])
         aliases = {len(operands): 0}
         if result is None:
             result, aliases = jnp.zeros((1,), jnp.bfloat16), {}
         return pl.pallas_call(
-            functools.partial(finish_kernel, first, at, count, chip_count, model_dim),
+            functools.partial(finish_kernel, first, at, line_at, count, chip_count, model_dim),
             in_specs=[vmem] * len(operands) + [pl.BlockSpec(memory_space=pl.ANY)],
             out_shape=jax.ShapeDtypeStruct((slot_rows, columns), jnp.bfloat16),
             out_specs=pl.BlockSpec(memory_space=pltpu.HBM),
@@ -275,18 +281,23 @@
 
     def add_halves(made, counts):
         sizes = [count * TILE for count in counts]
-        sizes[0] += 2 * SUBLANES
-        added = [
-            pl.pallas_call(
-                add_carrier_kernel,
-                out_shape=[jax.ShapeDtypeStruct(squares.shape, squares.dtype)]
-                + [jax.ShapeDtypeStruct((size, columns), keep.dtype) for size in sizes],
-                compiler_params=PARAMS,
-                cost_estimate=COST,
-            )(keep, lax.ppermute(send, "tensor", swap), squares)
-            for keep, send, squares in made
-        ]
-        return [list(parts) for parts in zip(*[parts[1:] for parts in added])], added[0][0]
+        added = []
+        for keep, send, *squares in made:
+            lines = squares[0].shape[0] if squares else 0
+            out_shape = [jax.ShapeDtypeStruct((size, columns), keep.dtype) for size in sizes]
+            if lines:
+                out_shape[0] = jax.ShapeDtypeStruct((sizes[0] + 2 * SUBLANES, columns), keep.dtype)
+                out_shape.insert(0, jax.ShapeDtypeStruct(squares[0].shape, squares[0].dtype))
+            added.append(
+                pl.pallas_call(
+                    functools.partial(add_kernel, lines),
+                    out_shape=out_shape,
+                    compiler_params=PARAMS,
+                    cost_estimate=COST,
+                )(keep, lax.ppermute(send, "tensor", swap), *squares)
+            )
+        parts = [list(same) for same in zip(*added)]
+        return (parts[1:], parts[0][0]) if lines else (parts, None)
 
     def cross(sums):
         return [lax.ppermute(part, "tensor", shift(step)) for step, part in zip(others, sums)]
@@ -300,7 +311,8 @@
 
     arrivals = [([cross(part) for part in sums[0]], sums[1])]
     for index in range(1, chunk_count):
-        made = [product(gain, step, *chunks[index]) for step in others]
+        more = sum(CHUNKS[2:]) if index == 1 else 0
+        made = [product(gain, step, *chunks[index], carrier=index == 1, more=more) for step in others]
         count = chunks[index][1]
         sums = add_halves(made, (count - 1, 1) if count > 2 else (count,))
         if index == 2:
@@ -312,11 +324,14 @@
     result = None
     for (first, count), (keep, send), (arrived, squares) in zip(chunks, own, arrivals):
         received = lax.ppermute(send, "tensor", swap)
+        if squares is not None:
+            carriers, pair_squares, line_at = arrived[0], squares, 0
         at = 0
         for part in arrived:
             size = part[0].shape[0] // TILE
-            result = finish(first, at, size, keep, received, table, squares, arrived[0], part, result)
+            result = finish(first, at, line_at, size, keep, received, table, pair_squares, carriers, part, result)
             at += size
+            line_at += size
     return result
 
 

time: 46.4 us -> 46.1 us (level)
  no operation moved by 1% of the time
where the time goes in v19:
time: 46.1 us; the launch traced here: 45.9 us
  waiting for transfers between devices  16.4 us (36%)
  Pallas kernels  15.9 us (34%)
  starting transfers between devices  8.61 us (19%)
  local copies, waits for them, and re-layouts  4.77 us (10%)
    ppermute x4, waiting for transfers between devices, cross(): lax.ppermute(part, 'tensor', shift(step))  15.6 us
    pallas_call x6, Pallas kernels, product(): pl.pallas_call(functools.partial(product_kernel, step, chip_count, first,...  9.82 us
    ppermute x4, starting transfers between devices, cross(): lax.ppermute(part, 'tensor', shift(step))  6.83 us
    pallas_call x4, Pallas kernels, finish(): pl.pallas_call(functools.partial(finish_kernel, first, at, line_at, count...  5.01 us
    unnamed x14, local copies, waits for them, and re-layouts  4.77 us
    ppermute x3, starting transfers between devices, add_halves(): lax.ppermute(send, 'tensor', swap)  1.55 us
  transfers between devices with their start and end apart: 10, of which 5 were waited for; matrix products, arithmetic and copies ran while one was open for 0% of the time, Pallas kernels for 25%

profile of v19, /device:TPU:0, one launch (start us, length us, event | category | flops | bytes accessed | tf_op | source)
XLA Modules:
  0.0 45.9 jit_solution(3538260699786138086)
XLA Ops:
  0.0 0.0 copy-start.3
  0.0 0.7 %copy-done.3 = bf16[1024]{0:T(1024)(128)(2,1)S(1)} copy-done((bf16[1024]{0:T(1024)(128)(2,1)S(1)}, bf16[1024]{0:T(1024)(128)(2,1)}, u32[]{:S(2)}) %copy-start.3) | copy-done | bytes 2072
  0.7 0.0 copy-start.4
  0.7 0.0 copy-start.5
  0.7 0.0 copy-start.6
  0.7 3.1 %shard_map.64 = (bf16[512,512]{1,0:T(8,128)(2,1)S(1)}, bf16[528,512]{1,0:T(8,128)(2,1)S(1)}, f32[4,128]{1,0:T(4,128)S(1)}) custom-call(bf16[1536,1024]{1,0:T(8,128)(2,1)} %tokens.11, bf16[1024]{0:T(1024)(128)(2,1)S(1)} %copy-done.3, bf16[1024,2048]{1,0:T(8,128)(2,1)} %weight.11), custom_call_target="tpu_custom_call" | custom-call | flops 999999995904 | bytes 1 | tf_op jit(solution)/shard_map/pallas_call | solution.py:234
  3.8 0.5 %collective-permute-start = (bf16[528,512]{1,0:T(8,128)(2,1)S(1)}, bf16[528,512]{1,0:T(8,128)(2,1)S(1)}, u32[]{:S(2)}, u32[]{:S(2)}) collective-permute-start(bf16[528,512]{1,0:T(8,128)(2,1)S(1)} %get-tuple-element.51), channel_id=1, source_target_pairs={{0,1},{1,0},{2,3},{3,2},{4,5},{5,4},{6,7},{7,6},{8,9},{9,8},{10,11... | collective-permute-start | bytes 1622024 | tf_op jit(solution)/shard_map/ppermute | solution.py:297
  4.3 0.0 copy-done.4
  4.3 0.0 copy-done.5
  4.3 0.0 copy-done.6
  4.3 0.7 %shard_map.66 = (s32[8,128]{1,0:T(8,128)S(1)}, f32[24,128]{1,0:T(8,128)S(1)}, f32[24,128]{1,0:T(8,128)S(1)}, f32[64,128]{1,0:T(8,128)S(1)}, f32[64,128]{1,0:T(8,128)S(1)}) custom-call(s32[4]{0:T(128)S(1)} %copy-done.4, s32[4]{0:T(128)S(1)} %copy-done.5, f32[1,128]{1,0:T(1,128)S(1)} %copy-done.6), custom_call_target="tpu_custom_call" | custom-call | flops 1 | bytes 1 | tf_op jit(solution)/shard_map/pallas_call | solution.py:248
  5.0 0.8 %collective-permute-done.received = bf16[528,512]{1,0:T(8,128)(2,1)S(1)} collective-permute-done((bf16[528,512]{1,0:T(8,128)(2,1)S(1)}, bf16[528,512]{1,0:T(8,128)(2,1)S(1)}, u32[]{:S(2)}, u32[]{:S(2)}) %collective-permute-start) | collective-permute-done | bytes 540704 | tf_op jit(solution)/shard_map/ppermute | solution.py:297
  5.9 0.1 shard_map.65
  6.0 2.9 %collective-permute-start.9 = (bf16[528,512]{1,0:T(8,128)(2,1)S(1)}, bf16[528,512]{1,0:T(8,128)(2,1)S(1)}, u32[]{:S(2)}, u32[]{:S(2)}) collective-permute-start(bf16[528,512]{1,0:T(8,128)(2,1)S(1)} %get-tuple-element.88), channel_id=1, source_target_pairs={{0,2},{1,3},{2,0},{3,1},{4,6},{5,7},{6,4},{7,5},{8,10},{9,11},{10,... | collective-permute-start | bytes 1622024 | tf_op jit(solution)/shard_map/ppermute | solution.py:303
  8.9 0.0 copy-start
  8.9 2.2 %copy-done = bf16[1024,2048]{1,0:T(8,128)(2,1)S(1)} copy-done((bf16[1024,2048]{1,0:T(8,128)(2,1)S(1)}, bf16[1024,2048]{1,0:T(8,128)(2,1)}, u32[]{:S(2)}) %copy-start) | copy-done | bytes 4194328
  11.1 0.0 copy-start.1
  11.1 1.9 %copy-done.1 = bf16[1536,1024]{1,0:T(8,128)(2,1)S(1)} copy-done((bf16[1536,1024]{1,0:T(8,128)(2,1)S(1)}, bf16[1536,1024]{1,0:T(8,128)(2,1)}, u32[]{:S(2)}) %copy-start.1) | copy-done | bytes 3145752
  13.0 1.3 %shard_map.73 = (bf16[512,512]{1,0:T(8,128)(2,1)S(1)}, bf16[512,512]{1,0:T(8,128)(2,1)S(1)}) custom-call(bf16[1536,1024]{1,0:T(8,128)(2,1)S(1)} %copy-done.1, bf16[1024]{0:T(1024)(128)(2,1)S(1)} %copy-done.3, bf16[1024,2048]{1,0:T(8,128)(2,1)S(1)} %copy-done), custom_call_target="tpu_custom_call" | custom-call | flops 1 | bytes 1 | tf_op jit(solution)/shard_map/pallas_call | solution.py:234
  14.3 0.1 collective-permute-start.8
  14.4 1.0 %shard_map.70 = (bf16[256,512]{1,0:T(8,128)(2,1)S(1)}, bf16[272,512]{1,0:T(8,128)(2,1)S(1)}, f32[8,128]{1,0:T(8,128)S(1)}) custom-call(bf16[1536,1024]{1,0:T(8,128)(2,1)S(1)} %copy-done.1, bf16[1024]{0:T(1024)(128)(2,1)S(1)} %copy-done.3, bf16[1024,2048]{1,0:T(8,128)(2,1)S(1)} %copy-done), custom_call_target="tpu_custom_call" | custom-call | flops 1 | bytes 1 | tf_op jit(solution)/shard_map/pallas_call | solution.py:234
  15.4 0.6 %collective-permute-start.3 = (bf16[272,512]{1,0:T(8,128)(2,1)S(1)}, bf16[272,512]{1,0:T(8,128)(2,1)S(1)}, u32[]{:S(2)}, u32[]{:S(2)}) collective-permute-start(bf16[272,512]{1,0:T(8,128)(2,1)S(1)} %get-tuple-element.77), channel_id=1, source_target_pairs={{0,1},{1,0},{2,3},{3,2},{4,5},{5,4},{6,7},{7,6},{8,9},{9,8},{10,11... | collective-permute-start | bytes 835592 | tf_op jit(solution)/shard_map/ppermute | solution.py:297
  16.0 0.7 %shard_map.72 = (bf16[256,512]{1,0:T(8,128)(2,1)S(1)}, bf16[256,512]{1,0:T(8,128)(2,1)S(1)}) custom-call(bf16[1536,1024]{1,0:T(8,128)(2,1)S(1)} %copy-done.1, bf16[1024]{0:T(1024)(128)(2,1)S(1)} %copy-done.3, bf16[1024,2048]{1,0:T(8,128)(2,1)S(1)} %copy-done), custom_call_target="tpu_custom_call" | custom-call | flops 1 | bytes 1 | tf_op jit(solution)/shard_map/pallas_call | solution.py:234
  16.7 1.9 %shard_map.67 = (bf16[768,512]{1,0:T(8,128)(2,1)S(1)}, bf16[768,512]{1,0:T(8,128)(2,1)S(1)}) custom-call(bf16[1536,1024]{1,0:T(8,128)(2,1)S(1)} %copy-done.1, bf16[1024]{0:T(1024)(128)(2,1)S(1)} %copy-done.3, bf16[1024,2048]{1,0:T(8,128)(2,1)S(1)} %copy-done), custom_call_target="tpu_custom_call" | custom-call | flops 1 | bytes 1 | tf_op jit(solution)/shard_map/pallas_call | solution.py:234
  18.6 0.1 collective-permute-start.7
  18.7 0.5 %collective-permute-start.1 = (bf16[768,512]{1,0:T(8,128)(2,1)S(1)}, bf16[768,512]{1,0:T(8,128)(2,1)S(1)}, u32[]{:S(2)}, u32[]{:S(2)}) collective-permute-start(bf16[768,512]{1,0:T(8,128)(2,1)S(1)} %get-tuple-element.65), channel_id=1, source_target_pairs={{0,1},{1,0},{2,3},{3,2},{4,5},{5,4},{6,7},{7,6},{8,9},{9,8},{10,11... | collective-permute-start | bytes 2359304 | tf_op jit(solution)/shard_map/ppermute | solution.py:297
  19.2 0.0 collective-permute-done.3.received
  19.2 0.1 shard_map.71
  19.2 0.1 collective-permute-start.4
  19.3 0.0 collective-permute-done.8.refs_1_
  19.3 2.3 %collective-permute-done.9.refs_8_ = bf16[528,512]{1,0:T(8,128)(2,1)S(1)} collective-permute-done((bf16[528,512]{1,0:T(8,128)(2,1)S(1)}, bf16[528,512]{1,0:T(8,128)(2,1)S(1)}, u32[]{:S(2)}, u32[]{:S(2)}) %collective-permute-start.9) | collective-permute-done | bytes 540704 | tf_op jit(solution)/shard_map/ppermute | solution.py:303
  21.6 0.0 copy-start.2
  21.6 1.4 %shard_map.74.refs_9_ = bf16[1536,512]{1,0:T(8,128)(2,1)} custom-call(bf16[512,512]{1,0:T(8,128)(2,1)S(1)} %get-tuple-element.85.refs_0_, bf16[512,512]{1,0:T(8,128)(2,1)S(1)} %collective-permute-done.8.refs_1_, s32[8,128]{1,0:T(8,128)S(1)} %get-tuple-element.71.refs_2_, f32[24,128]{1,0:T(8,128)S(1)} %get-tuple-element.72.refs_3_, ...), custom_call_target="tpu_custom_call" | custom-call | flops 20000000000 | bytes 1 | tf_op jit(solution)/shard_map/pallas_call | solution.py:265
  23.0 0.0 collective-permute-done.1.received
  23.0 0.2 shard_map.68
  23.2 2.5 %collective-permute-start.6 = (bf16[512,512]{1,0:T(8,128)(2,1)S(1)}, bf16[512,512]{1,0:T(8,128)(2,1)S(1)}, u32[]{:S(2)}, u32[]{:S(2)}) collective-permute-start(bf16[512,512]{1,0:T(8,128)(2,1)S(1)} %get-tuple-element.82), channel_id=1, source_target_pairs={{0,2},{1,3},{2,0},{3,1},{4,6},{5,7},{6,4},{7,5},{8,10},{9,11},{10,... | collective-permute-start | bytes 1572872 | tf_op jit(solution)/shard_map/ppermute | solution.py:303
  25.7 0.0 copy-done.2
  25.7 1.8 %shard_map.69 = (bf16[768,512]{1,0:T(8,128)(2,1)S(1)}, bf16[768,512]{1,0:T(8,128)(2,1)S(1)}) custom-call(bf16[1536,1024]{1,0:T(8,128)(2,1)S(1)} %copy-done.2, bf16[1024]{0:T(1024)(128)(2,1)S(1)} %copy-done.3, bf16[1024,2048]{1,0:T(8,128)(2,1)S(1)} %copy-done), custom_call_target="tpu_custom_call" | custom-call | flops 1 | bytes 1 | tf_op jit(solution)/shard_map/pallas_call | solution.py:234
  27.6 0.1 collective-permute-start.2
  27.6 0.0 collective-permute-done.7.refs_1_
  27.7 1.2 %collective-permute-done.4.refs_8_ = bf16[272,512]{1,0:T(8,128)(2,1)S(1)} collective-permute-done((bf16[272,512]{1,0:T(8,128)(2,1)S(1)}, bf16[272,512]{1,0:T(8,128)(2,1)S(1)}, u32[]{:S(2)}, u32[]{:S(2)}) %collective-permute-start.4) | collective-permute-done | bytes 278560 | tf_op jit(solution)/shard_map/ppermute | solution.py:303
  28.8 1.1 %shard_map.75.refs_10_ = bf16[1536,512]{1,0:T(8,128)(2,1)} custom-call(bf16[256,512]{1,0:T(8,128)(2,1)S(1)} %get-tuple-element.83.refs_0_, bf16[256,512]{1,0:T(8,128)(2,1)S(1)} %collective-permute-done.7.refs_1_, s32[8,128]{1,0:T(8,128)S(1)} %get-tuple-element.71.refs_2_, f32[24,128]{1,0:T(8,128)S(1)} %get-tuple-element.72.refs_3_, ...), custom_call_target="tpu_custom_call", output_to_operand_aliasing={{}: (9, {})} | custom-call | flops 20000000000 | bytes 1 | tf_op jit(solution)/shard_map/pallas_call | solution.py:265
  29.9 1.3 %collective-permute-start.5 = (bf16[256,512]{1,0:T(8,128)(2,1)S(1)}, bf16[256,512]{1,0:T(8,128)(2,1)S(1)}, u32[]{:S(2)}, u32[]{:S(2)}) collective-permute-start(bf16[256,512]{1,0:T(8,128)(2,1)S(1)} %get-tuple-element.81), channel_id=1, source_target_pairs={{0,2},{1,3},{2,0},{3,1},{4,6},{5,7},{6,4},{7,5},{8,10},{9,11},{10,... | collective-permute-start | bytes 786440 | tf_op jit(solution)/shard_map/ppermute | solution.py:303
  31.2 8.8 %collective-permute-done.6.refs_9_ = bf16[512,512]{1,0:T(8,128)(2,1)S(1)} collective-permute-done((bf16[512,512]{1,0:T(8,128)(2,1)S(1)}, bf16[512,512]{1,0:T(8,128)(2,1)S(1)}, u32[]{:S(2)}, u32[]{:S(2)}) %collective-permute-start.6) | collective-permute-done | bytes 524320 | tf_op jit(solution)/shard_map/ppermute | solution.py:303
  40.0 0.0 collective-permute-done.2.refs_1_
  40.1 1.4 %shard_map.76.refs_10_ = bf16[1536,512]{1,0:T(8,128)(2,1)} custom-call(bf16[768,512]{1,0:T(8,128)(2,1)S(1)} %get-tuple-element.69.refs_0_, bf16[768,512]{1,0:T(8,128)(2,1)S(1)} %collective-permute-done.2.refs_1_, s32[8,128]{1,0:T(8,128)S(1)} %get-tuple-element.71.refs_2_, f32[24,128]{1,0:T(8,128)S(1)} %get-tuple-element.72.refs_3_, ...), custom_call_target="tpu_custom_call", output_to_operand_aliasing={{}: (10, {})} | custom-call | flops 20000000000 | bytes 1 | tf_op jit(solution)/shard_map/pallas_call | solution.py:265
  41.5 3.3 %collective-permute-done.5.refs_9_ = bf16[256,512]{1,0:T(8,128)(2,1)S(1)} collective-permute-done((bf16[256,512]{1,0:T(8,128)(2,1)S(1)}, bf16[256,512]{1,0:T(8,128)(2,1)S(1)}, u32[]{:S(2)}, u32[]{:S(2)}) %collective-permute-start.5) | collective-permute-done | bytes 262176 | tf_op jit(solution)/shard_map/ppermute | solution.py:303
  44.8 1.1 %shard_map.77 = bf16[1536,512]{1,0:T(8,128)(2,1)} custom-call(bf16[768,512]{1,0:T(8,128)(2,1)S(1)} %get-tuple-element.69.refs_0_, bf16[768,512]{1,0:T(8,128)(2,1)S(1)} %collective-permute-done.2.refs_1_, s32[8,128]{1,0:T(8,128)S(1)} %get-tuple-element.71.refs_2_, f32[24,128]{1,0:T(8,128)S(1)} %get-tuple-element.72.refs_3_, ...), custom_call_target="tpu_custom_call", output_to_operand_aliasing={{}: (10, {})} | custom-call | flops 20000000000 | bytes 1 | tf_op jit(solution)/shard_map/pallas_call | solution.py:265
Async XLA Ops:
  0.0 0.7 %copy-start.3 = (bf16[1024]{0:T(1024)(128)(2,1)S(1)}, bf16[1024]{0:T(1024)(128)(2,1)}, u32[]{:S(2)}) copy-start(bf16[1024]{0:T(1024)(128)(2,1)} %gain.6) | copy-start | bytes 6148
  0.7 3.6 %copy-start.4 = (s32[4]{0:T(128)S(1)}, s32[4]{0:T(128)}, u32[]{:S(2)}) copy-start(s32[4]{0:T(128)} %live) | copy-start | bytes 52
  0.7 3.6 %copy-start.5 = (s32[4]{0:T(128)S(1)}, s32[4]{0:T(128)}, u32[]{:S(2)}) copy-start(s32[4]{0:T(128)} %span) | copy-start | bytes 52
  0.7 3.6 %copy-start.6 = (f32[1,128]{1,0:T(1,128)S(1)}, f32[1,128]{1,0:T(1,128)}, u32[]{:S(2)}) copy-start(f32[1,128]{1,0:T(1,128)} %constant.4.clone.frequencies) | copy-start | bytes 1540
  3.8 2.1 %collective-permute-start = (bf16[528,512]{1,0:T(8,128)(2,1)S(1)}, bf16[528,512]{1,0:T(8,128)(2,1)S(1)}, u32[]{:S(2)}, u32[]{:S(2)}) collective-permute-start(bf16[528,512]{1,0:T(8,128)(2,1)S(1)} %get-tuple-element.51), channel_id=1, source_target_pairs={{0,1},{1,0},{2,3},{3,2},{4,5},{5,4},{6,7},{7,6},{8,9},{9,8},{10,11... | collective-permute-start | bytes 1622024 | tf_op jit(solution)/shard_map/ppermute | solution.py:297
  6.0 15.6 %collective-permute-start.9 = (bf16[528,512]{1,0:T(8,128)(2,1)S(1)}, bf16[528,512]{1,0:T(8,128)(2,1)S(1)}, u32[]{:S(2)}, u32[]{:S(2)}) collective-permute-start(bf16[528,512]{1,0:T(8,128)(2,1)S(1)} %get-tuple-element.88), channel_id=1, source_target_pairs={{0,2},{1,3},{2,0},{3,1},{4,6},{5,7},{6,4},{7,5},{8,10},{9,11},{10,... | collective-permute-start | bytes 1622024 | tf_op jit(solution)/shard_map/ppermute | solution.py:303
  8.9 2.2 %copy-start = (bf16[1024,2048]{1,0:T(8,128)(2,1)S(1)}, bf16[1024,2048]{1,0:T(8,128)(2,1)}, u32[]{:S(2)}) copy-start(bf16[1024,2048]{1,0:T(8,128)(2,1)} %weight.11) | copy-start | bytes 12582916
  11.1 1.9 %copy-start.1 = (bf16[1536,1024]{1,0:T(8,128)(2,1)S(1)}, bf16[1536,1024]{1,0:T(8,128)(2,1)}, u32[]{:S(2)}) copy-start(bf16[1536,1024]{1,0:T(8,128)(2,1)} %tokens.11) | copy-start | bytes 9437188
  14.3 5.0 %collective-permute-start.8 = (bf16[512,512]{1,0:T(8,128)(2,1)S(1)}, bf16[512,512]{1,0:T(8,128)(2,1)S(1)}, u32[]{:S(2)}, u32[]{:S(2)}) collective-permute-start(bf16[512,512]{1,0:T(8,128)(2,1)S(1)} %get-tuple-element.86), channel_id=1, source_target_pairs={{0,1},{1,0},{2,3},{3,2},{4,5},{5,4},{6,7},{7,6},{8,9},{9,8},{10,11... | collective-permute-start | bytes 1572872 | tf_op jit(solution)/shard_map/ppermute | solution.py:326
  15.4 3.8 %collective-permute-start.3 = (bf16[272,512]{1,0:T(8,128)(2,1)S(1)}, bf16[272,512]{1,0:T(8,128)(2,1)S(1)}, u32[]{:S(2)}, u32[]{:S(2)}) collective-permute-start(bf16[272,512]{1,0:T(8,128)(2,1)S(1)} %get-tuple-element.77), channel_id=1, source_target_pairs={{0,1},{1,0},{2,3},{3,2},{4,5},{5,4},{6,7},{7,6},{8,9},{9,8},{10,11... | collective-permute-start | bytes 835592 | tf_op jit(solution)/shard_map/ppermute | solution.py:297
  18.6 9.1 %collective-permute-start.7 = (bf16[256,512]{1,0:T(8,128)(2,1)S(1)}, bf16[256,512]{1,0:T(8,128)(2,1)S(1)}, u32[]{:S(2)}, u32[]{:S(2)}) collective-permute-start(bf16[256,512]{1,0:T(8,128)(2,1)S(1)} %get-tuple-element.84), channel_id=1, source_target_pairs={{0,1},{1,0},{2,3},{3,2},{4,5},{5,4},{6,7},{7,6},{8,9},{9,8},{10,11... | collective-permute-start | bytes 786440 | tf_op jit(solution)/shard_map/ppermute | solution.py:326
  18.7 4.3 %collective-permute-start.1 = (bf16[768,512]{1,0:T(8,128)(2,1)S(1)}, bf16[768,512]{1,0:T(8,128)(2,1)S(1)}, u32[]{:S(2)}, u32[]{:S(2)}) collective-permute-start(bf16[768,512]{1,0:T(8,128)(2,1)S(1)} %get-tuple-element.65), channel_id=1, source_target_pairs={{0,1},{1,0},{2,3},{3,2},{4,5},{5,4},{6,7},{7,6},{8,9},{9,8},{10,11... | collective-permute-start | bytes 2359304 | tf_op jit(solution)/shard_map/ppermute | solution.py:297
  19.2 9.6 %collective-permute-start.4 = (bf16[272,512]{1,0:T(8,128)(2,1)S(1)}, bf16[272,512]{1,0:T(8,128)(2,1)S(1)}, u32[]{:S(2)}, u32[]{:S(2)}) collective-permute-start(bf16[272,512]{1,0:T(8,128)(2,1)S(1)} %get-tuple-element.80), channel_id=1, source_target_pairs={{0,2},{1,3},{2,0},{3,1},{4,6},{5,7},{6,4},{7,5},{8,10},{9,11},{10,... | collective-permute-start | bytes 835592 | tf_op jit(solution)/shard_map/ppermute | solution.py:303
  21.6 4.2 %copy-start.2 = (bf16[1536,1024]{1,0:T(8,128)(2,1)S(1)}, bf16[1536,1024]{1,0:T(8,128)(2,1)}, u32[]{:S(2)}) copy-start(bf16[1536,1024]{1,0:T(8,128)(2,1)} %tokens.11) | copy-start | bytes 9437188
  23.2 16.9 %collective-permute-start.6 = (bf16[512,512]{1,0:T(8,128)(2,1)S(1)}, bf16[512,512]{1,0:T(8,128)(2,1)S(1)}, u32[]{:S(2)}, u32[]{:S(2)}) collective-permute-start(bf16[512,512]{1,0:T(8,128)(2,1)S(1)} %get-tuple-element.82), channel_id=1, source_target_pairs={{0,2},{1,3},{2,0},{3,1},{4,6},{5,7},{6,4},{7,5},{8,10},{9,11},{10,... | collective-permute-start | bytes 1572872 | tf_op jit(solution)/shard_map/ppermute | solution.py:303
  27.6 12.5 %collective-permute-start.2 = (bf16[768,512]{1,0:T(8,128)(2,1)S(1)}, bf16[768,512]{1,0:T(8,128)(2,1)S(1)}, u32[]{:S(2)}, u32[]{:S(2)}) collective-permute-start(bf16[768,512]{1,0:T(8,128)(2,1)S(1)} %get-tuple-element.70), channel_id=1, source_target_pairs={{0,1},{1,0},{2,3},{3,2},{4,5},{5,4},{6,7},{7,6},{8,9},{9,8},{10,11... | collective-permute-start | bytes 2359304 | tf_op jit(solution)/shard_map/ppermute | solution.py:326
  29.9 14.9 %collective-permute-start.5 = (bf16[256,512]{1,0:T(8,128)(2,1)S(1)}, bf16[256,512]{1,0:T(8,128)(2,1)S(1)}, u32[]{:S(2)}, u32[]{:S(2)}) collective-permute-start(bf16[256,512]{1,0:T(8,128)(2,1)S(1)} %get-tuple-element.81), channel_id=1, source_target_pairs={{0,2},{1,3},{2,0},{3,1},{4,6},{5,7},{6,4},{7,5},{8,10},{9,11},{10,... | collective-permute-start | bytes 786440 | tf_op jit(solution)/shard_map/ppermute | solution.py:303

commit v20 on v19

--- a/solution.py
+++ b/solution.py
@@ -22,9 +22,10 @@
 CHUNKS = (2, 1, 3)
 
 PARAMS = pltpu.CompilerParams(vmem_limit_bytes=16 * 1024 * 1024)
-FIRST = pltpu.CompilerParams(vmem_limit_bytes=53248 * 1024)
+FIRST = pltpu.CompilerParams(vmem_limit_bytes=51200 * 1024)
 LATER = pl.CostEstimate(flops=20000000000, bytes_accessed=1, transcendentals=0)
 HEAVY = pl.CostEstimate(flops=1000000000000, bytes_accessed=1, transcendentals=0)
+BRING = pltpu.CompilerParams(vmem_limit_bytes=47104 * 1024)
 COST = pl.CostEstimate(flops=1, bytes_accessed=1, transcendentals=0)
 
 
@@ -73,7 +74,7 @@
 
     weight_copies, row_copies = [], []
     if staged:
-        rows_buf, weight_buf, gain_buf, weight_sems, row_sems, gain_sem = refs
+        weight_buf, rows_buf, gain_buf, weight_sems, row_sems, gain_sem = refs
         cut = depth // CUTS
         gain_copy = pltpu.make_async_copy(gain, gain_buf, gain_sem)
         for index in range(CUTS):
@@ -110,7 +111,7 @@
                 product += jnp.dot(scaled[:, span], weight_buf[span, :], preferred_element_type=jnp.float32)
             weight_copies = []
         else:
-            columns = weight_buf[...] if staged else weight[:, place]
+            columns = weight_buf[...] if staged else weight[...]
             product = jnp.dot(scaled, columns, preferred_element_type=jnp.float32)
         left = product[:, : width // 2].astype(jnp.bfloat16)
         right = product[:, width // 2 :].astype(jnp.bfloat16)
@@ -124,6 +125,21 @@
         for index, line in enumerate(lines):
             squares[index : index + 1, :] = line
         send[pl.ds(keep.shape[0], 2 * SUBLANES), :] = packed(lines, send.shape[1])
+
+
+def bring_kernel(tokens, gain, weight, rows_out, gain_out, weight_out, sems):
+    width = weight_out.shape[1]
+    chip = lax.div(lax.axis_index("tensor"), 2)
+    place = pl.ds(pl.multiple_of(chip * width, width), width)
+    moves = [
+        pltpu.make_async_copy(tokens, rows_out, sems.at[0]),
+        pltpu.make_async_copy(gain, gain_out, sems.at[1]),
+        pltpu.make_async_copy(weight.at[:, place], weight_out, sems.at[2]),
+    ]
+    for move in moves:
+        move.start()
+    for move in moves:
+        move.wait()
 
 
 def add_kernel(lines, keep, received, *refs):
@@ -216,16 +232,17 @@
     def shift(step):
         return [(i, (i + 2 * step) % tensor_count) for i in range(tensor_count)]
 
-    def product(gain, step, first, count, staged=False, carrier=True, more=0):
+    def product(tokens, gain, kv_weight, step, first, count, staged=False, carrier=True, more=0):
         vmem = pl.BlockSpec(memory_space=pltpu.VMEM)
         rows = count * TILE
         out_shape = [jax.ShapeDtypeStruct((rows, columns), jnp.bfloat16)] * 2
         if carrier:
             out_shape[1] = jax.ShapeDtypeStruct((rows + 2 * SUBLANES, columns), jnp.bfloat16)
             out_shape.append(jax.ShapeDtypeStruct((rows // LANES + more * TILE // LANES, LANES), jnp.float32))
+        if staged:
+            out_shape.append(jax.ShapeDtypeStruct((depth, 2 * columns), jnp.bfloat16))
         scratch = [
             pltpu.VMEM((rows, depth), jnp.bfloat16),
-            pltpu.VMEM((depth, 2 * columns), jnp.bfloat16),
             pltpu.VMEM((depth,), jnp.bfloat16),
             pltpu.SemaphoreType.DMA((CUTS,)),
             pltpu.SemaphoreType.DMA((count,)),
@@ -303,23 +320,36 @@
         return [lax.ppermute(part, "tensor", shift(step)) for step, part in zip(others, sums)]
 
     hold = lax.optimization_barrier
-    made = [product(norm_gain, step, *chunks[0], staged=True) for step in others]
+    made = [product(tokens, norm_gain, kv_weight, step, *chunks[0], staged=True) for step in others]
+    weights = {step: parts[-1] for step, parts in zip(others, made)}
+    made = [parts[:-1] for parts in made]
     made, gain, span_offset, live_blocks = hold((made, norm_gain, span_offset, live_blocks))
     table = tables(live_blocks, span_offset)
     sums = add_halves(made, chunks[0][1:])
     sums, gain, table = hold((sums, gain, table))
+    tokens, gain, own_weight = pl.pallas_call(
+        bring_kernel,
+        in_specs=[pl.BlockSpec(memory_space=pltpu.HBM)] * 3,
+        out_shape=[
+            jax.ShapeDtypeStruct(shape, jnp.bfloat16) for shape in (tokens.shape, gain.shape, (depth, 2 * columns))
+        ],
+        out_specs=[pl.BlockSpec(memory_space=pltpu.VMEM)] * 3,
+        scratch_shapes=[pltpu.SemaphoreType.DMA((3,))],
+        compiler_params=BRING,
+        cost_estimate=COST,
+    )(tokens, gain, kv_weight)
 
     arrivals = [([cross(part) for part in sums[0]], sums[1])]
     for index in range(1, chunk_count):
         more = sum(CHUNKS[2:]) if index == 1 else 0
-        made = [product(gain, step, *chunks[index], carrier=index == 1, more=more) for step in others]
+        made = [product(tokens, gain, weights[step], step, *chunks[index], carrier=index == 1, more=more) for step in others]
         count = chunks[index][1]
         sums = add_halves(made, (count - 1, 1) if count > 2 else (count,))
         if index == 2:
             sums, late = hold((sums, gain))
         arrivals.append(([cross(part) for part in sums[0]], sums[1]))
-    own = [product(gain, 0, *chunk, carrier=False) for chunk in chunks[:-1]]
-    own.append(product(late, 0, *chunks[-1], carrier=False))
+    own = [product(tokens, gain, own_weight, 0, *chunk, carrier=False) for chunk in chunks[:-1]]
+    own.append(product(tokens, late, own_weight, 0, *chunks[-1], carrier=False))
 
     result = None
     for (first, count), (keep, send), (arrived, squares) in zip(chunks, own, arrivals):

time: 46.1 us -> 45.6 us (0.989)
  local copies, waits for them, and re-layouts: 4.77 us -> 0.7 us
  Pallas kernels: 15.9 us -> 18.6 us
  waiting for transfers between devices: 16.4 us -> 17 us
    unnamed x14 -> x10, local copies, waits for them, and re-layouts: 4.77 us -> 0.7 us
    pallas_call x0 -> x1, Pallas kernels: none -> 2.57 us  [shards(): pl.pallas_call(bring_kernel, in_specs=[pl.BlockSpec(memory_space=pltpu.HB...]
    ppermute x4, waiting for transfers between devices: 15.6 us -> 16.2 us  [cross(): lax.ppermute(part, 'tensor', shift(step))]
  transfers between devices with their start and end apart: 10 -> 10, of which waited for: 5 -> 5; matrix products, arithmetic and copies ran while one was open for 0% -> 0% of each run, Pallas kernels for 25% -> 31%
where the time goes in v20:
time: 45.6 us; the launch traced here: 45.5 us
  Pallas kernels  18.6 us (41%)
  waiting for transfers between devices  17 us (37%)
  starting transfers between devices  9.05 us (20%)
  local copies, waits for them, and re-layouts  0.7 us (2%)
    ppermute x4, waiting for transfers between devices, cross(): lax.ppermute(part, 'tensor', shift(step))  16.2 us
    pallas_call x6, Pallas kernels, product(): pl.pallas_call(functools.partial(product_kernel, step, chip_count, first,...  9.87 us
    ppermute x4, starting transfers between devices, cross(): lax.ppermute(part, 'tensor', shift(step))  7.26 us
    pallas_call x4, Pallas kernels, finish(): pl.pallas_call(functools.partial(finish_kernel, first, at, line_at, count...  5.01 us
    pallas_call x1, Pallas kernels, shards(): pl.pallas_call(bring_kernel, in_specs=[pl.BlockSpec(memory_space=pltpu.HB...  2.57 us
    ppermute x3, starting transfers between devices, add_halves(): lax.ppermute(send, 'tensor', swap)  1.56 us
  transfers between devices with their start and end apart: 10, of which 5 were waited for; matrix products, arithmetic and copies ran while one was open for 0% of the time, Pallas kernels for 31%

profile of v20, /device:TPU:0, one launch (start us, length us, event | category | flops | bytes accessed | tf_op | source)
XLA Modules:
  0.0 45.5 jit_solution(11956449995228502572)
XLA Ops:
  0.0 0.0 copy-start
  0.0 0.7 %copy-done = bf16[1024]{0:T(1024)(128)(2,1)S(1)} copy-done((bf16[1024]{0:T(1024)(128)(2,1)S(1)}, bf16[1024]{0:T(1024)(128)(2,1)}, u32[]{:S(2)}) %copy-start) | copy-done | bytes 2072
  0.7 0.0 copy-start.2
  0.7 0.0 copy-start.3
  0.7 0.0 copy-start.4
  0.7 0.0 copy-start.1
  0.7 3.1 %shard_map.64 = (bf16[512,512]{1,0:T(8,128)(2,1)S(1)}, bf16[528,512]{1,0:T(8,128)(2,1)S(1)}, f32[4,128]{1,0:T(4,128)S(1)}, bf16[1024,1024]{1,0:T(8,128)(2,1)S(1)}) custom-call(bf16[1536,1024]{1,0:T(8,128)(2,1)} %tokens.3, bf16[1024]{0:T(1024)(128)(2,1)S(1)} %copy-done, bf16[1024,2048]{1,0:T(8,128)(2,1)} %weight.3), custom_call_target="tpu_custom_call" | custom-call | flops 999999995904 | bytes 1 | tf_op jit(solution)/shard_map/pallas_call | solution.py:251
  3.8 0.5 %collective-permute-start = (bf16[528,512]{1,0:T(8,128)(2,1)S(1)}, bf16[528,512]{1,0:T(8,128)(2,1)S(1)}, u32[]{:S(2)}, u32[]{:S(2)}) collective-permute-start(bf16[528,512]{1,0:T(8,128)(2,1)S(1)} %get-tuple-element.55), channel_id=1, source_target_pairs={{0,1},{1,0},{2,3},{3,2},{4,5},{5,4},{6,7},{7,6},{8,9},{9,8},{10,11... | collective-permute-start | bytes 1622024 | tf_op jit(solution)/shard_map/ppermute | solution.py:314
  4.4 0.0 copy-done.2
  4.4 0.0 copy-done.3
  4.4 0.0 copy-done.4
  4.4 0.7 %shard_map.66 = (s32[8,128]{1,0:T(8,128)S(1)}, f32[24,128]{1,0:T(8,128)S(1)}, f32[24,128]{1,0:T(8,128)S(1)}, f32[64,128]{1,0:T(8,128)S(1)}, f32[64,128]{1,0:T(8,128)S(1)}) custom-call(s32[4]{0:T(128)S(1)} %copy-done.2, s32[4]{0:T(128)S(1)} %copy-done.3, f32[1,128]{1,0:T(1,128)S(1)} %copy-done.4), custom_call_target="tpu_custom_call" | custom-call | flops 1 | bytes 1 | tf_op jit(solution)/shard_map/pallas_call | solution.py:265
  5.1 0.8 %collective-permute-done.received = bf16[528,512]{1,0:T(8,128)(2,1)S(1)} collective-permute-done((bf16[528,512]{1,0:T(8,128)(2,1)S(1)}, bf16[528,512]{1,0:T(8,128)(2,1)S(1)}, u32[]{:S(2)}, u32[]{:S(2)}) %collective-permute-start) | collective-permute-done | bytes 540704 | tf_op jit(solution)/shard_map/ppermute | solution.py:314
  5.9 0.1 shard_map.65
  6.1 2.9 %collective-permute-start.9 = (bf16[528,512]{1,0:T(8,128)(2,1)S(1)}, bf16[528,512]{1,0:T(8,128)(2,1)S(1)}, u32[]{:S(2)}, u32[]{:S(2)}) collective-permute-start(bf16[528,512]{1,0:T(8,128)(2,1)S(1)} %get-tuple-element.96), channel_id=1, source_target_pairs={{0,2},{1,3},{2,0},{3,1},{4,6},{5,7},{6,4},{7,5},{8,10},{9,11},{10,... | collective-permute-start | bytes 1622024 | tf_op jit(solution)/shard_map/ppermute | solution.py:320
  9.0 0.0 copy-done.1
  9.0 2.6 %shard_map.67 = (bf16[1536,1024]{1,0:T(8,128)(2,1)S(1)}, bf16[1024]{0:T(1024)(128)(2,1)S(1)}, bf16[1024,1024]{1,0:T(8,128)(2,1)S(1)}) custom-call(bf16[1536,1024]{1,0:T(8,128)(2,1)} %tokens.3, bf16[1024]{0:T(1024)(128)(2,1)S(1)} %copy-done.1, bf16[1024,2048]{1,0:T(8,128)(2,1)} %weight.3), custom_call_target="tpu_custom_call" | custom-call | flops 1 | bytes 1 | tf_op jit(solution)/shard_map/pallas_call | solution.py:330
  11.6 1.3 %shard_map.74 = (bf16[512,512]{1,0:T(8,128)(2,1)S(1)}, bf16[512,512]{1,0:T(8,128)(2,1)S(1)}) custom-call(bf16[1536,1024]{1,0:T(8,128)(2,1)S(1)} %get-tuple-element.68.tokens, bf16[1024]{0:T(1024)(128)(2,1)S(1)} %get-tuple-element.75.gain, bf16[1024,1024]{1,0:T(8,128)(2,1)S(1)} %get-tuple-element.76.weight), custom_call_target="tpu_custom_call" | custom-call | flops 1 | bytes 1 | tf_op jit(solution)/shard_map/pallas_call | solution.py:251
  12.9 0.1 collective-permute-start.8
  12.9 1.0 %shard_map.71 = (bf16[256,512]{1,0:T(8,128)(2,1)S(1)}, bf16[272,512]{1,0:T(8,128)(2,1)S(1)}, f32[8,128]{1,0:T(8,128)S(1)}) custom-call(bf16[1536,1024]{1,0:T(8,128)(2,1)S(1)} %get-tuple-element.68.tokens, bf16[1024]{0:T(1024)(128)(2,1)S(1)} %get-tuple-element.75.gain, bf16[1024,1024]{1,0:T(8,128)(2,1)S(1)} %get-tuple-element.70.weight), custom_call_target="tpu_custom_call" | custom-call | flops 1 | bytes 1 | tf_op jit(solution)/shard_map/pallas_call | solution.py:251
  13.9 0.6 %collective-permute-start.3 = (bf16[272,512]{1,0:T(8,128)(2,1)S(1)}, bf16[272,512]{1,0:T(8,128)(2,1)S(1)}, u32[]{:S(2)}, u32[]{:S(2)}) collective-permute-start(bf16[272,512]{1,0:T(8,128)(2,1)S(1)} %get-tuple-element.85), channel_id=1, source_target_pairs={{0,1},{1,0},{2,3},{3,2},{4,5},{5,4},{6,7},{7,6},{8,9},{9,8},{10,11... | collective-permute-start | bytes 835592 | tf_op jit(solution)/shard_map/ppermute | solution.py:314
  14.5 0.7 %shard_map.73 = (bf16[256,512]{1,0:T(8,128)(2,1)S(1)}, bf16[256,512]{1,0:T(8,128)(2,1)S(1)}) custom-call(bf16[1536,1024]{1,0:T(8,128)(2,1)S(1)} %get-tuple-element.68.tokens, bf16[1024]{0:T(1024)(128)(2,1)S(1)} %get-tuple-element.75.gain, bf16[1024,1024]{1,0:T(8,128)(2,1)S(1)} %get-tuple-element.76.weight), custom_call_target="tpu_custom_call" | custom-call | flops 1 | bytes 1 | tf_op jit(solution)/shard_map/pallas_call | solution.py:251
  15.2 1.9 %shard_map.68 = (bf16[768,512]{1,0:T(8,128)(2,1)S(1)}, bf16[768,512]{1,0:T(8,128)(2,1)S(1)}) custom-call(bf16[1536,1024]{1,0:T(8,128)(2,1)S(1)} %get-tuple-element.68.tokens, bf16[1024]{0:T(1024)(128)(2,1)S(1)} %get-tuple-element.75.gain, bf16[1024,1024]{1,0:T(8,128)(2,1)S(1)} %get-tuple-element.70.weight), custom_call_target="tpu_custom_call" | custom-call | flops 1 | bytes 1 | tf_op jit(solution)/shard_map/pallas_call | solution.py:251
  17.1 0.1 collective-permute-start.7
  17.2 0.5 %collective-permute-start.1 = (bf16[768,512]{1,0:T(8,128)(2,1)S(1)}, bf16[768,512]{1,0:T(8,128)(2,1)S(1)}, u32[]{:S(2)}, u32[]{:S(2)}) collective-permute-start(bf16[768,512]{1,0:T(8,128)(2,1)S(1)} %get-tuple-element.72), channel_id=1, source_target_pairs={{0,1},{1,0},{2,3},{3,2},{4,5},{5,4},{6,7},{7,6},{8,9},{9,8},{10,11... | collective-permute-start | bytes 2359304 | tf_op jit(solution)/shard_map/ppermute | solution.py:314
  17.7 0.0 collective-permute-done.3.received
  17.7 0.1 shard_map.72
  17.8 0.1 collective-permute-start.4
  17.9 0.0 collective-permute-done.8.refs_1_
  17.9 4.2 %collective-permute-done.9.refs_8_ = bf16[528,512]{1,0:T(8,128)(2,1)S(1)} collective-permute-done((bf16[528,512]{1,0:T(8,128)(2,1)S(1)}, bf16[528,512]{1,0:T(8,128)(2,1)S(1)}, u32[]{:S(2)}, u32[]{:S(2)}) %collective-permute-start.9) | collective-permute-done | bytes 540704 | tf_op jit(solution)/shard_map/ppermute | solution.py:320
  22.0 1.4 %shard_map.75.refs_9_ = bf16[1536,512]{1,0:T(8,128)(2,1)} custom-call(bf16[512,512]{1,0:T(8,128)(2,1)S(1)} %get-tuple-element.93.refs_0_, bf16[512,512]{1,0:T(8,128)(2,1)S(1)} %collective-permute-done.8.refs_1_, s32[8,128]{1,0:T(8,128)S(1)} %get-tuple-element.79.refs_2_, f32[24,128]{1,0:T(8,128)S(1)} %get-tuple-element.80.refs_3_, ...), custom_call_target="tpu_custom_call" | custom-call | flops 20000000000 | bytes 1 | tf_op jit(solution)/shard_map/pallas_call | solution.py:282
  23.5 0.0 collective-permute-done.1.received
  23.5 0.2 shard_map.69
  23.7 2.1 %collective-permute-start.6 = (bf16[512,512]{1,0:T(8,128)(2,1)S(1)}, bf16[512,512]{1,0:T(8,128)(2,1)S(1)}, u32[]{:S(2)}, u32[]{:S(2)}) collective-permute-start(bf16[512,512]{1,0:T(8,128)(2,1)S(1)} %get-tuple-element.90), channel_id=1, source_target_pairs={{0,2},{1,3},{2,0},{3,1},{4,6},{5,7},{6,4},{7,5},{8,10},{9,11},{10,... | collective-permute-start | bytes 1572872 | tf_op jit(solution)/shard_map/ppermute | solution.py:320
  25.8 1.9 %shard_map.70 = (bf16[768,512]{1,0:T(8,128)(2,1)S(1)}, bf16[768,512]{1,0:T(8,128)(2,1)S(1)}) custom-call(bf16[1536,1024]{1,0:T(8,128)(2,1)S(1)} %get-tuple-element.68.tokens, bf16[1024]{0:T(1024)(128)(2,1)S(1)} %get-tuple-element.75.gain, bf16[1024,1024]{1,0:T(8,128)(2,1)S(1)} %get-tuple-element.76.weight), custom_call_target="tpu_custom_call" | custom-call | flops 1 | bytes 1 | tf_op jit(solution)/shard_map/pallas_call | solution.py:251
  27.7 0.1 collective-permute-start.2
  27.7 0.0 collective-permute-done.7.refs_1_
  27.7 0.3 collective-permute-done.4.refs_8_
  28.0 1.1 %shard_map.76.refs_10_ = bf16[1536,512]{1,0:T(8,128)(2,1)} custom-call(bf16[256,512]{1,0:T(8,128)(2,1)S(1)} %get-tuple-element.91.refs_0_, bf16[256,512]{1,0:T(8,128)(2,1)S(1)} %collective-permute-done.7.refs_1_, s32[8,128]{1,0:T(8,128)S(1)} %get-tuple-element.79.refs_2_, f32[24,128]{1,0:T(8,128)S(1)} %get-tuple-element.80.refs_3_, ...), custom_call_target="tpu_custom_call", output_to_operand_aliasing={{}: (9, {})} | custom-call | flops 20000000000 | bytes 1 | tf_op jit(solution)/shard_map/pallas_call | solution.py:282
  29.1 2.1 %collective-permute-start.5 = (bf16[256,512]{1,0:T(8,128)(2,1)S(1)}, bf16[256,512]{1,0:T(8,128)(2,1)S(1)}, u32[]{:S(2)}, u32[]{:S(2)}) collective-permute-start(bf16[256,512]{1,0:T(8,128)(2,1)S(1)} %get-tuple-element.89), channel_id=1, source_target_pairs={{0,2},{1,3},{2,0},{3,1},{4,6},{5,7},{6,4},{7,5},{8,10},{9,11},{10,... | collective-permute-start | bytes 786440 | tf_op jit(solution)/shard_map/ppermute | solution.py:320
  31.3 8.0 %collective-permute-done.6.refs_9_ = bf16[512,512]{1,0:T(8,128)(2,1)S(1)} collective-permute-done((bf16[512,512]{1,0:T(8,128)(2,1)S(1)}, bf16[512,512]{1,0:T(8,128)(2,1)S(1)}, u32[]{:S(2)}, u32[]{:S(2)}) %collective-permute-start.6) | collective-permute-done | bytes 524320 | tf_op jit(solution)/shard_map/ppermute | solution.py:320
  39.2 0.0 collective-permute-done.2.refs_1_
  39.3 1.4 %shard_map.77.refs_10_ = bf16[1536,512]{1,0:T(8,128)(2,1)} custom-call(bf16[768,512]{1,0:T(8,128)(2,1)S(1)} %get-tuple-element.77.refs_0_, bf16[768,512]{1,0:T(8,128)(2,1)S(1)} %collective-permute-done.2.refs_1_, s32[8,128]{1,0:T(8,128)S(1)} %get-tuple-element.79.refs_2_, f32[24,128]{1,0:T(8,128)S(1)} %get-tuple-element.80.refs_3_, ...), custom_call_target="tpu_custom_call", output_to_operand_aliasing={{}: (10, {})} | custom-call | flops 20000000000 | bytes 1 | tf_op jit(solution)/shard_map/pallas_call | solution.py:282
  40.7 3.7 %collective-permute-done.5.refs_9_ = bf16[256,512]{1,0:T(8,128)(2,1)S(1)} collective-permute-done((bf16[256,512]{1,0:T(8,128)(2,1)S(1)}, bf16[256,512]{1,0:T(8,128)(2,1)S(1)}, u32[]{:S(2)}, u32[]{:S(2)}) %collective-permute-start.5) | collective-permute-done | bytes 262176 | tf_op jit(solution)/shard_map/ppermute | solution.py:320
  44.4 1.1 %shard_map.78 = bf16[1536,512]{1,0:T(8,128)(2,1)} custom-call(bf16[768,512]{1,0:T(8,128)(2,1)S(1)} %get-tuple-element.77.refs_0_, bf16[768,512]{1,0:T(8,128)(2,1)S(1)} %collective-permute-done.2.refs_1_, s32[8,128]{1,0:T(8,128)S(1)} %get-tuple-element.79.refs_2_, f32[24,128]{1,0:T(8,128)S(1)} %get-tuple-element.80.refs_3_, ...), custom_call_target="tpu_custom_call", output_to_operand_aliasing={{}: (10, {})} | custom-call | flops 20000000000 | bytes 1 | tf_op jit(solution)/shard_map/pallas_call | solution.py:282
Async XLA Ops:
  0.0 0.7 %copy-start = (bf16[1024]{0:T(1024)(128)(2,1)S(1)}, bf16[1024]{0:T(1024)(128)(2,1)}, u32[]{:S(2)}) copy-start(bf16[1024]{0:T(1024)(128)(2,1)} %gain.2) | copy-start | bytes 6148
  0.7 3.7 %copy-start.2 = (s32[4]{0:T(128)S(1)}, s32[4]{0:T(128)}, u32[]{:S(2)}) copy-start(s32[4]{0:T(128)} %live) | copy-start | bytes 52
  0.7 3.7 %copy-start.3 = (s32[4]{0:T(128)S(1)}, s32[4]{0:T(128)}, u32[]{:S(2)}) copy-start(s32[4]{0:T(128)} %span) | copy-start | bytes 52
  0.7 3.7 %copy-start.4 = (f32[1,128]{1,0:T(1,128)S(1)}, f32[1,128]{1,0:T(1,128)}, u32[]{:S(2)}) copy-start(f32[1,128]{1,0:T(1,128)} %constant.4.clone.frequencies) | copy-start | bytes 1540
  0.7 8.3 %copy-start.1 = (bf16[1024]{0:T(1024)(128)(2,1)S(1)}, bf16[1024]{0:T(1024)(128)(2,1)}, u32[]{:S(2)}) copy-start(bf16[1024]{0:T(1024)(128)(2,1)} %gain.2) | copy-start | bytes 6148
  3.8 2.1 %collective-permute-start = (bf16[528,512]{1,0:T(8,128)(2,1)S(1)}, bf16[528,512]{1,0:T(8,128)(2,1)S(1)}, u32[]{:S(2)}, u32[]{:S(2)}) collective-permute-start(bf16[528,512]{1,0:T(8,128)(2,1)S(1)} %get-tuple-element.55), channel_id=1, source_target_pairs={{0,1},{1,0},{2,3},{3,2},{4,5},{5,4},{6,7},{7,6},{8,9},{9,8},{10,11... | collective-permute-start | bytes 1622024 | tf_op jit(solution)/shard_map/ppermute | solution.py:314
  6.1 16.0 %collective-permute-start.9 = (bf16[528,512]{1,0:T(8,128)(2,1)S(1)}, bf16[528,512]{1,0:T(8,128)(2,1)S(1)}, u32[]{:S(2)}, u32[]{:S(2)}) collective-permute-start(bf16[528,512]{1,0:T(8,128)(2,1)S(1)} %get-tuple-element.96), channel_id=1, source_target_pairs={{0,2},{1,3},{2,0},{3,1},{4,6},{5,7},{6,4},{7,5},{8,10},{9,11},{10,... | collective-permute-start | bytes 1622024 | tf_op jit(solution)/shard_map/ppermute | solution.py:320
  12.9 5.0 %collective-permute-start.8 = (bf16[512,512]{1,0:T(8,128)(2,1)S(1)}, bf16[512,512]{1,0:T(8,128)(2,1)S(1)}, u32[]{:S(2)}, u32[]{:S(2)}) collective-permute-start(bf16[512,512]{1,0:T(8,128)(2,1)S(1)} %get-tuple-element.94), channel_id=1, source_target_pairs={{0,1},{1,0},{2,3},{3,2},{4,5},{5,4},{6,7},{7,6},{8,9},{9,8},{10,11... | collective-permute-start | bytes 1572872 | tf_op jit(solution)/shard_map/ppermute | solution.py:356
  13.9 3.7 %collective-permute-start.3 = (bf16[272,512]{1,0:T(8,128)(2,1)S(1)}, bf16[272,512]{1,0:T(8,128)(2,1)S(1)}, u32[]{:S(2)}, u32[]{:S(2)}) collective-permute-start(bf16[272,512]{1,0:T(8,128)(2,1)S(1)} %get-tuple-element.85), channel_id=1, source_target_pairs={{0,1},{1,0},{2,3},{3,2},{4,5},{5,4},{6,7},{7,6},{8,9},{9,8},{10,11... | collective-permute-start | bytes 835592 | tf_op jit(solution)/shard_map/ppermute | solution.py:314
  17.1 10.6 %collective-permute-start.7 = (bf16[256,512]{1,0:T(8,128)(2,1)S(1)}, bf16[256,512]{1,0:T(8,128)(2,1)S(1)}, u32[]{:S(2)}, u32[]{:S(2)}) collective-permute-start(bf16[256,512]{1,0:T(8,128)(2,1)S(1)} %get-tuple-element.92), channel_id=1, source_target_pairs={{0,1},{1,0},{2,3},{3,2},{4,5},{5,4},{6,7},{7,6},{8,9},{9,8},{10,11... | collective-permute-start | bytes 786440 | tf_op jit(solution)/shard_map/ppermute | solution.py:356
  17.2 6.3 %collective-permute-start.1 = (bf16[768,512]{1,0:T(8,128)(2,1)S(1)}, bf16[768,512]{1,0:T(8,128)(2,1)S(1)}, u32[]{:S(2)}, u32[]{:S(2)}) collective-permute-start(bf16[768,512]{1,0:T(8,128)(2,1)S(1)} %get-tuple-element.72), channel_id=1, source_target_pairs={{0,1},{1,0},{2,3},{3,2},{4,5},{5,4},{6,7},{7,6},{8,9},{9,8},{10,11... | collective-permute-start | bytes 2359304 | tf_op jit(solution)/shard_map/ppermute | solution.py:314
  17.8 10.2 %collective-permute-start.4 = (bf16[272,512]{1,0:T(8,128)(2,1)S(1)}, bf16[272,512]{1,0:T(8,128)(2,1)S(1)}, u32[]{:S(2)}, u32[]{:S(2)}) collective-permute-start(bf16[272,512]{1,0:T(8,128)(2,1)S(1)} %get-tuple-element.88), channel_id=1, source_target_pairs={{0,2},{1,3},{2,0},{3,1},{4,6},{5,7},{6,4},{7,5},{8,10},{9,11},{10,... | collective-permute-start | bytes 835592 | tf_op jit(solution)/shard_map/ppermute | solution.py:320
  23.7 15.6 %collective-permute-start.6 = (bf16[512,512]{1,0:T(8,128)(2,1)S(1)}, bf16[512,512]{1,0:T(8,128)(2,1)S(1)}, u32[]{:S(2)}, u32[]{:S(2)}) collective-permute-start(bf16[512,512]{1,0:T(8,128)(2,1)S(1)} %get-tuple-element.90), channel_id=1, source_target_pairs={{0,2},{1,3},{2,0},{3,1},{4,6},{5,7},{6,4},{7,5},{8,10},{9,11},{10,... | collective-permute-start | bytes 1572872 | tf_op jit(solution)/shard_map/ppermute | solution.py:320
  27.7 11.6 %collective-permute-start.2 = (bf16[768,512]{1,0:T(8,128)(2,1)S(1)}, bf16[768,512]{1,0:T(8,128)(2,1)S(1)}, u32[]{:S(2)}, u32[]{:S(2)}) collective-permute-start(bf16[768,512]{1,0:T(8,128)(2,1)S(1)} %get-tuple-element.78), channel_id=1, source_target_pairs={{0,1},{1,0},{2,3},{3,2},{4,5},{5,4},{6,7},{7,6},{8,9},{9,8},{10,11... | collective-permute-start | bytes 2359304 | tf_op jit(solution)/shard_map/ppermute | solution.py:356
  29.1 15.3 %collective-permute-start.5 = (bf16[256,512]{1,0:T(8,128)(2,1)S(1)}, bf16[256,512]{1,0:T(8,128)(2,1)S(1)}, u32[]{:S(2)}, u32[]{:S(2)}) collective-permute-start(bf16[256,512]{1,0:T(8,128)(2,1)S(1)} %get-tuple-element.89), channel_id=1, source_target_pairs={{0,2},{1,3},{2,0},{3,1},{4,6},{5,7},{6,4},{7,5},{8,10},{9,11},{10,... | collective-permute-start | bytes 786440 | tf_op jit(solution)/shard_map/ppermute | solution.py:320

commit v21 on v20

--- a/solution.py
+++ b/solution.py
@@ -87,32 +87,32 @@
             row_copies.append(
                 pltpu.make_async_copy(rows, rows_buf.at[pl.ds(tile * TILE, TILE), :], row_sems.at[tile])
             )
-        for copy in [gain_copy] + row_copies[:1] + weight_copies + row_copies[1:]:
+        for copy in [gain_copy] + row_copies + weight_copies:
             copy.start()
         gain_copy.wait()
         gains = gain_buf[...].reshape(1, depth)
     else:
         gains = gain[...].reshape(1, depth)
 
-    lines = []
+    products, lines = [], []
+    if staged:
+        scaled = []
+        for tile in range(count):
+            row_copies[tile].wait()
+            scaled.append(rows_buf[pl.ds(tile * TILE, TILE), :] * gains)
+        for index, copy in enumerate(weight_copies):
+            copy.wait()
+            span = slice(index * cut, (index + 1) * cut)
+            for tile in range(count):
+                part = jnp.dot(scaled[tile][:, span], weight_buf[span, :], preferred_element_type=jnp.float32)
+                products[tile : tile + 1] = [products[tile] + part if index else part]
     for tile in range(count):
         inside = pl.ds(tile * TILE, TILE)
         if staged:
-            row_copies[tile].wait()
-            rows = rows_buf[inside, :]
+            rows, product = rows_buf[inside, :], products[tile]
         else:
             rows = tokens[pl.ds((first + tile) * TILE, TILE), :]
-        scaled = rows * gains
-        if weight_copies:
-            product = jnp.zeros((TILE, width), jnp.float32)
-            for index, copy in enumerate(weight_copies):
-                copy.wait()
-                span = slice(index * cut, (index + 1) * cut)
-                product += jnp.dot(scaled[:, span], weight_buf[span, :], preferred_element_type=jnp.float32)
-            weight_copies = []
-        else:
-            columns = weight_buf[...] if staged else weight[...]
-            product = jnp.dot(scaled, columns, preferred_element_type=jnp.float32)
+            product = jnp.dot(rows * gains, weight[...], preferred_element_type=jnp.float32)
         left = product[:, : width // 2].astype(jnp.bfloat16)
         right = product[:, width // 2 :].astype(jnp.bfloat16)
         keep[inside, :] = jnp.where(core == 0, left, right)

time: 45.6 us -> 45.8 us (level)
  no operation moved by 1% of the time
where the time goes in v21:
time: 45.8 us; the launch traced here: 45.7 us
  Pallas kernels  18.7 us (41%)
  waiting for transfers between devices  17 us (37%)
  starting transfers between devices  9.06 us (20%)
  local copies, waits for them, and re-layouts  0.7 us (2%)
    ppermute x4, waiting for transfers between devices, cross(): lax.ppermute(part, 'tensor', shift(step))  16.2 us
    pallas_call x6, Pallas kernels, product(): pl.pallas_call(functools.partial(product_kernel, step, chip_count, first,...  10 us
    ppermute x4, starting transfers between devices, cross(): lax.ppermute(part, 'tensor', shift(step))  7.26 us
    pallas_call x4, Pallas kernels, finish(): pl.pallas_call(functools.partial(finish_kernel, first, at, line_at, count...  5.01 us
    pallas_call x1, Pallas kernels, shards(): pl.pallas_call(bring_kernel, in_specs=[pl.BlockSpec(memory_space=pltpu.HB...  2.57 us
    ppermute x3, starting transfers between devices, add_halves(): lax.ppermute(send, 'tensor', swap)  1.57 us
  transfers between devices with their start and end apart: 10, of which 5 were waited for; matrix products, arithmetic and copies ran while one was open for 0% of the time, Pallas kernels for 31%

profile of v21, /device:TPU:0, one launch (start us, length us, event | category | flops | bytes accessed | tf_op | source)
XLA Modules:
  0.0 45.7 jit_solution(2319939806103150558)
XLA Ops:
  0.0 0.0 copy-start
  0.0 0.7 %copy-done = bf16[1024]{0:T(1024)(128)(2,1)S(1)} copy-done((bf16[1024]{0:T(1024)(128)(2,1)S(1)}, bf16[1024]{0:T(1024)(128)(2,1)}, u32[]{:S(2)}) %copy-start) | copy-done | bytes 2072
  0.7 0.0 copy-start.2
  0.7 0.0 copy-start.3
  0.7 0.0 copy-start.4
  0.7 0.0 copy-start.1
  0.7 3.3 %shard_map.64 = (bf16[512,512]{1,0:T(8,128)(2,1)S(1)}, bf16[528,512]{1,0:T(8,128)(2,1)S(1)}, f32[4,128]{1,0:T(4,128)S(1)}, bf16[1024,1024]{1,0:T(8,128)(2,1)S(1)}) custom-call(bf16[1536,1024]{1,0:T(8,128)(2,1)} %tokens.3, bf16[1024]{0:T(1024)(128)(2,1)S(1)} %copy-done, bf16[1024,2048]{1,0:T(8,128)(2,1)} %weight.3), custom_call_target="tpu_custom_call" | custom-call | flops 999999995904 | bytes 1 | tf_op jit(solution)/shard_map/pallas_call | solution.py:251
  4.0 0.5 %collective-permute-start = (bf16[528,512]{1,0:T(8,128)(2,1)S(1)}, bf16[528,512]{1,0:T(8,128)(2,1)S(1)}, u32[]{:S(2)}, u32[]{:S(2)}) collective-permute-start(bf16[528,512]{1,0:T(8,128)(2,1)S(1)} %get-tuple-element.55), channel_id=1, source_target_pairs={{0,1},{1,0},{2,3},{3,2},{4,5},{5,4},{6,7},{7,6},{8,9},{9,8},{10,11... | collective-permute-start | bytes 1622024 | tf_op jit(solution)/shard_map/ppermute | solution.py:314
  4.5 0.0 copy-done.2
  4.5 0.0 copy-done.3
  4.5 0.0 copy-done.4
  4.5 0.7 %shard_map.66 = (s32[8,128]{1,0:T(8,128)S(1)}, f32[24,128]{1,0:T(8,128)S(1)}, f32[24,128]{1,0:T(8,128)S(1)}, f32[64,128]{1,0:T(8,128)S(1)}, f32[64,128]{1,0:T(8,128)S(1)}) custom-call(s32[4]{0:T(128)S(1)} %copy-done.2, s32[4]{0:T(128)S(1)} %copy-done.3, f32[1,128]{1,0:T(1,128)S(1)} %copy-done.4), custom_call_target="tpu_custom_call" | custom-call | flops 1 | bytes 1 | tf_op jit(solution)/shard_map/pallas_call | solution.py:265
  5.3 0.8 %collective-permute-done.received = bf16[528,512]{1,0:T(8,128)(2,1)S(1)} collective-permute-done((bf16[528,512]{1,0:T(8,128)(2,1)S(1)}, bf16[528,512]{1,0:T(8,128)(2,1)S(1)}, u32[]{:S(2)}, u32[]{:S(2)}) %collective-permute-start) | collective-permute-done | bytes 540704 | tf_op jit(solution)/shard_map/ppermute | solution.py:314
  6.1 0.1 shard_map.65
  6.2 2.9 %collective-permute-start.9 = (bf16[528,512]{1,0:T(8,128)(2,1)S(1)}, bf16[528,512]{1,0:T(8,128)(2,1)S(1)}, u32[]{:S(2)}, u32[]{:S(2)}) collective-permute-start(bf16[528,512]{1,0:T(8,128)(2,1)S(1)} %get-tuple-element.96), channel_id=1, source_target_pairs={{0,2},{1,3},{2,0},{3,1},{4,6},{5,7},{6,4},{7,5},{8,10},{9,11},{10,... | collective-permute-start | bytes 1622024 | tf_op jit(solution)/shard_map/ppermute | solution.py:320
  9.2 0.0 copy-done.1
  9.2 2.6 %shard_map.67 = (bf16[1536,1024]{1,0:T(8,128)(2,1)S(1)}, bf16[1024]{0:T(1024)(128)(2,1)S(1)}, bf16[1024,1024]{1,0:T(8,128)(2,1)S(1)}) custom-call(bf16[1536,1024]{1,0:T(8,128)(2,1)} %tokens.3, bf16[1024]{0:T(1024)(128)(2,1)S(1)} %copy-done.1, bf16[1024,2048]{1,0:T(8,128)(2,1)} %weight.3), custom_call_target="tpu_custom_call" | custom-call | flops 1 | bytes 1 | tf_op jit(solution)/shard_map/pallas_call | solution.py:330
  11.7 1.3 %shard_map.74 = (bf16[512,512]{1,0:T(8,128)(2,1)S(1)}, bf16[512,512]{1,0:T(8,128)(2,1)S(1)}) custom-call(bf16[1536,1024]{1,0:T(8,128)(2,1)S(1)} %get-tuple-element.68.tokens, bf16[1024]{0:T(1024)(128)(2,1)S(1)} %get-tuple-element.75.gain, bf16[1024,1024]{1,0:T(8,128)(2,1)S(1)} %get-tuple-element.76.weight), custom_call_target="tpu_custom_call" | custom-call | flops 1 | bytes 1 | tf_op jit(solution)/shard_map/pallas_call | solution.py:251
  13.1 0.1 collective-permute-start.8
  13.1 1.0 %shard_map.71 = (bf16[256,512]{1,0:T(8,128)(2,1)S(1)}, bf16[272,512]{1,0:T(8,128)(2,1)S(1)}, f32[8,128]{1,0:T(8,128)S(1)}) custom-call(bf16[1536,1024]{1,0:T(8,128)(2,1)S(1)} %get-tuple-element.68.tokens, bf16[1024]{0:T(1024)(128)(2,1)S(1)} %get-tuple-element.75.gain, bf16[1024,1024]{1,0:T(8,128)(2,1)S(1)} %get-tuple-element.70.weight), custom_call_target="tpu_custom_call" | custom-call | flops 1 | bytes 1 | tf_op jit(solution)/shard_map/pallas_call | solution.py:251
  14.1 0.6 %collective-permute-start.3 = (bf16[272,512]{1,0:T(8,128)(2,1)S(1)}, bf16[272,512]{1,0:T(8,128)(2,1)S(1)}, u32[]{:S(2)}, u32[]{:S(2)}) collective-permute-start(bf16[272,512]{1,0:T(8,128)(2,1)S(1)} %get-tuple-element.85), channel_id=1, source_target_pairs={{0,1},{1,0},{2,3},{3,2},{4,5},{5,4},{6,7},{7,6},{8,9},{9,8},{10,11... | collective-permute-start | bytes 835592 | tf_op jit(solution)/shard_map/ppermute | solution.py:314
  14.7 0.7 %shard_map.73 = (bf16[256,512]{1,0:T(8,128)(2,1)S(1)}, bf16[256,512]{1,0:T(8,128)(2,1)S(1)}) custom-call(bf16[1536,1024]{1,0:T(8,128)(2,1)S(1)} %get-tuple-element.68.tokens, bf16[1024]{0:T(1024)(128)(2,1)S(1)} %get-tuple-element.75.gain, bf16[1024,1024]{1,0:T(8,128)(2,1)S(1)} %get-tuple-element.76.weight), custom_call_target="tpu_custom_call" | custom-call | flops 1 | bytes 1 | tf_op jit(solution)/shard_map/pallas_call | solution.py:251
  15.4 1.9 %shard_map.68 = (bf16[768,512]{1,0:T(8,128)(2,1)S(1)}, bf16[768,512]{1,0:T(8,128)(2,1)S(1)}) custom-call(bf16[1536,1024]{1,0:T(8,128)(2,1)S(1)} %get-tuple-element.68.tokens, bf16[1024]{0:T(1024)(128)(2,1)S(1)} %get-tuple-element.75.gain, bf16[1024,1024]{1,0:T(8,128)(2,1)S(1)} %get-tuple-element.70.weight), custom_call_target="tpu_custom_call" | custom-call | flops 1 | bytes 1 | tf_op jit(solution)/shard_map/pallas_call | solution.py:251
  17.3 0.1 collective-permute-start.7
  17.4 0.5 %collective-permute-start.1 = (bf16[768,512]{1,0:T(8,128)(2,1)S(1)}, bf16[768,512]{1,0:T(8,128)(2,1)S(1)}, u32[]{:S(2)}, u32[]{:S(2)}) collective-permute-start(bf16[768,512]{1,0:T(8,128)(2,1)S(1)} %get-tuple-element.72), channel_id=1, source_target_pairs={{0,1},{1,0},{2,3},{3,2},{4,5},{5,4},{6,7},{7,6},{8,9},{9,8},{10,11... | collective-permute-start | bytes 2359304 | tf_op jit(solution)/shard_map/ppermute | solution.py:314
  17.9 0.0 collective-permute-done.3.received
  17.9 0.1 shard_map.72
  17.9 0.1 collective-permute-start.4
  18.0 0.0 collective-permute-done.8.refs_1_
  18.0 4.2 %collective-permute-done.9.refs_8_ = bf16[528,512]{1,0:T(8,128)(2,1)S(1)} collective-permute-done((bf16[528,512]{1,0:T(8,128)(2,1)S(1)}, bf16[528,512]{1,0:T(8,128)(2,1)S(1)}, u32[]{:S(2)}, u32[]{:S(2)}) %collective-permute-start.9) | collective-permute-done | bytes 540704 | tf_op jit(solution)/shard_map/ppermute | solution.py:320
  22.2 1.4 %shard_map.75.refs_9_ = bf16[1536,512]{1,0:T(8,128)(2,1)} custom-call(bf16[512,512]{1,0:T(8,128)(2,1)S(1)} %get-tuple-element.93.refs_0_, bf16[512,512]{1,0:T(8,128)(2,1)S(1)} %collective-permute-done.8.refs_1_, s32[8,128]{1,0:T(8,128)S(1)} %get-tuple-element.79.refs_2_, f32[24,128]{1,0:T(8,128)S(1)} %get-tuple-element.80.refs_3_, ...), custom_call_target="tpu_custom_call" | custom-call | flops 20000000000 | bytes 1 | tf_op jit(solution)/shard_map/pallas_call | solution.py:282
  23.6 0.0 collective-permute-done.1.received
  23.7 0.2 shard_map.69
  23.8 2.1 %collective-permute-start.6 = (bf16[512,512]{1,0:T(8,128)(2,1)S(1)}, bf16[512,512]{1,0:T(8,128)(2,1)S(1)}, u32[]{:S(2)}, u32[]{:S(2)}) collective-permute-start(bf16[512,512]{1,0:T(8,128)(2,1)S(1)} %get-tuple-element.90), channel_id=1, source_target_pairs={{0,2},{1,3},{2,0},{3,1},{4,6},{5,7},{6,4},{7,5},{8,10},{9,11},{10,... | collective-permute-start | bytes 1572872 | tf_op jit(solution)/shard_map/ppermute | solution.py:320
  26.0 1.9 %shard_map.70 = (bf16[768,512]{1,0:T(8,128)(2,1)S(1)}, bf16[768,512]{1,0:T(8,128)(2,1)S(1)}) custom-call(bf16[1536,1024]{1,0:T(8,128)(2,1)S(1)} %get-tuple-element.68.tokens, bf16[1024]{0:T(1024)(128)(2,1)S(1)} %get-tuple-element.75.gain, bf16[1024,1024]{1,0:T(8,128)(2,1)S(1)} %get-tuple-element.76.weight), custom_call_target="tpu_custom_call" | custom-call | flops 1 | bytes 1 | tf_op jit(solution)/shard_map/pallas_call | solution.py:251
  27.8 0.1 collective-permute-start.2
  27.9 0.0 collective-permute-done.7.refs_1_
  27.9 0.3 collective-permute-done.4.refs_8_
  28.2 1.1 %shard_map.76.refs_10_ = bf16[1536,512]{1,0:T(8,128)(2,1)} custom-call(bf16[256,512]{1,0:T(8,128)(2,1)S(1)} %get-tuple-element.91.refs_0_, bf16[256,512]{1,0:T(8,128)(2,1)S(1)} %collective-permute-done.7.refs_1_, s32[8,128]{1,0:T(8,128)S(1)} %get-tuple-element.79.refs_2_, f32[24,128]{1,0:T(8,128)S(1)} %get-tuple-element.80.refs_3_, ...), custom_call_target="tpu_custom_call", output_to_operand_aliasing={{}: (9, {})} | custom-call | flops 20000000000 | bytes 1 | tf_op jit(solution)/shard_map/pallas_call | solution.py:282
  29.3 2.1 %collective-permute-start.5 = (bf16[256,512]{1,0:T(8,128)(2,1)S(1)}, bf16[256,512]{1,0:T(8,128)(2,1)S(1)}, u32[]{:S(2)}, u32[]{:S(2)}) collective-permute-start(bf16[256,512]{1,0:T(8,128)(2,1)S(1)} %get-tuple-element.89), channel_id=1, source_target_pairs={{0,2},{1,3},{2,0},{3,1},{4,6},{5,7},{6,4},{7,5},{8,10},{9,11},{10,... | collective-permute-start | bytes 786440 | tf_op jit(solution)/shard_map/ppermute | solution.py:320
  31.4 8.0 %collective-permute-done.6.refs_9_ = bf16[512,512]{1,0:T(8,128)(2,1)S(1)} collective-permute-done((bf16[512,512]{1,0:T(8,128)(2,1)S(1)}, bf16[512,512]{1,0:T(8,128)(2,1)S(1)}, u32[]{:S(2)}, u32[]{:S(2)}) %collective-permute-start.6) | collective-permute-done | bytes 524320 | tf_op jit(solution)/shard_map/ppermute | solution.py:320
  39.4 0.0 collective-permute-done.2.refs_1_
  39.4 1.4 %shard_map.77.refs_10_ = bf16[1536,512]{1,0:T(8,128)(2,1)} custom-call(bf16[768,512]{1,0:T(8,128)(2,1)S(1)} %get-tuple-element.77.refs_0_, bf16[768,512]{1,0:T(8,128)(2,1)S(1)} %collective-permute-done.2.refs_1_, s32[8,128]{1,0:T(8,128)S(1)} %get-tuple-element.79.refs_2_, f32[24,128]{1,0:T(8,128)S(1)} %get-tuple-element.80.refs_3_, ...), custom_call_target="tpu_custom_call", output_to_operand_aliasing={{}: (10, {})} | custom-call | flops 20000000000 | bytes 1 | tf_op jit(solution)/shard_map/pallas_call | solution.py:282
  40.8 3.7 %collective-permute-done.5.refs_9_ = bf16[256,512]{1,0:T(8,128)(2,1)S(1)} collective-permute-done((bf16[256,512]{1,0:T(8,128)(2,1)S(1)}, bf16[256,512]{1,0:T(8,128)(2,1)S(1)}, u32[]{:S(2)}, u32[]{:S(2)}) %collective-permute-start.5) | collective-permute-done | bytes 262176 | tf_op jit(solution)/shard_map/ppermute | solution.py:320
  44.6 1.1 %shard_map.78 = bf16[1536,512]{1,0:T(8,128)(2,1)} custom-call(bf16[768,512]{1,0:T(8,128)(2,1)S(1)} %get-tuple-element.77.refs_0_, bf16[768,512]{1,0:T(8,128)(2,1)S(1)} %collective-permute-done.2.refs_1_, s32[8,128]{1,0:T(8,128)S(1)} %get-tuple-element.79.refs_2_, f32[24,128]{1,0:T(8,128)S(1)} %get-tuple-element.80.refs_3_, ...), custom_call_target="tpu_custom_call", output_to_operand_aliasing={{}: (10, {})} | custom-call | flops 20000000000 | bytes 1 | tf_op jit(solution)/shard_map/pallas_call | solution.py:282
Async XLA Ops:
  0.0 0.7 %copy-start = (bf16[1024]{0:T(1024)(128)(2,1)S(1)}, bf16[1024]{0:T(1024)(128)(2,1)}, u32[]{:S(2)}) copy-start(bf16[1024]{0:T(1024)(128)(2,1)} %gain.2) | copy-start | bytes 6148
  0.7 3.9 %copy-start.2 = (s32[4]{0:T(128)S(1)}, s32[4]{0:T(128)}, u32[]{:S(2)}) copy-start(s32[4]{0:T(128)} %live) | copy-start | bytes 52
  0.7 3.9 %copy-start.3 = (s32[4]{0:T(128)S(1)}, s32[4]{0:T(128)}, u32[]{:S(2)}) copy-start(s32[4]{0:T(128)} %span) | copy-start | bytes 52
  0.7 3.9 %copy-start.4 = (f32[1,128]{1,0:T(1,128)S(1)}, f32[1,128]{1,0:T(1,128)}, u32[]{:S(2)}) copy-start(f32[1,128]{1,0:T(1,128)} %constant.4.clone.frequencies) | copy-start | bytes 1540
  0.7 8.5 %copy-start.1 = (bf16[1024]{0:T(1024)(128)(2,1)S(1)}, bf16[1024]{0:T(1024)(128)(2,1)}, u32[]{:S(2)}) copy-start(bf16[1024]{0:T(1024)(128)(2,1)} %gain.2) | copy-start | bytes 6148
  4.0 2.1 %collective-permute-start = (bf16[528,512]{1,0:T(8,128)(2,1)S(1)}, bf16[528,512]{1,0:T(8,128)(2,1)S(1)}, u32[]{:S(2)}, u32[]{:S(2)}) collective-permute-start(bf16[528,512]{1,0:T(8,128)(2,1)S(1)} %get-tuple-element.55), channel_id=1, source_target_pairs={{0,1},{1,0},{2,3},{3,2},{4,5},{5,4},{6,7},{7,6},{8,9},{9,8},{10,11... | collective-permute-start | bytes 1622024 | tf_op jit(solution)/shard_map/ppermute | solution.py:314
  6.2 16.0 %collective-permute-start.9 = (bf16[528,512]{1,0:T(8,128)(2,1)S(1)}, bf16[528,512]{1,0:T(8,128)(2,1)S(1)}, u32[]{:S(2)}, u32[]{:S(2)}) collective-permute-start(bf16[528,512]{1,0:T(8,128)(2,1)S(1)} %get-tuple-element.96), channel_id=1, source_target_pairs={{0,2},{1,3},{2,0},{3,1},{4,6},{5,7},{6,4},{7,5},{8,10},{9,11},{10,... | collective-permute-start | bytes 1622024 | tf_op jit(solution)/shard_map/ppermute | solution.py:320
  13.1 5.0 %collective-permute-start.8 = (bf16[512,512]{1,0:T(8,128)(2,1)S(1)}, bf16[512,512]{1,0:T(8,128)(2,1)S(1)}, u32[]{:S(2)}, u32[]{:S(2)}) collective-permute-start(bf16[512,512]{1,0:T(8,128)(2,1)S(1)} %get-tuple-element.94), channel_id=1, source_target_pairs={{0,1},{1,0},{2,3},{3,2},{4,5},{5,4},{6,7},{7,6},{8,9},{9,8},{10,11... | collective-permute-start | bytes 1572872 | tf_op jit(solution)/shard_map/ppermute | solution.py:356
  14.1 3.7 %collective-permute-start.3 = (bf16[272,512]{1,0:T(8,128)(2,1)S(1)}, bf16[272,512]{1,0:T(8,128)(2,1)S(1)}, u32[]{:S(2)}, u32[]{:S(2)}) collective-permute-start(bf16[272,512]{1,0:T(8,128)(2,1)S(1)} %get-tuple-element.85), channel_id=1, source_target_pairs={{0,1},{1,0},{2,3},{3,2},{4,5},{5,4},{6,7},{7,6},{8,9},{9,8},{10,11... | collective-permute-start | bytes 835592 | tf_op jit(solution)/shard_map/ppermute | solution.py:314
  17.3 10.6 %collective-permute-start.7 = (bf16[256,512]{1,0:T(8,128)(2,1)S(1)}, bf16[256,512]{1,0:T(8,128)(2,1)S(1)}, u32[]{:S(2)}, u32[]{:S(2)}) collective-permute-start(bf16[256,512]{1,0:T(8,128)(2,1)S(1)} %get-tuple-element.92), channel_id=1, source_target_pairs={{0,1},{1,0},{2,3},{3,2},{4,5},{5,4},{6,7},{7,6},{8,9},{9,8},{10,11... | collective-permute-start | bytes 786440 | tf_op jit(solution)/shard_map/ppermute | solution.py:356
  17.4 6.3 %collective-permute-start.1 = (bf16[768,512]{1,0:T(8,128)(2,1)S(1)}, bf16[768,512]{1,0:T(8,128)(2,1)S(1)}, u32[]{:S(2)}, u32[]{:S(2)}) collective-permute-start(bf16[768,512]{1,0:T(8,128)(2,1)S(1)} %get-tuple-element.72), channel_id=1, source_target_pairs={{0,1},{1,0},{2,3},{3,2},{4,5},{5,4},{6,7},{7,6},{8,9},{9,8},{10,11... | collective-permute-start | bytes 2359304 | tf_op jit(solution)/shard_map/ppermute | solution.py:314
  17.9 10.3 %collective-permute-start.4 = (bf16[272,512]{1,0:T(8,128)(2,1)S(1)}, bf16[272,512]{1,0:T(8,128)(2,1)S(1)}, u32[]{:S(2)}, u32[]{:S(2)}) collective-permute-start(bf16[272,512]{1,0:T(8,128)(2,1)S(1)} %get-tuple-element.88), channel_id=1, source_target_pairs={{0,2},{1,3},{2,0},{3,1},{4,6},{5,7},{6,4},{7,5},{8,10},{9,11},{10,... | collective-permute-start | bytes 835592 | tf_op jit(solution)/shard_map/ppermute | solution.py:320
  23.8 15.6 %collective-permute-start.6 = (bf16[512,512]{1,0:T(8,128)(2,1)S(1)}, bf16[512,512]{1,0:T(8,128)(2,1)S(1)}, u32[]{:S(2)}, u32[]{:S(2)}) collective-permute-start(bf16[512,512]{1,0:T(8,128)(2,1)S(1)} %get-tuple-element.90), channel_id=1, source_target_pairs={{0,2},{1,3},{2,0},{3,1},{4,6},{5,7},{6,4},{7,5},{8,10},{9,11},{10,... | collective-permute-start | bytes 1572872 | tf_op jit(solution)/shard_map/ppermute | solution.py:320
  27.8 11.6 %collective-permute-start.2 = (bf16[768,512]{1,0:T(8,128)(2,1)S(1)}, bf16[768,512]{1,0:T(8,128)(2,1)S(1)}, u32[]{:S(2)}, u32[]{:S(2)}) collective-permute-start(bf16[768,512]{1,0:T(8,128)(2,1)S(1)} %get-tuple-element.78), channel_id=1, source_target_pairs={{0,1},{1,0},{2,3},{3,2},{4,5},{5,4},{6,7},{7,6},{8,9},{9,8},{10,11... | collective-permute-start | bytes 2359304 | tf_op jit(solution)/shard_map/ppermute | solution.py:356
  29.3 15.3 %collective-permute-start.5 = (bf16[256,512]{1,0:T(8,128)(2,1)S(1)}, bf16[256,512]{1,0:T(8,128)(2,1)S(1)}, u32[]{:S(2)}, u32[]{:S(2)}) collective-permute-start(bf16[256,512]{1,0:T(8,128)(2,1)S(1)} %get-tuple-element.89), channel_id=1, source_target_pairs={{0,2},{1,3},{2,0},{3,1},{4,6},{5,7},{6,4},{7,5},{8,10},{9,11},{10,... | collective-permute-start | bytes 786440 | tf_op jit(solution)/shard_map/ppermute | solution.py:320

commit v22 on v20

--- a/solution.py
+++ b/solution.py
@@ -18,7 +18,7 @@
 norm_eps = 1e-05
 
 TILE = 256
-CUTS = 4
+CUTS = 2
 CHUNKS = (2, 1, 3)
 
 PARAMS = pltpu.CompilerParams(vmem_limit_bytes=16 * 1024 * 1024)

time: 45.6 us -> 45.7 us (level)
  no operation moved by 1% of the time
where the time goes in v22:
time: 45.7 us; the launch traced here: 45.6 us
  Pallas kernels  18.7 us (41%)
  waiting for transfers between devices  17 us (37%)
  starting transfers between devices  9.06 us (20%)
  local copies, waits for them, and re-layouts  0.7 us (2%)
    ppermute x4, waiting for transfers between devices, cross(): lax.ppermute(part, 'tensor', shift(step))  16.2 us
    pallas_call x6, Pallas kernels, product(): pl.pallas_call(functools.partial(product_kernel, step, chip_count, first,...  9.96 us
    ppermute x4, starting transfers between devices, cross(): lax.ppermute(part, 'tensor', shift(step))  7.27 us
    pallas_call x4, Pallas kernels, finish(): pl.pallas_call(functools.partial(finish_kernel, first, at, line_at, count...  5.01 us
    pallas_call x1, Pallas kernels, shards(): pl.pallas_call(bring_kernel, in_specs=[pl.BlockSpec(memory_space=pltpu.HB...  2.57 us
    ppermute x3, starting transfers between devices, add_halves(): lax.ppermute(send, 'tensor', swap)  1.57 us
  transfers between devices with their start and end apart: 10, of which 5 were waited for; matrix products, arithmetic and copies ran while one was open for 0% of the time, Pallas kernels for 31%

profile of v22, /device:TPU:0, one launch (start us, length us, event | category | flops | bytes accessed | tf_op | source)
XLA Modules:
  0.0 45.6 jit_solution(11804350942892627955)
XLA Ops:
  0.0 0.0 copy-start
  0.0 0.7 %copy-done = bf16[1024]{0:T(1024)(128)(2,1)S(1)} copy-done((bf16[1024]{0:T(1024)(128)(2,1)S(1)}, bf16[1024]{0:T(1024)(128)(2,1)}, u32[]{:S(2)}) %copy-start) | copy-done | bytes 2072
  0.7 0.0 copy-start.2
  0.7 0.0 copy-start.3
  0.7 0.0 copy-start.4
  0.7 0.0 copy-start.1
  0.7 3.2 %shard_map.64 = (bf16[512,512]{1,0:T(8,128)(2,1)S(1)}, bf16[528,512]{1,0:T(8,128)(2,1)S(1)}, f32[4,128]{1,0:T(4,128)S(1)}, bf16[1024,1024]{1,0:T(8,128)(2,1)S(1)}) custom-call(bf16[1536,1024]{1,0:T(8,128)(2,1)} %tokens.3, bf16[1024]{0:T(1024)(128)(2,1)S(1)} %copy-done, bf16[1024,2048]{1,0:T(8,128)(2,1)} %weight.3), custom_call_target="tpu_custom_call" | custom-call | flops 999999995904 | bytes 1 | tf_op jit(solution)/shard_map/pallas_call | solution.py:251
  3.9 0.5 %collective-permute-start = (bf16[528,512]{1,0:T(8,128)(2,1)S(1)}, bf16[528,512]{1,0:T(8,128)(2,1)S(1)}, u32[]{:S(2)}, u32[]{:S(2)}) collective-permute-start(bf16[528,512]{1,0:T(8,128)(2,1)S(1)} %get-tuple-element.55), channel_id=1, source_target_pairs={{0,1},{1,0},{2,3},{3,2},{4,5},{5,4},{6,7},{7,6},{8,9},{9,8},{10,11... | collective-permute-start | bytes 1622024 | tf_op jit(solution)/shard_map/ppermute | solution.py:314
  4.5 0.0 copy-done.2
  4.5 0.0 copy-done.3
  4.5 0.0 copy-done.4
  4.5 0.7 %shard_map.66 = (s32[8,128]{1,0:T(8,128)S(1)}, f32[24,128]{1,0:T(8,128)S(1)}, f32[24,128]{1,0:T(8,128)S(1)}, f32[64,128]{1,0:T(8,128)S(1)}, f32[64,128]{1,0:T(8,128)S(1)}) custom-call(s32[4]{0:T(128)S(1)} %copy-done.2, s32[4]{0:T(128)S(1)} %copy-done.3, f32[1,128]{1,0:T(1,128)S(1)} %copy-done.4), custom_call_target="tpu_custom_call" | custom-call | flops 1 | bytes 1 | tf_op jit(solution)/shard_map/pallas_call | solution.py:265
  5.2 0.8 %collective-permute-done.received = bf16[528,512]{1,0:T(8,128)(2,1)S(1)} collective-permute-done((bf16[528,512]{1,0:T(8,128)(2,1)S(1)}, bf16[528,512]{1,0:T(8,128)(2,1)S(1)}, u32[]{:S(2)}, u32[]{:S(2)}) %collective-permute-start) | collective-permute-done | bytes 540704 | tf_op jit(solution)/shard_map/ppermute | solution.py:314
  6.0 0.1 shard_map.65
  6.2 2.9 %collective-permute-start.9 = (bf16[528,512]{1,0:T(8,128)(2,1)S(1)}, bf16[528,512]{1,0:T(8,128)(2,1)S(1)}, u32[]{:S(2)}, u32[]{:S(2)}) collective-permute-start(bf16[528,512]{1,0:T(8,128)(2,1)S(1)} %get-tuple-element.96), channel_id=1, source_target_pairs={{0,2},{1,3},{2,0},{3,1},{4,6},{5,7},{6,4},{7,5},{8,10},{9,11},{10,... | collective-permute-start | bytes 1622024 | tf_op jit(solution)/shard_map/ppermute | solution.py:320
  9.1 0.0 copy-done.1
  9.1 2.6 %shard_map.67 = (bf16[1536,1024]{1,0:T(8,128)(2,1)S(1)}, bf16[1024]{0:T(1024)(128)(2,1)S(1)}, bf16[1024,1024]{1,0:T(8,128)(2,1)S(1)}) custom-call(bf16[1536,1024]{1,0:T(8,128)(2,1)} %tokens.3, bf16[1024]{0:T(1024)(128)(2,1)S(1)} %copy-done.1, bf16[1024,2048]{1,0:T(8,128)(2,1)} %weight.3), custom_call_target="tpu_custom_call" | custom-call | flops 1 | bytes 1 | tf_op jit(solution)/shard_map/pallas_call | solution.py:330
  11.7 1.3 %shard_map.74 = (bf16[512,512]{1,0:T(8,128)(2,1)S(1)}, bf16[512,512]{1,0:T(8,128)(2,1)S(1)}) custom-call(bf16[1536,1024]{1,0:T(8,128)(2,1)S(1)} %get-tuple-element.68.tokens, bf16[1024]{0:T(1024)(128)(2,1)S(1)} %get-tuple-element.75.gain, bf16[1024,1024]{1,0:T(8,128)(2,1)S(1)} %get-tuple-element.76.weight), custom_call_target="tpu_custom_call" | custom-call | flops 1 | bytes 1 | tf_op jit(solution)/shard_map/pallas_call | solution.py:251
  13.0 0.1 collective-permute-start.8
  13.0 1.0 %shard_map.71 = (bf16[256,512]{1,0:T(8,128)(2,1)S(1)}, bf16[272,512]{1,0:T(8,128)(2,1)S(1)}, f32[8,128]{1,0:T(8,128)S(1)}) custom-call(bf16[1536,1024]{1,0:T(8,128)(2,1)S(1)} %get-tuple-element.68.tokens, bf16[1024]{0:T(1024)(128)(2,1)S(1)} %get-tuple-element.75.gain, bf16[1024,1024]{1,0:T(8,128)(2,1)S(1)} %get-tuple-element.70.weight), custom_call_target="tpu_custom_call" | custom-call | flops 1 | bytes 1 | tf_op jit(solution)/shard_map/pallas_call | solution.py:251
  14.0 0.6 %collective-permute-start.3 = (bf16[272,512]{1,0:T(8,128)(2,1)S(1)}, bf16[272,512]{1,0:T(8,128)(2,1)S(1)}, u32[]{:S(2)}, u32[]{:S(2)}) collective-permute-start(bf16[272,512]{1,0:T(8,128)(2,1)S(1)} %get-tuple-element.85), channel_id=1, source_target_pairs={{0,1},{1,0},{2,3},{3,2},{4,5},{5,4},{6,7},{7,6},{8,9},{9,8},{10,11... | collective-permute-start | bytes 835592 | tf_op jit(solution)/shard_map/ppermute | solution.py:314
  14.6 0.7 %shard_map.73 = (bf16[256,512]{1,0:T(8,128)(2,1)S(1)}, bf16[256,512]{1,0:T(8,128)(2,1)S(1)}) custom-call(bf16[1536,1024]{1,0:T(8,128)(2,1)S(1)} %get-tuple-element.68.tokens, bf16[1024]{0:T(1024)(128)(2,1)S(1)} %get-tuple-element.75.gain, bf16[1024,1024]{1,0:T(8,128)(2,1)S(1)} %get-tuple-element.76.weight), custom_call_target="tpu_custom_call" | custom-call | flops 1 | bytes 1 | tf_op jit(solution)/shard_map/pallas_call | solution.py:251
  15.3 1.9 %shard_map.68 = (bf16[768,512]{1,0:T(8,128)(2,1)S(1)}, bf16[768,512]{1,0:T(8,128)(2,1)S(1)}) custom-call(bf16[1536,1024]{1,0:T(8,128)(2,1)S(1)} %get-tuple-element.68.tokens, bf16[1024]{0:T(1024)(128)(2,1)S(1)} %get-tuple-element.75.gain, bf16[1024,1024]{1,0:T(8,128)(2,1)S(1)} %get-tuple-element.70.weight), custom_call_target="tpu_custom_call" | custom-call | flops 1 | bytes 1 | tf_op jit(solution)/shard_map/pallas_call | solution.py:251
  17.2 0.1 collective-permute-start.7
  17.3 0.5 %collective-permute-start.1 = (bf16[768,512]{1,0:T(8,128)(2,1)S(1)}, bf16[768,512]{1,0:T(8,128)(2,1)S(1)}, u32[]{:S(2)}, u32[]{:S(2)}) collective-permute-start(bf16[768,512]{1,0:T(8,128)(2,1)S(1)} %get-tuple-element.72), channel_id=1, source_target_pairs={{0,1},{1,0},{2,3},{3,2},{4,5},{5,4},{6,7},{7,6},{8,9},{9,8},{10,11... | collective-permute-start | bytes 2359304 | tf_op jit(solution)/shard_map/ppermute | solution.py:314
  17.8 0.0 collective-permute-done.3.received
  17.8 0.1 shard_map.72
  17.9 0.1 collective-permute-start.4
  18.0 0.0 collective-permute-done.8.refs_1_
  18.0 4.2 %collective-permute-done.9.refs_8_ = bf16[528,512]{1,0:T(8,128)(2,1)S(1)} collective-permute-done((bf16[528,512]{1,0:T(8,128)(2,1)S(1)}, bf16[528,512]{1,0:T(8,128)(2,1)S(1)}, u32[]{:S(2)}, u32[]{:S(2)}) %collective-permute-start.9) | collective-permute-done | bytes 540704 | tf_op jit(solution)/shard_map/ppermute | solution.py:320
  22.1 1.4 %shard_map.75.refs_9_ = bf16[1536,512]{1,0:T(8,128)(2,1)} custom-call(bf16[512,512]{1,0:T(8,128)(2,1)S(1)} %get-tuple-element.93.refs_0_, bf16[512,512]{1,0:T(8,128)(2,1)S(1)} %collective-permute-done.8.refs_1_, s32[8,128]{1,0:T(8,128)S(1)} %get-tuple-element.79.refs_2_, f32[24,128]{1,0:T(8,128)S(1)} %get-tuple-element.80.refs_3_, ...), custom_call_target="tpu_custom_call" | custom-call | flops 20000000000 | bytes 1 | tf_op jit(solution)/shard_map/pallas_call | solution.py:282
  23.6 0.0 collective-permute-done.1.received
  23.6 0.2 shard_map.69
  23.8 2.1 %collective-permute-start.6 = (bf16[512,512]{1,0:T(8,128)(2,1)S(1)}, bf16[512,512]{1,0:T(8,128)(2,1)S(1)}, u32[]{:S(2)}, u32[]{:S(2)}) collective-permute-start(bf16[512,512]{1,0:T(8,128)(2,1)S(1)} %get-tuple-element.90), channel_id=1, source_target_pairs={{0,2},{1,3},{2,0},{3,1},{4,6},{5,7},{6,4},{7,5},{8,10},{9,11},{10,... | collective-permute-start | bytes 1572872 | tf_op jit(solution)/shard_map/ppermute | solution.py:320
  25.9 1.9 %shard_map.70 = (bf16[768,512]{1,0:T(8,128)(2,1)S(1)}, bf16[768,512]{1,0:T(8,128)(2,1)S(1)}) custom-call(bf16[1536,1024]{1,0:T(8,128)(2,1)S(1)} %get-tuple-element.68.tokens, bf16[1024]{0:T(1024)(128)(2,1)S(1)} %get-tuple-element.75.gain, bf16[1024,1024]{1,0:T(8,128)(2,1)S(1)} %get-tuple-element.76.weight), custom_call_target="tpu_custom_call" | custom-call | flops 1 | bytes 1 | tf_op jit(solution)/shard_map/pallas_call | solution.py:251
  27.8 0.1 collective-permute-start.2
  27.8 0.0 collective-permute-done.7.refs_1_
  27.8 0.3 collective-permute-done.4.refs_8_
  28.1 1.1 %shard_map.76.refs_10_ = bf16[1536,512]{1,0:T(8,128)(2,1)} custom-call(bf16[256,512]{1,0:T(8,128)(2,1)S(1)} %get-tuple-element.91.refs_0_, bf16[256,512]{1,0:T(8,128)(2,1)S(1)} %collective-permute-done.7.refs_1_, s32[8,128]{1,0:T(8,128)S(1)} %get-tuple-element.79.refs_2_, f32[24,128]{1,0:T(8,128)S(1)} %get-tuple-element.80.refs_3_, ...), custom_call_target="tpu_custom_call", output_to_operand_aliasing={{}: (9, {})} | custom-call | flops 20000000000 | bytes 1 | tf_op jit(solution)/shard_map/pallas_call | solution.py:282
  29.2 2.1 %collective-permute-start.5 = (bf16[256,512]{1,0:T(8,128)(2,1)S(1)}, bf16[256,512]{1,0:T(8,128)(2,1)S(1)}, u32[]{:S(2)}, u32[]{:S(2)}) collective-permute-start(bf16[256,512]{1,0:T(8,128)(2,1)S(1)} %get-tuple-element.89), channel_id=1, source_target_pairs={{0,2},{1,3},{2,0},{3,1},{4,6},{5,7},{6,4},{7,5},{8,10},{9,11},{10,... | collective-permute-start | bytes 786440 | tf_op jit(solution)/shard_map/ppermute | solution.py:320
  31.4 8.0 %collective-permute-done.6.refs_9_ = bf16[512,512]{1,0:T(8,128)(2,1)S(1)} collective-permute-done((bf16[512,512]{1,0:T(8,128)(2,1)S(1)}, bf16[512,512]{1,0:T(8,128)(2,1)S(1)}, u32[]{:S(2)}, u32[]{:S(2)}) %collective-permute-start.6) | collective-permute-done | bytes 524320 | tf_op jit(solution)/shard_map/ppermute | solution.py:320
  39.3 0.0 collective-permute-done.2.refs_1_
  39.4 1.4 %shard_map.77.refs_10_ = bf16[1536,512]{1,0:T(8,128)(2,1)} custom-call(bf16[768,512]{1,0:T(8,128)(2,1)S(1)} %get-tuple-element.77.refs_0_, bf16[768,512]{1,0:T(8,128)(2,1)S(1)} %collective-permute-done.2.refs_1_, s32[8,128]{1,0:T(8,128)S(1)} %get-tuple-element.79.refs_2_, f32[24,128]{1,0:T(8,128)S(1)} %get-tuple-element.80.refs_3_, ...), custom_call_target="tpu_custom_call", output_to_operand_aliasing={{}: (10, {})} | custom-call | flops 20000000000 | bytes 1 | tf_op jit(solution)/shard_map/pallas_call | solution.py:282
  40.8 3.7 %collective-permute-done.5.refs_9_ = bf16[256,512]{1,0:T(8,128)(2,1)S(1)} collective-permute-done((bf16[256,512]{1,0:T(8,128)(2,1)S(1)}, bf16[256,512]{1,0:T(8,128)(2,1)S(1)}, u32[]{:S(2)}, u32[]{:S(2)}) %collective-permute-start.5) | collective-permute-done | bytes 262176 | tf_op jit(solution)/shard_map/ppermute | solution.py:320
  44.5 1.1 %shard_map.78 = bf16[1536,512]{1,0:T(8,128)(2,1)} custom-call(bf16[768,512]{1,0:T(8,128)(2,1)S(1)} %get-tuple-element.77.refs_0_, bf16[768,512]{1,0:T(8,128)(2,1)S(1)} %collective-permute-done.2.refs_1_, s32[8,128]{1,0:T(8,128)S(1)} %get-tuple-element.79.refs_2_, f32[24,128]{1,0:T(8,128)S(1)} %get-tuple-element.80.refs_3_, ...), custom_call_target="tpu_custom_call", output_to_operand_aliasing={{}: (10, {})} | custom-call | flops 20000000000 | bytes 1 | tf_op jit(solution)/shard_map/pallas_call | solution.py:282
Async XLA Ops:
  0.0 0.7 %copy-start = (bf16[1024]{0:T(1024)(128)(2,1)S(1)}, bf16[1024]{0:T(1024)(128)(2,1)}, u32[]{:S(2)}) copy-start(bf16[1024]{0:T(1024)(128)(2,1)} %gain.2) | copy-start | bytes 6148
  0.7 3.8 %copy-start.2 = (s32[4]{0:T(128)S(1)}, s32[4]{0:T(128)}, u32[]{:S(2)}) copy-start(s32[4]{0:T(128)} %live) | copy-start | bytes 52
  0.7 3.8 %copy-start.3 = (s32[4]{0:T(128)S(1)}, s32[4]{0:T(128)}, u32[]{:S(2)}) copy-start(s32[4]{0:T(128)} %span) | copy-start | bytes 52
  0.7 3.8 %copy-start.4 = (f32[1,128]{1,0:T(1,128)S(1)}, f32[1,128]{1,0:T(1,128)}, u32[]{:S(2)}) copy-start(f32[1,128]{1,0:T(1,128)} %constant.4.clone.frequencies) | copy-start | bytes 1540
  0.7 8.4 %copy-start.1 = (bf16[1024]{0:T(1024)(128)(2,1)S(1)}, bf16[1024]{0:T(1024)(128)(2,1)}, u32[]{:S(2)}) copy-start(bf16[1024]{0:T(1024)(128)(2,1)} %gain.2) | copy-start | bytes 6148
  3.9 2.1 %collective-permute-start = (bf16[528,512]{1,0:T(8,128)(2,1)S(1)}, bf16[528,512]{1,0:T(8,128)(2,1)S(1)}, u32[]{:S(2)}, u32[]{:S(2)}) collective-permute-start(bf16[528,512]{1,0:T(8,128)(2,1)S(1)} %get-tuple-element.55), channel_id=1, source_target_pairs={{0,1},{1,0},{2,3},{3,2},{4,5},{5,4},{6,7},{7,6},{8,9},{9,8},{10,11... | collective-permute-start | bytes 1622024 | tf_op jit(solution)/shard_map/ppermute | solution.py:314
  6.2 16.0 %collective-permute-start.9 = (bf16[528,512]{1,0:T(8,128)(2,1)S(1)}, bf16[528,512]{1,0:T(8,128)(2,1)S(1)}, u32[]{:S(2)}, u32[]{:S(2)}) collective-permute-start(bf16[528,512]{1,0:T(8,128)(2,1)S(1)} %get-tuple-element.96), channel_id=1, source_target_pairs={{0,2},{1,3},{2,0},{3,1},{4,6},{5,7},{6,4},{7,5},{8,10},{9,11},{10,... | collective-permute-start | bytes 1622024 | tf_op jit(solution)/shard_map/ppermute | solution.py:320
  13.0 5.0 %collective-permute-start.8 = (bf16[512,512]{1,0:T(8,128)(2,1)S(1)}, bf16[512,512]{1,0:T(8,128)(2,1)S(1)}, u32[]{:S(2)}, u32[]{:S(2)}) collective-permute-start(bf16[512,512]{1,0:T(8,128)(2,1)S(1)} %get-tuple-element.94), channel_id=1, source_target_pairs={{0,1},{1,0},{2,3},{3,2},{4,5},{5,4},{6,7},{7,6},{8,9},{9,8},{10,11... | collective-permute-start | bytes 1572872 | tf_op jit(solution)/shard_map/ppermute | solution.py:356
  14.0 3.7 %collective-permute-start.3 = (bf16[272,512]{1,0:T(8,128)(2,1)S(1)}, bf16[272,512]{1,0:T(8,128)(2,1)S(1)}, u32[]{:S(2)}, u32[]{:S(2)}) collective-permute-start(bf16[272,512]{1,0:T(8,128)(2,1)S(1)} %get-tuple-element.85), channel_id=1, source_target_pairs={{0,1},{1,0},{2,3},{3,2},{4,5},{5,4},{6,7},{7,6},{8,9},{9,8},{10,11... | collective-permute-start | bytes 835592 | tf_op jit(solution)/shard_map/ppermute | solution.py:314
  17.2 10.6 %collective-permute-start.7 = (bf16[256,512]{1,0:T(8,128)(2,1)S(1)}, bf16[256,512]{1,0:T(8,128)(2,1)S(1)}, u32[]{:S(2)}, u32[]{:S(2)}) collective-permute-start(bf16[256,512]{1,0:T(8,128)(2,1)S(1)} %get-tuple-element.92), channel_id=1, source_target_pairs={{0,1},{1,0},{2,3},{3,2},{4,5},{5,4},{6,7},{7,6},{8,9},{9,8},{10,11... | collective-permute-start | bytes 786440 | tf_op jit(solution)/shard_map/ppermute | solution.py:356
  17.3 6.3 %collective-permute-start.1 = (bf16[768,512]{1,0:T(8,128)(2,1)S(1)}, bf16[768,512]{1,0:T(8,128)(2,1)S(1)}, u32[]{:S(2)}, u32[]{:S(2)}) collective-permute-start(bf16[768,512]{1,0:T(8,128)(2,1)S(1)} %get-tuple-element.72), channel_id=1, source_target_pairs={{0,1},{1,0},{2,3},{3,2},{4,5},{5,4},{6,7},{7,6},{8,9},{9,8},{10,11... | collective-permute-start | bytes 2359304 | tf_op jit(solution)/shard_map/ppermute | solution.py:314
  17.9 10.3 %collective-permute-start.4 = (bf16[272,512]{1,0:T(8,128)(2,1)S(1)}, bf16[272,512]{1,0:T(8,128)(2,1)S(1)}, u32[]{:S(2)}, u32[]{:S(2)}) collective-permute-start(bf16[272,512]{1,0:T(8,128)(2,1)S(1)} %get-tuple-element.88), channel_id=1, source_target_pairs={{0,2},{1,3},{2,0},{3,1},{4,6},{5,7},{6,4},{7,5},{8,10},{9,11},{10,... | collective-permute-start | bytes 835592 | tf_op jit(solution)/shard_map/ppermute | solution.py:320
  23.8 15.6 %collective-permute-start.6 = (bf16[512,512]{1,0:T(8,128)(2,1)S(1)}, bf16[512,512]{1,0:T(8,128)(2,1)S(1)}, u32[]{:S(2)}, u32[]{:S(2)}) collective-permute-start(bf16[512,512]{1,0:T(8,128)(2,1)S(1)} %get-tuple-element.90), channel_id=1, source_target_pairs={{0,2},{1,3},{2,0},{3,1},{4,6},{5,7},{6,4},{7,5},{8,10},{9,11},{10,... | collective-permute-start | bytes 1572872 | tf_op jit(solution)/shard_map/ppermute | solution.py:320
  27.8 11.6 %collective-permute-start.2 = (bf16[768,512]{1,0:T(8,128)(2,1)S(1)}, bf16[768,512]{1,0:T(8,128)(2,1)S(1)}, u32[]{:S(2)}, u32[]{:S(2)}) collective-permute-start(bf16[768,512]{1,0:T(8,128)(2,1)S(1)} %get-tuple-element.78), channel_id=1, source_target_pairs={{0,1},{1,0},{2,3},{3,2},{4,5},{5,4},{6,7},{7,6},{8,9},{9,8},{10,11... | collective-permute-start | bytes 2359304 | tf_op jit(solution)/shard_map/ppermute | solution.py:356
  29.2 15.3 %collective-permute-start.5 = (bf16[256,512]{1,0:T(8,128)(2,1)S(1)}, bf16[256,512]{1,0:T(8,128)(2,1)S(1)}, u32[]{:S(2)}, u32[]{:S(2)}) collective-permute-start(bf16[256,512]{1,0:T(8,128)(2,1)S(1)} %get-tuple-element.89), channel_id=1, source_target_pairs={{0,2},{1,3},{2,0},{3,1},{4,6},{5,7},{6,4},{7,5},{8,10},{9,11},{10,... | collective-permute-start | bytes 786440 | tf_op jit(solution)/shard_map/ppermute | solution.py:320

commit v23 on v22

--- a/solution.py
+++ b/solution.py
@@ -18,7 +18,7 @@
 norm_eps = 1e-05
 
 TILE = 256
-CUTS = 2
+CUTS = 8
 CHUNKS = (2, 1, 3)
 
 PARAMS = pltpu.CompilerParams(vmem_limit_bytes=16 * 1024 * 1024)

time: 45.7 us -> 46.4 us (1.015)
  Pallas kernels: 18.7 us -> 19.3 us
    pallas_call x6, Pallas kernels: 9.96 us -> 10.6 us  [product(): pl.pallas_call(functools.partial(product_kernel, step, chip_count, first,...]
where the time goes in v23:
time: 46.4 us; the launch traced here: 46.2 us
  Pallas kernels  19.3 us (42%)
  waiting for transfers between devices  17 us (37%)
  starting transfers between devices  9.06 us (20%)
  local copies, waits for them, and re-layouts  0.7 us (2%)
    ppermute x4, waiting for transfers between devices, cross(): lax.ppermute(part, 'tensor', shift(step))  16.2 us
    pallas_call x6, Pallas kernels, product(): pl.pallas_call(functools.partial(product_kernel, step, chip_count, first,...  10.6 us
    ppermute x4, starting transfers between devices, cross(): lax.ppermute(part, 'tensor', shift(step))  7.27 us
    pallas_call x4, Pallas kernels, finish(): pl.pallas_call(functools.partial(finish_kernel, first, at, line_at, count...  5.01 us
    pallas_call x1, Pallas kernels, shards(): pl.pallas_call(bring_kernel, in_specs=[pl.BlockSpec(memory_space=pltpu.HB...  2.57 us
    ppermute x3, starting transfers between devices, add_halves(): lax.ppermute(send, 'tensor', swap)  1.57 us
  transfers between devices with their start and end apart: 10, of which 5 were waited for; matrix products, arithmetic and copies ran while one was open for 0% of the time, Pallas kernels for 31%

profile of v23, /device:TPU:0, one launch (start us, length us, event | category | flops | bytes accessed | tf_op | source)
XLA Modules:
  0.0 46.2 jit_solution(10830916322202886826)
XLA Ops:
  0.0 0.0 copy-start
  0.0 0.7 %copy-done = bf16[1024]{0:T(1024)(128)(2,1)S(1)} copy-done((bf16[1024]{0:T(1024)(128)(2,1)S(1)}, bf16[1024]{0:T(1024)(128)(2,1)}, u32[]{:S(2)}) %copy-start) | copy-done | bytes 2072
  0.7 0.0 copy-start.2
  0.7 0.0 copy-start.3
  0.7 0.0 copy-start.4
  0.7 0.0 copy-start.1
  0.7 3.9 %shard_map.64 = (bf16[512,512]{1,0:T(8,128)(2,1)S(1)}, bf16[528,512]{1,0:T(8,128)(2,1)S(1)}, f32[4,128]{1,0:T(4,128)S(1)}, bf16[1024,1024]{1,0:T(8,128)(2,1)S(1)}) custom-call(bf16[1536,1024]{1,0:T(8,128)(2,1)} %tokens.3, bf16[1024]{0:T(1024)(128)(2,1)S(1)} %copy-done, bf16[1024,2048]{1,0:T(8,128)(2,1)} %weight.3), custom_call_target="tpu_custom_call" | custom-call | flops 999999995904 | bytes 1 | tf_op jit(solution)/shard_map/pallas_call | solution.py:251
  4.6 0.5 %collective-permute-start = (bf16[528,512]{1,0:T(8,128)(2,1)S(1)}, bf16[528,512]{1,0:T(8,128)(2,1)S(1)}, u32[]{:S(2)}, u32[]{:S(2)}) collective-permute-start(bf16[528,512]{1,0:T(8,128)(2,1)S(1)} %get-tuple-element.55), channel_id=1, source_target_pairs={{0,1},{1,0},{2,3},{3,2},{4,5},{5,4},{6,7},{7,6},{8,9},{9,8},{10,11... | collective-permute-start | bytes 1622024 | tf_op jit(solution)/shard_map/ppermute | solution.py:314
  5.1 0.0 copy-done.2
  5.1 0.0 copy-done.3
  5.1 0.0 copy-done.4
  5.1 0.7 %shard_map.66 = (s32[8,128]{1,0:T(8,128)S(1)}, f32[24,128]{1,0:T(8,128)S(1)}, f32[24,128]{1,0:T(8,128)S(1)}, f32[64,128]{1,0:T(8,128)S(1)}, f32[64,128]{1,0:T(8,128)S(1)}) custom-call(s32[4]{0:T(128)S(1)} %copy-done.2, s32[4]{0:T(128)S(1)} %copy-done.3, f32[1,128]{1,0:T(1,128)S(1)} %copy-done.4), custom_call_target="tpu_custom_call" | custom-call | flops 1 | bytes 1 | tf_op jit(solution)/shard_map/pallas_call | solution.py:265
  5.8 0.8 %collective-permute-done.received = bf16[528,512]{1,0:T(8,128)(2,1)S(1)} collective-permute-done((bf16[528,512]{1,0:T(8,128)(2,1)S(1)}, bf16[528,512]{1,0:T(8,128)(2,1)S(1)}, u32[]{:S(2)}, u32[]{:S(2)}) %collective-permute-start) | collective-permute-done | bytes 540704 | tf_op jit(solution)/shard_map/ppermute | solution.py:314
  6.7 0.1 shard_map.65
  6.8 2.9 %collective-permute-start.9 = (bf16[528,512]{1,0:T(8,128)(2,1)S(1)}, bf16[528,512]{1,0:T(8,128)(2,1)S(1)}, u32[]{:S(2)}, u32[]{:S(2)}) collective-permute-start(bf16[528,512]{1,0:T(8,128)(2,1)S(1)} %get-tuple-element.96), channel_id=1, source_target_pairs={{0,2},{1,3},{2,0},{3,1},{4,6},{5,7},{6,4},{7,5},{8,10},{9,11},{10,... | collective-permute-start | bytes 1622024 | tf_op jit(solution)/shard_map/ppermute | solution.py:320
  9.7 0.0 copy-done.1
  9.7 2.6 %shard_map.67 = (bf16[1536,1024]{1,0:T(8,128)(2,1)S(1)}, bf16[1024]{0:T(1024)(128)(2,1)S(1)}, bf16[1024,1024]{1,0:T(8,128)(2,1)S(1)}) custom-call(bf16[1536,1024]{1,0:T(8,128)(2,1)} %tokens.3, bf16[1024]{0:T(1024)(128)(2,1)S(1)} %copy-done.1, bf16[1024,2048]{1,0:T(8,128)(2,1)} %weight.3), custom_call_target="tpu_custom_call" | custom-call | flops 1 | bytes 1 | tf_op jit(solution)/shard_map/pallas_call | solution.py:330
  12.3 1.3 %shard_map.74 = (bf16[512,512]{1,0:T(8,128)(2,1)S(1)}, bf16[512,512]{1,0:T(8,128)(2,1)S(1)}) custom-call(bf16[1536,1024]{1,0:T(8,128)(2,1)S(1)} %get-tuple-element.68.tokens, bf16[1024]{0:T(1024)(128)(2,1)S(1)} %get-tuple-element.75.gain, bf16[1024,1024]{1,0:T(8,128)(2,1)S(1)} %get-tuple-element.76.weight), custom_call_target="tpu_custom_call" | custom-call | flops 1 | bytes 1 | tf_op jit(solution)/shard_map/pallas_call | solution.py:251
  13.6 0.1 collective-permute-start.8
  13.7 1.0 %shard_map.71 = (bf16[256,512]{1,0:T(8,128)(2,1)S(1)}, bf16[272,512]{1,0:T(8,128)(2,1)S(1)}, f32[8,128]{1,0:T(8,128)S(1)}) custom-call(bf16[1536,1024]{1,0:T(8,128)(2,1)S(1)} %get-tuple-element.68.tokens, bf16[1024]{0:T(1024)(128)(2,1)S(1)} %get-tuple-element.75.gain, bf16[1024,1024]{1,0:T(8,128)(2,1)S(1)} %get-tuple-element.70.weight), custom_call_target="tpu_custom_call" | custom-call | flops 1 | bytes 1 | tf_op jit(solution)/shard_map/pallas_call | solution.py:251
  14.7 0.6 %collective-permute-start.3 = (bf16[272,512]{1,0:T(8,128)(2,1)S(1)}, bf16[272,512]{1,0:T(8,128)(2,1)S(1)}, u32[]{:S(2)}, u32[]{:S(2)}) collective-permute-start(bf16[272,512]{1,0:T(8,128)(2,1)S(1)} %get-tuple-element.85), channel_id=1, source_target_pairs={{0,1},{1,0},{2,3},{3,2},{4,5},{5,4},{6,7},{7,6},{8,9},{9,8},{10,11... | collective-permute-start | bytes 835592 | tf_op jit(solution)/shard_map/ppermute | solution.py:314
  15.3 0.7 %shard_map.73 = (bf16[256,512]{1,0:T(8,128)(2,1)S(1)}, bf16[256,512]{1,0:T(8,128)(2,1)S(1)}) custom-call(bf16[1536,1024]{1,0:T(8,128)(2,1)S(1)} %get-tuple-element.68.tokens, bf16[1024]{0:T(1024)(128)(2,1)S(1)} %get-tuple-element.75.gain, bf16[1024,1024]{1,0:T(8,128)(2,1)S(1)} %get-tuple-element.76.weight), custom_call_target="tpu_custom_call" | custom-call | flops 1 | bytes 1 | tf_op jit(solution)/shard_map/pallas_call | solution.py:251
  16.0 1.9 %shard_map.68 = (bf16[768,512]{1,0:T(8,128)(2,1)S(1)}, bf16[768,512]{1,0:T(8,128)(2,1)S(1)}) custom-call(bf16[1536,1024]{1,0:T(8,128)(2,1)S(1)} %get-tuple-element.68.tokens, bf16[1024]{0:T(1024)(128)(2,1)S(1)} %get-tuple-element.75.gain, bf16[1024,1024]{1,0:T(8,128)(2,1)S(1)} %get-tuple-element.70.weight), custom_call_target="tpu_custom_call" | custom-call | flops 1 | bytes 1 | tf_op jit(solution)/shard_map/pallas_call | solution.py:251
  17.9 0.1 collective-permute-start.7
  17.9 0.5 %collective-permute-start.1 = (bf16[768,512]{1,0:T(8,128)(2,1)S(1)}, bf16[768,512]{1,0:T(8,128)(2,1)S(1)}, u32[]{:S(2)}, u32[]{:S(2)}) collective-permute-start(bf16[768,512]{1,0:T(8,128)(2,1)S(1)} %get-tuple-element.72), channel_id=1, source_target_pairs={{0,1},{1,0},{2,3},{3,2},{4,5},{5,4},{6,7},{7,6},{8,9},{9,8},{10,11... | collective-permute-start | bytes 2359304 | tf_op jit(solution)/shard_map/ppermute | solution.py:314
  18.4 0.0 collective-permute-done.3.received
  18.4 0.1 shard_map.72
  18.5 0.1 collective-permute-start.4
  18.6 0.0 collective-permute-done.8.refs_1_
  18.6 4.2 %collective-permute-done.9.refs_8_ = bf16[528,512]{1,0:T(8,128)(2,1)S(1)} collective-permute-done((bf16[528,512]{1,0:T(8,128)(2,1)S(1)}, bf16[528,512]{1,0:T(8,128)(2,1)S(1)}, u32[]{:S(2)}, u32[]{:S(2)}) %collective-permute-start.9) | collective-permute-done | bytes 540704 | tf_op jit(solution)/shard_map/ppermute | solution.py:320
  22.8 1.4 %shard_map.75.refs_9_ = bf16[1536,512]{1,0:T(8,128)(2,1)} custom-call(bf16[512,512]{1,0:T(8,128)(2,1)S(1)} %get-tuple-element.93.refs_0_, bf16[512,512]{1,0:T(8,128)(2,1)S(1)} %collective-permute-done.8.refs_1_, s32[8,128]{1,0:T(8,128)S(1)} %get-tuple-element.79.refs_2_, f32[24,128]{1,0:T(8,128)S(1)} %get-tuple-element.80.refs_3_, ...), custom_call_target="tpu_custom_call" | custom-call | flops 20000000000 | bytes 1 | tf_op jit(solution)/shard_map/pallas_call | solution.py:282
  24.2 0.0 collective-permute-done.1.received
  24.2 0.2 shard_map.69
  24.4 2.1 %collective-permute-start.6 = (bf16[512,512]{1,0:T(8,128)(2,1)S(1)}, bf16[512,512]{1,0:T(8,128)(2,1)S(1)}, u32[]{:S(2)}, u32[]{:S(2)}) collective-permute-start(bf16[512,512]{1,0:T(8,128)(2,1)S(1)} %get-tuple-element.90), channel_id=1, source_target_pairs={{0,2},{1,3},{2,0},{3,1},{4,6},{5,7},{6,4},{7,5},{8,10},{9,11},{10,... | collective-permute-start | bytes 1572872 | tf_op jit(solution)/shard_map/ppermute | solution.py:320
  26.5 1.9 %shard_map.70 = (bf16[768,512]{1,0:T(8,128)(2,1)S(1)}, bf16[768,512]{1,0:T(8,128)(2,1)S(1)}) custom-call(bf16[1536,1024]{1,0:T(8,128)(2,1)S(1)} %get-tuple-element.68.tokens, bf16[1024]{0:T(1024)(128)(2,1)S(1)} %get-tuple-element.75.gain, bf16[1024,1024]{1,0:T(8,128)(2,1)S(1)} %get-tuple-element.76.weight), custom_call_target="tpu_custom_call" | custom-call | flops 1 | bytes 1 | tf_op jit(solution)/shard_map/pallas_call | solution.py:251
  28.4 0.1 collective-permute-start.2
  28.5 0.0 collective-permute-done.7.refs_1_
  28.5 0.3 collective-permute-done.4.refs_8_
  28.8 1.1 %shard_map.76.refs_10_ = bf16[1536,512]{1,0:T(8,128)(2,1)} custom-call(bf16[256,512]{1,0:T(8,128)(2,1)S(1)} %get-tuple-element.91.refs_0_, bf16[256,512]{1,0:T(8,128)(2,1)S(1)} %collective-permute-done.7.refs_1_, s32[8,128]{1,0:T(8,128)S(1)} %get-tuple-element.79.refs_2_, f32[24,128]{1,0:T(8,128)S(1)} %get-tuple-element.80.refs_3_, ...), custom_call_target="tpu_custom_call", output_to_operand_aliasing={{}: (9, {})} | custom-call | flops 20000000000 | bytes 1 | tf_op jit(solution)/shard_map/pallas_call | solution.py:282
  29.9 2.1 %collective-permute-start.5 = (bf16[256,512]{1,0:T(8,128)(2,1)S(1)}, bf16[256,512]{1,0:T(8,128)(2,1)S(1)}, u32[]{:S(2)}, u32[]{:S(2)}) collective-permute-start(bf16[256,512]{1,0:T(8,128)(2,1)S(1)} %get-tuple-element.89), channel_id=1, source_target_pairs={{0,2},{1,3},{2,0},{3,1},{4,6},{5,7},{6,4},{7,5},{8,10},{9,11},{10,... | collective-permute-start | bytes 786440 | tf_op jit(solution)/shard_map/ppermute | solution.py:320
  32.0 8.0 %collective-permute-done.6.refs_9_ = bf16[512,512]{1,0:T(8,128)(2,1)S(1)} collective-permute-done((bf16[512,512]{1,0:T(8,128)(2,1)S(1)}, bf16[512,512]{1,0:T(8,128)(2,1)S(1)}, u32[]{:S(2)}, u32[]{:S(2)}) %collective-permute-start.6) | collective-permute-done | bytes 524320 | tf_op jit(solution)/shard_map/ppermute | solution.py:320
  40.0 0.0 collective-permute-done.2.refs_1_
  40.0 1.4 %shard_map.77.refs_10_ = bf16[1536,512]{1,0:T(8,128)(2,1)} custom-call(bf16[768,512]{1,0:T(8,128)(2,1)S(1)} %get-tuple-element.77.refs_0_, bf16[768,512]{1,0:T(8,128)(2,1)S(1)} %collective-permute-done.2.refs_1_, s32[8,128]{1,0:T(8,128)S(1)} %get-tuple-element.79.refs_2_, f32[24,128]{1,0:T(8,128)S(1)} %get-tuple-element.80.refs_3_, ...), custom_call_target="tpu_custom_call", output_to_operand_aliasing={{}: (10, {})} | custom-call | flops 20000000000 | bytes 1 | tf_op jit(solution)/shard_map/pallas_call | solution.py:282
  41.4 3.7 %collective-permute-done.5.refs_9_ = bf16[256,512]{1,0:T(8,128)(2,1)S(1)} collective-permute-done((bf16[256,512]{1,0:T(8,128)(2,1)S(1)}, bf16[256,512]{1,0:T(8,128)(2,1)S(1)}, u32[]{:S(2)}, u32[]{:S(2)}) %collective-permute-start.5) | collective-permute-done | bytes 262176 | tf_op jit(solution)/shard_map/ppermute | solution.py:320
  45.1 1.1 %shard_map.78 = bf16[1536,512]{1,0:T(8,128)(2,1)} custom-call(bf16[768,512]{1,0:T(8,128)(2,1)S(1)} %get-tuple-element.77.refs_0_, bf16[768,512]{1,0:T(8,128)(2,1)S(1)} %collective-permute-done.2.refs_1_, s32[8,128]{1,0:T(8,128)S(1)} %get-tuple-element.79.refs_2_, f32[24,128]{1,0:T(8,128)S(1)} %get-tuple-element.80.refs_3_, ...), custom_call_target="tpu_custom_call", output_to_operand_aliasing={{}: (10, {})} | custom-call | flops 20000000000 | bytes 1 | tf_op jit(solution)/shard_map/pallas_call | solution.py:282
Async XLA Ops:
  0.0 0.7 %copy-start = (bf16[1024]{0:T(1024)(128)(2,1)S(1)}, bf16[1024]{0:T(1024)(128)(2,1)}, u32[]{:S(2)}) copy-start(bf16[1024]{0:T(1024)(128)(2,1)} %gain.2) | copy-start | bytes 6148
  0.7 4.4 %copy-start.2 = (s32[4]{0:T(128)S(1)}, s32[4]{0:T(128)}, u32[]{:S(2)}) copy-start(s32[4]{0:T(128)} %live) | copy-start | bytes 52
  0.7 4.4 %copy-start.3 = (s32[4]{0:T(128)S(1)}, s32[4]{0:T(128)}, u32[]{:S(2)}) copy-start(s32[4]{0:T(128)} %span) | copy-start | bytes 52
  0.7 4.4 %copy-start.4 = (f32[1,128]{1,0:T(1,128)S(1)}, f32[1,128]{1,0:T(1,128)}, u32[]{:S(2)}) copy-start(f32[1,128]{1,0:T(1,128)} %constant.4.clone.frequencies) | copy-start | bytes 1540
  0.7 9.1 %copy-start.1 = (bf16[1024]{0:T(1024)(128)(2,1)S(1)}, bf16[1024]{0:T(1024)(128)(2,1)}, u32[]{:S(2)}) copy-start(bf16[1024]{0:T(1024)(128)(2,1)} %gain.2) | copy-start | bytes 6148
  4.6 2.1 %collective-permute-start = (bf16[528,512]{1,0:T(8,128)(2,1)S(1)}, bf16[528,512]{1,0:T(8,128)(2,1)S(1)}, u32[]{:S(2)}, u32[]{:S(2)}) collective-permute-start(bf16[528,512]{1,0:T(8,128)(2,1)S(1)} %get-tuple-element.55), channel_id=1, source_target_pairs={{0,1},{1,0},{2,3},{3,2},{4,5},{5,4},{6,7},{7,6},{8,9},{9,8},{10,11... | collective-permute-start | bytes 1622024 | tf_op jit(solution)/shard_map/ppermute | solution.py:314
  6.8 16.0 %collective-permute-start.9 = (bf16[528,512]{1,0:T(8,128)(2,1)S(1)}, bf16[528,512]{1,0:T(8,128)(2,1)S(1)}, u32[]{:S(2)}, u32[]{:S(2)}) collective-permute-start(bf16[528,512]{1,0:T(8,128)(2,1)S(1)} %get-tuple-element.96), channel_id=1, source_target_pairs={{0,2},{1,3},{2,0},{3,1},{4,6},{5,7},{6,4},{7,5},{8,10},{9,11},{10,... | collective-permute-start | bytes 1622024 | tf_op jit(solution)/shard_map/ppermute | solution.py:320
  13.6 5.0 %collective-permute-start.8 = (bf16[512,512]{1,0:T(8,128)(2,1)S(1)}, bf16[512,512]{1,0:T(8,128)(2,1)S(1)}, u32[]{:S(2)}, u32[]{:S(2)}) collective-permute-start(bf16[512,512]{1,0:T(8,128)(2,1)S(1)} %get-tuple-element.94), channel_id=1, source_target_pairs={{0,1},{1,0},{2,3},{3,2},{4,5},{5,4},{6,7},{7,6},{8,9},{9,8},{10,11... | collective-permute-start | bytes 1572872 | tf_op jit(solution)/shard_map/ppermute | solution.py:356
  14.7 3.7 %collective-permute-start.3 = (bf16[272,512]{1,0:T(8,128)(2,1)S(1)}, bf16[272,512]{1,0:T(8,128)(2,1)S(1)}, u32[]{:S(2)}, u32[]{:S(2)}) collective-permute-start(bf16[272,512]{1,0:T(8,128)(2,1)S(1)} %get-tuple-element.85), channel_id=1, source_target_pairs={{0,1},{1,0},{2,3},{3,2},{4,5},{5,4},{6,7},{7,6},{8,9},{9,8},{10,11... | collective-permute-start | bytes 835592 | tf_op jit(solution)/shard_map/ppermute | solution.py:314
  17.9 10.6 %collective-permute-start.7 = (bf16[256,512]{1,0:T(8,128)(2,1)S(1)}, bf16[256,512]{1,0:T(8,128)(2,1)S(1)}, u32[]{:S(2)}, u32[]{:S(2)}) collective-permute-start(bf16[256,512]{1,0:T(8,128)(2,1)S(1)} %get-tuple-element.92), channel_id=1, source_target_pairs={{0,1},{1,0},{2,3},{3,2},{4,5},{5,4},{6,7},{7,6},{8,9},{9,8},{10,11... | collective-permute-start | bytes 786440 | tf_op jit(solution)/shard_map/ppermute | solution.py:356
  17.9 6.3 %collective-permute-start.1 = (bf16[768,512]{1,0:T(8,128)(2,1)S(1)}, bf16[768,512]{1,0:T(8,128)(2,1)S(1)}, u32[]{:S(2)}, u32[]{:S(2)}) collective-permute-start(bf16[768,512]{1,0:T(8,128)(2,1)S(1)} %get-tuple-element.72), channel_id=1, source_target_pairs={{0,1},{1,0},{2,3},{3,2},{4,5},{5,4},{6,7},{7,6},{8,9},{9,8},{10,11... | collective-permute-start | bytes 2359304 | tf_op jit(solution)/shard_map/ppermute | solution.py:314
  18.5 10.3 %collective-permute-start.4 = (bf16[272,512]{1,0:T(8,128)(2,1)S(1)}, bf16[272,512]{1,0:T(8,128)(2,1)S(1)}, u32[]{:S(2)}, u32[]{:S(2)}) collective-permute-start(bf16[272,512]{1,0:T(8,128)(2,1)S(1)} %get-tuple-element.88), channel_id=1, source_target_pairs={{0,2},{1,3},{2,0},{3,1},{4,6},{5,7},{6,4},{7,5},{8,10},{9,11},{10,... | collective-permute-start | bytes 835592 | tf_op jit(solution)/shard_map/ppermute | solution.py:320
  24.4 15.6 %collective-permute-start.6 = (bf16[512,512]{1,0:T(8,128)(2,1)S(1)}, bf16[512,512]{1,0:T(8,128)(2,1)S(1)}, u32[]{:S(2)}, u32[]{:S(2)}) collective-permute-start(bf16[512,512]{1,0:T(8,128)(2,1)S(1)} %get-tuple-element.90), channel_id=1, source_target_pairs={{0,2},{1,3},{2,0},{3,1},{4,6},{5,7},{6,4},{7,5},{8,10},{9,11},{10,... | collective-permute-start | bytes 1572872 | tf_op jit(solution)/shard_map/ppermute | solution.py:320
  28.4 11.6 %collective-permute-start.2 = (bf16[768,512]{1,0:T(8,128)(2,1)S(1)}, bf16[768,512]{1,0:T(8,128)(2,1)S(1)}, u32[]{:S(2)}, u32[]{:S(2)}) collective-permute-start(bf16[768,512]{1,0:T(8,128)(2,1)S(1)} %get-tuple-element.78), channel_id=1, source_target_pairs={{0,1},{1,0},{2,3},{3,2},{4,5},{5,4},{6,7},{7,6},{8,9},{9,8},{10,11... | collective-permute-start | bytes 2359304 | tf_op jit(solution)/shard_map/ppermute | solution.py:356
  29.9 15.3 %collective-permute-start.5 = (bf16[256,512]{1,0:T(8,128)(2,1)S(1)}, bf16[256,512]{1,0:T(8,128)(2,1)S(1)}, u32[]{:S(2)}, u32[]{:S(2)}) collective-permute-start(bf16[256,512]{1,0:T(8,128)(2,1)S(1)} %get-tuple-element.89), channel_id=1, source_target_pairs={{0,2},{1,3},{2,0},{3,1},{4,6},{5,7},{6,4},{7,5},{8,10},{9,11},{10,... | collective-permute-start | bytes 786440 | tf_op jit(solution)/shard_map/ppermute | solution.py:320

commit v24 on v20

--- a/solution.py
+++ b/solution.py
@@ -13,6 +13,7 @@
 BLOCK = 64
 LANES = 128
 SUBLANES = 8
+BF16_MAX = float(jnp.finfo(jnp.bfloat16).max)
 
 rope_base = 500000.0
 norm_eps = 1e-05
@@ -47,9 +48,10 @@
     for place in range(per_row):
         part = jnp.zeros((2 * SUBLANES, LANES), jnp.float32)
         for index, line in enumerate(squares[place::per_row]):
-            high = line.astype(jnp.bfloat16).astype(jnp.float32)
+            finite = line < jnp.inf
+            high = jnp.where(finite, jnp.minimum(line, BF16_MAX), line).astype(jnp.bfloat16).astype(jnp.float32)
             part = jnp.where(row == index, high, part)
-            part = jnp.where(row == SUBLANES + index, line - high, part)
+            part = jnp.where(row == SUBLANES + index, jnp.where(finite, line - high, 0.0), part)
         parts.append(part)
     return jnp.concatenate(parts, axis=1).astype(jnp.bfloat16)
 

time: 45.6 us -> 45.6 us (level)
  no operation moved by 1% of the time
where the time goes in v24:
time: 45.6 us; the launch traced here: 45.5 us
  Pallas kernels  18.6 us (41%)
  waiting for transfers between devices  17 us (37%)
  starting transfers between devices  9.04 us (20%)
  local copies, waits for them, and re-layouts  0.7 us (2%)
    ppermute x4, waiting for transfers between devices, cross(): lax.ppermute(part, 'tensor', shift(step))  16.2 us
    pallas_call x6, Pallas kernels, product(): pl.pallas_call(functools.partial(product_kernel, step, chip_count, first,...  9.88 us
    ppermute x4, starting transfers between devices, cross(): lax.ppermute(part, 'tensor', shift(step))  7.26 us
    pallas_call x4, Pallas kernels, finish(): pl.pallas_call(functools.partial(finish_kernel, first, at, line_at, count...  5.01 us
    pallas_call x1, Pallas kernels, shards(): pl.pallas_call(bring_kernel, in_specs=[pl.BlockSpec(memory_space=pltpu.HB...  2.57 us
    ppermute x3, starting transfers between devices, add_halves(): lax.ppermute(send, 'tensor', swap)  1.56 us
  transfers between devices with their start and end apart: 10, of which 5 were waited for; matrix products, arithmetic and copies ran while one was open for 0% of the time, Pallas kernels for 31%

profile of v24, /device:TPU:0, one launch (start us, length us, event | category | flops | bytes accessed | tf_op | source)
XLA Modules:
  0.0 45.5 jit_solution(5185739597955746051)
XLA Ops:
  0.0 0.0 copy-start
  0.0 0.7 %copy-done = bf16[1024]{0:T(1024)(128)(2,1)S(1)} copy-done((bf16[1024]{0:T(1024)(128)(2,1)S(1)}, bf16[1024]{0:T(1024)(128)(2,1)}, u32[]{:S(2)}) %copy-start) | copy-done | bytes 2072
  0.7 0.0 copy-start.2
  0.7 0.0 copy-start.3
  0.7 0.0 copy-start.4
  0.7 0.0 copy-start.1
  0.7 3.1 %shard_map.64 = (bf16[512,512]{1,0:T(8,128)(2,1)S(1)}, bf16[528,512]{1,0:T(8,128)(2,1)S(1)}, f32[4,128]{1,0:T(4,128)S(1)}, bf16[1024,1024]{1,0:T(8,128)(2,1)S(1)}) custom-call(bf16[1536,1024]{1,0:T(8,128)(2,1)} %tokens.3, bf16[1024]{0:T(1024)(128)(2,1)S(1)} %copy-done, bf16[1024,2048]{1,0:T(8,128)(2,1)} %weight.3), custom_call_target="tpu_custom_call" | custom-call | flops 999999995904 | bytes 1 | tf_op jit(solution)/shard_map/pallas_call | solution.py:253
  3.8 0.5 %collective-permute-start = (bf16[528,512]{1,0:T(8,128)(2,1)S(1)}, bf16[528,512]{1,0:T(8,128)(2,1)S(1)}, u32[]{:S(2)}, u32[]{:S(2)}) collective-permute-start(bf16[528,512]{1,0:T(8,128)(2,1)S(1)} %get-tuple-element.55), channel_id=1, source_target_pairs={{0,1},{1,0},{2,3},{3,2},{4,5},{5,4},{6,7},{7,6},{8,9},{9,8},{10,11... | collective-permute-start | bytes 1622024 | tf_op jit(solution)/shard_map/ppermute | solution.py:316
  4.4 0.0 copy-done.2
  4.4 0.0 copy-done.3
  4.4 0.0 copy-done.4
  4.4 0.7 %shard_map.66 = (s32[8,128]{1,0:T(8,128)S(1)}, f32[24,128]{1,0:T(8,128)S(1)}, f32[24,128]{1,0:T(8,128)S(1)}, f32[64,128]{1,0:T(8,128)S(1)}, f32[64,128]{1,0:T(8,128)S(1)}) custom-call(s32[4]{0:T(128)S(1)} %copy-done.2, s32[4]{0:T(128)S(1)} %copy-done.3, f32[1,128]{1,0:T(1,128)S(1)} %copy-done.4), custom_call_target="tpu_custom_call" | custom-call | flops 1 | bytes 1 | tf_op jit(solution)/shard_map/pallas_call | solution.py:267
  5.1 0.8 %collective-permute-done.received = bf16[528,512]{1,0:T(8,128)(2,1)S(1)} collective-permute-done((bf16[528,512]{1,0:T(8,128)(2,1)S(1)}, bf16[528,512]{1,0:T(8,128)(2,1)S(1)}, u32[]{:S(2)}, u32[]{:S(2)}) %collective-permute-start) | collective-permute-done | bytes 540704 | tf_op jit(solution)/shard_map/ppermute | solution.py:316
  5.9 0.1 shard_map.65
  6.1 2.9 %collective-permute-start.9 = (bf16[528,512]{1,0:T(8,128)(2,1)S(1)}, bf16[528,512]{1,0:T(8,128)(2,1)S(1)}, u32[]{:S(2)}, u32[]{:S(2)}) collective-permute-start(bf16[528,512]{1,0:T(8,128)(2,1)S(1)} %get-tuple-element.96), channel_id=1, source_target_pairs={{0,2},{1,3},{2,0},{3,1},{4,6},{5,7},{6,4},{7,5},{8,10},{9,11},{10,... | collective-permute-start | bytes 1622024 | tf_op jit(solution)/shard_map/ppermute | solution.py:322
  9.0 0.0 copy-done.1
  9.0 2.6 %shard_map.67 = (bf16[1536,1024]{1,0:T(8,128)(2,1)S(1)}, bf16[1024]{0:T(1024)(128)(2,1)S(1)}, bf16[1024,1024]{1,0:T(8,128)(2,1)S(1)}) custom-call(bf16[1536,1024]{1,0:T(8,128)(2,1)} %tokens.3, bf16[1024]{0:T(1024)(128)(2,1)S(1)} %copy-done.1, bf16[1024,2048]{1,0:T(8,128)(2,1)} %weight.3), custom_call_target="tpu_custom_call" | custom-call | flops 1 | bytes 1 | tf_op jit(solution)/shard_map/pallas_call | solution.py:332
  11.6 1.3 %shard_map.74 = (bf16[512,512]{1,0:T(8,128)(2,1)S(1)}, bf16[512,512]{1,0:T(8,128)(2,1)S(1)}) custom-call(bf16[1536,1024]{1,0:T(8,128)(2,1)S(1)} %get-tuple-element.68.tokens, bf16[1024]{0:T(1024)(128)(2,1)S(1)} %get-tuple-element.75.gain, bf16[1024,1024]{1,0:T(8,128)(2,1)S(1)} %get-tuple-element.76.weight), custom_call_target="tpu_custom_call" | custom-call | flops 1 | bytes 1 | tf_op jit(solution)/shard_map/pallas_call | solution.py:253
  12.9 0.1 collective-permute-start.8
  13.0 1.0 %shard_map.71 = (bf16[256,512]{1,0:T(8,128)(2,1)S(1)}, bf16[272,512]{1,0:T(8,128)(2,1)S(1)}, f32[8,128]{1,0:T(8,128)S(1)}) custom-call(bf16[1536,1024]{1,0:T(8,128)(2,1)S(1)} %get-tuple-element.68.tokens, bf16[1024]{0:T(1024)(128)(2,1)S(1)} %get-tuple-element.75.gain, bf16[1024,1024]{1,0:T(8,128)(2,1)S(1)} %get-tuple-element.70.weight), custom_call_target="tpu_custom_call" | custom-call | flops 1 | bytes 1 | tf_op jit(solution)/shard_map/pallas_call | solution.py:253
  13.9 0.6 %collective-permute-start.3 = (bf16[272,512]{1,0:T(8,128)(2,1)S(1)}, bf16[272,512]{1,0:T(8,128)(2,1)S(1)}, u32[]{:S(2)}, u32[]{:S(2)}) collective-permute-start(bf16[272,512]{1,0:T(8,128)(2,1)S(1)} %get-tuple-element.85), channel_id=1, source_target_pairs={{0,1},{1,0},{2,3},{3,2},{4,5},{5,4},{6,7},{7,6},{8,9},{9,8},{10,11... | collective-permute-start | bytes 835592 | tf_op jit(solution)/shard_map/ppermute | solution.py:316
  14.5 0.7 %shard_map.73 = (bf16[256,512]{1,0:T(8,128)(2,1)S(1)}, bf16[256,512]{1,0:T(8,128)(2,1)S(1)}) custom-call(bf16[1536,1024]{1,0:T(8,128)(2,1)S(1)} %get-tuple-element.68.tokens, bf16[1024]{0:T(1024)(128)(2,1)S(1)} %get-tuple-element.75.gain, bf16[1024,1024]{1,0:T(8,128)(2,1)S(1)} %get-tuple-element.76.weight), custom_call_target="tpu_custom_call" | custom-call | flops 1 | bytes 1 | tf_op jit(solution)/shard_map/pallas_call | solution.py:253
  15.2 1.9 %shard_map.68 = (bf16[768,512]{1,0:T(8,128)(2,1)S(1)}, bf16[768,512]{1,0:T(8,128)(2,1)S(1)}) custom-call(bf16[1536,1024]{1,0:T(8,128)(2,1)S(1)} %get-tuple-element.68.tokens, bf16[1024]{0:T(1024)(128)(2,1)S(1)} %get-tuple-element.75.gain, bf16[1024,1024]{1,0:T(8,128)(2,1)S(1)} %get-tuple-element.70.weight), custom_call_target="tpu_custom_call" | custom-call | flops 1 | bytes 1 | tf_op jit(solution)/shard_map/pallas_call | solution.py:253
  17.1 0.1 collective-permute-start.7
  17.2 0.5 %collective-permute-start.1 = (bf16[768,512]{1,0:T(8,128)(2,1)S(1)}, bf16[768,512]{1,0:T(8,128)(2,1)S(1)}, u32[]{:S(2)}, u32[]{:S(2)}) collective-permute-start(bf16[768,512]{1,0:T(8,128)(2,1)S(1)} %get-tuple-element.72), channel_id=1, source_target_pairs={{0,1},{1,0},{2,3},{3,2},{4,5},{5,4},{6,7},{7,6},{8,9},{9,8},{10,11... | collective-permute-start | bytes 2359304 | tf_op jit(solution)/shard_map/ppermute | solution.py:316
  17.7 0.0 collective-permute-done.3.received
  17.7 0.1 shard_map.72
  17.8 0.1 collective-permute-start.4
  17.9 0.0 collective-permute-done.8.refs_1_
  17.9 4.2 %collective-permute-done.9.refs_8_ = bf16[528,512]{1,0:T(8,128)(2,1)S(1)} collective-permute-done((bf16[528,512]{1,0:T(8,128)(2,1)S(1)}, bf16[528,512]{1,0:T(8,128)(2,1)S(1)}, u32[]{:S(2)}, u32[]{:S(2)}) %collective-permute-start.9) | collective-permute-done | bytes 540704 | tf_op jit(solution)/shard_map/ppermute | solution.py:322
  22.1 1.4 %shard_map.75.refs_9_ = bf16[1536,512]{1,0:T(8,128)(2,1)} custom-call(bf16[512,512]{1,0:T(8,128)(2,1)S(1)} %get-tuple-element.93.refs_0_, bf16[512,512]{1,0:T(8,128)(2,1)S(1)} %collective-permute-done.8.refs_1_, s32[8,128]{1,0:T(8,128)S(1)} %get-tuple-element.79.refs_2_, f32[24,128]{1,0:T(8,128)S(1)} %get-tuple-element.80.refs_3_, ...), custom_call_target="tpu_custom_call" | custom-call | flops 20000000000 | bytes 1 | tf_op jit(solution)/shard_map/pallas_call | solution.py:284
  23.5 0.0 collective-permute-done.1.received
  23.5 0.2 shard_map.69
  23.7 2.1 %collective-permute-start.6 = (bf16[512,512]{1,0:T(8,128)(2,1)S(1)}, bf16[512,512]{1,0:T(8,128)(2,1)S(1)}, u32[]{:S(2)}, u32[]{:S(2)}) collective-permute-start(bf16[512,512]{1,0:T(8,128)(2,1)S(1)} %get-tuple-element.90), channel_id=1, source_target_pairs={{0,2},{1,3},{2,0},{3,1},{4,6},{5,7},{6,4},{7,5},{8,10},{9,11},{10,... | collective-permute-start | bytes 1572872 | tf_op jit(solution)/shard_map/ppermute | solution.py:322
  25.8 1.9 %shard_map.70 = (bf16[768,512]{1,0:T(8,128)(2,1)S(1)}, bf16[768,512]{1,0:T(8,128)(2,1)S(1)}) custom-call(bf16[1536,1024]{1,0:T(8,128)(2,1)S(1)} %get-tuple-element.68.tokens, bf16[1024]{0:T(1024)(128)(2,1)S(1)} %get-tuple-element.75.gain, bf16[1024,1024]{1,0:T(8,128)(2,1)S(1)} %get-tuple-element.76.weight), custom_call_target="tpu_custom_call" | custom-call | flops 1 | bytes 1 | tf_op jit(solution)/shard_map/pallas_call | solution.py:253
  27.7 0.1 collective-permute-start.2
  27.7 0.0 collective-permute-done.7.refs_1_
  27.8 0.3 collective-permute-done.4.refs_8_
  28.0 1.1 %shard_map.76.refs_10_ = bf16[1536,512]{1,0:T(8,128)(2,1)} custom-call(bf16[256,512]{1,0:T(8,128)(2,1)S(1)} %get-tuple-element.91.refs_0_, bf16[256,512]{1,0:T(8,128)(2,1)S(1)} %collective-permute-done.7.refs_1_, s32[8,128]{1,0:T(8,128)S(1)} %get-tuple-element.79.refs_2_, f32[24,128]{1,0:T(8,128)S(1)} %get-tuple-element.80.refs_3_, ...), custom_call_target="tpu_custom_call", output_to_operand_aliasing={{}: (9, {})} | custom-call | flops 20000000000 | bytes 1 | tf_op jit(solution)/shard_map/pallas_call | solution.py:284
  29.1 2.1 %collective-permute-start.5 = (bf16[256,512]{1,0:T(8,128)(2,1)S(1)}, bf16[256,512]{1,0:T(8,128)(2,1)S(1)}, u32[]{:S(2)}, u32[]{:S(2)}) collective-permute-start(bf16[256,512]{1,0:T(8,128)(2,1)S(1)} %get-tuple-element.89), channel_id=1, source_target_pairs={{0,2},{1,3},{2,0},{3,1},{4,6},{5,7},{6,4},{7,5},{8,10},{9,11},{10,... | collective-permute-start | bytes 786440 | tf_op jit(solution)/shard_map/ppermute | solution.py:322
  31.3 8.0 %collective-permute-done.6.refs_9_ = bf16[512,512]{1,0:T(8,128)(2,1)S(1)} collective-permute-done((bf16[512,512]{1,0:T(8,128)(2,1)S(1)}, bf16[512,512]{1,0:T(8,128)(2,1)S(1)}, u32[]{:S(2)}, u32[]{:S(2)}) %collective-permute-start.6) | collective-permute-done | bytes 524320 | tf_op jit(solution)/shard_map/ppermute | solution.py:322
  39.3 0.0 collective-permute-done.2.refs_1_
  39.3 1.4 %shard_map.77.refs_10_ = bf16[1536,512]{1,0:T(8,128)(2,1)} custom-call(bf16[768,512]{1,0:T(8,128)(2,1)S(1)} %get-tuple-element.77.refs_0_, bf16[768,512]{1,0:T(8,128)(2,1)S(1)} %collective-permute-done.2.refs_1_, s32[8,128]{1,0:T(8,128)S(1)} %get-tuple-element.79.refs_2_, f32[24,128]{1,0:T(8,128)S(1)} %get-tuple-element.80.refs_3_, ...), custom_call_target="tpu_custom_call", output_to_operand_aliasing={{}: (10, {})} | custom-call | flops 20000000000 | bytes 1 | tf_op jit(solution)/shard_map/pallas_call | solution.py:284
  40.7 3.7 %collective-permute-done.5.refs_9_ = bf16[256,512]{1,0:T(8,128)(2,1)S(1)} collective-permute-done((bf16[256,512]{1,0:T(8,128)(2,1)S(1)}, bf16[256,512]{1,0:T(8,128)(2,1)S(1)}, u32[]{:S(2)}, u32[]{:S(2)}) %collective-permute-start.5) | collective-permute-done | bytes 262176 | tf_op jit(solution)/shard_map/ppermute | solution.py:322
  44.4 1.1 %shard_map.78 = bf16[1536,512]{1,0:T(8,128)(2,1)} custom-call(bf16[768,512]{1,0:T(8,128)(2,1)S(1)} %get-tuple-element.77.refs_0_, bf16[768,512]{1,0:T(8,128)(2,1)S(1)} %collective-permute-done.2.refs_1_, s32[8,128]{1,0:T(8,128)S(1)} %get-tuple-element.79.refs_2_, f32[24,128]{1,0:T(8,128)S(1)} %get-tuple-element.80.refs_3_, ...), custom_call_target="tpu_custom_call", output_to_operand_aliasing={{}: (10, {})} | custom-call | flops 20000000000 | bytes 1 | tf_op jit(solution)/shard_map/pallas_call | solution.py:284
Async XLA Ops:
  0.0 0.7 %copy-start = (bf16[1024]{0:T(1024)(128)(2,1)S(1)}, bf16[1024]{0:T(1024)(128)(2,1)}, u32[]{:S(2)}) copy-start(bf16[1024]{0:T(1024)(128)(2,1)} %gain.2) | copy-start | bytes 6148
  0.7 3.7 %copy-start.2 = (s32[4]{0:T(128)S(1)}, s32[4]{0:T(128)}, u32[]{:S(2)}) copy-start(s32[4]{0:T(128)} %live) | copy-start | bytes 52
  0.7 3.7 %copy-start.3 = (s32[4]{0:T(128)S(1)}, s32[4]{0:T(128)}, u32[]{:S(2)}) copy-start(s32[4]{0:T(128)} %span) | copy-start | bytes 52
  0.7 3.7 %copy-start.4 = (f32[1,128]{1,0:T(1,128)S(1)}, f32[1,128]{1,0:T(1,128)}, u32[]{:S(2)}) copy-start(f32[1,128]{1,0:T(1,128)} %constant.4.clone.frequencies) | copy-start | bytes 1540
  0.7 8.3 %copy-start.1 = (bf16[1024]{0:T(1024)(128)(2,1)S(1)}, bf16[1024]{0:T(1024)(128)(2,1)}, u32[]{:S(2)}) copy-start(bf16[1024]{0:T(1024)(128)(2,1)} %gain.2) | copy-start | bytes 6148
  3.8 2.1 %collective-permute-start = (bf16[528,512]{1,0:T(8,128)(2,1)S(1)}, bf16[528,512]{1,0:T(8,128)(2,1)S(1)}, u32[]{:S(2)}, u32[]{:S(2)}) collective-permute-start(bf16[528,512]{1,0:T(8,128)(2,1)S(1)} %get-tuple-element.55), channel_id=1, source_target_pairs={{0,1},{1,0},{2,3},{3,2},{4,5},{5,4},{6,7},{7,6},{8,9},{9,8},{10,11... | collective-permute-start | bytes 1622024 | tf_op jit(solution)/shard_map/ppermute | solution.py:316
  6.1 16.0 %collective-permute-start.9 = (bf16[528,512]{1,0:T(8,128)(2,1)S(1)}, bf16[528,512]{1,0:T(8,128)(2,1)S(1)}, u32[]{:S(2)}, u32[]{:S(2)}) collective-permute-start(bf16[528,512]{1,0:T(8,128)(2,1)S(1)} %get-tuple-element.96), channel_id=1, source_target_pairs={{0,2},{1,3},{2,0},{3,1},{4,6},{5,7},{6,4},{7,5},{8,10},{9,11},{10,... | collective-permute-start | bytes 1622024 | tf_op jit(solution)/shard_map/ppermute | solution.py:322
  12.9 5.0 %collective-permute-start.8 = (bf16[512,512]{1,0:T(8,128)(2,1)S(1)}, bf16[512,512]{1,0:T(8,128)(2,1)S(1)}, u32[]{:S(2)}, u32[]{:S(2)}) collective-permute-start(bf16[512,512]{1,0:T(8,128)(2,1)S(1)} %get-tuple-element.94), channel_id=1, source_target_pairs={{0,1},{1,0},{2,3},{3,2},{4,5},{5,4},{6,7},{7,6},{8,9},{9,8},{10,11... | collective-permute-start | bytes 1572872 | tf_op jit(solution)/shard_map/ppermute | solution.py:358
  13.9 3.7 %collective-permute-start.3 = (bf16[272,512]{1,0:T(8,128)(2,1)S(1)}, bf16[272,512]{1,0:T(8,128)(2,1)S(1)}, u32[]{:S(2)}, u32[]{:S(2)}) collective-permute-start(bf16[272,512]{1,0:T(8,128)(2,1)S(1)} %get-tuple-element.85), channel_id=1, source_target_pairs={{0,1},{1,0},{2,3},{3,2},{4,5},{5,4},{6,7},{7,6},{8,9},{9,8},{10,11... | collective-permute-start | bytes 835592 | tf_op jit(solution)/shard_map/ppermute | solution.py:316
  17.1 10.6 %collective-permute-start.7 = (bf16[256,512]{1,0:T(8,128)(2,1)S(1)}, bf16[256,512]{1,0:T(8,128)(2,1)S(1)}, u32[]{:S(2)}, u32[]{:S(2)}) collective-permute-start(bf16[256,512]{1,0:T(8,128)(2,1)S(1)} %get-tuple-element.92), channel_id=1, source_target_pairs={{0,1},{1,0},{2,3},{3,2},{4,5},{5,4},{6,7},{7,6},{8,9},{9,8},{10,11... | collective-permute-start | bytes 786440 | tf_op jit(solution)/shard_map/ppermute | solution.py:358
  17.2 6.3 %collective-permute-start.1 = (bf16[768,512]{1,0:T(8,128)(2,1)S(1)}, bf16[768,512]{1,0:T(8,128)(2,1)S(1)}, u32[]{:S(2)}, u32[]{:S(2)}) collective-permute-start(bf16[768,512]{1,0:T(8,128)(2,1)S(1)} %get-tuple-element.72), channel_id=1, source_target_pairs={{0,1},{1,0},{2,3},{3,2},{4,5},{5,4},{6,7},{7,6},{8,9},{9,8},{10,11... | collective-permute-start | bytes 2359304 | tf_op jit(solution)/shard_map/ppermute | solution.py:316
  17.8 10.2 %collective-permute-start.4 = (bf16[272,512]{1,0:T(8,128)(2,1)S(1)}, bf16[272,512]{1,0:T(8,128)(2,1)S(1)}, u32[]{:S(2)}, u32[]{:S(2)}) collective-permute-start(bf16[272,512]{1,0:T(8,128)(2,1)S(1)} %get-tuple-element.88), channel_id=1, source_target_pairs={{0,2},{1,3},{2,0},{3,1},{4,6},{5,7},{6,4},{7,5},{8,10},{9,11},{10,... | collective-permute-start | bytes 835592 | tf_op jit(solution)/shard_map/ppermute | solution.py:322
  23.7 15.6 %collective-permute-start.6 = (bf16[512,512]{1,0:T(8,128)(2,1)S(1)}, bf16[512,512]{1,0:T(8,128)(2,1)S(1)}, u32[]{:S(2)}, u32[]{:S(2)}) collective-permute-start(bf16[512,512]{1,0:T(8,128)(2,1)S(1)} %get-tuple-element.90), channel_id=1, source_target_pairs={{0,2},{1,3},{2,0},{3,1},{4,6},{5,7},{6,4},{7,5},{8,10},{9,11},{10,... | collective-permute-start | bytes 1572872 | tf_op jit(solution)/shard_map/ppermute | solution.py:322
  27.7 11.6 %collective-permute-start.2 = (bf16[768,512]{1,0:T(8,128)(2,1)S(1)}, bf16[768,512]{1,0:T(8,128)(2,1)S(1)}, u32[]{:S(2)}, u32[]{:S(2)}) collective-permute-start(bf16[768,512]{1,0:T(8,128)(2,1)S(1)} %get-tuple-element.78), channel_id=1, source_target_pairs={{0,1},{1,0},{2,3},{3,2},{4,5},{5,4},{6,7},{7,6},{8,9},{9,8},{10,11... | collective-permute-start | bytes 2359304 | tf_op jit(solution)/shard_map/ppermute | solution.py:358
  29.1 15.3 %collective-permute-start.5 = (bf16[256,512]{1,0:T(8,128)(2,1)S(1)}, bf16[256,512]{1,0:T(8,128)(2,1)S(1)}, u32[]{:S(2)}, u32[]{:S(2)}) collective-permute-start(bf16[256,512]{1,0:T(8,128)(2,1)S(1)} %get-tuple-element.89), channel_id=1, source_target_pairs={{0,2},{1,3},{2,0},{3,1},{4,6},{5,7},{6,4},{7,5},{8,10},{9,11},{10,... | collective-permute-start | bytes 786440 | tf_op jit(solution)/shard_map/ppermute | solution.py:322

commit v25 on v24

--- a/solution.py
+++ b/solution.py
@@ -214,8 +214,9 @@
             staged[inside, low : low + HD] = jnp.where(alive, turned, 0.0).astype(out.dtype)
             value = values[:, low + HD : low + 2 * HD] * scales
             staged[inside, low + HD : low + 2 * HD] = jnp.where(alive, value, 0.0).astype(out.dtype)
-        copies.append(pltpu.make_async_copy(staged.at[inside, :], out.at[rows, :], sems.at[index]))
-        copies[-1].start()
+            head = pl.ds(low, 2 * HD)
+            copies.append(pltpu.make_async_copy(staged.at[inside, head], out.at[rows, head], sems.at[len(copies)]))
+            copies[-1].start()
     for copy in copies:
         copy.wait()
 
@@ -286,7 +287,7 @@
             in_specs=[vmem] * len(operands) + [pl.BlockSpec(memory_space=pl.ANY)],
             out_shape=jax.ShapeDtypeStruct((slot_rows, columns), jnp.bfloat16),
             out_specs=pl.BlockSpec(memory_space=pltpu.HBM),
-            scratch_shapes=[pltpu.VMEM((count * TILE, columns), jnp.bfloat16), pltpu.SemaphoreType.DMA((count,))],
+            scratch_shapes=[pltpu.VMEM((count * TILE, columns), jnp.bfloat16), pltpu.SemaphoreType.DMA((count * columns // (2 * HD),))],
             input_output_aliases=aliases,
             compiler_params=PARAMS,
             cost_estimate=LATER,

time: 45.6 us -> 45.6 us (level)
  no operation moved by 1% of the time
where the time goes in v25:
time: 45.6 us; the launch traced here: 45.5 us
  Pallas kernels  18.5 us (41%)
  waiting for transfers between devices  17.1 us (38%)
  starting transfers between devices  9.04 us (20%)
  local copies, waits for them, and re-layouts  0.7 us (2%)
    ppermute x4, waiting for transfers between devices, cross(): lax.ppermute(part, 'tensor', shift(step))  16.3 us
    pallas_call x6, Pallas kernels, product(): pl.pallas_call(functools.partial(product_kernel, step, chip_count, first,...  9.88 us
    ppermute x4, starting transfers between devices, cross(): lax.ppermute(part, 'tensor', shift(step))  7.26 us
    pallas_call x4, Pallas kernels, finish(): pl.pallas_call(functools.partial(finish_kernel, first, at, line_at, count...  4.9 us
    pallas_call x1, Pallas kernels, shards(): pl.pallas_call(bring_kernel, in_specs=[pl.BlockSpec(memory_space=pltpu.HB...  2.57 us
    ppermute x3, starting transfers between devices, add_halves(): lax.ppermute(send, 'tensor', swap)  1.56 us
  transfers between devices with their start and end apart: 10, of which 5 were waited for; matrix products, arithmetic and copies ran while one was open for 0% of the time, Pallas kernels for 31%

profile of v25, /device:TPU:0, one launch (start us, length us, event | category | flops | bytes accessed | tf_op | source)
XLA Modules:
  0.0 45.5 jit_solution(10958468716229166900)
XLA Ops:
  0.0 0.0 copy-start
  0.0 0.7 %copy-done = bf16[1024]{0:T(1024)(128)(2,1)S(1)} copy-done((bf16[1024]{0:T(1024)(128)(2,1)S(1)}, bf16[1024]{0:T(1024)(128)(2,1)}, u32[]{:S(2)}) %copy-start) | copy-done | bytes 2072
  0.7 0.0 copy-start.2
  0.7 0.0 copy-start.3
  0.7 0.0 copy-start.4
  0.7 0.0 copy-start.1
  0.7 3.1 %shard_map.64 = (bf16[512,512]{1,0:T(8,128)(2,1)S(1)}, bf16[528,512]{1,0:T(8,128)(2,1)S(1)}, f32[4,128]{1,0:T(4,128)S(1)}, bf16[1024,1024]{1,0:T(8,128)(2,1)S(1)}) custom-call(bf16[1536,1024]{1,0:T(8,128)(2,1)} %tokens.3, bf16[1024]{0:T(1024)(128)(2,1)S(1)} %copy-done, bf16[1024,2048]{1,0:T(8,128)(2,1)} %weight.3), custom_call_target="tpu_custom_call" | custom-call | flops 999999995904 | bytes 1 | tf_op jit(solution)/shard_map/pallas_call | solution.py:254
  3.8 0.5 %collective-permute-start = (bf16[528,512]{1,0:T(8,128)(2,1)S(1)}, bf16[528,512]{1,0:T(8,128)(2,1)S(1)}, u32[]{:S(2)}, u32[]{:S(2)}) collective-permute-start(bf16[528,512]{1,0:T(8,128)(2,1)S(1)} %get-tuple-element.55), channel_id=1, source_target_pairs={{0,1},{1,0},{2,3},{3,2},{4,5},{5,4},{6,7},{7,6},{8,9},{9,8},{10,11... | collective-permute-start | bytes 1622024 | tf_op jit(solution)/shard_map/ppermute | solution.py:317
  4.4 0.0 copy-done.2
  4.4 0.0 copy-done.3
  4.4 0.0 copy-done.4
  4.4 0.7 %shard_map.66 = (s32[8,128]{1,0:T(8,128)S(1)}, f32[24,128]{1,0:T(8,128)S(1)}, f32[24,128]{1,0:T(8,128)S(1)}, f32[64,128]{1,0:T(8,128)S(1)}, f32[64,128]{1,0:T(8,128)S(1)}) custom-call(s32[4]{0:T(128)S(1)} %copy-done.2, s32[4]{0:T(128)S(1)} %copy-done.3, f32[1,128]{1,0:T(1,128)S(1)} %copy-done.4), custom_call_target="tpu_custom_call" | custom-call | flops 1 | bytes 1 | tf_op jit(solution)/shard_map/pallas_call | solution.py:268
  5.1 0.8 %collective-permute-done.received = bf16[528,512]{1,0:T(8,128)(2,1)S(1)} collective-permute-done((bf16[528,512]{1,0:T(8,128)(2,1)S(1)}, bf16[528,512]{1,0:T(8,128)(2,1)S(1)}, u32[]{:S(2)}, u32[]{:S(2)}) %collective-permute-start) | collective-permute-done | bytes 540704 | tf_op jit(solution)/shard_map/ppermute | solution.py:317
  5.9 0.1 shard_map.65
  6.1 2.9 %collective-permute-start.9 = (bf16[528,512]{1,0:T(8,128)(2,1)S(1)}, bf16[528,512]{1,0:T(8,128)(2,1)S(1)}, u32[]{:S(2)}, u32[]{:S(2)}) collective-permute-start(bf16[528,512]{1,0:T(8,128)(2,1)S(1)} %get-tuple-element.96), channel_id=1, source_target_pairs={{0,2},{1,3},{2,0},{3,1},{4,6},{5,7},{6,4},{7,5},{8,10},{9,11},{10,... | collective-permute-start | bytes 1622024 | tf_op jit(solution)/shard_map/ppermute | solution.py:323
  9.0 0.0 copy-done.1
  9.0 2.6 %shard_map.67 = (bf16[1536,1024]{1,0:T(8,128)(2,1)S(1)}, bf16[1024]{0:T(1024)(128)(2,1)S(1)}, bf16[1024,1024]{1,0:T(8,128)(2,1)S(1)}) custom-call(bf16[1536,1024]{1,0:T(8,128)(2,1)} %tokens.3, bf16[1024]{0:T(1024)(128)(2,1)S(1)} %copy-done.1, bf16[1024,2048]{1,0:T(8,128)(2,1)} %weight.3), custom_call_target="tpu_custom_call" | custom-call | flops 1 | bytes 1 | tf_op jit(solution)/shard_map/pallas_call | solution.py:333
  11.6 1.3 %shard_map.74 = (bf16[512,512]{1,0:T(8,128)(2,1)S(1)}, bf16[512,512]{1,0:T(8,128)(2,1)S(1)}) custom-call(bf16[1536,1024]{1,0:T(8,128)(2,1)S(1)} %get-tuple-element.68.tokens, bf16[1024]{0:T(1024)(128)(2,1)S(1)} %get-tuple-element.75.gain, bf16[1024,1024]{1,0:T(8,128)(2,1)S(1)} %get-tuple-element.76.weight), custom_call_target="tpu_custom_call" | custom-call | flops 1 | bytes 1 | tf_op jit(solution)/shard_map/pallas_call | solution.py:254
  12.9 0.1 collective-permute-start.8
  13.0 1.0 %shard_map.71 = (bf16[256,512]{1,0:T(8,128)(2,1)S(1)}, bf16[272,512]{1,0:T(8,128)(2,1)S(1)}, f32[8,128]{1,0:T(8,128)S(1)}) custom-call(bf16[1536,1024]{1,0:T(8,128)(2,1)S(1)} %get-tuple-element.68.tokens, bf16[1024]{0:T(1024)(128)(2,1)S(1)} %get-tuple-element.75.gain, bf16[1024,1024]{1,0:T(8,128)(2,1)S(1)} %get-tuple-element.70.weight), custom_call_target="tpu_custom_call" | custom-call | flops 1 | bytes 1 | tf_op jit(solution)/shard_map/pallas_call | solution.py:254
  13.9 0.6 %collective-permute-start.3 = (bf16[272,512]{1,0:T(8,128)(2,1)S(1)}, bf16[272,512]{1,0:T(8,128)(2,1)S(1)}, u32[]{:S(2)}, u32[]{:S(2)}) collective-permute-start(bf16[272,512]{1,0:T(8,128)(2,1)S(1)} %get-tuple-element.85), channel_id=1, source_target_pairs={{0,1},{1,0},{2,3},{3,2},{4,5},{5,4},{6,7},{7,6},{8,9},{9,8},{10,11... | collective-permute-start | bytes 835592 | tf_op jit(solution)/shard_map/ppermute | solution.py:317
  14.5 0.7 %shard_map.73 = (bf16[256,512]{1,0:T(8,128)(2,1)S(1)}, bf16[256,512]{1,0:T(8,128)(2,1)S(1)}) custom-call(bf16[1536,1024]{1,0:T(8,128)(2,1)S(1)} %get-tuple-element.68.tokens, bf16[1024]{0:T(1024)(128)(2,1)S(1)} %get-tuple-element.75.gain, bf16[1024,1024]{1,0:T(8,128)(2,1)S(1)} %get-tuple-element.76.weight), custom_call_target="tpu_custom_call" | custom-call | flops 1 | bytes 1 | tf_op jit(solution)/shard_map/pallas_call | solution.py:254
  15.2 1.9 %shard_map.68 = (bf16[768,512]{1,0:T(8,128)(2,1)S(1)}, bf16[768,512]{1,0:T(8,128)(2,1)S(1)}) custom-call(bf16[1536,1024]{1,0:T(8,128)(2,1)S(1)} %get-tuple-element.68.tokens, bf16[1024]{0:T(1024)(128)(2,1)S(1)} %get-tuple-element.75.gain, bf16[1024,1024]{1,0:T(8,128)(2,1)S(1)} %get-tuple-element.70.weight), custom_call_target="tpu_custom_call" | custom-call | flops 1 | bytes 1 | tf_op jit(solution)/shard_map/pallas_call | solution.py:254
  17.1 0.1 collective-permute-start.7
  17.2 0.5 %collective-permute-start.1 = (bf16[768,512]{1,0:T(8,128)(2,1)S(1)}, bf16[768,512]{1,0:T(8,128)(2,1)S(1)}, u32[]{:S(2)}, u32[]{:S(2)}) collective-permute-start(bf16[768,512]{1,0:T(8,128)(2,1)S(1)} %get-tuple-element.72), channel_id=1, source_target_pairs={{0,1},{1,0},{2,3},{3,2},{4,5},{5,4},{6,7},{7,6},{8,9},{9,8},{10,11... | collective-permute-start | bytes 2359304 | tf_op jit(solution)/shard_map/ppermute | solution.py:317
  17.7 0.0 collective-permute-done.3.received
  17.7 0.1 shard_map.72
  17.8 0.1 collective-permute-start.4
  17.9 0.0 collective-permute-done.8.refs_1_
  17.9 4.2 %collective-permute-done.9.refs_8_ = bf16[528,512]{1,0:T(8,128)(2,1)S(1)} collective-permute-done((bf16[528,512]{1,0:T(8,128)(2,1)S(1)}, bf16[528,512]{1,0:T(8,128)(2,1)S(1)}, u32[]{:S(2)}, u32[]{:S(2)}) %collective-permute-start.9) | collective-permute-done | bytes 540704 | tf_op jit(solution)/shard_map/ppermute | solution.py:323
  22.1 1.4 %shard_map.75.refs_9_ = bf16[1536,512]{1,0:T(8,128)(2,1)} custom-call(bf16[512,512]{1,0:T(8,128)(2,1)S(1)} %get-tuple-element.93.refs_0_, bf16[512,512]{1,0:T(8,128)(2,1)S(1)} %collective-permute-done.8.refs_1_, s32[8,128]{1,0:T(8,128)S(1)} %get-tuple-element.79.refs_2_, f32[24,128]{1,0:T(8,128)S(1)} %get-tuple-element.80.refs_3_, ...), custom_call_target="tpu_custom_call" | custom-call | flops 20000000000 | bytes 1 | tf_op jit(solution)/shard_map/pallas_call | solution.py:285
  23.5 0.0 collective-permute-done.1.received
  23.5 0.2 shard_map.69
  23.7 2.1 %collective-permute-start.6 = (bf16[512,512]{1,0:T(8,128)(2,1)S(1)}, bf16[512,512]{1,0:T(8,128)(2,1)S(1)}, u32[]{:S(2)}, u32[]{:S(2)}) collective-permute-start(bf16[512,512]{1,0:T(8,128)(2,1)S(1)} %get-tuple-element.90), channel_id=1, source_target_pairs={{0,2},{1,3},{2,0},{3,1},{4,6},{5,7},{6,4},{7,5},{8,10},{9,11},{10,... | collective-permute-start | bytes 1572872 | tf_op jit(solution)/shard_map/ppermute | solution.py:323
  25.8 1.9 %shard_map.70 = (bf16[768,512]{1,0:T(8,128)(2,1)S(1)}, bf16[768,512]{1,0:T(8,128)(2,1)S(1)}) custom-call(bf16[1536,1024]{1,0:T(8,128)(2,1)S(1)} %get-tuple-element.68.tokens, bf16[1024]{0:T(1024)(128)(2,1)S(1)} %get-tuple-element.75.gain, bf16[1024,1024]{1,0:T(8,128)(2,1)S(1)} %get-tuple-element.76.weight), custom_call_target="tpu_custom_call" | custom-call | flops 1 | bytes 1 | tf_op jit(solution)/shard_map/pallas_call | solution.py:254
  27.6 0.1 collective-permute-start.2
  27.7 0.0 collective-permute-done.7.refs_1_
  27.7 0.3 collective-permute-done.4.refs_8_
  28.0 1.1 %shard_map.76.refs_10_ = bf16[1536,512]{1,0:T(8,128)(2,1)} custom-call(bf16[256,512]{1,0:T(8,128)(2,1)S(1)} %get-tuple-element.91.refs_0_, bf16[256,512]{1,0:T(8,128)(2,1)S(1)} %collective-permute-done.7.refs_1_, s32[8,128]{1,0:T(8,128)S(1)} %get-tuple-element.79.refs_2_, f32[24,128]{1,0:T(8,128)S(1)} %get-tuple-element.80.refs_3_, ...), custom_call_target="tpu_custom_call", output_to_operand_aliasing={{}: (9, {})} | custom-call | flops 20000000000 | bytes 1 | tf_op jit(solution)/shard_map/pallas_call | solution.py:285
  29.1 2.1 %collective-permute-start.5 = (bf16[256,512]{1,0:T(8,128)(2,1)S(1)}, bf16[256,512]{1,0:T(8,128)(2,1)S(1)}, u32[]{:S(2)}, u32[]{:S(2)}) collective-permute-start(bf16[256,512]{1,0:T(8,128)(2,1)S(1)} %get-tuple-element.89), channel_id=1, source_target_pairs={{0,2},{1,3},{2,0},{3,1},{4,6},{5,7},{6,4},{7,5},{8,10},{9,11},{10,... | collective-permute-start | bytes 786440 | tf_op jit(solution)/shard_map/ppermute | solution.py:323
  31.2 8.0 %collective-permute-done.6.refs_9_ = bf16[512,512]{1,0:T(8,128)(2,1)S(1)} collective-permute-done((bf16[512,512]{1,0:T(8,128)(2,1)S(1)}, bf16[512,512]{1,0:T(8,128)(2,1)S(1)}, u32[]{:S(2)}, u32[]{:S(2)}) %collective-permute-start.6) | collective-permute-done | bytes 524320 | tf_op jit(solution)/shard_map/ppermute | solution.py:323
  39.3 0.0 collective-permute-done.2.refs_1_
  39.3 1.4 %shard_map.77.refs_10_ = bf16[1536,512]{1,0:T(8,128)(2,1)} custom-call(bf16[768,512]{1,0:T(8,128)(2,1)S(1)} %get-tuple-element.77.refs_0_, bf16[768,512]{1,0:T(8,128)(2,1)S(1)} %collective-permute-done.2.refs_1_, s32[8,128]{1,0:T(8,128)S(1)} %get-tuple-element.79.refs_2_, f32[24,128]{1,0:T(8,128)S(1)} %get-tuple-element.80.refs_3_, ...), custom_call_target="tpu_custom_call", output_to_operand_aliasing={{}: (10, {})} | custom-call | flops 20000000000 | bytes 1 | tf_op jit(solution)/shard_map/pallas_call | solution.py:285
  40.6 3.8 %collective-permute-done.5.refs_9_ = bf16[256,512]{1,0:T(8,128)(2,1)S(1)} collective-permute-done((bf16[256,512]{1,0:T(8,128)(2,1)S(1)}, bf16[256,512]{1,0:T(8,128)(2,1)S(1)}, u32[]{:S(2)}, u32[]{:S(2)}) %collective-permute-start.5) | collective-permute-done | bytes 262176 | tf_op jit(solution)/shard_map/ppermute | solution.py:323
  44.4 1.1 %shard_map.78 = bf16[1536,512]{1,0:T(8,128)(2,1)} custom-call(bf16[768,512]{1,0:T(8,128)(2,1)S(1)} %get-tuple-element.77.refs_0_, bf16[768,512]{1,0:T(8,128)(2,1)S(1)} %collective-permute-done.2.refs_1_, s32[8,128]{1,0:T(8,128)S(1)} %get-tuple-element.79.refs_2_, f32[24,128]{1,0:T(8,128)S(1)} %get-tuple-element.80.refs_3_, ...), custom_call_target="tpu_custom_call", output_to_operand_aliasing={{}: (10, {})} | custom-call | flops 20000000000 | bytes 1 | tf_op jit(solution)/shard_map/pallas_call | solution.py:285
Async XLA Ops:
  0.0 0.7 %copy-start = (bf16[1024]{0:T(1024)(128)(2,1)S(1)}, bf16[1024]{0:T(1024)(128)(2,1)}, u32[]{:S(2)}) copy-start(bf16[1024]{0:T(1024)(128)(2,1)} %gain.2) | copy-start | bytes 6148
  0.7 3.7 %copy-start.2 = (s32[4]{0:T(128)S(1)}, s32[4]{0:T(128)}, u32[]{:S(2)}) copy-start(s32[4]{0:T(128)} %live) | copy-start | bytes 52
  0.7 3.7 %copy-start.3 = (s32[4]{0:T(128)S(1)}, s32[4]{0:T(128)}, u32[]{:S(2)}) copy-start(s32[4]{0:T(128)} %span) | copy-start | bytes 52
  0.7 3.7 %copy-start.4 = (f32[1,128]{1,0:T(1,128)S(1)}, f32[1,128]{1,0:T(1,128)}, u32[]{:S(2)}) copy-start(f32[1,128]{1,0:T(1,128)} %constant.4.clone.frequencies) | copy-start | bytes 1540
  0.7 8.3 %copy-start.1 = (bf16[1024]{0:T(1024)(128)(2,1)S(1)}, bf16[1024]{0:T(1024)(128)(2,1)}, u32[]{:S(2)}) copy-start(bf16[1024]{0:T(1024)(128)(2,1)} %gain.2) | copy-start | bytes 6148
  3.8 2.1 %collective-permute-start = (bf16[528,512]{1,0:T(8,128)(2,1)S(1)}, bf16[528,512]{1,0:T(8,128)(2,1)S(1)}, u32[]{:S(2)}, u32[]{:S(2)}) collective-permute-start(bf16[528,512]{1,0:T(8,128)(2,1)S(1)} %get-tuple-element.55), channel_id=1, source_target_pairs={{0,1},{1,0},{2,3},{3,2},{4,5},{5,4},{6,7},{7,6},{8,9},{9,8},{10,11... | collective-permute-start | bytes 1622024 | tf_op jit(solution)/shard_map/ppermute | solution.py:317
  6.1 16.0 %collective-permute-start.9 = (bf16[528,512]{1,0:T(8,128)(2,1)S(1)}, bf16[528,512]{1,0:T(8,128)(2,1)S(1)}, u32[]{:S(2)}, u32[]{:S(2)}) collective-permute-start(bf16[528,512]{1,0:T(8,128)(2,1)S(1)} %get-tuple-element.96), channel_id=1, source_target_pairs={{0,2},{1,3},{2,0},{3,1},{4,6},{5,7},{6,4},{7,5},{8,10},{9,11},{10,... | collective-permute-start | bytes 1622024 | tf_op jit(solution)/shard_map/ppermute | solution.py:323
  12.9 5.0 %collective-permute-start.8 = (bf16[512,512]{1,0:T(8,128)(2,1)S(1)}, bf16[512,512]{1,0:T(8,128)(2,1)S(1)}, u32[]{:S(2)}, u32[]{:S(2)}) collective-permute-start(bf16[512,512]{1,0:T(8,128)(2,1)S(1)} %get-tuple-element.94), channel_id=1, source_target_pairs={{0,1},{1,0},{2,3},{3,2},{4,5},{5,4},{6,7},{7,6},{8,9},{9,8},{10,11... | collective-permute-start | bytes 1572872 | tf_op jit(solution)/shard_map/ppermute | solution.py:359
  13.9 3.7 %collective-permute-start.3 = (bf16[272,512]{1,0:T(8,128)(2,1)S(1)}, bf16[272,512]{1,0:T(8,128)(2,1)S(1)}, u32[]{:S(2)}, u32[]{:S(2)}) collective-permute-start(bf16[272,512]{1,0:T(8,128)(2,1)S(1)} %get-tuple-element.85), channel_id=1, source_target_pairs={{0,1},{1,0},{2,3},{3,2},{4,5},{5,4},{6,7},{7,6},{8,9},{9,8},{10,11... | collective-permute-start | bytes 835592 | tf_op jit(solution)/shard_map/ppermute | solution.py:317
  17.1 10.6 %collective-permute-start.7 = (bf16[256,512]{1,0:T(8,128)(2,1)S(1)}, bf16[256,512]{1,0:T(8,128)(2,1)S(1)}, u32[]{:S(2)}, u32[]{:S(2)}) collective-permute-start(bf16[256,512]{1,0:T(8,128)(2,1)S(1)} %get-tuple-element.92), channel_id=1, source_target_pairs={{0,1},{1,0},{2,3},{3,2},{4,5},{5,4},{6,7},{7,6},{8,9},{9,8},{10,11... | collective-permute-start | bytes 786440 | tf_op jit(solution)/shard_map/ppermute | solution.py:359
  17.2 6.3 %collective-permute-start.1 = (bf16[768,512]{1,0:T(8,128)(2,1)S(1)}, bf16[768,512]{1,0:T(8,128)(2,1)S(1)}, u32[]{:S(2)}, u32[]{:S(2)}) collective-permute-start(bf16[768,512]{1,0:T(8,128)(2,1)S(1)} %get-tuple-element.72), channel_id=1, source_target_pairs={{0,1},{1,0},{2,3},{3,2},{4,5},{5,4},{6,7},{7,6},{8,9},{9,8},{10,11... | collective-permute-start | bytes 2359304 | tf_op jit(solution)/shard_map/ppermute | solution.py:317
  17.8 10.2 %collective-permute-start.4 = (bf16[272,512]{1,0:T(8,128)(2,1)S(1)}, bf16[272,512]{1,0:T(8,128)(2,1)S(1)}, u32[]{:S(2)}, u32[]{:S(2)}) collective-permute-start(bf16[272,512]{1,0:T(8,128)(2,1)S(1)} %get-tuple-element.88), channel_id=1, source_target_pairs={{0,2},{1,3},{2,0},{3,1},{4,6},{5,7},{6,4},{7,5},{8,10},{9,11},{10,... | collective-permute-start | bytes 835592 | tf_op jit(solution)/shard_map/ppermute | solution.py:323
  23.7 15.6 %collective-permute-start.6 = (bf16[512,512]{1,0:T(8,128)(2,1)S(1)}, bf16[512,512]{1,0:T(8,128)(2,1)S(1)}, u32[]{:S(2)}, u32[]{:S(2)}) collective-permute-start(bf16[512,512]{1,0:T(8,128)(2,1)S(1)} %get-tuple-element.90), channel_id=1, source_target_pairs={{0,2},{1,3},{2,0},{3,1},{4,6},{5,7},{6,4},{7,5},{8,10},{9,11},{10,... | collective-permute-start | bytes 1572872 | tf_op jit(solution)/shard_map/ppermute | solution.py:323
  27.6 11.6 %collective-permute-start.2 = (bf16[768,512]{1,0:T(8,128)(2,1)S(1)}, bf16[768,512]{1,0:T(8,128)(2,1)S(1)}, u32[]{:S(2)}, u32[]{:S(2)}) collective-permute-start(bf16[768,512]{1,0:T(8,128)(2,1)S(1)} %get-tuple-element.78), channel_id=1, source_target_pairs={{0,1},{1,0},{2,3},{3,2},{4,5},{5,4},{6,7},{7,6},{8,9},{9,8},{10,11... | collective-permute-start | bytes 2359304 | tf_op jit(solution)/shard_map/ppermute | solution.py:359
  29.1 15.3 %collective-permute-start.5 = (bf16[256,512]{1,0:T(8,128)(2,1)S(1)}, bf16[256,512]{1,0:T(8,128)(2,1)S(1)}, u32[]{:S(2)}, u32[]{:S(2)}) collective-permute-start(bf16[256,512]{1,0:T(8,128)(2,1)S(1)} %get-tuple-element.89), channel_id=1, source_target_pairs={{0,2},{1,3},{2,0},{3,1},{4,6},{5,7},{6,4},{7,5},{8,10},{9,11},{10,... | collective-permute-start | bytes 786440 | tf_op jit(solution)/shard_map/ppermute | solution.py:323
